TPU v7x, 32 devices: a whole 2x2x4 slice. The times are simulated.
32 devices in a mesh: blk: 8 (over z, x), grp: 4 (over y, core).
Axes of the slice: x: 2, y: 2, z: 4, core: 2. Of those that a mesh axis runs over, the one named last changes fastest.
Arguments:
- picture_embedding_matrix: bfloat16 [13312, 1152], P(('blk', 'grp')), may hold values from -0.1875 to 0.1875
- caption_embedding_matrix: bfloat16 [13312, 1152], P(('blk', 'grp')), may hold values from -0.1875 to 0.1875
- matching_target_entry: int32 [32, 416], P(('blk', 'grp')), may hold values from 0 to 415, each once within a row
- sharpness_factor: float32 [1], replicated, may hold values from 5 to 20
- score_shift_array: float32 [1], replicated, may hold values from -4 to -1
Outputs:
- image_grad: bfloat16 [13312, 1152], P(('blk', 'grp'))
- text_grad: bfloat16 [13312, 1152], P(('blk', 'grp'))
Inputs may be any that keep to these rules, and one draw needn't show every extreme that they name: Each row of matching_target_entry is a permutation of 0 to 415.
All inputs are finite; a program needn't handle non-finite values.
Results may differ from a plain program's by a relative error of at most 0.0056.
Values may be sent and summed in bfloat16 or wider, within the bound.
No kernel may reach another device: no remote copies, remote signals or barrier semaphores. Data moves between devices by JAX's collectives and lax.ppermute only.
A program may use at most 64 MiB of HBM per device.

v0:
```python
import jax
import jax.numpy as jnp
from jax import lax
from jax.sharding import PartitionSpec as P


def shifted(shard, axis, by):
    devices = lax.axis_size(axis)
    return lax.ppermute(shard, axis, [(i, (i + by) % devices) for i in range(devices)])


def body(
    picture_embedding_matrix,
    caption_embedding_matrix,
    matching_target_entry,
    sharpness_factor,
    score_shift_array,
):
    row_count = picture_embedding_matrix.shape[0]
    beside_grp = shifted(caption_embedding_matrix, "grp", 1)
    moved = shifted(jnp.stack([caption_embedding_matrix, beside_grp], 0), "blk", 1)
    beside_blk = moved[0]
    corner = moved[1]
    already_seen = jnp.concatenate(
        [caption_embedding_matrix, beside_blk, beside_grp, corner], axis=0
    )
    sharpness_multiplier = sharpness_factor[0]
    shift_amount_term = score_shift_array[0]
    score_matrix = lax.dot_general(
        picture_embedding_matrix,
        already_seen,
        (((1,), (1,)), ((), ())),
        preferred_element_type=jnp.float32,
    )
    score_matrix = score_matrix * sharpness_multiplier + shift_amount_term
    column = lax.broadcasted_iota(jnp.int32, score_matrix.shape, 1)
    label = (column == matching_target_entry[0][:, None]).astype(jnp.float32)
    score_derivative = (jax.nn.sigmoid(score_matrix) - label).astype(jnp.bfloat16)
    image_grad = (
        sharpness_multiplier
        * jnp.dot(score_derivative, already_seen, preferred_element_type=jnp.float32)
    ).astype(jnp.bfloat16)
    running_subtotal = sharpness_multiplier * lax.dot_general(
        score_derivative,
        picture_embedding_matrix,
        (((0,), (0,)), ((), ())),
        preferred_element_type=jnp.float32,
    )
    own_part = running_subtotal[:row_count]
    part_blk = running_subtotal[row_count : 2 * row_count].astype(jnp.bfloat16)
    part_grp = running_subtotal[2 * row_count : 3 * row_count].astype(jnp.bfloat16)
    part_corner = running_subtotal[3 * row_count :].astype(jnp.bfloat16)
    returned = shifted(jnp.stack([part_blk, part_corner], 0), "blk", -1)
    middle = returned[1].astype(jnp.float32) + part_grp.astype(jnp.float32)
    arrived = shifted(middle, "grp", -1)
    total = own_part + returned[0].astype(jnp.float32) + arrived
    return (image_grad, total.astype(jnp.bfloat16))


def solution(mesh):
    in_specs = (P(("blk", "grp"), None), P(("blk", "grp"), None), P(("blk", "grp"), None), P(), P())
    out_specs = (P(("blk", "grp"), None), P(("blk", "grp"), None))
    return jax.shard_map(body, mesh=mesh, in_specs=in_specs, out_specs=out_specs, check_vma=False)
```

profile of v0, /device:TPU:0, one launch (start us, length us, event | category | flops | bytes accessed | tf_op | source)
XLA Modules:
  0.0 133.5 jit_solution(5240771897201071034)
XLA Ops:
  0.6 0.0 copy-start
  0.6 0.5 collective-permute-start
  1.1 13.7 %collective-permute-done = bf16[416,1152]{1,0:T(8,128)(2,1)S(1)} collective-permute-done((bf16[416,1152]{1,0:T(8,128)(2,1)}, bf16[416,1152]{1,0:T(8,128)(2,1)S(1)}, u32[]{:S(2)}, u32[]{:S(2)}) %collective-permute-start) | collective-permute-done | bytes 958496 | tf_op jit(solution)/shard_map/ppermute | solution.py:9
  14.8 1.4 %pad_maximum_fusion.1 = bf16[2,416,1152]{2,1,0:T(8,128)(2,1)S(1)} fusion(bf16[1,416,1152]{2,1,0:T(8,128)(2,1)S(1)} %bitcast.38, bf16[1,416,1152]{2,1,0:T(8,128)(2,1)} %bitcast.37), kind=kLoop, calls=%fused_computation.17 | loop fusion | flops 958464 | bytes 3833856 | tf_op jit(solution)/shard_map/stack | solution.py:21
  16.2 0.0 copy-start.1
  16.2 0.0 copy-start.2
  16.2 2.3 %collective-permute-start.1 = (bf16[2,416,1152]{2,1,0:T(8,128)(2,1)S(1)}, bf16[2,416,1152]{2,1,0:T(8,128)(2,1)S(1)}, u32[]{:S(2)}, u32[]{:S(2)}) collective-permute-start(bf16[2,416,1152]{2,1,0:T(8,128)(2,1)S(1)} %pad_maximum_fusion.1), channel_id=1, source_target_pairs={{0,4},{4,8},{8,12},{12,16},{16,20},{20,24},{24,28},{28,0},{1,5},{5... | collective-permute-start | bytes 5750792 | tf_op jit(solution)/shard_map/ppermute | solution.py:9
  19.9 42.9 %collective-permute-done.1 = bf16[2,416,1152]{2,1,0:T(8,128)(2,1)S(1)} collective-permute-done((bf16[2,416,1152]{2,1,0:T(8,128)(2,1)S(1)}, bf16[2,416,1152]{2,1,0:T(8,128)(2,1)S(1)}, u32[]{:S(2)}, u32[]{:S(2)}) %collective-permute-start.1) | collective-permute-done | bytes 1916960 | tf_op jit(solution)/shard_map/ppermute | solution.py:9
  62.8 0.1 slice_bitcast_fusion.5
  63.0 0.0 copy-done
  63.0 0.0 copy-done.1
  63.0 0.0 copy-done.2
  63.0 2.2 %fusion.7 = bf16[416,1664]{1,0:T(8,128)(2,1)S(1)} fusion(bf16[416,1152]{1,0:T(8,128)(2,1)S(1)} %copy-done, s32[416]{0:T(512)S(1)} %bitcast.39, f32[]{:T(128)} %bitcast.36, f32[]{:T(128)} %bitcast.34, bf16[416,1152]{1,0:T(8,128)(2,1)S(1)} %get-tuple-element.5, bf16[416,1152]{1,0:T(8,128)(2,1)S(1)} %collective-permute-done, ...), kind=kOutput, calls=%fused_computation.11 | convolution fusion | flops 1616449536 | bytes 6178440 | tf_op jit(solution)/shard_map/dot_general | solution.py:29
  65.2 2.4 %fusion.13 = (bf16[1664,1152]{1,0:T(8,128)(2,1)S(1)}, f32[1664,1152]{1,0:T(8,128)S(1)}) fusion(bf16[416,1664]{1,0:T(8,128)(2,1)S(1)} %fusion.7, bf16[416,1152]{1,0:T(8,128)(2,1)S(1)} %copy-done, f32[]{:T(128)} %bitcast.35), kind=kOutput, calls=%fused_computation.28 | convolution fusion | flops 1598717952 | bytes 13844484 | tf_op jit(solution)/shard_map/dot_general | solution.py:43
  67.6 0.1 slice_bitcast_fusion.3
  67.8 0.2 pad_maximum_fusion.2
  68.0 1.8 %collective-permute-start.2 = (bf16[2,416,1152]{2,1,0:T(8,128)(2,1)S(1)}, bf16[2,416,1152]{2,1,0:T(8,128)(2,1)S(1)}, u32[]{:S(2)}, u32[]{:S(2)}) collective-permute-start(bf16[2,416,1152]{2,1,0:T(8,128)(2,1)S(1)} %pad_maximum_fusion.2), channel_id=1, source_target_pairs={{0,28},{4,0},{8,4},{12,8},{16,12},{20,16},{24,20},{28,24},{1,29},{... | collective-permute-start | bytes 5750792 | tf_op jit(solution)/shard_map/ppermute | solution.py:9
  69.8 40.6 %collective-permute-done.2 = bf16[2,416,1152]{2,1,0:T(8,128)(2,1)S(1)} collective-permute-done((bf16[2,416,1152]{2,1,0:T(8,128)(2,1)S(1)}, bf16[2,416,1152]{2,1,0:T(8,128)(2,1)S(1)}, u32[]{:S(2)}, u32[]{:S(2)}) %collective-permute-start.2) | collective-permute-done | bytes 1916960 | tf_op jit(solution)/shard_map/ppermute | solution.py:9
  110.3 0.2 convert_add_fusion
  110.6 0.1 collective-permute-start.3
  110.6 3.5 %fusion.8 = bf16[416,1152]{1,0:T(8,128)(2,1)} fusion(bf16[416,1664]{1,0:T(8,128)(2,1)S(1)} %fusion.7, f32[]{:T(128)} %bitcast.33, bf16[416,1152]{1,0:T(8,128)(2,1)S(1)} %get-tuple-element.5, bf16[416,1152]{1,0:T(8,128)(2,1)S(1)} %collective-permute-done, bf16[416,1152]{1,0:T(8,128)(2,1)S(1)} %get-tuple-element.4, bf16[416,1152]{1,0:T(8,128)(2,1)S(1)} %copy-done.1), kind=kOutput, calls=%fused_computation.12 | convolution fusion | flops 1611177984 | bytes 6176772 | tf_op jit(solution)/shard_map/dot_general | solution.py:41
  114.1 18.1 %collective-permute-done.3 = f32[416,1152]{1,0:T(8,128)S(1)} collective-permute-done((f32[416,1152]{1,0:T(8,128)S(1)}, f32[416,1152]{1,0:T(8,128)S(1)}, u32[]{:S(2)}, u32[]{:S(2)}) %collective-permute-start.3) | collective-permute-done | bytes 1916960 | tf_op jit(solution)/shard_map/ppermute | solution.py:9
  132.3 1.2 fusion.10
Async XLA Ops:
  0.6 62.3 %copy-start = (bf16[416,1152]{1,0:T(8,128)(2,1)S(1)}, bf16[416,1152]{1,0:T(8,128)(2,1)}, u32[]{:S(2)}) copy-start(bf16[416,1152]{1,0:T(8,128)(2,1)} %param.5) | copy-start | bytes 2875396
  0.6 14.2 %collective-permute-start = (bf16[416,1152]{1,0:T(8,128)(2,1)}, bf16[416,1152]{1,0:T(8,128)(2,1)S(1)}, u32[]{:S(2)}, u32[]{:S(2)}) collective-permute-start(bf16[416,1152]{1,0:T(8,128)(2,1)} %param.6), channel_id=1, source_target_pairs={{0,1},{1,2},{2,3},{3,0},{4,5},{5,6},{6,7},{7,4},{8,9},{9,10},{10,1... | collective-permute-start | bytes 2875400 | tf_op jit(solution)/shard_map/ppermute | solution.py:9
  16.2 46.7 %copy-start.1 = (bf16[416,1152]{1,0:T(8,128)(2,1)S(1)}, bf16[416,1152]{1,0:T(8,128)(2,1)}, u32[]{:S(2)}) copy-start(bf16[416,1152]{1,0:T(8,128)(2,1)} %param.6) | copy-start | bytes 2875396
  16.2 46.7 %copy-start.2 = (s32[1,416]{1,0:T(1,128)S(1)}, s32[1,416]{1,0:T(1,128)}, u32[]{:S(2)}) copy-start(s32[1,416]{1,0:T(1,128)} %param.7) | copy-start | bytes 4996
  16.2 46.6 %collective-permute-start.1 = (bf16[2,416,1152]{2,1,0:T(8,128)(2,1)S(1)}, bf16[2,416,1152]{2,1,0:T(8,128)(2,1)S(1)}, u32[]{:S(2)}, u32[]{:S(2)}) collective-permute-start(bf16[2,416,1152]{2,1,0:T(8,128)(2,1)S(1)} %pad_maximum_fusion.1), channel_id=1, source_target_pairs={{0,4},{4,8},{8,12},{12,16},{16,20},{20,24},{24,28},{28,0},{1,5},{5... | collective-permute-start | bytes 5750792 | tf_op jit(solution)/shard_map/ppermute | solution.py:9
  68.0 42.4 %collective-permute-start.2 = (bf16[2,416,1152]{2,1,0:T(8,128)(2,1)S(1)}, bf16[2,416,1152]{2,1,0:T(8,128)(2,1)S(1)}, u32[]{:S(2)}, u32[]{:S(2)}) collective-permute-start(bf16[2,416,1152]{2,1,0:T(8,128)(2,1)S(1)} %pad_maximum_fusion.2), channel_id=1, source_target_pairs={{0,28},{4,0},{8,4},{12,8},{16,12},{20,16},{24,20},{28,24},{1,29},{... | collective-permute-start | bytes 5750792 | tf_op jit(solution)/shard_map/ppermute | solution.py:9
  110.6 21.7 %collective-permute-start.3 = (f32[416,1152]{1,0:T(8,128)S(1)}, f32[416,1152]{1,0:T(8,128)S(1)}, u32[]{:S(2)}, u32[]{:S(2)}) collective-permute-start(f32[416,1152]{1,0:T(8,128)S(1)} %convert_add_fusion), channel_id=1, source_target_pairs={{0,3},{1,0},{2,1},{3,2},{4,7},{5,4},{6,5},{7,6},{8,11},{9,8},{10,9... | collective-permute-start | bytes 5750792 | tf_op jit(solution)/shard_map/ppermute | solution.py:9
where the time goes:
time: 134 us; the launch traced here: 133 us
  waiting for transfers between devices  115 us (86%)
  matrix products  8.09 us (6%)
  starting transfers between devices  4.69 us (4%)
  other arithmetic  3.07 us (2%)
  between operations  2.03 us (2%)
    ppermute x4, waiting for transfers between devices, shifted(): lax.ppermute(shard, axis, [(i, (i + by) % devices) for i in range(devices)])  115 us
    ppermute x4, starting transfers between devices, shifted(): lax.ppermute(shard, axis, [(i, (i + by) % devices) for i in range(devices)])  4.69 us
    dot_general x1, matrix products, body(): jnp.dot(score_derivative, already_seen, preferred_element_type=jnp.float32)  3.48 us
  transfers between devices with their start and end apart: 4, of which 4 were waited for; matrix products, arithmetic and copies ran while one was open for 3% of the time, Pallas kernels for 0%

commit v1 on v0

v1 whole, which is shorter than its diff:
```python
import jax
import jax.numpy as jnp
from jax import lax
from jax.sharding import PartitionSpec as P


def shifted(shard, axis, by):
    devices = lax.axis_size(axis)
    return lax.ppermute(shard, axis, [(i, (i + by) % devices) for i in range(devices)])


def dot_nt(a, b):
    return lax.dot_general(a, b, (((1,), (1,)), ((), ())), preferred_element_type=jnp.float32)


def dot_tn(a, b):
    return lax.dot_general(a, b, (((0,), (0,)), ((), ())), preferred_element_type=jnp.float32)


def dot_nn(a, b):
    return jnp.dot(a, b, preferred_element_type=jnp.float32)


def body(image, text, target, factor, shift):
    scale = factor[0]
    bias = shift[0]
    text_prev = shifted(text, "blk", 1)
    image_next = shifted(image, "grp", -1)

    own = jax.nn.sigmoid(dot_nt(image, text) * scale + bias)
    column = lax.broadcasted_iota(jnp.int32, own.shape, 1)
    own = (own - (column == target[0][:, None]).astype(jnp.float32)).astype(jnp.bfloat16)

    def derivative(a, b):
        return jax.nn.sigmoid(dot_nt(a, b) * scale + bias).astype(jnp.bfloat16)

    next_own = derivative(image_next, text)
    own_prev = derivative(image, text_prev)
    next_prev = derivative(image_next, text_prev)

    text_sent = scale * (dot_tn(own_prev, image) + dot_tn(next_prev, image_next))
    text_back = shifted(text_sent.astype(jnp.bfloat16), "blk", -1)
    image_sent = scale * (dot_nn(next_own, text) + dot_nn(next_prev, text_prev))
    image_back = shifted(image_sent.astype(jnp.bfloat16), "grp", 1)

    image_grad = scale * (dot_nn(own, text) + dot_nn(own_prev, text_prev))
    text_grad = scale * (dot_tn(own, image) + dot_tn(next_own, image_next))
    image_grad = (image_grad + image_back.astype(jnp.float32)).astype(jnp.bfloat16)
    text_grad = (text_grad + text_back.astype(jnp.float32)).astype(jnp.bfloat16)
    return image_grad, text_grad


def solution(mesh):
    block = P(("blk", "grp"), None)
    return jax.shard_map(
        body, mesh=mesh, in_specs=(block, block, block, P(), P()), out_specs=(block, block), check_vma=False
    )
```

time: 134 us -> 57.4 us (0.43)
  waiting for transfers between devices: 115 us -> 36.9 us
  matrix products: 8.09 us -> 12.8 us
  other arithmetic: 3.07 us -> 0 us
    ppermute x4, waiting for transfers between devices: 115 us -> 36.9 us  [shifted(): lax.ppermute(shard, axis, [(i, (i + by) % devices) for i in range(devices)])]
    dot_general x3 -> x12, matrix products: 8.09 us -> 12.8 us  [the longest x4 4.95 us: dot_nt(): lax.dot_general(a, b, (((1,), (1,)), ((), ())), preferred_element_type=jn...]
    another operation x2 -> x0, other arithmetic: 1.58 us -> none  [the longest x1 1.39 us: body(): jnp.stack([caption_embedding_matrix, beside_grp], 0)]
  transfers between devices with their start and end apart: 4 -> 4, of which waited for: 4 -> 2; matrix products, arithmetic and copies ran while one was open for 3% -> 17% of each run, Pallas kernels for 0% -> 0%
where the time goes in v1:
time: 57.4 us; the launch traced here: 57.3 us
  waiting for transfers between devices  36.9 us (64%)
  matrix products  12.8 us (22%)
  starting transfers between devices  5.52 us (10%)
  between operations  2.03 us (4%)
    ppermute x4, waiting for transfers between devices, shifted(): lax.ppermute(shard, axis, [(i, (i + by) % devices) for i in range(devices)])  36.9 us
    ppermute x4, starting transfers between devices, shifted(): lax.ppermute(shard, axis, [(i, (i + by) % devices) for i in range(devices)])  5.52 us
    dot_general x4, matrix products, dot_nt(): lax.dot_general(a, b, (((1,), (1,)), ((), ())), preferred_element_type=jn...  4.95 us
    dot_general x4, matrix products, dot_tn(): lax.dot_general(a, b, (((0,), (0,)), ((), ())), preferred_element_type=jn...  3.99 us
    dot_general x4, matrix products, dot_nn(): return jnp.dot(a, b, preferred_element_type=jnp.float32)  3.83 us
  transfers between devices with their start and end apart: 4, of which 2 were waited for; matrix products, arithmetic and copies ran while one was open for 17% of the time, Pallas kernels for 0%

profile of v1, /device:TPU:0, one launch (start us, length us, event | category | flops | bytes accessed | tf_op | source)
XLA Modules:
  0.0 57.3 jit_solution(15150561114044164523)
XLA Ops:
  0.6 3.0 %collective-permute-start = (bf16[416,1152]{1,0:T(8,128)(2,1)}, bf16[416,1152]{1,0:T(8,128)(2,1)S(1)}, u32[]{:S(2)}, u32[]{:S(2)}) collective-permute-start(bf16[416,1152]{1,0:T(8,128)(2,1)} %param.6), channel_id=1, source_target_pairs={{0,4},{4,8},{8,12},{12,16},{16,20},{20,24},{24,28},{28,0},{1,5},{5... | collective-permute-start | bytes 2875400 | tf_op jit(solution)/shard_map/ppermute | solution.py:9
  3.6 0.7 %collective-permute-start.1 = (bf16[416,1152]{1,0:T(8,128)(2,1)}, bf16[416,1152]{1,0:T(8,128)(2,1)S(1)}, u32[]{:S(2)}, u32[]{:S(2)}) collective-permute-start(bf16[416,1152]{1,0:T(8,128)(2,1)} %param.5), channel_id=1, source_target_pairs={{0,3},{1,0},{2,1},{3,2},{4,7},{5,4},{6,5},{7,6},{8,11},{9,8},{10,9... | collective-permute-start | bytes 2875400 | tf_op jit(solution)/shard_map/ppermute | solution.py:9
  5.6 0.0 copy-start
  5.6 2.4 %fusion.34 = bf16[416,416]{1,0:T(8,128)(2,1)S(1)} fusion(bf16[416,1152]{1,0:T(8,128)(2,1)} %param.5, bf16[416,1152]{1,0:T(8,128)(2,1)} %param.6, s32[416]{0:T(512)} %bitcast.39, f32[]{:T(128)} %bitcast.35, f32[]{:T(128)} %bitcast.28), kind=kOutput, calls=%fused_computation.42 | convolution fusion | flops 400278528 | bytes 2264712 | tf_op jit(solution)/shard_map/dot_general | solution.py:13
  8.1 20.0 %collective-permute-done = bf16[416,1152]{1,0:T(8,128)(2,1)S(1)} collective-permute-done((bf16[416,1152]{1,0:T(8,128)(2,1)}, bf16[416,1152]{1,0:T(8,128)(2,1)S(1)}, u32[]{:S(2)}, u32[]{:S(2)}) %collective-permute-start) | collective-permute-done | bytes 958496 | tf_op jit(solution)/shard_map/ppermute | solution.py:9
  28.1 0.0 copy-done
  28.1 0.8 %fusion.31 = bf16[416,416]{1,0:T(8,128)(2,1)S(1)} fusion(bf16[416,1152]{1,0:T(8,128)(2,1)S(1)} %copy-done, bf16[416,1152]{1,0:T(8,128)(2,1)S(1)} %collective-permute-done, f32[]{:T(128)} %bitcast.38, f32[]{:T(128)} %bitcast.34), kind=kOutput, calls=%fused_computation.39 | convolution fusion | flops 399759360 | bytes 2263048 | tf_op jit(solution)/shard_map/dot_general | solution.py:13
  28.9 0.7 %fusion.38 = f32[416,1152]{1,0:T(8,128)S(1)} fusion(bf16[416,416]{1,0:T(8,128)(2,1)S(1)} %fusion.31, bf16[416,1152]{1,0:T(8,128)(2,1)S(1)} %copy-done), kind=kOutput, calls=%fused_computation.47 | convolution fusion | flops 398721024 | bytes 3221504 | tf_op jit(solution)/shard_map/dot_general | solution.py:17
  29.7 0.0 collective-permute-done.1
  29.7 0.8 %fusion.33 = bf16[416,416]{1,0:T(8,128)(2,1)S(1)} fusion(bf16[416,1152]{1,0:T(8,128)(2,1)S(1)} %collective-permute-done.1, bf16[416,1152]{1,0:T(8,128)(2,1)S(1)} %collective-permute-done, f32[]{:T(128)} %bitcast.36, f32[]{:T(128)} %bitcast.32), kind=kOutput, calls=%fused_computation.41 | convolution fusion | flops 399759360 | bytes 2263048 | tf_op jit(solution)/shard_map/dot_general | solution.py:13
  30.5 0.0 copy-start.1
  30.6 0.8 %fusion.9 = bf16[416,1152]{1,0:T(8,128)(2,1)S(1)} fusion(f32[416,1152]{1,0:T(8,128)S(1)} %fusion.38, bf16[416,416]{1,0:T(8,128)(2,1)S(1)} %fusion.33, bf16[416,1152]{1,0:T(8,128)(2,1)S(1)} %collective-permute-done.1, f32[]{:T(128)} %bitcast.29), kind=kOutput, calls=%fused_computation.13 | convolution fusion | flops 400158720 | bytes 4179972 | tf_op jit(solution)/shard_map/dot_general | solution.py:17
  31.3 1.8 %collective-permute-start.3 = (bf16[416,1152]{1,0:T(8,128)(2,1)S(1)}, bf16[416,1152]{1,0:T(8,128)(2,1)S(1)}, u32[]{:S(2)}, u32[]{:S(2)}) collective-permute-start(bf16[416,1152]{1,0:T(8,128)(2,1)S(1)} %fusion.9), channel_id=1, source_target_pairs={{0,28},{4,0},{8,4},{12,8},{16,12},{20,16},{24,20},{28,24},{1,29},{... | collective-permute-start | bytes 2875400 | tf_op jit(solution)/shard_map/ppermute | solution.py:9
  33.1 0.0 copy-done.1
  33.1 0.8 %fusion.32 = bf16[416,416]{1,0:T(8,128)(2,1)S(1)} fusion(bf16[416,1152]{1,0:T(8,128)(2,1)S(1)} %collective-permute-done.1, bf16[416,1152]{1,0:T(8,128)(2,1)S(1)} %copy-done.1, f32[]{:T(128)} %bitcast.37, f32[]{:T(128)} %bitcast.33), kind=kOutput, calls=%fused_computation.40 | convolution fusion | flops 399759360 | bytes 2263048 | tf_op jit(solution)/shard_map/dot_general | solution.py:13
  34.0 0.7 %fusion.36 = f32[416,1152]{1,0:T(8,128)S(1)} fusion(bf16[416,416]{1,0:T(8,128)(2,1)S(1)} %fusion.32, bf16[416,1152]{1,0:T(8,128)(2,1)S(1)} %copy-done.1), kind=kOutput, calls=%fused_computation.45 | convolution fusion | flops 398721024 | bytes 3221504 | tf_op jit(solution)/shard_map/dot_general | solution.py:21
  34.7 0.7 %fusion.8 = bf16[416,1152]{1,0:T(8,128)(2,1)S(1)} fusion(f32[416,1152]{1,0:T(8,128)S(1)} %fusion.36, bf16[416,416]{1,0:T(8,128)(2,1)S(1)} %fusion.33, bf16[416,1152]{1,0:T(8,128)(2,1)S(1)} %collective-permute-done, f32[]{:T(128)} %bitcast.31), kind=kOutput, calls=%fused_computation.12 | convolution fusion | flops 400158720 | bytes 4179972 | tf_op jit(solution)/shard_map/dot_general | solution.py:21
  35.4 0.1 collective-permute-start.2
  35.4 0.7 %fusion.37 = f32[416,1152]{1,0:T(8,128)S(1)} fusion(bf16[416,416]{1,0:T(8,128)(2,1)S(1)} %fusion.34, bf16[416,1152]{1,0:T(8,128)(2,1)S(1)} %copy-done), kind=kOutput, calls=%fused_computation.46 | convolution fusion | flops 398721024 | bytes 3221504 | tf_op jit(solution)/shard_map/dot_general | solution.py:17
  36.2 0.7 %fusion.35 = f32[416,1152]{1,0:T(8,128)S(1)} fusion(bf16[416,416]{1,0:T(8,128)(2,1)S(1)} %fusion.34, bf16[416,1152]{1,0:T(8,128)(2,1)S(1)} %copy-done.1), kind=kOutput, calls=%fused_computation.44 | convolution fusion | flops 398721024 | bytes 3221504 | tf_op jit(solution)/shard_map/dot_general | solution.py:21
  36.9 16.9 %collective-permute-done.3 = bf16[416,1152]{1,0:T(8,128)(2,1)S(1)} collective-permute-done((bf16[416,1152]{1,0:T(8,128)(2,1)S(1)}, bf16[416,1152]{1,0:T(8,128)(2,1)S(1)}, u32[]{:S(2)}, u32[]{:S(2)}) %collective-permute-start.3) | collective-permute-done | bytes 958496 | tf_op jit(solution)/shard_map/ppermute | solution.py:9
  53.8 1.8 %fusion.6 = bf16[416,1152]{1,0:T(8,128)(2,1)} fusion(f32[416,1152]{1,0:T(8,128)S(1)} %fusion.37, bf16[416,416]{1,0:T(8,128)(2,1)S(1)} %fusion.32, bf16[416,1152]{1,0:T(8,128)(2,1)S(1)} %collective-permute-done.1, bf16[416,1152]{1,0:T(8,128)(2,1)S(1)} %collective-permute-done.3, f32[]{:T(128)} %bitcast.30), kind=kOutput, calls=%fused_computation.10 | convolution fusion | flops 401117184 | bytes 5138436 | tf_op jit(solution)/shard_map/dot_general | solution.py:17
  55.5 0.0 collective-permute-done.2
  55.5 1.7 %fusion.7 = bf16[416,1152]{1,0:T(8,128)(2,1)} fusion(f32[416,1152]{1,0:T(8,128)S(1)} %fusion.35, bf16[416,416]{1,0:T(8,128)(2,1)S(1)} %fusion.31, bf16[416,1152]{1,0:T(8,128)(2,1)S(1)} %collective-permute-done, bf16[416,1152]{1,0:T(8,128)(2,1)S(1)} %collective-permute-done.2, f32[]{:T(128)} %bitcast.27), kind=kOutput, calls=%fused_computation.11 | convolution fusion | flops 401117184 | bytes 5138436 | tf_op jit(solution)/shard_map/dot_general | solution.py:21
Async XLA Ops:
  0.6 27.5 %collective-permute-start = (bf16[416,1152]{1,0:T(8,128)(2,1)}, bf16[416,1152]{1,0:T(8,128)(2,1)S(1)}, u32[]{:S(2)}, u32[]{:S(2)}) collective-permute-start(bf16[416,1152]{1,0:T(8,128)(2,1)} %param.6), channel_id=1, source_target_pairs={{0,4},{4,8},{8,12},{12,16},{16,20},{20,24},{24,28},{28,0},{1,5},{5... | collective-permute-start | bytes 2875400 | tf_op jit(solution)/shard_map/ppermute | solution.py:9
  3.6 26.1 %collective-permute-start.1 = (bf16[416,1152]{1,0:T(8,128)(2,1)}, bf16[416,1152]{1,0:T(8,128)(2,1)S(1)}, u32[]{:S(2)}, u32[]{:S(2)}) collective-permute-start(bf16[416,1152]{1,0:T(8,128)(2,1)} %param.5), channel_id=1, source_target_pairs={{0,3},{1,0},{2,1},{3,2},{4,7},{5,4},{6,5},{7,6},{8,11},{9,8},{10,9... | collective-permute-start | bytes 2875400 | tf_op jit(solution)/shard_map/ppermute | solution.py:9
  5.6 22.5 %copy-start = (bf16[416,1152]{1,0:T(8,128)(2,1)S(1)}, bf16[416,1152]{1,0:T(8,128)(2,1)}, u32[]{:S(2)}) copy-start(bf16[416,1152]{1,0:T(8,128)(2,1)} %param.5) | copy-start | bytes 2875396
  30.5 2.6 %copy-start.1 = (bf16[416,1152]{1,0:T(8,128)(2,1)S(1)}, bf16[416,1152]{1,0:T(8,128)(2,1)}, u32[]{:S(2)}) copy-start(bf16[416,1152]{1,0:T(8,128)(2,1)} %param.6) | copy-start | bytes 2875396
  31.3 22.5 %collective-permute-start.3 = (bf16[416,1152]{1,0:T(8,128)(2,1)S(1)}, bf16[416,1152]{1,0:T(8,128)(2,1)S(1)}, u32[]{:S(2)}, u32[]{:S(2)}) collective-permute-start(bf16[416,1152]{1,0:T(8,128)(2,1)S(1)} %fusion.9), channel_id=1, source_target_pairs={{0,28},{4,0},{8,4},{12,8},{16,12},{20,16},{24,20},{28,24},{1,29},{... | collective-permute-start | bytes 2875400 | tf_op jit(solution)/shard_map/ppermute | solution.py:9
  35.4 20.2 %collective-permute-start.2 = (bf16[416,1152]{1,0:T(8,128)(2,1)S(1)}, bf16[416,1152]{1,0:T(8,128)(2,1)S(1)}, u32[]{:S(2)}, u32[]{:S(2)}) collective-permute-start(bf16[416,1152]{1,0:T(8,128)(2,1)S(1)} %fusion.8), channel_id=1, source_target_pairs={{0,1},{1,2},{2,3},{3,0},{4,5},{5,6},{6,7},{7,4},{8,9},{9,10},{10,1... | collective-permute-start | bytes 2875400 | tf_op jit(solution)/shard_map/ppermute | solution.py:9

commit v2 on v1

v2 whole, which is shorter than its diff:
```python
import jax
import jax.numpy as jnp
from jax import lax
from jax.sharding import PartitionSpec as P

CHUNKS = 2


def shifted(shard, axis, by):
    devices = lax.axis_size(axis)
    return lax.ppermute(shard, axis, [(i, (i + by) % devices) for i in range(devices)])


def dot_nt(a, b):
    return lax.dot_general(a, b, (((1,), (1,)), ((), ())), preferred_element_type=jnp.float32)


def dot_tn(a, b):
    return lax.dot_general(a, b, (((0,), (0,)), ((), ())), preferred_element_type=jnp.float32)


def dot_nn(a, b):
    return jnp.dot(a, b, preferred_element_type=jnp.float32)


def row_cuts(rows):
    tiles = rows // 16
    cuts = [tiles * i // CHUNKS * 16 for i in range(CHUNKS)] + [rows]
    return list(zip(cuts[:-1], cuts[1:]))


def body(image, text, target, factor, shift):
    scale = factor[0]
    bias = shift[0]
    cuts = row_cuts(text.shape[0])
    text_prev = [shifted(text[lo:hi], "blk", 1) for lo, hi in cuts]
    image_next = shifted(image, "grp", -1)

    own = jax.nn.sigmoid(dot_nt(image, text) * scale + bias)
    column = lax.broadcasted_iota(jnp.int32, own.shape, 1)
    own = (own - (column == target[0][:, None]).astype(jnp.float32)).astype(jnp.bfloat16)

    def derivative(a, b):
        return jax.nn.sigmoid(dot_nt(a, b) * scale + bias).astype(jnp.bfloat16)

    image_grad = dot_nn(own, text)
    text_grad = dot_tn(own, image)

    next_own = derivative(image_next, text)
    image_sent = dot_nn(next_own, text)
    text_grad = scale * (text_grad + dot_tn(next_own, image_next))

    text_back = []
    for part in text_prev:
        own_prev = derivative(image, part)
        next_prev = derivative(image_next, part)
        text_sent = scale * (dot_tn(own_prev, image) + dot_tn(next_prev, image_next))
        text_back.append(shifted(text_sent.astype(jnp.bfloat16), "blk", -1))
        image_sent = image_sent + dot_nn(next_prev, part)
        image_grad = image_grad + dot_nn(own_prev, part)

    image_back = shifted((scale * image_sent).astype(jnp.bfloat16), "grp", 1)
    image_grad, text_grad = lax.optimization_barrier((scale * image_grad, text_grad))
    text_back = jnp.concatenate(text_back, axis=0)
    image_grad = (image_grad + image_back.astype(jnp.float32)).astype(jnp.bfloat16)
    text_grad = (text_grad + text_back.astype(jnp.float32)).astype(jnp.bfloat16)
    return image_grad, text_grad


def solution(mesh):
    block = P(("blk", "grp"), None)
    return jax.shard_map(
        body, mesh=mesh, in_specs=(block, block, block, P(), P()), out_specs=(block, block), check_vma=False
    )
```

time: 57.4 us -> 57.1 us (level)
  waiting for transfers between devices: 36.9 us -> 32.6 us
  starting transfers between devices: 5.52 us -> 8.27 us
  matrix products: 12.8 us -> 10.3 us
  other arithmetic: 0 us -> 2.32 us
  local copies, waits for them, and re-layouts: 0.01 us -> 1.39 us
    ppermute x4 -> x6, waiting for transfers between devices: 36.9 us -> 32.6 us  [shifted(): lax.ppermute(shard, axis, [(i, (i + by) % devices) for i in range(devices)])]
    ppermute x4 -> x6, starting transfers between devices: 5.52 us -> 8.27 us  [shifted(): lax.ppermute(shard, axis, [(i, (i + by) % devices) for i in range(devices)])]
    convert_element_type x0 -> x2, other arithmetic: none -> 2.32 us  [the longest x1 1.17 us: body(): (image_grad + image_back.astype(jnp.float32)).astype(jnp.bfloat16)]
    slice x0 -> x1, local copies, waits for them, and re-layouts: none -> 1.38 us  [body(): text_prev = [shifted(text[lo:hi], 'blk', 1) for lo, hi in cuts]]
    dot_general x4 -> x6, matrix products: 4.95 us -> 3.64 us  [dot_nt(): lax.dot_general(a, b, (((1,), (1,)), ((), ())), preferred_element_type=jn...]
    dot_general x4 -> x6, matrix products: 3.83 us -> 3.21 us  [dot_nn(): return jnp.dot(a, b, preferred_element_type=jnp.float32)]
    dot_general x4 -> x6, matrix products: 3.99 us -> 3.43 us  [dot_tn(): lax.dot_general(a, b, (((0,), (0,)), ((), ())), preferred_element_type=jn...]
  transfers between devices with their start and end apart: 4 -> 6, of which waited for: 2 -> 4; matrix products, arithmetic and copies ran while one was open for 17% -> 18% of each run, Pallas kernels for 0% -> 0%
where the time goes in v2:
time: 57.1 us; the launch traced here: 57 us
  waiting for transfers between devices  32.6 us (57%)
  matrix products  10.3 us (18%)
  starting transfers between devices  8.27 us (14%)
  other arithmetic  2.32 us (4%)
  between operations  2.11 us (4%)
  local copies, waits for them, and re-layouts  1.39 us (2%)
    ppermute x6, waiting for transfers between devices, shifted(): lax.ppermute(shard, axis, [(i, (i + by) % devices) for i in range(devices)])  32.6 us
    ppermute x6, starting transfers between devices, shifted(): lax.ppermute(shard, axis, [(i, (i + by) % devices) for i in range(devices)])  8.27 us
    dot_general x6, matrix products, dot_nt(): lax.dot_general(a, b, (((1,), (1,)), ((), ())), preferred_element_type=jn...  3.64 us
    dot_general x6, matrix products, dot_tn(): lax.dot_general(a, b, (((0,), (0,)), ((), ())), preferred_element_type=jn...  3.43 us
    dot_general x6, matrix products, dot_nn(): return jnp.dot(a, b, preferred_element_type=jnp.float32)  3.21 us
    slice x1, local copies, waits for them, and re-layouts, body(): text_prev = [shifted(text[lo:hi], 'blk', 1) for lo, hi in cuts]  1.38 us
    convert_element_type x1, other arithmetic, body(): (image_grad + image_back.astype(jnp.float32)).astype(jnp.bfloat16)  1.17 us
    convert_element_type x1, other arithmetic, body(): text_grad = (text_grad + text_back.astype(jnp.float32)).astype(jnp.bfloat16)  1.15 us
  transfers between devices with their start and end apart: 6, of which 4 were waited for; matrix products, arithmetic and copies ran while one was open for 18% of the time, Pallas kernels for 0%

profile of v2, /device:TPU:0, one launch (start us, length us, event | category | flops | bytes accessed | tf_op | source)
XLA Modules:
  0.0 57.0 jit_solution(13470238365308068097)
XLA Ops:
  0.7 1.4 %fusion.45 = (bf16[208,1152]{1,0:T(8,128)(2,1)S(1)}, bf16[208,1152]{1,0:T(8,128)(2,1)S(1)}) fusion(bf16[416,1152]{1,0:T(8,128)(2,1)} %param.6), kind=kLoop, calls=%fused_computation.61 | loop fusion | bytes 1916928 | tf_op jit(solution)/shard_map/slice | solution.py:36
  2.0 3.0 %collective-permute-start.1 = (bf16[208,1152]{1,0:T(8,128)(2,1)S(1)}, bf16[208,1152]{1,0:T(8,128)(2,1)S(1)}, u32[]{:S(2)}, u32[]{:S(2)}) collective-permute-start(bf16[208,1152]{1,0:T(8,128)(2,1)S(1)} %get-tuple-element.6), channel_id=1, source_target_pairs={{0,4},{4,8},{8,12},{12,16},{16,20},{20,24},{24,28},{28,0},{1,5},{5... | collective-permute-start | bytes 1437704 | tf_op jit(solution)/shard_map/ppermute | solution.py:11
  5.0 1.5 %collective-permute-start = (bf16[208,1152]{1,0:T(8,128)(2,1)S(1)}, bf16[208,1152]{1,0:T(8,128)(2,1)S(1)}, u32[]{:S(2)}, u32[]{:S(2)}) collective-permute-start(bf16[208,1152]{1,0:T(8,128)(2,1)S(1)} %get-tuple-element.7), channel_id=1, source_target_pairs={{0,4},{4,8},{8,12},{12,16},{16,20},{20,24},{24,28},{28,0},{1,5},{5... | collective-permute-start | bytes 1437704 | tf_op jit(solution)/shard_map/ppermute | solution.py:11
  6.6 0.4 collective-permute-start.2
  8.3 0.9 %fusion.20 = bf16[416,416]{1,0:T(8,128)(2,1)S(1)} fusion(bf16[416,1152]{1,0:T(8,128)(2,1)S(1)} %copy-done.1, bf16[416,1152]{1,0:T(8,128)(2,1)S(1)} %copy-done, s32[416]{0:T(512)S(1)} %bitcast.56, f32[]{:T(128)} %bitcast.50, f32[]{:T(128)} %bitcast.40), kind=kOutput, calls=%fused_computation.31 | convolution fusion | flops 400278528 | bytes 2264712 | tf_op jit(solution)/shard_map/dot_general | solution.py:15
  9.2 0.8 %fusion.47 = f32[416,1152]{1,0:T(8,128)S(1)} fusion(bf16[416,416]{1,0:T(8,128)(2,1)S(1)} %fusion.20, bf16[416,1152]{1,0:T(8,128)(2,1)S(1)} %copy-done.1), kind=kOutput, calls=%fused_computation.63 | convolution fusion | flops 398721024 | bytes 3221504 | tf_op jit(solution)/shard_map/dot_general | solution.py:19
  10.0 0.7 %fusion.46 = f32[416,1152]{1,0:T(8,128)S(1)} fusion(bf16[416,416]{1,0:T(8,128)(2,1)S(1)} %fusion.20, bf16[416,1152]{1,0:T(8,128)(2,1)S(1)} %copy-done), kind=kOutput, calls=%fused_computation.62 | convolution fusion | flops 398721024 | bytes 3221504 | tf_op jit(solution)/shard_map/dot_general | solution.py:23
  10.7 9.2 %collective-permute-done.1 = bf16[208,1152]{1,0:T(8,128)(2,1)S(1)} collective-permute-done((bf16[208,1152]{1,0:T(8,128)(2,1)S(1)}, bf16[208,1152]{1,0:T(8,128)(2,1)S(1)}, u32[]{:S(2)}, u32[]{:S(2)}) %collective-permute-start.1) | collective-permute-done | bytes 479264 | tf_op jit(solution)/shard_map/ppermute | solution.py:11
  19.9 0.5 fusion.42
  20.3 9.0 %collective-permute-done = bf16[208,1152]{1,0:T(8,128)(2,1)S(1)} collective-permute-done((bf16[208,1152]{1,0:T(8,128)(2,1)S(1)}, bf16[208,1152]{1,0:T(8,128)(2,1)S(1)}, u32[]{:S(2)}, u32[]{:S(2)}) %collective-permute-start) | collective-permute-done | bytes 479264 | tf_op jit(solution)/shard_map/ppermute | solution.py:11
  29.3 0.5 fusion.41
  29.8 0.5 fusion.49
  30.3 0.5 fusion.50
  30.7 0.4 convolution_add_fusion.3
  31.2 0.0 collective-permute-done.2
  31.2 0.5 fusion.43
  31.7 0.5 fusion.7
  32.2 1.8 %collective-permute-start.4 = (bf16[208,1152]{1,0:T(8,128)(2,1)S(1)}, bf16[208,1152]{1,0:T(8,128)(2,1)S(1)}, u32[]{:S(2)}, u32[]{:S(2)}) collective-permute-start(bf16[208,1152]{1,0:T(8,128)(2,1)S(1)} %fusion.7), channel_id=1, source_target_pairs={{0,28},{4,0},{8,4},{12,8},{16,12},{20,16},{24,20},{28,24},{1,29},{... | collective-permute-start | bytes 1437704 | tf_op jit(solution)/shard_map/ppermute | solution.py:11
  34.0 0.5 fusion.44
  34.4 0.5 fusion.6
  34.9 1.5 %collective-permute-start.5 = (bf16[208,1152]{1,0:T(8,128)(2,1)S(1)}, bf16[208,1152]{1,0:T(8,128)(2,1)S(1)}, u32[]{:S(2)}, u32[]{:S(2)}) collective-permute-start(bf16[208,1152]{1,0:T(8,128)(2,1)S(1)} %fusion.6), channel_id=1, source_target_pairs={{0,28},{4,0},{8,4},{12,8},{16,12},{20,16},{24,20},{28,24},{1,29},{... | collective-permute-start | bytes 1437704 | tf_op jit(solution)/shard_map/ppermute | solution.py:11
  36.4 0.8 %fusion.19 = bf16[416,416]{1,0:T(8,128)(2,1)S(1)} fusion(bf16[416,1152]{1,0:T(8,128)(2,1)S(1)} %collective-permute-done.2, bf16[416,1152]{1,0:T(8,128)(2,1)S(1)} %copy-done, f32[]{:T(128)} %bitcast.52, f32[]{:T(128)} %bitcast.46), kind=kOutput, calls=%fused_computation.30 | convolution fusion | flops 399759360 | bytes 2263048 | tf_op jit(solution)/shard_map/dot_general | solution.py:15
  37.3 0.7 %fusion.48 = f32[416,1152]{1,0:T(8,128)S(1)} fusion(bf16[416,416]{1,0:T(8,128)(2,1)S(1)} %fusion.19, bf16[416,1152]{1,0:T(8,128)(2,1)S(1)} %copy-done), kind=kOutput, calls=%fused_computation.64 | convolution fusion | flops 398721024 | bytes 3221504 | tf_op jit(solution)/shard_map/dot_general | solution.py:23
  38.0 0.4 convolution_add_fusion.1
  38.4 0.4 fusion.3
  38.9 0.1 collective-permute-start.3
  38.9 0.5 fusion.1
  39.4 0.8 %fusion = f32[416,1152]{1,0:T(8,128)S(1)} fusion(f32[416,1152]{1,0:T(8,128)S(1)} %fusion.47, bf16[416,416]{1,0:T(8,128)(2,1)S(1)} %fusion.19, bf16[416,1152]{1,0:T(8,128)(2,1)S(1)} %collective-permute-done.2, f32[]{:T(128)} %bitcast.44), kind=kOutput, calls=%fused_computation.5 | convolution fusion | flops 399679488 | bytes 5138436 | tf_op jit(solution)/shard_map/dot_general | solution.py:19
  40.2 5.9 %collective-permute-done.4 = bf16[208,1152]{1,0:T(8,128)(2,1)S(1)} collective-permute-done((bf16[208,1152]{1,0:T(8,128)(2,1)S(1)}, bf16[208,1152]{1,0:T(8,128)(2,1)S(1)}, u32[]{:S(2)}, u32[]{:S(2)}) %collective-permute-start.4) | collective-permute-done | bytes 479264 | tf_op jit(solution)/shard_map/ppermute | solution.py:11
  46.1 8.5 %collective-permute-done.5 = bf16[208,1152]{1,0:T(8,128)(2,1)S(1)} collective-permute-done((bf16[208,1152]{1,0:T(8,128)(2,1)S(1)}, bf16[208,1152]{1,0:T(8,128)(2,1)S(1)}, u32[]{:S(2)}, u32[]{:S(2)}) %collective-permute-start.5) | collective-permute-done | bytes 479264 | tf_op jit(solution)/shard_map/ppermute | solution.py:11
  54.6 1.2 %add_convert_fusion = bf16[416,1152]{1,0:T(8,128)(2,1)} fusion(f32[416,1152]{1,0:T(8,128)S(1)} %fusion, bf16[208,1152]{1,0:T(8,128)(2,1)S(1)} %collective-permute-done.5, bf16[208,1152]{1,0:T(8,128)(2,1)S(1)} %collective-permute-done.4), kind=kLoop, calls=%fused_computation.15 | loop fusion | flops 2875392 | bytes 3833856 | tf_op jit(solution)/shard_map/convert_element_type | solution.py:66
  55.8 1.2 %add_convert_fusion.1 = bf16[416,1152]{1,0:T(8,128)(2,1)} fusion(f32[416,1152]{1,0:T(8,128)S(1)} %fusion.1, bf16[416,1152]{1,0:T(8,128)(2,1)S(1)} %collective-permute-done.3), kind=kLoop, calls=%fused_computation.16 | loop fusion | flops 1437696 | bytes 3833856 | tf_op jit(solution)/shard_map/convert_element_type | solution.py:65
  (7 shorter events, 0.0 us)
Async XLA Ops:
  0.6 7.7 %copy-start = (bf16[416,1152]{1,0:T(8,128)(2,1)S(1)}, bf16[416,1152]{1,0:T(8,128)(2,1)}, u32[]{:S(2)}) copy-start(bf16[416,1152]{1,0:T(8,128)(2,1)} %param.6) | copy-start | bytes 2875396
  0.6 5.9 %copy-start.1 = (bf16[416,1152]{1,0:T(8,128)(2,1)S(1)}, bf16[416,1152]{1,0:T(8,128)(2,1)}, u32[]{:S(2)}) copy-start(bf16[416,1152]{1,0:T(8,128)(2,1)} %param.5) | copy-start | bytes 2875396
  0.6 7.6 %copy-start.2 = (s32[1,416]{1,0:T(1,128)S(1)}, s32[1,416]{1,0:T(1,128)}, u32[]{:S(2)}) copy-start(s32[1,416]{1,0:T(1,128)} %param.7) | copy-start | bytes 4996
  2.0 17.8 %collective-permute-start.1 = (bf16[208,1152]{1,0:T(8,128)(2,1)S(1)}, bf16[208,1152]{1,0:T(8,128)(2,1)S(1)}, u32[]{:S(2)}, u32[]{:S(2)}) collective-permute-start(bf16[208,1152]{1,0:T(8,128)(2,1)S(1)} %get-tuple-element.6), channel_id=1, source_target_pairs={{0,4},{4,8},{8,12},{12,16},{16,20},{20,24},{24,28},{28,0},{1,5},{5... | collective-permute-start | bytes 1437704 | tf_op jit(solution)/shard_map/ppermute | solution.py:11
  5.0 24.3 %collective-permute-start = (bf16[208,1152]{1,0:T(8,128)(2,1)S(1)}, bf16[208,1152]{1,0:T(8,128)(2,1)S(1)}, u32[]{:S(2)}, u32[]{:S(2)}) collective-permute-start(bf16[208,1152]{1,0:T(8,128)(2,1)S(1)} %get-tuple-element.7), channel_id=1, source_target_pairs={{0,4},{4,8},{8,12},{12,16},{16,20},{20,24},{24,28},{28,0},{1,5},{5... | collective-permute-start | bytes 1437704 | tf_op jit(solution)/shard_map/ppermute | solution.py:11
  6.6 24.6 %collective-permute-start.2 = (bf16[416,1152]{1,0:T(8,128)(2,1)S(1)}, bf16[416,1152]{1,0:T(8,128)(2,1)S(1)}, u32[]{:S(2)}, u32[]{:S(2)}) collective-permute-start(bf16[416,1152]{1,0:T(8,128)(2,1)S(1)} %copy-done.1), channel_id=1, source_target_pairs={{0,3},{1,0},{2,1},{3,2},{4,7},{5,4},{6,5},{7,6},{8,11},{9,8},{10,9... | collective-permute-start | bytes 2875400 | tf_op jit(solution)/shard_map/ppermute | solution.py:11
  32.2 13.9 %collective-permute-start.4 = (bf16[208,1152]{1,0:T(8,128)(2,1)S(1)}, bf16[208,1152]{1,0:T(8,128)(2,1)S(1)}, u32[]{:S(2)}, u32[]{:S(2)}) collective-permute-start(bf16[208,1152]{1,0:T(8,128)(2,1)S(1)} %fusion.7), channel_id=1, source_target_pairs={{0,28},{4,0},{8,4},{12,8},{16,12},{20,16},{24,20},{28,24},{1,29},{... | collective-permute-start | bytes 1437704 | tf_op jit(solution)/shard_map/ppermute | solution.py:11
  34.9 19.7 %collective-permute-start.5 = (bf16[208,1152]{1,0:T(8,128)(2,1)S(1)}, bf16[208,1152]{1,0:T(8,128)(2,1)S(1)}, u32[]{:S(2)}, u32[]{:S(2)}) collective-permute-start(bf16[208,1152]{1,0:T(8,128)(2,1)S(1)} %fusion.6), channel_id=1, source_target_pairs={{0,28},{4,0},{8,4},{12,8},{16,12},{20,16},{24,20},{28,24},{1,29},{... | collective-permute-start | bytes 1437704 | tf_op jit(solution)/shard_map/ppermute | solution.py:11
  38.9 16.9 %collective-permute-start.3 = (bf16[416,1152]{1,0:T(8,128)(2,1)S(1)}, bf16[416,1152]{1,0:T(8,128)(2,1)S(1)}, u32[]{:S(2)}, u32[]{:S(2)}) collective-permute-start(bf16[416,1152]{1,0:T(8,128)(2,1)S(1)} %fusion.3), channel_id=1, source_target_pairs={{0,1},{1,2},{2,3},{3,0},{4,5},{5,6},{6,7},{7,4},{8,9},{9,10},{10,1... | collective-permute-start | bytes 2875400 | tf_op jit(solution)/shard_map/ppermute | solution.py:11

commit v3 on v2

v3 whole, which is shorter than its diff:
```python
import jax
import jax.numpy as jnp
from jax import lax
from jax.experimental import pallas as pl
from jax.experimental.pallas import tpu as pltpu
from jax.sharding import PartitionSpec as P

CHUNKS = 2
MIB = 2**20
SMEM = pl.BlockSpec(memory_space=pltpu.SMEM)
VMEM = pl.BlockSpec(memory_space=pltpu.VMEM)
HBM = pl.BlockSpec(memory_space=pltpu.HBM)
ANY = pl.BlockSpec(memory_space=pl.ANY)


def shifted(shard, axis, by):
    devices = lax.axis_size(axis)
    return lax.ppermute(shard, axis, [(i, (i + by) % devices) for i in range(devices)])


def dot_nt(a, b):
    return lax.dot_general(a, b, (((1,), (1,)), ((), ())), preferred_element_type=jnp.float32)


def dot_tn(a, b):
    return lax.dot_general(a, b, (((0,), (0,)), ((), ())), preferred_element_type=jnp.float32)


def dot_nn(a, b):
    return jnp.dot(a, b, preferred_element_type=jnp.float32)


def row_cuts(rows):
    tiles = rows // 16
    cuts = [tiles * i // CHUNKS * 16 for i in range(CHUNKS)] + [rows]
    return list(zip(cuts[:-1], cuts[1:]))


def fetch(sources, after):
    count = len(sources)

    def kernel(*refs):
        sems = refs[-1]
        outs = refs[-1 - count : -1]
        copies = [
            pltpu.make_async_copy(refs[i].at[pl.ds(lo, hi - lo), :], outs[i], sems.at[i])
            for i, (_, lo, hi) in enumerate(sources)
        ]
        for copy in copies:
            copy.start()
        for copy in copies:
            copy.wait()

    return pl.pallas_call(
        kernel,
        out_shape=[jax.ShapeDtypeStruct((hi - lo, a.shape[1]), a.dtype) for a, lo, hi in sources],
        in_specs=[HBM] * count + [ANY] * len(after),
        out_specs=[VMEM] * count,
        scratch_shapes=[pltpu.SemaphoreType.DMA((count,))],
        compiler_params=pltpu.CompilerParams(vmem_limit_bytes=2 * MIB),
        name="fetch",
    )(*[a for a, _, _ in sources], *after)


def partial_kernel(scale_ref, bias_ref, image_ref, next_ref, part_ref, *refs):
    sent_ref, own_ref, other_ref = refs[-3:]
    scale = scale_ref[0]
    bias = bias_ref[0]
    part = part_ref[...]
    own = jax.nn.sigmoid(dot_nt(part, image_ref[...]) * scale + bias).astype(jnp.bfloat16)
    own_ref[...] = own
    total = dot_nn(own, image_ref[...])
    other = jax.nn.sigmoid(dot_nt(part, next_ref[...]) * scale + bias).astype(jnp.bfloat16)
    other_ref[...] = other
    total += dot_nn(other, next_ref[...])
    sent_ref[...] = (scale * total).astype(jnp.bfloat16)


def partial(factor, shift, image, image_next, part, after):
    rows, width = part.shape
    columns = image.shape[0]
    return pl.pallas_call(
        partial_kernel,
        out_shape=(
            jax.ShapeDtypeStruct((rows, width), jnp.bfloat16),
            jax.ShapeDtypeStruct((rows, columns), jnp.bfloat16),
            jax.ShapeDtypeStruct((rows, columns), jnp.bfloat16),
        ),
        in_specs=[SMEM, SMEM, VMEM, VMEM, VMEM] + [ANY] * len(after),
        out_specs=(VMEM, VMEM, VMEM),
        compiler_params=pltpu.CompilerParams(vmem_limit_bytes=16 * MIB),
        cost_estimate=pl.CostEstimate(
            flops=8 * rows * columns * width,
            bytes_accessed=2 * (2 * columns + 2 * rows) * width,
            transcendentals=2 * rows * columns,
        ),
        name="partial",
    )(factor, shift, image, image_next, part, *after)


def add_rows(total, back, lo, result, after):
    rows, width = back.shape

    def kernel(total_ref, back_ref, *refs):
        result_ref, buffer, sem = refs[-3:]
        buffer[...] = (total_ref[pl.ds(lo, rows), :] + back_ref[...].astype(jnp.float32)).astype(jnp.bfloat16)
        copy = pltpu.make_async_copy(buffer, result_ref.at[pl.ds(lo, rows), :], sem)
        copy.start()
        copy.wait()

    kept = [] if result is None else [result]
    return pl.pallas_call(
        kernel,
        out_shape=jax.ShapeDtypeStruct(total.shape, jnp.bfloat16),
        in_specs=[VMEM, VMEM] + [HBM] * (len(kept) + len(after)),
        out_specs=HBM,
        scratch_shapes=[pltpu.VMEM((rows, width), jnp.bfloat16), pltpu.SemaphoreType.DMA],
        input_output_aliases={2: 0} if kept else {},
        compiler_params=pltpu.CompilerParams(vmem_limit_bytes=4 * MIB),
        name="add_rows",
    )(total, back, *kept, *after)


def body(image, text, target, factor, shift):
    scale = factor[0]
    bias = shift[0]
    cuts = row_cuts(text.shape[0])
    first = fetch([(text, *cuts[0])], [])
    *rest, held = fetch([(text, *cut) for cut in cuts[1:]] + [(image, 0, image.shape[0])], first)
    text_prev = [shifted(part, "blk", 1) for part in first]
    image_next = shifted(held, "grp", -1)
    text_prev += [shifted(part, "blk", 1) for part in rest]

    own = jax.nn.sigmoid(dot_nt(held, text) * scale + bias)
    column = lax.broadcasted_iota(jnp.int32, own.shape, 1)
    own = (own - (column == target[0][:, None]).astype(jnp.float32)).astype(jnp.bfloat16)

    image_grad = dot_nn(own, text)
    text_grad = dot_tn(own, held)

    next_own = jax.nn.sigmoid(dot_nt(image_next, text) * scale + bias).astype(jnp.bfloat16)
    image_sent = dot_nn(next_own, text)
    text_grad = scale * (text_grad + dot_tn(next_own, image_next))

    text_back = []
    after = []
    for part in text_prev:
        sent, own_prev, next_prev = partial(factor, shift, held, image_next, part, after)
        after = [sent]
        text_back.append(shifted(sent, "blk", -1))
        image_sent = image_sent + dot_tn(next_prev, part)
        image_grad = image_grad + dot_tn(own_prev, part)

    image_back = shifted((scale * image_sent).astype(jnp.bfloat16), "grp", 1)
    image_grad = add_rows(scale * image_grad, image_back, 0, None, [])
    result = None
    for (lo, _), back in zip(cuts, text_back):
        result = add_rows(text_grad, back, lo, result, [image_grad] if lo == cuts[-1][0] else [])
    return image_grad, result


def solution(mesh):
    block = P(("blk", "grp"), None)
    return jax.shard_map(
        body, mesh=mesh, in_specs=(block, block, block, P(), P()), out_specs=(block, block), check_vma=False
    )
```

time: 57.1 us -> 64.7 us (1.13)
  Pallas kernels: 0 us -> 6.66 us
  starting transfers between devices: 8.27 us -> 13 us
  matrix products: 10.3 us -> 6.65 us
  other arithmetic: 2.32 us -> 0 us
  local copies, waits for them, and re-layouts: 1.39 us -> 3.57 us
    pallas_call x0 -> x7, Pallas kernels: none -> 6.66 us  [the longest x3 2.92 us: add_rows(): pl.pallas_call(kernel, out_shape=jax.ShapeDtypeStruct(total.shape, jnp.bf...]
    ppermute x6, starting transfers between devices: 8.27 us -> 13 us  [shifted(): lax.ppermute(shard, axis, [(i, (i + by) % devices) for i in range(devices)])]
    unnamed x6 -> x10, local copies, waits for them, and re-layouts: 0.01 us -> 3.57 us
    convert_element_type x2 -> x0, other arithmetic: 2.32 us -> none  [the longest x1 1.17 us: body(): (image_grad + image_back.astype(jnp.float32)).astype(jnp.bfloat16)]
    dot_general x6 -> x2, matrix products: 3.64 us -> 1.72 us  [dot_nt(): lax.dot_general(a, b, (((1,), (1,)), ((), ())), preferred_element_type=jn...]
    dot_general x6 -> x2, matrix products: 3.21 us -> 1.42 us  [dot_nn(): return jnp.dot(a, b, preferred_element_type=jnp.float32)]
    slice x1 -> x0, local copies, waits for them, and re-layouts: 1.38 us -> none  [body(): text_prev = [shifted(text[lo:hi], 'blk', 1) for lo, hi in cuts]]
  transfers between devices with their start and end apart: 6 -> 6, of which waited for: 4 -> 3; matrix products, arithmetic and copies ran while one was open for 18% -> 10% of each run, Pallas kernels for 0% -> 8%
where the time goes in v3:
time: 64.7 us; the launch traced here: 64.5 us
  waiting for transfers between devices  32.5 us (50%)
  starting transfers between devices  13 us (20%)
  Pallas kernels  6.66 us (10%)
  matrix products  6.65 us (10%)
  local copies, waits for them, and re-layouts  3.57 us (6%)
  between operations  2.11 us (3%)
    ppermute x6, waiting for transfers between devices, shifted(): lax.ppermute(shard, axis, [(i, (i + by) % devices) for i in range(devices)])  32.5 us
    ppermute x6, starting transfers between devices, shifted(): lax.ppermute(shard, axis, [(i, (i + by) % devices) for i in range(devices)])  13 us
    unnamed x10, local copies, waits for them, and re-layouts  3.57 us
    dot_general x6, matrix products, dot_tn(): lax.dot_general(a, b, (((0,), (0,)), ((), ())), preferred_element_type=jn...  3.51 us
    pallas_call x3, Pallas kernels, add_rows(): pl.pallas_call(kernel, out_shape=jax.ShapeDtypeStruct(total.shape, jnp.bf...  2.92 us
    pallas_call x2, Pallas kernels, partial(): pl.pallas_call(partial_kernel, out_shape=(jax.ShapeDtypeStruct((rows, wid...  2.86 us
    dot_general x2, matrix products, dot_nt(): lax.dot_general(a, b, (((1,), (1,)), ((), ())), preferred_element_type=jn...  1.72 us
    dot_general x2, matrix products, dot_nn(): return jnp.dot(a, b, preferred_element_type=jnp.float32)  1.42 us
  transfers between devices with their start and end apart: 6, of which 3 were waited for; matrix products, arithmetic and copies ran while one was open for 10% of the time, Pallas kernels for 8%

profile of v3, /device:TPU:0, one launch (start us, length us, event | category | flops | bytes accessed | tf_op | source)
XLA Modules:
  0.0 64.5 jit_solution(18269617889866266910)
XLA Ops:
  0.6 1.2 %copy-done = bf16[416,1152]{1,0:T(8,128)(2,1)S(1)} copy-done((bf16[416,1152]{1,0:T(8,128)(2,1)S(1)}, bf16[416,1152]{1,0:T(8,128)(2,1)}, u32[]{:S(2)}) %copy-start) | copy-done | bytes 958488
  1.8 0.3 fetch.2.refs_2_
  2.1 0.0 copy-start.3
  2.2 1.2 %copy-done.3 = bf16[416,1152]{1,0:T(8,128)(2,1)S(1)} copy-done((bf16[416,1152]{1,0:T(8,128)(2,1)S(1)}, bf16[416,1152]{1,0:T(8,128)(2,1)}, u32[]{:S(2)}) %copy-start.3) | copy-done | bytes 958488
  3.3 0.6 fetch.3
  3.9 2.5 %collective-permute-start = (bf16[416,1152]{1,0:T(8,128)(2,1)S(1)}, bf16[416,1152]{1,0:T(8,128)(2,1)S(1)}, u32[]{:S(2)}, u32[]{:S(2)}) collective-permute-start(bf16[416,1152]{1,0:T(8,128)(2,1)S(1)} %get-tuple-element.10.image_ref), channel_id=1, source_target_pairs={{0,3},{1,0},{2,1},{3,2},{4,7},{5,4},{6,5},{7,6},{8,11},{9,8},{10,9... | collective-permute-start | bytes 2875400 | tf_op jit(solution)/shard_map/ppermute | solution.py:18
  6.4 1.5 %collective-permute-start.1 = (bf16[208,1152]{1,0:T(8,128)(2,1)S(1)}, bf16[208,1152]{1,0:T(8,128)(2,1)S(1)}, u32[]{:S(2)}, u32[]{:S(2)}) collective-permute-start(bf16[208,1152]{1,0:T(8,128)(2,1)S(1)} %fetch.2.refs_2_), channel_id=1, source_target_pairs={{0,4},{4,8},{8,12},{12,16},{16,20},{20,24},{24,28},{28,0},{1,5},{5... | collective-permute-start | bytes 1437704 | tf_op jit(solution)/shard_map/ppermute | solution.py:18
  7.9 1.5 %collective-permute-start.2 = (bf16[208,1152]{1,0:T(8,128)(2,1)S(1)}, bf16[208,1152]{1,0:T(8,128)(2,1)S(1)}, u32[]{:S(2)}, u32[]{:S(2)}) collective-permute-start(bf16[208,1152]{1,0:T(8,128)(2,1)S(1)} %get-tuple-element.12), channel_id=1, source_target_pairs={{0,4},{4,8},{8,12},{12,16},{16,20},{20,24},{24,28},{28,0},{1,5},{5... | collective-permute-start | bytes 1437704 | tf_op jit(solution)/shard_map/ppermute | solution.py:18
  10.7 0.9 %fusion.16 = bf16[416,416]{1,0:T(8,128)(2,1)S(1)} fusion(bf16[416,1152]{1,0:T(8,128)(2,1)S(1)} %get-tuple-element.10.image_ref, bf16[416,1152]{1,0:T(8,128)(2,1)S(1)} %copy-done.1, s32[416]{0:T(512)S(1)} %bitcast.30, f32[]{:T(128)} %bitcast.28, f32[]{:T(128)} %bitcast.24), kind=kOutput, calls=%fused_computation.23 | convolution fusion | flops 400278528 | bytes 2264712 | tf_op jit(solution)/shard_map/dot_general | solution.py:22
  11.6 0.7 %fusion.19 = f32[416,1152]{1,0:T(8,128)S(1)} fusion(bf16[416,416]{1,0:T(8,128)(2,1)S(1)} %fusion.16, bf16[416,1152]{1,0:T(8,128)(2,1)S(1)} %get-tuple-element.10.image_ref), kind=kOutput, calls=%fused_computation.27 | convolution fusion | flops 398721024 | bytes 3221504 | tf_op jit(solution)/shard_map/dot_general | solution.py:26
  12.4 0.7 %fusion.17 = f32[416,1152]{1,0:T(8,128)S(1)} fusion(bf16[416,416]{1,0:T(8,128)(2,1)S(1)} %fusion.16, bf16[416,1152]{1,0:T(8,128)(2,1)S(1)} %copy-done.1), kind=kOutput, calls=%fused_computation.25 | convolution fusion | flops 398721024 | bytes 3221504 | tf_op jit(solution)/shard_map/dot_general | solution.py:30
  13.1 9.9 %collective-permute-done.1.part_ref = bf16[208,1152]{1,0:T(8,128)(2,1)S(1)} collective-permute-done((bf16[208,1152]{1,0:T(8,128)(2,1)S(1)}, bf16[208,1152]{1,0:T(8,128)(2,1)S(1)}, u32[]{:S(2)}, u32[]{:S(2)}) %collective-permute-start.1) | collective-permute-done | bytes 479264 | tf_op jit(solution)/shard_map/ppermute | solution.py:18
  23.0 0.0 collective-permute-done.next_ref
  23.0 1.4 %partial.2 = (bf16[208,1152]{1,0:T(8,128)(2,1)S(1)}, bf16[208,416]{1,0:T(8,128)(2,1)S(1)}, bf16[208,416]{1,0:T(8,128)(2,1)S(1)}) custom-call(f32[1]{0:T(128)} %copy.9.scale_ref, f32[1]{0:T(128)} %copy.10.bias_ref, bf16[416,1152]{1,0:T(8,128)(2,1)S(1)} %get-tuple-element.10.image_ref, bf16[416,1152]{1,0:T(8,128)(2,1)S(1)} %collective-permute-done.next_ref, ...), custom_call_target="tpu_custom_call" | custom-call | flops 797442048 | bytes 2875392 | tf_op jit(solution)/shard_map/partial/pallas_call | solution.py:82
  24.4 1.9 %collective-permute-start.5 = (bf16[208,1152]{1,0:T(8,128)(2,1)S(1)}, bf16[208,1152]{1,0:T(8,128)(2,1)S(1)}, u32[]{:S(2)}, u32[]{:S(2)}) collective-permute-start(bf16[208,1152]{1,0:T(8,128)(2,1)S(1)} %get-tuple-element.13.refs_0_), channel_id=1, source_target_pairs={{0,28},{4,0},{8,4},{12,8},{16,12},{20,16},{24,20},{28,24},{1,29},{... | collective-permute-start | bytes 1437704 | tf_op jit(solution)/shard_map/ppermute | solution.py:18
  26.3 12.1 %collective-permute-done.2.part_ref = bf16[208,1152]{1,0:T(8,128)(2,1)S(1)} collective-permute-done((bf16[208,1152]{1,0:T(8,128)(2,1)S(1)}, bf16[208,1152]{1,0:T(8,128)(2,1)S(1)}, u32[]{:S(2)}, u32[]{:S(2)}) %collective-permute-start.2) | collective-permute-done | bytes 479264 | tf_op jit(solution)/shard_map/ppermute | solution.py:18
  38.4 1.4 %partial.3 = (bf16[208,1152]{1,0:T(8,128)(2,1)S(1)}, bf16[208,416]{1,0:T(8,128)(2,1)S(1)}, bf16[208,416]{1,0:T(8,128)(2,1)S(1)}) custom-call(f32[1]{0:T(128)} %copy.9.scale_ref, f32[1]{0:T(128)} %copy.10.bias_ref, bf16[416,1152]{1,0:T(8,128)(2,1)S(1)} %get-tuple-element.10.image_ref, bf16[416,1152]{1,0:T(8,128)(2,1)S(1)} %collective-permute-done.next_ref, ...), custom_call_target="tpu_custom_call" | custom-call | flops 797442048 | bytes 2875392 | tf_op jit(solution)/shard_map/partial/pallas_call | solution.py:82
  39.8 5.6 %collective-permute-start.4 = (bf16[208,1152]{1,0:T(8,128)(2,1)S(1)}, bf16[208,1152]{1,0:T(8,128)(2,1)S(1)}, u32[]{:S(2)}, u32[]{:S(2)}) collective-permute-start(bf16[208,1152]{1,0:T(8,128)(2,1)S(1)} %get-tuple-element.17), channel_id=1, source_target_pairs={{0,28},{4,0},{8,4},{12,8},{16,12},{20,16},{24,20},{28,24},{1,29},{... | collective-permute-start | bytes 1437704 | tf_op jit(solution)/shard_map/ppermute | solution.py:18
  45.4 0.8 %fusion.15 = bf16[416,416]{1,0:T(8,128)(2,1)S(1)} fusion(bf16[416,1152]{1,0:T(8,128)(2,1)S(1)} %collective-permute-done.next_ref, bf16[416,1152]{1,0:T(8,128)(2,1)S(1)} %copy-done.1, f32[]{:T(128)} %bitcast.29, f32[]{:T(128)} %bitcast.27), kind=kOutput, calls=%fused_computation.22 | convolution fusion | flops 399759360 | bytes 2263048 | tf_op jit(solution)/shard_map/dot_general | solution.py:22
  46.2 0.7 %fusion.18 = f32[416,1152]{1,0:T(8,128)S(1)} fusion(bf16[416,416]{1,0:T(8,128)(2,1)S(1)} %fusion.15, bf16[416,1152]{1,0:T(8,128)(2,1)S(1)} %copy-done.1), kind=kOutput, calls=%fused_computation.26 | convolution fusion | flops 398721024 | bytes 3221504 | tf_op jit(solution)/shard_map/dot_general | solution.py:30
  46.9 0.5 convolution_add_fusion.1
  47.4 0.5 fusion.3
  47.9 0.1 collective-permute-start.3
  48.0 0.5 convolution_add_fusion.3
  48.5 0.5 fusion.1.total_ref
  49.0 0.8 %fusion.total_ref = f32[416,1152]{1,0:T(8,128)S(1)} fusion(f32[416,1152]{1,0:T(8,128)S(1)} %fusion.19, bf16[416,416]{1,0:T(8,128)(2,1)S(1)} %fusion.15, bf16[416,1152]{1,0:T(8,128)(2,1)S(1)} %collective-permute-done.next_ref, f32[]{:T(128)} %bitcast.25), kind=kOutput, calls=%fused_computation.5 | convolution fusion | flops 399679488 | bytes 5138436 | tf_op jit(solution)/shard_map/dot_general | solution.py:26
  49.8 0.9 %add_rows.4.refs_0_ = bf16[416,1152]{1,0:T(8,128)(2,1)} custom-call(f32[416,1152]{1,0:T(8,128)S(1)} %fusion.total_ref, bf16[208,1152]{1,0:T(8,128)(2,1)S(1)} %collective-permute-done.5.back_ref), custom_call_target="tpu_custom_call" | custom-call | tf_op jit(solution)/shard_map/add_rows/pallas_call | solution.py:112
  50.7 10.5 %collective-permute-done.3.back_ref = bf16[416,1152]{1,0:T(8,128)(2,1)S(1)} collective-permute-done((bf16[416,1152]{1,0:T(8,128)(2,1)S(1)}, bf16[416,1152]{1,0:T(8,128)(2,1)S(1)}, u32[]{:S(2)}, u32[]{:S(2)}) %collective-permute-start.3) | collective-permute-done | bytes 958496 | tf_op jit(solution)/shard_map/ppermute | solution.py:18
  61.3 1.2 %add_rows.3.refs_1_ = bf16[416,1152]{1,0:T(8,128)(2,1)} custom-call(f32[416,1152]{1,0:T(8,128)S(1)} %fusion.1.total_ref, bf16[416,1152]{1,0:T(8,128)(2,1)S(1)} %collective-permute-done.3.back_ref), custom_call_target="tpu_custom_call" | custom-call | tf_op jit(solution)/shard_map/add_rows/pallas_call | solution.py:112
  62.4 0.0 copy-start.2
  62.4 1.2 %copy-done.2 = bf16[416,1152]{1,0:T(8,128)(2,1)S(1)} copy-done((bf16[416,1152]{1,0:T(8,128)(2,1)S(1)}, bf16[416,1152]{1,0:T(8,128)(2,1)}, u32[]{:S(2)}) %copy-start.2) | copy-done | bytes 958488
  63.6 0.9 %add_rows.5 = bf16[416,1152]{1,0:T(8,128)(2,1)} custom-call(f32[416,1152]{1,0:T(8,128)S(1)} %fusion.total_ref, bf16[208,1152]{1,0:T(8,128)(2,1)S(1)} %collective-permute-done.4.back_ref, bf16[416,1152]{1,0:T(8,128)(2,1)} %add_rows.4.refs_0_, bf16[416,1152]{1,0:T(8,128)(2,1)S(1)} %copy-done.2), custom_call_target="tpu_custom_call", output_to_operand_aliasing={{}: (2, {})} | custom-call | tf_op jit(solution)/shard_map/add_rows/pallas_call | solution.py:112
  (7 shorter events, 0.0 us)
Async XLA Ops:
  0.6 1.2 %copy-start = (bf16[416,1152]{1,0:T(8,128)(2,1)S(1)}, bf16[416,1152]{1,0:T(8,128)(2,1)}, u32[]{:S(2)}) copy-start(bf16[416,1152]{1,0:T(8,128)(2,1)} %refs_0_.3) | copy-start | bytes 2875396
  1.8 8.9 %copy-start.1 = (bf16[416,1152]{1,0:T(8,128)(2,1)S(1)}, bf16[416,1152]{1,0:T(8,128)(2,1)}, u32[]{:S(2)}) copy-start(bf16[416,1152]{1,0:T(8,128)(2,1)} %refs_0_.3) | copy-start | bytes 2875396
  1.8 8.9 %copy-start.4 = (s32[1,416]{1,0:T(1,128)S(1)}, s32[1,416]{1,0:T(1,128)}, u32[]{:S(2)}) copy-start(s32[1,416]{1,0:T(1,128)} %param.7) | copy-start | bytes 4996
  2.1 1.2 %copy-start.3 = (bf16[416,1152]{1,0:T(8,128)(2,1)S(1)}, bf16[416,1152]{1,0:T(8,128)(2,1)}, u32[]{:S(2)}) copy-start(bf16[416,1152]{1,0:T(8,128)(2,1)} %refs_1_.1) | copy-start | bytes 2875396
  3.9 19.0 %collective-permute-start = (bf16[416,1152]{1,0:T(8,128)(2,1)S(1)}, bf16[416,1152]{1,0:T(8,128)(2,1)S(1)}, u32[]{:S(2)}, u32[]{:S(2)}) collective-permute-start(bf16[416,1152]{1,0:T(8,128)(2,1)S(1)} %get-tuple-element.10.image_ref), channel_id=1, source_target_pairs={{0,3},{1,0},{2,1},{3,2},{4,7},{5,4},{6,5},{7,6},{8,11},{9,8},{10,9... | collective-permute-start | bytes 2875400 | tf_op jit(solution)/shard_map/ppermute | solution.py:18
  6.4 16.6 %collective-permute-start.1 = (bf16[208,1152]{1,0:T(8,128)(2,1)S(1)}, bf16[208,1152]{1,0:T(8,128)(2,1)S(1)}, u32[]{:S(2)}, u32[]{:S(2)}) collective-permute-start(bf16[208,1152]{1,0:T(8,128)(2,1)S(1)} %fetch.2.refs_2_), channel_id=1, source_target_pairs={{0,4},{4,8},{8,12},{12,16},{16,20},{20,24},{24,28},{28,0},{1,5},{5... | collective-permute-start | bytes 1437704 | tf_op jit(solution)/shard_map/ppermute | solution.py:18
  7.9 30.5 %collective-permute-start.2 = (bf16[208,1152]{1,0:T(8,128)(2,1)S(1)}, bf16[208,1152]{1,0:T(8,128)(2,1)S(1)}, u32[]{:S(2)}, u32[]{:S(2)}) collective-permute-start(bf16[208,1152]{1,0:T(8,128)(2,1)S(1)} %get-tuple-element.12), channel_id=1, source_target_pairs={{0,4},{4,8},{8,12},{12,16},{16,20},{20,24},{24,28},{28,0},{1,5},{5... | collective-permute-start | bytes 1437704 | tf_op jit(solution)/shard_map/ppermute | solution.py:18
  24.4 25.4 %collective-permute-start.5 = (bf16[208,1152]{1,0:T(8,128)(2,1)S(1)}, bf16[208,1152]{1,0:T(8,128)(2,1)S(1)}, u32[]{:S(2)}, u32[]{:S(2)}) collective-permute-start(bf16[208,1152]{1,0:T(8,128)(2,1)S(1)} %get-tuple-element.13.refs_0_), channel_id=1, source_target_pairs={{0,28},{4,0},{8,4},{12,8},{16,12},{20,16},{24,20},{28,24},{1,29},{... | collective-permute-start | bytes 1437704 | tf_op jit(solution)/shard_map/ppermute | solution.py:18
  39.8 22.6 %collective-permute-start.4 = (bf16[208,1152]{1,0:T(8,128)(2,1)S(1)}, bf16[208,1152]{1,0:T(8,128)(2,1)S(1)}, u32[]{:S(2)}, u32[]{:S(2)}) collective-permute-start(bf16[208,1152]{1,0:T(8,128)(2,1)S(1)} %get-tuple-element.17), channel_id=1, source_target_pairs={{0,28},{4,0},{8,4},{12,8},{16,12},{20,16},{24,20},{28,24},{1,29},{... | collective-permute-start | bytes 1437704 | tf_op jit(solution)/shard_map/ppermute | solution.py:18
  47.9 13.3 %collective-permute-start.3 = (bf16[416,1152]{1,0:T(8,128)(2,1)S(1)}, bf16[416,1152]{1,0:T(8,128)(2,1)S(1)}, u32[]{:S(2)}, u32[]{:S(2)}) collective-permute-start(bf16[416,1152]{1,0:T(8,128)(2,1)S(1)} %fusion.3), channel_id=1, source_target_pairs={{0,1},{1,2},{2,3},{3,0},{4,5},{5,6},{6,7},{7,4},{8,9},{9,10},{10,1... | collective-permute-start | bytes 2875400 | tf_op jit(solution)/shard_map/ppermute | solution.py:18
  62.4 1.2 %copy-start.2 = (bf16[416,1152]{1,0:T(8,128)(2,1)S(1)}, bf16[416,1152]{1,0:T(8,128)(2,1)}, u32[]{:S(2)}) copy-start(bf16[416,1152]{1,0:T(8,128)(2,1)} %add_rows.3.refs_1_) | copy-start | bytes 2875396

commit v4 on v3

--- a/solution.py
+++ b/solution.py
@@ -5,7 +5,6 @@
 from jax.experimental.pallas import tpu as pltpu
 from jax.sharding import PartitionSpec as P
 
-CHUNKS = 2
 MIB = 2**20
 SMEM = pl.BlockSpec(memory_space=pltpu.SMEM)
 VMEM = pl.BlockSpec(memory_space=pltpu.VMEM)
@@ -32,7 +31,7 @@
 
 def row_cuts(rows):
     tiles = rows // 16
-    cuts = [tiles * i // CHUNKS * 16 for i in range(CHUNKS)] + [rows]
+    cuts = [0, tiles * 2 // 5 * 16, tiles * 17 // 20 * 16, rows]
     return list(zip(cuts[:-1], cuts[1:]))
 
 
@@ -100,21 +99,34 @@
 
 def add_rows(total, back, lo, result, after):
     rows, width = back.shape
+    step = rows // 16 // 3 * 16 if rows >= 96 else rows
+    cuts = [(i, min(i + step, rows)) for i in range(0, rows, step)]
 
     def kernel(total_ref, back_ref, *refs):
-        result_ref, buffer, sem = refs[-3:]
-        buffer[...] = (total_ref[pl.ds(lo, rows), :] + back_ref[...].astype(jnp.float32)).astype(jnp.bfloat16)
-        copy = pltpu.make_async_copy(buffer, result_ref.at[pl.ds(lo, rows), :], sem)
-        copy.start()
-        copy.wait()
+        result_ref, mark_ref, buffer, sems = refs[-4:]
+        copies = []
+        for i, (a, b) in enumerate(cuts):
+            buffer[a:b, :] = (total_ref[lo + a : lo + b, :] + back_ref[a:b, :].astype(jnp.float32)).astype(jnp.bfloat16)
+            copies.append(
+                pltpu.make_async_copy(
+                    buffer.at[pl.ds(a, b - a), :], result_ref.at[pl.ds(lo + a, b - a), :], sems.at[i]
+                )
+            )
+            copies[-1].start()
+        mark_ref[...] = jnp.zeros(mark_ref.shape, mark_ref.dtype)
+        for copy in copies:
+            copy.wait()
 
     kept = [] if result is None else [result]
     return pl.pallas_call(
         kernel,
-        out_shape=jax.ShapeDtypeStruct(total.shape, jnp.bfloat16),
-        in_specs=[VMEM, VMEM] + [HBM] * (len(kept) + len(after)),
-        out_specs=HBM,
-        scratch_shapes=[pltpu.VMEM((rows, width), jnp.bfloat16), pltpu.SemaphoreType.DMA],
+        out_shape=(
+            jax.ShapeDtypeStruct(total.shape, jnp.bfloat16),
+            jax.ShapeDtypeStruct((8, 128), jnp.float32),
+        ),
+        in_specs=[VMEM, VMEM] + [HBM] * len(kept) + [ANY] * len(after),
+        out_specs=(HBM, VMEM),
+        scratch_shapes=[pltpu.VMEM((rows, width), jnp.bfloat16), pltpu.SemaphoreType.DMA((len(cuts),))],
         input_output_aliases={2: 0} if kept else {},
         compiler_params=pltpu.CompilerParams(vmem_limit_bytes=4 * MIB),
         name="add_rows",
@@ -125,37 +137,36 @@
     scale = factor[0]
     bias = shift[0]
     cuts = row_cuts(text.shape[0])
-    first = fetch([(text, *cuts[0])], [])
-    *rest, held = fetch([(text, *cut) for cut in cuts[1:]] + [(image, 0, image.shape[0])], first)
-    text_prev = [shifted(part, "blk", 1) for part in first]
-    image_next = shifted(held, "grp", -1)
-    text_prev += [shifted(part, "blk", 1) for part in rest]
+    first = text[: cuts[0][1]]
+    rest = fetch([(text, *cut) for cut in cuts[1:]], [first])
+    text_prev = [shifted(part, "blk", 1) for part in [first, *rest]]
+    image_next = shifted(image, "grp", -1)
 
-    own = jax.nn.sigmoid(dot_nt(held, text) * scale + bias)
+    own = jax.nn.sigmoid(dot_nt(image, text) * scale + bias)
     column = lax.broadcasted_iota(jnp.int32, own.shape, 1)
     own = (own - (column == target[0][:, None]).astype(jnp.float32)).astype(jnp.bfloat16)
 
     image_grad = dot_nn(own, text)
-    text_grad = dot_tn(own, held)
+    text_grad = dot_tn(own, image)
 
     next_own = jax.nn.sigmoid(dot_nt(image_next, text) * scale + bias).astype(jnp.bfloat16)
     image_sent = dot_nn(next_own, text)
     text_grad = scale * (text_grad + dot_tn(next_own, image_next))
 
     text_back = []
-    after = []
+    after = [text_prev[1]]
     for part in text_prev:
-        sent, own_prev, next_prev = partial(factor, shift, held, image_next, part, after)
+        sent, own_prev, next_prev = partial(factor, shift, image, image_next, part, after)
         after = [sent]
         text_back.append(shifted(sent, "blk", -1))
         image_sent = image_sent + dot_tn(next_prev, part)
         image_grad = image_grad + dot_tn(own_prev, part)
 
     image_back = shifted((scale * image_sent).astype(jnp.bfloat16), "grp", 1)
-    image_grad = add_rows(scale * image_grad, image_back, 0, None, [])
+    image_grad, image_mark = add_rows(scale * image_grad, image_back, 0, None, [])
     result = None
     for (lo, _), back in zip(cuts, text_back):
-        result = add_rows(text_grad, back, lo, result, [image_grad] if lo == cuts[-1][0] else [])
+        result, _ = add_rows(text_grad, back, lo, result, [image_mark] if lo == cuts[-1][0] else [])
     return image_grad, result
 
 

time: 64.7 us -> 54 us (0.83)
  waiting for transfers between devices: 32.5 us -> 21.5 us
  Pallas kernels: 6.66 us -> 9.38 us
  starting transfers between devices: 13 us -> 11 us
  local copies, waits for them, and re-layouts: 3.57 us -> 2.22 us
  matrix products: 6.65 us -> 7.46 us
    ppermute x6 -> x8, waiting for transfers between devices: 32.5 us -> 21.5 us  [shifted(): lax.ppermute(shard, axis, [(i, (i + by) % devices) for i in range(devices)])]
    unnamed x10 -> x8, local copies, waits for them, and re-layouts: 3.57 us -> 1.2 us
    pallas_call x3 -> x4, Pallas kernels: 2.92 us -> 5.09 us  [add_rows(): pl.pallas_call(kernel, out_shape=(jax.ShapeDtypeStruct(total.shape, jnp.b...]
    ppermute x6 -> x8, starting transfers between devices: 13 us -> 11 us  [shifted(): lax.ppermute(shard, axis, [(i, (i + by) % devices) for i in range(devices)])]
    slice x0 -> x1, local copies, waits for them, and re-layouts: none -> 1.02 us  [body(): first = text[:cuts[0][1]]]
    pallas_call x2 -> x3, Pallas kernels: 2.86 us -> 3.84 us  [partial(): pl.pallas_call(partial_kernel, out_shape=(jax.ShapeDtypeStruct((rows, wid...]
    dot_general x6 -> x8, matrix products: 3.51 us -> 4.35 us  [dot_tn(): lax.dot_general(a, b, (((0,), (0,)), ((), ())), preferred_element_type=jn...]
  transfers between devices with their start and end apart: 6 -> 8, of which waited for: 3 -> 4; matrix products, arithmetic and copies ran while one was open for 10% -> 16% of each run, Pallas kernels for 8% -> 15%
where the time goes in v4:
time: 54 us; the launch traced here: 53.7 us
  waiting for transfers between devices  21.5 us (40%)
  starting transfers between devices  11 us (20%)
  Pallas kernels  9.38 us (17%)
  matrix products  7.46 us (14%)
  local copies, waits for them, and re-layouts  2.22 us (4%)
  between operations  2.13 us (4%)
    ppermute x8, waiting for transfers between devices, shifted(): lax.ppermute(shard, axis, [(i, (i + by) % devices) for i in range(devices)])  21.5 us
    ppermute x8, starting transfers between devices, shifted(): lax.ppermute(shard, axis, [(i, (i + by) % devices) for i in range(devices)])  11 us
    pallas_call x4, Pallas kernels, add_rows(): pl.pallas_call(kernel, out_shape=(jax.ShapeDtypeStruct(total.shape, jnp.b...  5.09 us
    dot_general x8, matrix products, dot_tn(): lax.dot_general(a, b, (((0,), (0,)), ((), ())), preferred_element_type=jn...  4.35 us
    pallas_call x3, Pallas kernels, partial(): pl.pallas_call(partial_kernel, out_shape=(jax.ShapeDtypeStruct((rows, wid...  3.84 us
    dot_general x2, matrix products, dot_nt(): lax.dot_general(a, b, (((1,), (1,)), ((), ())), preferred_element_type=jn...  1.72 us
    dot_general x2, matrix products, dot_nn(): return jnp.dot(a, b, preferred_element_type=jnp.float32)  1.4 us
    unnamed x8, local copies, waits for them, and re-layouts  1.2 us
  transfers between devices with their start and end apart: 8, of which 4 were waited for; matrix products, arithmetic and copies ran while one was open for 16% of the time, Pallas kernels for 15%

profile of v4, /device:TPU:0, one launch (start us, length us, event | category | flops | bytes accessed | tf_op | source)
XLA Modules:
  0.0 53.7 jit_solution(6241213775214099531)
XLA Ops:
  0.6 2.5 %collective-permute-start = (bf16[416,1152]{1,0:T(8,128)(2,1)}, bf16[416,1152]{1,0:T(8,128)(2,1)S(1)}, u32[]{:S(2)}, u32[]{:S(2)}) collective-permute-start(bf16[416,1152]{1,0:T(8,128)(2,1)} %image_ref.5), channel_id=1, source_target_pairs={{0,3},{1,0},{2,1},{3,2},{4,7},{5,4},{6,5},{7,6},{8,11},{9,8},{10,9... | collective-permute-start | bytes 2875400 | tf_op jit(solution)/shard_map/ppermute | solution.py:17
  3.1 1.0 %slice.3.refs_2_ = bf16[160,1152]{1,0:T(8,128)(2,1)S(1)} slice(bf16[416,1152]{1,0:T(8,128)(2,1)} %refs_1_.1), slice={[0:160], [0:1152]} | slice | bytes 737280 | tf_op jit(solution)/shard_map/slice | solution.py:140
  4.1 1.5 %collective-permute-start.1 = (bf16[160,1152]{1,0:T(8,128)(2,1)S(1)}, bf16[160,1152]{1,0:T(8,128)(2,1)S(1)}, u32[]{:S(2)}, u32[]{:S(2)}) collective-permute-start(bf16[160,1152]{1,0:T(8,128)(2,1)S(1)} %slice.3.refs_2_), channel_id=1, source_target_pairs={{0,4},{4,8},{8,12},{12,16},{16,20},{20,24},{24,28},{28,0},{1,5},{5... | collective-permute-start | bytes 1105928 | tf_op jit(solution)/shard_map/ppermute | solution.py:17
  5.7 1.2 %copy-done = bf16[416,1152]{1,0:T(8,128)(2,1)S(1)} copy-done((bf16[416,1152]{1,0:T(8,128)(2,1)S(1)}, bf16[416,1152]{1,0:T(8,128)(2,1)}, u32[]{:S(2)}) %copy-start) | copy-done | bytes 958488
  6.9 0.5 fetch.1
  7.3 1.6 %collective-permute-start.2 = (bf16[192,1152]{1,0:T(8,128)(2,1)S(1)}, bf16[192,1152]{1,0:T(8,128)(2,1)S(1)}, u32[]{:S(2)}, u32[]{:S(2)}) collective-permute-start(bf16[192,1152]{1,0:T(8,128)(2,1)S(1)} %get-tuple-element.18), channel_id=1, source_target_pairs={{0,4},{4,8},{8,12},{12,16},{16,20},{20,24},{24,28},{28,0},{1,5},{5... | collective-permute-start | bytes 1327112 | tf_op jit(solution)/shard_map/ppermute | solution.py:17
  8.9 1.5 %collective-permute-start.3 = (bf16[64,1152]{1,0:T(8,128)(2,1)S(1)}, bf16[64,1152]{1,0:T(8,128)(2,1)S(1)}, u32[]{:S(2)}, u32[]{:S(2)}) collective-permute-start(bf16[64,1152]{1,0:T(8,128)(2,1)S(1)} %get-tuple-element.22), channel_id=1, source_target_pairs={{0,4},{4,8},{8,12},{12,16},{16,20},{20,24},{24,28},{28,0},{1,5},{5... | collective-permute-start | bytes 442376 | tf_op jit(solution)/shard_map/ppermute | solution.py:17
  11.7 0.9 %fusion.18 = bf16[416,416]{1,0:T(8,128)(2,1)S(1)} fusion(bf16[416,1152]{1,0:T(8,128)(2,1)S(1)} %copy-done.2, bf16[416,1152]{1,0:T(8,128)(2,1)S(1)} %copy-done.1, s32[416]{0:T(512)S(1)} %bitcast.34, f32[]{:T(128)} %bitcast.32, f32[]{:T(128)} %bitcast.28), kind=kOutput, calls=%fused_computation.25 | convolution fusion | flops 400278528 | bytes 2264712 | tf_op jit(solution)/shard_map/dot_general | solution.py:21
  12.6 0.7 %fusion.23 = f32[416,1152]{1,0:T(8,128)S(1)} fusion(bf16[416,416]{1,0:T(8,128)(2,1)S(1)} %fusion.18, bf16[416,1152]{1,0:T(8,128)(2,1)S(1)} %copy-done.2), kind=kOutput, calls=%fused_computation.31 | convolution fusion | flops 398721024 | bytes 3221504 | tf_op jit(solution)/shard_map/dot_general | solution.py:25
  13.4 0.7 %fusion.19 = f32[416,1152]{1,0:T(8,128)S(1)} fusion(bf16[416,416]{1,0:T(8,128)(2,1)S(1)} %fusion.18, bf16[416,1152]{1,0:T(8,128)(2,1)S(1)} %copy-done.1), kind=kOutput, calls=%fused_computation.27 | convolution fusion | flops 398721024 | bytes 3221504 | tf_op jit(solution)/shard_map/dot_general | solution.py:29
  14.1 4.3 %collective-permute-done.1.part_ref = bf16[160,1152]{1,0:T(8,128)(2,1)S(1)} collective-permute-done((bf16[160,1152]{1,0:T(8,128)(2,1)S(1)}, bf16[160,1152]{1,0:T(8,128)(2,1)S(1)}, u32[]{:S(2)}, u32[]{:S(2)}) %collective-permute-start.1) | collective-permute-done | bytes 368672 | tf_op jit(solution)/shard_map/ppermute | solution.py:17
  18.4 9.5 %collective-permute-done.2.refs_0_.part_ref = bf16[192,1152]{1,0:T(8,128)(2,1)S(1)} collective-permute-done((bf16[192,1152]{1,0:T(8,128)(2,1)S(1)}, bf16[192,1152]{1,0:T(8,128)(2,1)S(1)}, u32[]{:S(2)}, u32[]{:S(2)}) %collective-permute-start.2) | collective-permute-done | bytes 442400 | tf_op jit(solution)/shard_map/ppermute | solution.py:17
  27.9 1.3 %partial.3 = (bf16[160,1152]{1,0:T(8,128)(2,1)S(1)}, bf16[160,416]{1,0:T(8,128)(2,1)S(1)}, bf16[160,416]{1,0:T(8,128)(2,1)S(1)}) custom-call(f32[1]{0:T(128)} %copy.11.scale_ref, f32[1]{0:T(128)} %copy.12.bias_ref, bf16[416,1152]{1,0:T(8,128)(2,1)S(1)} %copy-done.2, bf16[416,1152]{1,0:T(8,128)(2,1)S(1)} %collective-permute-done.next_ref, ...), custom_call_target="tpu_custom_call" | custom-call | flops 613416960 | bytes 2654208 | tf_op jit(solution)/shard_map/partial/pallas_call | solution.py:81
  29.1 1.9 %collective-permute-start.7 = (bf16[160,1152]{1,0:T(8,128)(2,1)S(1)}, bf16[160,1152]{1,0:T(8,128)(2,1)S(1)}, u32[]{:S(2)}, u32[]{:S(2)}) collective-permute-start(bf16[160,1152]{1,0:T(8,128)(2,1)S(1)} %get-tuple-element.20.refs_0_), channel_id=1, source_target_pairs={{0,28},{4,0},{8,4},{12,8},{16,12},{20,16},{24,20},{28,24},{1,29},{... | collective-permute-start | bytes 1105928 | tf_op jit(solution)/shard_map/ppermute | solution.py:17
  31.0 1.4 %partial.4 = (bf16[192,1152]{1,0:T(8,128)(2,1)S(1)}, bf16[192,416]{1,0:T(8,128)(2,1)S(1)}, bf16[192,416]{1,0:T(8,128)(2,1)S(1)}) custom-call(f32[1]{0:T(128)} %copy.11.scale_ref, f32[1]{0:T(128)} %copy.12.bias_ref, bf16[416,1152]{1,0:T(8,128)(2,1)S(1)} %copy-done.2, bf16[416,1152]{1,0:T(8,128)(2,1)S(1)} %collective-permute-done.next_ref, ...), custom_call_target="tpu_custom_call" | custom-call | flops 736100352 | bytes 2801664 | tf_op jit(solution)/shard_map/partial/pallas_call | solution.py:81
  32.4 1.5 %collective-permute-start.6 = (bf16[192,1152]{1,0:T(8,128)(2,1)S(1)}, bf16[192,1152]{1,0:T(8,128)(2,1)S(1)}, u32[]{:S(2)}, u32[]{:S(2)}) collective-permute-start(bf16[192,1152]{1,0:T(8,128)(2,1)S(1)} %get-tuple-element.23.refs_0_), channel_id=1, source_target_pairs={{0,28},{4,0},{8,4},{12,8},{16,12},{20,16},{24,20},{28,24},{1,29},{... | collective-permute-start | bytes 1327112 | tf_op jit(solution)/shard_map/ppermute | solution.py:17
  33.9 0.8 %fusion.17 = bf16[416,416]{1,0:T(8,128)(2,1)S(1)} fusion(bf16[416,1152]{1,0:T(8,128)(2,1)S(1)} %collective-permute-done.next_ref, bf16[416,1152]{1,0:T(8,128)(2,1)S(1)} %copy-done.1, f32[]{:T(128)} %bitcast.33, f32[]{:T(128)} %bitcast.31), kind=kOutput, calls=%fused_computation.24 | convolution fusion | flops 399759360 | bytes 2263048 | tf_op jit(solution)/shard_map/dot_general | solution.py:21
  34.8 0.7 %fusion.21 = f32[416,1152]{1,0:T(8,128)S(1)} fusion(bf16[416,416]{1,0:T(8,128)(2,1)S(1)} %fusion.17, bf16[416,1152]{1,0:T(8,128)(2,1)S(1)} %copy-done.1), kind=kOutput, calls=%fused_computation.29 | convolution fusion | flops 398721024 | bytes 3221504 | tf_op jit(solution)/shard_map/dot_general | solution.py:29
  35.5 1.2 %partial.5 = (bf16[64,1152]{1,0:T(8,128)(2,1)S(1)}, bf16[64,416]{1,0:T(8,128)(2,1)S(1)}, bf16[64,416]{1,0:T(8,128)(2,1)S(1)}) custom-call(f32[1]{0:T(128)} %copy.11.scale_ref, f32[1]{0:T(128)} %copy.12.bias_ref, bf16[416,1152]{1,0:T(8,128)(2,1)S(1)} %copy-done.2, bf16[416,1152]{1,0:T(8,128)(2,1)S(1)} %collective-permute-done.next_ref, ...), custom_call_target="tpu_custom_call" | custom-call | flops 245366784 | bytes 2211840 | tf_op jit(solution)/shard_map/partial/pallas_call | solution.py:81
  36.6 0.4 fusion.22
  37.1 0.5 convolution_add_fusion.2
  37.6 0.5 fusion.5
  38.2 0.5 collective-permute-start.5
  38.7 0.5 convolution_add_fusion.4
  39.6 0.5 fusion.4.total_ref
  40.1 0.7 %fusion.total_ref = f32[416,1152]{1,0:T(8,128)S(1)} fusion(f32[416,1152]{1,0:T(8,128)S(1)} %fusion.23, bf16[416,416]{1,0:T(8,128)(2,1)S(1)} %fusion.17, bf16[416,1152]{1,0:T(8,128)(2,1)S(1)} %collective-permute-done.next_ref, f32[]{:T(128)} %bitcast.29), kind=kOutput, calls=%fused_computation.1 | convolution fusion | flops 399679488 | bytes 5138436 | tf_op jit(solution)/shard_map/dot_general | solution.py:25
  40.9 1.4 %add_rows.5 = (bf16[416,1152]{1,0:T(8,128)(2,1)}, f32[8,128]{1,0:T(8,128)}) custom-call(f32[416,1152]{1,0:T(8,128)S(1)} %fusion.total_ref, bf16[160,1152]{1,0:T(8,128)(2,1)S(1)} %collective-permute-done.7.back_ref), custom_call_target="tpu_custom_call" | custom-call | tf_op jit(solution)/shard_map/add_rows/pallas_call | solution.py:121
  42.3 6.3 %collective-permute-done.6.back_ref = bf16[192,1152]{1,0:T(8,128)(2,1)S(1)} collective-permute-done((bf16[192,1152]{1,0:T(8,128)(2,1)S(1)}, bf16[192,1152]{1,0:T(8,128)(2,1)S(1)}, u32[]{:S(2)}, u32[]{:S(2)}) %collective-permute-start.6) | collective-permute-done | bytes 442400 | tf_op jit(solution)/shard_map/ppermute | solution.py:17
  48.6 1.4 %add_rows.6 = (bf16[416,1152]{1,0:T(8,128)(2,1)}, f32[8,128]{1,0:T(8,128)}) custom-call(f32[416,1152]{1,0:T(8,128)S(1)} %fusion.total_ref, bf16[192,1152]{1,0:T(8,128)(2,1)S(1)} %collective-permute-done.6.back_ref, bf16[416,1152]{1,0:T(8,128)(2,1)} %get-tuple-element.30.refs_0_), custom_call_target="tpu_custom_call", output_to_operand_aliasing={{0}: (2, {})} | custom-call | tf_op jit(solution)/shard_map/add_rows/pallas_call | solution.py:121
  50.0 1.4 %collective-permute-done.4.back_ref = bf16[416,1152]{1,0:T(8,128)(2,1)S(1)} collective-permute-done((bf16[416,1152]{1,0:T(8,128)(2,1)S(1)}, bf16[416,1152]{1,0:T(8,128)(2,1)S(1)}, u32[]{:S(2)}, u32[]{:S(2)}) %collective-permute-start.4) | collective-permute-done | bytes 958496 | tf_op jit(solution)/shard_map/ppermute | solution.py:17
  51.4 1.0 %add_rows.4 = (bf16[416,1152]{1,0:T(8,128)(2,1)}, f32[8,128]{1,0:T(8,128)S(1)}) custom-call(f32[416,1152]{1,0:T(8,128)S(1)} %fusion.4.total_ref, bf16[416,1152]{1,0:T(8,128)(2,1)S(1)} %collective-permute-done.4.back_ref), custom_call_target="tpu_custom_call" | custom-call | tf_op jit(solution)/shard_map/add_rows/pallas_call | solution.py:121
  52.4 1.3 %add_rows.7 = (bf16[416,1152]{1,0:T(8,128)(2,1)}, f32[8,128]{1,0:T(8,128)}) custom-call(f32[416,1152]{1,0:T(8,128)S(1)} %fusion.total_ref, bf16[64,1152]{1,0:T(8,128)(2,1)S(1)} %collective-permute-done.5.back_ref, bf16[416,1152]{1,0:T(8,128)(2,1)} %get-tuple-element.31.refs_0_, f32[8,128]{1,0:T(8,128)S(1)} %get-tuple-element.32.refs_1_), custom_call_target="tpu_custom_call", output_to_operand_aliasing={{0}: (2, {})} | custom-call | tf_op jit(solution)/shard_map/add_rows/pallas_call | solution.py:121
  (13 shorter events, 0.5 us)
Async XLA Ops:
  0.6 11.1 %copy-start.3 = (s32[1,416]{1,0:T(1,128)S(1)}, s32[1,416]{1,0:T(1,128)}, u32[]{:S(2)}) copy-start(s32[1,416]{1,0:T(1,128)} %param.7) | copy-start | bytes 4996
  0.6 27.2 %collective-permute-start = (bf16[416,1152]{1,0:T(8,128)(2,1)}, bf16[416,1152]{1,0:T(8,128)(2,1)S(1)}, u32[]{:S(2)}, u32[]{:S(2)}) collective-permute-start(bf16[416,1152]{1,0:T(8,128)(2,1)} %image_ref.5), channel_id=1, source_target_pairs={{0,3},{1,0},{2,1},{3,2},{4,7},{5,4},{6,5},{7,6},{8,11},{9,8},{10,9... | collective-permute-start | bytes 2875400 | tf_op jit(solution)/shard_map/ppermute | solution.py:17
  4.1 14.3 %collective-permute-start.1 = (bf16[160,1152]{1,0:T(8,128)(2,1)S(1)}, bf16[160,1152]{1,0:T(8,128)(2,1)S(1)}, u32[]{:S(2)}, u32[]{:S(2)}) collective-permute-start(bf16[160,1152]{1,0:T(8,128)(2,1)S(1)} %slice.3.refs_2_), channel_id=1, source_target_pairs={{0,4},{4,8},{8,12},{12,16},{16,20},{20,24},{24,28},{28,0},{1,5},{5... | collective-permute-start | bytes 1105928 | tf_op jit(solution)/shard_map/ppermute | solution.py:17
  5.7 1.2 %copy-start = (bf16[416,1152]{1,0:T(8,128)(2,1)S(1)}, bf16[416,1152]{1,0:T(8,128)(2,1)}, u32[]{:S(2)}) copy-start(bf16[416,1152]{1,0:T(8,128)(2,1)} %refs_1_.1) | copy-start | bytes 2875396
  6.9 4.9 %copy-start.1 = (bf16[416,1152]{1,0:T(8,128)(2,1)S(1)}, bf16[416,1152]{1,0:T(8,128)(2,1)}, u32[]{:S(2)}) copy-start(bf16[416,1152]{1,0:T(8,128)(2,1)} %refs_1_.1) | copy-start | bytes 2875396
  6.9 4.9 %copy-start.2 = (bf16[416,1152]{1,0:T(8,128)(2,1)S(1)}, bf16[416,1152]{1,0:T(8,128)(2,1)}, u32[]{:S(2)}) copy-start(bf16[416,1152]{1,0:T(8,128)(2,1)} %image_ref.5) | copy-start | bytes 2875396
  7.3 20.5 %collective-permute-start.2 = (bf16[192,1152]{1,0:T(8,128)(2,1)S(1)}, bf16[192,1152]{1,0:T(8,128)(2,1)S(1)}, u32[]{:S(2)}, u32[]{:S(2)}) collective-permute-start(bf16[192,1152]{1,0:T(8,128)(2,1)S(1)} %get-tuple-element.18), channel_id=1, source_target_pairs={{0,4},{4,8},{8,12},{12,16},{16,20},{20,24},{24,28},{28,0},{1,5},{5... | collective-permute-start | bytes 1327112 | tf_op jit(solution)/shard_map/ppermute | solution.py:17
  8.9 26.6 %collective-permute-start.3 = (bf16[64,1152]{1,0:T(8,128)(2,1)S(1)}, bf16[64,1152]{1,0:T(8,128)(2,1)S(1)}, u32[]{:S(2)}, u32[]{:S(2)}) collective-permute-start(bf16[64,1152]{1,0:T(8,128)(2,1)S(1)} %get-tuple-element.22), channel_id=1, source_target_pairs={{0,4},{4,8},{8,12},{12,16},{16,20},{20,24},{24,28},{28,0},{1,5},{5... | collective-permute-start | bytes 442376 | tf_op jit(solution)/shard_map/ppermute | solution.py:17
  29.1 11.7 %collective-permute-start.7 = (bf16[160,1152]{1,0:T(8,128)(2,1)S(1)}, bf16[160,1152]{1,0:T(8,128)(2,1)S(1)}, u32[]{:S(2)}, u32[]{:S(2)}) collective-permute-start(bf16[160,1152]{1,0:T(8,128)(2,1)S(1)} %get-tuple-element.20.refs_0_), channel_id=1, source_target_pairs={{0,28},{4,0},{8,4},{12,8},{16,12},{20,16},{24,20},{28,24},{1,29},{... | collective-permute-start | bytes 1105928 | tf_op jit(solution)/shard_map/ppermute | solution.py:17
  32.4 16.2 %collective-permute-start.6 = (bf16[192,1152]{1,0:T(8,128)(2,1)S(1)}, bf16[192,1152]{1,0:T(8,128)(2,1)S(1)}, u32[]{:S(2)}, u32[]{:S(2)}) collective-permute-start(bf16[192,1152]{1,0:T(8,128)(2,1)S(1)} %get-tuple-element.23.refs_0_), channel_id=1, source_target_pairs={{0,28},{4,0},{8,4},{12,8},{16,12},{20,16},{24,20},{28,24},{1,29},{... | collective-permute-start | bytes 1327112 | tf_op jit(solution)/shard_map/ppermute | solution.py:17
  38.1 13.3 %collective-permute-start.4 = (bf16[416,1152]{1,0:T(8,128)(2,1)S(1)}, bf16[416,1152]{1,0:T(8,128)(2,1)S(1)}, u32[]{:S(2)}, u32[]{:S(2)}) collective-permute-start(bf16[416,1152]{1,0:T(8,128)(2,1)S(1)} %fusion.5), channel_id=1, source_target_pairs={{0,1},{1,2},{2,3},{3,0},{4,5},{5,6},{6,7},{7,4},{8,9},{9,10},{10,1... | collective-permute-start | bytes 2875400 | tf_op jit(solution)/shard_map/ppermute | solution.py:17
  38.2 14.3 %collective-permute-start.5 = (bf16[64,1152]{1,0:T(8,128)(2,1)S(1)}, bf16[64,1152]{1,0:T(8,128)(2,1)S(1)}, u32[]{:S(2)}, u32[]{:S(2)}) collective-permute-start(bf16[64,1152]{1,0:T(8,128)(2,1)S(1)} %get-tuple-element.29), channel_id=1, source_target_pairs={{0,28},{4,0},{8,4},{12,8},{16,12},{20,16},{24,20},{28,24},{1,29},{... | collective-permute-start | bytes 442376 | tf_op jit(solution)/shard_map/ppermute | solution.py:17

commit v5 on v4

v5 whole, which is shorter than its diff:
```python
import jax
import jax.numpy as jnp
from jax import lax
from jax.experimental import pallas as pl
from jax.experimental.pallas import tpu as pltpu
from jax.sharding import PartitionSpec as P

MIB = 2**20
SMEM = pl.BlockSpec(memory_space=pltpu.SMEM)
VMEM = pl.BlockSpec(memory_space=pltpu.VMEM)
HBM = pl.BlockSpec(memory_space=pltpu.HBM)
ANY = pl.BlockSpec(memory_space=pl.ANY)


def shifted(shard, axis, by):
    devices = lax.axis_size(axis)
    return lax.ppermute(shard, axis, [(i, (i + by) % devices) for i in range(devices)])


def dot_nt(a, b):
    return lax.dot_general(a, b, (((1,), (1,)), ((), ())), preferred_element_type=jnp.float32)


def dot_tn(a, b):
    return lax.dot_general(a, b, (((0,), (0,)), ((), ())), preferred_element_type=jnp.float32)


def dot_nn(a, b):
    return jnp.dot(a, b, preferred_element_type=jnp.float32)


def row_cuts(rows):
    tiles = rows // 16
    cuts = [0, tiles * 6 // 26 * 16, tiles * 16 // 26 * 16, tiles * 23 // 26 * 16, rows]
    return list(zip(cuts[:-1], cuts[1:]))


def fetch(array, lo, hi, after):
    def kernel(array_ref, *refs):
        out_ref, sem = refs[-2:]
        copy = pltpu.make_async_copy(array_ref.at[pl.ds(lo, hi - lo), :], out_ref, sem)
        copy.start()
        copy.wait()

    return pl.pallas_call(
        kernel,
        out_shape=jax.ShapeDtypeStruct((hi - lo, array.shape[1]), array.dtype),
        in_specs=[ANY] * (1 + len(after)),
        out_specs=VMEM,
        scratch_shapes=[pltpu.SemaphoreType.DMA],
        compiler_params=pltpu.CompilerParams(vmem_limit_bytes=2 * MIB),
        name="fetch",
    )(array, *after)


def pass_on(array, after):
    return pl.pallas_call(
        lambda *refs: None,
        out_shape=jax.ShapeDtypeStruct(array.shape, array.dtype),
        in_specs=[ANY] * (1 + len(after)),
        out_specs=ANY,
        input_output_aliases={0: 0},
        compiler_params=pltpu.CompilerParams(vmem_limit_bytes=MIB),
        name="pass_on",
    )(array, *after)


def chunk_kernel(scale_ref, bias_ref, image_ref, next_ref, upper_ref, lower_ref, *refs):
    sent_ref, joined_ref, own_ref, other_ref = refs[-4:]
    scale, bias = scale_ref[0], bias_ref[0]
    rows = upper_ref.shape[0]
    joined_ref[:rows, :] = upper_ref[...]
    joined_ref[rows:, :] = lower_ref[...]
    part = joined_ref[...]
    image = image_ref[...]
    own = jax.nn.sigmoid(dot_nt(part, image) * scale + bias).astype(jnp.bfloat16)
    own_ref[...] = own
    total = dot_nn(own, image)
    image = next_ref[...]
    other = jax.nn.sigmoid(dot_nt(part, image) * scale + bias).astype(jnp.bfloat16)
    other_ref[...] = other
    total += dot_nn(other, image)
    sent_ref[...] = (scale * total).astype(jnp.bfloat16)


def chunk(factor, shift, image, image_next, upper, lower, after):
    rows, width = upper.shape[0] + lower.shape[0], upper.shape[1]
    columns = image.shape[0]
    text = jax.ShapeDtypeStruct((rows, width), jnp.bfloat16)
    tile = jax.ShapeDtypeStruct((rows, columns), jnp.bfloat16)
    return pl.pallas_call(
        chunk_kernel,
        out_shape=(text, text, tile, tile),
        in_specs=[SMEM] * 2 + [VMEM] * 4 + [ANY] * len(after),
        out_specs=(VMEM,) * 4,
        compiler_params=pltpu.CompilerParams(vmem_limit_bytes=16 * MIB),
        cost_estimate=pl.CostEstimate(
            flops=8 * rows * columns * width,
            bytes_accessed=2 * (2 * columns + 3 * rows) * width,
            transcendentals=2 * rows * columns,
        ),
        name="chunk",
    )(factor, shift, image, image_next, upper, lower, *after)


def add_rows(total, back, lo, result, after, mark=False):
    rows, width = back.shape
    step = rows // 16 // 3 * 16 if rows >= 96 else rows
    cuts = [(i, min(i + step, rows)) for i in range(0, rows, step)]

    def kernel(total_ref, back_ref, *refs):
        buffer, sems = refs[-2:]
        result_ref = refs[-4] if mark else refs[-3]
        copies = []
        for i, (a, b) in enumerate(cuts):
            buffer[a:b, :] = (total_ref[lo + a : lo + b, :] + back_ref[a:b, :].astype(jnp.float32)).astype(jnp.bfloat16)
            copies.append(
                pltpu.make_async_copy(
                    buffer.at[pl.ds(a, b - a), :], result_ref.at[pl.ds(lo + a, b - a), :], sems.at[i]
                )
            )
            copies[-1].start()
        if mark:
            refs[-3][...] = jnp.zeros((8, 128), jnp.float32)
        for copy in copies:
            copy.wait()

    kept = [] if result is None else [result]
    out = jax.ShapeDtypeStruct(total.shape, jnp.bfloat16)
    return pl.pallas_call(
        kernel,
        out_shape=(out, jax.ShapeDtypeStruct((8, 128), jnp.float32)) if mark else out,
        in_specs=[VMEM, VMEM] + [HBM] * len(kept) + [ANY] * len(after),
        out_specs=(HBM, VMEM) if mark else HBM,
        scratch_shapes=[pltpu.VMEM((rows, width), jnp.bfloat16), pltpu.SemaphoreType.DMA((len(cuts),))],
        input_output_aliases={2: 0} if kept else {},
        compiler_params=pltpu.CompilerParams(vmem_limit_bytes=4 * MIB),
        name="add_rows",
    )(total, back, *kept, *after)


def body(image, text, target, factor, shift):
    scale = factor[0]
    bias = shift[0]
    cuts = row_cuts(text.shape[0])
    first = text[: cuts[0][1]]
    part = [shifted(first, "blk", 1)]
    image_next = shifted(image, "grp", -1)
    part.append(shifted(fetch(text, *cuts[1], [first]), "blk", 1))

    target = fetch(target, 0, 1, [part[0]])
    part.append(shifted(fetch(text, *cuts[2], [target]), "blk", 1))
    own = jax.nn.sigmoid(dot_nt(image, text) * scale + bias)
    column = lax.broadcasted_iota(jnp.int32, own.shape, 1)
    own = (own - (column == target[0][:, None]).astype(jnp.float32)).astype(jnp.bfloat16)
    part.append(shifted(fetch(text, *cuts[3], [own]), "blk", 1))
    image_grad = dot_nn(own, text)
    text_grad = dot_tn(own, image)

    image_next = pass_on(image_next, [image_grad, text_grad])
    sent0, part0, own0, next0 = chunk(factor, shift, image, image_next, part[0], part[1], [])
    next_own = jax.nn.sigmoid(dot_nt(image_next, text) * scale + bias).astype(jnp.bfloat16)
    text_grad = scale * (text_grad + dot_tn(next_own, image_next))
    image_sent = dot_nn(next_own, text) + dot_tn(next0, part0)
    image_grad = image_grad + dot_tn(own0, part0)

    sent0 = pass_on(sent0, [part[2], image_sent])
    back0 = shifted(sent0, "blk", -1)

    sent1, part1, own1, next1 = chunk(factor, shift, image, image_next, part[2], part[3], [sent0])
    image_sent = (scale * (image_sent + dot_tn(next1, part1))).astype(jnp.bfloat16)
    image_back = shifted(image_sent, "grp", 1)
    sent1 = pass_on(sent1, [image_sent])
    back1 = shifted(sent1, "blk", -1)
    image_grad = scale * (image_grad + dot_tn(own1, part1))

    result = add_rows(text_grad, back0, 0, None, [])
    image_grad, mark = add_rows(image_grad, image_back, 0, None, [], mark=True)
    result = add_rows(text_grad, back1, cuts[2][0], result, [mark])
    return image_grad, result


def solution(mesh):
    block = P(("blk", "grp"), None)
    return jax.shard_map(
        body, mesh=mesh, in_specs=(block, block, block, P(), P()), out_specs=(block, block), check_vma=False
    )
```

time: 54 us -> 50.4 us (0.933)
  Pallas kernels: 9.38 us -> 6.28 us
  waiting for transfers between devices: 21.5 us -> 22.6 us
  matrix products: 7.46 us -> 6.58 us
  starting transfers between devices: 11 us -> 10.4 us
    pallas_call x8 -> x12, Pallas kernels: 9.38 us -> 6.28 us  [the longest x2 2.9 us: chunk(): pl.pallas_call(chunk_kernel, out_shape=(text, text, tile, tile), in_specs...]
    ppermute x8, waiting for transfers between devices: 21.5 us -> 22.6 us  [shifted(): lax.ppermute(shard, axis, [(i, (i + by) % devices) for i in range(devices)])]
    dot_general x8 -> x6, matrix products: 4.35 us -> 3.45 us  [dot_tn(): lax.dot_general(a, b, (((0,), (0,)), ((), ())), preferred_element_type=jn...]
    ppermute x8, starting transfers between devices: 11 us -> 10.4 us  [shifted(): lax.ppermute(shard, axis, [(i, (i + by) % devices) for i in range(devices)])]
  transfers between devices with their start and end apart: 8 -> 8, of which waited for: 4 -> 5; matrix products, arithmetic and copies ran while one was open for 16% -> 13% of each run, Pallas kernels for 15% -> 11%
where the time goes in v5:
time: 50.4 us; the launch traced here: 50.2 us
  waiting for transfers between devices  22.6 us (45%)
  starting transfers between devices  10.4 us (21%)
  matrix products  6.58 us (13%)
  Pallas kernels  6.28 us (12%)
  local copies, waits for them, and re-layouts  2.16 us (4%)
  between operations  2.14 us (4%)
    ppermute x8, waiting for transfers between devices, shifted(): lax.ppermute(shard, axis, [(i, (i + by) % devices) for i in range(devices)])  22.6 us
    ppermute x8, starting transfers between devices, shifted(): lax.ppermute(shard, axis, [(i, (i + by) % devices) for i in range(devices)])  10.4 us
    dot_general x6, matrix products, dot_tn(): lax.dot_general(a, b, (((0,), (0,)), ((), ())), preferred_element_type=jn...  3.45 us
    pallas_call x2, Pallas kernels, chunk(): pl.pallas_call(chunk_kernel, out_shape=(text, text, tile, tile), in_specs...  2.9 us
    pallas_call x3, Pallas kernels, add_rows(): pl.pallas_call(kernel, out_shape=(out, jax.ShapeDtypeStruct((8, 128), jnp...  2.71 us
    dot_general x2, matrix products, dot_nt(): lax.dot_general(a, b, (((1,), (1,)), ((), ())), preferred_element_type=jn...  1.72 us
    dot_general x2, matrix products, dot_nn(): return jnp.dot(a, b, preferred_element_type=jnp.float32)  1.4 us
    unnamed x8, local copies, waits for them, and re-layouts  1.2 us
  transfers between devices with their start and end apart: 8, of which 5 were waited for; matrix products, arithmetic and copies ran while one was open for 13% of the time, Pallas kernels for 11%

profile of v5, /device:TPU:0, one launch (start us, length us, event | category | flops | bytes accessed | tf_op | source)
XLA Modules:
  0.0 50.2 jit_solution(7520454354852342047)
XLA Ops:
  0.6 1.0 %slice.3.refs_0_ = bf16[96,1152]{1,0:T(8,128)(2,1)S(1)} slice(bf16[416,1152]{1,0:T(8,128)(2,1)} %array_ref.7), slice={[0:96], [0:1152]} | slice | bytes 442368 | tf_op jit(solution)/shard_map/slice | solution.py:146
  1.6 3.0 %collective-permute-start = (bf16[96,1152]{1,0:T(8,128)(2,1)S(1)}, bf16[96,1152]{1,0:T(8,128)(2,1)S(1)}, u32[]{:S(2)}, u32[]{:S(2)}) collective-permute-start(bf16[96,1152]{1,0:T(8,128)(2,1)S(1)} %slice.3.refs_0_), channel_id=1, source_target_pairs={{0,4},{4,8},{8,12},{12,16},{16,20},{20,24},{24,28},{28,0},{1,5},{5... | collective-permute-start | bytes 663560 | tf_op jit(solution)/shard_map/ppermute | solution.py:17
  4.6 0.7 %collective-permute-start.1 = (bf16[416,1152]{1,0:T(8,128)(2,1)}, bf16[416,1152]{1,0:T(8,128)(2,1)S(1)}, u32[]{:S(2)}, u32[]{:S(2)}) collective-permute-start(bf16[416,1152]{1,0:T(8,128)(2,1)} %image_ref.3), channel_id=1, source_target_pairs={{0,3},{1,0},{2,1},{3,2},{4,7},{5,4},{6,5},{7,6},{8,11},{9,8},{10,9... | collective-permute-start | bytes 2875400 | tf_op jit(solution)/shard_map/ppermute | solution.py:17
  5.3 1.2 %copy-done = bf16[416,1152]{1,0:T(8,128)(2,1)S(1)} copy-done((bf16[416,1152]{1,0:T(8,128)(2,1)S(1)}, bf16[416,1152]{1,0:T(8,128)(2,1)}, u32[]{:S(2)}) %copy-start) | copy-done | bytes 958488
  6.5 0.2 fetch.5
  6.6 1.6 %collective-permute-start.2 = (bf16[160,1152]{1,0:T(8,128)(2,1)S(1)}, bf16[160,1152]{1,0:T(8,128)(2,1)S(1)}, u32[]{:S(2)}, u32[]{:S(2)}) collective-permute-start(bf16[160,1152]{1,0:T(8,128)(2,1)S(1)} %fetch.5), channel_id=1, source_target_pairs={{0,4},{4,8},{8,12},{12,16},{16,20},{20,24},{24,28},{28,0},{1,5},{5... | collective-permute-start | bytes 1105928 | tf_op jit(solution)/shard_map/ppermute | solution.py:17
  9.5 4.3 %collective-permute-done.refs_0_.upper_ref = bf16[96,1152]{1,0:T(8,128)(2,1)S(1)} collective-permute-done((bf16[96,1152]{1,0:T(8,128)(2,1)S(1)}, bf16[96,1152]{1,0:T(8,128)(2,1)S(1)}, u32[]{:S(2)}, u32[]{:S(2)}) %collective-permute-start) | collective-permute-done | bytes 221216 | tf_op jit(solution)/shard_map/ppermute | solution.py:17
  13.9 0.3 fetch.6
  14.3 0.1 collective-permute-start.3
  14.3 0.9 %subtract_convert_fusion.refs_0_ = bf16[416,416]{1,0:T(8,128)(2,1)S(1)} fusion(s32[416]{0:T(512)S(1)} %bitcast.30, f32[]{:T(128)} %bitcast.28, bf16[416,1152]{1,0:T(8,128)(2,1)S(1)} %copy-done.2, bf16[416,1152]{1,0:T(8,128)(2,1)S(1)} %copy-done.1, f32[]{:T(128)} %bitcast.24), kind=kOutput, calls=%fused_computation.22 | convolution fusion | flops 400278528 | bytes 2264712 | tf_op jit(solution)/shard_map/dot_general | solution.py:21
  15.2 0.2 fetch.7
  15.4 1.5 %collective-permute-start.4 = (bf16[48,1152]{1,0:T(8,128)(2,1)S(1)}, bf16[48,1152]{1,0:T(8,128)(2,1)S(1)}, u32[]{:S(2)}, u32[]{:S(2)}) collective-permute-start(bf16[48,1152]{1,0:T(8,128)(2,1)S(1)} %fetch.7), channel_id=1, source_target_pairs={{0,4},{4,8},{8,12},{12,16},{16,20},{20,24},{24,28},{28,0},{1,5},{5... | collective-permute-start | bytes 331784 | tf_op jit(solution)/shard_map/ppermute | solution.py:17
  16.9 0.7 %fusion.16.refs_2_ = f32[416,1152]{1,0:T(8,128)S(1)} fusion(bf16[416,416]{1,0:T(8,128)(2,1)S(1)} %subtract_convert_fusion.refs_0_, bf16[416,1152]{1,0:T(8,128)(2,1)S(1)} %copy-done.2), kind=kOutput, calls=%fused_computation.25 | convolution fusion | flops 398721024 | bytes 3221504 | tf_op jit(solution)/shard_map/dot_general | solution.py:25
  17.6 0.7 %fusion.15.refs_1_ = f32[416,1152]{1,0:T(8,128)S(1)} fusion(bf16[416,416]{1,0:T(8,128)(2,1)S(1)} %subtract_convert_fusion.refs_0_, bf16[416,1152]{1,0:T(8,128)(2,1)S(1)} %copy-done.1), kind=kOutput, calls=%fused_computation.24 | convolution fusion | flops 398721024 | bytes 3221504 | tf_op jit(solution)/shard_map/dot_general | solution.py:29
  18.4 0.8 %fusion.14 = bf16[416,416]{1,0:T(8,128)(2,1)S(1)} fusion(bf16[416,1152]{1,0:T(8,128)(2,1)S(1)} %pass_on.3.next_ref, bf16[416,1152]{1,0:T(8,128)(2,1)S(1)} %copy-done.1, f32[]{:T(128)} %bitcast.29, f32[]{:T(128)} %bitcast.27), kind=kOutput, calls=%fused_computation.21 | convolution fusion | flops 399759360 | bytes 2263048 | tf_op jit(solution)/shard_map/dot_general | solution.py:21
  19.2 0.7 %fusion.17 = f32[416,1152]{1,0:T(8,128)S(1)} fusion(bf16[416,416]{1,0:T(8,128)(2,1)S(1)} %fusion.14, bf16[416,1152]{1,0:T(8,128)(2,1)S(1)} %copy-done.1), kind=kOutput, calls=%fused_computation.26 | convolution fusion | flops 398721024 | bytes 3221504 | tf_op jit(solution)/shard_map/dot_general | solution.py:29
  19.9 1.9 %collective-permute-done.2.lower_ref = bf16[160,1152]{1,0:T(8,128)(2,1)S(1)} collective-permute-done((bf16[160,1152]{1,0:T(8,128)(2,1)S(1)}, bf16[160,1152]{1,0:T(8,128)(2,1)S(1)}, u32[]{:S(2)}, u32[]{:S(2)}) %collective-permute-start.2) | collective-permute-done | bytes 368672 | tf_op jit(solution)/shard_map/ppermute | solution.py:17
  21.8 1.6 %chunk.2 = (bf16[256,1152]{1,0:T(8,128)(2,1)S(1)}, bf16[256,1152]{1,0:T(8,128)(2,1)S(1)}, bf16[256,416]{1,0:T(8,128)(2,1)S(1)}, bf16[256,416]{1,0:T(8,128)(2,1)S(1)}) custom-call(f32[1]{0:T(128)} %copy.15.scale_ref, f32[1]{0:T(128)} %copy.16.bias_ref, bf16[416,1152]{1,0:T(8,128)(2,1)S(1)} %copy-done.2, bf16[416,1152]{1,0:T(8,128)(2,1)S(1)} %pass_on.3.next_ref, ...), custom_call_target="tpu_custom_call" | custom-call | flops 981467136 | bytes 3686400 | tf_op jit(solution)/shard_map/chunk/pallas_call | solution.py:91
  23.4 0.5 convolution_add_fusion.3.refs_2_
  23.9 3.4 %collective-permute-done.3.refs_1_.upper_ref = bf16[112,1152]{1,0:T(8,128)(2,1)S(1)} collective-permute-done((bf16[112,1152]{1,0:T(8,128)(2,1)S(1)}, bf16[112,1152]{1,0:T(8,128)(2,1)S(1)}, u32[]{:S(2)}, u32[]{:S(2)}) %collective-permute-start.3) | collective-permute-done | bytes 258080 | tf_op jit(solution)/shard_map/ppermute | solution.py:17
  27.3 2.1 %collective-permute-start.7 = (bf16[256,1152]{1,0:T(8,128)(2,1)S(1)}, bf16[256,1152]{1,0:T(8,128)(2,1)S(1)}, u32[]{:S(2)}, u32[]{:S(2)}) collective-permute-start(bf16[256,1152]{1,0:T(8,128)(2,1)S(1)} %pass_on.4.refs_0_), channel_id=1, source_target_pairs={{0,28},{4,0},{8,4},{12,8},{16,12},{20,16},{24,20},{28,24},{1,29},{... | collective-permute-start | bytes 1769480 | tf_op jit(solution)/shard_map/ppermute | solution.py:17
  29.4 1.3 %chunk.3 = (bf16[160,1152]{1,0:T(8,128)(2,1)S(1)}, bf16[160,1152]{1,0:T(8,128)(2,1)S(1)}, bf16[160,416]{1,0:T(8,128)(2,1)S(1)}, bf16[160,416]{1,0:T(8,128)(2,1)S(1)}) custom-call(f32[1]{0:T(128)} %copy.15.scale_ref, f32[1]{0:T(128)} %copy.16.bias_ref, bf16[416,1152]{1,0:T(8,128)(2,1)S(1)} %copy-done.2, bf16[416,1152]{1,0:T(8,128)(2,1)S(1)} %pass_on.3.next_ref, ...), custom_call_target="tpu_custom_call" | custom-call | flops 613416960 | bytes 3022848 | tf_op jit(solution)/shard_map/chunk/pallas_call | solution.py:91
  30.7 0.5 fusion.3.refs_1_
  31.2 1.5 %collective-permute-start.6 = (bf16[160,1152]{1,0:T(8,128)(2,1)S(1)}, bf16[160,1152]{1,0:T(8,128)(2,1)S(1)}, u32[]{:S(2)}, u32[]{:S(2)}) collective-permute-start(bf16[160,1152]{1,0:T(8,128)(2,1)S(1)} %pass_on.5), channel_id=1, source_target_pairs={{0,28},{4,0},{8,4},{12,8},{16,12},{20,16},{24,20},{28,24},{1,29},{... | collective-permute-start | bytes 1105928 | tf_op jit(solution)/shard_map/ppermute | solution.py:17
  32.7 0.5 convolution_add_fusion.4
  33.2 0.5 fusion.2.total_ref
  33.7 0.7 %fusion.total_ref = f32[416,1152]{1,0:T(8,128)S(1)} fusion(f32[416,1152]{1,0:T(8,128)S(1)} %fusion.16.refs_2_, bf16[416,416]{1,0:T(8,128)(2,1)S(1)} %fusion.14, bf16[416,1152]{1,0:T(8,128)(2,1)S(1)} %pass_on.3.next_ref, f32[]{:T(128)} %bitcast.25), kind=kOutput, calls=%fused_computation.1 | convolution fusion | flops 399679488 | bytes 5138436 | tf_op jit(solution)/shard_map/dot_general | solution.py:25
  34.5 9.1 %collective-permute-done.7.back_ref = bf16[256,1152]{1,0:T(8,128)(2,1)S(1)} collective-permute-done((bf16[256,1152]{1,0:T(8,128)(2,1)S(1)}, bf16[256,1152]{1,0:T(8,128)(2,1)S(1)}, u32[]{:S(2)}, u32[]{:S(2)}) %collective-permute-start.7) | collective-permute-done | bytes 589856 | tf_op jit(solution)/shard_map/ppermute | solution.py:17
  43.6 0.9 %add_rows.4.refs_0_ = bf16[416,1152]{1,0:T(8,128)(2,1)} custom-call(f32[416,1152]{1,0:T(8,128)S(1)} %fusion.total_ref, bf16[256,1152]{1,0:T(8,128)(2,1)S(1)} %collective-permute-done.7.back_ref), custom_call_target="tpu_custom_call" | custom-call | tf_op jit(solution)/shard_map/add_rows/pallas_call | solution.py:130
  44.5 1.0 %add_rows.3 = (bf16[416,1152]{1,0:T(8,128)(2,1)}, f32[8,128]{1,0:T(8,128)S(1)}) custom-call(f32[416,1152]{1,0:T(8,128)S(1)} %fusion.2.total_ref, bf16[416,1152]{1,0:T(8,128)(2,1)S(1)} %collective-permute-done.5.back_ref), custom_call_target="tpu_custom_call" | custom-call | tf_op jit(solution)/shard_map/add_rows/pallas_call | solution.py:130
  45.5 3.9 %collective-permute-done.6.back_ref = bf16[160,1152]{1,0:T(8,128)(2,1)S(1)} collective-permute-done((bf16[160,1152]{1,0:T(8,128)(2,1)S(1)}, bf16[160,1152]{1,0:T(8,128)(2,1)S(1)}, u32[]{:S(2)}, u32[]{:S(2)}) %collective-permute-start.6) | collective-permute-done | bytes 368672 | tf_op jit(solution)/shard_map/ppermute | solution.py:17
  49.4 0.8 %add_rows.5 = bf16[416,1152]{1,0:T(8,128)(2,1)} custom-call(f32[416,1152]{1,0:T(8,128)S(1)} %fusion.total_ref, bf16[160,1152]{1,0:T(8,128)(2,1)S(1)} %collective-permute-done.6.back_ref, bf16[416,1152]{1,0:T(8,128)(2,1)} %add_rows.4.refs_0_, f32[8,128]{1,0:T(8,128)S(1)} %get-tuple-element.21.refs_1_), custom_call_target="tpu_custom_call", output_to_operand_aliasing={{}: (2, {})} | custom-call | tf_op jit(solution)/shard_map/add_rows/pallas_call | solution.py:130
  (15 shorter events, 0.1 us)
Async XLA Ops:
  0.6 13.3 %copy-start.3 = (s32[1,416]{1,0:T(1,128)S(1)}, s32[1,416]{1,0:T(1,128)}, u32[]{:S(2)}) copy-start(s32[1,416]{1,0:T(1,128)} %array_ref.4) | copy-start | bytes 4996
  1.6 12.3 %collective-permute-start = (bf16[96,1152]{1,0:T(8,128)(2,1)S(1)}, bf16[96,1152]{1,0:T(8,128)(2,1)S(1)}, u32[]{:S(2)}, u32[]{:S(2)}) collective-permute-start(bf16[96,1152]{1,0:T(8,128)(2,1)S(1)} %slice.3.refs_0_), channel_id=1, source_target_pairs={{0,4},{4,8},{8,12},{12,16},{16,20},{20,24},{24,28},{28,0},{1,5},{5... | collective-permute-start | bytes 663560 | tf_op jit(solution)/shard_map/ppermute | solution.py:17
  4.6 13.8 %collective-permute-start.1 = (bf16[416,1152]{1,0:T(8,128)(2,1)}, bf16[416,1152]{1,0:T(8,128)(2,1)S(1)}, u32[]{:S(2)}, u32[]{:S(2)}) collective-permute-start(bf16[416,1152]{1,0:T(8,128)(2,1)} %image_ref.3), channel_id=1, source_target_pairs={{0,3},{1,0},{2,1},{3,2},{4,7},{5,4},{6,5},{7,6},{8,11},{9,8},{10,9... | collective-permute-start | bytes 2875400 | tf_op jit(solution)/shard_map/ppermute | solution.py:17
  5.3 1.2 %copy-start = (bf16[416,1152]{1,0:T(8,128)(2,1)S(1)}, bf16[416,1152]{1,0:T(8,128)(2,1)}, u32[]{:S(2)}) copy-start(bf16[416,1152]{1,0:T(8,128)(2,1)} %array_ref.7) | copy-start | bytes 2875396
  6.5 7.4 %copy-start.1 = (bf16[416,1152]{1,0:T(8,128)(2,1)S(1)}, bf16[416,1152]{1,0:T(8,128)(2,1)}, u32[]{:S(2)}) copy-start(bf16[416,1152]{1,0:T(8,128)(2,1)} %array_ref.7) | copy-start | bytes 2875396
  6.5 7.9 %copy-start.2 = (bf16[416,1152]{1,0:T(8,128)(2,1)S(1)}, bf16[416,1152]{1,0:T(8,128)(2,1)}, u32[]{:S(2)}) copy-start(bf16[416,1152]{1,0:T(8,128)(2,1)} %image_ref.3) | copy-start | bytes 2875396
  6.6 15.1 %collective-permute-start.2 = (bf16[160,1152]{1,0:T(8,128)(2,1)S(1)}, bf16[160,1152]{1,0:T(8,128)(2,1)S(1)}, u32[]{:S(2)}, u32[]{:S(2)}) collective-permute-start(bf16[160,1152]{1,0:T(8,128)(2,1)S(1)} %fetch.5), channel_id=1, source_target_pairs={{0,4},{4,8},{8,12},{12,16},{16,20},{20,24},{24,28},{28,0},{1,5},{5... | collective-permute-start | bytes 1105928 | tf_op jit(solution)/shard_map/ppermute | solution.py:17
  14.3 13.0 %collective-permute-start.3 = (bf16[112,1152]{1,0:T(8,128)(2,1)S(1)}, bf16[112,1152]{1,0:T(8,128)(2,1)S(1)}, u32[]{:S(2)}, u32[]{:S(2)}) collective-permute-start(bf16[112,1152]{1,0:T(8,128)(2,1)S(1)} %fetch.6), channel_id=1, source_target_pairs={{0,4},{4,8},{8,12},{12,16},{16,20},{20,24},{24,28},{28,0},{1,5},{5... | collective-permute-start | bytes 774152 | tf_op jit(solution)/shard_map/ppermute | solution.py:17
  15.4 14.0 %collective-permute-start.4 = (bf16[48,1152]{1,0:T(8,128)(2,1)S(1)}, bf16[48,1152]{1,0:T(8,128)(2,1)S(1)}, u32[]{:S(2)}, u32[]{:S(2)}) collective-permute-start(bf16[48,1152]{1,0:T(8,128)(2,1)S(1)} %fetch.7), channel_id=1, source_target_pairs={{0,4},{4,8},{8,12},{12,16},{16,20},{20,24},{24,28},{28,0},{1,5},{5... | collective-permute-start | bytes 331784 | tf_op jit(solution)/shard_map/ppermute | solution.py:17
  27.3 16.3 %collective-permute-start.7 = (bf16[256,1152]{1,0:T(8,128)(2,1)S(1)}, bf16[256,1152]{1,0:T(8,128)(2,1)S(1)}, u32[]{:S(2)}, u32[]{:S(2)}) collective-permute-start(bf16[256,1152]{1,0:T(8,128)(2,1)S(1)} %pass_on.4.refs_0_), channel_id=1, source_target_pairs={{0,28},{4,0},{8,4},{12,8},{16,12},{20,16},{24,20},{28,24},{1,29},{... | collective-permute-start | bytes 1769480 | tf_op jit(solution)/shard_map/ppermute | solution.py:17
  31.2 13.3 %collective-permute-start.5 = (bf16[416,1152]{1,0:T(8,128)(2,1)S(1)}, bf16[416,1152]{1,0:T(8,128)(2,1)S(1)}, u32[]{:S(2)}, u32[]{:S(2)}) collective-permute-start(bf16[416,1152]{1,0:T(8,128)(2,1)S(1)} %fusion.3.refs_1_), channel_id=1, source_target_pairs={{0,1},{1,2},{2,3},{3,0},{4,5},{5,6},{6,7},{7,4},{8,9},{9,10},{10,1... | collective-permute-start | bytes 2875400 | tf_op jit(solution)/shard_map/ppermute | solution.py:17
  31.2 18.2 %collective-permute-start.6 = (bf16[160,1152]{1,0:T(8,128)(2,1)S(1)}, bf16[160,1152]{1,0:T(8,128)(2,1)S(1)}, u32[]{:S(2)}, u32[]{:S(2)}) collective-permute-start(bf16[160,1152]{1,0:T(8,128)(2,1)S(1)} %pass_on.5), channel_id=1, source_target_pairs={{0,28},{4,0},{8,4},{12,8},{16,12},{20,16},{24,20},{28,24},{1,29},{... | collective-permute-start | bytes 1105928 | tf_op jit(solution)/shard_map/ppermute | solution.py:17

commit v6 on v5

--- a/solution.py
+++ b/solution.py
@@ -31,7 +31,7 @@
 
 def row_cuts(rows):
     tiles = rows // 16
-    cuts = [0, tiles * 6 // 26 * 16, tiles * 16 // 26 * 16, tiles * 23 // 26 * 16, rows]
+    cuts = [0, tiles * 6 // 26 * 16, tiles * 16 // 26 * 16, tiles * 20 // 26 * 16, rows]
     return list(zip(cuts[:-1], cuts[1:]))
 
 

time: 50.4 us -> 54.9 us (1.089)
  waiting for transfers between devices: 22.6 us -> 28.5 us
  starting transfers between devices: 10.4 us -> 9 us
    ppermute x8, waiting for transfers between devices: 22.6 us -> 28.5 us  [shifted(): lax.ppermute(shard, axis, [(i, (i + by) % devices) for i in range(devices)])]
    ppermute x8, starting transfers between devices: 10.4 us -> 9 us  [shifted(): lax.ppermute(shard, axis, [(i, (i + by) % devices) for i in range(devices)])]
  transfers between devices with their start and end apart: 8 -> 8, of which waited for: 5 -> 6; matrix products, arithmetic and copies ran while one was open for 13% -> 12% of each run, Pallas kernels for 11% -> 10%
where the time goes in v6:
time: 54.9 us; the launch traced here: 54.7 us
  waiting for transfers between devices  28.5 us (52%)
  starting transfers between devices  9 us (16%)
  matrix products  6.57 us (12%)
  Pallas kernels  6.27 us (11%)
  local copies, waits for them, and re-layouts  2.16 us (4%)
  between operations  2.14 us (4%)
    ppermute x8, waiting for transfers between devices, shifted(): lax.ppermute(shard, axis, [(i, (i + by) % devices) for i in range(devices)])  28.5 us
    ppermute x8, starting transfers between devices, shifted(): lax.ppermute(shard, axis, [(i, (i + by) % devices) for i in range(devices)])  9 us
    dot_general x6, matrix products, dot_tn(): lax.dot_general(a, b, (((0,), (0,)), ((), ())), preferred_element_type=jn...  3.45 us
    pallas_call x2, Pallas kernels, chunk(): pl.pallas_call(chunk_kernel, out_shape=(text, text, tile, tile), in_specs...  2.9 us
    pallas_call x3, Pallas kernels, add_rows(): pl.pallas_call(kernel, out_shape=(out, jax.ShapeDtypeStruct((8, 128), jnp...  2.69 us
    dot_general x2, matrix products, dot_nt(): lax.dot_general(a, b, (((1,), (1,)), ((), ())), preferred_element_type=jn...  1.72 us
    dot_general x2, matrix products, dot_nn(): return jnp.dot(a, b, preferred_element_type=jnp.float32)  1.4 us
    unnamed x8, local copies, waits for them, and re-layouts  1.2 us
  transfers between devices with their start and end apart: 8, of which 6 were waited for; matrix products, arithmetic and copies ran while one was open for 12% of the time, Pallas kernels for 10%

profile of v6, /device:TPU:0, one launch (start us, length us, event | category | flops | bytes accessed | tf_op | source)
XLA Modules:
  0.0 54.7 jit_solution(11135761171665598321)
XLA Ops:
  0.6 1.0 %slice.3.refs_0_ = bf16[96,1152]{1,0:T(8,128)(2,1)S(1)} slice(bf16[416,1152]{1,0:T(8,128)(2,1)} %array_ref.7), slice={[0:96], [0:1152]} | slice | bytes 442368 | tf_op jit(solution)/shard_map/slice | solution.py:146
  1.6 3.0 %collective-permute-start = (bf16[96,1152]{1,0:T(8,128)(2,1)S(1)}, bf16[96,1152]{1,0:T(8,128)(2,1)S(1)}, u32[]{:S(2)}, u32[]{:S(2)}) collective-permute-start(bf16[96,1152]{1,0:T(8,128)(2,1)S(1)} %slice.3.refs_0_), channel_id=1, source_target_pairs={{0,4},{4,8},{8,12},{12,16},{16,20},{20,24},{24,28},{28,0},{1,5},{5... | collective-permute-start | bytes 663560 | tf_op jit(solution)/shard_map/ppermute | solution.py:17
  4.6 0.7 %collective-permute-start.1 = (bf16[416,1152]{1,0:T(8,128)(2,1)}, bf16[416,1152]{1,0:T(8,128)(2,1)S(1)}, u32[]{:S(2)}, u32[]{:S(2)}) collective-permute-start(bf16[416,1152]{1,0:T(8,128)(2,1)} %image_ref.3), channel_id=1, source_target_pairs={{0,3},{1,0},{2,1},{3,2},{4,7},{5,4},{6,5},{7,6},{8,11},{9,8},{10,9... | collective-permute-start | bytes 2875400 | tf_op jit(solution)/shard_map/ppermute | solution.py:17
  5.3 1.2 %copy-done = bf16[416,1152]{1,0:T(8,128)(2,1)S(1)} copy-done((bf16[416,1152]{1,0:T(8,128)(2,1)S(1)}, bf16[416,1152]{1,0:T(8,128)(2,1)}, u32[]{:S(2)}) %copy-start) | copy-done | bytes 958488
  6.5 0.2 fetch.5
  6.6 1.6 %collective-permute-start.2 = (bf16[160,1152]{1,0:T(8,128)(2,1)S(1)}, bf16[160,1152]{1,0:T(8,128)(2,1)S(1)}, u32[]{:S(2)}, u32[]{:S(2)}) collective-permute-start(bf16[160,1152]{1,0:T(8,128)(2,1)S(1)} %fetch.5), channel_id=1, source_target_pairs={{0,4},{4,8},{8,12},{12,16},{16,20},{20,24},{24,28},{28,0},{1,5},{5... | collective-permute-start | bytes 1105928 | tf_op jit(solution)/shard_map/ppermute | solution.py:17
  9.5 4.3 %collective-permute-done.refs_0_.upper_ref = bf16[96,1152]{1,0:T(8,128)(2,1)S(1)} collective-permute-done((bf16[96,1152]{1,0:T(8,128)(2,1)S(1)}, bf16[96,1152]{1,0:T(8,128)(2,1)S(1)}, u32[]{:S(2)}, u32[]{:S(2)}) %collective-permute-start) | collective-permute-done | bytes 221216 | tf_op jit(solution)/shard_map/ppermute | solution.py:17
  13.9 0.2 fetch.6
  14.1 0.1 collective-permute-start.3
  14.2 0.9 %subtract_convert_fusion.refs_0_ = bf16[416,416]{1,0:T(8,128)(2,1)S(1)} fusion(s32[416]{0:T(512)S(1)} %bitcast.30, f32[]{:T(128)} %bitcast.28, bf16[416,1152]{1,0:T(8,128)(2,1)S(1)} %copy-done.2, bf16[416,1152]{1,0:T(8,128)(2,1)S(1)} %copy-done.1, f32[]{:T(128)} %bitcast.24), kind=kOutput, calls=%fused_computation.22 | convolution fusion | flops 400278528 | bytes 2264712 | tf_op jit(solution)/shard_map/dot_general | solution.py:21
  15.1 0.3 fetch.7
  15.4 1.5 %collective-permute-start.4 = (bf16[96,1152]{1,0:T(8,128)(2,1)S(1)}, bf16[96,1152]{1,0:T(8,128)(2,1)S(1)}, u32[]{:S(2)}, u32[]{:S(2)}) collective-permute-start(bf16[96,1152]{1,0:T(8,128)(2,1)S(1)} %fetch.7), channel_id=1, source_target_pairs={{0,4},{4,8},{8,12},{12,16},{16,20},{20,24},{24,28},{28,0},{1,5},{5... | collective-permute-start | bytes 663560 | tf_op jit(solution)/shard_map/ppermute | solution.py:17
  16.9 0.7 %fusion.16.refs_2_ = f32[416,1152]{1,0:T(8,128)S(1)} fusion(bf16[416,416]{1,0:T(8,128)(2,1)S(1)} %subtract_convert_fusion.refs_0_, bf16[416,1152]{1,0:T(8,128)(2,1)S(1)} %copy-done.2), kind=kOutput, calls=%fused_computation.25 | convolution fusion | flops 398721024 | bytes 3221504 | tf_op jit(solution)/shard_map/dot_general | solution.py:25
  17.6 0.7 %fusion.15.refs_1_ = f32[416,1152]{1,0:T(8,128)S(1)} fusion(bf16[416,416]{1,0:T(8,128)(2,1)S(1)} %subtract_convert_fusion.refs_0_, bf16[416,1152]{1,0:T(8,128)(2,1)S(1)} %copy-done.1), kind=kOutput, calls=%fused_computation.24 | convolution fusion | flops 398721024 | bytes 3221504 | tf_op jit(solution)/shard_map/dot_general | solution.py:29
  18.4 0.8 %fusion.14 = bf16[416,416]{1,0:T(8,128)(2,1)S(1)} fusion(bf16[416,1152]{1,0:T(8,128)(2,1)S(1)} %pass_on.3.next_ref, bf16[416,1152]{1,0:T(8,128)(2,1)S(1)} %copy-done.1, f32[]{:T(128)} %bitcast.29, f32[]{:T(128)} %bitcast.27), kind=kOutput, calls=%fused_computation.21 | convolution fusion | flops 399759360 | bytes 2263048 | tf_op jit(solution)/shard_map/dot_general | solution.py:21
  19.2 0.7 %fusion.17 = f32[416,1152]{1,0:T(8,128)S(1)} fusion(bf16[416,416]{1,0:T(8,128)(2,1)S(1)} %fusion.14, bf16[416,1152]{1,0:T(8,128)(2,1)S(1)} %copy-done.1), kind=kOutput, calls=%fused_computation.26 | convolution fusion | flops 398721024 | bytes 3221504 | tf_op jit(solution)/shard_map/dot_general | solution.py:29
  19.9 1.9 %collective-permute-done.2.lower_ref = bf16[160,1152]{1,0:T(8,128)(2,1)S(1)} collective-permute-done((bf16[160,1152]{1,0:T(8,128)(2,1)S(1)}, bf16[160,1152]{1,0:T(8,128)(2,1)S(1)}, u32[]{:S(2)}, u32[]{:S(2)}) %collective-permute-start.2) | collective-permute-done | bytes 368672 | tf_op jit(solution)/shard_map/ppermute | solution.py:17
  21.8 1.6 %chunk.2 = (bf16[256,1152]{1,0:T(8,128)(2,1)S(1)}, bf16[256,1152]{1,0:T(8,128)(2,1)S(1)}, bf16[256,416]{1,0:T(8,128)(2,1)S(1)}, bf16[256,416]{1,0:T(8,128)(2,1)S(1)}) custom-call(f32[1]{0:T(128)} %copy.15.scale_ref, f32[1]{0:T(128)} %copy.16.bias_ref, bf16[416,1152]{1,0:T(8,128)(2,1)S(1)} %copy-done.2, bf16[416,1152]{1,0:T(8,128)(2,1)S(1)} %pass_on.3.next_ref, ...), custom_call_target="tpu_custom_call" | custom-call | flops 981467136 | bytes 3686400 | tf_op jit(solution)/shard_map/chunk/pallas_call | solution.py:91
  23.4 0.5 convolution_add_fusion.3.refs_2_
  23.9 1.0 %collective-permute-done.3.refs_1_.upper_ref = bf16[64,1152]{1,0:T(8,128)(2,1)S(1)} collective-permute-done((bf16[64,1152]{1,0:T(8,128)(2,1)S(1)}, bf16[64,1152]{1,0:T(8,128)(2,1)S(1)}, u32[]{:S(2)}, u32[]{:S(2)}) %collective-permute-start.3) | collective-permute-done | bytes 147488 | tf_op jit(solution)/shard_map/ppermute | solution.py:17
  24.9 2.1 %collective-permute-start.7 = (bf16[256,1152]{1,0:T(8,128)(2,1)S(1)}, bf16[256,1152]{1,0:T(8,128)(2,1)S(1)}, u32[]{:S(2)}, u32[]{:S(2)}) collective-permute-start(bf16[256,1152]{1,0:T(8,128)(2,1)S(1)} %pass_on.4.refs_0_), channel_id=1, source_target_pairs={{0,28},{4,0},{8,4},{12,8},{16,12},{20,16},{24,20},{28,24},{1,29},{... | collective-permute-start | bytes 1769480 | tf_op jit(solution)/shard_map/ppermute | solution.py:17
  27.0 10.7 %collective-permute-done.4.lower_ref = bf16[96,1152]{1,0:T(8,128)(2,1)S(1)} collective-permute-done((bf16[96,1152]{1,0:T(8,128)(2,1)S(1)}, bf16[96,1152]{1,0:T(8,128)(2,1)S(1)}, u32[]{:S(2)}, u32[]{:S(2)}) %collective-permute-start.4) | collective-permute-done | bytes 221216 | tf_op jit(solution)/shard_map/ppermute | solution.py:17
  37.8 1.3 %chunk.3 = (bf16[160,1152]{1,0:T(8,128)(2,1)S(1)}, bf16[160,1152]{1,0:T(8,128)(2,1)S(1)}, bf16[160,416]{1,0:T(8,128)(2,1)S(1)}, bf16[160,416]{1,0:T(8,128)(2,1)S(1)}) custom-call(f32[1]{0:T(128)} %copy.15.scale_ref, f32[1]{0:T(128)} %copy.16.bias_ref, bf16[416,1152]{1,0:T(8,128)(2,1)S(1)} %copy-done.2, bf16[416,1152]{1,0:T(8,128)(2,1)S(1)} %pass_on.3.next_ref, ...), custom_call_target="tpu_custom_call" | custom-call | flops 613416960 | bytes 3022848 | tf_op jit(solution)/shard_map/chunk/pallas_call | solution.py:91
  39.0 0.5 fusion.3.refs_1_
  39.7 0.5 convolution_add_fusion.4
  40.2 0.5 fusion.2.total_ref
  40.7 0.7 %fusion.total_ref = f32[416,1152]{1,0:T(8,128)S(1)} fusion(f32[416,1152]{1,0:T(8,128)S(1)} %fusion.16.refs_2_, bf16[416,416]{1,0:T(8,128)(2,1)S(1)} %fusion.14, bf16[416,1152]{1,0:T(8,128)(2,1)S(1)} %pass_on.3.next_ref, f32[]{:T(128)} %bitcast.25), kind=kOutput, calls=%fused_computation.1 | convolution fusion | flops 399679488 | bytes 5138436 | tf_op jit(solution)/shard_map/dot_general | solution.py:25
  41.4 0.1 collective-permute-done.7.back_ref
  41.5 0.9 %add_rows.4.refs_0_ = bf16[416,1152]{1,0:T(8,128)(2,1)} custom-call(f32[416,1152]{1,0:T(8,128)S(1)} %fusion.total_ref, bf16[256,1152]{1,0:T(8,128)(2,1)S(1)} %collective-permute-done.7.back_ref), custom_call_target="tpu_custom_call" | custom-call | tf_op jit(solution)/shard_map/add_rows/pallas_call | solution.py:130
  42.4 10.5 %collective-permute-done.5.back_ref = bf16[416,1152]{1,0:T(8,128)(2,1)S(1)} collective-permute-done((bf16[416,1152]{1,0:T(8,128)(2,1)S(1)}, bf16[416,1152]{1,0:T(8,128)(2,1)S(1)}, u32[]{:S(2)}, u32[]{:S(2)}) %collective-permute-start.5) | collective-permute-done | bytes 958496 | tf_op jit(solution)/shard_map/ppermute | solution.py:17
  52.8 1.0 %add_rows.3 = (bf16[416,1152]{1,0:T(8,128)(2,1)}, f32[8,128]{1,0:T(8,128)S(1)}) custom-call(f32[416,1152]{1,0:T(8,128)S(1)} %fusion.2.total_ref, bf16[416,1152]{1,0:T(8,128)(2,1)S(1)} %collective-permute-done.5.back_ref), custom_call_target="tpu_custom_call" | custom-call | tf_op jit(solution)/shard_map/add_rows/pallas_call | solution.py:130
  53.9 0.8 %add_rows.5 = bf16[416,1152]{1,0:T(8,128)(2,1)} custom-call(f32[416,1152]{1,0:T(8,128)S(1)} %fusion.total_ref, bf16[160,1152]{1,0:T(8,128)(2,1)S(1)} %collective-permute-done.6.back_ref, bf16[416,1152]{1,0:T(8,128)(2,1)} %add_rows.4.refs_0_, f32[8,128]{1,0:T(8,128)S(1)} %get-tuple-element.21.refs_1_), custom_call_target="tpu_custom_call", output_to_operand_aliasing={{}: (2, {})} | custom-call | tf_op jit(solution)/shard_map/add_rows/pallas_call | solution.py:130
  (15 shorter events, 0.2 us)
Async XLA Ops:
  0.6 13.3 %copy-start.3 = (s32[1,416]{1,0:T(1,128)S(1)}, s32[1,416]{1,0:T(1,128)}, u32[]{:S(2)}) copy-start(s32[1,416]{1,0:T(1,128)} %array_ref.4) | copy-start | bytes 4996
  1.6 12.3 %collective-permute-start = (bf16[96,1152]{1,0:T(8,128)(2,1)S(1)}, bf16[96,1152]{1,0:T(8,128)(2,1)S(1)}, u32[]{:S(2)}, u32[]{:S(2)}) collective-permute-start(bf16[96,1152]{1,0:T(8,128)(2,1)S(1)} %slice.3.refs_0_), channel_id=1, source_target_pairs={{0,4},{4,8},{8,12},{12,16},{16,20},{20,24},{24,28},{28,0},{1,5},{5... | collective-permute-start | bytes 663560 | tf_op jit(solution)/shard_map/ppermute | solution.py:17
  4.6 13.8 %collective-permute-start.1 = (bf16[416,1152]{1,0:T(8,128)(2,1)}, bf16[416,1152]{1,0:T(8,128)(2,1)S(1)}, u32[]{:S(2)}, u32[]{:S(2)}) collective-permute-start(bf16[416,1152]{1,0:T(8,128)(2,1)} %image_ref.3), channel_id=1, source_target_pairs={{0,3},{1,0},{2,1},{3,2},{4,7},{5,4},{6,5},{7,6},{8,11},{9,8},{10,9... | collective-permute-start | bytes 2875400 | tf_op jit(solution)/shard_map/ppermute | solution.py:17
  5.3 1.2 %copy-start = (bf16[416,1152]{1,0:T(8,128)(2,1)S(1)}, bf16[416,1152]{1,0:T(8,128)(2,1)}, u32[]{:S(2)}) copy-start(bf16[416,1152]{1,0:T(8,128)(2,1)} %array_ref.7) | copy-start | bytes 2875396
  6.5 7.4 %copy-start.1 = (bf16[416,1152]{1,0:T(8,128)(2,1)S(1)}, bf16[416,1152]{1,0:T(8,128)(2,1)}, u32[]{:S(2)}) copy-start(bf16[416,1152]{1,0:T(8,128)(2,1)} %array_ref.7) | copy-start | bytes 2875396
  6.5 7.7 %copy-start.2 = (bf16[416,1152]{1,0:T(8,128)(2,1)S(1)}, bf16[416,1152]{1,0:T(8,128)(2,1)}, u32[]{:S(2)}) copy-start(bf16[416,1152]{1,0:T(8,128)(2,1)} %image_ref.3) | copy-start | bytes 2875396
  6.6 15.1 %collective-permute-start.2 = (bf16[160,1152]{1,0:T(8,128)(2,1)S(1)}, bf16[160,1152]{1,0:T(8,128)(2,1)S(1)}, u32[]{:S(2)}, u32[]{:S(2)}) collective-permute-start(bf16[160,1152]{1,0:T(8,128)(2,1)S(1)} %fetch.5), channel_id=1, source_target_pairs={{0,4},{4,8},{8,12},{12,16},{16,20},{20,24},{24,28},{28,0},{1,5},{5... | collective-permute-start | bytes 1105928 | tf_op jit(solution)/shard_map/ppermute | solution.py:17
  14.1 10.8 %collective-permute-start.3 = (bf16[64,1152]{1,0:T(8,128)(2,1)S(1)}, bf16[64,1152]{1,0:T(8,128)(2,1)S(1)}, u32[]{:S(2)}, u32[]{:S(2)}) collective-permute-start(bf16[64,1152]{1,0:T(8,128)(2,1)S(1)} %fetch.6), channel_id=1, source_target_pairs={{0,4},{4,8},{8,12},{12,16},{16,20},{20,24},{24,28},{28,0},{1,5},{5... | collective-permute-start | bytes 442376 | tf_op jit(solution)/shard_map/ppermute | solution.py:17
  15.4 22.3 %collective-permute-start.4 = (bf16[96,1152]{1,0:T(8,128)(2,1)S(1)}, bf16[96,1152]{1,0:T(8,128)(2,1)S(1)}, u32[]{:S(2)}, u32[]{:S(2)}) collective-permute-start(bf16[96,1152]{1,0:T(8,128)(2,1)S(1)} %fetch.7), channel_id=1, source_target_pairs={{0,4},{4,8},{8,12},{12,16},{16,20},{20,24},{24,28},{28,0},{1,5},{5... | collective-permute-start | bytes 663560 | tf_op jit(solution)/shard_map/ppermute | solution.py:17
  24.9 16.6 %collective-permute-start.7 = (bf16[256,1152]{1,0:T(8,128)(2,1)S(1)}, bf16[256,1152]{1,0:T(8,128)(2,1)S(1)}, u32[]{:S(2)}, u32[]{:S(2)}) collective-permute-start(bf16[256,1152]{1,0:T(8,128)(2,1)S(1)} %pass_on.4.refs_0_), channel_id=1, source_target_pairs={{0,28},{4,0},{8,4},{12,8},{16,12},{20,16},{24,20},{28,24},{1,29},{... | collective-permute-start | bytes 1769480 | tf_op jit(solution)/shard_map/ppermute | solution.py:17
  39.5 13.3 %collective-permute-start.5 = (bf16[416,1152]{1,0:T(8,128)(2,1)S(1)}, bf16[416,1152]{1,0:T(8,128)(2,1)S(1)}, u32[]{:S(2)}, u32[]{:S(2)}) collective-permute-start(bf16[416,1152]{1,0:T(8,128)(2,1)S(1)} %fusion.3.refs_1_), channel_id=1, source_target_pairs={{0,1},{1,2},{2,3},{3,0},{4,5},{5,6},{6,7},{7,4},{8,9},{9,10},{10,1... | collective-permute-start | bytes 2875400 | tf_op jit(solution)/shard_map/ppermute | solution.py:17
  39.6 14.3 %collective-permute-start.6 = (bf16[160,1152]{1,0:T(8,128)(2,1)S(1)}, bf16[160,1152]{1,0:T(8,128)(2,1)S(1)}, u32[]{:S(2)}, u32[]{:S(2)}) collective-permute-start(bf16[160,1152]{1,0:T(8,128)(2,1)S(1)} %pass_on.5), channel_id=1, source_target_pairs={{0,28},{4,0},{8,4},{12,8},{16,12},{20,16},{24,20},{28,24},{1,29},{... | collective-permute-start | bytes 1105928 | tf_op jit(solution)/shard_map/ppermute | solution.py:17

commit v7 on v6

--- a/solution.py
+++ b/solution.py
@@ -31,24 +31,31 @@
 
 def row_cuts(rows):
     tiles = rows // 16
-    cuts = [0, tiles * 6 // 26 * 16, tiles * 16 // 26 * 16, tiles * 20 // 26 * 16, rows]
+    cuts = [0, tiles * 4 // 26 * 16, tiles * 16 // 26 * 16, tiles * 23 // 26 * 16, rows]
     return list(zip(cuts[:-1], cuts[1:]))
 
 
-def fetch(array, lo, hi, after):
+def fetch(array, spans, after, space, limit):
+    count = len(spans)
+
     def kernel(array_ref, *refs):
-        out_ref, sem = refs[-2:]
-        copy = pltpu.make_async_copy(array_ref.at[pl.ds(lo, hi - lo), :], out_ref, sem)
-        copy.start()
-        copy.wait()
+        sems = refs[-1]
+        copies = [
+            pltpu.make_async_copy(array_ref.at[pl.ds(lo, hi - lo), :], out_ref, sems.at[i])
+            for i, ((lo, hi), out_ref) in enumerate(zip(spans, refs[-1 - count : -1]))
+        ]
+        for copy in copies:
+            copy.start()
+        for copy in copies:
+            copy.wait()
 
     return pl.pallas_call(
         kernel,
-        out_shape=jax.ShapeDtypeStruct((hi - lo, array.shape[1]), array.dtype),
+        out_shape=[jax.ShapeDtypeStruct((hi - lo, array.shape[1]), array.dtype) for lo, hi in spans],
         in_specs=[ANY] * (1 + len(after)),
-        out_specs=VMEM,
-        scratch_shapes=[pltpu.SemaphoreType.DMA],
-        compiler_params=pltpu.CompilerParams(vmem_limit_bytes=2 * MIB),
+        out_specs=[space] * count,
+        scratch_shapes=[pltpu.SemaphoreType.DMA((count,))],
+        compiler_params=pltpu.CompilerParams(vmem_limit_bytes=limit),
         name="fetch",
     )(array, *after)
 
@@ -143,17 +150,17 @@
     scale = factor[0]
     bias = shift[0]
     cuts = row_cuts(text.shape[0])
-    first = text[: cuts[0][1]]
-    part = [shifted(first, "blk", 1)]
+    part = [shifted(rows, "blk", 1) for rows in fetch(text, cuts[:2], [], ANY, 60 * MIB)]
     image_next = shifted(image, "grp", -1)
-    part.append(shifted(fetch(text, *cuts[1], [first]), "blk", 1))
 
-    target = fetch(target, 0, 1, [part[0]])
-    part.append(shifted(fetch(text, *cuts[2], [target]), "blk", 1))
+    [target] = fetch(target, [(0, 1)], [part[0]], VMEM, MIB)
+    [rows] = fetch(text, cuts[2:3], [target], VMEM, 2 * MIB)
+    part.append(shifted(rows, "blk", 1))
     own = jax.nn.sigmoid(dot_nt(image, text) * scale + bias)
     column = lax.broadcasted_iota(jnp.int32, own.shape, 1)
     own = (own - (column == target[0][:, None]).astype(jnp.float32)).astype(jnp.bfloat16)
-    part.append(shifted(fetch(text, *cuts[3], [own]), "blk", 1))
+    [rows] = fetch(text, cuts[3:], [own], VMEM, 2 * MIB)
+    part.append(shifted(rows, "blk", 1))
     image_grad = dot_nn(own, text)
     text_grad = dot_tn(own, image)
 

time: 54.9 us -> 68.7 us (1.25)
  Pallas kernels: 6.27 us -> 25.1 us
  waiting for transfers between devices: 28.5 us -> 21.5 us
  matrix products: 6.57 us -> 7.78 us
  starting transfers between devices: 9 us -> 10.1 us
    pallas_call x4, Pallas kernels: 0.67 us -> 19.5 us  [fetch(): pl.pallas_call(kernel, out_shape=[jax.ShapeDtypeStruct((hi - lo, array.sh...]
    ppermute x8, waiting for transfers between devices: 28.5 us -> 21.5 us  [shifted(): lax.ppermute(shard, axis, [(i, (i + by) % devices) for i in range(devices)])]
    dot_general x2, matrix products: 1.72 us -> 2.91 us  [dot_nt(): lax.dot_general(a, b, (((1,), (1,)), ((), ())), preferred_element_type=jn...]
    ppermute x8, starting transfers between devices: 9 us -> 10.1 us  [shifted(): lax.ppermute(shard, axis, [(i, (i + by) % devices) for i in range(devices)])]
    slice x1 -> x0, local copies, waits for them, and re-layouts: 0.96 us -> none  [body(): first = text[:cuts[0][1]]]
  transfers between devices with their start and end apart: 8 -> 8, of which waited for: 6 -> 5; matrix products, arithmetic and copies ran while one was open for 12% -> 11% of each run, Pallas kernels for 10% -> 8%
where the time goes in v7:
time: 68.7 us; the launch traced here: 68.4 us
  Pallas kernels  25.1 us (37%)
  waiting for transfers between devices  21.5 us (31%)
  starting transfers between devices  10.1 us (15%)
  matrix products  7.78 us (11%)
  between operations  2.14 us (3%)
  local copies, waits for them, and re-layouts  1.88 us (3%)
    ppermute x8, waiting for transfers between devices, shifted(): lax.ppermute(shard, axis, [(i, (i + by) % devices) for i in range(devices)])  21.5 us
    pallas_call x4, Pallas kernels, fetch(): pl.pallas_call(kernel, out_shape=[jax.ShapeDtypeStruct((hi - lo, array.sh...  19.5 us
    ppermute x8, starting transfers between devices, shifted(): lax.ppermute(shard, axis, [(i, (i + by) % devices) for i in range(devices)])  10.1 us
    dot_general x6, matrix products, dot_tn(): lax.dot_general(a, b, (((0,), (0,)), ((), ())), preferred_element_type=jn...  3.46 us
    dot_general x2, matrix products, dot_nt(): lax.dot_general(a, b, (((1,), (1,)), ((), ())), preferred_element_type=jn...  2.91 us
    pallas_call x2, Pallas kernels, chunk(): pl.pallas_call(chunk_kernel, out_shape=(text, text, tile, tile), in_specs...  2.9 us
    pallas_call x3, Pallas kernels, add_rows(): pl.pallas_call(kernel, out_shape=(out, jax.ShapeDtypeStruct((8, 128), jnp...  2.71 us
    unnamed x8, local copies, waits for them, and re-layouts  1.88 us
  transfers between devices with their start and end apart: 8, of which 5 were waited for; matrix products, arithmetic and copies ran while one was open for 11% of the time, Pallas kernels for 8%

profile of v7, /device:TPU:0, one launch (start us, length us, event | category | flops | bytes accessed | tf_op | source)
XLA Modules:
  0.0 68.4 jit_solution(14571150907617544520)
XLA Ops:
  0.6 19.0 %fetch.4 = (bf16[64,1152]{1,0:T(8,128)(2,1)}, bf16[192,1152]{1,0:T(8,128)(2,1)}) custom-call(bf16[416,1152]{1,0:T(8,128)(2,1)} %array_ref.7), custom_call_target="tpu_custom_call" | custom-call | tf_op jit(solution)/shard_map/fetch/pallas_call | solution.py:52
  19.6 3.0 %collective-permute-start = (bf16[64,1152]{1,0:T(8,128)(2,1)}, bf16[64,1152]{1,0:T(8,128)(2,1)S(1)}, u32[]{:S(2)}, u32[]{:S(2)}) collective-permute-start(bf16[64,1152]{1,0:T(8,128)(2,1)} %get-tuple-element.14), channel_id=1, source_target_pairs={{0,4},{4,8},{8,12},{12,16},{16,20},{20,24},{24,28},{28,0},{1,5},{5... | collective-permute-start | bytes 442376 | tf_op jit(solution)/shard_map/ppermute | solution.py:17
  22.6 0.7 collective-permute-start.1
  23.3 1.5 %collective-permute-start.2 = (bf16[192,1152]{1,0:T(8,128)(2,1)}, bf16[192,1152]{1,0:T(8,128)(2,1)S(1)}, u32[]{:S(2)}, u32[]{:S(2)}) collective-permute-start(bf16[192,1152]{1,0:T(8,128)(2,1)} %get-tuple-element.15), channel_id=1, source_target_pairs={{0,4},{4,8},{8,12},{12,16},{16,20},{20,24},{24,28},{28,0},{1,5},{5... | collective-permute-start | bytes 1327112 | tf_op jit(solution)/shard_map/ppermute | solution.py:17
  26.2 4.4 %collective-permute-done.refs_0_.upper_ref = bf16[64,1152]{1,0:T(8,128)(2,1)S(1)} collective-permute-done((bf16[64,1152]{1,0:T(8,128)(2,1)}, bf16[64,1152]{1,0:T(8,128)(2,1)S(1)}, u32[]{:S(2)}, u32[]{:S(2)}) %collective-permute-start) | collective-permute-done | bytes 147488 | tf_op jit(solution)/shard_map/ppermute | solution.py:17
  30.6 0.7 copy-done.3
  31.3 1.2 %copy-done = bf16[416,1152]{1,0:T(8,128)(2,1)S(1)} copy-done((bf16[416,1152]{1,0:T(8,128)(2,1)S(1)}, bf16[416,1152]{1,0:T(8,128)(2,1)}, u32[]{:S(2)}) %copy-start) | copy-done | bytes 958488
  32.5 0.3 fetch.6
  32.8 0.1 collective-permute-start.3
  32.8 2.1 %subtract_convert_fusion.refs_0_ = bf16[416,416]{1,0:T(8,128)(2,1)S(1)} fusion(s32[416]{0:T(512)S(1)} %bitcast.30, f32[]{:T(128)} %bitcast.28, bf16[416,1152]{1,0:T(8,128)(2,1)} %image_ref.3, bf16[416,1152]{1,0:T(8,128)(2,1)S(1)} %copy-done.1, f32[]{:T(128)} %bitcast.24), kind=kOutput, calls=%fused_computation.22 | convolution fusion | flops 400278528 | bytes 2264712 | tf_op jit(solution)/shard_map/dot_general | solution.py:21
  34.9 0.2 fetch.7
  35.1 1.3 %collective-permute-start.4 = (bf16[48,1152]{1,0:T(8,128)(2,1)S(1)}, bf16[48,1152]{1,0:T(8,128)(2,1)S(1)}, u32[]{:S(2)}, u32[]{:S(2)}) collective-permute-start(bf16[48,1152]{1,0:T(8,128)(2,1)S(1)} %fetch.7), channel_id=1, source_target_pairs={{0,4},{4,8},{8,12},{12,16},{16,20},{20,24},{24,28},{28,0},{1,5},{5... | collective-permute-start | bytes 331784 | tf_op jit(solution)/shard_map/ppermute | solution.py:17
  36.4 0.7 %fusion.16.refs_2_ = f32[416,1152]{1,0:T(8,128)S(1)} fusion(bf16[416,416]{1,0:T(8,128)(2,1)S(1)} %subtract_convert_fusion.refs_0_, bf16[416,1152]{1,0:T(8,128)(2,1)S(1)} %copy-done.2), kind=kOutput, calls=%fused_computation.25 | convolution fusion | flops 398721024 | bytes 3221504 | tf_op jit(solution)/shard_map/dot_general | solution.py:25
  37.2 0.7 %fusion.15.refs_1_ = f32[416,1152]{1,0:T(8,128)S(1)} fusion(bf16[416,416]{1,0:T(8,128)(2,1)S(1)} %subtract_convert_fusion.refs_0_, bf16[416,1152]{1,0:T(8,128)(2,1)S(1)} %copy-done.1), kind=kOutput, calls=%fused_computation.24 | convolution fusion | flops 398721024 | bytes 3221504 | tf_op jit(solution)/shard_map/dot_general | solution.py:29
  37.9 0.8 %fusion.14 = bf16[416,416]{1,0:T(8,128)(2,1)S(1)} fusion(bf16[416,1152]{1,0:T(8,128)(2,1)S(1)} %pass_on.3.next_ref, bf16[416,1152]{1,0:T(8,128)(2,1)S(1)} %copy-done.1, f32[]{:T(128)} %bitcast.29, f32[]{:T(128)} %bitcast.27), kind=kOutput, calls=%fused_computation.21 | convolution fusion | flops 399759360 | bytes 2263048 | tf_op jit(solution)/shard_map/dot_general | solution.py:21
  38.8 0.7 %fusion.17 = f32[416,1152]{1,0:T(8,128)S(1)} fusion(bf16[416,416]{1,0:T(8,128)(2,1)S(1)} %fusion.14, bf16[416,1152]{1,0:T(8,128)(2,1)S(1)} %copy-done.1), kind=kOutput, calls=%fused_computation.26 | convolution fusion | flops 398721024 | bytes 3221504 | tf_op jit(solution)/shard_map/dot_general | solution.py:29
  39.5 0.6 collective-permute-done.2.lower_ref
  40.0 1.6 %chunk.2 = (bf16[256,1152]{1,0:T(8,128)(2,1)S(1)}, bf16[256,1152]{1,0:T(8,128)(2,1)S(1)}, bf16[256,416]{1,0:T(8,128)(2,1)S(1)}, bf16[256,416]{1,0:T(8,128)(2,1)S(1)}) custom-call(f32[1]{0:T(128)} %copy.15.scale_ref, f32[1]{0:T(128)} %copy.16.bias_ref, bf16[416,1152]{1,0:T(8,128)(2,1)S(1)} %copy-done.2, bf16[416,1152]{1,0:T(8,128)(2,1)S(1)} %pass_on.3.next_ref, ...), custom_call_target="tpu_custom_call" | custom-call | flops 981467136 | bytes 3686400 | tf_op jit(solution)/shard_map/chunk/pallas_call | solution.py:98
  41.7 0.5 convolution_add_fusion.3.refs_2_
  42.2 3.4 %collective-permute-done.3.refs_1_.upper_ref = bf16[112,1152]{1,0:T(8,128)(2,1)S(1)} collective-permute-done((bf16[112,1152]{1,0:T(8,128)(2,1)S(1)}, bf16[112,1152]{1,0:T(8,128)(2,1)S(1)}, u32[]{:S(2)}, u32[]{:S(2)}) %collective-permute-start.3) | collective-permute-done | bytes 258080 | tf_op jit(solution)/shard_map/ppermute | solution.py:17
  45.6 2.1 %collective-permute-start.7 = (bf16[256,1152]{1,0:T(8,128)(2,1)S(1)}, bf16[256,1152]{1,0:T(8,128)(2,1)S(1)}, u32[]{:S(2)}, u32[]{:S(2)}) collective-permute-start(bf16[256,1152]{1,0:T(8,128)(2,1)S(1)} %pass_on.4.refs_0_), channel_id=1, source_target_pairs={{0,28},{4,0},{8,4},{12,8},{16,12},{20,16},{24,20},{28,24},{1,29},{... | collective-permute-start | bytes 1769480 | tf_op jit(solution)/shard_map/ppermute | solution.py:17
  47.6 1.3 %chunk.3 = (bf16[160,1152]{1,0:T(8,128)(2,1)S(1)}, bf16[160,1152]{1,0:T(8,128)(2,1)S(1)}, bf16[160,416]{1,0:T(8,128)(2,1)S(1)}, bf16[160,416]{1,0:T(8,128)(2,1)S(1)}) custom-call(f32[1]{0:T(128)} %copy.15.scale_ref, f32[1]{0:T(128)} %copy.16.bias_ref, bf16[416,1152]{1,0:T(8,128)(2,1)S(1)} %copy-done.2, bf16[416,1152]{1,0:T(8,128)(2,1)S(1)} %pass_on.3.next_ref, ...), custom_call_target="tpu_custom_call" | custom-call | flops 613416960 | bytes 3022848 | tf_op jit(solution)/shard_map/chunk/pallas_call | solution.py:98
  48.9 0.5 fusion.3.refs_1_
  49.5 1.3 %collective-permute-start.6 = (bf16[160,1152]{1,0:T(8,128)(2,1)S(1)}, bf16[160,1152]{1,0:T(8,128)(2,1)S(1)}, u32[]{:S(2)}, u32[]{:S(2)}) collective-permute-start(bf16[160,1152]{1,0:T(8,128)(2,1)S(1)} %pass_on.5), channel_id=1, source_target_pairs={{0,28},{4,0},{8,4},{12,8},{16,12},{20,16},{24,20},{28,24},{1,29},{... | collective-permute-start | bytes 1105928 | tf_op jit(solution)/shard_map/ppermute | solution.py:17
  50.8 0.5 convolution_add_fusion.4
  51.3 0.5 fusion.2.total_ref
  51.8 0.7 %fusion.total_ref = f32[416,1152]{1,0:T(8,128)S(1)} fusion(f32[416,1152]{1,0:T(8,128)S(1)} %fusion.16.refs_2_, bf16[416,416]{1,0:T(8,128)(2,1)S(1)} %fusion.14, bf16[416,1152]{1,0:T(8,128)(2,1)S(1)} %pass_on.3.next_ref, f32[]{:T(128)} %bitcast.25), kind=kOutput, calls=%fused_computation.1 | convolution fusion | flops 399679488 | bytes 5138436 | tf_op jit(solution)/shard_map/dot_general | solution.py:25
  52.6 9.3 %collective-permute-done.7.back_ref = bf16[256,1152]{1,0:T(8,128)(2,1)S(1)} collective-permute-done((bf16[256,1152]{1,0:T(8,128)(2,1)S(1)}, bf16[256,1152]{1,0:T(8,128)(2,1)S(1)}, u32[]{:S(2)}, u32[]{:S(2)}) %collective-permute-start.7) | collective-permute-done | bytes 589856 | tf_op jit(solution)/shard_map/ppermute | solution.py:17
  61.8 0.9 %add_rows.4.refs_0_ = bf16[416,1152]{1,0:T(8,128)(2,1)} custom-call(f32[416,1152]{1,0:T(8,128)S(1)} %fusion.total_ref, bf16[256,1152]{1,0:T(8,128)(2,1)S(1)} %collective-permute-done.7.back_ref), custom_call_target="tpu_custom_call" | custom-call | tf_op jit(solution)/shard_map/add_rows/pallas_call | solution.py:137
  62.7 1.0 %add_rows.3 = (bf16[416,1152]{1,0:T(8,128)(2,1)}, f32[8,128]{1,0:T(8,128)S(1)}) custom-call(f32[416,1152]{1,0:T(8,128)S(1)} %fusion.2.total_ref, bf16[416,1152]{1,0:T(8,128)(2,1)S(1)} %collective-permute-done.5.back_ref), custom_call_target="tpu_custom_call" | custom-call | tf_op jit(solution)/shard_map/add_rows/pallas_call | solution.py:137
  63.8 3.9 %collective-permute-done.6.back_ref = bf16[160,1152]{1,0:T(8,128)(2,1)S(1)} collective-permute-done((bf16[160,1152]{1,0:T(8,128)(2,1)S(1)}, bf16[160,1152]{1,0:T(8,128)(2,1)S(1)}, u32[]{:S(2)}, u32[]{:S(2)}) %collective-permute-start.6) | collective-permute-done | bytes 368672 | tf_op jit(solution)/shard_map/ppermute | solution.py:17
  67.6 0.8 %add_rows.5 = bf16[416,1152]{1,0:T(8,128)(2,1)} custom-call(f32[416,1152]{1,0:T(8,128)S(1)} %fusion.total_ref, bf16[160,1152]{1,0:T(8,128)(2,1)S(1)} %collective-permute-done.6.back_ref, bf16[416,1152]{1,0:T(8,128)(2,1)} %add_rows.4.refs_0_, f32[8,128]{1,0:T(8,128)S(1)} %get-tuple-element.25.refs_1_), custom_call_target="tpu_custom_call", output_to_operand_aliasing={{}: (2, {})} | custom-call | tf_op jit(solution)/shard_map/add_rows/pallas_call | solution.py:137
  (14 shorter events, 0.1 us)
Async XLA Ops:
  0.6 32.2 %copy-start.1 = (bf16[416,1152]{1,0:T(8,128)(2,1)S(1)}, bf16[416,1152]{1,0:T(8,128)(2,1)}, u32[]{:S(2)}) copy-start(bf16[416,1152]{1,0:T(8,128)(2,1)} %array_ref.7) | copy-start | bytes 2875396
  19.6 10.9 %collective-permute-start = (bf16[64,1152]{1,0:T(8,128)(2,1)}, bf16[64,1152]{1,0:T(8,128)(2,1)S(1)}, u32[]{:S(2)}, u32[]{:S(2)}) collective-permute-start(bf16[64,1152]{1,0:T(8,128)(2,1)} %get-tuple-element.14), channel_id=1, source_target_pairs={{0,4},{4,8},{8,12},{12,16},{16,20},{20,24},{24,28},{28,0},{1,5},{5... | collective-permute-start | bytes 442376 | tf_op jit(solution)/shard_map/ppermute | solution.py:17
  22.6 15.3 %collective-permute-start.1 = (bf16[416,1152]{1,0:T(8,128)(2,1)}, bf16[416,1152]{1,0:T(8,128)(2,1)S(1)}, u32[]{:S(2)}, u32[]{:S(2)}) collective-permute-start(bf16[416,1152]{1,0:T(8,128)(2,1)} %image_ref.3), channel_id=1, source_target_pairs={{0,3},{1,0},{2,1},{3,2},{4,7},{5,4},{6,5},{7,6},{8,11},{9,8},{10,9... | collective-permute-start | bytes 2875400 | tf_op jit(solution)/shard_map/ppermute | solution.py:17
  23.3 16.7 %collective-permute-start.2 = (bf16[192,1152]{1,0:T(8,128)(2,1)}, bf16[192,1152]{1,0:T(8,128)(2,1)S(1)}, u32[]{:S(2)}, u32[]{:S(2)}) collective-permute-start(bf16[192,1152]{1,0:T(8,128)(2,1)} %get-tuple-element.15), channel_id=1, source_target_pairs={{0,4},{4,8},{8,12},{12,16},{16,20},{20,24},{24,28},{28,0},{1,5},{5... | collective-permute-start | bytes 1327112 | tf_op jit(solution)/shard_map/ppermute | solution.py:17
  30.6 0.7 copy-start.3
  31.3 1.2 %copy-start = (bf16[416,1152]{1,0:T(8,128)(2,1)S(1)}, bf16[416,1152]{1,0:T(8,128)(2,1)}, u32[]{:S(2)}) copy-start(bf16[416,1152]{1,0:T(8,128)(2,1)} %array_ref.7) | copy-start | bytes 2875396
  32.8 12.8 %collective-permute-start.3 = (bf16[112,1152]{1,0:T(8,128)(2,1)S(1)}, bf16[112,1152]{1,0:T(8,128)(2,1)S(1)}, u32[]{:S(2)}, u32[]{:S(2)}) collective-permute-start(bf16[112,1152]{1,0:T(8,128)(2,1)S(1)} %fetch.6), channel_id=1, source_target_pairs={{0,4},{4,8},{8,12},{12,16},{16,20},{20,24},{24,28},{28,0},{1,5},{5... | collective-permute-start | bytes 774152 | tf_op jit(solution)/shard_map/ppermute | solution.py:17
  34.9 1.5 %copy-start.2 = (bf16[416,1152]{1,0:T(8,128)(2,1)S(1)}, bf16[416,1152]{1,0:T(8,128)(2,1)}, u32[]{:S(2)}) copy-start(bf16[416,1152]{1,0:T(8,128)(2,1)} %image_ref.3) | copy-start | bytes 2875396
  35.1 12.5 %collective-permute-start.4 = (bf16[48,1152]{1,0:T(8,128)(2,1)S(1)}, bf16[48,1152]{1,0:T(8,128)(2,1)S(1)}, u32[]{:S(2)}, u32[]{:S(2)}) collective-permute-start(bf16[48,1152]{1,0:T(8,128)(2,1)S(1)} %fetch.7), channel_id=1, source_target_pairs={{0,4},{4,8},{8,12},{12,16},{16,20},{20,24},{24,28},{28,0},{1,5},{5... | collective-permute-start | bytes 331784 | tf_op jit(solution)/shard_map/ppermute | solution.py:17
  45.6 16.3 %collective-permute-start.7 = (bf16[256,1152]{1,0:T(8,128)(2,1)S(1)}, bf16[256,1152]{1,0:T(8,128)(2,1)S(1)}, u32[]{:S(2)}, u32[]{:S(2)}) collective-permute-start(bf16[256,1152]{1,0:T(8,128)(2,1)S(1)} %pass_on.4.refs_0_), channel_id=1, source_target_pairs={{0,28},{4,0},{8,4},{12,8},{16,12},{20,16},{24,20},{28,24},{1,29},{... | collective-permute-start | bytes 1769480 | tf_op jit(solution)/shard_map/ppermute | solution.py:17
  49.4 13.3 %collective-permute-start.5 = (bf16[416,1152]{1,0:T(8,128)(2,1)S(1)}, bf16[416,1152]{1,0:T(8,128)(2,1)S(1)}, u32[]{:S(2)}, u32[]{:S(2)}) collective-permute-start(bf16[416,1152]{1,0:T(8,128)(2,1)S(1)} %fusion.3.refs_1_), channel_id=1, source_target_pairs={{0,1},{1,2},{2,3},{3,0},{4,5},{5,6},{6,7},{7,4},{8,9},{9,10},{10,1... | collective-permute-start | bytes 2875400 | tf_op jit(solution)/shard_map/ppermute | solution.py:17
  49.5 18.2 %collective-permute-start.6 = (bf16[160,1152]{1,0:T(8,128)(2,1)S(1)}, bf16[160,1152]{1,0:T(8,128)(2,1)S(1)}, u32[]{:S(2)}, u32[]{:S(2)}) collective-permute-start(bf16[160,1152]{1,0:T(8,128)(2,1)S(1)} %pass_on.5), channel_id=1, source_target_pairs={{0,28},{4,0},{8,4},{12,8},{16,12},{20,16},{24,20},{28,24},{1,29},{... | collective-permute-start | bytes 1105928 | tf_op jit(solution)/shard_map/ppermute | solution.py:17

commit v8 on v6

--- a/solution.py
+++ b/solution.py
@@ -1,3 +1,5 @@
+import functools
+
 import jax
 import jax.numpy as jnp
 from jax import lax
@@ -6,6 +8,7 @@
 from jax.sharding import PartitionSpec as P
 
 MIB = 2**20
+ENDS = (6, 16, 18, 23)
 SMEM = pl.BlockSpec(memory_space=pltpu.SMEM)
 VMEM = pl.BlockSpec(memory_space=pltpu.VMEM)
 HBM = pl.BlockSpec(memory_space=pltpu.HBM)
@@ -31,8 +34,16 @@
 
 def row_cuts(rows):
     tiles = rows // 16
-    cuts = [0, tiles * 6 // 26 * 16, tiles * 16 // 26 * 16, tiles * 20 // 26 * 16, rows]
+    cuts = [0] + [tiles * ends // 26 * 16 for ends in ENDS] + [rows]
     return list(zip(cuts[:-1], cuts[1:]))
+
+
+def shifted_with_relay(shard, axis, order):
+    devices = lax.axis_size(axis)
+    near = lax.ppermute(shard, axis, [(i, i + 1) for i in range(devices - 1)])
+    relay = lax.ppermute(shard, axis, [(devices - 1, devices - 2)])
+    far = lax.ppermute(order(relay), axis, [(devices - 2, 0)])
+    return near, far
 
 
 def fetch(array, lo, hi, after):
@@ -65,12 +76,15 @@
     )(array, *after)
 
 
-def chunk_kernel(scale_ref, bias_ref, image_ref, next_ref, upper_ref, lower_ref, *refs):
+def chunk_kernel(lows, scale_ref, bias_ref, image_ref, next_ref, *refs):
     sent_ref, joined_ref, own_ref, other_ref = refs[-4:]
     scale, bias = scale_ref[0], bias_ref[0]
-    rows = upper_ref.shape[0]
-    joined_ref[:rows, :] = upper_ref[...]
-    joined_ref[rows:, :] = lower_ref[...]
+    for i, lo in enumerate(lows):
+        rows = pl.ds(lo, refs[i].shape[0])
+        if lo in lows[:i]:
+            joined_ref[rows, :] += refs[i][...]
+        else:
+            joined_ref[rows, :] = refs[i][...]
     part = joined_ref[...]
     image = image_ref[...]
     own = jax.nn.sigmoid(dot_nt(part, image) * scale + bias).astype(jnp.bfloat16)
@@ -83,15 +97,16 @@
     sent_ref[...] = (scale * total).astype(jnp.bfloat16)
 
 
-def chunk(factor, shift, image, image_next, upper, lower, after):
-    rows, width = upper.shape[0] + lower.shape[0], upper.shape[1]
+def chunk(factor, shift, image, image_next, pieces, after):
+    width = image.shape[1]
     columns = image.shape[0]
+    rows = max(lo + piece.shape[0] for lo, piece in pieces)
     text = jax.ShapeDtypeStruct((rows, width), jnp.bfloat16)
     tile = jax.ShapeDtypeStruct((rows, columns), jnp.bfloat16)
     return pl.pallas_call(
-        chunk_kernel,
+        functools.partial(chunk_kernel, [lo for lo, _ in pieces]),
         out_shape=(text, text, tile, tile),
-        in_specs=[SMEM] * 2 + [VMEM] * 4 + [ANY] * len(after),
+        in_specs=[SMEM] * 2 + [VMEM] * (2 + len(pieces)) + [ANY] * len(after),
         out_specs=(VMEM,) * 4,
         compiler_params=pltpu.CompilerParams(vmem_limit_bytes=16 * MIB),
         cost_estimate=pl.CostEstimate(
@@ -100,7 +115,7 @@
             transcendentals=2 * rows * columns,
         ),
         name="chunk",
-    )(factor, shift, image, image_next, upper, lower, *after)
+    )(factor, shift, image, image_next, *[piece for _, piece in pieces], *after)
 
 
 def add_rows(total, back, lo, result, after, mark=False):
@@ -149,16 +164,21 @@
     part.append(shifted(fetch(text, *cuts[1], [first]), "blk", 1))
 
     target = fetch(target, 0, 1, [part[0]])
-    part.append(shifted(fetch(text, *cuts[2], [target]), "blk", 1))
+    relayed = fetch(text, *cuts[2], [target])
     own = jax.nn.sigmoid(dot_nt(image, text) * scale + bias)
     column = lax.broadcasted_iota(jnp.int32, own.shape, 1)
     own = (own - (column == target[0][:, None]).astype(jnp.float32)).astype(jnp.bfloat16)
-    part.append(shifted(fetch(text, *cuts[3], [own]), "blk", 1))
+    rows = fetch(text, *cuts[3], [own])
     image_grad = dot_nn(own, text)
     text_grad = dot_tn(own, image)
+    near, far = shifted_with_relay(relayed, "blk", lambda relay: pass_on(relay, [image_grad, text_grad]))
+    part.append(shifted(rows, "blk", 1))
+    part.append(shifted(fetch(text, *cuts[4], [text_grad]), "blk", 1))
 
     image_next = pass_on(image_next, [image_grad, text_grad])
-    sent0, part0, own0, next0 = chunk(factor, shift, image, image_next, part[0], part[1], [])
+    sent0, part0, own0, next0 = chunk(
+        factor, shift, image, image_next, [(0, part[0]), (cuts[1][0], part[1])], []
+    )
     next_own = jax.nn.sigmoid(dot_nt(image_next, text) * scale + bias).astype(jnp.bfloat16)
     text_grad = scale * (text_grad + dot_tn(next_own, image_next))
     image_sent = dot_nn(next_own, text) + dot_tn(next0, part0)
@@ -167,7 +187,9 @@
     sent0 = pass_on(sent0, [part[2], image_sent])
     back0 = shifted(sent0, "blk", -1)
 
-    sent1, part1, own1, next1 = chunk(factor, shift, image, image_next, part[2], part[3], [sent0])
+    base = cuts[2][0]
+    pieces = [(0, near), (0, far), (cuts[3][0] - base, part[2]), (cuts[4][0] - base, part[3])]
+    sent1, part1, own1, next1 = chunk(factor, shift, image, image_next, pieces, [sent0])
     image_sent = (scale * (image_sent + dot_tn(next1, part1))).astype(jnp.bfloat16)
     image_back = shifted(image_sent, "grp", 1)
     sent1 = pass_on(sent1, [image_sent])

time: 54.9 us -> 53.6 us (0.976)
  the two profiles are of different devices: /device:TPU:0 before, /device:TPU:18 now
where the time goes in v8:
time: 53.6 us; the launch traced here: 53.3 us
  waiting for transfers between devices  19.9 us (37%)
  starting transfers between devices  16.2 us (30%)
  matrix products  6.58 us (12%)
  Pallas kernels  6.27 us (12%)
  between operations  2.22 us (4%)
  local copies, waits for them, and re-layouts  2.16 us (4%)
    ppermute x8, waiting for transfers between devices, shifted(): lax.ppermute(shard, axis, [(i, (i + by) % devices) for i in range(devices)])  19.9 us
    ppermute x8, starting transfers between devices, shifted(): lax.ppermute(shard, axis, [(i, (i + by) % devices) for i in range(devices)])  9.77 us
    ppermute x1, starting transfers between devices, shifted_with_relay(): near = lax.ppermute(shard, axis, [(i, i + 1) for i in range(devices - 1)])  5.1 us
    dot_general x6, matrix products, dot_tn(): lax.dot_general(a, b, (((0,), (0,)), ((), ())), preferred_element_type=jn...  3.46 us
    pallas_call x2, Pallas kernels, chunk(): pl.pallas_call(functools.partial(chunk_kernel, [lo for lo, _ in pieces]),...  2.91 us
    pallas_call x3, Pallas kernels, add_rows(): pl.pallas_call(kernel, out_shape=(out, jax.ShapeDtypeStruct((8, 128), jnp...  2.7 us
    dot_general x2, matrix products, dot_nt(): lax.dot_general(a, b, (((1,), (1,)), ((), ())), preferred_element_type=jn...  1.72 us
    dot_general x2, matrix products, dot_nn(): return jnp.dot(a, b, preferred_element_type=jnp.float32)  1.4 us
  transfers between devices with their start and end apart: 11, of which 3 were waited for; matrix products, arithmetic and copies ran while one was open for 12% of the time, Pallas kernels for 10%

profile of v8, /device:TPU:18, one launch (start us, length us, event | category | flops | bytes accessed | tf_op | source)
XLA Modules:
  0.0 53.3 jit_solution(4881896789667929625)
XLA Ops:
  0.6 1.0 %slice.3.refs_0_ = bf16[96,1152]{1,0:T(8,128)(2,1)S(1)} slice(bf16[416,1152]{1,0:T(8,128)(2,1)} %array_ref.9), slice={[0:96], [0:1152]} | slice | bytes 442368 | tf_op jit(solution)/shard_map/slice | solution.py:161
  1.6 1.6 %collective-permute-start = (bf16[96,1152]{1,0:T(8,128)(2,1)S(1)}, bf16[96,1152]{1,0:T(8,128)(2,1)S(1)}, u32[]{:S(2)}, u32[]{:S(2)}) collective-permute-start(bf16[96,1152]{1,0:T(8,128)(2,1)S(1)} %slice.3.refs_0_), channel_id=1, source_target_pairs={{0,4},{4,8},{8,12},{12,16},{16,20},{20,24},{24,28},{28,0},{1,5},{5... | collective-permute-start | bytes 663560 | tf_op jit(solution)/shard_map/ppermute | solution.py:20
  3.2 0.7 %collective-permute-start.1 = (bf16[416,1152]{1,0:T(8,128)(2,1)}, bf16[416,1152]{1,0:T(8,128)(2,1)S(1)}, u32[]{:S(2)}, u32[]{:S(2)}) collective-permute-start(bf16[416,1152]{1,0:T(8,128)(2,1)} %image_ref.3), channel_id=1, source_target_pairs={{0,3},{1,0},{2,1},{3,2},{4,7},{5,4},{6,5},{7,6},{8,11},{9,8},{10,9... | collective-permute-start | bytes 2875400 | tf_op jit(solution)/shard_map/ppermute | solution.py:20
  3.9 1.2 %copy-done = bf16[416,1152]{1,0:T(8,128)(2,1)S(1)} copy-done((bf16[416,1152]{1,0:T(8,128)(2,1)S(1)}, bf16[416,1152]{1,0:T(8,128)(2,1)}, u32[]{:S(2)}) %copy-start) | copy-done | bytes 958488
  5.1 0.2 fetch.6
  5.2 1.5 %collective-permute-start.2 = (bf16[160,1152]{1,0:T(8,128)(2,1)S(1)}, bf16[160,1152]{1,0:T(8,128)(2,1)S(1)}, u32[]{:S(2)}, u32[]{:S(2)}) collective-permute-start(bf16[160,1152]{1,0:T(8,128)(2,1)S(1)} %fetch.6), channel_id=1, source_target_pairs={{0,4},{4,8},{8,12},{12,16},{16,20},{20,24},{24,28},{28,0},{1,5},{5... | collective-permute-start | bytes 1105928 | tf_op jit(solution)/shard_map/ppermute | solution.py:20
  8.1 1.8 %collective-permute-done.refs_0_ = bf16[96,1152]{1,0:T(8,128)(2,1)S(1)} collective-permute-done((bf16[96,1152]{1,0:T(8,128)(2,1)S(1)}, bf16[96,1152]{1,0:T(8,128)(2,1)S(1)}, u32[]{:S(2)}, u32[]{:S(2)}) %collective-permute-start) | collective-permute-done | bytes 221216 | tf_op jit(solution)/shard_map/ppermute | solution.py:20
  9.9 0.1 fetch.7
  10.0 0.7 %collective-permute-start.4 = (bf16[32,1152]{1,0:T(8,128)(2,1)S(1)}, bf16[32,1152]{1,0:T(8,128)(2,1)S(1)}, u32[]{:S(2)}, u32[]{:S(2)}) collective-permute-start(bf16[32,1152]{1,0:T(8,128)(2,1)S(1)} %fetch.7), channel_id=1, source_target_pairs={{28,24},{29,25},{30,26},{31,27}} | collective-permute-start | bytes 221192 | tf_op jit(solution)/shard_map/ppermute | solution.py:44
  10.7 5.1 %collective-permute-start.3 = (bf16[32,1152]{1,0:T(8,128)(2,1)S(1)}, bf16[32,1152]{1,0:T(8,128)(2,1)S(1)}, u32[]{:S(2)}, u32[]{:S(2)}) collective-permute-start(bf16[32,1152]{1,0:T(8,128)(2,1)S(1)} %fetch.7), channel_id=1, source_target_pairs={{0,4},{4,8},{8,12},{12,16},{16,20},{20,24},{24,28},{1,5},{5,9},{9,... | collective-permute-start | bytes 221192 | tf_op jit(solution)/shard_map/ppermute | solution.py:43
  15.8 0.9 %subtract_convert_fusion.refs_0_ = bf16[416,416]{1,0:T(8,128)(2,1)S(1)} fusion(s32[416]{0:T(512)S(1)} %bitcast.30, f32[]{:T(128)} %bitcast.28, bf16[416,1152]{1,0:T(8,128)(2,1)S(1)} %copy-done.2, bf16[416,1152]{1,0:T(8,128)(2,1)S(1)} %copy-done.1, f32[]{:T(128)} %bitcast.24), kind=kOutput, calls=%fused_computation.22 | convolution fusion | flops 400278528 | bytes 2264712 | tf_op jit(solution)/shard_map/dot_general | solution.py:24
  16.7 0.7 %fusion.16.refs_2_.refs_0_ = f32[416,1152]{1,0:T(8,128)S(1)} fusion(bf16[416,416]{1,0:T(8,128)(2,1)S(1)} %subtract_convert_fusion.refs_0_, bf16[416,1152]{1,0:T(8,128)(2,1)S(1)} %copy-done.2), kind=kOutput, calls=%fused_computation.25 | convolution fusion | flops 398721024 | bytes 3221504 | tf_op jit(solution)/shard_map/dot_general | solution.py:28
  17.4 0.7 %fusion.15.refs_1_ = f32[416,1152]{1,0:T(8,128)S(1)} fusion(bf16[416,416]{1,0:T(8,128)(2,1)S(1)} %subtract_convert_fusion.refs_0_, bf16[416,1152]{1,0:T(8,128)(2,1)S(1)} %copy-done.1), kind=kOutput, calls=%fused_computation.24 | convolution fusion | flops 398721024 | bytes 3221504 | tf_op jit(solution)/shard_map/dot_general | solution.py:32
  18.1 0.2 fetch.8
  18.4 2.7 %collective-permute-start.6 = (bf16[80,1152]{1,0:T(8,128)(2,1)S(1)}, bf16[80,1152]{1,0:T(8,128)(2,1)S(1)}, u32[]{:S(2)}, u32[]{:S(2)}) collective-permute-start(bf16[80,1152]{1,0:T(8,128)(2,1)S(1)} %fetch.8), channel_id=1, source_target_pairs={{0,4},{4,8},{8,12},{12,16},{16,20},{20,24},{24,28},{28,0},{1,5},{5... | collective-permute-start | bytes 552968 | tf_op jit(solution)/shard_map/ppermute | solution.py:20
  21.1 0.1 fetch.9
  21.2 3.1 %collective-permute-start.7 = (bf16[48,1152]{1,0:T(8,128)(2,1)S(1)}, bf16[48,1152]{1,0:T(8,128)(2,1)S(1)}, u32[]{:S(2)}, u32[]{:S(2)}) collective-permute-start(bf16[48,1152]{1,0:T(8,128)(2,1)S(1)} %fetch.9), channel_id=1, source_target_pairs={{0,4},{4,8},{8,12},{12,16},{16,20},{20,24},{24,28},{28,0},{1,5},{5... | collective-permute-start | bytes 331784 | tf_op jit(solution)/shard_map/ppermute | solution.py:20
  24.3 0.7 %collective-permute-start.5 = (bf16[32,1152]{1,0:T(8,128)(2,1)S(1)}, bf16[32,1152]{1,0:T(8,128)(2,1)S(1)}, u32[]{:S(2)}, u32[]{:S(2)}) collective-permute-start(bf16[32,1152]{1,0:T(8,128)(2,1)S(1)} %pass_on.5), channel_id=1, source_target_pairs={{24,0},{25,1},{26,2},{27,3}} | collective-permute-start | bytes 221192 | tf_op jit(solution)/shard_map/ppermute | solution.py:45
  25.0 0.8 %fusion.14 = bf16[416,416]{1,0:T(8,128)(2,1)S(1)} fusion(bf16[416,1152]{1,0:T(8,128)(2,1)S(1)} %pass_on.4.next_ref, bf16[416,1152]{1,0:T(8,128)(2,1)S(1)} %copy-done.1, f32[]{:T(128)} %bitcast.29, f32[]{:T(128)} %bitcast.27), kind=kOutput, calls=%fused_computation.21 | convolution fusion | flops 399759360 | bytes 2263048 | tf_op jit(solution)/shard_map/dot_general | solution.py:24
  25.8 0.7 %fusion.17 = f32[416,1152]{1,0:T(8,128)S(1)} fusion(bf16[416,416]{1,0:T(8,128)(2,1)S(1)} %fusion.14, bf16[416,1152]{1,0:T(8,128)(2,1)S(1)} %copy-done.1), kind=kOutput, calls=%fused_computation.26 | convolution fusion | flops 398721024 | bytes 3221504 | tf_op jit(solution)/shard_map/dot_general | solution.py:32
  26.5 1.6 %chunk.2 = (bf16[256,1152]{1,0:T(8,128)(2,1)S(1)}, bf16[256,1152]{1,0:T(8,128)(2,1)S(1)}, bf16[256,416]{1,0:T(8,128)(2,1)S(1)}, bf16[256,416]{1,0:T(8,128)(2,1)S(1)}) custom-call(f32[1]{0:T(128)} %copy.17.scale_ref, f32[1]{0:T(128)} %copy.18.bias_ref, bf16[416,1152]{1,0:T(8,128)(2,1)S(1)} %copy-done.2, bf16[416,1152]{1,0:T(8,128)(2,1)S(1)} %pass_on.4.next_ref, ...), custom_call_target="tpu_custom_call" | custom-call | flops 981467136 | bytes 3686400 | tf_op jit(solution)/shard_map/chunk/pallas_call | solution.py:106
  28.2 0.5 convolution_add_fusion.3.refs_2_
  28.8 1.3 %chunk.3 = (bf16[160,1152]{1,0:T(8,128)(2,1)S(1)}, bf16[160,1152]{1,0:T(8,128)(2,1)S(1)}, bf16[160,416]{1,0:T(8,128)(2,1)S(1)}, bf16[160,416]{1,0:T(8,128)(2,1)S(1)}) custom-call(f32[1]{0:T(128)} %copy.17.scale_ref, f32[1]{0:T(128)} %copy.18.bias_ref, bf16[416,1152]{1,0:T(8,128)(2,1)S(1)} %copy-done.2, bf16[416,1152]{1,0:T(8,128)(2,1)S(1)} %pass_on.4.next_ref, ...), custom_call_target="tpu_custom_call" | custom-call | flops 613416960 | bytes 3022848 | tf_op jit(solution)/shard_map/chunk/pallas_call | solution.py:106
  30.1 0.5 fusion.3.refs_1_
  30.7 0.5 convolution_add_fusion.4
  31.2 0.5 fusion.2.total_ref
  31.7 0.7 %fusion.total_ref = f32[416,1152]{1,0:T(8,128)S(1)} fusion(f32[416,1152]{1,0:T(8,128)S(1)} %fusion.16.refs_2_.refs_0_, bf16[416,416]{1,0:T(8,128)(2,1)S(1)} %fusion.14, bf16[416,1152]{1,0:T(8,128)(2,1)S(1)} %pass_on.4.next_ref, f32[]{:T(128)} %bitcast.25), kind=kOutput, calls=%fused_computation.1 | convolution fusion | flops 399679488 | bytes 5138436 | tf_op jit(solution)/shard_map/dot_general | solution.py:28
  32.5 13.4 %collective-permute-done.10.back_ref = bf16[256,1152]{1,0:T(8,128)(2,1)S(1)} collective-permute-done((bf16[256,1152]{1,0:T(8,128)(2,1)S(1)}, bf16[256,1152]{1,0:T(8,128)(2,1)S(1)}, u32[]{:S(2)}, u32[]{:S(2)}) %collective-permute-start.10) | collective-permute-done | bytes 589856 | tf_op jit(solution)/shard_map/ppermute | solution.py:20
  45.9 0.9 %add_rows.4.refs_0_ = bf16[416,1152]{1,0:T(8,128)(2,1)} custom-call(f32[416,1152]{1,0:T(8,128)S(1)} %fusion.total_ref, bf16[256,1152]{1,0:T(8,128)(2,1)S(1)} %collective-permute-done.10.back_ref), custom_call_target="tpu_custom_call" | custom-call | tf_op jit(solution)/shard_map/add_rows/pallas_call | solution.py:145
  46.8 1.0 %add_rows.3 = (bf16[416,1152]{1,0:T(8,128)(2,1)}, f32[8,128]{1,0:T(8,128)S(1)}) custom-call(f32[416,1152]{1,0:T(8,128)S(1)} %fusion.2.total_ref, bf16[416,1152]{1,0:T(8,128)(2,1)S(1)} %collective-permute-done.8.back_ref), custom_call_target="tpu_custom_call" | custom-call | tf_op jit(solution)/shard_map/add_rows/pallas_call | solution.py:145
  47.8 4.7 %collective-permute-done.9.back_ref = bf16[160,1152]{1,0:T(8,128)(2,1)S(1)} collective-permute-done((bf16[160,1152]{1,0:T(8,128)(2,1)S(1)}, bf16[160,1152]{1,0:T(8,128)(2,1)S(1)}, u32[]{:S(2)}, u32[]{:S(2)}) %collective-permute-start.9) | collective-permute-done | bytes 368672 | tf_op jit(solution)/shard_map/ppermute | solution.py:20
  52.5 0.8 %add_rows.5 = bf16[416,1152]{1,0:T(8,128)(2,1)} custom-call(f32[416,1152]{1,0:T(8,128)S(1)} %fusion.total_ref, bf16[160,1152]{1,0:T(8,128)(2,1)S(1)} %collective-permute-done.9.back_ref, bf16[416,1152]{1,0:T(8,128)(2,1)} %add_rows.4.refs_0_, f32[8,128]{1,0:T(8,128)S(1)} %get-tuple-element.21.refs_1_), custom_call_target="tpu_custom_call", output_to_operand_aliasing={{}: (2, {})} | custom-call | tf_op jit(solution)/shard_map/add_rows/pallas_call | solution.py:145
  (23 shorter events, 0.2 us)
Async XLA Ops:
  0.6 9.2 %copy-start.3 = (s32[1,416]{1,0:T(1,128)S(1)}, s32[1,416]{1,0:T(1,128)}, u32[]{:S(2)}) copy-start(s32[1,416]{1,0:T(1,128)} %array_ref.5) | copy-start | bytes 4996
  1.6 8.3 %collective-permute-start = (bf16[96,1152]{1,0:T(8,128)(2,1)S(1)}, bf16[96,1152]{1,0:T(8,128)(2,1)S(1)}, u32[]{:S(2)}, u32[]{:S(2)}) collective-permute-start(bf16[96,1152]{1,0:T(8,128)(2,1)S(1)} %slice.3.refs_0_), channel_id=1, source_target_pairs={{0,4},{4,8},{8,12},{12,16},{16,20},{20,24},{24,28},{28,0},{1,5},{5... | collective-permute-start | bytes 663560 | tf_op jit(solution)/shard_map/ppermute | solution.py:20
  3.2 21.1 %collective-permute-start.1 = (bf16[416,1152]{1,0:T(8,128)(2,1)}, bf16[416,1152]{1,0:T(8,128)(2,1)S(1)}, u32[]{:S(2)}, u32[]{:S(2)}) collective-permute-start(bf16[416,1152]{1,0:T(8,128)(2,1)} %image_ref.3), channel_id=1, source_target_pairs={{0,3},{1,0},{2,1},{3,2},{4,7},{5,4},{6,5},{7,6},{8,11},{9,8},{10,9... | collective-permute-start | bytes 2875400 | tf_op jit(solution)/shard_map/ppermute | solution.py:20
  3.9 1.2 %copy-start = (bf16[416,1152]{1,0:T(8,128)(2,1)S(1)}, bf16[416,1152]{1,0:T(8,128)(2,1)}, u32[]{:S(2)}) copy-start(bf16[416,1152]{1,0:T(8,128)(2,1)} %array_ref.9) | copy-start | bytes 2875396
  5.1 4.8 %copy-start.1 = (bf16[416,1152]{1,0:T(8,128)(2,1)S(1)}, bf16[416,1152]{1,0:T(8,128)(2,1)}, u32[]{:S(2)}) copy-start(bf16[416,1152]{1,0:T(8,128)(2,1)} %array_ref.9) | copy-start | bytes 2875396
  5.1 10.7 %copy-start.2 = (bf16[416,1152]{1,0:T(8,128)(2,1)S(1)}, bf16[416,1152]{1,0:T(8,128)(2,1)}, u32[]{:S(2)}) copy-start(bf16[416,1152]{1,0:T(8,128)(2,1)} %image_ref.3) | copy-start | bytes 2875396
  5.2 21.3 %collective-permute-start.2 = (bf16[160,1152]{1,0:T(8,128)(2,1)S(1)}, bf16[160,1152]{1,0:T(8,128)(2,1)S(1)}, u32[]{:S(2)}, u32[]{:S(2)}) collective-permute-start(bf16[160,1152]{1,0:T(8,128)(2,1)S(1)} %fetch.6), channel_id=1, source_target_pairs={{0,4},{4,8},{8,12},{12,16},{16,20},{20,24},{24,28},{28,0},{1,5},{5... | collective-permute-start | bytes 1105928 | tf_op jit(solution)/shard_map/ppermute | solution.py:20
  10.0 11.2 %collective-permute-start.4 = (bf16[32,1152]{1,0:T(8,128)(2,1)S(1)}, bf16[32,1152]{1,0:T(8,128)(2,1)S(1)}, u32[]{:S(2)}, u32[]{:S(2)}) collective-permute-start(bf16[32,1152]{1,0:T(8,128)(2,1)S(1)} %fetch.7), channel_id=1, source_target_pairs={{28,24},{29,25},{30,26},{31,27}} | collective-permute-start | bytes 221192 | tf_op jit(solution)/shard_map/ppermute | solution.py:44
  10.7 18.1 %collective-permute-start.3 = (bf16[32,1152]{1,0:T(8,128)(2,1)S(1)}, bf16[32,1152]{1,0:T(8,128)(2,1)S(1)}, u32[]{:S(2)}, u32[]{:S(2)}) collective-permute-start(bf16[32,1152]{1,0:T(8,128)(2,1)S(1)} %fetch.7), channel_id=1, source_target_pairs={{0,4},{4,8},{8,12},{12,16},{16,20},{20,24},{24,28},{1,5},{5,9},{9,... | collective-permute-start | bytes 221192 | tf_op jit(solution)/shard_map/ppermute | solution.py:43
  18.4 10.3 %collective-permute-start.6 = (bf16[80,1152]{1,0:T(8,128)(2,1)S(1)}, bf16[80,1152]{1,0:T(8,128)(2,1)S(1)}, u32[]{:S(2)}, u32[]{:S(2)}) collective-permute-start(bf16[80,1152]{1,0:T(8,128)(2,1)S(1)} %fetch.8), channel_id=1, source_target_pairs={{0,4},{4,8},{8,12},{12,16},{16,20},{20,24},{24,28},{28,0},{1,5},{5... | collective-permute-start | bytes 552968 | tf_op jit(solution)/shard_map/ppermute | solution.py:20
  21.2 7.6 %collective-permute-start.7 = (bf16[48,1152]{1,0:T(8,128)(2,1)S(1)}, bf16[48,1152]{1,0:T(8,128)(2,1)S(1)}, u32[]{:S(2)}, u32[]{:S(2)}) collective-permute-start(bf16[48,1152]{1,0:T(8,128)(2,1)S(1)} %fetch.9), channel_id=1, source_target_pairs={{0,4},{4,8},{8,12},{12,16},{16,20},{20,24},{24,28},{28,0},{1,5},{5... | collective-permute-start | bytes 331784 | tf_op jit(solution)/shard_map/ppermute | solution.py:20
  24.3 4.5 %collective-permute-start.5 = (bf16[32,1152]{1,0:T(8,128)(2,1)S(1)}, bf16[32,1152]{1,0:T(8,128)(2,1)S(1)}, u32[]{:S(2)}, u32[]{:S(2)}) collective-permute-start(bf16[32,1152]{1,0:T(8,128)(2,1)S(1)} %pass_on.5), channel_id=1, source_target_pairs={{24,0},{25,1},{26,2},{27,3}} | collective-permute-start | bytes 221192 | tf_op jit(solution)/shard_map/ppermute | solution.py:45
  28.7 17.2 %collective-permute-start.10 = (bf16[256,1152]{1,0:T(8,128)(2,1)S(1)}, bf16[256,1152]{1,0:T(8,128)(2,1)S(1)}, u32[]{:S(2)}, u32[]{:S(2)}) collective-permute-start(bf16[256,1152]{1,0:T(8,128)(2,1)S(1)} %pass_on.6.refs_4_), channel_id=1, source_target_pairs={{0,28},{4,0},{8,4},{12,8},{16,12},{20,16},{24,20},{28,24},{1,29},{... | collective-permute-start | bytes 1769480 | tf_op jit(solution)/shard_map/ppermute | solution.py:20
  30.6 16.2 %collective-permute-start.8 = (bf16[416,1152]{1,0:T(8,128)(2,1)S(1)}, bf16[416,1152]{1,0:T(8,128)(2,1)S(1)}, u32[]{:S(2)}, u32[]{:S(2)}) collective-permute-start(bf16[416,1152]{1,0:T(8,128)(2,1)S(1)} %fusion.3.refs_1_), channel_id=1, source_target_pairs={{0,1},{1,2},{2,3},{3,0},{4,5},{5,6},{6,7},{7,4},{8,9},{9,10},{10,1... | collective-permute-start | bytes 2875400 | tf_op jit(solution)/shard_map/ppermute | solution.py:20
  30.7 21.9 %collective-permute-start.9 = (bf16[160,1152]{1,0:T(8,128)(2,1)S(1)}, bf16[160,1152]{1,0:T(8,128)(2,1)S(1)}, u32[]{:S(2)}, u32[]{:S(2)}) collective-permute-start(bf16[160,1152]{1,0:T(8,128)(2,1)S(1)} %pass_on.7), channel_id=1, source_target_pairs={{0,28},{4,0},{8,4},{12,8},{16,12},{20,16},{24,20},{28,24},{1,29},{... | collective-permute-start | bytes 1105928 | tf_op jit(solution)/shard_map/ppermute | solution.py:20

commit v9 on v6

--- a/solution.py
+++ b/solution.py
@@ -1,3 +1,5 @@
+import functools
+
 import jax
 import jax.numpy as jnp
 from jax import lax
@@ -6,6 +8,7 @@
 from jax.sharding import PartitionSpec as P
 
 MIB = 2**20
+APART = 32
 SMEM = pl.BlockSpec(memory_space=pltpu.SMEM)
 VMEM = pl.BlockSpec(memory_space=pltpu.VMEM)
 HBM = pl.BlockSpec(memory_space=pltpu.HBM)
@@ -31,7 +34,7 @@
 
 def row_cuts(rows):
     tiles = rows // 16
-    cuts = [0, tiles * 6 // 26 * 16, tiles * 16 // 26 * 16, tiles * 20 // 26 * 16, rows]
+    cuts = [0] + [tiles * ends // 26 * 16 for ends in (6, 16, 23)] + [rows]
     return list(zip(cuts[:-1], cuts[1:]))
 
 
@@ -65,8 +68,8 @@
     )(array, *after)
 
 
-def chunk_kernel(scale_ref, bias_ref, image_ref, next_ref, upper_ref, lower_ref, *refs):
-    sent_ref, joined_ref, own_ref, other_ref = refs[-4:]
+def chunk_kernel(apart, scale_ref, bias_ref, image_ref, next_ref, upper_ref, lower_ref, *refs):
+    joined_ref, own_ref, other_ref, *sent_refs = refs[-4 - bool(apart) :]
     scale, bias = scale_ref[0], bias_ref[0]
     rows = upper_ref.shape[0]
     joined_ref[:rows, :] = upper_ref[...]
@@ -80,19 +83,24 @@
     other = jax.nn.sigmoid(dot_nt(part, image) * scale + bias).astype(jnp.bfloat16)
     other_ref[...] = other
     total += dot_nn(other, image)
-    sent_ref[...] = (scale * total).astype(jnp.bfloat16)
-
-
-def chunk(factor, shift, image, image_next, upper, lower, after):
+    total = (scale * total).astype(jnp.bfloat16)
+    start = 0
+    for sent_ref in sent_refs:
+        sent_ref[...] = total[start : start + sent_ref.shape[0], :]
+        start += sent_ref.shape[0]
+
+
+def chunk(factor, shift, image, image_next, upper, lower, after, apart=0):
     rows, width = upper.shape[0] + lower.shape[0], upper.shape[1]
     columns = image.shape[0]
-    text = jax.ShapeDtypeStruct((rows, width), jnp.bfloat16)
     tile = jax.ShapeDtypeStruct((rows, columns), jnp.bfloat16)
-    return pl.pallas_call(
-        chunk_kernel,
-        out_shape=(text, text, tile, tile),
+    shapes = [jax.ShapeDtypeStruct((rows, width), jnp.bfloat16), tile, tile]
+    shapes += [jax.ShapeDtypeStruct((r, width), jnp.bfloat16) for r in (rows - apart, apart) if r]
+    return pl.pallas_call(
+        functools.partial(chunk_kernel, apart),
+        out_shape=shapes,
         in_specs=[SMEM] * 2 + [VMEM] * 4 + [ANY] * len(after),
-        out_specs=(VMEM,) * 4,
+        out_specs=[VMEM] * len(shapes),
         compiler_params=pltpu.CompilerParams(vmem_limit_bytes=16 * MIB),
         cost_estimate=pl.CostEstimate(
             flops=8 * rows * columns * width,
@@ -103,21 +111,33 @@
     )(factor, shift, image, image_next, upper, lower, *after)
 
 
-def add_rows(total, back, lo, result, after, mark=False):
-    rows, width = back.shape
-    step = rows // 16 // 3 * 16 if rows >= 96 else rows
-    cuts = [(i, min(i + step, rows)) for i in range(0, rows, step)]
-
-    def kernel(total_ref, back_ref, *refs):
+def add_rows(total, pieces, result, after, mark=False):
+    width = total.shape[1]
+    arrays = [array for _, backs in pieces for array in backs]
+    steps = []
+    first = 0
+    for lo, backs in pieces:
+        rows = backs[0].shape[0]
+        step = rows // 16 // 3 * 16 if rows >= 96 else rows
+        for start in range(0, rows, step):
+            stop = min(start + step, rows)
+            steps.append((lo, start, stop, range(first, first + len(backs))))
+        first += len(backs)
+    low = min(lo for lo, _ in pieces)
+    high = max(lo + backs[0].shape[0] for lo, backs in pieces)
+
+    def kernel(total_ref, *refs):
         buffer, sems = refs[-2:]
         result_ref = refs[-4] if mark else refs[-3]
         copies = []
-        for i, (a, b) in enumerate(cuts):
-            buffer[a:b, :] = (total_ref[lo + a : lo + b, :] + back_ref[a:b, :].astype(jnp.float32)).astype(jnp.bfloat16)
+        for i, (lo, start, stop, backs) in enumerate(steps):
+            rows = total_ref[lo + start : lo + stop, :]
+            for back in backs:
+                rows += refs[back][start:stop, :].astype(jnp.float32)
+            held = buffer.at[pl.ds(lo + start - low, stop - start), :]
+            held[...] = rows.astype(jnp.bfloat16)
             copies.append(
-                pltpu.make_async_copy(
-                    buffer.at[pl.ds(a, b - a), :], result_ref.at[pl.ds(lo + a, b - a), :], sems.at[i]
-                )
+                pltpu.make_async_copy(held, result_ref.at[pl.ds(lo + start, stop - start), :], sems.at[i])
             )
             copies[-1].start()
         if mark:
@@ -130,13 +150,13 @@
     return pl.pallas_call(
         kernel,
         out_shape=(out, jax.ShapeDtypeStruct((8, 128), jnp.float32)) if mark else out,
-        in_specs=[VMEM, VMEM] + [HBM] * len(kept) + [ANY] * len(after),
+        in_specs=[VMEM] * (1 + len(arrays)) + [HBM] * len(kept) + [ANY] * len(after),
         out_specs=(HBM, VMEM) if mark else HBM,
-        scratch_shapes=[pltpu.VMEM((rows, width), jnp.bfloat16), pltpu.SemaphoreType.DMA((len(cuts),))],
-        input_output_aliases={2: 0} if kept else {},
+        scratch_shapes=[pltpu.VMEM((high - low, width), jnp.bfloat16), pltpu.SemaphoreType.DMA((len(steps),))],
+        input_output_aliases={1 + len(arrays): 0} if kept else {},
         compiler_params=pltpu.CompilerParams(vmem_limit_bytes=4 * MIB),
         name="add_rows",
-    )(total, back, *kept, *after)
+    )(total, *arrays, *kept, *after)
 
 
 def body(image, text, target, factor, shift):
@@ -158,25 +178,29 @@
     text_grad = dot_tn(own, image)
 
     image_next = pass_on(image_next, [image_grad, text_grad])
-    sent0, part0, own0, next0 = chunk(factor, shift, image, image_next, part[0], part[1], [])
+    part0, own0, next0, sent0, apart = chunk(factor, shift, image, image_next, part[0], part[1], [], apart=APART)
     next_own = jax.nn.sigmoid(dot_nt(image_next, text) * scale + bias).astype(jnp.bfloat16)
     text_grad = scale * (text_grad + dot_tn(next_own, image_next))
     image_sent = dot_nn(next_own, text) + dot_tn(next0, part0)
     image_grad = image_grad + dot_tn(own0, part0)
 
-    sent0 = pass_on(sent0, [part[2], image_sent])
+    devices = lax.axis_size("blk")
+    sent0, apart = pass_on(sent0, [part[2], image_sent]), pass_on(apart, [part[2], image_sent])
     back0 = shifted(sent0, "blk", -1)
-
-    sent1, part1, own1, next1 = chunk(factor, shift, image, image_next, part[2], part[3], [sent0])
+    half_way = lax.ppermute(apart, "blk", [(1, 2)])
+    near = lax.ppermute(apart, "blk", [(i, (i - 1) % devices) for i in range(devices) if i != 1])
+
+    part1, own1, next1, sent1 = chunk(factor, shift, image, image_next, part[2], part[3], [sent0, half_way])
     image_sent = (scale * (image_sent + dot_tn(next1, part1))).astype(jnp.bfloat16)
     image_back = shifted(image_sent, "grp", 1)
     sent1 = pass_on(sent1, [image_sent])
     back1 = shifted(sent1, "blk", -1)
+    far = lax.ppermute(half_way, "blk", [(2, 0)])
     image_grad = scale * (image_grad + dot_tn(own1, part1))
 
-    result = add_rows(text_grad, back0, 0, None, [])
-    image_grad, mark = add_rows(image_grad, image_back, 0, None, [], mark=True)
-    result = add_rows(text_grad, back1, cuts[2][0], result, [mark])
+    result = add_rows(text_grad, [(0, [back0]), (cuts[2][0] - APART, [near, far])], None, [])
+    image_grad, mark = add_rows(image_grad, [(0, [image_back])], None, [], mark=True)
+    result = add_rows(text_grad, [(cuts[2][0], [back1])], result, [mark])
     return image_grad, result
 
 

time: 54.9 us -> 57.2 us (1.042)
  starting transfers between devices: 9 us -> 14.7 us
  waiting for transfers between devices: 28.5 us -> 25.1 us
    ppermute x8, waiting for transfers between devices: 28.5 us -> 9.61 us  [shifted(): lax.ppermute(shard, axis, [(i, (i + by) % devices) for i in range(devices)])]
    ppermute x0 -> x3, waiting for transfers between devices: none -> 15.5 us  [the longest x1 15.5 us: body(): far = lax.ppermute(half_way, 'blk', [(2, 0)])]
    ppermute x0 -> x3, starting transfers between devices: none -> 5.91 us  [the longest x1 3.97 us: body(): lax.ppermute(apart, 'blk', [(i, (i - 1) % devices) for i in range(devices...]
  transfers between devices with their start and end apart: 8 -> 11, of which waited for: 6 -> 4; matrix products, arithmetic and copies ran while one was open for 12% -> 12% of each run, Pallas kernels for 10% -> 10%
where the time goes in v9:
time: 57.2 us; the launch traced here: 57 us
  waiting for transfers between devices  25.1 us (44%)
  starting transfers between devices  14.7 us (26%)
  matrix products  6.58 us (12%)
  Pallas kernels  6.28 us (11%)
  between operations  2.19 us (4%)
  local copies, waits for them, and re-layouts  2.16 us (4%)
    ppermute x1, waiting for transfers between devices, body(): far = lax.ppermute(half_way, 'blk', [(2, 0)])  15.5 us
    ppermute x8, waiting for transfers between devices, shifted(): lax.ppermute(shard, axis, [(i, (i + by) % devices) for i in range(devices)])  9.61 us
    ppermute x8, starting transfers between devices, shifted(): lax.ppermute(shard, axis, [(i, (i + by) % devices) for i in range(devices)])  8.79 us
    ppermute x1, starting transfers between devices, body(): lax.ppermute(apart, 'blk', [(i, (i - 1) % devices) for i in range(devices...  3.97 us
    dot_general x6, matrix products, dot_tn(): lax.dot_general(a, b, (((0,), (0,)), ((), ())), preferred_element_type=jn...  3.46 us
    pallas_call x2, Pallas kernels, chunk(): pl.pallas_call(functools.partial(chunk_kernel, apart), out_shape=shapes,...  2.9 us
    pallas_call x3, Pallas kernels, add_rows(): pl.pallas_call(kernel, out_shape=(out, jax.ShapeDtypeStruct((8, 128), jnp...  2.7 us
    dot_general x2, matrix products, dot_nt(): lax.dot_general(a, b, (((1,), (1,)), ((), ())), preferred_element_type=jn...  1.72 us
  transfers between devices with their start and end apart: 11, of which 4 were waited for; matrix products, arithmetic and copies ran while one was open for 12% of the time, Pallas kernels for 10%

profile of v9, /device:TPU:0, one launch (start us, length us, event | category | flops | bytes accessed | tf_op | source)
XLA Modules:
  0.0 57.0 jit_solution(5120917310354560467)
XLA Ops:
  0.6 1.0 %slice.3.refs_0_ = bf16[96,1152]{1,0:T(8,128)(2,1)S(1)} slice(bf16[416,1152]{1,0:T(8,128)(2,1)} %array_ref.7), slice={[0:96], [0:1152]} | slice | bytes 442368 | tf_op jit(solution)/shard_map/slice | solution.py:166
  1.6 3.0 %collective-permute-start = (bf16[96,1152]{1,0:T(8,128)(2,1)S(1)}, bf16[96,1152]{1,0:T(8,128)(2,1)S(1)}, u32[]{:S(2)}, u32[]{:S(2)}) collective-permute-start(bf16[96,1152]{1,0:T(8,128)(2,1)S(1)} %slice.3.refs_0_), channel_id=1, source_target_pairs={{0,4},{4,8},{8,12},{12,16},{16,20},{20,24},{24,28},{28,0},{1,5},{5... | collective-permute-start | bytes 663560 | tf_op jit(solution)/shard_map/ppermute | solution.py:20
  4.6 0.7 %collective-permute-start.1 = (bf16[416,1152]{1,0:T(8,128)(2,1)}, bf16[416,1152]{1,0:T(8,128)(2,1)S(1)}, u32[]{:S(2)}, u32[]{:S(2)}) collective-permute-start(bf16[416,1152]{1,0:T(8,128)(2,1)} %image_ref.3), channel_id=1, source_target_pairs={{0,3},{1,0},{2,1},{3,2},{4,7},{5,4},{6,5},{7,6},{8,11},{9,8},{10,9... | collective-permute-start | bytes 2875400 | tf_op jit(solution)/shard_map/ppermute | solution.py:20
  5.3 1.2 %copy-done = bf16[416,1152]{1,0:T(8,128)(2,1)S(1)} copy-done((bf16[416,1152]{1,0:T(8,128)(2,1)S(1)}, bf16[416,1152]{1,0:T(8,128)(2,1)}, u32[]{:S(2)}) %copy-start) | copy-done | bytes 958488
  6.5 0.2 fetch.5
  6.6 1.6 %collective-permute-start.2 = (bf16[160,1152]{1,0:T(8,128)(2,1)S(1)}, bf16[160,1152]{1,0:T(8,128)(2,1)S(1)}, u32[]{:S(2)}, u32[]{:S(2)}) collective-permute-start(bf16[160,1152]{1,0:T(8,128)(2,1)S(1)} %fetch.5), channel_id=1, source_target_pairs={{0,4},{4,8},{8,12},{12,16},{16,20},{20,24},{24,28},{28,0},{1,5},{5... | collective-permute-start | bytes 1105928 | tf_op jit(solution)/shard_map/ppermute | solution.py:20
  9.5 4.3 %collective-permute-done.refs_0_.upper_ref = bf16[96,1152]{1,0:T(8,128)(2,1)S(1)} collective-permute-done((bf16[96,1152]{1,0:T(8,128)(2,1)S(1)}, bf16[96,1152]{1,0:T(8,128)(2,1)S(1)}, u32[]{:S(2)}, u32[]{:S(2)}) %collective-permute-start) | collective-permute-done | bytes 221216 | tf_op jit(solution)/shard_map/ppermute | solution.py:20
  13.9 0.3 fetch.6
  14.3 0.9 %subtract_convert_fusion.refs_0_ = bf16[416,416]{1,0:T(8,128)(2,1)S(1)} fusion(s32[416]{0:T(512)S(1)} %bitcast.30, f32[]{:T(128)} %bitcast.28, bf16[416,1152]{1,0:T(8,128)(2,1)S(1)} %copy-done.2, bf16[416,1152]{1,0:T(8,128)(2,1)S(1)} %copy-done.1, f32[]{:T(128)} %bitcast.24), kind=kOutput, calls=%fused_computation.22 | convolution fusion | flops 400278528 | bytes 2264712 | tf_op jit(solution)/shard_map/dot_general | solution.py:24
  15.4 1.5 %collective-permute-start.4 = (bf16[48,1152]{1,0:T(8,128)(2,1)S(1)}, bf16[48,1152]{1,0:T(8,128)(2,1)S(1)}, u32[]{:S(2)}, u32[]{:S(2)}) collective-permute-start(bf16[48,1152]{1,0:T(8,128)(2,1)S(1)} %fetch.7), channel_id=1, source_target_pairs={{0,4},{4,8},{8,12},{12,16},{16,20},{20,24},{24,28},{28,0},{1,5},{5... | collective-permute-start | bytes 331784 | tf_op jit(solution)/shard_map/ppermute | solution.py:20
  16.9 0.7 %fusion.16.refs_2_ = f32[416,1152]{1,0:T(8,128)S(1)} fusion(bf16[416,416]{1,0:T(8,128)(2,1)S(1)} %subtract_convert_fusion.refs_0_, bf16[416,1152]{1,0:T(8,128)(2,1)S(1)} %copy-done.2), kind=kOutput, calls=%fused_computation.25 | convolution fusion | flops 398721024 | bytes 3221504 | tf_op jit(solution)/shard_map/dot_general | solution.py:28
  17.6 0.7 %fusion.15.refs_1_ = f32[416,1152]{1,0:T(8,128)S(1)} fusion(bf16[416,416]{1,0:T(8,128)(2,1)S(1)} %subtract_convert_fusion.refs_0_, bf16[416,1152]{1,0:T(8,128)(2,1)S(1)} %copy-done.1), kind=kOutput, calls=%fused_computation.24 | convolution fusion | flops 398721024 | bytes 3221504 | tf_op jit(solution)/shard_map/dot_general | solution.py:32
  18.4 0.8 %fusion.14 = bf16[416,416]{1,0:T(8,128)(2,1)S(1)} fusion(bf16[416,1152]{1,0:T(8,128)(2,1)S(1)} %pass_on.4.next_ref, bf16[416,1152]{1,0:T(8,128)(2,1)S(1)} %copy-done.1, f32[]{:T(128)} %bitcast.29, f32[]{:T(128)} %bitcast.27), kind=kOutput, calls=%fused_computation.21 | convolution fusion | flops 399759360 | bytes 2263048 | tf_op jit(solution)/shard_map/dot_general | solution.py:24
  19.2 0.7 %fusion.17 = f32[416,1152]{1,0:T(8,128)S(1)} fusion(bf16[416,416]{1,0:T(8,128)(2,1)S(1)} %fusion.14, bf16[416,1152]{1,0:T(8,128)(2,1)S(1)} %copy-done.1), kind=kOutput, calls=%fused_computation.26 | convolution fusion | flops 398721024 | bytes 3221504 | tf_op jit(solution)/shard_map/dot_general | solution.py:32
  19.9 1.9 %collective-permute-done.2.lower_ref = bf16[160,1152]{1,0:T(8,128)(2,1)S(1)} collective-permute-done((bf16[160,1152]{1,0:T(8,128)(2,1)S(1)}, bf16[160,1152]{1,0:T(8,128)(2,1)S(1)}, u32[]{:S(2)}, u32[]{:S(2)}) %collective-permute-start.2) | collective-permute-done | bytes 368672 | tf_op jit(solution)/shard_map/ppermute | solution.py:20
  21.8 1.6 %chunk.2 = (bf16[256,1152]{1,0:T(8,128)(2,1)S(1)}, bf16[256,416]{1,0:T(8,128)(2,1)S(1)}, bf16[256,416]{1,0:T(8,128)(2,1)S(1)}, bf16[224,1152]{1,0:T(8,128)(2,1)S(1)}, bf16[32,1152]{1,0:T(8,128)(2,1)S(1)}) custom-call(f32[1]{0:T(128)} %copy.17.scale_ref, f32[1]{0:T(128)} %copy.18.bias_ref, bf16[416,1152]{1,0:T(8,128)(2,1)S(1)} %copy-done.2, ...), custom_call_target="tpu_custom_call" | custom-call | flops 981467136 | bytes 3686400 | tf_op jit(solution)/shard_map/chunk/pallas_call | solution.py:99
  23.4 0.5 convolution_add_fusion.3.refs_2_
  23.9 3.4 %collective-permute-done.3.refs_1_.upper_ref = bf16[112,1152]{1,0:T(8,128)(2,1)S(1)} collective-permute-done((bf16[112,1152]{1,0:T(8,128)(2,1)S(1)}, bf16[112,1152]{1,0:T(8,128)(2,1)S(1)}, u32[]{:S(2)}, u32[]{:S(2)}) %collective-permute-start.3) | collective-permute-done | bytes 258080 | tf_op jit(solution)/shard_map/ppermute | solution.py:20
  27.3 0.7 %collective-permute-start.5 = (bf16[32,1152]{1,0:T(8,128)(2,1)S(1)}, bf16[32,1152]{1,0:T(8,128)(2,1)S(1)}, u32[]{:S(2)}, u32[]{:S(2)}) collective-permute-start(bf16[32,1152]{1,0:T(8,128)(2,1)S(1)} %pass_on.6), channel_id=1, source_target_pairs={{4,8},{5,9},{6,10},{7,11}} | collective-permute-start | bytes 221192 | tf_op jit(solution)/shard_map/ppermute | solution.py:190
  28.0 4.0 %collective-permute-start.9 = (bf16[32,1152]{1,0:T(8,128)(2,1)S(1)}, bf16[32,1152]{1,0:T(8,128)(2,1)S(1)}, u32[]{:S(2)}, u32[]{:S(2)}) collective-permute-start(bf16[32,1152]{1,0:T(8,128)(2,1)S(1)} %pass_on.6), channel_id=1, source_target_pairs={{0,28},{8,4},{12,8},{16,12},{20,16},{24,20},{28,24},{1,29},{9,5},{... | collective-permute-start | bytes 221192 | tf_op jit(solution)/shard_map/ppermute | solution.py:191
  32.0 1.5 %collective-permute-start.8 = (bf16[224,1152]{1,0:T(8,128)(2,1)S(1)}, bf16[224,1152]{1,0:T(8,128)(2,1)S(1)}, u32[]{:S(2)}, u32[]{:S(2)}) collective-permute-start(bf16[224,1152]{1,0:T(8,128)(2,1)S(1)} %pass_on.5.refs_0_), channel_id=1, source_target_pairs={{0,28},{4,0},{8,4},{12,8},{16,12},{20,16},{24,20},{28,24},{1,29},{... | collective-permute-start | bytes 1548296 | tf_op jit(solution)/shard_map/ppermute | solution.py:20
  33.5 1.3 %chunk.3 = (bf16[160,1152]{1,0:T(8,128)(2,1)S(1)}, bf16[160,416]{1,0:T(8,128)(2,1)S(1)}, bf16[160,416]{1,0:T(8,128)(2,1)S(1)}, bf16[160,1152]{1,0:T(8,128)(2,1)S(1)}) custom-call(f32[1]{0:T(128)} %copy.17.scale_ref, f32[1]{0:T(128)} %copy.18.bias_ref, bf16[416,1152]{1,0:T(8,128)(2,1)S(1)} %copy-done.2, bf16[416,1152]{1,0:T(8,128)(2,1)S(1)} %pass_on.4.next_ref, ...), custom_call_target="tpu_custom_call" | custom-call | flops 613416960 | bytes 3022848 | tf_op jit(solution)/shard_map/chunk/pallas_call | solution.py:99
  34.7 0.5 fusion.3.refs_1_
  35.3 0.7 %fusion.total_ref = f32[416,1152]{1,0:T(8,128)S(1)} fusion(f32[416,1152]{1,0:T(8,128)S(1)} %fusion.16.refs_2_, bf16[416,416]{1,0:T(8,128)(2,1)S(1)} %fusion.14, bf16[416,1152]{1,0:T(8,128)(2,1)S(1)} %pass_on.4.next_ref, f32[]{:T(128)} %bitcast.25), kind=kOutput, calls=%fused_computation.1 | convolution fusion | flops 399679488 | bytes 5138436 | tf_op jit(solution)/shard_map/dot_general | solution.py:28
  36.1 0.4 collective-permute-start.7
  36.5 0.5 convolution_add_fusion.4
  37.0 1.3 %collective-permute-start.10 = (bf16[32,1152]{1,0:T(8,128)(2,1)S(1)}, bf16[32,1152]{1,0:T(8,128)(2,1)S(1)}, u32[]{:S(2)}, u32[]{:S(2)}) collective-permute-start(bf16[32,1152]{1,0:T(8,128)(2,1)S(1)} %collective-permute-done.5.refs_1_), channel_id=1, source_target_pairs={{8,0},{9,1},{10,2},{11,3}} | collective-permute-start | bytes 221192 | tf_op jit(solution)/shard_map/ppermute | solution.py:198
  38.3 0.5 fusion.2.total_ref
  38.8 15.5 %collective-permute-done.10.refs_2_ = bf16[32,1152]{1,0:T(8,128)(2,1)S(1)} collective-permute-done((bf16[32,1152]{1,0:T(8,128)(2,1)S(1)}, bf16[32,1152]{1,0:T(8,128)(2,1)S(1)}, u32[]{:S(2)}, u32[]{:S(2)}) %collective-permute-start.10) | collective-permute-done | bytes 73760 | tf_op jit(solution)/shard_map/ppermute | solution.py:198
  54.3 0.9 %add_rows.4.refs_1_ = bf16[416,1152]{1,0:T(8,128)(2,1)} custom-call(f32[416,1152]{1,0:T(8,128)S(1)} %fusion.total_ref, bf16[224,1152]{1,0:T(8,128)(2,1)S(1)} %collective-permute-done.8.refs_0_, bf16[32,1152]{1,0:T(8,128)(2,1)S(1)} %collective-permute-done.9.refs_1_, bf16[32,1152]{1,0:T(8,128)(2,1)S(1)} %collective-permute-done.10.refs_2_), custom_call_target="tpu_custom_call" | custom-call | tf_op jit(solution)/shard_map/add_rows/pallas_call | solution.py:150
  55.2 1.0 %add_rows.3 = (bf16[416,1152]{1,0:T(8,128)(2,1)}, f32[8,128]{1,0:T(8,128)S(1)}) custom-call(f32[416,1152]{1,0:T(8,128)S(1)} %fusion.2.total_ref, bf16[416,1152]{1,0:T(8,128)(2,1)S(1)} %collective-permute-done.6.refs_0_), custom_call_target="tpu_custom_call" | custom-call | tf_op jit(solution)/shard_map/add_rows/pallas_call | solution.py:150
  56.2 0.8 %add_rows.5 = bf16[416,1152]{1,0:T(8,128)(2,1)} custom-call(f32[416,1152]{1,0:T(8,128)S(1)} %fusion.total_ref, bf16[160,1152]{1,0:T(8,128)(2,1)S(1)} %collective-permute-done.7.refs_0_, bf16[416,1152]{1,0:T(8,128)(2,1)} %add_rows.4.refs_1_, f32[8,128]{1,0:T(8,128)S(1)} %get-tuple-element.23.refs_2_), custom_call_target="tpu_custom_call", output_to_operand_aliasing={{}: (2, {})} | custom-call | tf_op jit(solution)/shard_map/add_rows/pallas_call | solution.py:150
  (22 shorter events, 0.3 us)
Async XLA Ops:
  0.6 13.3 %copy-start.3 = (s32[1,416]{1,0:T(1,128)S(1)}, s32[1,416]{1,0:T(1,128)}, u32[]{:S(2)}) copy-start(s32[1,416]{1,0:T(1,128)} %array_ref.4) | copy-start | bytes 4996
  1.6 12.3 %collective-permute-start = (bf16[96,1152]{1,0:T(8,128)(2,1)S(1)}, bf16[96,1152]{1,0:T(8,128)(2,1)S(1)}, u32[]{:S(2)}, u32[]{:S(2)}) collective-permute-start(bf16[96,1152]{1,0:T(8,128)(2,1)S(1)} %slice.3.refs_0_), channel_id=1, source_target_pairs={{0,4},{4,8},{8,12},{12,16},{16,20},{20,24},{24,28},{28,0},{1,5},{5... | collective-permute-start | bytes 663560 | tf_op jit(solution)/shard_map/ppermute | solution.py:20
  4.6 13.8 %collective-permute-start.1 = (bf16[416,1152]{1,0:T(8,128)(2,1)}, bf16[416,1152]{1,0:T(8,128)(2,1)S(1)}, u32[]{:S(2)}, u32[]{:S(2)}) collective-permute-start(bf16[416,1152]{1,0:T(8,128)(2,1)} %image_ref.3), channel_id=1, source_target_pairs={{0,3},{1,0},{2,1},{3,2},{4,7},{5,4},{6,5},{7,6},{8,11},{9,8},{10,9... | collective-permute-start | bytes 2875400 | tf_op jit(solution)/shard_map/ppermute | solution.py:20
  5.3 1.2 %copy-start = (bf16[416,1152]{1,0:T(8,128)(2,1)S(1)}, bf16[416,1152]{1,0:T(8,128)(2,1)}, u32[]{:S(2)}) copy-start(bf16[416,1152]{1,0:T(8,128)(2,1)} %array_ref.7) | copy-start | bytes 2875396
  6.5 7.4 %copy-start.1 = (bf16[416,1152]{1,0:T(8,128)(2,1)S(1)}, bf16[416,1152]{1,0:T(8,128)(2,1)}, u32[]{:S(2)}) copy-start(bf16[416,1152]{1,0:T(8,128)(2,1)} %array_ref.7) | copy-start | bytes 2875396
  6.5 7.9 %copy-start.2 = (bf16[416,1152]{1,0:T(8,128)(2,1)S(1)}, bf16[416,1152]{1,0:T(8,128)(2,1)}, u32[]{:S(2)}) copy-start(bf16[416,1152]{1,0:T(8,128)(2,1)} %image_ref.3) | copy-start | bytes 2875396
  6.6 15.1 %collective-permute-start.2 = (bf16[160,1152]{1,0:T(8,128)(2,1)S(1)}, bf16[160,1152]{1,0:T(8,128)(2,1)S(1)}, u32[]{:S(2)}, u32[]{:S(2)}) collective-permute-start(bf16[160,1152]{1,0:T(8,128)(2,1)S(1)} %fetch.5), channel_id=1, source_target_pairs={{0,4},{4,8},{8,12},{12,16},{16,20},{20,24},{24,28},{28,0},{1,5},{5... | collective-permute-start | bytes 1105928 | tf_op jit(solution)/shard_map/ppermute | solution.py:20
  14.3 13.0 %collective-permute-start.3 = (bf16[112,1152]{1,0:T(8,128)(2,1)S(1)}, bf16[112,1152]{1,0:T(8,128)(2,1)S(1)}, u32[]{:S(2)}, u32[]{:S(2)}) collective-permute-start(bf16[112,1152]{1,0:T(8,128)(2,1)S(1)} %fetch.6), channel_id=1, source_target_pairs={{0,4},{4,8},{8,12},{12,16},{16,20},{20,24},{24,28},{28,0},{1,5},{5... | collective-permute-start | bytes 774152 | tf_op jit(solution)/shard_map/ppermute | solution.py:20
  15.4 18.1 %collective-permute-start.4 = (bf16[48,1152]{1,0:T(8,128)(2,1)S(1)}, bf16[48,1152]{1,0:T(8,128)(2,1)S(1)}, u32[]{:S(2)}, u32[]{:S(2)}) collective-permute-start(bf16[48,1152]{1,0:T(8,128)(2,1)S(1)} %fetch.7), channel_id=1, source_target_pairs={{0,4},{4,8},{8,12},{12,16},{16,20},{20,24},{24,28},{28,0},{1,5},{5... | collective-permute-start | bytes 331784 | tf_op jit(solution)/shard_map/ppermute | solution.py:20
  27.3 6.1 %collective-permute-start.5 = (bf16[32,1152]{1,0:T(8,128)(2,1)S(1)}, bf16[32,1152]{1,0:T(8,128)(2,1)S(1)}, u32[]{:S(2)}, u32[]{:S(2)}) collective-permute-start(bf16[32,1152]{1,0:T(8,128)(2,1)S(1)} %pass_on.6), channel_id=1, source_target_pairs={{4,8},{5,9},{6,10},{7,11}} | collective-permute-start | bytes 221192 | tf_op jit(solution)/shard_map/ppermute | solution.py:190
  28.0 10.8 %collective-permute-start.9 = (bf16[32,1152]{1,0:T(8,128)(2,1)S(1)}, bf16[32,1152]{1,0:T(8,128)(2,1)S(1)}, u32[]{:S(2)}, u32[]{:S(2)}) collective-permute-start(bf16[32,1152]{1,0:T(8,128)(2,1)S(1)} %pass_on.6), channel_id=1, source_target_pairs={{0,28},{8,4},{12,8},{16,12},{20,16},{24,20},{28,24},{1,29},{9,5},{... | collective-permute-start | bytes 221192 | tf_op jit(solution)/shard_map/ppermute | solution.py:191
  32.0 22.3 %collective-permute-start.8 = (bf16[224,1152]{1,0:T(8,128)(2,1)S(1)}, bf16[224,1152]{1,0:T(8,128)(2,1)S(1)}, u32[]{:S(2)}, u32[]{:S(2)}) collective-permute-start(bf16[224,1152]{1,0:T(8,128)(2,1)S(1)} %pass_on.5.refs_0_), channel_id=1, source_target_pairs={{0,28},{4,0},{8,4},{12,8},{16,12},{20,16},{24,20},{28,24},{1,29},{... | collective-permute-start | bytes 1548296 | tf_op jit(solution)/shard_map/ppermute | solution.py:20
  35.2 19.9 %collective-permute-start.6 = (bf16[416,1152]{1,0:T(8,128)(2,1)S(1)}, bf16[416,1152]{1,0:T(8,128)(2,1)S(1)}, u32[]{:S(2)}, u32[]{:S(2)}) collective-permute-start(bf16[416,1152]{1,0:T(8,128)(2,1)S(1)} %fusion.3.refs_1_), channel_id=1, source_target_pairs={{0,1},{1,2},{2,3},{3,0},{4,5},{5,6},{6,7},{7,4},{8,9},{9,10},{10,1... | collective-permute-start | bytes 2875400 | tf_op jit(solution)/shard_map/ppermute | solution.py:20
  36.1 20.1 %collective-permute-start.7 = (bf16[160,1152]{1,0:T(8,128)(2,1)S(1)}, bf16[160,1152]{1,0:T(8,128)(2,1)S(1)}, u32[]{:S(2)}, u32[]{:S(2)}) collective-permute-start(bf16[160,1152]{1,0:T(8,128)(2,1)S(1)} %pass_on.7), channel_id=1, source_target_pairs={{0,28},{4,0},{8,4},{12,8},{16,12},{20,16},{24,20},{28,24},{1,29},{... | collective-permute-start | bytes 1105928 | tf_op jit(solution)/shard_map/ppermute | solution.py:20
  37.0 17.3 %collective-permute-start.10 = (bf16[32,1152]{1,0:T(8,128)(2,1)S(1)}, bf16[32,1152]{1,0:T(8,128)(2,1)S(1)}, u32[]{:S(2)}, u32[]{:S(2)}) collective-permute-start(bf16[32,1152]{1,0:T(8,128)(2,1)S(1)} %collective-permute-done.5.refs_1_), channel_id=1, source_target_pairs={{8,0},{9,1},{10,2},{11,3}} | collective-permute-start | bytes 221192 | tf_op jit(solution)/shard_map/ppermute | solution.py:198

commit v10 on v8

--- a/solution.py
+++ b/solution.py
@@ -8,7 +8,7 @@
 from jax.sharding import PartitionSpec as P
 
 MIB = 2**20
-ENDS = (6, 16, 18, 23)
+ENDS = (6, 16, 21, 23)
 SMEM = pl.BlockSpec(memory_space=pltpu.SMEM)
 VMEM = pl.BlockSpec(memory_space=pltpu.VMEM)
 HBM = pl.BlockSpec(memory_space=pltpu.HBM)
@@ -36,14 +36,6 @@
     tiles = rows // 16
     cuts = [0] + [tiles * ends // 26 * 16 for ends in ENDS] + [rows]
     return list(zip(cuts[:-1], cuts[1:]))
-
-
-def shifted_with_relay(shard, axis, order):
-    devices = lax.axis_size(axis)
-    near = lax.ppermute(shard, axis, [(i, i + 1) for i in range(devices - 1)])
-    relay = lax.ppermute(shard, axis, [(devices - 1, devices - 2)])
-    far = lax.ppermute(order(relay), axis, [(devices - 2, 0)])
-    return near, far
 
 
 def fetch(array, lo, hi, after):
@@ -160,20 +152,23 @@
     cuts = row_cuts(text.shape[0])
     first = text[: cuts[0][1]]
     part = [shifted(first, "blk", 1)]
+    devices = lax.axis_size("blk")
+    relayed = fetch(text, *cuts[3], [first])
+    half_way = lax.ppermute(relayed, "blk", [(devices - 1, devices - 2)])
     image_next = shifted(image, "grp", -1)
-    part.append(shifted(fetch(text, *cuts[1], [first]), "blk", 1))
-
-    target = fetch(target, 0, 1, [part[0]])
-    relayed = fetch(text, *cuts[2], [target])
+    part.append(shifted(fetch(text, *cuts[1], [relayed]), "blk", 1))
+
+    target = fetch(target, 0, 1, [part[0], half_way])
+    far = lax.ppermute(half_way, "blk", [(devices - 2, 0)])
     own = jax.nn.sigmoid(dot_nt(image, text) * scale + bias)
     column = lax.broadcasted_iota(jnp.int32, own.shape, 1)
     own = (own - (column == target[0][:, None]).astype(jnp.float32)).astype(jnp.bfloat16)
-    rows = fetch(text, *cuts[3], [own])
+    part.append(shifted(fetch(text, *cuts[2], [own]), "blk", 1))
     image_grad = dot_nn(own, text)
     text_grad = dot_tn(own, image)
-    near, far = shifted_with_relay(relayed, "blk", lambda relay: pass_on(relay, [image_grad, text_grad]))
-    part.append(shifted(rows, "blk", 1))
-    part.append(shifted(fetch(text, *cuts[4], [text_grad]), "blk", 1))
+    relayed = pass_on(relayed, [image_grad, text_grad])
+    near = lax.ppermute(relayed, "blk", [(i, i + 1) for i in range(devices - 1)])
+    part.append(shifted(fetch(text, *cuts[4], [relayed]), "blk", 1))
 
     image_next = pass_on(image_next, [image_grad, text_grad])
     sent0, part0, own0, next0 = chunk(
@@ -184,11 +179,11 @@
     image_sent = dot_nn(next_own, text) + dot_tn(next0, part0)
     image_grad = image_grad + dot_tn(own0, part0)
 
-    sent0 = pass_on(sent0, [part[2], image_sent])
+    sent0 = pass_on(sent0, [part[2], near, far, image_sent])
     back0 = shifted(sent0, "blk", -1)
 
     base = cuts[2][0]
-    pieces = [(0, near), (0, far), (cuts[3][0] - base, part[2]), (cuts[4][0] - base, part[3])]
+    pieces = [(0, part[2]), (cuts[3][0] - base, near), (cuts[3][0] - base, far), (cuts[4][0] - base, part[3])]
     sent1, part1, own1, next1 = chunk(factor, shift, image, image_next, pieces, [sent0])
     image_sent = (scale * (image_sent + dot_tn(next1, part1))).astype(jnp.bfloat16)
     image_back = shifted(image_sent, "grp", 1)

time: 53.6 us -> 58.7 us (1.095)
  the two profiles are of different devices: /device:TPU:18 before, /device:TPU:0 now
where the time goes in v10:
time: 58.7 us; the launch traced here: 58.5 us
  waiting for transfers between devices  21 us (36%)
  starting transfers between devices  20.3 us (35%)
  matrix products  6.58 us (11%)
  Pallas kernels  6.28 us (11%)
  local copies, waits for them, and re-layouts  2.16 us (4%)
  between operations  2.16 us (4%)
    ppermute x8, waiting for transfers between devices, shifted(): lax.ppermute(shard, axis, [(i, (i + by) % devices) for i in range(devices)])  17.8 us
    ppermute x8, starting transfers between devices, shifted(): lax.ppermute(shard, axis, [(i, (i + by) % devices) for i in range(devices)])  16.7 us
    dot_general x6, matrix products, dot_tn(): lax.dot_general(a, b, (((0,), (0,)), ((), ())), preferred_element_type=jn...  3.46 us
    ppermute x1, waiting for transfers between devices, body(): far = lax.ppermute(half_way, 'blk', [(devices - 2, 0)])  3.17 us
    pallas_call x2, Pallas kernels, chunk(): pl.pallas_call(functools.partial(chunk_kernel, [lo for lo, _ in pieces]),...  2.91 us
    pallas_call x3, Pallas kernels, add_rows(): pl.pallas_call(kernel, out_shape=(out, jax.ShapeDtypeStruct((8, 128), jnp...  2.7 us
    dot_general x2, matrix products, dot_nt(): lax.dot_general(a, b, (((1,), (1,)), ((), ())), preferred_element_type=jn...  1.72 us
    ppermute x1, starting transfers between devices, body(): lax.ppermute(relayed, 'blk', [(i, i + 1) for i in range(devices - 1)])  1.53 us
  transfers between devices with their start and end apart: 11, of which 7 were waited for; matrix products, arithmetic and copies ran while one was open for 11% of the time, Pallas kernels for 9%

profile of v10, /device:TPU:0, one launch (start us, length us, event | category | flops | bytes accessed | tf_op | source)
XLA Modules:
  0.0 58.5 jit_solution(17014886085324585331)
XLA Ops:
  0.6 1.0 %slice.3.refs_0_ = bf16[96,1152]{1,0:T(8,128)(2,1)S(1)} slice(bf16[416,1152]{1,0:T(8,128)(2,1)} %array_ref.9), slice={[0:96], [0:1152]} | slice | bytes 442368 | tf_op jit(solution)/shard_map/slice | solution.py:153
  1.6 3.0 %collective-permute-start = (bf16[96,1152]{1,0:T(8,128)(2,1)S(1)}, bf16[96,1152]{1,0:T(8,128)(2,1)S(1)}, u32[]{:S(2)}, u32[]{:S(2)}) collective-permute-start(bf16[96,1152]{1,0:T(8,128)(2,1)S(1)} %slice.3.refs_0_), channel_id=1, source_target_pairs={{0,4},{4,8},{8,12},{12,16},{16,20},{20,24},{24,28},{28,0},{1,5},{5... | collective-permute-start | bytes 663560 | tf_op jit(solution)/shard_map/ppermute | solution.py:20
  4.6 1.2 %copy-done = bf16[416,1152]{1,0:T(8,128)(2,1)S(1)} copy-done((bf16[416,1152]{1,0:T(8,128)(2,1)S(1)}, bf16[416,1152]{1,0:T(8,128)(2,1)}, u32[]{:S(2)}) %copy-start) | copy-done | bytes 958488
  5.9 0.8 %collective-permute-start.1 = (bf16[32,1152]{1,0:T(8,128)(2,1)S(1)}, bf16[32,1152]{1,0:T(8,128)(2,1)S(1)}, u32[]{:S(2)}, u32[]{:S(2)}) collective-permute-start(bf16[32,1152]{1,0:T(8,128)(2,1)S(1)} %fetch.5.refs_0_), channel_id=1, source_target_pairs={{28,24},{29,25},{30,26},{31,27}} | collective-permute-start | bytes 221192 | tf_op jit(solution)/shard_map/ppermute | solution.py:157
  6.7 0.7 %collective-permute-start.2 = (bf16[416,1152]{1,0:T(8,128)(2,1)}, bf16[416,1152]{1,0:T(8,128)(2,1)S(1)}, u32[]{:S(2)}, u32[]{:S(2)}) collective-permute-start(bf16[416,1152]{1,0:T(8,128)(2,1)} %image_ref.3), channel_id=1, source_target_pairs={{0,3},{1,0},{2,1},{3,2},{4,7},{5,4},{6,5},{7,6},{8,11},{9,8},{10,9... | collective-permute-start | bytes 2875400 | tf_op jit(solution)/shard_map/ppermute | solution.py:20
  7.6 1.6 %collective-permute-start.3 = (bf16[160,1152]{1,0:T(8,128)(2,1)S(1)}, bf16[160,1152]{1,0:T(8,128)(2,1)S(1)}, u32[]{:S(2)}, u32[]{:S(2)}) collective-permute-start(bf16[160,1152]{1,0:T(8,128)(2,1)S(1)} %fetch.7), channel_id=1, source_target_pairs={{0,4},{4,8},{8,12},{12,16},{16,20},{20,24},{24,28},{28,0},{1,5},{5... | collective-permute-start | bytes 1105928 | tf_op jit(solution)/shard_map/ppermute | solution.py:20
  10.5 1.3 %collective-permute-start.6 = (bf16[32,1152]{1,0:T(8,128)(2,1)S(1)}, bf16[32,1152]{1,0:T(8,128)(2,1)S(1)}, u32[]{:S(2)}, u32[]{:S(2)}) collective-permute-start(bf16[32,1152]{1,0:T(8,128)(2,1)S(1)} %collective-permute-done.1.refs_1_), channel_id=1, source_target_pairs={{24,0},{25,1},{26,2},{27,3}} | collective-permute-start | bytes 221192 | tf_op jit(solution)/shard_map/ppermute | solution.py:162
  11.8 1.3 %collective-permute-done.refs_0_ = bf16[96,1152]{1,0:T(8,128)(2,1)S(1)} collective-permute-done((bf16[96,1152]{1,0:T(8,128)(2,1)S(1)}, bf16[96,1152]{1,0:T(8,128)(2,1)S(1)}, u32[]{:S(2)}, u32[]{:S(2)}) %collective-permute-start) | collective-permute-done | bytes 221216 | tf_op jit(solution)/shard_map/ppermute | solution.py:20
  13.1 0.9 %subtract_convert_fusion.refs_0_ = bf16[416,416]{1,0:T(8,128)(2,1)S(1)} fusion(s32[416]{0:T(512)S(1)} %bitcast.30, f32[]{:T(128)} %bitcast.28, bf16[416,1152]{1,0:T(8,128)(2,1)S(1)} %copy-done.2, bf16[416,1152]{1,0:T(8,128)(2,1)S(1)} %copy-done.1, f32[]{:T(128)} %bitcast.24), kind=kOutput, calls=%fused_computation.22 | convolution fusion | flops 400278528 | bytes 2264712 | tf_op jit(solution)/shard_map/dot_general | solution.py:24
  14.3 0.7 %fusion.16.refs_2_ = f32[416,1152]{1,0:T(8,128)S(1)} fusion(bf16[416,416]{1,0:T(8,128)(2,1)S(1)} %subtract_convert_fusion.refs_0_, bf16[416,1152]{1,0:T(8,128)(2,1)S(1)} %copy-done.2), kind=kOutput, calls=%fused_computation.25 | convolution fusion | flops 398721024 | bytes 3221504 | tf_op jit(solution)/shard_map/dot_general | solution.py:28
  15.0 0.7 %fusion.15.refs_1_ = f32[416,1152]{1,0:T(8,128)S(1)} fusion(bf16[416,416]{1,0:T(8,128)(2,1)S(1)} %subtract_convert_fusion.refs_0_, bf16[416,1152]{1,0:T(8,128)(2,1)S(1)} %copy-done.1), kind=kOutput, calls=%fused_computation.24 | convolution fusion | flops 398721024 | bytes 3221504 | tf_op jit(solution)/shard_map/dot_general | solution.py:32
  15.7 1.5 %collective-permute-start.5 = (bf16[32,1152]{1,0:T(8,128)(2,1)S(1)}, bf16[32,1152]{1,0:T(8,128)(2,1)S(1)}, u32[]{:S(2)}, u32[]{:S(2)}) collective-permute-start(bf16[32,1152]{1,0:T(8,128)(2,1)S(1)} %pass_on.5.refs_0_), channel_id=1, source_target_pairs={{0,4},{4,8},{8,12},{12,16},{16,20},{20,24},{24,28},{1,5},{5,9},{9,... | collective-permute-start | bytes 221192 | tf_op jit(solution)/shard_map/ppermute | solution.py:170
  17.4 1.7 %collective-permute-start.4 = (bf16[80,1152]{1,0:T(8,128)(2,1)S(1)}, bf16[80,1152]{1,0:T(8,128)(2,1)S(1)}, u32[]{:S(2)}, u32[]{:S(2)}) collective-permute-start(bf16[80,1152]{1,0:T(8,128)(2,1)S(1)} %fetch.8), channel_id=1, source_target_pairs={{0,4},{4,8},{8,12},{12,16},{16,20},{20,24},{24,28},{28,0},{1,5},{5... | collective-permute-start | bytes 552968 | tf_op jit(solution)/shard_map/ppermute | solution.py:20
  19.1 1.5 %collective-permute-start.7 = (bf16[48,1152]{1,0:T(8,128)(2,1)S(1)}, bf16[48,1152]{1,0:T(8,128)(2,1)S(1)}, u32[]{:S(2)}, u32[]{:S(2)}) collective-permute-start(bf16[48,1152]{1,0:T(8,128)(2,1)S(1)} %fetch.9), channel_id=1, source_target_pairs={{0,4},{4,8},{8,12},{12,16},{16,20},{20,24},{24,28},{28,0},{1,5},{5... | collective-permute-start | bytes 331784 | tf_op jit(solution)/shard_map/ppermute | solution.py:20
  20.6 0.8 %fusion.14 = bf16[416,416]{1,0:T(8,128)(2,1)S(1)} fusion(bf16[416,1152]{1,0:T(8,128)(2,1)S(1)} %pass_on.4.next_ref, bf16[416,1152]{1,0:T(8,128)(2,1)S(1)} %copy-done.1, f32[]{:T(128)} %bitcast.29, f32[]{:T(128)} %bitcast.27), kind=kOutput, calls=%fused_computation.21 | convolution fusion | flops 399759360 | bytes 2263048 | tf_op jit(solution)/shard_map/dot_general | solution.py:24
  21.5 0.7 %fusion.17 = f32[416,1152]{1,0:T(8,128)S(1)} fusion(bf16[416,416]{1,0:T(8,128)(2,1)S(1)} %fusion.14, bf16[416,1152]{1,0:T(8,128)(2,1)S(1)} %copy-done.1), kind=kOutput, calls=%fused_computation.26 | convolution fusion | flops 398721024 | bytes 3221504 | tf_op jit(solution)/shard_map/dot_general | solution.py:32
  22.5 1.6 %chunk.2 = (bf16[256,1152]{1,0:T(8,128)(2,1)S(1)}, bf16[256,1152]{1,0:T(8,128)(2,1)S(1)}, bf16[256,416]{1,0:T(8,128)(2,1)S(1)}, bf16[256,416]{1,0:T(8,128)(2,1)S(1)}) custom-call(f32[1]{0:T(128)} %copy.17.scale_ref, f32[1]{0:T(128)} %copy.18.bias_ref, bf16[416,1152]{1,0:T(8,128)(2,1)S(1)} %copy-done.2, bf16[416,1152]{1,0:T(8,128)(2,1)S(1)} %pass_on.4.next_ref, ...), custom_call_target="tpu_custom_call" | custom-call | flops 981467136 | bytes 3686400 | tf_op jit(solution)/shard_map/chunk/pallas_call | solution.py:98
  24.2 0.5 convolution_add_fusion.3.refs_4_
  24.7 3.2 %collective-permute-done.6.refs_3_.refs_2_ = bf16[32,1152]{1,0:T(8,128)(2,1)S(1)} collective-permute-done((bf16[32,1152]{1,0:T(8,128)(2,1)S(1)}, bf16[32,1152]{1,0:T(8,128)(2,1)S(1)}, u32[]{:S(2)}, u32[]{:S(2)}) %collective-permute-start.6) | collective-permute-done | bytes 73760 | tf_op jit(solution)/shard_map/ppermute | solution.py:162
  27.9 5.7 %collective-permute-done.4.refs_1_.refs_0_ = bf16[80,1152]{1,0:T(8,128)(2,1)S(1)} collective-permute-done((bf16[80,1152]{1,0:T(8,128)(2,1)S(1)}, bf16[80,1152]{1,0:T(8,128)(2,1)S(1)}, u32[]{:S(2)}, u32[]{:S(2)}) %collective-permute-start.4) | collective-permute-done | bytes 184352 | tf_op jit(solution)/shard_map/ppermute | solution.py:20
  33.6 5.1 %collective-permute-start.10 = (bf16[256,1152]{1,0:T(8,128)(2,1)S(1)}, bf16[256,1152]{1,0:T(8,128)(2,1)S(1)}, u32[]{:S(2)}, u32[]{:S(2)}) collective-permute-start(bf16[256,1152]{1,0:T(8,128)(2,1)S(1)} %pass_on.6.refs_4_), channel_id=1, source_target_pairs={{0,28},{4,0},{8,4},{12,8},{16,12},{20,16},{24,20},{28,24},{1,29},{... | collective-permute-start | bytes 1769480 | tf_op jit(solution)/shard_map/ppermute | solution.py:20
  38.6 1.3 %chunk.3 = (bf16[160,1152]{1,0:T(8,128)(2,1)S(1)}, bf16[160,1152]{1,0:T(8,128)(2,1)S(1)}, bf16[160,416]{1,0:T(8,128)(2,1)S(1)}, bf16[160,416]{1,0:T(8,128)(2,1)S(1)}) custom-call(f32[1]{0:T(128)} %copy.17.scale_ref, f32[1]{0:T(128)} %copy.18.bias_ref, bf16[416,1152]{1,0:T(8,128)(2,1)S(1)} %copy-done.2, bf16[416,1152]{1,0:T(8,128)(2,1)S(1)} %pass_on.4.next_ref, ...), custom_call_target="tpu_custom_call" | custom-call | flops 613416960 | bytes 3022848 | tf_op jit(solution)/shard_map/chunk/pallas_call | solution.py:98
  39.9 0.5 fusion.3.refs_1_
  40.5 3.0 %collective-permute-start.9 = (bf16[160,1152]{1,0:T(8,128)(2,1)S(1)}, bf16[160,1152]{1,0:T(8,128)(2,1)S(1)}, u32[]{:S(2)}, u32[]{:S(2)}) collective-permute-start(bf16[160,1152]{1,0:T(8,128)(2,1)S(1)} %pass_on.7), channel_id=1, source_target_pairs={{0,28},{4,0},{8,4},{12,8},{16,12},{20,16},{24,20},{28,24},{1,29},{... | collective-permute-start | bytes 1105928 | tf_op jit(solution)/shard_map/ppermute | solution.py:20
  43.5 0.5 convolution_add_fusion.4
  44.0 0.5 fusion.2.total_ref
  44.5 0.7 %fusion.total_ref = f32[416,1152]{1,0:T(8,128)S(1)} fusion(f32[416,1152]{1,0:T(8,128)S(1)} %fusion.16.refs_2_, bf16[416,416]{1,0:T(8,128)(2,1)S(1)} %fusion.14, bf16[416,1152]{1,0:T(8,128)(2,1)S(1)} %pass_on.4.next_ref, f32[]{:T(128)} %bitcast.25), kind=kOutput, calls=%fused_computation.1 | convolution fusion | flops 399679488 | bytes 5138436 | tf_op jit(solution)/shard_map/dot_general | solution.py:28
  45.2 7.2 %collective-permute-done.10.back_ref = bf16[256,1152]{1,0:T(8,128)(2,1)S(1)} collective-permute-done((bf16[256,1152]{1,0:T(8,128)(2,1)S(1)}, bf16[256,1152]{1,0:T(8,128)(2,1)S(1)}, u32[]{:S(2)}, u32[]{:S(2)}) %collective-permute-start.10) | collective-permute-done | bytes 589856 | tf_op jit(solution)/shard_map/ppermute | solution.py:20
  52.4 0.9 %add_rows.4.refs_0_ = bf16[416,1152]{1,0:T(8,128)(2,1)} custom-call(f32[416,1152]{1,0:T(8,128)S(1)} %fusion.total_ref, bf16[256,1152]{1,0:T(8,128)(2,1)S(1)} %collective-permute-done.10.back_ref), custom_call_target="tpu_custom_call" | custom-call | tf_op jit(solution)/shard_map/add_rows/pallas_call | solution.py:137
  53.7 1.0 %add_rows.3 = (bf16[416,1152]{1,0:T(8,128)(2,1)}, f32[8,128]{1,0:T(8,128)S(1)}) custom-call(f32[416,1152]{1,0:T(8,128)S(1)} %fusion.2.total_ref, bf16[416,1152]{1,0:T(8,128)(2,1)S(1)} %collective-permute-done.8.back_ref), custom_call_target="tpu_custom_call" | custom-call | tf_op jit(solution)/shard_map/add_rows/pallas_call | solution.py:137
  54.8 2.9 %collective-permute-done.9.back_ref = bf16[160,1152]{1,0:T(8,128)(2,1)S(1)} collective-permute-done((bf16[160,1152]{1,0:T(8,128)(2,1)S(1)}, bf16[160,1152]{1,0:T(8,128)(2,1)S(1)}, u32[]{:S(2)}, u32[]{:S(2)}) %collective-permute-start.9) | collective-permute-done | bytes 368672 | tf_op jit(solution)/shard_map/ppermute | solution.py:20
  57.7 0.8 %add_rows.5 = bf16[416,1152]{1,0:T(8,128)(2,1)} custom-call(f32[416,1152]{1,0:T(8,128)S(1)} %fusion.total_ref, bf16[160,1152]{1,0:T(8,128)(2,1)S(1)} %collective-permute-done.9.back_ref, bf16[416,1152]{1,0:T(8,128)(2,1)} %add_rows.4.refs_0_, f32[8,128]{1,0:T(8,128)S(1)} %get-tuple-element.21.refs_1_), custom_call_target="tpu_custom_call", output_to_operand_aliasing={{}: (2, {})} | custom-call | tf_op jit(solution)/shard_map/add_rows/pallas_call | solution.py:137
  (23 shorter events, 1.5 us)
Async XLA Ops:
  0.6 12.4 %copy-start.3 = (s32[1,416]{1,0:T(1,128)S(1)}, s32[1,416]{1,0:T(1,128)}, u32[]{:S(2)}) copy-start(s32[1,416]{1,0:T(1,128)} %array_ref.6) | copy-start | bytes 4996
  1.6 11.5 %collective-permute-start = (bf16[96,1152]{1,0:T(8,128)(2,1)S(1)}, bf16[96,1152]{1,0:T(8,128)(2,1)S(1)}, u32[]{:S(2)}, u32[]{:S(2)}) collective-permute-start(bf16[96,1152]{1,0:T(8,128)(2,1)S(1)} %slice.3.refs_0_), channel_id=1, source_target_pairs={{0,4},{4,8},{8,12},{12,16},{16,20},{20,24},{24,28},{28,0},{1,5},{5... | collective-permute-start | bytes 663560 | tf_op jit(solution)/shard_map/ppermute | solution.py:20
  4.6 1.2 %copy-start = (bf16[416,1152]{1,0:T(8,128)(2,1)S(1)}, bf16[416,1152]{1,0:T(8,128)(2,1)}, u32[]{:S(2)}) copy-start(bf16[416,1152]{1,0:T(8,128)(2,1)} %array_ref.9) | copy-start | bytes 2875396
  5.8 7.3 %copy-start.1 = (bf16[416,1152]{1,0:T(8,128)(2,1)S(1)}, bf16[416,1152]{1,0:T(8,128)(2,1)}, u32[]{:S(2)}) copy-start(bf16[416,1152]{1,0:T(8,128)(2,1)} %array_ref.9) | copy-start | bytes 2875396
  5.8 7.3 %copy-start.2 = (bf16[416,1152]{1,0:T(8,128)(2,1)S(1)}, bf16[416,1152]{1,0:T(8,128)(2,1)}, u32[]{:S(2)}) copy-start(bf16[416,1152]{1,0:T(8,128)(2,1)} %image_ref.3) | copy-start | bytes 2875396
  5.9 4.6 %collective-permute-start.1 = (bf16[32,1152]{1,0:T(8,128)(2,1)S(1)}, bf16[32,1152]{1,0:T(8,128)(2,1)S(1)}, u32[]{:S(2)}, u32[]{:S(2)}) collective-permute-start(bf16[32,1152]{1,0:T(8,128)(2,1)S(1)} %fetch.5.refs_0_), channel_id=1, source_target_pairs={{28,24},{29,25},{30,26},{31,27}} | collective-permute-start | bytes 221192 | tf_op jit(solution)/shard_map/ppermute | solution.py:157
  6.7 12.4 %collective-permute-start.2 = (bf16[416,1152]{1,0:T(8,128)(2,1)}, bf16[416,1152]{1,0:T(8,128)(2,1)S(1)}, u32[]{:S(2)}, u32[]{:S(2)}) collective-permute-start(bf16[416,1152]{1,0:T(8,128)(2,1)} %image_ref.3), channel_id=1, source_target_pairs={{0,3},{1,0},{2,1},{3,2},{4,7},{5,4},{6,5},{7,6},{8,11},{9,8},{10,9... | collective-permute-start | bytes 2875400 | tf_op jit(solution)/shard_map/ppermute | solution.py:20
  7.6 14.9 %collective-permute-start.3 = (bf16[160,1152]{1,0:T(8,128)(2,1)S(1)}, bf16[160,1152]{1,0:T(8,128)(2,1)S(1)}, u32[]{:S(2)}, u32[]{:S(2)}) collective-permute-start(bf16[160,1152]{1,0:T(8,128)(2,1)S(1)} %fetch.7), channel_id=1, source_target_pairs={{0,4},{4,8},{8,12},{12,16},{16,20},{20,24},{24,28},{28,0},{1,5},{5... | collective-permute-start | bytes 1105928 | tf_op jit(solution)/shard_map/ppermute | solution.py:20
  10.5 17.3 %collective-permute-start.6 = (bf16[32,1152]{1,0:T(8,128)(2,1)S(1)}, bf16[32,1152]{1,0:T(8,128)(2,1)S(1)}, u32[]{:S(2)}, u32[]{:S(2)}) collective-permute-start(bf16[32,1152]{1,0:T(8,128)(2,1)S(1)} %collective-permute-done.1.refs_1_), channel_id=1, source_target_pairs={{24,0},{25,1},{26,2},{27,3}} | collective-permute-start | bytes 221192 | tf_op jit(solution)/shard_map/ppermute | solution.py:162
  15.7 12.1 %collective-permute-start.5 = (bf16[32,1152]{1,0:T(8,128)(2,1)S(1)}, bf16[32,1152]{1,0:T(8,128)(2,1)S(1)}, u32[]{:S(2)}, u32[]{:S(2)}) collective-permute-start(bf16[32,1152]{1,0:T(8,128)(2,1)S(1)} %pass_on.5.refs_0_), channel_id=1, source_target_pairs={{0,4},{4,8},{8,12},{12,16},{16,20},{20,24},{24,28},{1,5},{5,9},{9,... | collective-permute-start | bytes 221192 | tf_op jit(solution)/shard_map/ppermute | solution.py:170
  17.4 16.2 %collective-permute-start.4 = (bf16[80,1152]{1,0:T(8,128)(2,1)S(1)}, bf16[80,1152]{1,0:T(8,128)(2,1)S(1)}, u32[]{:S(2)}, u32[]{:S(2)}) collective-permute-start(bf16[80,1152]{1,0:T(8,128)(2,1)S(1)} %fetch.8), channel_id=1, source_target_pairs={{0,4},{4,8},{8,12},{12,16},{16,20},{20,24},{24,28},{28,0},{1,5},{5... | collective-permute-start | bytes 552968 | tf_op jit(solution)/shard_map/ppermute | solution.py:20
  19.1 19.5 %collective-permute-start.7 = (bf16[48,1152]{1,0:T(8,128)(2,1)S(1)}, bf16[48,1152]{1,0:T(8,128)(2,1)S(1)}, u32[]{:S(2)}, u32[]{:S(2)}) collective-permute-start(bf16[48,1152]{1,0:T(8,128)(2,1)S(1)} %fetch.9), channel_id=1, source_target_pairs={{0,4},{4,8},{8,12},{12,16},{16,20},{20,24},{24,28},{28,0},{1,5},{5... | collective-permute-start | bytes 331784 | tf_op jit(solution)/shard_map/ppermute | solution.py:20
  33.6 18.8 %collective-permute-start.10 = (bf16[256,1152]{1,0:T(8,128)(2,1)S(1)}, bf16[256,1152]{1,0:T(8,128)(2,1)S(1)}, u32[]{:S(2)}, u32[]{:S(2)}) collective-permute-start(bf16[256,1152]{1,0:T(8,128)(2,1)S(1)} %pass_on.6.refs_4_), channel_id=1, source_target_pairs={{0,28},{4,0},{8,4},{12,8},{16,12},{20,16},{24,20},{28,24},{1,29},{... | collective-permute-start | bytes 1769480 | tf_op jit(solution)/shard_map/ppermute | solution.py:20
  40.4 13.3 %collective-permute-start.8 = (bf16[416,1152]{1,0:T(8,128)(2,1)S(1)}, bf16[416,1152]{1,0:T(8,128)(2,1)S(1)}, u32[]{:S(2)}, u32[]{:S(2)}) collective-permute-start(bf16[416,1152]{1,0:T(8,128)(2,1)S(1)} %fusion.3.refs_1_), channel_id=1, source_target_pairs={{0,1},{1,2},{2,3},{3,0},{4,5},{5,6},{6,7},{7,4},{8,9},{9,10},{10,1... | collective-permute-start | bytes 2875400 | tf_op jit(solution)/shard_map/ppermute | solution.py:20
  40.5 17.2 %collective-permute-start.9 = (bf16[160,1152]{1,0:T(8,128)(2,1)S(1)}, bf16[160,1152]{1,0:T(8,128)(2,1)S(1)}, u32[]{:S(2)}, u32[]{:S(2)}) collective-permute-start(bf16[160,1152]{1,0:T(8,128)(2,1)S(1)} %pass_on.7), channel_id=1, source_target_pairs={{0,28},{4,0},{8,4},{12,8},{16,12},{20,16},{24,20},{28,24},{1,29},{... | collective-permute-start | bytes 1105928 | tf_op jit(solution)/shard_map/ppermute | solution.py:20

commit v11 on v9

--- a/solution.py
+++ b/solution.py
@@ -8,7 +8,8 @@
 from jax.sharding import PartitionSpec as P
 
 MIB = 2**20
-APART = 32
+FIRST = 10
+WAIT = 10**10
 SMEM = pl.BlockSpec(memory_space=pltpu.SMEM)
 VMEM = pl.BlockSpec(memory_space=pltpu.VMEM)
 HBM = pl.BlockSpec(memory_space=pltpu.HBM)
@@ -32,10 +33,12 @@
     return jnp.dot(a, b, preferred_element_type=jnp.float32)
 
 
-def row_cuts(rows):
-    tiles = rows // 16
-    cuts = [0] + [tiles * ends // 26 * 16 for ends in (6, 16, 23)] + [rows]
-    return list(zip(cuts[:-1], cuts[1:]))
+def shifted_half(shard, by, parity):
+    blocks, groups = lax.axis_size("blk"), lax.axis_size("grp")
+    pairs = [
+        (b * groups + g, (b + by) % blocks * groups + g) for b in range(blocks) for g in range(parity, groups, 2)
+    ]
+    return lax.ppermute(shard, ("blk", "grp"), pairs)
 
 
 def fetch(array, lo, hi, after):
@@ -56,7 +59,7 @@
     )(array, *after)
 
 
-def pass_on(array, after):
+def pass_on(array, after, flops=0):
     return pl.pallas_call(
         lambda *refs: None,
         out_shape=jax.ShapeDtypeStruct(array.shape, array.dtype),
@@ -64,17 +67,17 @@
         out_specs=ANY,
         input_output_aliases={0: 0},
         compiler_params=pltpu.CompilerParams(vmem_limit_bytes=MIB),
+        cost_estimate=pl.CostEstimate(flops=flops, bytes_accessed=0, transcendentals=0),
         name="pass_on",
     )(array, *after)
 
 
-def chunk_kernel(apart, scale_ref, bias_ref, image_ref, next_ref, upper_ref, lower_ref, *refs):
-    joined_ref, own_ref, other_ref, *sent_refs = refs[-4 - bool(apart) :]
+def chunk_kernel(lo, scale_ref, bias_ref, image_ref, next_ref, even_ref, odd_ref, *refs):
+    sent_ref, part_ref, own_ref, other_ref = refs[-4:]
     scale, bias = scale_ref[0], bias_ref[0]
-    rows = upper_ref.shape[0]
-    joined_ref[:rows, :] = upper_ref[...]
-    joined_ref[rows:, :] = lower_ref[...]
-    part = joined_ref[...]
+    rows = pl.ds(lo, part_ref.shape[0])
+    part = even_ref[rows, :] + odd_ref[rows, :]
+    part_ref[...] = part
     image = image_ref[...]
     own = jax.nn.sigmoid(dot_nt(part, image) * scale + bias).astype(jnp.bfloat16)
     own_ref[...] = own
@@ -83,32 +86,26 @@
     other = jax.nn.sigmoid(dot_nt(part, image) * scale + bias).astype(jnp.bfloat16)
     other_ref[...] = other
     total += dot_nn(other, image)
-    total = (scale * total).astype(jnp.bfloat16)
-    start = 0
-    for sent_ref in sent_refs:
-        sent_ref[...] = total[start : start + sent_ref.shape[0], :]
-        start += sent_ref.shape[0]
-
-
-def chunk(factor, shift, image, image_next, upper, lower, after, apart=0):
-    rows, width = upper.shape[0] + lower.shape[0], upper.shape[1]
-    columns = image.shape[0]
+    sent_ref[...] = (scale * total).astype(jnp.bfloat16)
+
+
+def chunk(factor, shift, image, image_next, texts, lo, hi, after):
+    rows, (columns, width) = hi - lo, image.shape
+    text = jax.ShapeDtypeStruct((rows, width), jnp.bfloat16)
     tile = jax.ShapeDtypeStruct((rows, columns), jnp.bfloat16)
-    shapes = [jax.ShapeDtypeStruct((rows, width), jnp.bfloat16), tile, tile]
-    shapes += [jax.ShapeDtypeStruct((r, width), jnp.bfloat16) for r in (rows - apart, apart) if r]
-    return pl.pallas_call(
-        functools.partial(chunk_kernel, apart),
-        out_shape=shapes,
+    return pl.pallas_call(
+        functools.partial(chunk_kernel, lo),
+        out_shape=(text, text, tile, tile),
         in_specs=[SMEM] * 2 + [VMEM] * 4 + [ANY] * len(after),
-        out_specs=[VMEM] * len(shapes),
+        out_specs=(VMEM,) * 4,
         compiler_params=pltpu.CompilerParams(vmem_limit_bytes=16 * MIB),
         cost_estimate=pl.CostEstimate(
             flops=8 * rows * columns * width,
-            bytes_accessed=2 * (2 * columns + 3 * rows) * width,
+            bytes_accessed=2 * (2 * columns + 4 * rows) * width,
             transcendentals=2 * rows * columns,
         ),
         name="chunk",
-    )(factor, shift, image, image_next, upper, lower, *after)
+    )(factor, shift, image, image_next, *texts, *after)
 
 
 def add_rows(total, pieces, result, after, mark=False):
@@ -162,45 +159,38 @@
 def body(image, text, target, factor, shift):
     scale = factor[0]
     bias = shift[0]
-    cuts = row_cuts(text.shape[0])
-    first = text[: cuts[0][1]]
-    part = [shifted(first, "blk", 1)]
+    count = text.shape[0]
+    cut = count // 16 * FIRST // 26 * 16
+    even = shifted_half(text, 1, 0)
     image_next = shifted(image, "grp", -1)
-    part.append(shifted(fetch(text, *cuts[1], [first]), "blk", 1))
-
-    target = fetch(target, 0, 1, [part[0]])
-    part.append(shifted(fetch(text, *cuts[2], [target]), "blk", 1))
+
     own = jax.nn.sigmoid(dot_nt(image, text) * scale + bias)
     column = lax.broadcasted_iota(jnp.int32, own.shape, 1)
     own = (own - (column == target[0][:, None]).astype(jnp.float32)).astype(jnp.bfloat16)
-    part.append(shifted(fetch(text, *cuts[3], [own]), "blk", 1))
+    odd = shifted_half(fetch(text, 0, count, [own]), 1, 1)
     image_grad = dot_nn(own, text)
     text_grad = dot_tn(own, image)
 
-    image_next = pass_on(image_next, [image_grad, text_grad])
-    part0, own0, next0, sent0, apart = chunk(factor, shift, image, image_next, part[0], part[1], [], apart=APART)
+    even = pass_on(even, [image_grad, text_grad], WAIT)
+    image_next = pass_on(image_next, [even])
+    odd = pass_on(odd, [image_next])
+    sent0, part0, own0, next0 = chunk(factor, shift, image, image_next, [even, odd], 0, cut, [])
+    back0 = shifted(sent0, "blk", -1)
+
+    image_next = pass_on(image_next, [sent0])
+    sent1, part1, own1, next1 = chunk(factor, shift, image, image_next, [even, odd], cut, count, [])
     next_own = jax.nn.sigmoid(dot_nt(image_next, text) * scale + bias).astype(jnp.bfloat16)
     text_grad = scale * (text_grad + dot_tn(next_own, image_next))
     image_sent = dot_nn(next_own, text) + dot_tn(next0, part0)
-    image_grad = image_grad + dot_tn(own0, part0)
-
-    devices = lax.axis_size("blk")
-    sent0, apart = pass_on(sent0, [part[2], image_sent]), pass_on(apart, [part[2], image_sent])
-    back0 = shifted(sent0, "blk", -1)
-    half_way = lax.ppermute(apart, "blk", [(1, 2)])
-    near = lax.ppermute(apart, "blk", [(i, (i - 1) % devices) for i in range(devices) if i != 1])
-
-    part1, own1, next1, sent1 = chunk(factor, shift, image, image_next, part[2], part[3], [sent0, half_way])
     image_sent = (scale * (image_sent + dot_tn(next1, part1))).astype(jnp.bfloat16)
     image_back = shifted(image_sent, "grp", 1)
-    sent1 = pass_on(sent1, [image_sent])
     back1 = shifted(sent1, "blk", -1)
-    far = lax.ppermute(half_way, "blk", [(2, 0)])
+    result, mark = add_rows(text_grad, [(0, [back0])], None, [], mark=True)
+    own0, own1 = pass_on(own0, [mark]), pass_on(own1, [mark])
+    image_grad = image_grad + dot_tn(own0, part0)
     image_grad = scale * (image_grad + dot_tn(own1, part1))
-
-    result = add_rows(text_grad, [(0, [back0]), (cuts[2][0] - APART, [near, far])], None, [])
     image_grad, mark = add_rows(image_grad, [(0, [image_back])], None, [], mark=True)
-    result = add_rows(text_grad, [(cuts[2][0], [back1])], result, [mark])
+    result = add_rows(text_grad, [(cut, [back1])], result, [mark])
     return image_grad, result
 
 

time: 57.2 us -> 54.4 us (0.951)
  waiting for transfers between devices: 25.1 us -> 21.7 us
  local copies, waits for them, and re-layouts: 2.16 us -> 0.01 us
  matrix products: 6.58 us -> 8.18 us
  starting transfers between devices: 14.7 us -> 16.2 us
    ppermute x3 -> x2, waiting for transfers between devices: 15.5 us -> 11.6 us  [shifted_half(): return lax.ppermute(shard, ('blk', 'grp'), pairs)]
    ppermute x8 -> x4, starting transfers between devices: 8.79 us -> 10.5 us  [shifted(): lax.ppermute(shard, axis, [(i, (i + by) % devices) for i in range(devices)])]
    dot_general x2, matrix products: 1.72 us -> 3.29 us  [dot_nt(): lax.dot_general(a, b, (((1,), (1,)), ((), ())), preferred_element_type=jn...]
    unnamed x8 -> x4, local copies, waits for them, and re-layouts: 1.2 us -> 0.01 us
    slice x1 -> x0, local copies, waits for them, and re-layouts: 0.96 us -> none  [body(): first = text[:cuts[0][1]]]
    ppermute x8 -> x4, waiting for transfers between devices: 9.61 us -> 10.1 us  [shifted(): lax.ppermute(shard, axis, [(i, (i + by) % devices) for i in range(devices)])]
    ppermute x3 -> x2, starting transfers between devices: 5.91 us -> 5.7 us  [shifted_half(): return lax.ppermute(shard, ('blk', 'grp'), pairs)]
  transfers between devices with their start and end apart: 11 -> 6, of which waited for: 4 -> 3; matrix products, arithmetic and copies ran while one was open for 12% -> 15% of each run, Pallas kernels for 10% -> 7%
where the time goes in v11:
time: 54.4 us; the launch traced here: 54.2 us
  waiting for transfers between devices  21.7 us (40%)
  starting transfers between devices  16.2 us (30%)
  matrix products  8.18 us (15%)
  Pallas kernels  5.91 us (11%)
  between operations  2.12 us (4%)
    ppermute x2, waiting for transfers between devices, shifted_half(): return lax.ppermute(shard, ('blk', 'grp'), pairs)  11.6 us
    ppermute x4, starting transfers between devices, shifted(): lax.ppermute(shard, axis, [(i, (i + by) % devices) for i in range(devices)])  10.5 us
    ppermute x4, waiting for transfers between devices, shifted(): lax.ppermute(shard, axis, [(i, (i + by) % devices) for i in range(devices)])  10.1 us
    ppermute x2, starting transfers between devices, shifted_half(): return lax.ppermute(shard, ('blk', 'grp'), pairs)  5.7 us
    dot_general x6, matrix products, dot_tn(): lax.dot_general(a, b, (((0,), (0,)), ((), ())), preferred_element_type=jn...  3.49 us
    dot_general x2, matrix products, dot_nt(): lax.dot_general(a, b, (((1,), (1,)), ((), ())), preferred_element_type=jn...  3.29 us
    pallas_call x2, Pallas kernels, chunk(): pl.pallas_call(functools.partial(chunk_kernel, lo), out_shape=(text, text...  2.91 us
    pallas_call x3, Pallas kernels, add_rows(): pl.pallas_call(kernel, out_shape=(out, jax.ShapeDtypeStruct((8, 128), jnp...  2.7 us
  transfers between devices with their start and end apart: 6, of which 3 were waited for; matrix products, arithmetic and copies ran while one was open for 15% of the time, Pallas kernels for 7%

profile of v11, /device:TPU:0, one launch (start us, length us, event | category | flops | bytes accessed | tf_op | source)
XLA Modules:
  0.0 54.2 jit_solution(12563289420662193964)
XLA Ops:
  0.6 4.8 %collective-permute-start.1 = (bf16[416,1152]{1,0:T(8,128)(2,1)}, bf16[416,1152]{1,0:T(8,128)(2,1)S(1)}, u32[]{:S(2)}, u32[]{:S(2)}) collective-permute-start(bf16[416,1152]{1,0:T(8,128)(2,1)} %array_ref.1), channel_id=1, source_target_pairs={{0,4},{2,6},{4,8},{6,10},{8,12},{10,14},{12,16},{14,18},{16,20},{1... | collective-permute-start | bytes 2875400 | tf_op jit(solution)/shard_map/ppermute | solution.py:41
  5.5 0.1 collective-permute-start
  6.8 0.0 copy-start.1
  6.9 2.4 %fusion.18.refs_0_ = bf16[416,416]{1,0:T(8,128)(2,1)S(1)} fusion(bf16[416,1152]{1,0:T(8,128)(2,1)} %image_ref.3, bf16[416,1152]{1,0:T(8,128)(2,1)} %array_ref.1, s32[416]{0:T(512)} %bitcast.30, f32[]{:T(128)} %bitcast.28, f32[]{:T(128)} %bitcast.24), kind=kOutput, calls=%fused_computation.23 | convolution fusion | flops 400278528 | bytes 2264712 | tf_op jit(solution)/shard_map/dot_general | solution.py:25
  9.3 0.0 copy-done.1
  9.3 0.3 fetch.1
  9.6 0.0 copy-start
  9.6 0.9 %collective-permute-start.2 = (bf16[416,1152]{1,0:T(8,128)(2,1)S(1)}, bf16[416,1152]{1,0:T(8,128)(2,1)S(1)}, u32[]{:S(2)}, u32[]{:S(2)}) collective-permute-start(bf16[416,1152]{1,0:T(8,128)(2,1)S(1)} %fetch.1), channel_id=1, source_target_pairs={{1,5},{3,7},{5,9},{7,11},{9,13},{11,15},{13,17},{15,19},{17,21},{1... | collective-permute-start | bytes 2875400 | tf_op jit(solution)/shard_map/ppermute | solution.py:41
  10.5 0.7 %fusion.19.refs_1_ = f32[416,1152]{1,0:T(8,128)S(1)} fusion(bf16[416,416]{1,0:T(8,128)(2,1)S(1)} %fusion.18.refs_0_, bf16[416,1152]{1,0:T(8,128)(2,1)S(1)} %copy-done.1), kind=kOutput, calls=%fused_computation.25 | convolution fusion | flops 398721024 | bytes 3221504 | tf_op jit(solution)/shard_map/dot_general | solution.py:33
  11.2 0.0 copy-done
  11.2 0.7 %fusion.20.refs_2_ = f32[416,1152]{1,0:T(8,128)S(1)} fusion(bf16[416,416]{1,0:T(8,128)(2,1)S(1)} %fusion.18.refs_0_, bf16[416,1152]{1,0:T(8,128)(2,1)S(1)} %copy-done), kind=kOutput, calls=%fused_computation.26 | convolution fusion | flops 398721024 | bytes 3221504 | tf_op jit(solution)/shard_map/dot_general | solution.py:29
  11.9 11.6 %collective-permute-done.1.refs_0_ = bf16[416,1152]{1,0:T(8,128)(2,1)S(1)} collective-permute-done((bf16[416,1152]{1,0:T(8,128)(2,1)}, bf16[416,1152]{1,0:T(8,128)(2,1)S(1)}, u32[]{:S(2)}, u32[]{:S(2)}) %collective-permute-start.1) | collective-permute-done | bytes 958496 | tf_op jit(solution)/shard_map/ppermute | solution.py:41
  23.6 0.0 collective-permute-done.refs_0_
  23.6 0.0 collective-permute-done.2.refs_0_
  23.6 1.3 %chunk.2 = (bf16[160,1152]{1,0:T(8,128)(2,1)S(1)}, bf16[160,1152]{1,0:T(8,128)(2,1)S(1)}, bf16[160,416]{1,0:T(8,128)(2,1)S(1)}, bf16[160,416]{1,0:T(8,128)(2,1)S(1)}) custom-call(f32[1]{0:T(128)} %copy.21.scale_ref, f32[1]{0:T(128)} %copy.22.bias_ref, bf16[416,1152]{1,0:T(8,128)(2,1)S(1)} %copy-done, bf16[416,1152]{1,0:T(8,128)(2,1)S(1)} %pass_on.7.refs_1_.next_ref.refs_0_, ...), custom_call_target="tpu_custom_call" | custom-call | flops 613416960 | bytes 3391488 | tf_op jit(solution)/shard_map/chunk/pallas_call | solution.py:96
  24.9 3.5 %collective-permute-start.3 = (bf16[160,1152]{1,0:T(8,128)(2,1)S(1)}, bf16[160,1152]{1,0:T(8,128)(2,1)S(1)}, u32[]{:S(2)}, u32[]{:S(2)}) collective-permute-start(bf16[160,1152]{1,0:T(8,128)(2,1)S(1)} %get-tuple-element.15.refs_1_), channel_id=1, source_target_pairs={{0,28},{4,0},{8,4},{12,8},{16,12},{20,16},{24,20},{28,24},{1,29},{... | collective-permute-start | bytes 1105928 | tf_op jit(solution)/shard_map/ppermute | solution.py:21
  28.3 1.6 %chunk.3 = (bf16[256,1152]{1,0:T(8,128)(2,1)S(1)}, bf16[256,1152]{1,0:T(8,128)(2,1)S(1)}, bf16[256,416]{1,0:T(8,128)(2,1)S(1)}, bf16[256,416]{1,0:T(8,128)(2,1)S(1)}) custom-call(f32[1]{0:T(128)} %copy.21.scale_ref, f32[1]{0:T(128)} %copy.22.bias_ref, bf16[416,1152]{1,0:T(8,128)(2,1)S(1)} %copy-done, bf16[416,1152]{1,0:T(8,128)(2,1)S(1)} %pass_on.9.next_ref, ...), custom_call_target="tpu_custom_call" | custom-call | flops 981467136 | bytes 4276224 | tf_op jit(solution)/shard_map/chunk/pallas_call | solution.py:96
  30.0 0.8 %fusion.17 = bf16[416,416]{1,0:T(8,128)(2,1)S(1)} fusion(bf16[416,1152]{1,0:T(8,128)(2,1)S(1)} %pass_on.9.next_ref, bf16[416,1152]{1,0:T(8,128)(2,1)S(1)} %copy-done.1, f32[]{:T(128)} %bitcast.29, f32[]{:T(128)} %bitcast.27), kind=kOutput, calls=%fused_computation.22 | convolution fusion | flops 399759360 | bytes 2263048 | tf_op jit(solution)/shard_map/dot_general | solution.py:25
  30.8 0.7 %fusion.22 = f32[416,1152]{1,0:T(8,128)S(1)} fusion(bf16[416,416]{1,0:T(8,128)(2,1)S(1)} %fusion.17, bf16[416,1152]{1,0:T(8,128)(2,1)S(1)} %copy-done.1), kind=kOutput, calls=%fused_computation.28 | convolution fusion | flops 398721024 | bytes 3221504 | tf_op jit(solution)/shard_map/dot_general | solution.py:33
  31.5 0.5 fusion.23
  32.0 0.5 fusion.5
  32.6 5.4 %collective-permute-start.4 = (bf16[416,1152]{1,0:T(8,128)(2,1)S(1)}, bf16[416,1152]{1,0:T(8,128)(2,1)S(1)}, u32[]{:S(2)}, u32[]{:S(2)}) collective-permute-start(bf16[416,1152]{1,0:T(8,128)(2,1)S(1)} %fusion.5), channel_id=1, source_target_pairs={{0,1},{1,2},{2,3},{3,0},{4,5},{5,6},{6,7},{7,4},{8,9},{9,10},{10,1... | collective-permute-start | bytes 2875400 | tf_op jit(solution)/shard_map/ppermute | solution.py:21
  38.0 1.5 %collective-permute-start.5 = (bf16[256,1152]{1,0:T(8,128)(2,1)S(1)}, bf16[256,1152]{1,0:T(8,128)(2,1)S(1)}, u32[]{:S(2)}, u32[]{:S(2)}) collective-permute-start(bf16[256,1152]{1,0:T(8,128)(2,1)S(1)} %get-tuple-element.23), channel_id=1, source_target_pairs={{0,28},{4,0},{8,4},{12,8},{16,12},{20,16},{24,20},{28,24},{1,29},{... | collective-permute-start | bytes 1769480 | tf_op jit(solution)/shard_map/ppermute | solution.py:21
  39.5 0.8 %fusion.total_ref = f32[416,1152]{1,0:T(8,128)S(1)} fusion(f32[416,1152]{1,0:T(8,128)S(1)} %fusion.20.refs_2_, bf16[416,416]{1,0:T(8,128)(2,1)S(1)} %fusion.17, bf16[416,1152]{1,0:T(8,128)(2,1)S(1)} %pass_on.9.next_ref, f32[]{:T(128)} %bitcast.23), kind=kOutput, calls=%fused_computation.1 | convolution fusion | flops 399679488 | bytes 5138436 | tf_op jit(solution)/shard_map/dot_general | solution.py:29
  40.3 0.0 collective-permute-done.3.refs_0_
  40.3 0.8 %add_rows.3 = (bf16[416,1152]{1,0:T(8,128)(2,1)}, f32[8,128]{1,0:T(8,128)S(1)}) custom-call(f32[416,1152]{1,0:T(8,128)S(1)} %fusion.total_ref, bf16[160,1152]{1,0:T(8,128)(2,1)S(1)} %collective-permute-done.3.refs_0_), custom_call_target="tpu_custom_call" | custom-call | tf_op jit(solution)/shard_map/add_rows/pallas_call | solution.py:147
  41.1 0.5 fusion.21
  41.6 0.5 fusion.4.total_ref
  42.1 8.5 %collective-permute-done.4.refs_0_ = bf16[416,1152]{1,0:T(8,128)(2,1)S(1)} collective-permute-done((bf16[416,1152]{1,0:T(8,128)(2,1)S(1)}, bf16[416,1152]{1,0:T(8,128)(2,1)S(1)}, u32[]{:S(2)}, u32[]{:S(2)}) %collective-permute-start.4) | collective-permute-done | bytes 958496 | tf_op jit(solution)/shard_map/ppermute | solution.py:21
  50.6 1.0 %add_rows.4 = (bf16[416,1152]{1,0:T(8,128)(2,1)}, f32[8,128]{1,0:T(8,128)S(1)}) custom-call(f32[416,1152]{1,0:T(8,128)S(1)} %fusion.4.total_ref, bf16[416,1152]{1,0:T(8,128)(2,1)S(1)} %collective-permute-done.4.refs_0_), custom_call_target="tpu_custom_call" | custom-call | tf_op jit(solution)/shard_map/add_rows/pallas_call | solution.py:147
  51.7 1.6 %collective-permute-done.5.refs_0_ = bf16[256,1152]{1,0:T(8,128)(2,1)S(1)} collective-permute-done((bf16[256,1152]{1,0:T(8,128)(2,1)S(1)}, bf16[256,1152]{1,0:T(8,128)(2,1)S(1)}, u32[]{:S(2)}, u32[]{:S(2)}) %collective-permute-start.5) | collective-permute-done | bytes 589856 | tf_op jit(solution)/shard_map/ppermute | solution.py:21
  53.3 0.9 %add_rows.5 = bf16[416,1152]{1,0:T(8,128)(2,1)} custom-call(f32[416,1152]{1,0:T(8,128)S(1)} %fusion.total_ref, bf16[256,1152]{1,0:T(8,128)(2,1)S(1)} %collective-permute-done.5.refs_0_, bf16[416,1152]{1,0:T(8,128)(2,1)} %get-tuple-element.24.refs_1_, f32[8,128]{1,0:T(8,128)S(1)} %get-tuple-element.25.refs_2_), custom_call_target="tpu_custom_call", output_to_operand_aliasing={{}: (2, {})} | custom-call | tf_op jit(solution)/shard_map/add_rows/pallas_call | solution.py:147
  (6 shorter events, 0.0 us)
Async XLA Ops:
  0.6 22.9 %collective-permute-start.1 = (bf16[416,1152]{1,0:T(8,128)(2,1)}, bf16[416,1152]{1,0:T(8,128)(2,1)S(1)}, u32[]{:S(2)}, u32[]{:S(2)}) collective-permute-start(bf16[416,1152]{1,0:T(8,128)(2,1)} %array_ref.1), channel_id=1, source_target_pairs={{0,4},{2,6},{4,8},{6,10},{8,12},{10,14},{12,16},{14,18},{16,20},{1... | collective-permute-start | bytes 2875400 | tf_op jit(solution)/shard_map/ppermute | solution.py:41
  5.5 18.1 %collective-permute-start = (bf16[416,1152]{1,0:T(8,128)(2,1)}, bf16[416,1152]{1,0:T(8,128)(2,1)S(1)}, u32[]{:S(2)}, u32[]{:S(2)}) collective-permute-start(bf16[416,1152]{1,0:T(8,128)(2,1)} %image_ref.3), channel_id=1, source_target_pairs={{0,3},{1,0},{2,1},{3,2},{4,7},{5,4},{6,5},{7,6},{8,11},{9,8},{10,9... | collective-permute-start | bytes 2875400 | tf_op jit(solution)/shard_map/ppermute | solution.py:21
  6.8 2.5 %copy-start.1 = (bf16[416,1152]{1,0:T(8,128)(2,1)S(1)}, bf16[416,1152]{1,0:T(8,128)(2,1)}, u32[]{:S(2)}) copy-start(bf16[416,1152]{1,0:T(8,128)(2,1)} %array_ref.1) | copy-start | bytes 2875396
  9.6 1.6 %copy-start = (bf16[416,1152]{1,0:T(8,128)(2,1)S(1)}, bf16[416,1152]{1,0:T(8,128)(2,1)}, u32[]{:S(2)}) copy-start(bf16[416,1152]{1,0:T(8,128)(2,1)} %image_ref.3) | copy-start | bytes 2875396
  9.6 13.9 %collective-permute-start.2 = (bf16[416,1152]{1,0:T(8,128)(2,1)S(1)}, bf16[416,1152]{1,0:T(8,128)(2,1)S(1)}, u32[]{:S(2)}, u32[]{:S(2)}) collective-permute-start(bf16[416,1152]{1,0:T(8,128)(2,1)S(1)} %fetch.1), channel_id=1, source_target_pairs={{1,5},{3,7},{5,9},{7,11},{9,13},{11,15},{13,17},{15,19},{17,21},{1... | collective-permute-start | bytes 2875400 | tf_op jit(solution)/shard_map/ppermute | solution.py:41
  24.9 15.4 %collective-permute-start.3 = (bf16[160,1152]{1,0:T(8,128)(2,1)S(1)}, bf16[160,1152]{1,0:T(8,128)(2,1)S(1)}, u32[]{:S(2)}, u32[]{:S(2)}) collective-permute-start(bf16[160,1152]{1,0:T(8,128)(2,1)S(1)} %get-tuple-element.15.refs_1_), channel_id=1, source_target_pairs={{0,28},{4,0},{8,4},{12,8},{16,12},{20,16},{24,20},{28,24},{1,29},{... | collective-permute-start | bytes 1105928 | tf_op jit(solution)/shard_map/ppermute | solution.py:21
  32.6 18.1 %collective-permute-start.4 = (bf16[416,1152]{1,0:T(8,128)(2,1)S(1)}, bf16[416,1152]{1,0:T(8,128)(2,1)S(1)}, u32[]{:S(2)}, u32[]{:S(2)}) collective-permute-start(bf16[416,1152]{1,0:T(8,128)(2,1)S(1)} %fusion.5), channel_id=1, source_target_pairs={{0,1},{1,2},{2,3},{3,0},{4,5},{5,6},{6,7},{7,4},{8,9},{9,10},{10,1... | collective-permute-start | bytes 2875400 | tf_op jit(solution)/shard_map/ppermute | solution.py:21
  38.0 15.3 %collective-permute-start.5 = (bf16[256,1152]{1,0:T(8,128)(2,1)S(1)}, bf16[256,1152]{1,0:T(8,128)(2,1)S(1)}, u32[]{:S(2)}, u32[]{:S(2)}) collective-permute-start(bf16[256,1152]{1,0:T(8,128)(2,1)S(1)} %get-tuple-element.23), channel_id=1, source_target_pairs={{0,28},{4,0},{8,4},{12,8},{16,12},{20,16},{24,20},{28,24},{1,29},{... | collective-permute-start | bytes 1769480 | tf_op jit(solution)/shard_map/ppermute | solution.py:21

commit v12 on v5

--- a/solution.py
+++ b/solution.py
@@ -142,42 +142,40 @@
 def body(image, text, target, factor, shift):
     scale = factor[0]
     bias = shift[0]
-    cuts = row_cuts(text.shape[0])
-    first = text[: cuts[0][1]]
-    part = [shifted(first, "blk", 1)]
-    image_next = shifted(image, "grp", -1)
-    part.append(shifted(fetch(text, *cuts[1], [first]), "blk", 1))
+    cuts = row_cuts(image.shape[0])
+    first = image[: cuts[0][1]]
+    part = [shifted(first, "blk", -1)]
+    text_prev = shifted(text, "grp", 1)
+    part.append(shifted(fetch(image, *cuts[1], [first]), "blk", -1))
 
     target = fetch(target, 0, 1, [part[0]])
-    part.append(shifted(fetch(text, *cuts[2], [target]), "blk", 1))
+    part.append(shifted(fetch(image, *cuts[2], [target]), "blk", -1))
     own = jax.nn.sigmoid(dot_nt(image, text) * scale + bias)
     column = lax.broadcasted_iota(jnp.int32, own.shape, 1)
     own = (own - (column == target[0][:, None]).astype(jnp.float32)).astype(jnp.bfloat16)
-    part.append(shifted(fetch(text, *cuts[3], [own]), "blk", 1))
+    part.append(shifted(fetch(image, *cuts[3], [own]), "blk", -1))
     image_grad = dot_nn(own, text)
     text_grad = dot_tn(own, image)
 
-    image_next = pass_on(image_next, [image_grad, text_grad])
-    sent0, part0, own0, next0 = chunk(factor, shift, image, image_next, part[0], part[1], [])
-    next_own = jax.nn.sigmoid(dot_nt(image_next, text) * scale + bias).astype(jnp.bfloat16)
-    text_grad = scale * (text_grad + dot_tn(next_own, image_next))
-    image_sent = dot_nn(next_own, text) + dot_tn(next0, part0)
-    image_grad = image_grad + dot_tn(own0, part0)
+    text_prev = pass_on(text_prev, [image_grad, text_grad])
+    sent0, part0, own0, prev0 = chunk(factor, shift, text, text_prev, part[0], part[1], [])
+    back0 = shifted(sent0, "blk", 1)
+    prev_own = jax.nn.sigmoid(dot_nt(text_prev, image) * scale + bias).astype(jnp.bfloat16)
+    image_grad = scale * (image_grad + dot_tn(prev_own, text_prev))
+    text_sent = dot_nn(prev_own, image) + dot_tn(prev0, part0)
+    text_grad = text_grad + dot_tn(own0, part0)
 
-    sent0 = pass_on(sent0, [part[2], image_sent])
-    back0 = shifted(sent0, "blk", -1)
+    sent1, part1, own1, prev1 = chunk(factor, shift, text, text_prev, part[2], part[3], [text_sent])
+    text_sent = (scale * (text_sent + dot_tn(prev1, part1))).astype(jnp.bfloat16)
+    text_back = shifted(text_sent, "grp", -1)
+    sent1 = pass_on(sent1, [text_sent])
+    back1 = shifted(sent1, "blk", 1)
+    text_grad = scale * (text_grad + dot_tn(own1, part1))
 
-    sent1, part1, own1, next1 = chunk(factor, shift, image, image_next, part[2], part[3], [sent0])
-    image_sent = (scale * (image_sent + dot_tn(next1, part1))).astype(jnp.bfloat16)
-    image_back = shifted(image_sent, "grp", 1)
-    sent1 = pass_on(sent1, [image_sent])
-    back1 = shifted(sent1, "blk", -1)
-    image_grad = scale * (image_grad + dot_tn(own1, part1))
-
-    result = add_rows(text_grad, back0, 0, None, [])
-    image_grad, mark = add_rows(image_grad, image_back, 0, None, [], mark=True)
-    result = add_rows(text_grad, back1, cuts[2][0], result, [mark])
-    return image_grad, result
+    result = add_rows(image_grad, back0, 0, None, [])
+    text_grad, mark = add_rows(text_grad, text_back, 0, None, [], mark=True)
+    result = add_rows(image_grad, back1, cuts[2][0], result, [mark])
+    return result, text_grad
 
 
 def solution(mesh):

time: 50.4 us -> 58 us (1.15)
  starting transfers between devices: 10.4 us -> 14 us
  waiting for transfers between devices: 22.6 us -> 24.6 us
  matrix products: 6.58 us -> 8.14 us
    ppermute x8, starting transfers between devices: 10.4 us -> 14 us  [shifted(): lax.ppermute(shard, axis, [(i, (i + by) % devices) for i in range(devices)])]
    ppermute x8, waiting for transfers between devices: 22.6 us -> 24.6 us  [shifted(): lax.ppermute(shard, axis, [(i, (i + by) % devices) for i in range(devices)])]
    dot_general x2, matrix products: 1.72 us -> 3.28 us  [dot_nt(): lax.dot_general(a, b, (((1,), (1,)), ((), ())), preferred_element_type=jn...]
  transfers between devices with their start and end apart: 8 -> 8, of which waited for: 5 -> 4; matrix products, arithmetic and copies ran while one was open for 13% -> 14% of each run, Pallas kernels for 11% -> 10%
where the time goes in v12:
time: 58 us; the launch traced here: 57.4 us
  waiting for transfers between devices  24.6 us (42%)
  starting transfers between devices  14 us (24%)
  matrix products  8.14 us (14%)
  Pallas kernels  6.27 us (11%)
  local copies, waits for them, and re-layouts  2.17 us (4%)
  between operations  2.15 us (4%)
    ppermute x8, waiting for transfers between devices, shifted(): lax.ppermute(shard, axis, [(i, (i + by) % devices) for i in range(devices)])  24.6 us
    ppermute x8, starting transfers between devices, shifted(): lax.ppermute(shard, axis, [(i, (i + by) % devices) for i in range(devices)])  14 us
    dot_general x6, matrix products, dot_tn(): lax.dot_general(a, b, (((0,), (0,)), ((), ())), preferred_element_type=jn...  3.46 us
    dot_general x2, matrix products, dot_nt(): lax.dot_general(a, b, (((1,), (1,)), ((), ())), preferred_element_type=jn...  3.28 us
    pallas_call x2, Pallas kernels, chunk(): pl.pallas_call(chunk_kernel, out_shape=(text, text, tile, tile), in_specs...  2.92 us
    pallas_call x3, Pallas kernels, add_rows(): pl.pallas_call(kernel, out_shape=(out, jax.ShapeDtypeStruct((8, 128), jnp...  2.67 us
    dot_general x2, matrix products, dot_nn(): return jnp.dot(a, b, preferred_element_type=jnp.float32)  1.4 us
    unnamed x8, local copies, waits for them, and re-layouts  1.21 us
  transfers between devices with their start and end apart: 8, of which 4 were waited for; matrix products, arithmetic and copies ran while one was open for 14% of the time, Pallas kernels for 10%

profile of v12, /device:TPU:0, one launch (start us, length us, event | category | flops | bytes accessed | tf_op | source)
XLA Modules:
  0.0 57.4 jit_solution(15587135296069356834)
XLA Ops:
  0.6 1.0 %slice.3.refs_0_ = bf16[96,1152]{1,0:T(8,128)(2,1)S(1)} slice(bf16[416,1152]{1,0:T(8,128)(2,1)} %array_ref.7), slice={[0:96], [0:1152]} | slice | bytes 442368 | tf_op jit(solution)/shard_map/slice | solution.py:146
  1.6 6.0 %collective-permute-start = (bf16[96,1152]{1,0:T(8,128)(2,1)S(1)}, bf16[96,1152]{1,0:T(8,128)(2,1)S(1)}, u32[]{:S(2)}, u32[]{:S(2)}) collective-permute-start(bf16[96,1152]{1,0:T(8,128)(2,1)S(1)} %slice.3.refs_0_), channel_id=1, source_target_pairs={{0,28},{4,0},{8,4},{12,8},{16,12},{20,16},{24,20},{28,24},{1,29},{... | collective-permute-start | bytes 663560 | tf_op jit(solution)/shard_map/ppermute | solution.py:17
  7.6 1.2 %copy-done = bf16[416,1152]{1,0:T(8,128)(2,1)S(1)} copy-done((bf16[416,1152]{1,0:T(8,128)(2,1)S(1)}, bf16[416,1152]{1,0:T(8,128)(2,1)}, u32[]{:S(2)}) %copy-start) | copy-done | bytes 958488
  8.8 0.2 fetch.7
  9.0 0.6 %collective-permute-start.4 = (bf16[160,1152]{1,0:T(8,128)(2,1)S(1)}, bf16[160,1152]{1,0:T(8,128)(2,1)S(1)}, u32[]{:S(2)}, u32[]{:S(2)}) collective-permute-start(bf16[160,1152]{1,0:T(8,128)(2,1)S(1)} %fetch.7), channel_id=1, source_target_pairs={{0,28},{4,0},{8,4},{12,8},{16,12},{20,16},{24,20},{28,24},{1,29},{... | collective-permute-start | bytes 1105928 | tf_op jit(solution)/shard_map/ppermute | solution.py:17
  10.9 2.4 %collective-permute-done.refs_0_.upper_ref = bf16[96,1152]{1,0:T(8,128)(2,1)S(1)} collective-permute-done((bf16[96,1152]{1,0:T(8,128)(2,1)S(1)}, bf16[96,1152]{1,0:T(8,128)(2,1)S(1)}, u32[]{:S(2)}, u32[]{:S(2)}) %collective-permute-start) | collective-permute-done | bytes 221216 | tf_op jit(solution)/shard_map/ppermute | solution.py:17
  13.3 0.0 copy-start.1
  13.3 2.4 %subtract_convert_fusion.refs_0_ = bf16[416,416]{1,0:T(8,128)(2,1)S(1)} fusion(s32[416]{0:T(512)S(1)} %bitcast.30, f32[]{:T(128)} %bitcast.28, bf16[416,1152]{1,0:T(8,128)(2,1)} %array_ref.7, bf16[416,1152]{1,0:T(8,128)(2,1)} %image_ref.3, f32[]{:T(128)} %bitcast.24), kind=kOutput, calls=%fused_computation.22 | convolution fusion | flops 400278528 | bytes 2264712 | tf_op jit(solution)/shard_map/dot_general | solution.py:21
  15.7 0.7 %fusion.16.refs_2_ = f32[416,1152]{1,0:T(8,128)S(1)} fusion(bf16[416,416]{1,0:T(8,128)(2,1)S(1)} %subtract_convert_fusion.refs_0_, bf16[416,1152]{1,0:T(8,128)(2,1)S(1)} %copy-done.1), kind=kOutput, calls=%fused_computation.25 | convolution fusion | flops 398721024 | bytes 3221504 | tf_op jit(solution)/shard_map/dot_general | solution.py:25
  16.5 0.3 fetch.5
  16.8 0.2 fetch.6
  17.0 5.2 %collective-permute-start.2 = (bf16[112,1152]{1,0:T(8,128)(2,1)S(1)}, bf16[112,1152]{1,0:T(8,128)(2,1)S(1)}, u32[]{:S(2)}, u32[]{:S(2)}) collective-permute-start(bf16[112,1152]{1,0:T(8,128)(2,1)S(1)} %fetch.5), channel_id=1, source_target_pairs={{0,28},{4,0},{8,4},{12,8},{16,12},{20,16},{24,20},{28,24},{1,29},{... | collective-permute-start | bytes 774152 | tf_op jit(solution)/shard_map/ppermute | solution.py:17
  22.2 0.1 collective-permute-start.3
  22.3 0.7 %fusion.15.refs_1_ = f32[416,1152]{1,0:T(8,128)S(1)} fusion(bf16[416,416]{1,0:T(8,128)(2,1)S(1)} %subtract_convert_fusion.refs_0_, bf16[416,1152]{1,0:T(8,128)(2,1)S(1)} %copy-done.2), kind=kOutput, calls=%fused_computation.24 | convolution fusion | flops 398721024 | bytes 3221504 | tf_op jit(solution)/shard_map/dot_general | solution.py:29
  23.0 1.6 %chunk.2 = (bf16[256,1152]{1,0:T(8,128)(2,1)S(1)}, bf16[256,1152]{1,0:T(8,128)(2,1)S(1)}, bf16[256,416]{1,0:T(8,128)(2,1)S(1)}, bf16[256,416]{1,0:T(8,128)(2,1)S(1)}) custom-call(f32[1]{0:T(128)} %copy.13.scale_ref, f32[1]{0:T(128)} %copy.14.bias_ref, bf16[416,1152]{1,0:T(8,128)(2,1)S(1)} %copy-done.2, bf16[416,1152]{1,0:T(8,128)(2,1)S(1)} %pass_on.2.next_ref, ...), custom_call_target="tpu_custom_call" | custom-call | flops 981467136 | bytes 3686400 | tf_op jit(solution)/shard_map/chunk/pallas_call | solution.py:91
  24.7 2.0 %collective-permute-start.6 = (bf16[256,1152]{1,0:T(8,128)(2,1)S(1)}, bf16[256,1152]{1,0:T(8,128)(2,1)S(1)}, u32[]{:S(2)}, u32[]{:S(2)}) collective-permute-start(bf16[256,1152]{1,0:T(8,128)(2,1)S(1)} %get-tuple-element.17), channel_id=1, source_target_pairs={{0,4},{4,8},{8,12},{12,16},{16,20},{20,24},{24,28},{28,0},{1,5},{5... | collective-permute-start | bytes 1769480 | tf_op jit(solution)/shard_map/ppermute | solution.py:17
  26.7 0.8 %fusion.14 = bf16[416,416]{1,0:T(8,128)(2,1)S(1)} fusion(bf16[416,1152]{1,0:T(8,128)(2,1)S(1)} %pass_on.2.next_ref, bf16[416,1152]{1,0:T(8,128)(2,1)S(1)} %copy-done.1, f32[]{:T(128)} %bitcast.29, f32[]{:T(128)} %bitcast.27), kind=kOutput, calls=%fused_computation.21 | convolution fusion | flops 399759360 | bytes 2263048 | tf_op jit(solution)/shard_map/dot_general | solution.py:21
  27.5 0.7 %fusion.17 = f32[416,1152]{1,0:T(8,128)S(1)} fusion(bf16[416,416]{1,0:T(8,128)(2,1)S(1)} %fusion.14, bf16[416,1152]{1,0:T(8,128)(2,1)S(1)} %copy-done.1), kind=kOutput, calls=%fused_computation.26 | convolution fusion | flops 398721024 | bytes 3221504 | tf_op jit(solution)/shard_map/dot_general | solution.py:29
  28.2 0.5 convolution_add_fusion.4.refs_0_
  28.7 12.3 %collective-permute-done.3.lower_ref = bf16[48,1152]{1,0:T(8,128)(2,1)S(1)} collective-permute-done((bf16[48,1152]{1,0:T(8,128)(2,1)S(1)}, bf16[48,1152]{1,0:T(8,128)(2,1)S(1)}, u32[]{:S(2)}, u32[]{:S(2)}) %collective-permute-start.3) | collective-permute-done | bytes 110624 | tf_op jit(solution)/shard_map/ppermute | solution.py:17
  41.1 1.3 %chunk.3 = (bf16[160,1152]{1,0:T(8,128)(2,1)S(1)}, bf16[160,1152]{1,0:T(8,128)(2,1)S(1)}, bf16[160,416]{1,0:T(8,128)(2,1)S(1)}, bf16[160,416]{1,0:T(8,128)(2,1)S(1)}) custom-call(f32[1]{0:T(128)} %copy.13.scale_ref, f32[1]{0:T(128)} %copy.14.bias_ref, bf16[416,1152]{1,0:T(8,128)(2,1)S(1)} %copy-done.2, bf16[416,1152]{1,0:T(8,128)(2,1)S(1)} %pass_on.2.next_ref, ...), custom_call_target="tpu_custom_call" | custom-call | flops 613416960 | bytes 3022848 | tf_op jit(solution)/shard_map/chunk/pallas_call | solution.py:91
  42.3 0.5 fusion.3.refs_1_
  42.8 0.1 collective-permute-start.7
  42.9 0.1 collective-permute-start.5
  43.0 0.5 convolution_add_fusion.3
  43.5 0.5 fusion.1.total_ref
  44.0 0.7 %fusion.total_ref = f32[416,1152]{1,0:T(8,128)S(1)} fusion(f32[416,1152]{1,0:T(8,128)S(1)} %fusion.15.refs_1_, bf16[416,416]{1,0:T(8,128)(2,1)S(1)} %fusion.14, bf16[416,1152]{1,0:T(8,128)(2,1)S(1)} %pass_on.2.next_ref, f32[]{:T(128)} %bitcast.23), kind=kOutput, calls=%fused_computation.1 | convolution fusion | flops 399679488 | bytes 5138436 | tf_op jit(solution)/shard_map/dot_general | solution.py:25
  44.8 0.9 %add_rows.3.refs_0_ = bf16[416,1152]{1,0:T(8,128)(2,1)} custom-call(f32[416,1152]{1,0:T(8,128)S(1)} %fusion.total_ref, bf16[256,1152]{1,0:T(8,128)(2,1)S(1)} %collective-permute-done.6.back_ref), custom_call_target="tpu_custom_call" | custom-call | tf_op jit(solution)/shard_map/add_rows/pallas_call | solution.py:130
  45.6 8.6 %collective-permute-done.7.back_ref = bf16[416,1152]{1,0:T(8,128)(2,1)S(1)} collective-permute-done((bf16[416,1152]{1,0:T(8,128)(2,1)S(1)}, bf16[416,1152]{1,0:T(8,128)(2,1)S(1)}, u32[]{:S(2)}, u32[]{:S(2)}) %collective-permute-start.7) | collective-permute-done | bytes 958496 | tf_op jit(solution)/shard_map/ppermute | solution.py:17
  54.3 1.0 %add_rows.4 = (bf16[416,1152]{1,0:T(8,128)(2,1)}, f32[8,128]{1,0:T(8,128)S(1)}) custom-call(f32[416,1152]{1,0:T(8,128)S(1)} %fusion.1.total_ref, bf16[416,1152]{1,0:T(8,128)(2,1)S(1)} %collective-permute-done.7.back_ref), custom_call_target="tpu_custom_call" | custom-call | tf_op jit(solution)/shard_map/add_rows/pallas_call | solution.py:130
  55.3 1.3 %collective-permute-done.5.back_ref = bf16[160,1152]{1,0:T(8,128)(2,1)S(1)} collective-permute-done((bf16[160,1152]{1,0:T(8,128)(2,1)S(1)}, bf16[160,1152]{1,0:T(8,128)(2,1)S(1)}, u32[]{:S(2)}, u32[]{:S(2)}) %collective-permute-start.5) | collective-permute-done | bytes 368672 | tf_op jit(solution)/shard_map/ppermute | solution.py:17
  56.6 0.8 %add_rows.5 = bf16[416,1152]{1,0:T(8,128)(2,1)} custom-call(f32[416,1152]{1,0:T(8,128)S(1)} %fusion.total_ref, bf16[160,1152]{1,0:T(8,128)(2,1)S(1)} %collective-permute-done.5.back_ref, bf16[416,1152]{1,0:T(8,128)(2,1)} %add_rows.3.refs_0_, f32[8,128]{1,0:T(8,128)S(1)} %get-tuple-element.20.refs_1_), custom_call_target="tpu_custom_call", output_to_operand_aliasing={{}: (2, {})} | custom-call | tf_op jit(solution)/shard_map/add_rows/pallas_call | solution.py:130
  (14 shorter events, 0.0 us)
Async XLA Ops:
  0.6 12.6 %copy-start.3 = (s32[1,416]{1,0:T(1,128)S(1)}, s32[1,416]{1,0:T(1,128)}, u32[]{:S(2)}) copy-start(s32[1,416]{1,0:T(1,128)} %array_ref.4) | copy-start | bytes 4996
  1.6 11.6 %collective-permute-start = (bf16[96,1152]{1,0:T(8,128)(2,1)S(1)}, bf16[96,1152]{1,0:T(8,128)(2,1)S(1)}, u32[]{:S(2)}, u32[]{:S(2)}) collective-permute-start(bf16[96,1152]{1,0:T(8,128)(2,1)S(1)} %slice.3.refs_0_), channel_id=1, source_target_pairs={{0,28},{4,0},{8,4},{12,8},{16,12},{20,16},{24,20},{28,24},{1,29},{... | collective-permute-start | bytes 663560 | tf_op jit(solution)/shard_map/ppermute | solution.py:17
  7.6 15.4 %collective-permute-start.1 = (bf16[416,1152]{1,0:T(8,128)(2,1)}, bf16[416,1152]{1,0:T(8,128)(2,1)S(1)}, u32[]{:S(2)}, u32[]{:S(2)}) collective-permute-start(bf16[416,1152]{1,0:T(8,128)(2,1)} %image_ref.3), channel_id=1, source_target_pairs={{0,1},{1,2},{2,3},{3,0},{4,5},{5,6},{6,7},{7,4},{8,9},{9,10},{10,1... | collective-permute-start | bytes 2875400 | tf_op jit(solution)/shard_map/ppermute | solution.py:17
  7.6 1.2 %copy-start = (bf16[416,1152]{1,0:T(8,128)(2,1)S(1)}, bf16[416,1152]{1,0:T(8,128)(2,1)}, u32[]{:S(2)}) copy-start(bf16[416,1152]{1,0:T(8,128)(2,1)} %array_ref.7) | copy-start | bytes 2875396
  9.0 14.0 %collective-permute-start.4 = (bf16[160,1152]{1,0:T(8,128)(2,1)S(1)}, bf16[160,1152]{1,0:T(8,128)(2,1)S(1)}, u32[]{:S(2)}, u32[]{:S(2)}) collective-permute-start(bf16[160,1152]{1,0:T(8,128)(2,1)S(1)} %fetch.7), channel_id=1, source_target_pairs={{0,28},{4,0},{8,4},{12,8},{16,12},{20,16},{24,20},{28,24},{1,29},{... | collective-permute-start | bytes 1105928 | tf_op jit(solution)/shard_map/ppermute | solution.py:17
  13.3 2.5 %copy-start.1 = (bf16[416,1152]{1,0:T(8,128)(2,1)S(1)}, bf16[416,1152]{1,0:T(8,128)(2,1)}, u32[]{:S(2)}) copy-start(bf16[416,1152]{1,0:T(8,128)(2,1)} %array_ref.7) | copy-start | bytes 2875396
  16.5 5.8 %copy-start.2 = (bf16[416,1152]{1,0:T(8,128)(2,1)S(1)}, bf16[416,1152]{1,0:T(8,128)(2,1)}, u32[]{:S(2)}) copy-start(bf16[416,1152]{1,0:T(8,128)(2,1)} %image_ref.3) | copy-start | bytes 2875396
  17.0 24.0 %collective-permute-start.2 = (bf16[112,1152]{1,0:T(8,128)(2,1)S(1)}, bf16[112,1152]{1,0:T(8,128)(2,1)S(1)}, u32[]{:S(2)}, u32[]{:S(2)}) collective-permute-start(bf16[112,1152]{1,0:T(8,128)(2,1)S(1)} %fetch.5), channel_id=1, source_target_pairs={{0,28},{4,0},{8,4},{12,8},{16,12},{20,16},{24,20},{28,24},{1,29},{... | collective-permute-start | bytes 774152 | tf_op jit(solution)/shard_map/ppermute | solution.py:17
  22.2 18.8 %collective-permute-start.3 = (bf16[48,1152]{1,0:T(8,128)(2,1)S(1)}, bf16[48,1152]{1,0:T(8,128)(2,1)S(1)}, u32[]{:S(2)}, u32[]{:S(2)}) collective-permute-start(bf16[48,1152]{1,0:T(8,128)(2,1)S(1)} %fetch.6), channel_id=1, source_target_pairs={{0,28},{4,0},{8,4},{12,8},{16,12},{20,16},{24,20},{28,24},{1,29},{... | collective-permute-start | bytes 331784 | tf_op jit(solution)/shard_map/ppermute | solution.py:17
  24.7 20.1 %collective-permute-start.6 = (bf16[256,1152]{1,0:T(8,128)(2,1)S(1)}, bf16[256,1152]{1,0:T(8,128)(2,1)S(1)}, u32[]{:S(2)}, u32[]{:S(2)}) collective-permute-start(bf16[256,1152]{1,0:T(8,128)(2,1)S(1)} %get-tuple-element.17), channel_id=1, source_target_pairs={{0,4},{4,8},{8,12},{12,16},{16,20},{20,24},{24,28},{28,0},{1,5},{5... | collective-permute-start | bytes 1769480 | tf_op jit(solution)/shard_map/ppermute | solution.py:17
  42.8 11.4 %collective-permute-start.7 = (bf16[416,1152]{1,0:T(8,128)(2,1)S(1)}, bf16[416,1152]{1,0:T(8,128)(2,1)S(1)}, u32[]{:S(2)}, u32[]{:S(2)}) collective-permute-start(bf16[416,1152]{1,0:T(8,128)(2,1)S(1)} %fusion.3.refs_1_), channel_id=1, source_target_pairs={{0,3},{1,0},{2,1},{3,2},{4,7},{5,4},{6,5},{7,6},{8,11},{9,8},{10,9... | collective-permute-start | bytes 2875400 | tf_op jit(solution)/shard_map/ppermute | solution.py:17
  42.9 13.7 %collective-permute-start.5 = (bf16[160,1152]{1,0:T(8,128)(2,1)S(1)}, bf16[160,1152]{1,0:T(8,128)(2,1)S(1)}, u32[]{:S(2)}, u32[]{:S(2)}) collective-permute-start(bf16[160,1152]{1,0:T(8,128)(2,1)S(1)} %pass_on.3), channel_id=1, source_target_pairs={{0,4},{4,8},{8,12},{12,16},{16,20},{20,24},{24,28},{28,0},{1,5},{5... | collective-permute-start | bytes 1105928 | tf_op jit(solution)/shard_map/ppermute | solution.py:17

commit v13 on v6

--- a/solution.py
+++ b/solution.py
@@ -1,3 +1,5 @@
+import functools
+
 import jax
 import jax.numpy as jnp
 from jax import lax
@@ -6,6 +8,7 @@
 from jax.sharding import PartitionSpec as P
 
 MIB = 2**20
+ENDS = (8, 23)
 SMEM = pl.BlockSpec(memory_space=pltpu.SMEM)
 VMEM = pl.BlockSpec(memory_space=pltpu.VMEM)
 HBM = pl.BlockSpec(memory_space=pltpu.HBM)
@@ -31,7 +34,7 @@
 
 def row_cuts(rows):
     tiles = rows // 16
-    cuts = [0, tiles * 6 // 26 * 16, tiles * 16 // 26 * 16, tiles * 20 // 26 * 16, rows]
+    cuts = [0] + [tiles * ends // 26 * 16 for ends in ENDS] + [rows]
     return list(zip(cuts[:-1], cuts[1:]))
 
 
@@ -65,12 +68,14 @@
     )(array, *after)
 
 
-def chunk_kernel(scale_ref, bias_ref, image_ref, next_ref, upper_ref, lower_ref, *refs):
+def chunk_kernel(count, scale_ref, bias_ref, image_ref, next_ref, *refs):
     sent_ref, joined_ref, own_ref, other_ref = refs[-4:]
     scale, bias = scale_ref[0], bias_ref[0]
-    rows = upper_ref.shape[0]
-    joined_ref[:rows, :] = upper_ref[...]
-    joined_ref[rows:, :] = lower_ref[...]
+    start = 0
+    for piece_ref in refs[:count]:
+        rows = piece_ref.shape[0]
+        joined_ref[start : start + rows, :] = piece_ref[...]
+        start += rows
     part = joined_ref[...]
     image = image_ref[...]
     own = jax.nn.sigmoid(dot_nt(part, image) * scale + bias).astype(jnp.bfloat16)
@@ -83,15 +88,14 @@
     sent_ref[...] = (scale * total).astype(jnp.bfloat16)
 
 
-def chunk(factor, shift, image, image_next, upper, lower, after):
-    rows, width = upper.shape[0] + lower.shape[0], upper.shape[1]
-    columns = image.shape[0]
+def chunk(factor, shift, image, image_next, pieces, after):
+    rows, (columns, width) = sum(piece.shape[0] for piece in pieces), image.shape
     text = jax.ShapeDtypeStruct((rows, width), jnp.bfloat16)
     tile = jax.ShapeDtypeStruct((rows, columns), jnp.bfloat16)
     return pl.pallas_call(
-        chunk_kernel,
+        functools.partial(chunk_kernel, len(pieces)),
         out_shape=(text, text, tile, tile),
-        in_specs=[SMEM] * 2 + [VMEM] * 4 + [ANY] * len(after),
+        in_specs=[SMEM] * 2 + [VMEM] * (2 + len(pieces)) + [ANY] * len(after),
         out_specs=(VMEM,) * 4,
         compiler_params=pltpu.CompilerParams(vmem_limit_bytes=16 * MIB),
         cost_estimate=pl.CostEstimate(
@@ -100,7 +104,7 @@
             transcendentals=2 * rows * columns,
         ),
         name="chunk",
-    )(factor, shift, image, image_next, upper, lower, *after)
+    )(factor, shift, image, image_next, *pieces, *after)
 
 
 def add_rows(total, back, lo, result, after, mark=False):
@@ -149,34 +153,33 @@
     part.append(shifted(fetch(text, *cuts[1], [first]), "blk", 1))
 
     target = fetch(target, 0, 1, [part[0]])
-    part.append(shifted(fetch(text, *cuts[2], [target]), "blk", 1))
     own = jax.nn.sigmoid(dot_nt(image, text) * scale + bias)
     column = lax.broadcasted_iota(jnp.int32, own.shape, 1)
     own = (own - (column == target[0][:, None]).astype(jnp.float32)).astype(jnp.bfloat16)
-    part.append(shifted(fetch(text, *cuts[3], [own]), "blk", 1))
+    part.append(shifted(fetch(text, *cuts[2], [own]), "blk", 1))
     image_grad = dot_nn(own, text)
     text_grad = dot_tn(own, image)
 
     image_next = pass_on(image_next, [image_grad, text_grad])
-    sent0, part0, own0, next0 = chunk(factor, shift, image, image_next, part[0], part[1], [])
+    sent0, part0, own0, next0 = chunk(factor, shift, image, image_next, part[:1], [])
     next_own = jax.nn.sigmoid(dot_nt(image_next, text) * scale + bias).astype(jnp.bfloat16)
     text_grad = scale * (text_grad + dot_tn(next_own, image_next))
     image_sent = dot_nn(next_own, text) + dot_tn(next0, part0)
     image_grad = image_grad + dot_tn(own0, part0)
 
-    sent0 = pass_on(sent0, [part[2], image_sent])
+    sent0 = pass_on(sent0, [part[1], image_sent])
     back0 = shifted(sent0, "blk", -1)
 
-    sent1, part1, own1, next1 = chunk(factor, shift, image, image_next, part[2], part[3], [sent0])
+    sent1, part1, own1, next1 = chunk(factor, shift, image, image_next, part[1:], [sent0])
     image_sent = (scale * (image_sent + dot_tn(next1, part1))).astype(jnp.bfloat16)
     image_back = shifted(image_sent, "grp", 1)
     sent1 = pass_on(sent1, [image_sent])
     back1 = shifted(sent1, "blk", -1)
+    result, mark = add_rows(text_grad, back0, 0, None, [], mark=True)
+    own1 = pass_on(own1, [mark])
     image_grad = scale * (image_grad + dot_tn(own1, part1))
-
-    result = add_rows(text_grad, back0, 0, None, [])
     image_grad, mark = add_rows(image_grad, image_back, 0, None, [], mark=True)
-    result = add_rows(text_grad, back1, cuts[2][0], result, [mark])
+    result = add_rows(text_grad, back1, cuts[1][0], result, [mark])
     return image_grad, result
 
 

time: 54.9 us -> 50.5 us (0.920)
  waiting for transfers between devices: 28.5 us -> 24.1 us
    ppermute x8 -> x7, waiting for transfers between devices: 28.5 us -> 24.1 us  [shifted(): lax.ppermute(shard, axis, [(i, (i + by) % devices) for i in range(devices)])]
    ppermute x8 -> x7, starting transfers between devices: 9 us -> 8.93 us  [shifted(): lax.ppermute(shard, axis, [(i, (i + by) % devices) for i in range(devices)])]
  transfers between devices with their start and end apart: 8 -> 7, of which waited for: 6 -> 5; matrix products, arithmetic and copies ran while one was open for 12% -> 14% of each run, Pallas kernels for 10% -> 10%
where the time goes in v13:
time: 50.5 us; the launch traced here: 50.3 us
  waiting for transfers between devices  24.1 us (48%)
  starting transfers between devices  8.93 us (18%)
  matrix products  6.94 us (14%)
  Pallas kernels  6.01 us (12%)
  local copies, waits for them, and re-layouts  2.2 us (4%)
  between operations  2.13 us (4%)
    ppermute x7, waiting for transfers between devices, shifted(): lax.ppermute(shard, axis, [(i, (i + by) % devices) for i in range(devices)])  24.1 us
    ppermute x7, starting transfers between devices, shifted(): lax.ppermute(shard, axis, [(i, (i + by) % devices) for i in range(devices)])  8.93 us
    dot_general x6, matrix products, dot_tn(): lax.dot_general(a, b, (((0,), (0,)), ((), ())), preferred_element_type=jn...  3.81 us
    pallas_call x2, Pallas kernels, chunk(): pl.pallas_call(functools.partial(chunk_kernel, len(pieces)), out_shape=(t...  3.07 us
    pallas_call x3, Pallas kernels, add_rows(): pl.pallas_call(kernel, out_shape=(out, jax.ShapeDtypeStruct((8, 128), jnp...  2.68 us
    dot_general x2, matrix products, dot_nt(): lax.dot_general(a, b, (((1,), (1,)), ((), ())), preferred_element_type=jn...  1.72 us
    dot_general x2, matrix products, dot_nn(): return jnp.dot(a, b, preferred_element_type=jnp.float32)  1.4 us
    unnamed x8, local copies, waits for them, and re-layouts  1.2 us
  transfers between devices with their start and end apart: 7, of which 5 were waited for; matrix products, arithmetic and copies ran while one was open for 14% of the time, Pallas kernels for 10%

profile of v13, /device:TPU:0, one launch (start us, length us, event | category | flops | bytes accessed | tf_op | source)
XLA Modules:
  0.0 50.3 jit_solution(18142792807789566977)
XLA Ops:
  0.6 1.0 %slice.3.refs_0_ = bf16[128,1152]{1,0:T(8,128)(2,1)S(1)} slice(bf16[416,1152]{1,0:T(8,128)(2,1)} %array_ref.5), slice={[0:128], [0:1152]} | slice | bytes 589824 | tf_op jit(solution)/shard_map/slice | solution.py:150
  1.6 3.0 %collective-permute-start = (bf16[128,1152]{1,0:T(8,128)(2,1)S(1)}, bf16[128,1152]{1,0:T(8,128)(2,1)S(1)}, u32[]{:S(2)}, u32[]{:S(2)}) collective-permute-start(bf16[128,1152]{1,0:T(8,128)(2,1)S(1)} %slice.3.refs_0_), channel_id=1, source_target_pairs={{0,4},{4,8},{8,12},{12,16},{16,20},{20,24},{24,28},{28,0},{1,5},{5... | collective-permute-start | bytes 884744 | tf_op jit(solution)/shard_map/ppermute | solution.py:20
  4.6 0.7 %collective-permute-start.1 = (bf16[416,1152]{1,0:T(8,128)(2,1)}, bf16[416,1152]{1,0:T(8,128)(2,1)S(1)}, u32[]{:S(2)}, u32[]{:S(2)}) collective-permute-start(bf16[416,1152]{1,0:T(8,128)(2,1)} %image_ref.3), channel_id=1, source_target_pairs={{0,3},{1,0},{2,1},{3,2},{4,7},{5,4},{6,5},{7,6},{8,11},{9,8},{10,9... | collective-permute-start | bytes 2875400 | tf_op jit(solution)/shard_map/ppermute | solution.py:20
  5.3 1.2 %copy-done = bf16[416,1152]{1,0:T(8,128)(2,1)S(1)} copy-done((bf16[416,1152]{1,0:T(8,128)(2,1)S(1)}, bf16[416,1152]{1,0:T(8,128)(2,1)}, u32[]{:S(2)}) %copy-start) | copy-done | bytes 958488
  6.5 0.1 fetch.4
  6.6 1.6 %collective-permute-start.2 = (bf16[240,1152]{1,0:T(8,128)(2,1)S(1)}, bf16[240,1152]{1,0:T(8,128)(2,1)S(1)}, u32[]{:S(2)}, u32[]{:S(2)}) collective-permute-start(bf16[240,1152]{1,0:T(8,128)(2,1)S(1)} %fetch.4), channel_id=1, source_target_pairs={{0,4},{4,8},{8,12},{12,16},{16,20},{20,24},{24,28},{28,0},{1,5},{5... | collective-permute-start | bytes 1658888 | tf_op jit(solution)/shard_map/ppermute | solution.py:20
  9.5 6.0 %collective-permute-done.refs_0_ = bf16[128,1152]{1,0:T(8,128)(2,1)S(1)} collective-permute-done((bf16[128,1152]{1,0:T(8,128)(2,1)S(1)}, bf16[128,1152]{1,0:T(8,128)(2,1)S(1)}, u32[]{:S(2)}, u32[]{:S(2)}) %collective-permute-start) | collective-permute-done | bytes 294944 | tf_op jit(solution)/shard_map/ppermute | solution.py:20
  15.5 0.9 %subtract_convert_fusion.refs_0_ = bf16[416,416]{1,0:T(8,128)(2,1)S(1)} fusion(s32[416]{0:T(512)S(1)} %bitcast.30, f32[]{:T(128)} %bitcast.28, bf16[416,1152]{1,0:T(8,128)(2,1)S(1)} %copy-done.2, bf16[416,1152]{1,0:T(8,128)(2,1)S(1)} %copy-done.1, f32[]{:T(128)} %bitcast.24), kind=kOutput, calls=%fused_computation.22 | convolution fusion | flops 400278528 | bytes 2264712 | tf_op jit(solution)/shard_map/dot_general | solution.py:24
  16.4 0.2 fetch.5
  16.6 0.1 collective-permute-start.3
  16.7 0.7 %fusion.17.refs_2_ = f32[416,1152]{1,0:T(8,128)S(1)} fusion(bf16[416,416]{1,0:T(8,128)(2,1)S(1)} %subtract_convert_fusion.refs_0_, bf16[416,1152]{1,0:T(8,128)(2,1)S(1)} %copy-done.2), kind=kOutput, calls=%fused_computation.25 | convolution fusion | flops 398721024 | bytes 3221504 | tf_op jit(solution)/shard_map/dot_general | solution.py:28
  17.4 0.7 %fusion.16.refs_1_ = f32[416,1152]{1,0:T(8,128)S(1)} fusion(bf16[416,416]{1,0:T(8,128)(2,1)S(1)} %subtract_convert_fusion.refs_0_, bf16[416,1152]{1,0:T(8,128)(2,1)S(1)} %copy-done.1), kind=kOutput, calls=%fused_computation.24 | convolution fusion | flops 398721024 | bytes 3221504 | tf_op jit(solution)/shard_map/dot_general | solution.py:32
  18.1 0.0 collective-permute-done.1.refs_0_
  18.1 0.8 %fusion.15 = bf16[416,416]{1,0:T(8,128)(2,1)S(1)} fusion(bf16[416,1152]{1,0:T(8,128)(2,1)S(1)} %pass_on.4.next_ref, bf16[416,1152]{1,0:T(8,128)(2,1)S(1)} %copy-done.1, f32[]{:T(128)} %bitcast.29, f32[]{:T(128)} %bitcast.27), kind=kOutput, calls=%fused_computation.21 | convolution fusion | flops 399759360 | bytes 2263048 | tf_op jit(solution)/shard_map/dot_general | solution.py:24
  19.0 1.2 %chunk.2 = (bf16[128,1152]{1,0:T(8,128)(2,1)S(1)}, bf16[128,1152]{1,0:T(8,128)(2,1)S(1)}, bf16[128,416]{1,0:T(8,128)(2,1)S(1)}, bf16[128,416]{1,0:T(8,128)(2,1)S(1)}) custom-call(f32[1]{0:T(128)} %copy.17.scale_ref, f32[1]{0:T(128)} %copy.18.bias_ref, bf16[416,1152]{1,0:T(8,128)(2,1)S(1)} %copy-done.2, bf16[416,1152]{1,0:T(8,128)(2,1)S(1)} %pass_on.4.next_ref, ...), custom_call_target="tpu_custom_call" | custom-call | flops 490733568 | bytes 2801664 | tf_op jit(solution)/shard_map/chunk/pallas_call | solution.py:95
  20.2 0.7 %fusion.18 = f32[416,1152]{1,0:T(8,128)S(1)} fusion(bf16[416,416]{1,0:T(8,128)(2,1)S(1)} %fusion.15, bf16[416,1152]{1,0:T(8,128)(2,1)S(1)} %copy-done.1), kind=kOutput, calls=%fused_computation.26 | convolution fusion | flops 398721024 | bytes 3221504 | tf_op jit(solution)/shard_map/dot_general | solution.py:32
  20.9 0.4 convolution_add_fusion.1.refs_2_
  21.3 6.0 %collective-permute-done.2.refs_1_.refs_0_ = bf16[240,1152]{1,0:T(8,128)(2,1)S(1)} collective-permute-done((bf16[240,1152]{1,0:T(8,128)(2,1)S(1)}, bf16[240,1152]{1,0:T(8,128)(2,1)S(1)}, u32[]{:S(2)}, u32[]{:S(2)}) %collective-permute-start.2) | collective-permute-done | bytes 552992 | tf_op jit(solution)/shard_map/ppermute | solution.py:20
  27.4 2.1 %collective-permute-start.4 = (bf16[128,1152]{1,0:T(8,128)(2,1)S(1)}, bf16[128,1152]{1,0:T(8,128)(2,1)S(1)}, u32[]{:S(2)}, u32[]{:S(2)}) collective-permute-start(bf16[128,1152]{1,0:T(8,128)(2,1)S(1)} %pass_on.5.refs_2_), channel_id=1, source_target_pairs={{0,28},{4,0},{8,4},{12,8},{16,12},{20,16},{24,20},{28,24},{1,29},{... | collective-permute-start | bytes 884744 | tf_op jit(solution)/shard_map/ppermute | solution.py:20
  29.4 1.9 %chunk.3 = (bf16[288,1152]{1,0:T(8,128)(2,1)S(1)}, bf16[288,1152]{1,0:T(8,128)(2,1)S(1)}, bf16[288,416]{1,0:T(8,128)(2,1)S(1)}, bf16[288,416]{1,0:T(8,128)(2,1)S(1)}) custom-call(f32[1]{0:T(128)} %copy.17.scale_ref, f32[1]{0:T(128)} %copy.18.bias_ref, bf16[416,1152]{1,0:T(8,128)(2,1)S(1)} %copy-done.2, bf16[416,1152]{1,0:T(8,128)(2,1)S(1)} %pass_on.4.next_ref, ...), custom_call_target="tpu_custom_call" | custom-call | flops 1104150528 | bytes 3907584 | tf_op jit(solution)/shard_map/chunk/pallas_call | solution.py:95
  31.3 0.7 %fusion.4.refs_1_ = bf16[416,1152]{1,0:T(8,128)(2,1)S(1)} fusion(f32[416,1152]{1,0:T(8,128)S(1)} %convolution_add_fusion.1.refs_2_, bf16[288,416]{1,0:T(8,128)(2,1)S(1)} %get-tuple-element.21, bf16[288,1152]{1,0:T(8,128)(2,1)S(1)} %get-tuple-element.20, f32[]{:T(128)} %bitcast.25), kind=kOutput, calls=%fused_computation.8 | convolution fusion | flops 277475328 | bytes 3778564 | tf_op jit(solution)/shard_map/dot_general | solution.py:28
  32.0 0.1 collective-permute-start.5
  32.1 1.5 %collective-permute-start.6 = (bf16[288,1152]{1,0:T(8,128)(2,1)S(1)}, bf16[288,1152]{1,0:T(8,128)(2,1)S(1)}, u32[]{:S(2)}, u32[]{:S(2)}) collective-permute-start(bf16[288,1152]{1,0:T(8,128)(2,1)S(1)} %pass_on.7), channel_id=1, source_target_pairs={{0,28},{4,0},{8,4},{12,8},{16,12},{20,16},{24,20},{28,24},{1,29},{... | collective-permute-start | bytes 1990664 | tf_op jit(solution)/shard_map/ppermute | solution.py:20
  33.6 0.7 %fusion.total_ref = f32[416,1152]{1,0:T(8,128)S(1)} fusion(f32[416,1152]{1,0:T(8,128)S(1)} %fusion.17.refs_2_, bf16[416,416]{1,0:T(8,128)(2,1)S(1)} %fusion.15, bf16[416,1152]{1,0:T(8,128)(2,1)S(1)} %pass_on.4.next_ref, f32[]{:T(128)} %bitcast.23), kind=kOutput, calls=%fused_computation.1 | convolution fusion | flops 399679488 | bytes 5138436 | tf_op jit(solution)/shard_map/dot_general | solution.py:28
  34.3 0.9 %collective-permute-done.4.back_ref = bf16[128,1152]{1,0:T(8,128)(2,1)S(1)} collective-permute-done((bf16[128,1152]{1,0:T(8,128)(2,1)S(1)}, bf16[128,1152]{1,0:T(8,128)(2,1)S(1)}, u32[]{:S(2)}, u32[]{:S(2)}) %collective-permute-start.4) | collective-permute-done | bytes 294944 | tf_op jit(solution)/shard_map/ppermute | solution.py:20
  35.2 0.8 %add_rows.3 = (bf16[416,1152]{1,0:T(8,128)(2,1)}, f32[8,128]{1,0:T(8,128)S(1)}) custom-call(f32[416,1152]{1,0:T(8,128)S(1)} %fusion.total_ref, bf16[128,1152]{1,0:T(8,128)(2,1)S(1)} %collective-permute-done.4.back_ref), custom_call_target="tpu_custom_call" | custom-call | tf_op jit(solution)/shard_map/add_rows/pallas_call | solution.py:134
  36.0 0.7 %fusion.19 = f32[416,1152]{1,0:T(8,128)S(1)} fusion(bf16[288,416]{1,0:T(8,128)(2,1)S(1)} %pass_on.6, bf16[288,1152]{1,0:T(8,128)(2,1)S(1)} %get-tuple-element.20), kind=kOutput, calls=%fused_computation.27 | convolution fusion | flops 276037632 | bytes 2820096 | tf_op jit(solution)/shard_map/dot_general | solution.py:28
  36.7 0.4 fusion.2.total_ref
  37.2 8.2 %collective-permute-done.5.back_ref = bf16[416,1152]{1,0:T(8,128)(2,1)S(1)} collective-permute-done((bf16[416,1152]{1,0:T(8,128)(2,1)S(1)}, bf16[416,1152]{1,0:T(8,128)(2,1)S(1)}, u32[]{:S(2)}, u32[]{:S(2)}) %collective-permute-start.5) | collective-permute-done | bytes 958496 | tf_op jit(solution)/shard_map/ppermute | solution.py:20
  45.3 1.0 %add_rows.4 = (bf16[416,1152]{1,0:T(8,128)(2,1)}, f32[8,128]{1,0:T(8,128)S(1)}) custom-call(f32[416,1152]{1,0:T(8,128)S(1)} %fusion.2.total_ref, bf16[416,1152]{1,0:T(8,128)(2,1)S(1)} %collective-permute-done.5.back_ref), custom_call_target="tpu_custom_call" | custom-call | tf_op jit(solution)/shard_map/add_rows/pallas_call | solution.py:134
  46.4 3.1 %collective-permute-done.6.back_ref = bf16[288,1152]{1,0:T(8,128)(2,1)S(1)} collective-permute-done((bf16[288,1152]{1,0:T(8,128)(2,1)S(1)}, bf16[288,1152]{1,0:T(8,128)(2,1)S(1)}, u32[]{:S(2)}, u32[]{:S(2)}) %collective-permute-start.6) | collective-permute-done | bytes 663584 | tf_op jit(solution)/shard_map/ppermute | solution.py:20
  49.4 0.9 %add_rows.5 = bf16[416,1152]{1,0:T(8,128)(2,1)} custom-call(f32[416,1152]{1,0:T(8,128)S(1)} %fusion.total_ref, bf16[288,1152]{1,0:T(8,128)(2,1)S(1)} %collective-permute-done.6.back_ref, bf16[416,1152]{1,0:T(8,128)(2,1)} %get-tuple-element.24.refs_0_, f32[8,128]{1,0:T(8,128)S(1)} %get-tuple-element.25.refs_1_), custom_call_target="tpu_custom_call", output_to_operand_aliasing={{}: (2, {})} | custom-call | tf_op jit(solution)/shard_map/add_rows/pallas_call | solution.py:134
  (13 shorter events, 0.0 us)
Async XLA Ops:
  0.6 14.9 %copy-start.3 = (s32[1,416]{1,0:T(1,128)S(1)}, s32[1,416]{1,0:T(1,128)}, u32[]{:S(2)}) copy-start(s32[1,416]{1,0:T(1,128)} %array_ref.3) | copy-start | bytes 4996
  1.6 13.9 %collective-permute-start = (bf16[128,1152]{1,0:T(8,128)(2,1)S(1)}, bf16[128,1152]{1,0:T(8,128)(2,1)S(1)}, u32[]{:S(2)}, u32[]{:S(2)}) collective-permute-start(bf16[128,1152]{1,0:T(8,128)(2,1)S(1)} %slice.3.refs_0_), channel_id=1, source_target_pairs={{0,4},{4,8},{8,12},{12,16},{16,20},{20,24},{24,28},{28,0},{1,5},{5... | collective-permute-start | bytes 884744 | tf_op jit(solution)/shard_map/ppermute | solution.py:20
  4.6 13.5 %collective-permute-start.1 = (bf16[416,1152]{1,0:T(8,128)(2,1)}, bf16[416,1152]{1,0:T(8,128)(2,1)S(1)}, u32[]{:S(2)}, u32[]{:S(2)}) collective-permute-start(bf16[416,1152]{1,0:T(8,128)(2,1)} %image_ref.3), channel_id=1, source_target_pairs={{0,3},{1,0},{2,1},{3,2},{4,7},{5,4},{6,5},{7,6},{8,11},{9,8},{10,9... | collective-permute-start | bytes 2875400 | tf_op jit(solution)/shard_map/ppermute | solution.py:20
  5.3 1.2 %copy-start = (bf16[416,1152]{1,0:T(8,128)(2,1)S(1)}, bf16[416,1152]{1,0:T(8,128)(2,1)}, u32[]{:S(2)}) copy-start(bf16[416,1152]{1,0:T(8,128)(2,1)} %array_ref.5) | copy-start | bytes 2875396
  6.5 9.0 %copy-start.1 = (bf16[416,1152]{1,0:T(8,128)(2,1)S(1)}, bf16[416,1152]{1,0:T(8,128)(2,1)}, u32[]{:S(2)}) copy-start(bf16[416,1152]{1,0:T(8,128)(2,1)} %array_ref.5) | copy-start | bytes 2875396
  6.5 9.0 %copy-start.2 = (bf16[416,1152]{1,0:T(8,128)(2,1)S(1)}, bf16[416,1152]{1,0:T(8,128)(2,1)}, u32[]{:S(2)}) copy-start(bf16[416,1152]{1,0:T(8,128)(2,1)} %image_ref.3) | copy-start | bytes 2875396
  6.6 20.8 %collective-permute-start.2 = (bf16[240,1152]{1,0:T(8,128)(2,1)S(1)}, bf16[240,1152]{1,0:T(8,128)(2,1)S(1)}, u32[]{:S(2)}, u32[]{:S(2)}) collective-permute-start(bf16[240,1152]{1,0:T(8,128)(2,1)S(1)} %fetch.4), channel_id=1, source_target_pairs={{0,4},{4,8},{8,12},{12,16},{16,20},{20,24},{24,28},{28,0},{1,5},{5... | collective-permute-start | bytes 1658888 | tf_op jit(solution)/shard_map/ppermute | solution.py:20
  16.6 12.8 %collective-permute-start.3 = (bf16[48,1152]{1,0:T(8,128)(2,1)S(1)}, bf16[48,1152]{1,0:T(8,128)(2,1)S(1)}, u32[]{:S(2)}, u32[]{:S(2)}) collective-permute-start(bf16[48,1152]{1,0:T(8,128)(2,1)S(1)} %fetch.5), channel_id=1, source_target_pairs={{0,4},{4,8},{8,12},{12,16},{16,20},{20,24},{24,28},{28,0},{1,5},{5... | collective-permute-start | bytes 331784 | tf_op jit(solution)/shard_map/ppermute | solution.py:20
  27.4 7.9 %collective-permute-start.4 = (bf16[128,1152]{1,0:T(8,128)(2,1)S(1)}, bf16[128,1152]{1,0:T(8,128)(2,1)S(1)}, u32[]{:S(2)}, u32[]{:S(2)}) collective-permute-start(bf16[128,1152]{1,0:T(8,128)(2,1)S(1)} %pass_on.5.refs_2_), channel_id=1, source_target_pairs={{0,28},{4,0},{8,4},{12,8},{16,12},{20,16},{24,20},{28,24},{1,29},{... | collective-permute-start | bytes 884744 | tf_op jit(solution)/shard_map/ppermute | solution.py:20
  32.0 13.3 %collective-permute-start.5 = (bf16[416,1152]{1,0:T(8,128)(2,1)S(1)}, bf16[416,1152]{1,0:T(8,128)(2,1)S(1)}, u32[]{:S(2)}, u32[]{:S(2)}) collective-permute-start(bf16[416,1152]{1,0:T(8,128)(2,1)S(1)} %fusion.4.refs_1_), channel_id=1, source_target_pairs={{0,1},{1,2},{2,3},{3,0},{4,5},{5,6},{6,7},{7,4},{8,9},{9,10},{10,1... | collective-permute-start | bytes 2875400 | tf_op jit(solution)/shard_map/ppermute | solution.py:20
  32.1 17.3 %collective-permute-start.6 = (bf16[288,1152]{1,0:T(8,128)(2,1)S(1)}, bf16[288,1152]{1,0:T(8,128)(2,1)S(1)}, u32[]{:S(2)}, u32[]{:S(2)}) collective-permute-start(bf16[288,1152]{1,0:T(8,128)(2,1)S(1)} %pass_on.7), channel_id=1, source_target_pairs={{0,28},{4,0},{8,4},{12,8},{16,12},{20,16},{24,20},{28,24},{1,29},{... | collective-permute-start | bytes 1990664 | tf_op jit(solution)/shard_map/ppermute | solution.py:20

commit v14 on v11

--- a/solution.py
+++ b/solution.py
@@ -8,7 +8,7 @@
 from jax.sharding import PartitionSpec as P
 
 MIB = 2**20
-FIRST = 10
+FIRST = 8
 WAIT = 10**10
 SMEM = pl.BlockSpec(memory_space=pltpu.SMEM)
 VMEM = pl.BlockSpec(memory_space=pltpu.VMEM)
@@ -36,7 +36,7 @@
 def shifted_half(shard, by, parity):
     blocks, groups = lax.axis_size("blk"), lax.axis_size("grp")
     pairs = [
-        (b * groups + g, (b + by) % blocks * groups + g) for b in range(blocks) for g in range(parity, groups, 2)
+        (b * groups + g, (b + by * (g % 2 == parity)) % blocks * groups + g) for b in range(blocks) for g in range(groups)
     ]
     return lax.ppermute(shard, ("blk", "grp"), pairs)
 
@@ -72,12 +72,20 @@
     )(array, *after)
 
 
-def chunk_kernel(lo, scale_ref, bias_ref, image_ref, next_ref, even_ref, odd_ref, *refs):
+def chunk_kernel(lo, parity_ref, scale_ref, bias_ref, image_ref, next_ref, even_ref, odd_ref, *refs):
     sent_ref, part_ref, own_ref, other_ref = refs[-4:]
     scale, bias = scale_ref[0], bias_ref[0]
     rows = pl.ds(lo, part_ref.shape[0])
-    part = even_ref[rows, :] + odd_ref[rows, :]
-    part_ref[...] = part
+
+    @pl.when(parity_ref[0] == 0)
+    def _():
+        part_ref[...] = even_ref[rows, :]
+
+    @pl.when(parity_ref[0] != 0)
+    def _():
+        part_ref[...] = odd_ref[rows, :]
+
+    part = part_ref[...]
     image = image_ref[...]
     own = jax.nn.sigmoid(dot_nt(part, image) * scale + bias).astype(jnp.bfloat16)
     own_ref[...] = own
@@ -89,14 +97,14 @@
     sent_ref[...] = (scale * total).astype(jnp.bfloat16)
 
 
-def chunk(factor, shift, image, image_next, texts, lo, hi, after):
+def chunk(parity, factor, shift, image, image_next, texts, lo, hi, after):
     rows, (columns, width) = hi - lo, image.shape
     text = jax.ShapeDtypeStruct((rows, width), jnp.bfloat16)
     tile = jax.ShapeDtypeStruct((rows, columns), jnp.bfloat16)
     return pl.pallas_call(
         functools.partial(chunk_kernel, lo),
         out_shape=(text, text, tile, tile),
-        in_specs=[SMEM] * 2 + [VMEM] * 4 + [ANY] * len(after),
+        in_specs=[SMEM] * 3 + [VMEM] * 4 + [ANY] * len(after),
         out_specs=(VMEM,) * 4,
         compiler_params=pltpu.CompilerParams(vmem_limit_bytes=16 * MIB),
         cost_estimate=pl.CostEstimate(
@@ -105,10 +113,10 @@
             transcendentals=2 * rows * columns,
         ),
         name="chunk",
-    )(factor, shift, image, image_next, *texts, *after)
-
-
-def add_rows(total, pieces, result, after, mark=False):
+    )(parity, factor, shift, image, image_next, *texts, *after)
+
+
+def add_rows(total, pieces, result, after, mark=False, flops=0):
     width = total.shape[1]
     arrays = [array for _, backs in pieces for array in backs]
     steps = []
@@ -152,6 +160,7 @@
         scratch_shapes=[pltpu.VMEM((high - low, width), jnp.bfloat16), pltpu.SemaphoreType.DMA((len(steps),))],
         input_output_aliases={1 + len(arrays): 0} if kept else {},
         compiler_params=pltpu.CompilerParams(vmem_limit_bytes=4 * MIB),
+        cost_estimate=pl.CostEstimate(flops=flops, bytes_accessed=0, transcendentals=0),
         name="add_rows",
     )(total, *arrays, *kept, *after)
 
@@ -161,36 +170,38 @@
     bias = shift[0]
     count = text.shape[0]
     cut = count // 16 * FIRST // 26 * 16
+    parity = (lax.axis_index("grp") % 2).astype(jnp.int32).reshape(1)
     even = shifted_half(text, 1, 0)
-    image_next = shifted(image, "grp", -1)
+    held = fetch(image, 0, count, [])
+    image_next = shifted(held, "grp", -1)
 
     own = jax.nn.sigmoid(dot_nt(image, text) * scale + bias)
     column = lax.broadcasted_iota(jnp.int32, own.shape, 1)
     own = (own - (column == target[0][:, None]).astype(jnp.float32)).astype(jnp.bfloat16)
-    odd = shifted_half(fetch(text, 0, count, [own]), 1, 1)
+    odd = shifted_half(fetch(text, 0, count, [held]), 1, 1)
     image_grad = dot_nn(own, text)
     text_grad = dot_tn(own, image)
 
     even = pass_on(even, [image_grad, text_grad], WAIT)
-    image_next = pass_on(image_next, [even])
+    image_next = pass_on(image_next, [even], WAIT)
     odd = pass_on(odd, [image_next])
-    sent0, part0, own0, next0 = chunk(factor, shift, image, image_next, [even, odd], 0, cut, [])
+    sent0, part0, own0, next0 = chunk(parity, factor, shift, image, image_next, [even, odd], 0, cut, [])
     back0 = shifted(sent0, "blk", -1)
-
-    image_next = pass_on(image_next, [sent0])
-    sent1, part1, own1, next1 = chunk(factor, shift, image, image_next, [even, odd], cut, count, [])
+    image_next = pass_on(image_next, [sent0], WAIT)
+    sent1, part1, own1, next1 = chunk(parity, factor, shift, image, image_next, [even, odd], cut, count, [])
+    back1 = shifted(sent1, "blk", -1)
+    image_next = pass_on(image_next, [sent1], WAIT)
     next_own = jax.nn.sigmoid(dot_nt(image_next, text) * scale + bias).astype(jnp.bfloat16)
-    text_grad = scale * (text_grad + dot_tn(next_own, image_next))
     image_sent = dot_nn(next_own, text) + dot_tn(next0, part0)
     image_sent = (scale * (image_sent + dot_tn(next1, part1))).astype(jnp.bfloat16)
     image_back = shifted(image_sent, "grp", 1)
-    back1 = shifted(sent1, "blk", -1)
-    result, mark = add_rows(text_grad, [(0, [back0])], None, [], mark=True)
-    own0, own1 = pass_on(own0, [mark]), pass_on(own1, [mark])
+    text_grad = scale * (text_grad + dot_tn(next_own, image_next))
     image_grad = image_grad + dot_tn(own0, part0)
     image_grad = scale * (image_grad + dot_tn(own1, part1))
-    image_grad, mark = add_rows(image_grad, [(0, [image_back])], None, [], mark=True)
-    result = add_rows(text_grad, [(cut, [back1])], result, [mark])
+
+    result = add_rows(text_grad, [(0, [back0])], None, [])
+    result, mark = add_rows(text_grad, [(cut, [back1])], result, [], mark=True, flops=2 * WAIT)
+    image_grad = add_rows(image_grad, [(0, [image_back])], None, [mark])
     return image_grad, result
 
 

time: 54.4 us -> 64 us (1.18); the launches traced: 54.2 us -> 63 us
  waiting for transfers between devices: 21.7 us -> 8.25 us
  starting transfers between devices: 16.2 us -> 25.5 us
  local copies, waits for them, and re-layouts: 0.01 us -> 6.34 us
  Pallas kernels: 5.91 us -> 11.2 us
  matrix products: 8.18 us -> 9.54 us
    ppermute x2, waiting for transfers between devices: 11.6 us -> 0.01 us  [shifted_half(): return lax.ppermute(shard, ('blk', 'grp'), pairs)]
    ppermute x2, starting transfers between devices: 5.7 us -> 13.8 us  [shifted_half(): return lax.ppermute(shard, ('blk', 'grp'), pairs)]
    unnamed x4 -> x16, local copies, waits for them, and re-layouts: 0.01 us -> 6.34 us
    pallas_call x2, Pallas kernels: 2.91 us -> 6.12 us  [chunk(): pl.pallas_call(functools.partial(chunk_kernel, lo), out_shape=(text, text...]
    pallas_call x1 -> x2, Pallas kernels: 0.29 us -> 2.43 us  [fetch(): pl.pallas_call(kernel, out_shape=jax.ShapeDtypeStruct((hi - lo, array.sha...]
    ppermute x4, waiting for transfers between devices: 10.1 us -> 8.24 us  [shifted(): lax.ppermute(shard, axis, [(i, (i + by) % devices) for i in range(devices)])]
    dot_general x6, matrix products: 3.49 us -> 5.15 us  [dot_tn(): lax.dot_general(a, b, (((0,), (0,)), ((), ())), preferred_element_type=jn...]
    dot_general x2, matrix products: 3.29 us -> 1.71 us  [dot_nt(): lax.dot_general(a, b, (((1,), (1,)), ((), ())), preferred_element_type=jn...]
  transfers between devices with their start and end apart: 6 -> 6, of which waited for: 3 -> 2; matrix products, arithmetic and copies ran while one was open for 15% -> 15% of each run, Pallas kernels for 7% -> 12%
where the time goes in v14:
time: 64 us; the launch traced here: 63 us
  starting transfers between devices  25.5 us (40%)
  Pallas kernels  11.2 us (18%)
  matrix products  9.54 us (15%)
  waiting for transfers between devices  8.25 us (13%)
  local copies, waits for them, and re-layouts  6.34 us (10%)
  between operations  2.14 us (3%)
    ppermute x2, starting transfers between devices, shifted_half(): return lax.ppermute(shard, ('blk', 'grp'), pairs)  13.8 us
    ppermute x4, starting transfers between devices, shifted(): lax.ppermute(shard, axis, [(i, (i + by) % devices) for i in range(devices)])  11.7 us
    ppermute x4, waiting for transfers between devices, shifted(): lax.ppermute(shard, axis, [(i, (i + by) % devices) for i in range(devices)])  8.24 us
    unnamed x16, local copies, waits for them, and re-layouts  6.34 us
    pallas_call x2, Pallas kernels, chunk(): pl.pallas_call(functools.partial(chunk_kernel, lo), out_shape=(text, text...  6.12 us
    dot_general x6, matrix products, dot_tn(): lax.dot_general(a, b, (((0,), (0,)), ((), ())), preferred_element_type=jn...  5.15 us
    pallas_call x3, Pallas kernels, add_rows(): pl.pallas_call(kernel, out_shape=(out, jax.ShapeDtypeStruct((8, 128), jnp...  2.69 us
    dot_general x2, matrix products, dot_nn(): return jnp.dot(a, b, preferred_element_type=jnp.float32)  2.67 us
  transfers between devices with their start and end apart: 6, of which 2 were waited for; matrix products, arithmetic and copies ran while one was open for 15% of the time, Pallas kernels for 12%

profile of v14, /device:TPU:0, one launch (start us, length us, event | category | flops | bytes accessed | tf_op | source)
XLA Modules:
  0.0 63.0 jit_solution(8002080191021433177)
XLA Ops:
  0.6 5.0 %collective-permute-start.1 = (bf16[416,1152]{1,0:T(8,128)(2,1)}, bf16[416,1152]{1,0:T(8,128)(2,1)}, u32[]{:S(2)}, u32[]{:S(2)}) collective-permute-start(bf16[416,1152]{1,0:T(8,128)(2,1)} %array_ref.3), channel_id=1, source_target_pairs={{0,4},{1,1},{2,6},{3,3},{4,8},{5,5},{6,10},{7,7},{8,12},{9,9},{10,... | collective-permute-start | bytes 2875400 | tf_op jit(solution)/shard_map/ppermute | solution.py:41
  5.6 0.0 copy-start.1
  5.6 1.2 %copy-done.1 = bf16[416,1152]{1,0:T(8,128)(2,1)S(1)} copy-done((bf16[416,1152]{1,0:T(8,128)(2,1)S(1)}, bf16[416,1152]{1,0:T(8,128)(2,1)}, u32[]{:S(2)}) %copy-start.1) | copy-done | bytes 958488
  6.8 1.2 %fetch.2.refs_0_ = bf16[416,1152]{1,0:T(8,128)(2,1)} custom-call(bf16[416,1152]{1,0:T(8,128)(2,1)S(1)} %copy-done.1), custom_call_target="tpu_custom_call" | custom-call | tf_op jit(solution)/shard_map/fetch/pallas_call | solution.py:51
  8.0 0.0 copy-start.2
  8.1 6.4 %collective-permute-start = (bf16[416,1152]{1,0:T(8,128)(2,1)}, bf16[416,1152]{1,0:T(8,128)(2,1)S(1)}, u32[]{:S(2)}, u32[]{:S(2)}) collective-permute-start(bf16[416,1152]{1,0:T(8,128)(2,1)} %fetch.2.refs_0_), channel_id=1, source_target_pairs={{0,3},{1,0},{2,1},{3,2},{4,7},{5,4},{6,5},{7,6},{8,11},{9,8},{10,9... | collective-permute-start | bytes 2875400 | tf_op jit(solution)/shard_map/ppermute | solution.py:21
  14.5 1.2 %fetch.3 = bf16[416,1152]{1,0:T(8,128)(2,1)} custom-call(bf16[416,1152]{1,0:T(8,128)(2,1)S(1)} %copy-done, bf16[416,1152]{1,0:T(8,128)(2,1)} %fetch.2.refs_0_), custom_call_target="tpu_custom_call" | custom-call | tf_op jit(solution)/shard_map/fetch/pallas_call | solution.py:51
  15.7 8.9 %collective-permute-start.2 = (bf16[416,1152]{1,0:T(8,128)(2,1)}, bf16[416,1152]{1,0:T(8,128)(2,1)}, u32[]{:S(2)}, u32[]{:S(2)}) collective-permute-start(bf16[416,1152]{1,0:T(8,128)(2,1)} %fetch.3), channel_id=1, source_target_pairs={{0,0},{1,5},{2,2},{3,7},{4,4},{5,9},{6,6},{7,11},{8,8},{9,13},{10,... | collective-permute-start | bytes 2875400 | tf_op jit(solution)/shard_map/ppermute | solution.py:41
  25.9 0.9 %fusion.18 = bf16[416,416]{1,0:T(8,128)(2,1)S(1)} fusion(bf16[416,1152]{1,0:T(8,128)(2,1)S(1)} %copy-done.2, bf16[416,1152]{1,0:T(8,128)(2,1)S(1)} %copy-done, s32[416]{0:T(512)S(1)} %bitcast.31, f32[]{:T(128)} %bitcast.29, f32[]{:T(128)} %bitcast.25), kind=kOutput, calls=%fused_computation.23 | convolution fusion | flops 400278528 | bytes 2264712 | tf_op jit(solution)/shard_map/dot_general | solution.py:25
  26.8 2.0 %fusion.20.refs_2_ = f32[416,1152]{1,0:T(8,128)} fusion(bf16[416,416]{1,0:T(8,128)(2,1)S(1)} %fusion.18, bf16[416,1152]{1,0:T(8,128)(2,1)S(1)} %copy-done.2), kind=kOutput, calls=%fused_computation.26 | convolution fusion | flops 398721024 | bytes 3221504 | tf_op jit(solution)/shard_map/dot_general | solution.py:29
  28.8 2.0 %fusion.19.refs_1_ = f32[416,1152]{1,0:T(8,128)} fusion(bf16[416,416]{1,0:T(8,128)(2,1)S(1)} %fusion.18, bf16[416,1152]{1,0:T(8,128)(2,1)S(1)} %copy-done), kind=kOutput, calls=%fused_computation.25 | convolution fusion | flops 398721024 | bytes 3221504 | tf_op jit(solution)/shard_map/dot_general | solution.py:33
  30.8 1.5 %copy-done.3 = f32[416,1152]{1,0:T(8,128)S(1)} copy-done((f32[416,1152]{1,0:T(8,128)S(1)}, f32[416,1152]{1,0:T(8,128)}, u32[]{:S(2)}) %copy-start.3) | copy-done | bytes 1916952
  32.3 1.5 %copy-done.5 = f32[416,1152]{1,0:T(8,128)S(1)} copy-done((f32[416,1152]{1,0:T(8,128)S(1)}, f32[416,1152]{1,0:T(8,128)}, u32[]{:S(2)}) %copy-start.5) | copy-done | bytes 1916952
  33.9 2.7 %chunk.2 = (bf16[128,1152]{1,0:T(8,128)(2,1)S(1)}, bf16[128,1152]{1,0:T(8,128)(2,1)S(1)}, bf16[128,416]{1,0:T(8,128)(2,1)S(1)}, bf16[128,416]{1,0:T(8,128)(2,1)S(1)}) custom-call(s32[1]{0:T(128)} %bitcast.3.parity_ref, f32[1]{0:T(128)} %copy.19.scale_ref, f32[1]{0:T(128)} %copy.20.bias_ref, bf16[416,1152]{1,0:T(8,128)(2,1)S(1)} %copy-done.2, ...), custom_call_target="tpu_custom_call" | custom-call | flops 490733568 | bytes 3096576 | tf_op jit(solution)/shard_map/chunk/pallas_call | solution.py:104
  36.6 4.6 %collective-permute-start.5 = (bf16[128,1152]{1,0:T(8,128)(2,1)S(1)}, bf16[128,1152]{1,0:T(8,128)(2,1)S(1)}, u32[]{:S(2)}, u32[]{:S(2)}) collective-permute-start(bf16[128,1152]{1,0:T(8,128)(2,1)S(1)} %get-tuple-element.14.refs_1_), channel_id=1, source_target_pairs={{0,28},{4,0},{8,4},{12,8},{16,12},{20,16},{24,20},{28,24},{1,29},{... | collective-permute-start | bytes 884744 | tf_op jit(solution)/shard_map/ppermute | solution.py:21
  41.2 3.4 %chunk.3 = (bf16[288,1152]{1,0:T(8,128)(2,1)S(1)}, bf16[288,1152]{1,0:T(8,128)(2,1)S(1)}, bf16[288,416]{1,0:T(8,128)(2,1)S(1)}, bf16[288,416]{1,0:T(8,128)(2,1)S(1)}) custom-call(s32[1]{0:T(128)} %bitcast.3.parity_ref, f32[1]{0:T(128)} %copy.19.scale_ref, f32[1]{0:T(128)} %copy.20.bias_ref, bf16[416,1152]{1,0:T(8,128)(2,1)S(1)} %copy-done.2, ...), custom_call_target="tpu_custom_call" | custom-call | flops 1104150528 | bytes 4571136 | tf_op jit(solution)/shard_map/chunk/pallas_call | solution.py:104
  44.6 0.6 collective-permute-start.4
  45.2 0.8 %fusion.17 = bf16[416,416]{1,0:T(8,128)(2,1)S(1)} fusion(bf16[416,1152]{1,0:T(8,128)(2,1)S(1)} %pass_on.9, bf16[416,1152]{1,0:T(8,128)(2,1)S(1)} %copy-done, f32[]{:T(128)} %bitcast.30, f32[]{:T(128)} %bitcast.28), kind=kOutput, calls=%fused_computation.22 | convolution fusion | flops 399759360 | bytes 2263048 | tf_op jit(solution)/shard_map/dot_general | solution.py:25
  46.0 0.7 %fusion.22 = f32[416,1152]{1,0:T(8,128)S(1)} fusion(bf16[416,416]{1,0:T(8,128)(2,1)S(1)} %fusion.17, bf16[416,1152]{1,0:T(8,128)(2,1)S(1)} %copy-done), kind=kOutput, calls=%fused_computation.28 | convolution fusion | flops 398721024 | bytes 3221504 | tf_op jit(solution)/shard_map/dot_general | solution.py:33
  46.8 0.7 %fusion.21 = f32[416,1152]{1,0:T(8,128)S(1)} fusion(bf16[288,416]{1,0:T(8,128)(2,1)S(1)} %get-tuple-element.15, bf16[288,1152]{1,0:T(8,128)(2,1)S(1)} %get-tuple-element.16), kind=kOutput, calls=%fused_computation.27 | convolution fusion | flops 276037632 | bytes 2820096 | tf_op jit(solution)/shard_map/dot_general | solution.py:29
  47.5 0.7 %fusion.23 = f32[416,1152]{1,0:T(8,128)S(1)} fusion(bf16[288,416]{1,0:T(8,128)(2,1)S(1)} %get-tuple-element.19, bf16[288,1152]{1,0:T(8,128)(2,1)S(1)} %get-tuple-element.16), kind=kOutput, calls=%fused_computation.29 | convolution fusion | flops 276037632 | bytes 2820096 | tf_op jit(solution)/shard_map/dot_general | solution.py:29
  48.3 0.4 fusion.5
  48.7 0.1 collective-permute-start.3
  48.8 1.0 %copy-done.4 = f32[416,1152]{1,0:T(8,128)S(1)} copy-done((f32[416,1152]{1,0:T(8,128)S(1)}, f32[416,1152]{1,0:T(8,128)}, u32[]{:S(2)}) %copy-start.4) | copy-done | bytes 1916952
  49.8 0.4 fusion.4.total_ref
  50.2 1.1 %copy-done.6 = f32[416,1152]{1,0:T(8,128)S(1)} copy-done((f32[416,1152]{1,0:T(8,128)S(1)}, f32[416,1152]{1,0:T(8,128)}, u32[]{:S(2)}) %copy-start.6) | copy-done | bytes 1916952
  51.3 0.8 %fusion.total_ref = f32[416,1152]{1,0:T(8,128)S(1)} fusion(f32[416,1152]{1,0:T(8,128)S(1)} %copy-done.6, bf16[416,416]{1,0:T(8,128)(2,1)S(1)} %fusion.17, bf16[416,1152]{1,0:T(8,128)(2,1)S(1)} %pass_on.9, f32[]{:T(128)} %bitcast.26), kind=kOutput, calls=%fused_computation.1 | convolution fusion | flops 399679488 | bytes 5138436 | tf_op jit(solution)/shard_map/dot_general | solution.py:29
  52.1 0.8 %add_rows.3.refs_1_ = bf16[416,1152]{1,0:T(8,128)(2,1)} custom-call(f32[416,1152]{1,0:T(8,128)S(1)} %fusion.total_ref, bf16[128,1152]{1,0:T(8,128)(2,1)S(1)} %collective-permute-done.5.refs_0_), custom_call_target="tpu_custom_call" | custom-call | tf_op jit(solution)/shard_map/add_rows/pallas_call | solution.py:155
  52.9 6.1 %collective-permute-done.4.refs_0_ = bf16[288,1152]{1,0:T(8,128)(2,1)S(1)} collective-permute-done((bf16[288,1152]{1,0:T(8,128)(2,1)S(1)}, bf16[288,1152]{1,0:T(8,128)(2,1)S(1)}, u32[]{:S(2)}, u32[]{:S(2)}) %collective-permute-start.4) | collective-permute-done | bytes 663584 | tf_op jit(solution)/shard_map/ppermute | solution.py:21
  58.9 0.9 %add_rows.4 = (bf16[416,1152]{1,0:T(8,128)(2,1)}, f32[8,128]{1,0:T(8,128)S(1)}) custom-call(f32[416,1152]{1,0:T(8,128)S(1)} %fusion.total_ref, bf16[288,1152]{1,0:T(8,128)(2,1)S(1)} %collective-permute-done.4.refs_0_, bf16[416,1152]{1,0:T(8,128)(2,1)} %add_rows.3.refs_1_), custom_call_target="tpu_custom_call", output_to_operand_aliasing={{0}: (2, {})} | custom-call | flops 20000000000 | tf_op jit(solution)/shard_map/add_rows/pallas_call | solution.py:155
  59.9 2.2 %collective-permute-done.3.refs_0_ = bf16[416,1152]{1,0:T(8,128)(2,1)S(1)} collective-permute-done((bf16[416,1152]{1,0:T(8,128)(2,1)S(1)}, bf16[416,1152]{1,0:T(8,128)(2,1)S(1)}, u32[]{:S(2)}, u32[]{:S(2)}) %collective-permute-start.3) | collective-permute-done | bytes 958496 | tf_op jit(solution)/shard_map/ppermute | solution.py:21
  62.0 1.0 %add_rows.5 = bf16[416,1152]{1,0:T(8,128)(2,1)} custom-call(f32[416,1152]{1,0:T(8,128)S(1)} %fusion.4.total_ref, bf16[416,1152]{1,0:T(8,128)(2,1)S(1)} %collective-permute-done.3.refs_0_, f32[8,128]{1,0:T(8,128)S(1)} %get-tuple-element.20.refs_1_), custom_call_target="tpu_custom_call" | custom-call | tf_op jit(solution)/shard_map/add_rows/pallas_call | solution.py:155
  (18 shorter events, 0.0 us)
Async XLA Ops:
  0.6 13.9 %copy-start = (bf16[416,1152]{1,0:T(8,128)(2,1)S(1)}, bf16[416,1152]{1,0:T(8,128)(2,1)}, u32[]{:S(2)}) copy-start(bf16[416,1152]{1,0:T(8,128)(2,1)} %array_ref.3) | copy-start | bytes 2875396
  0.6 30.2 %collective-permute-start.1 = (bf16[416,1152]{1,0:T(8,128)(2,1)}, bf16[416,1152]{1,0:T(8,128)(2,1)}, u32[]{:S(2)}, u32[]{:S(2)}) collective-permute-start(bf16[416,1152]{1,0:T(8,128)(2,1)} %array_ref.3), channel_id=1, source_target_pairs={{0,4},{1,1},{2,6},{3,3},{4,8},{5,5},{6,10},{7,7},{8,12},{9,9},{10,... | collective-permute-start | bytes 2875400 | tf_op jit(solution)/shard_map/ppermute | solution.py:41
  5.6 1.2 %copy-start.1 = (bf16[416,1152]{1,0:T(8,128)(2,1)S(1)}, bf16[416,1152]{1,0:T(8,128)(2,1)}, u32[]{:S(2)}) copy-start(bf16[416,1152]{1,0:T(8,128)(2,1)} %image_ref.3) | copy-start | bytes 2875396
  8.0 17.9 %copy-start.2 = (bf16[416,1152]{1,0:T(8,128)(2,1)S(1)}, bf16[416,1152]{1,0:T(8,128)(2,1)}, u32[]{:S(2)}) copy-start(bf16[416,1152]{1,0:T(8,128)(2,1)} %image_ref.3) | copy-start | bytes 2875396
  8.1 17.9 %copy-start.7 = (s32[1,416]{1,0:T(1,128)S(1)}, s32[1,416]{1,0:T(1,128)}, u32[]{:S(2)}) copy-start(s32[1,416]{1,0:T(1,128)} %param.7) | copy-start | bytes 4996
  8.1 25.8 %collective-permute-start = (bf16[416,1152]{1,0:T(8,128)(2,1)}, bf16[416,1152]{1,0:T(8,128)(2,1)S(1)}, u32[]{:S(2)}, u32[]{:S(2)}) collective-permute-start(bf16[416,1152]{1,0:T(8,128)(2,1)} %fetch.2.refs_0_), channel_id=1, source_target_pairs={{0,3},{1,0},{2,1},{3,2},{4,7},{5,4},{6,5},{7,6},{8,11},{9,8},{10,9... | collective-permute-start | bytes 2875400 | tf_op jit(solution)/shard_map/ppermute | solution.py:21
  15.7 18.1 %collective-permute-start.2 = (bf16[416,1152]{1,0:T(8,128)(2,1)}, bf16[416,1152]{1,0:T(8,128)(2,1)}, u32[]{:S(2)}, u32[]{:S(2)}) collective-permute-start(bf16[416,1152]{1,0:T(8,128)(2,1)} %fetch.3), channel_id=1, source_target_pairs={{0,0},{1,5},{2,2},{3,7},{4,4},{5,9},{6,6},{7,11},{8,8},{9,13},{10,... | collective-permute-start | bytes 2875400 | tf_op jit(solution)/shard_map/ppermute | solution.py:41
  30.8 1.5 %copy-start.3 = (f32[416,1152]{1,0:T(8,128)S(1)}, f32[416,1152]{1,0:T(8,128)}, u32[]{:S(2)}) copy-start(f32[416,1152]{1,0:T(8,128)} %fusion.19.refs_1_) | copy-start | bytes 5750788
  32.3 1.5 %copy-start.5 = (f32[416,1152]{1,0:T(8,128)S(1)}, f32[416,1152]{1,0:T(8,128)}, u32[]{:S(2)}) copy-start(f32[416,1152]{1,0:T(8,128)} %fusion.20.refs_2_) | copy-start | bytes 5750788
  36.6 15.5 %collective-permute-start.5 = (bf16[128,1152]{1,0:T(8,128)(2,1)S(1)}, bf16[128,1152]{1,0:T(8,128)(2,1)S(1)}, u32[]{:S(2)}, u32[]{:S(2)}) collective-permute-start(bf16[128,1152]{1,0:T(8,128)(2,1)S(1)} %get-tuple-element.14.refs_1_), channel_id=1, source_target_pairs={{0,28},{4,0},{8,4},{12,8},{16,12},{20,16},{24,20},{28,24},{1,29},{... | collective-permute-start | bytes 884744 | tf_op jit(solution)/shard_map/ppermute | solution.py:21
  44.6 14.3 %collective-permute-start.4 = (bf16[288,1152]{1,0:T(8,128)(2,1)S(1)}, bf16[288,1152]{1,0:T(8,128)(2,1)S(1)}, u32[]{:S(2)}, u32[]{:S(2)}) collective-permute-start(bf16[288,1152]{1,0:T(8,128)(2,1)S(1)} %get-tuple-element.17.refs_1_), channel_id=1, source_target_pairs={{0,28},{4,0},{8,4},{12,8},{16,12},{20,16},{24,20},{28,24},{1,29},{... | collective-permute-start | bytes 1990664 | tf_op jit(solution)/shard_map/ppermute | solution.py:21
  48.2 1.5 %copy-start.4 = (f32[416,1152]{1,0:T(8,128)S(1)}, f32[416,1152]{1,0:T(8,128)}, u32[]{:S(2)}) copy-start(f32[416,1152]{1,0:T(8,128)} %fusion.19.refs_1_) | copy-start | bytes 5750788
  48.7 13.3 %collective-permute-start.3 = (bf16[416,1152]{1,0:T(8,128)(2,1)S(1)}, bf16[416,1152]{1,0:T(8,128)(2,1)S(1)}, u32[]{:S(2)}, u32[]{:S(2)}) collective-permute-start(bf16[416,1152]{1,0:T(8,128)(2,1)S(1)} %fusion.5), channel_id=1, source_target_pairs={{0,1},{1,2},{2,3},{3,0},{4,5},{5,6},{6,7},{7,4},{8,9},{9,10},{10,1... | collective-permute-start | bytes 2875400 | tf_op jit(solution)/shard_map/ppermute | solution.py:21
  49.8 1.5 %copy-start.6 = (f32[416,1152]{1,0:T(8,128)S(1)}, f32[416,1152]{1,0:T(8,128)}, u32[]{:S(2)}) copy-start(f32[416,1152]{1,0:T(8,128)} %fusion.20.refs_2_) | copy-start | bytes 5750788

commit v15 on v13

--- a/solution.py
+++ b/solution.py
@@ -8,7 +8,7 @@
 from jax.sharding import PartitionSpec as P
 
 MIB = 2**20
-ENDS = (8, 23)
+ENDS = (8, 22)
 SMEM = pl.BlockSpec(memory_space=pltpu.SMEM)
 VMEM = pl.BlockSpec(memory_space=pltpu.VMEM)
 HBM = pl.BlockSpec(memory_space=pltpu.HBM)

time: 50.5 us -> 53.5 us (1.059); the launches traced: 50.3 us -> 52.5 us
  waiting for transfers between devices: 24.1 us -> 27.4 us
  starting transfers between devices: 8.93 us -> 7.5 us
    ppermute x7, waiting for transfers between devices: 24.1 us -> 27.4 us  [shifted(): lax.ppermute(shard, axis, [(i, (i + by) % devices) for i in range(devices)])]
    ppermute x7, starting transfers between devices: 8.93 us -> 7.5 us  [shifted(): lax.ppermute(shard, axis, [(i, (i + by) % devices) for i in range(devices)])]
  transfers between devices with their start and end apart: 7 -> 7, of which waited for: 5 -> 6; matrix products, arithmetic and copies ran while one was open for 14% -> 13% of each run, Pallas kernels for 10% -> 10%
where the time goes in v15:
time: 53.5 us; the launch traced here: 52.5 us
  waiting for transfers between devices  27.4 us (51%)
  starting transfers between devices  7.5 us (14%)
  matrix products  6.94 us (13%)
  Pallas kernels  6.35 us (12%)
  local copies, waits for them, and re-layouts  2.2 us (4%)
  between operations  2.13 us (4%)
    ppermute x7, waiting for transfers between devices, shifted(): lax.ppermute(shard, axis, [(i, (i + by) % devices) for i in range(devices)])  27.4 us
    ppermute x7, starting transfers between devices, shifted(): lax.ppermute(shard, axis, [(i, (i + by) % devices) for i in range(devices)])  7.5 us
    dot_general x6, matrix products, dot_tn(): lax.dot_general(a, b, (((0,), (0,)), ((), ())), preferred_element_type=jn...  3.81 us
    pallas_call x2, Pallas kernels, chunk(): pl.pallas_call(functools.partial(chunk_kernel, len(pieces)), out_shape=(t...  3.09 us
    pallas_call x3, Pallas kernels, add_rows(): pl.pallas_call(kernel, out_shape=(out, jax.ShapeDtypeStruct((8, 128), jnp...  2.68 us
    dot_general x2, matrix products, dot_nt(): lax.dot_general(a, b, (((1,), (1,)), ((), ())), preferred_element_type=jn...  1.72 us
    dot_general x2, matrix products, dot_nn(): return jnp.dot(a, b, preferred_element_type=jnp.float32)  1.4 us
    unnamed x8, local copies, waits for them, and re-layouts  1.2 us
  transfers between devices with their start and end apart: 7, of which 6 were waited for; matrix products, arithmetic and copies ran while one was open for 13% of the time, Pallas kernels for 10%

profile of v15, /device:TPU:0, one launch (start us, length us, event | category | flops | bytes accessed | tf_op | source)
XLA Modules:
  0.0 52.5 jit_solution(3958804432762363319)
XLA Ops:
  0.6 1.0 %slice.3.refs_0_ = bf16[128,1152]{1,0:T(8,128)(2,1)S(1)} slice(bf16[416,1152]{1,0:T(8,128)(2,1)} %array_ref.5), slice={[0:128], [0:1152]} | slice | bytes 589824 | tf_op jit(solution)/shard_map/slice | solution.py:150
  1.6 3.0 %collective-permute-start = (bf16[128,1152]{1,0:T(8,128)(2,1)S(1)}, bf16[128,1152]{1,0:T(8,128)(2,1)S(1)}, u32[]{:S(2)}, u32[]{:S(2)}) collective-permute-start(bf16[128,1152]{1,0:T(8,128)(2,1)S(1)} %slice.3.refs_0_), channel_id=1, source_target_pairs={{0,4},{4,8},{8,12},{12,16},{16,20},{20,24},{24,28},{28,0},{1,5},{5... | collective-permute-start | bytes 884744 | tf_op jit(solution)/shard_map/ppermute | solution.py:20
  4.6 0.7 %collective-permute-start.1 = (bf16[416,1152]{1,0:T(8,128)(2,1)}, bf16[416,1152]{1,0:T(8,128)(2,1)S(1)}, u32[]{:S(2)}, u32[]{:S(2)}) collective-permute-start(bf16[416,1152]{1,0:T(8,128)(2,1)} %image_ref.3), channel_id=1, source_target_pairs={{0,3},{1,0},{2,1},{3,2},{4,7},{5,4},{6,5},{7,6},{8,11},{9,8},{10,9... | collective-permute-start | bytes 2875400 | tf_op jit(solution)/shard_map/ppermute | solution.py:20
  5.3 1.2 %copy-done = bf16[416,1152]{1,0:T(8,128)(2,1)S(1)} copy-done((bf16[416,1152]{1,0:T(8,128)(2,1)S(1)}, bf16[416,1152]{1,0:T(8,128)(2,1)}, u32[]{:S(2)}) %copy-start) | copy-done | bytes 958488
  6.5 0.3 fetch.4
  6.9 1.6 %collective-permute-start.2 = (bf16[224,1152]{1,0:T(8,128)(2,1)S(1)}, bf16[224,1152]{1,0:T(8,128)(2,1)S(1)}, u32[]{:S(2)}, u32[]{:S(2)}) collective-permute-start(bf16[224,1152]{1,0:T(8,128)(2,1)S(1)} %fetch.4), channel_id=1, source_target_pairs={{0,4},{4,8},{8,12},{12,16},{16,20},{20,24},{24,28},{28,0},{1,5},{5... | collective-permute-start | bytes 1548296 | tf_op jit(solution)/shard_map/ppermute | solution.py:20
  9.8 5.7 %collective-permute-done.refs_0_ = bf16[128,1152]{1,0:T(8,128)(2,1)S(1)} collective-permute-done((bf16[128,1152]{1,0:T(8,128)(2,1)S(1)}, bf16[128,1152]{1,0:T(8,128)(2,1)S(1)}, u32[]{:S(2)}, u32[]{:S(2)}) %collective-permute-start) | collective-permute-done | bytes 294944 | tf_op jit(solution)/shard_map/ppermute | solution.py:20
  15.5 0.9 %subtract_convert_fusion.refs_0_ = bf16[416,416]{1,0:T(8,128)(2,1)S(1)} fusion(s32[416]{0:T(512)S(1)} %bitcast.30, f32[]{:T(128)} %bitcast.28, bf16[416,1152]{1,0:T(8,128)(2,1)S(1)} %copy-done.2, bf16[416,1152]{1,0:T(8,128)(2,1)S(1)} %copy-done.1, f32[]{:T(128)} %bitcast.24), kind=kOutput, calls=%fused_computation.22 | convolution fusion | flops 400278528 | bytes 2264712 | tf_op jit(solution)/shard_map/dot_general | solution.py:24
  16.4 0.2 fetch.5
  16.6 0.1 collective-permute-start.3
  16.7 0.7 %fusion.17.refs_2_ = f32[416,1152]{1,0:T(8,128)S(1)} fusion(bf16[416,416]{1,0:T(8,128)(2,1)S(1)} %subtract_convert_fusion.refs_0_, bf16[416,1152]{1,0:T(8,128)(2,1)S(1)} %copy-done.2), kind=kOutput, calls=%fused_computation.25 | convolution fusion | flops 398721024 | bytes 3221504 | tf_op jit(solution)/shard_map/dot_general | solution.py:28
  17.5 0.7 %fusion.16.refs_1_ = f32[416,1152]{1,0:T(8,128)S(1)} fusion(bf16[416,416]{1,0:T(8,128)(2,1)S(1)} %subtract_convert_fusion.refs_0_, bf16[416,1152]{1,0:T(8,128)(2,1)S(1)} %copy-done.1), kind=kOutput, calls=%fused_computation.24 | convolution fusion | flops 398721024 | bytes 3221504 | tf_op jit(solution)/shard_map/dot_general | solution.py:32
  18.2 0.8 %fusion.15 = bf16[416,416]{1,0:T(8,128)(2,1)S(1)} fusion(bf16[416,1152]{1,0:T(8,128)(2,1)S(1)} %pass_on.4.next_ref, bf16[416,1152]{1,0:T(8,128)(2,1)S(1)} %copy-done.1, f32[]{:T(128)} %bitcast.29, f32[]{:T(128)} %bitcast.27), kind=kOutput, calls=%fused_computation.21 | convolution fusion | flops 399759360 | bytes 2263048 | tf_op jit(solution)/shard_map/dot_general | solution.py:24
  19.0 1.2 %chunk.2 = (bf16[128,1152]{1,0:T(8,128)(2,1)S(1)}, bf16[128,1152]{1,0:T(8,128)(2,1)S(1)}, bf16[128,416]{1,0:T(8,128)(2,1)S(1)}, bf16[128,416]{1,0:T(8,128)(2,1)S(1)}) custom-call(f32[1]{0:T(128)} %copy.17.scale_ref, f32[1]{0:T(128)} %copy.18.bias_ref, bf16[416,1152]{1,0:T(8,128)(2,1)S(1)} %copy-done.2, bf16[416,1152]{1,0:T(8,128)(2,1)S(1)} %pass_on.4.next_ref, ...), custom_call_target="tpu_custom_call" | custom-call | flops 490733568 | bytes 2801664 | tf_op jit(solution)/shard_map/chunk/pallas_call | solution.py:95
  20.2 0.7 %fusion.18 = f32[416,1152]{1,0:T(8,128)S(1)} fusion(bf16[416,416]{1,0:T(8,128)(2,1)S(1)} %fusion.15, bf16[416,1152]{1,0:T(8,128)(2,1)S(1)} %copy-done.1), kind=kOutput, calls=%fused_computation.26 | convolution fusion | flops 398721024 | bytes 3221504 | tf_op jit(solution)/shard_map/dot_general | solution.py:32
  21.0 0.4 convolution_add_fusion.1.refs_2_
  21.4 5.1 %collective-permute-done.2.refs_1_.refs_0_ = bf16[224,1152]{1,0:T(8,128)(2,1)S(1)} collective-permute-done((bf16[224,1152]{1,0:T(8,128)(2,1)S(1)}, bf16[224,1152]{1,0:T(8,128)(2,1)S(1)}, u32[]{:S(2)}, u32[]{:S(2)}) %collective-permute-start.2) | collective-permute-done | bytes 516128 | tf_op jit(solution)/shard_map/ppermute | solution.py:20
  26.6 2.1 %collective-permute-start.4 = (bf16[128,1152]{1,0:T(8,128)(2,1)S(1)}, bf16[128,1152]{1,0:T(8,128)(2,1)S(1)}, u32[]{:S(2)}, u32[]{:S(2)}) collective-permute-start(bf16[128,1152]{1,0:T(8,128)(2,1)S(1)} %pass_on.5.refs_2_), channel_id=1, source_target_pairs={{0,28},{4,0},{8,4},{12,8},{16,12},{20,16},{24,20},{28,24},{1,29},{... | collective-permute-start | bytes 884744 | tf_op jit(solution)/shard_map/ppermute | solution.py:20
  28.6 2.8 %collective-permute-done.3.refs_1_ = bf16[64,1152]{1,0:T(8,128)(2,1)S(1)} collective-permute-done((bf16[64,1152]{1,0:T(8,128)(2,1)S(1)}, bf16[64,1152]{1,0:T(8,128)(2,1)S(1)}, u32[]{:S(2)}, u32[]{:S(2)}) %collective-permute-start.3) | collective-permute-done | bytes 147488 | tf_op jit(solution)/shard_map/ppermute | solution.py:20
  31.5 1.9 %chunk.3 = (bf16[288,1152]{1,0:T(8,128)(2,1)S(1)}, bf16[288,1152]{1,0:T(8,128)(2,1)S(1)}, bf16[288,416]{1,0:T(8,128)(2,1)S(1)}, bf16[288,416]{1,0:T(8,128)(2,1)S(1)}) custom-call(f32[1]{0:T(128)} %copy.17.scale_ref, f32[1]{0:T(128)} %copy.18.bias_ref, bf16[416,1152]{1,0:T(8,128)(2,1)S(1)} %copy-done.2, bf16[416,1152]{1,0:T(8,128)(2,1)S(1)} %pass_on.4.next_ref, ...), custom_call_target="tpu_custom_call" | custom-call | flops 1104150528 | bytes 3907584 | tf_op jit(solution)/shard_map/chunk/pallas_call | solution.py:95
  33.3 0.7 %fusion.4.refs_1_ = bf16[416,1152]{1,0:T(8,128)(2,1)S(1)} fusion(f32[416,1152]{1,0:T(8,128)S(1)} %convolution_add_fusion.1.refs_2_, bf16[288,416]{1,0:T(8,128)(2,1)S(1)} %get-tuple-element.21, bf16[288,1152]{1,0:T(8,128)(2,1)S(1)} %get-tuple-element.20, f32[]{:T(128)} %bitcast.25), kind=kOutput, calls=%fused_computation.8 | convolution fusion | flops 277475328 | bytes 3778564 | tf_op jit(solution)/shard_map/dot_general | solution.py:28
  34.1 0.1 collective-permute-start.5
  34.2 0.1 collective-permute-start.6
  34.2 0.7 %fusion.total_ref = f32[416,1152]{1,0:T(8,128)S(1)} fusion(f32[416,1152]{1,0:T(8,128)S(1)} %fusion.17.refs_2_, bf16[416,416]{1,0:T(8,128)(2,1)S(1)} %fusion.15, bf16[416,1152]{1,0:T(8,128)(2,1)S(1)} %pass_on.4.next_ref, f32[]{:T(128)} %bitcast.23), kind=kOutput, calls=%fused_computation.1 | convolution fusion | flops 399679488 | bytes 5138436 | tf_op jit(solution)/shard_map/dot_general | solution.py:28
  35.0 0.2 collective-permute-done.4.back_ref
  35.2 0.8 %add_rows.3 = (bf16[416,1152]{1,0:T(8,128)(2,1)}, f32[8,128]{1,0:T(8,128)S(1)}) custom-call(f32[416,1152]{1,0:T(8,128)S(1)} %fusion.total_ref, bf16[128,1152]{1,0:T(8,128)(2,1)S(1)} %collective-permute-done.4.back_ref), custom_call_target="tpu_custom_call" | custom-call | tf_op jit(solution)/shard_map/add_rows/pallas_call | solution.py:134
  36.0 0.7 %fusion.19 = f32[416,1152]{1,0:T(8,128)S(1)} fusion(bf16[288,416]{1,0:T(8,128)(2,1)S(1)} %pass_on.6, bf16[288,1152]{1,0:T(8,128)(2,1)S(1)} %get-tuple-element.20), kind=kOutput, calls=%fused_computation.27 | convolution fusion | flops 276037632 | bytes 2820096 | tf_op jit(solution)/shard_map/dot_general | solution.py:28
  36.7 0.4 fusion.2.total_ref
  37.2 10.2 %collective-permute-done.5.back_ref = bf16[416,1152]{1,0:T(8,128)(2,1)S(1)} collective-permute-done((bf16[416,1152]{1,0:T(8,128)(2,1)S(1)}, bf16[416,1152]{1,0:T(8,128)(2,1)S(1)}, u32[]{:S(2)}, u32[]{:S(2)}) %collective-permute-start.5) | collective-permute-done | bytes 958496 | tf_op jit(solution)/shard_map/ppermute | solution.py:20
  47.4 1.0 %add_rows.4 = (bf16[416,1152]{1,0:T(8,128)(2,1)}, f32[8,128]{1,0:T(8,128)S(1)}) custom-call(f32[416,1152]{1,0:T(8,128)S(1)} %fusion.2.total_ref, bf16[416,1152]{1,0:T(8,128)(2,1)S(1)} %collective-permute-done.5.back_ref), custom_call_target="tpu_custom_call" | custom-call | tf_op jit(solution)/shard_map/add_rows/pallas_call | solution.py:134
  48.4 3.2 %collective-permute-done.6.back_ref = bf16[288,1152]{1,0:T(8,128)(2,1)S(1)} collective-permute-done((bf16[288,1152]{1,0:T(8,128)(2,1)S(1)}, bf16[288,1152]{1,0:T(8,128)(2,1)S(1)}, u32[]{:S(2)}, u32[]{:S(2)}) %collective-permute-start.6) | collective-permute-done | bytes 663584 | tf_op jit(solution)/shard_map/ppermute | solution.py:20
  51.6 0.9 %add_rows.5 = bf16[416,1152]{1,0:T(8,128)(2,1)} custom-call(f32[416,1152]{1,0:T(8,128)S(1)} %fusion.total_ref, bf16[288,1152]{1,0:T(8,128)(2,1)S(1)} %collective-permute-done.6.back_ref, bf16[416,1152]{1,0:T(8,128)(2,1)} %get-tuple-element.24.refs_0_, f32[8,128]{1,0:T(8,128)S(1)} %get-tuple-element.25.refs_1_), custom_call_target="tpu_custom_call", output_to_operand_aliasing={{}: (2, {})} | custom-call | tf_op jit(solution)/shard_map/add_rows/pallas_call | solution.py:134
  (13 shorter events, 0.0 us)
Async XLA Ops:
  0.6 14.9 %copy-start.3 = (s32[1,416]{1,0:T(1,128)S(1)}, s32[1,416]{1,0:T(1,128)}, u32[]{:S(2)}) copy-start(s32[1,416]{1,0:T(1,128)} %array_ref.3) | copy-start | bytes 4996
  1.6 13.9 %collective-permute-start = (bf16[128,1152]{1,0:T(8,128)(2,1)S(1)}, bf16[128,1152]{1,0:T(8,128)(2,1)S(1)}, u32[]{:S(2)}, u32[]{:S(2)}) collective-permute-start(bf16[128,1152]{1,0:T(8,128)(2,1)S(1)} %slice.3.refs_0_), channel_id=1, source_target_pairs={{0,4},{4,8},{8,12},{12,16},{16,20},{20,24},{24,28},{28,0},{1,5},{5... | collective-permute-start | bytes 884744 | tf_op jit(solution)/shard_map/ppermute | solution.py:20
  4.6 13.5 %collective-permute-start.1 = (bf16[416,1152]{1,0:T(8,128)(2,1)}, bf16[416,1152]{1,0:T(8,128)(2,1)S(1)}, u32[]{:S(2)}, u32[]{:S(2)}) collective-permute-start(bf16[416,1152]{1,0:T(8,128)(2,1)} %image_ref.3), channel_id=1, source_target_pairs={{0,3},{1,0},{2,1},{3,2},{4,7},{5,4},{6,5},{7,6},{8,11},{9,8},{10,9... | collective-permute-start | bytes 2875400 | tf_op jit(solution)/shard_map/ppermute | solution.py:20
  5.3 1.2 %copy-start = (bf16[416,1152]{1,0:T(8,128)(2,1)S(1)}, bf16[416,1152]{1,0:T(8,128)(2,1)}, u32[]{:S(2)}) copy-start(bf16[416,1152]{1,0:T(8,128)(2,1)} %array_ref.5) | copy-start | bytes 2875396
  6.5 9.0 %copy-start.1 = (bf16[416,1152]{1,0:T(8,128)(2,1)S(1)}, bf16[416,1152]{1,0:T(8,128)(2,1)}, u32[]{:S(2)}) copy-start(bf16[416,1152]{1,0:T(8,128)(2,1)} %array_ref.5) | copy-start | bytes 2875396
  6.5 9.0 %copy-start.2 = (bf16[416,1152]{1,0:T(8,128)(2,1)S(1)}, bf16[416,1152]{1,0:T(8,128)(2,1)}, u32[]{:S(2)}) copy-start(bf16[416,1152]{1,0:T(8,128)(2,1)} %image_ref.3) | copy-start | bytes 2875396
  6.9 19.7 %collective-permute-start.2 = (bf16[224,1152]{1,0:T(8,128)(2,1)S(1)}, bf16[224,1152]{1,0:T(8,128)(2,1)S(1)}, u32[]{:S(2)}, u32[]{:S(2)}) collective-permute-start(bf16[224,1152]{1,0:T(8,128)(2,1)S(1)} %fetch.4), channel_id=1, source_target_pairs={{0,4},{4,8},{8,12},{12,16},{16,20},{20,24},{24,28},{28,0},{1,5},{5... | collective-permute-start | bytes 1548296 | tf_op jit(solution)/shard_map/ppermute | solution.py:20
  16.6 14.8 %collective-permute-start.3 = (bf16[64,1152]{1,0:T(8,128)(2,1)S(1)}, bf16[64,1152]{1,0:T(8,128)(2,1)S(1)}, u32[]{:S(2)}, u32[]{:S(2)}) collective-permute-start(bf16[64,1152]{1,0:T(8,128)(2,1)S(1)} %fetch.5), channel_id=1, source_target_pairs={{0,4},{4,8},{8,12},{12,16},{16,20},{20,24},{24,28},{28,0},{1,5},{5... | collective-permute-start | bytes 442376 | tf_op jit(solution)/shard_map/ppermute | solution.py:20
  26.6 8.7 %collective-permute-start.4 = (bf16[128,1152]{1,0:T(8,128)(2,1)S(1)}, bf16[128,1152]{1,0:T(8,128)(2,1)S(1)}, u32[]{:S(2)}, u32[]{:S(2)}) collective-permute-start(bf16[128,1152]{1,0:T(8,128)(2,1)S(1)} %pass_on.5.refs_2_), channel_id=1, source_target_pairs={{0,28},{4,0},{8,4},{12,8},{16,12},{20,16},{24,20},{28,24},{1,29},{... | collective-permute-start | bytes 884744 | tf_op jit(solution)/shard_map/ppermute | solution.py:20
  34.1 13.3 %collective-permute-start.5 = (bf16[416,1152]{1,0:T(8,128)(2,1)S(1)}, bf16[416,1152]{1,0:T(8,128)(2,1)S(1)}, u32[]{:S(2)}, u32[]{:S(2)}) collective-permute-start(bf16[416,1152]{1,0:T(8,128)(2,1)S(1)} %fusion.4.refs_1_), channel_id=1, source_target_pairs={{0,1},{1,2},{2,3},{3,0},{4,5},{5,6},{6,7},{7,4},{8,9},{9,10},{10,1... | collective-permute-start | bytes 2875400 | tf_op jit(solution)/shard_map/ppermute | solution.py:20
  34.2 17.4 %collective-permute-start.6 = (bf16[288,1152]{1,0:T(8,128)(2,1)S(1)}, bf16[288,1152]{1,0:T(8,128)(2,1)S(1)}, u32[]{:S(2)}, u32[]{:S(2)}) collective-permute-start(bf16[288,1152]{1,0:T(8,128)(2,1)S(1)} %pass_on.7), channel_id=1, source_target_pairs={{0,28},{4,0},{8,4},{12,8},{16,12},{20,16},{24,20},{28,24},{1,29},{... | collective-permute-start | bytes 1990664 | tf_op jit(solution)/shard_map/ppermute | solution.py:20

commit v16 on v6

--- a/solution.py
+++ b/solution.py
@@ -31,7 +31,7 @@
 
 def row_cuts(rows):
     tiles = rows // 16
-    cuts = [0, tiles * 6 // 26 * 16, tiles * 16 // 26 * 16, tiles * 20 // 26 * 16, rows]
+    cuts = [0, tiles * 6 // 26 * 16, tiles * 16 // 26 * 16, tiles * 24 // 26 * 16, rows]
     return list(zip(cuts[:-1], cuts[1:]))
 
 

time: 54.9 us -> 50.7 us (0.923)
  waiting for transfers between devices: 28.5 us -> 23.5 us
  starting transfers between devices: 9 us -> 10.1 us
    ppermute x8, waiting for transfers between devices: 28.5 us -> 23.5 us  [shifted(): lax.ppermute(shard, axis, [(i, (i + by) % devices) for i in range(devices)])]
    ppermute x8, starting transfers between devices: 9 us -> 10.1 us  [shifted(): lax.ppermute(shard, axis, [(i, (i + by) % devices) for i in range(devices)])]
  transfers between devices with their start and end apart: 8 -> 8, of which waited for: 6 -> 5; matrix products, arithmetic and copies ran while one was open for 12% -> 13% of each run, Pallas kernels for 10% -> 10%
where the time goes in v16:
time: 50.7 us; the launch traced here: 50.5 us
  waiting for transfers between devices  23.5 us (46%)
  starting transfers between devices  10.1 us (20%)
  matrix products  6.58 us (13%)
  Pallas kernels  5.95 us (12%)
  local copies, waits for them, and re-layouts  2.16 us (4%)
  between operations  2.14 us (4%)
    ppermute x8, waiting for transfers between devices, shifted(): lax.ppermute(shard, axis, [(i, (i + by) % devices) for i in range(devices)])  23.5 us
    ppermute x8, starting transfers between devices, shifted(): lax.ppermute(shard, axis, [(i, (i + by) % devices) for i in range(devices)])  10.1 us
    dot_general x6, matrix products, dot_tn(): lax.dot_general(a, b, (((0,), (0,)), ((), ())), preferred_element_type=jn...  3.45 us
    pallas_call x2, Pallas kernels, chunk(): pl.pallas_call(chunk_kernel, out_shape=(text, text, tile, tile), in_specs...  2.89 us
    pallas_call x3, Pallas kernels, add_rows(): pl.pallas_call(kernel, out_shape=(out, jax.ShapeDtypeStruct((8, 128), jnp...  2.71 us
    dot_general x2, matrix products, dot_nt(): lax.dot_general(a, b, (((1,), (1,)), ((), ())), preferred_element_type=jn...  1.72 us
    dot_general x2, matrix products, dot_nn(): return jnp.dot(a, b, preferred_element_type=jnp.float32)  1.4 us
    unnamed x8, local copies, waits for them, and re-layouts  1.2 us
  transfers between devices with their start and end apart: 8, of which 5 were waited for; matrix products, arithmetic and copies ran while one was open for 13% of the time, Pallas kernels for 10%

profile of v16, /device:TPU:0, one launch (start us, length us, event | category | flops | bytes accessed | tf_op | source)
XLA Modules:
  0.0 50.5 jit_solution(9918823211345871892)
XLA Ops:
  0.6 1.0 %slice.3.refs_0_ = bf16[96,1152]{1,0:T(8,128)(2,1)S(1)} slice(bf16[416,1152]{1,0:T(8,128)(2,1)} %array_ref.7), slice={[0:96], [0:1152]} | slice | bytes 442368 | tf_op jit(solution)/shard_map/slice | solution.py:146
  1.6 3.0 %collective-permute-start = (bf16[96,1152]{1,0:T(8,128)(2,1)S(1)}, bf16[96,1152]{1,0:T(8,128)(2,1)S(1)}, u32[]{:S(2)}, u32[]{:S(2)}) collective-permute-start(bf16[96,1152]{1,0:T(8,128)(2,1)S(1)} %slice.3.refs_0_), channel_id=1, source_target_pairs={{0,4},{4,8},{8,12},{12,16},{16,20},{20,24},{24,28},{28,0},{1,5},{5... | collective-permute-start | bytes 663560 | tf_op jit(solution)/shard_map/ppermute | solution.py:17
  4.6 0.7 %collective-permute-start.1 = (bf16[416,1152]{1,0:T(8,128)(2,1)}, bf16[416,1152]{1,0:T(8,128)(2,1)S(1)}, u32[]{:S(2)}, u32[]{:S(2)}) collective-permute-start(bf16[416,1152]{1,0:T(8,128)(2,1)} %image_ref.3), channel_id=1, source_target_pairs={{0,3},{1,0},{2,1},{3,2},{4,7},{5,4},{6,5},{7,6},{8,11},{9,8},{10,9... | collective-permute-start | bytes 2875400 | tf_op jit(solution)/shard_map/ppermute | solution.py:17
  5.3 1.2 %copy-done = bf16[416,1152]{1,0:T(8,128)(2,1)S(1)} copy-done((bf16[416,1152]{1,0:T(8,128)(2,1)S(1)}, bf16[416,1152]{1,0:T(8,128)(2,1)}, u32[]{:S(2)}) %copy-start) | copy-done | bytes 958488
  6.5 0.2 fetch.5
  6.6 1.6 %collective-permute-start.2 = (bf16[160,1152]{1,0:T(8,128)(2,1)S(1)}, bf16[160,1152]{1,0:T(8,128)(2,1)S(1)}, u32[]{:S(2)}, u32[]{:S(2)}) collective-permute-start(bf16[160,1152]{1,0:T(8,128)(2,1)S(1)} %fetch.5), channel_id=1, source_target_pairs={{0,4},{4,8},{8,12},{12,16},{16,20},{20,24},{24,28},{28,0},{1,5},{5... | collective-permute-start | bytes 1105928 | tf_op jit(solution)/shard_map/ppermute | solution.py:17
  9.5 4.3 %collective-permute-done.refs_0_.upper_ref = bf16[96,1152]{1,0:T(8,128)(2,1)S(1)} collective-permute-done((bf16[96,1152]{1,0:T(8,128)(2,1)S(1)}, bf16[96,1152]{1,0:T(8,128)(2,1)S(1)}, u32[]{:S(2)}, u32[]{:S(2)}) %collective-permute-start) | collective-permute-done | bytes 221216 | tf_op jit(solution)/shard_map/ppermute | solution.py:17
  13.9 0.1 fetch.6
  14.0 0.1 collective-permute-start.3
  14.1 0.9 %subtract_convert_fusion.refs_0_ = bf16[416,416]{1,0:T(8,128)(2,1)S(1)} fusion(s32[416]{0:T(512)S(1)} %bitcast.30, f32[]{:T(128)} %bitcast.28, bf16[416,1152]{1,0:T(8,128)(2,1)S(1)} %copy-done.2, bf16[416,1152]{1,0:T(8,128)(2,1)S(1)} %copy-done.1, f32[]{:T(128)} %bitcast.24), kind=kOutput, calls=%fused_computation.22 | convolution fusion | flops 400278528 | bytes 2264712 | tf_op jit(solution)/shard_map/dot_general | solution.py:21
  15.0 0.1 fetch.7
  15.1 1.5 %collective-permute-start.4 = (bf16[32,1152]{1,0:T(8,128)(2,1)S(1)}, bf16[32,1152]{1,0:T(8,128)(2,1)S(1)}, u32[]{:S(2)}, u32[]{:S(2)}) collective-permute-start(bf16[32,1152]{1,0:T(8,128)(2,1)S(1)} %fetch.7), channel_id=1, source_target_pairs={{0,4},{4,8},{8,12},{12,16},{16,20},{20,24},{24,28},{28,0},{1,5},{5... | collective-permute-start | bytes 221192 | tf_op jit(solution)/shard_map/ppermute | solution.py:17
  16.6 0.7 %fusion.16.refs_2_ = f32[416,1152]{1,0:T(8,128)S(1)} fusion(bf16[416,416]{1,0:T(8,128)(2,1)S(1)} %subtract_convert_fusion.refs_0_, bf16[416,1152]{1,0:T(8,128)(2,1)S(1)} %copy-done.2), kind=kOutput, calls=%fused_computation.25 | convolution fusion | flops 398721024 | bytes 3221504 | tf_op jit(solution)/shard_map/dot_general | solution.py:25
  17.3 0.7 %fusion.15.refs_1_ = f32[416,1152]{1,0:T(8,128)S(1)} fusion(bf16[416,416]{1,0:T(8,128)(2,1)S(1)} %subtract_convert_fusion.refs_0_, bf16[416,1152]{1,0:T(8,128)(2,1)S(1)} %copy-done.1), kind=kOutput, calls=%fused_computation.24 | convolution fusion | flops 398721024 | bytes 3221504 | tf_op jit(solution)/shard_map/dot_general | solution.py:29
  18.1 0.8 %fusion.14 = bf16[416,416]{1,0:T(8,128)(2,1)S(1)} fusion(bf16[416,1152]{1,0:T(8,128)(2,1)S(1)} %pass_on.3.next_ref, bf16[416,1152]{1,0:T(8,128)(2,1)S(1)} %copy-done.1, f32[]{:T(128)} %bitcast.29, f32[]{:T(128)} %bitcast.27), kind=kOutput, calls=%fused_computation.21 | convolution fusion | flops 399759360 | bytes 2263048 | tf_op jit(solution)/shard_map/dot_general | solution.py:21
  18.9 0.7 %fusion.17 = f32[416,1152]{1,0:T(8,128)S(1)} fusion(bf16[416,416]{1,0:T(8,128)(2,1)S(1)} %fusion.14, bf16[416,1152]{1,0:T(8,128)(2,1)S(1)} %copy-done.1), kind=kOutput, calls=%fused_computation.26 | convolution fusion | flops 398721024 | bytes 3221504 | tf_op jit(solution)/shard_map/dot_general | solution.py:29
  19.6 2.2 %collective-permute-done.2.lower_ref = bf16[160,1152]{1,0:T(8,128)(2,1)S(1)} collective-permute-done((bf16[160,1152]{1,0:T(8,128)(2,1)S(1)}, bf16[160,1152]{1,0:T(8,128)(2,1)S(1)}, u32[]{:S(2)}, u32[]{:S(2)}) %collective-permute-start.2) | collective-permute-done | bytes 368672 | tf_op jit(solution)/shard_map/ppermute | solution.py:17
  21.8 1.6 %chunk.2 = (bf16[256,1152]{1,0:T(8,128)(2,1)S(1)}, bf16[256,1152]{1,0:T(8,128)(2,1)S(1)}, bf16[256,416]{1,0:T(8,128)(2,1)S(1)}, bf16[256,416]{1,0:T(8,128)(2,1)S(1)}) custom-call(f32[1]{0:T(128)} %copy.15.scale_ref, f32[1]{0:T(128)} %copy.16.bias_ref, bf16[416,1152]{1,0:T(8,128)(2,1)S(1)} %copy-done.2, bf16[416,1152]{1,0:T(8,128)(2,1)S(1)} %pass_on.3.next_ref, ...), custom_call_target="tpu_custom_call" | custom-call | flops 981467136 | bytes 3686400 | tf_op jit(solution)/shard_map/chunk/pallas_call | solution.py:91
  23.4 0.5 convolution_add_fusion.3.refs_2_
  23.9 4.1 %collective-permute-done.3.refs_1_.upper_ref = bf16[128,1152]{1,0:T(8,128)(2,1)S(1)} collective-permute-done((bf16[128,1152]{1,0:T(8,128)(2,1)S(1)}, bf16[128,1152]{1,0:T(8,128)(2,1)S(1)}, u32[]{:S(2)}, u32[]{:S(2)}) %collective-permute-start.3) | collective-permute-done | bytes 294944 | tf_op jit(solution)/shard_map/ppermute | solution.py:17
  28.1 1.7 %collective-permute-start.7 = (bf16[256,1152]{1,0:T(8,128)(2,1)S(1)}, bf16[256,1152]{1,0:T(8,128)(2,1)S(1)}, u32[]{:S(2)}, u32[]{:S(2)}) collective-permute-start(bf16[256,1152]{1,0:T(8,128)(2,1)S(1)} %pass_on.4.refs_0_), channel_id=1, source_target_pairs={{0,28},{4,0},{8,4},{12,8},{16,12},{20,16},{24,20},{28,24},{1,29},{... | collective-permute-start | bytes 1769480 | tf_op jit(solution)/shard_map/ppermute | solution.py:17
  29.8 1.3 %chunk.3 = (bf16[160,1152]{1,0:T(8,128)(2,1)S(1)}, bf16[160,1152]{1,0:T(8,128)(2,1)S(1)}, bf16[160,416]{1,0:T(8,128)(2,1)S(1)}, bf16[160,416]{1,0:T(8,128)(2,1)S(1)}) custom-call(f32[1]{0:T(128)} %copy.15.scale_ref, f32[1]{0:T(128)} %copy.16.bias_ref, bf16[416,1152]{1,0:T(8,128)(2,1)S(1)} %copy-done.2, bf16[416,1152]{1,0:T(8,128)(2,1)S(1)} %pass_on.3.next_ref, ...), custom_call_target="tpu_custom_call" | custom-call | flops 613416960 | bytes 3022848 | tf_op jit(solution)/shard_map/chunk/pallas_call | solution.py:91
  31.1 0.5 fusion.3.refs_1_
  31.7 1.5 %collective-permute-start.6 = (bf16[160,1152]{1,0:T(8,128)(2,1)S(1)}, bf16[160,1152]{1,0:T(8,128)(2,1)S(1)}, u32[]{:S(2)}, u32[]{:S(2)}) collective-permute-start(bf16[160,1152]{1,0:T(8,128)(2,1)S(1)} %pass_on.5), channel_id=1, source_target_pairs={{0,28},{4,0},{8,4},{12,8},{16,12},{20,16},{24,20},{28,24},{1,29},{... | collective-permute-start | bytes 1105928 | tf_op jit(solution)/shard_map/ppermute | solution.py:17
  33.1 0.5 convolution_add_fusion.4
  33.6 0.5 fusion.2.total_ref
  34.1 0.7 %fusion.total_ref = f32[416,1152]{1,0:T(8,128)S(1)} fusion(f32[416,1152]{1,0:T(8,128)S(1)} %fusion.16.refs_2_, bf16[416,416]{1,0:T(8,128)(2,1)S(1)} %fusion.14, bf16[416,1152]{1,0:T(8,128)(2,1)S(1)} %pass_on.3.next_ref, f32[]{:T(128)} %bitcast.25), kind=kOutput, calls=%fused_computation.1 | convolution fusion | flops 399679488 | bytes 5138436 | tf_op jit(solution)/shard_map/dot_general | solution.py:25
  34.9 9.4 %collective-permute-done.7.back_ref = bf16[256,1152]{1,0:T(8,128)(2,1)S(1)} collective-permute-done((bf16[256,1152]{1,0:T(8,128)(2,1)S(1)}, bf16[256,1152]{1,0:T(8,128)(2,1)S(1)}, u32[]{:S(2)}, u32[]{:S(2)}) %collective-permute-start.7) | collective-permute-done | bytes 589856 | tf_op jit(solution)/shard_map/ppermute | solution.py:17
  44.3 0.9 %add_rows.4.refs_0_ = bf16[416,1152]{1,0:T(8,128)(2,1)} custom-call(f32[416,1152]{1,0:T(8,128)S(1)} %fusion.total_ref, bf16[256,1152]{1,0:T(8,128)(2,1)S(1)} %collective-permute-done.7.back_ref), custom_call_target="tpu_custom_call" | custom-call | tf_op jit(solution)/shard_map/add_rows/pallas_call | solution.py:130
  45.2 1.0 %add_rows.3 = (bf16[416,1152]{1,0:T(8,128)(2,1)}, f32[8,128]{1,0:T(8,128)S(1)}) custom-call(f32[416,1152]{1,0:T(8,128)S(1)} %fusion.2.total_ref, bf16[416,1152]{1,0:T(8,128)(2,1)S(1)} %collective-permute-done.5.back_ref), custom_call_target="tpu_custom_call" | custom-call | tf_op jit(solution)/shard_map/add_rows/pallas_call | solution.py:130
  46.3 3.4 %collective-permute-done.6.back_ref = bf16[160,1152]{1,0:T(8,128)(2,1)S(1)} collective-permute-done((bf16[160,1152]{1,0:T(8,128)(2,1)S(1)}, bf16[160,1152]{1,0:T(8,128)(2,1)S(1)}, u32[]{:S(2)}, u32[]{:S(2)}) %collective-permute-start.6) | collective-permute-done | bytes 368672 | tf_op jit(solution)/shard_map/ppermute | solution.py:17
  49.7 0.8 %add_rows.5 = bf16[416,1152]{1,0:T(8,128)(2,1)} custom-call(f32[416,1152]{1,0:T(8,128)S(1)} %fusion.total_ref, bf16[160,1152]{1,0:T(8,128)(2,1)S(1)} %collective-permute-done.6.back_ref, bf16[416,1152]{1,0:T(8,128)(2,1)} %add_rows.4.refs_0_, f32[8,128]{1,0:T(8,128)S(1)} %get-tuple-element.21.refs_1_), custom_call_target="tpu_custom_call", output_to_operand_aliasing={{}: (2, {})} | custom-call | tf_op jit(solution)/shard_map/add_rows/pallas_call | solution.py:130
  (15 shorter events, 0.1 us)
Async XLA Ops:
  0.6 13.3 %copy-start.3 = (s32[1,416]{1,0:T(1,128)S(1)}, s32[1,416]{1,0:T(1,128)}, u32[]{:S(2)}) copy-start(s32[1,416]{1,0:T(1,128)} %array_ref.4) | copy-start | bytes 4996
  1.6 12.3 %collective-permute-start = (bf16[96,1152]{1,0:T(8,128)(2,1)S(1)}, bf16[96,1152]{1,0:T(8,128)(2,1)S(1)}, u32[]{:S(2)}, u32[]{:S(2)}) collective-permute-start(bf16[96,1152]{1,0:T(8,128)(2,1)S(1)} %slice.3.refs_0_), channel_id=1, source_target_pairs={{0,4},{4,8},{8,12},{12,16},{16,20},{20,24},{24,28},{28,0},{1,5},{5... | collective-permute-start | bytes 663560 | tf_op jit(solution)/shard_map/ppermute | solution.py:17
  4.6 13.4 %collective-permute-start.1 = (bf16[416,1152]{1,0:T(8,128)(2,1)}, bf16[416,1152]{1,0:T(8,128)(2,1)S(1)}, u32[]{:S(2)}, u32[]{:S(2)}) collective-permute-start(bf16[416,1152]{1,0:T(8,128)(2,1)} %image_ref.3), channel_id=1, source_target_pairs={{0,3},{1,0},{2,1},{3,2},{4,7},{5,4},{6,5},{7,6},{8,11},{9,8},{10,9... | collective-permute-start | bytes 2875400 | tf_op jit(solution)/shard_map/ppermute | solution.py:17
  5.3 1.2 %copy-start = (bf16[416,1152]{1,0:T(8,128)(2,1)S(1)}, bf16[416,1152]{1,0:T(8,128)(2,1)}, u32[]{:S(2)}) copy-start(bf16[416,1152]{1,0:T(8,128)(2,1)} %array_ref.7) | copy-start | bytes 2875396
  6.5 7.4 %copy-start.1 = (bf16[416,1152]{1,0:T(8,128)(2,1)S(1)}, bf16[416,1152]{1,0:T(8,128)(2,1)}, u32[]{:S(2)}) copy-start(bf16[416,1152]{1,0:T(8,128)(2,1)} %array_ref.7) | copy-start | bytes 2875396
  6.5 7.6 %copy-start.2 = (bf16[416,1152]{1,0:T(8,128)(2,1)S(1)}, bf16[416,1152]{1,0:T(8,128)(2,1)}, u32[]{:S(2)}) copy-start(bf16[416,1152]{1,0:T(8,128)(2,1)} %image_ref.3) | copy-start | bytes 2875396
  6.6 15.1 %collective-permute-start.2 = (bf16[160,1152]{1,0:T(8,128)(2,1)S(1)}, bf16[160,1152]{1,0:T(8,128)(2,1)S(1)}, u32[]{:S(2)}, u32[]{:S(2)}) collective-permute-start(bf16[160,1152]{1,0:T(8,128)(2,1)S(1)} %fetch.5), channel_id=1, source_target_pairs={{0,4},{4,8},{8,12},{12,16},{16,20},{20,24},{24,28},{28,0},{1,5},{5... | collective-permute-start | bytes 1105928 | tf_op jit(solution)/shard_map/ppermute | solution.py:17
  14.0 14.1 %collective-permute-start.3 = (bf16[128,1152]{1,0:T(8,128)(2,1)S(1)}, bf16[128,1152]{1,0:T(8,128)(2,1)S(1)}, u32[]{:S(2)}, u32[]{:S(2)}) collective-permute-start(bf16[128,1152]{1,0:T(8,128)(2,1)S(1)} %fetch.6), channel_id=1, source_target_pairs={{0,4},{4,8},{8,12},{12,16},{16,20},{20,24},{24,28},{28,0},{1,5},{5... | collective-permute-start | bytes 884744 | tf_op jit(solution)/shard_map/ppermute | solution.py:17
  15.1 14.7 %collective-permute-start.4 = (bf16[32,1152]{1,0:T(8,128)(2,1)S(1)}, bf16[32,1152]{1,0:T(8,128)(2,1)S(1)}, u32[]{:S(2)}, u32[]{:S(2)}) collective-permute-start(bf16[32,1152]{1,0:T(8,128)(2,1)S(1)} %fetch.7), channel_id=1, source_target_pairs={{0,4},{4,8},{8,12},{12,16},{16,20},{20,24},{24,28},{28,0},{1,5},{5... | collective-permute-start | bytes 221192 | tf_op jit(solution)/shard_map/ppermute | solution.py:17
  28.1 16.3 %collective-permute-start.7 = (bf16[256,1152]{1,0:T(8,128)(2,1)S(1)}, bf16[256,1152]{1,0:T(8,128)(2,1)S(1)}, u32[]{:S(2)}, u32[]{:S(2)}) collective-permute-start(bf16[256,1152]{1,0:T(8,128)(2,1)S(1)} %pass_on.4.refs_0_), channel_id=1, source_target_pairs={{0,28},{4,0},{8,4},{12,8},{16,12},{20,16},{24,20},{28,24},{1,29},{... | collective-permute-start | bytes 1769480 | tf_op jit(solution)/shard_map/ppermute | solution.py:17
  31.6 13.6 %collective-permute-start.5 = (bf16[416,1152]{1,0:T(8,128)(2,1)S(1)}, bf16[416,1152]{1,0:T(8,128)(2,1)S(1)}, u32[]{:S(2)}, u32[]{:S(2)}) collective-permute-start(bf16[416,1152]{1,0:T(8,128)(2,1)S(1)} %fusion.3.refs_1_), channel_id=1, source_target_pairs={{0,1},{1,2},{2,3},{3,0},{4,5},{5,6},{6,7},{7,4},{8,9},{9,10},{10,1... | collective-permute-start | bytes 2875400 | tf_op jit(solution)/shard_map/ppermute | solution.py:17
  31.7 18.0 %collective-permute-start.6 = (bf16[160,1152]{1,0:T(8,128)(2,1)S(1)}, bf16[160,1152]{1,0:T(8,128)(2,1)S(1)}, u32[]{:S(2)}, u32[]{:S(2)}) collective-permute-start(bf16[160,1152]{1,0:T(8,128)(2,1)S(1)} %pass_on.5), channel_id=1, source_target_pairs={{0,28},{4,0},{8,4},{12,8},{16,12},{20,16},{24,20},{28,24},{1,29},{... | collective-permute-start | bytes 1105928 | tf_op jit(solution)/shard_map/ppermute | solution.py:17

commit v17 on v14

--- a/solution.py
+++ b/solution.py
@@ -36,7 +36,9 @@
 def shifted_half(shard, by, parity):
     blocks, groups = lax.axis_size("blk"), lax.axis_size("grp")
     pairs = [
-        (b * groups + g, (b + by * (g % 2 == parity)) % blocks * groups + g) for b in range(blocks) for g in range(groups)
+        (b * groups + g, (b + (by if g % 2 == parity else 2)) % blocks * groups + g)
+        for b in range(blocks)
+        for g in range(groups)
     ]
     return lax.ppermute(shard, ("blk", "grp"), pairs)
 
@@ -172,13 +174,12 @@
     cut = count // 16 * FIRST // 26 * 16
     parity = (lax.axis_index("grp") % 2).astype(jnp.int32).reshape(1)
     even = shifted_half(text, 1, 0)
-    held = fetch(image, 0, count, [])
-    image_next = shifted(held, "grp", -1)
+    image_next = shifted(image, "grp", -1)
 
     own = jax.nn.sigmoid(dot_nt(image, text) * scale + bias)
     column = lax.broadcasted_iota(jnp.int32, own.shape, 1)
     own = (own - (column == target[0][:, None]).astype(jnp.float32)).astype(jnp.bfloat16)
-    odd = shifted_half(fetch(text, 0, count, [held]), 1, 1)
+    odd = shifted_half(fetch(text, 0, count, [own]), 1, 1)
     image_grad = dot_nn(own, text)
     text_grad = dot_tn(own, image)
 

time: 64 us -> 75.9 us (1.19)
  waiting for transfers between devices: 8.25 us -> 23.2 us
  matrix products: 9.54 us -> 11.2 us
  starting transfers between devices: 25.5 us -> 23.9 us
  local copies, waits for them, and re-layouts: 6.34 us -> 5.11 us
  Pallas kernels: 11.2 us -> 10 us
    ppermute x2, waiting for transfers between devices: 0.01 us -> 14 us  [shifted_half(): return lax.ppermute(shard, ('blk', 'grp'), pairs)]
    ppermute x2, starting transfers between devices: 13.8 us -> 4.62 us  [shifted_half(): return lax.ppermute(shard, ('blk', 'grp'), pairs)]
    ppermute x4, starting transfers between devices: 11.7 us -> 19.3 us  [shifted(): lax.ppermute(shard, axis, [(i, (i + by) % devices) for i in range(devices)])]
    dot_general x2, matrix products: 1.71 us -> 3.28 us  [dot_nt(): lax.dot_general(a, b, (((1,), (1,)), ((), ())), preferred_element_type=jn...]
    unnamed x16 -> x12, local copies, waits for them, and re-layouts: 6.34 us -> 5.11 us
    pallas_call x2 -> x1, Pallas kernels: 2.43 us -> 1.22 us  [fetch(): pl.pallas_call(kernel, out_shape=jax.ShapeDtypeStruct((hi - lo, array.sha...]
    ppermute x4, waiting for transfers between devices: 8.24 us -> 9.22 us  [shifted(): lax.ppermute(shard, axis, [(i, (i + by) % devices) for i in range(devices)])]
  transfers between devices with their start and end apart: 6 -> 6, of which waited for: 2 -> 2; matrix products, arithmetic and copies ran while one was open for 15% -> 15% of each run, Pallas kernels for 12% -> 8%
where the time goes in v17:
time: 75.9 us; the launch traced here: 75.6 us
  starting transfers between devices  23.9 us (31%)
  waiting for transfers between devices  23.2 us (31%)
  matrix products  11.2 us (15%)
  Pallas kernels  10 us (13%)
  local copies, waits for them, and re-layouts  5.11 us (7%)
  between operations  2.11 us (3%)
    ppermute x4, starting transfers between devices, shifted(): lax.ppermute(shard, axis, [(i, (i + by) % devices) for i in range(devices)])  19.3 us
    ppermute x2, waiting for transfers between devices, shifted_half(): return lax.ppermute(shard, ('blk', 'grp'), pairs)  14 us
    ppermute x4, waiting for transfers between devices, shifted(): lax.ppermute(shard, axis, [(i, (i + by) % devices) for i in range(devices)])  9.22 us
    pallas_call x2, Pallas kernels, chunk(): pl.pallas_call(functools.partial(chunk_kernel, lo), out_shape=(text, text...  6.12 us
    dot_general x6, matrix products, dot_tn(): lax.dot_general(a, b, (((0,), (0,)), ((), ())), preferred_element_type=jn...  5.19 us
    unnamed x12, local copies, waits for them, and re-layouts  5.11 us
    ppermute x2, starting transfers between devices, shifted_half(): return lax.ppermute(shard, ('blk', 'grp'), pairs)  4.62 us
    dot_general x2, matrix products, dot_nt(): lax.dot_general(a, b, (((1,), (1,)), ((), ())), preferred_element_type=jn...  3.28 us
  transfers between devices with their start and end apart: 6, of which 2 were waited for; matrix products, arithmetic and copies ran while one was open for 15% of the time, Pallas kernels for 8%

profile of v17, /device:TPU:0, one launch (start us, length us, event | category | flops | bytes accessed | tf_op | source)
XLA Modules:
  0.0 75.6 jit_solution(8482388782420475434)
XLA Ops:
  0.6 3.0 %collective-permute-start.1 = (bf16[416,1152]{1,0:T(8,128)(2,1)}, bf16[416,1152]{1,0:T(8,128)(2,1)}, u32[]{:S(2)}, u32[]{:S(2)}) collective-permute-start(bf16[416,1152]{1,0:T(8,128)(2,1)} %array_ref.1), channel_id=1, source_target_pairs={{0,4},{1,9},{2,6},{3,11},{4,8},{5,13},{6,10},{7,15},{8,12},{9,17},... | collective-permute-start | bytes 2875400 | tf_op jit(solution)/shard_map/ppermute | solution.py:43
  3.6 0.8 %collective-permute-start = (bf16[416,1152]{1,0:T(8,128)(2,1)}, bf16[416,1152]{1,0:T(8,128)(2,1)S(1)}, u32[]{:S(2)}, u32[]{:S(2)}) collective-permute-start(bf16[416,1152]{1,0:T(8,128)(2,1)} %image_ref.3), channel_id=1, source_target_pairs={{0,3},{1,0},{2,1},{3,2},{4,7},{5,4},{6,5},{7,6},{8,11},{9,8},{10,9... | collective-permute-start | bytes 2875400 | tf_op jit(solution)/shard_map/ppermute | solution.py:21
  5.7 2.4 %fusion.18.refs_0_ = bf16[416,416]{1,0:T(8,128)(2,1)S(1)} fusion(bf16[416,1152]{1,0:T(8,128)(2,1)} %image_ref.3, bf16[416,1152]{1,0:T(8,128)(2,1)} %array_ref.1, s32[416]{0:T(512)} %bitcast.31, f32[]{:T(128)} %bitcast.29, f32[]{:T(128)} %bitcast.25), kind=kOutput, calls=%fused_computation.23 | convolution fusion | flops 400278528 | bytes 2264712 | tf_op jit(solution)/shard_map/dot_general | solution.py:25
  8.2 0.0 copy-start.5
  8.2 1.2 %fetch.1 = bf16[416,1152]{1,0:T(8,128)(2,1)} custom-call(bf16[416,1152]{1,0:T(8,128)(2,1)S(1)} %copy-done, bf16[416,416]{1,0:T(8,128)(2,1)S(1)} %fusion.18.refs_0_), custom_call_target="tpu_custom_call" | custom-call | tf_op jit(solution)/shard_map/fetch/pallas_call | solution.py:53
  9.4 1.6 %collective-permute-start.2 = (bf16[416,1152]{1,0:T(8,128)(2,1)}, bf16[416,1152]{1,0:T(8,128)(2,1)}, u32[]{:S(2)}, u32[]{:S(2)}) collective-permute-start(bf16[416,1152]{1,0:T(8,128)(2,1)} %fetch.1), channel_id=1, source_target_pairs={{0,8},{1,5},{2,10},{3,7},{4,12},{5,9},{6,14},{7,11},{8,16},{9,13},... | collective-permute-start | bytes 2875400 | tf_op jit(solution)/shard_map/ppermute | solution.py:43
  11.0 2.0 %fusion.20.refs_2_ = f32[416,1152]{1,0:T(8,128)} fusion(bf16[416,416]{1,0:T(8,128)(2,1)S(1)} %fusion.18.refs_0_, bf16[416,1152]{1,0:T(8,128)(2,1)S(1)} %copy-done.5), kind=kOutput, calls=%fused_computation.26 | convolution fusion | flops 398721024 | bytes 3221504 | tf_op jit(solution)/shard_map/dot_general | solution.py:29
  13.0 2.0 %fusion.19.refs_1_ = f32[416,1152]{1,0:T(8,128)} fusion(bf16[416,416]{1,0:T(8,128)(2,1)S(1)} %fusion.18.refs_0_, bf16[416,1152]{1,0:T(8,128)(2,1)S(1)} %copy-done), kind=kOutput, calls=%fused_computation.25 | convolution fusion | flops 398721024 | bytes 3221504 | tf_op jit(solution)/shard_map/dot_general | solution.py:33
  15.0 14.0 %collective-permute-done.1.refs_0_ = bf16[416,1152]{1,0:T(8,128)(2,1)} collective-permute-done((bf16[416,1152]{1,0:T(8,128)(2,1)}, bf16[416,1152]{1,0:T(8,128)(2,1)}, u32[]{:S(2)}, u32[]{:S(2)}) %collective-permute-start.1) | collective-permute-done | bytes 958496 | tf_op jit(solution)/shard_map/ppermute | solution.py:43
  29.0 1.5 %copy-done.1 = f32[416,1152]{1,0:T(8,128)S(1)} copy-done((f32[416,1152]{1,0:T(8,128)S(1)}, f32[416,1152]{1,0:T(8,128)}, u32[]{:S(2)}) %copy-start.1) | copy-done | bytes 1916952
  30.6 1.5 %copy-done.3 = f32[416,1152]{1,0:T(8,128)S(1)} copy-done((f32[416,1152]{1,0:T(8,128)S(1)}, f32[416,1152]{1,0:T(8,128)}, u32[]{:S(2)}) %copy-start.3) | copy-done | bytes 1916952
  32.1 0.0 collective-permute-done.refs_0_
  32.1 0.0 collective-permute-done.2.refs_0_
  32.1 2.7 %chunk.2 = (bf16[128,1152]{1,0:T(8,128)(2,1)S(1)}, bf16[128,1152]{1,0:T(8,128)(2,1)S(1)}, bf16[128,416]{1,0:T(8,128)(2,1)S(1)}, bf16[128,416]{1,0:T(8,128)(2,1)S(1)}) custom-call(s32[1]{0:T(128)} %bitcast.3.parity_ref, f32[1]{0:T(128)} %copy.19.scale_ref, f32[1]{0:T(128)} %copy.20.bias_ref, bf16[416,1152]{1,0:T(8,128)(2,1)S(1)} %copy-done.5, ...), custom_call_target="tpu_custom_call" | custom-call | flops 490733568 | bytes 3096576 | tf_op jit(solution)/shard_map/chunk/pallas_call | solution.py:106
  34.8 18.4 %collective-permute-start.5 = (bf16[128,1152]{1,0:T(8,128)(2,1)S(1)}, bf16[128,1152]{1,0:T(8,128)(2,1)S(1)}, u32[]{:S(2)}, u32[]{:S(2)}) collective-permute-start(bf16[128,1152]{1,0:T(8,128)(2,1)S(1)} %get-tuple-element.14.refs_1_), channel_id=1, source_target_pairs={{0,28},{4,0},{8,4},{12,8},{16,12},{20,16},{24,20},{28,24},{1,29},{... | collective-permute-start | bytes 884744 | tf_op jit(solution)/shard_map/ppermute | solution.py:21
  53.3 3.4 %chunk.3 = (bf16[288,1152]{1,0:T(8,128)(2,1)S(1)}, bf16[288,1152]{1,0:T(8,128)(2,1)S(1)}, bf16[288,416]{1,0:T(8,128)(2,1)S(1)}, bf16[288,416]{1,0:T(8,128)(2,1)S(1)}) custom-call(s32[1]{0:T(128)} %bitcast.3.parity_ref, f32[1]{0:T(128)} %copy.19.scale_ref, f32[1]{0:T(128)} %copy.20.bias_ref, bf16[416,1152]{1,0:T(8,128)(2,1)S(1)} %copy-done.5, ...), custom_call_target="tpu_custom_call" | custom-call | flops 1104150528 | bytes 4571136 | tf_op jit(solution)/shard_map/chunk/pallas_call | solution.py:106
  56.7 0.1 collective-permute-start.4
  56.8 0.8 %fusion.17 = bf16[416,416]{1,0:T(8,128)(2,1)S(1)} fusion(bf16[416,1152]{1,0:T(8,128)(2,1)S(1)} %pass_on.9, bf16[416,1152]{1,0:T(8,128)(2,1)S(1)} %copy-done, f32[]{:T(128)} %bitcast.30, f32[]{:T(128)} %bitcast.28), kind=kOutput, calls=%fused_computation.22 | convolution fusion | flops 399759360 | bytes 2263048 | tf_op jit(solution)/shard_map/dot_general | solution.py:25
  57.6 0.7 fusion.22
  58.3 0.7 fusion.21
  59.1 0.7 fusion.23
  59.8 0.4 fusion.5
  60.3 0.1 collective-permute-start.3
  60.3 1.0 %copy-done.2 = f32[416,1152]{1,0:T(8,128)S(1)} copy-done((f32[416,1152]{1,0:T(8,128)S(1)}, f32[416,1152]{1,0:T(8,128)}, u32[]{:S(2)}) %copy-start.2) | copy-done | bytes 1916952
  61.3 0.5 fusion.4.total_ref
  61.8 1.0 %copy-done.4 = f32[416,1152]{1,0:T(8,128)S(1)} copy-done((f32[416,1152]{1,0:T(8,128)S(1)}, f32[416,1152]{1,0:T(8,128)}, u32[]{:S(2)}) %copy-start.4) | copy-done | bytes 1916952
  62.9 0.8 %fusion.total_ref = f32[416,1152]{1,0:T(8,128)S(1)} fusion(f32[416,1152]{1,0:T(8,128)S(1)} %copy-done.4, bf16[416,416]{1,0:T(8,128)(2,1)S(1)} %fusion.17, bf16[416,1152]{1,0:T(8,128)(2,1)S(1)} %pass_on.9, f32[]{:T(128)} %bitcast.26), kind=kOutput, calls=%fused_computation.1 | convolution fusion | flops 399679488 | bytes 5138436 | tf_op jit(solution)/shard_map/dot_general | solution.py:29
  63.6 0.0 collective-permute-done.5.refs_0_
  63.7 0.8 %add_rows.3.refs_1_ = bf16[416,1152]{1,0:T(8,128)(2,1)} custom-call(f32[416,1152]{1,0:T(8,128)S(1)} %fusion.total_ref, bf16[128,1152]{1,0:T(8,128)(2,1)S(1)} %collective-permute-done.5.refs_0_), custom_call_target="tpu_custom_call" | custom-call | tf_op jit(solution)/shard_map/add_rows/pallas_call | solution.py:157
  64.4 9.2 %collective-permute-done.4.refs_0_ = bf16[288,1152]{1,0:T(8,128)(2,1)S(1)} collective-permute-done((bf16[288,1152]{1,0:T(8,128)(2,1)S(1)}, bf16[288,1152]{1,0:T(8,128)(2,1)S(1)}, u32[]{:S(2)}, u32[]{:S(2)}) %collective-permute-start.4) | collective-permute-done | bytes 663584 | tf_op jit(solution)/shard_map/ppermute | solution.py:21
  73.6 0.9 %add_rows.4 = (bf16[416,1152]{1,0:T(8,128)(2,1)}, f32[8,128]{1,0:T(8,128)S(1)}) custom-call(f32[416,1152]{1,0:T(8,128)S(1)} %fusion.total_ref, bf16[288,1152]{1,0:T(8,128)(2,1)S(1)} %collective-permute-done.4.refs_0_, bf16[416,1152]{1,0:T(8,128)(2,1)} %add_rows.3.refs_1_), custom_call_target="tpu_custom_call", output_to_operand_aliasing={{0}: (2, {})} | custom-call | flops 20000000000 | tf_op jit(solution)/shard_map/add_rows/pallas_call | solution.py:157
  74.6 1.0 %add_rows.5 = bf16[416,1152]{1,0:T(8,128)(2,1)} custom-call(f32[416,1152]{1,0:T(8,128)S(1)} %fusion.4.total_ref, bf16[416,1152]{1,0:T(8,128)(2,1)S(1)} %collective-permute-done.3.refs_0_, f32[8,128]{1,0:T(8,128)S(1)} %get-tuple-element.20.refs_1_), custom_call_target="tpu_custom_call" | custom-call | tf_op jit(solution)/shard_map/add_rows/pallas_call | solution.py:157
  (13 shorter events, 0.0 us)
Async XLA Ops:
  0.6 28.4 %collective-permute-start.1 = (bf16[416,1152]{1,0:T(8,128)(2,1)}, bf16[416,1152]{1,0:T(8,128)(2,1)}, u32[]{:S(2)}, u32[]{:S(2)}) collective-permute-start(bf16[416,1152]{1,0:T(8,128)(2,1)} %array_ref.1), channel_id=1, source_target_pairs={{0,4},{1,9},{2,6},{3,11},{4,8},{5,13},{6,10},{7,15},{8,12},{9,17},... | collective-permute-start | bytes 2875400 | tf_op jit(solution)/shard_map/ppermute | solution.py:43
  3.6 28.5 %collective-permute-start = (bf16[416,1152]{1,0:T(8,128)(2,1)}, bf16[416,1152]{1,0:T(8,128)(2,1)S(1)}, u32[]{:S(2)}, u32[]{:S(2)}) collective-permute-start(bf16[416,1152]{1,0:T(8,128)(2,1)} %image_ref.3), channel_id=1, source_target_pairs={{0,3},{1,0},{2,1},{3,2},{4,7},{5,4},{6,5},{7,6},{8,11},{9,8},{10,9... | collective-permute-start | bytes 2875400 | tf_op jit(solution)/shard_map/ppermute | solution.py:21
  5.7 2.5 %copy-start = (bf16[416,1152]{1,0:T(8,128)(2,1)S(1)}, bf16[416,1152]{1,0:T(8,128)(2,1)}, u32[]{:S(2)}) copy-start(bf16[416,1152]{1,0:T(8,128)(2,1)} %array_ref.1) | copy-start | bytes 2875396
  8.2 2.9 %copy-start.5 = (bf16[416,1152]{1,0:T(8,128)(2,1)S(1)}, bf16[416,1152]{1,0:T(8,128)(2,1)}, u32[]{:S(2)}) copy-start(bf16[416,1152]{1,0:T(8,128)(2,1)} %image_ref.3) | copy-start | bytes 2875396
  9.4 22.7 %collective-permute-start.2 = (bf16[416,1152]{1,0:T(8,128)(2,1)}, bf16[416,1152]{1,0:T(8,128)(2,1)}, u32[]{:S(2)}, u32[]{:S(2)}) collective-permute-start(bf16[416,1152]{1,0:T(8,128)(2,1)} %fetch.1), channel_id=1, source_target_pairs={{0,8},{1,5},{2,10},{3,7},{4,12},{5,9},{6,14},{7,11},{8,16},{9,13},... | collective-permute-start | bytes 2875400 | tf_op jit(solution)/shard_map/ppermute | solution.py:43
  29.0 1.5 %copy-start.1 = (f32[416,1152]{1,0:T(8,128)S(1)}, f32[416,1152]{1,0:T(8,128)}, u32[]{:S(2)}) copy-start(f32[416,1152]{1,0:T(8,128)} %fusion.19.refs_1_) | copy-start | bytes 5750788
  30.6 1.5 %copy-start.3 = (f32[416,1152]{1,0:T(8,128)S(1)}, f32[416,1152]{1,0:T(8,128)}, u32[]{:S(2)}) copy-start(f32[416,1152]{1,0:T(8,128)} %fusion.20.refs_2_) | copy-start | bytes 5750788
  34.8 28.8 %collective-permute-start.5 = (bf16[128,1152]{1,0:T(8,128)(2,1)S(1)}, bf16[128,1152]{1,0:T(8,128)(2,1)S(1)}, u32[]{:S(2)}, u32[]{:S(2)}) collective-permute-start(bf16[128,1152]{1,0:T(8,128)(2,1)S(1)} %get-tuple-element.14.refs_1_), channel_id=1, source_target_pairs={{0,28},{4,0},{8,4},{12,8},{16,12},{20,16},{24,20},{28,24},{1,29},{... | collective-permute-start | bytes 884744 | tf_op jit(solution)/shard_map/ppermute | solution.py:21
  56.7 17.0 %collective-permute-start.4 = (bf16[288,1152]{1,0:T(8,128)(2,1)S(1)}, bf16[288,1152]{1,0:T(8,128)(2,1)S(1)}, u32[]{:S(2)}, u32[]{:S(2)}) collective-permute-start(bf16[288,1152]{1,0:T(8,128)(2,1)S(1)} %get-tuple-element.17.refs_1_), channel_id=1, source_target_pairs={{0,28},{4,0},{8,4},{12,8},{16,12},{20,16},{24,20},{28,24},{1,29},{... | collective-permute-start | bytes 1990664 | tf_op jit(solution)/shard_map/ppermute | solution.py:21
  59.8 1.5 %copy-start.2 = (f32[416,1152]{1,0:T(8,128)S(1)}, f32[416,1152]{1,0:T(8,128)}, u32[]{:S(2)}) copy-start(f32[416,1152]{1,0:T(8,128)} %fusion.19.refs_1_) | copy-start | bytes 5750788
  60.3 14.3 %collective-permute-start.3 = (bf16[416,1152]{1,0:T(8,128)(2,1)S(1)}, bf16[416,1152]{1,0:T(8,128)(2,1)S(1)}, u32[]{:S(2)}, u32[]{:S(2)}) collective-permute-start(bf16[416,1152]{1,0:T(8,128)(2,1)S(1)} %fusion.5), channel_id=1, source_target_pairs={{0,1},{1,2},{2,3},{3,0},{4,5},{5,6},{6,7},{7,4},{8,9},{9,10},{10,1... | collective-permute-start | bytes 2875400 | tf_op jit(solution)/shard_map/ppermute | solution.py:21
  61.3 1.5 %copy-start.4 = (f32[416,1152]{1,0:T(8,128)S(1)}, f32[416,1152]{1,0:T(8,128)}, u32[]{:S(2)}) copy-start(f32[416,1152]{1,0:T(8,128)} %fusion.20.refs_2_) | copy-start | bytes 5750788

commit v18 on v13

--- a/solution.py
+++ b/solution.py
@@ -68,8 +68,8 @@
     )(array, *after)
 
 
-def chunk_kernel(count, scale_ref, bias_ref, image_ref, next_ref, *refs):
-    sent_ref, joined_ref, own_ref, other_ref = refs[-4:]
+def chunk_kernel(count, lasts, scale_ref, bias_ref, image_ref, next_ref, *refs):
+    joined_ref, own_ref, other_ref, *sent_refs = refs[-4 - bool(lasts) :]
     scale, bias = scale_ref[0], bias_ref[0]
     start = 0
     for piece_ref in refs[:count]:
@@ -85,18 +85,22 @@
     other = jax.nn.sigmoid(dot_nt(part, image) * scale + bias).astype(jnp.bfloat16)
     other_ref[...] = other
     total += dot_nn(other, image)
-    sent_ref[...] = (scale * total).astype(jnp.bfloat16)
+    total = (scale * total).astype(jnp.bfloat16)
+    start = 0
+    for sent_ref in sent_refs:
+        sent_ref[...] = total[start : start + sent_ref.shape[0], :]
+        start += sent_ref.shape[0]
 
 
-def chunk(factor, shift, image, image_next, pieces, after):
+def chunk(factor, shift, image, image_next, pieces, after, lasts=0):
     rows, (columns, width) = sum(piece.shape[0] for piece in pieces), image.shape
-    text = jax.ShapeDtypeStruct((rows, width), jnp.bfloat16)
+    text = [jax.ShapeDtypeStruct((r, width), jnp.bfloat16) for r in (rows, rows - lasts, lasts) if r]
     tile = jax.ShapeDtypeStruct((rows, columns), jnp.bfloat16)
     return pl.pallas_call(
-        functools.partial(chunk_kernel, len(pieces)),
-        out_shape=(text, text, tile, tile),
+        functools.partial(chunk_kernel, len(pieces), lasts),
+        out_shape=[text[0], tile, tile, *text[1:]],
         in_specs=[SMEM] * 2 + [VMEM] * (2 + len(pieces)) + [ANY] * len(after),
-        out_specs=(VMEM,) * 4,
+        out_specs=[VMEM] * (2 + len(text)),
         compiler_params=pltpu.CompilerParams(vmem_limit_bytes=16 * MIB),
         cost_estimate=pl.CostEstimate(
             flops=8 * rows * columns * width,
@@ -161,7 +165,7 @@
     text_grad = dot_tn(own, image)
 
     image_next = pass_on(image_next, [image_grad, text_grad])
-    sent0, part0, own0, next0 = chunk(factor, shift, image, image_next, part[:1], [])
+    part0, own0, next0, sent0 = chunk(factor, shift, image, image_next, part[:1], [])
     next_own = jax.nn.sigmoid(dot_nt(image_next, text) * scale + bias).astype(jnp.bfloat16)
     text_grad = scale * (text_grad + dot_tn(next_own, image_next))
     image_sent = dot_nn(next_own, text) + dot_tn(next0, part0)
@@ -170,16 +174,19 @@
     sent0 = pass_on(sent0, [part[1], image_sent])
     back0 = shifted(sent0, "blk", -1)
 
-    sent1, part1, own1, next1 = chunk(factor, shift, image, image_next, part[1:], [sent0])
+    lasts = part[2].shape[0]
+    part1, own1, next1, sent1, sent2 = chunk(factor, shift, image, image_next, part[1:], [sent0], lasts)
     image_sent = (scale * (image_sent + dot_tn(next1, part1))).astype(jnp.bfloat16)
     image_back = shifted(image_sent, "grp", 1)
     sent1 = pass_on(sent1, [image_sent])
     back1 = shifted(sent1, "blk", -1)
+    back2 = shifted(pass_on(sent2, [sent1]), "blk", -1)
     result, mark = add_rows(text_grad, back0, 0, None, [], mark=True)
     own1 = pass_on(own1, [mark])
     image_grad = scale * (image_grad + dot_tn(own1, part1))
     image_grad, mark = add_rows(image_grad, image_back, 0, None, [], mark=True)
     result = add_rows(text_grad, back1, cuts[1][0], result, [mark])
+    result = add_rows(text_grad, back2, cuts[2][0], result, [])
     return image_grad, result
 
 

time: 50.5 us -> 50.3 us (level)
  waiting for transfers between devices: 24.1 us -> 21.9 us
  starting transfers between devices: 8.93 us -> 10.2 us
  Pallas kernels: 6.01 us -> 6.65 us
    ppermute x7 -> x8, waiting for transfers between devices: 24.1 us -> 21.9 us  [shifted(): lax.ppermute(shard, axis, [(i, (i + by) % devices) for i in range(devices)])]
    ppermute x7 -> x8, starting transfers between devices: 8.93 us -> 10.2 us  [shifted(): lax.ppermute(shard, axis, [(i, (i + by) % devices) for i in range(devices)])]
    pallas_call x3 -> x4, Pallas kernels: 2.68 us -> 3.32 us  [add_rows(): pl.pallas_call(kernel, out_shape=(out, jax.ShapeDtypeStruct((8, 128), jnp...]
  transfers between devices with their start and end apart: 7 -> 8, of which waited for: 5 -> 5; matrix products, arithmetic and copies ran while one was open for 14% -> 14% of each run, Pallas kernels for 10% -> 12%
where the time goes in v18:
time: 50.3 us; the launch traced here: 50.1 us
  waiting for transfers between devices  21.9 us (44%)
  starting transfers between devices  10.2 us (20%)
  matrix products  6.97 us (14%)
  Pallas kernels  6.65 us (13%)
  local copies, waits for them, and re-layouts  2.2 us (4%)
  between operations  2.14 us (4%)
    ppermute x8, waiting for transfers between devices, shifted(): lax.ppermute(shard, axis, [(i, (i + by) % devices) for i in range(devices)])  21.9 us
    ppermute x8, starting transfers between devices, shifted(): lax.ppermute(shard, axis, [(i, (i + by) % devices) for i in range(devices)])  10.2 us
    dot_general x6, matrix products, dot_tn(): lax.dot_general(a, b, (((0,), (0,)), ((), ())), preferred_element_type=jn...  3.83 us
    pallas_call x4, Pallas kernels, add_rows(): pl.pallas_call(kernel, out_shape=(out, jax.ShapeDtypeStruct((8, 128), jnp...  3.32 us
    pallas_call x2, Pallas kernels, chunk(): pl.pallas_call(functools.partial(chunk_kernel, len(pieces), lasts), out_s...  3.08 us
    dot_general x2, matrix products, dot_nt(): lax.dot_general(a, b, (((1,), (1,)), ((), ())), preferred_element_type=jn...  1.72 us
    dot_general x2, matrix products, dot_nn(): return jnp.dot(a, b, preferred_element_type=jnp.float32)  1.42 us
    unnamed x8, local copies, waits for them, and re-layouts  1.2 us
  transfers between devices with their start and end apart: 8, of which 5 were waited for; matrix products, arithmetic and copies ran while one was open for 14% of the time, Pallas kernels for 12%

profile of v18, /device:TPU:0, one launch (start us, length us, event | category | flops | bytes accessed | tf_op | source)
XLA Modules:
  0.0 50.1 jit_solution(4031764063031088144)
XLA Ops:
  0.6 1.0 %slice.3.refs_0_ = bf16[128,1152]{1,0:T(8,128)(2,1)S(1)} slice(bf16[416,1152]{1,0:T(8,128)(2,1)} %array_ref.5), slice={[0:128], [0:1152]} | slice | bytes 589824 | tf_op jit(solution)/shard_map/slice | solution.py:154
  1.6 3.0 %collective-permute-start = (bf16[128,1152]{1,0:T(8,128)(2,1)S(1)}, bf16[128,1152]{1,0:T(8,128)(2,1)S(1)}, u32[]{:S(2)}, u32[]{:S(2)}) collective-permute-start(bf16[128,1152]{1,0:T(8,128)(2,1)S(1)} %slice.3.refs_0_), channel_id=1, source_target_pairs={{0,4},{4,8},{8,12},{12,16},{16,20},{20,24},{24,28},{28,0},{1,5},{5... | collective-permute-start | bytes 884744 | tf_op jit(solution)/shard_map/ppermute | solution.py:20
  4.6 0.7 %collective-permute-start.1 = (bf16[416,1152]{1,0:T(8,128)(2,1)}, bf16[416,1152]{1,0:T(8,128)(2,1)S(1)}, u32[]{:S(2)}, u32[]{:S(2)}) collective-permute-start(bf16[416,1152]{1,0:T(8,128)(2,1)} %image_ref.3), channel_id=1, source_target_pairs={{0,3},{1,0},{2,1},{3,2},{4,7},{5,4},{6,5},{7,6},{8,11},{9,8},{10,9... | collective-permute-start | bytes 2875400 | tf_op jit(solution)/shard_map/ppermute | solution.py:20
  5.3 1.2 %copy-done = bf16[416,1152]{1,0:T(8,128)(2,1)S(1)} copy-done((bf16[416,1152]{1,0:T(8,128)(2,1)S(1)}, bf16[416,1152]{1,0:T(8,128)(2,1)}, u32[]{:S(2)}) %copy-start) | copy-done | bytes 958488
  6.5 0.1 fetch.4
  6.6 1.6 %collective-permute-start.2 = (bf16[240,1152]{1,0:T(8,128)(2,1)S(1)}, bf16[240,1152]{1,0:T(8,128)(2,1)S(1)}, u32[]{:S(2)}, u32[]{:S(2)}) collective-permute-start(bf16[240,1152]{1,0:T(8,128)(2,1)S(1)} %fetch.4), channel_id=1, source_target_pairs={{0,4},{4,8},{8,12},{12,16},{16,20},{20,24},{24,28},{28,0},{1,5},{5... | collective-permute-start | bytes 1658888 | tf_op jit(solution)/shard_map/ppermute | solution.py:20
  9.5 6.0 %collective-permute-done.refs_0_ = bf16[128,1152]{1,0:T(8,128)(2,1)S(1)} collective-permute-done((bf16[128,1152]{1,0:T(8,128)(2,1)S(1)}, bf16[128,1152]{1,0:T(8,128)(2,1)S(1)}, u32[]{:S(2)}, u32[]{:S(2)}) %collective-permute-start) | collective-permute-done | bytes 294944 | tf_op jit(solution)/shard_map/ppermute | solution.py:20
  15.5 0.9 %subtract_convert_fusion.refs_0_ = bf16[416,416]{1,0:T(8,128)(2,1)S(1)} fusion(s32[416]{0:T(512)S(1)} %bitcast.30, f32[]{:T(128)} %bitcast.28, bf16[416,1152]{1,0:T(8,128)(2,1)S(1)} %copy-done.2, bf16[416,1152]{1,0:T(8,128)(2,1)S(1)} %copy-done.1, f32[]{:T(128)} %bitcast.24), kind=kOutput, calls=%fused_computation.22 | convolution fusion | flops 400278528 | bytes 2264712 | tf_op jit(solution)/shard_map/dot_general | solution.py:24
  16.4 0.2 fetch.5
  16.6 0.1 collective-permute-start.3
  16.7 0.7 %fusion.17.refs_2_ = f32[416,1152]{1,0:T(8,128)S(1)} fusion(bf16[416,416]{1,0:T(8,128)(2,1)S(1)} %subtract_convert_fusion.refs_0_, bf16[416,1152]{1,0:T(8,128)(2,1)S(1)} %copy-done.2), kind=kOutput, calls=%fused_computation.25 | convolution fusion | flops 398721024 | bytes 3221504 | tf_op jit(solution)/shard_map/dot_general | solution.py:28
  17.4 0.7 %fusion.16.refs_1_ = f32[416,1152]{1,0:T(8,128)S(1)} fusion(bf16[416,416]{1,0:T(8,128)(2,1)S(1)} %subtract_convert_fusion.refs_0_, bf16[416,1152]{1,0:T(8,128)(2,1)S(1)} %copy-done.1), kind=kOutput, calls=%fused_computation.24 | convolution fusion | flops 398721024 | bytes 3221504 | tf_op jit(solution)/shard_map/dot_general | solution.py:32
  18.1 0.8 %fusion.15 = bf16[416,416]{1,0:T(8,128)(2,1)S(1)} fusion(bf16[416,1152]{1,0:T(8,128)(2,1)S(1)} %pass_on.5.next_ref, bf16[416,1152]{1,0:T(8,128)(2,1)S(1)} %copy-done.1, f32[]{:T(128)} %bitcast.29, f32[]{:T(128)} %bitcast.27), kind=kOutput, calls=%fused_computation.21 | convolution fusion | flops 399759360 | bytes 2263048 | tf_op jit(solution)/shard_map/dot_general | solution.py:24
  19.0 1.2 %chunk.2 = (bf16[128,1152]{1,0:T(8,128)(2,1)S(1)}, bf16[128,416]{1,0:T(8,128)(2,1)S(1)}, bf16[128,416]{1,0:T(8,128)(2,1)S(1)}, bf16[128,1152]{1,0:T(8,128)(2,1)S(1)}) custom-call(f32[1]{0:T(128)} %copy.21.scale_ref, f32[1]{0:T(128)} %copy.22.bias_ref, bf16[416,1152]{1,0:T(8,128)(2,1)S(1)} %copy-done.2, bf16[416,1152]{1,0:T(8,128)(2,1)S(1)} %pass_on.5.next_ref, ...), custom_call_target="tpu_custom_call" | custom-call | flops 490733568 | bytes 2801664 | tf_op jit(solution)/shard_map/chunk/pallas_call | solution.py:99
  20.2 0.7 %fusion.18 = f32[416,1152]{1,0:T(8,128)S(1)} fusion(bf16[416,416]{1,0:T(8,128)(2,1)S(1)} %fusion.15, bf16[416,1152]{1,0:T(8,128)(2,1)S(1)} %copy-done.1), kind=kOutput, calls=%fused_computation.26 | convolution fusion | flops 398721024 | bytes 3221504 | tf_op jit(solution)/shard_map/dot_general | solution.py:32
  20.9 0.4 convolution_add_fusion.1.refs_2_
  21.4 6.0 %collective-permute-done.2.refs_1_.refs_0_ = bf16[240,1152]{1,0:T(8,128)(2,1)S(1)} collective-permute-done((bf16[240,1152]{1,0:T(8,128)(2,1)S(1)}, bf16[240,1152]{1,0:T(8,128)(2,1)S(1)}, u32[]{:S(2)}, u32[]{:S(2)}) %collective-permute-start.2) | collective-permute-done | bytes 552992 | tf_op jit(solution)/shard_map/ppermute | solution.py:20
  27.4 2.1 %collective-permute-start.4 = (bf16[128,1152]{1,0:T(8,128)(2,1)S(1)}, bf16[128,1152]{1,0:T(8,128)(2,1)S(1)}, u32[]{:S(2)}, u32[]{:S(2)}) collective-permute-start(bf16[128,1152]{1,0:T(8,128)(2,1)S(1)} %pass_on.6.refs_2_), channel_id=1, source_target_pairs={{0,28},{4,0},{8,4},{12,8},{16,12},{20,16},{24,20},{28,24},{1,29},{... | collective-permute-start | bytes 884744 | tf_op jit(solution)/shard_map/ppermute | solution.py:20
  29.4 1.9 %chunk.3 = (bf16[288,1152]{1,0:T(8,128)(2,1)S(1)}, bf16[288,416]{1,0:T(8,128)(2,1)S(1)}, bf16[288,416]{1,0:T(8,128)(2,1)S(1)}, bf16[240,1152]{1,0:T(8,128)(2,1)S(1)}, bf16[48,1152]{1,0:T(8,128)(2,1)S(1)}) custom-call(f32[1]{0:T(128)} %copy.21.scale_ref, f32[1]{0:T(128)} %copy.22.bias_ref, bf16[416,1152]{1,0:T(8,128)(2,1)S(1)} %copy-done.2, ...), custom_call_target="tpu_custom_call" | custom-call | flops 1104150528 | bytes 3907584 | tf_op jit(solution)/shard_map/chunk/pallas_call | solution.py:99
  31.3 0.7 %fusion.4.refs_1_ = bf16[416,1152]{1,0:T(8,128)(2,1)S(1)} fusion(f32[416,1152]{1,0:T(8,128)S(1)} %convolution_add_fusion.1.refs_2_, bf16[288,416]{1,0:T(8,128)(2,1)S(1)} %get-tuple-element.22, bf16[288,1152]{1,0:T(8,128)(2,1)S(1)} %get-tuple-element.21, f32[]{:T(128)} %bitcast.25), kind=kOutput, calls=%fused_computation.8 | convolution fusion | flops 277475328 | bytes 3778564 | tf_op jit(solution)/shard_map/dot_general | solution.py:28
  32.1 1.5 %collective-permute-start.7 = (bf16[240,1152]{1,0:T(8,128)(2,1)S(1)}, bf16[240,1152]{1,0:T(8,128)(2,1)S(1)}, u32[]{:S(2)}, u32[]{:S(2)}) collective-permute-start(bf16[240,1152]{1,0:T(8,128)(2,1)S(1)} %pass_on.8.refs_1_), channel_id=1, source_target_pairs={{0,28},{4,0},{8,4},{12,8},{16,12},{20,16},{24,20},{28,24},{1,29},{... | collective-permute-start | bytes 1658888 | tf_op jit(solution)/shard_map/ppermute | solution.py:20
  33.6 1.3 %collective-permute-start.6 = (bf16[48,1152]{1,0:T(8,128)(2,1)S(1)}, bf16[48,1152]{1,0:T(8,128)(2,1)S(1)}, u32[]{:S(2)}, u32[]{:S(2)}) collective-permute-start(bf16[48,1152]{1,0:T(8,128)(2,1)S(1)} %pass_on.9), channel_id=1, source_target_pairs={{0,28},{4,0},{8,4},{12,8},{16,12},{20,16},{24,20},{28,24},{1,29},{... | collective-permute-start | bytes 331784 | tf_op jit(solution)/shard_map/ppermute | solution.py:20
  34.9 0.8 %fusion.total_ref = f32[416,1152]{1,0:T(8,128)S(1)} fusion(f32[416,1152]{1,0:T(8,128)S(1)} %fusion.17.refs_2_, bf16[416,416]{1,0:T(8,128)(2,1)S(1)} %fusion.15, bf16[416,1152]{1,0:T(8,128)(2,1)S(1)} %pass_on.5.next_ref, f32[]{:T(128)} %bitcast.23), kind=kOutput, calls=%fused_computation.1 | convolution fusion | flops 399679488 | bytes 5138436 | tf_op jit(solution)/shard_map/dot_general | solution.py:28
  35.7 0.8 %add_rows.4 = (bf16[416,1152]{1,0:T(8,128)(2,1)}, f32[8,128]{1,0:T(8,128)S(1)}) custom-call(f32[416,1152]{1,0:T(8,128)S(1)} %fusion.total_ref, bf16[128,1152]{1,0:T(8,128)(2,1)S(1)} %collective-permute-done.4.back_ref), custom_call_target="tpu_custom_call" | custom-call | tf_op jit(solution)/shard_map/add_rows/pallas_call | solution.py:138
  36.5 0.7 %fusion.19 = f32[416,1152]{1,0:T(8,128)S(1)} fusion(bf16[288,416]{1,0:T(8,128)(2,1)S(1)} %pass_on.7, bf16[288,1152]{1,0:T(8,128)(2,1)S(1)} %get-tuple-element.21), kind=kOutput, calls=%fused_computation.27 | convolution fusion | flops 276037632 | bytes 2820096 | tf_op jit(solution)/shard_map/dot_general | solution.py:28
  37.2 0.4 fusion.2.total_ref
  37.6 7.7 %collective-permute-done.5.back_ref = bf16[416,1152]{1,0:T(8,128)(2,1)S(1)} collective-permute-done((bf16[416,1152]{1,0:T(8,128)(2,1)S(1)}, bf16[416,1152]{1,0:T(8,128)(2,1)S(1)}, u32[]{:S(2)}, u32[]{:S(2)}) %collective-permute-start.5) | collective-permute-done | bytes 958496 | tf_op jit(solution)/shard_map/ppermute | solution.py:20
  45.3 1.0 %add_rows.5 = (bf16[416,1152]{1,0:T(8,128)(2,1)}, f32[8,128]{1,0:T(8,128)S(1)}) custom-call(f32[416,1152]{1,0:T(8,128)S(1)} %fusion.2.total_ref, bf16[416,1152]{1,0:T(8,128)(2,1)S(1)} %collective-permute-done.5.back_ref), custom_call_target="tpu_custom_call" | custom-call | tf_op jit(solution)/shard_map/add_rows/pallas_call | solution.py:138
  46.4 0.7 %collective-permute-done.7.back_ref = bf16[240,1152]{1,0:T(8,128)(2,1)S(1)} collective-permute-done((bf16[240,1152]{1,0:T(8,128)(2,1)S(1)}, bf16[240,1152]{1,0:T(8,128)(2,1)S(1)}, u32[]{:S(2)}, u32[]{:S(2)}) %collective-permute-start.7) | collective-permute-done | bytes 552992 | tf_op jit(solution)/shard_map/ppermute | solution.py:20
  47.0 0.9 %add_rows.6.refs_0_ = bf16[416,1152]{1,0:T(8,128)(2,1)} custom-call(f32[416,1152]{1,0:T(8,128)S(1)} %fusion.total_ref, bf16[240,1152]{1,0:T(8,128)(2,1)S(1)} %collective-permute-done.7.back_ref, bf16[416,1152]{1,0:T(8,128)(2,1)} %get-tuple-element.26.refs_0_, f32[8,128]{1,0:T(8,128)S(1)} %get-tuple-element.27.refs_1_), custom_call_target="tpu_custom_call", output_to_operand_aliasing={{}: (2, {})} | custom-call | tf_op jit(solution)/shard_map/add_rows/pallas_call | solution.py:138
  47.9 1.5 %collective-permute-done.6.back_ref = bf16[48,1152]{1,0:T(8,128)(2,1)S(1)} collective-permute-done((bf16[48,1152]{1,0:T(8,128)(2,1)S(1)}, bf16[48,1152]{1,0:T(8,128)(2,1)S(1)}, u32[]{:S(2)}, u32[]{:S(2)}) %collective-permute-start.6) | collective-permute-done | bytes 110624 | tf_op jit(solution)/shard_map/ppermute | solution.py:20
  49.4 0.7 %add_rows.7 = bf16[416,1152]{1,0:T(8,128)(2,1)} custom-call(f32[416,1152]{1,0:T(8,128)S(1)} %fusion.total_ref, bf16[48,1152]{1,0:T(8,128)(2,1)S(1)} %collective-permute-done.6.back_ref, bf16[416,1152]{1,0:T(8,128)(2,1)} %add_rows.6.refs_0_), custom_call_target="tpu_custom_call", output_to_operand_aliasing={{}: (2, {})} | custom-call | tf_op jit(solution)/shard_map/add_rows/pallas_call | solution.py:138
  (17 shorter events, 0.1 us)
Async XLA Ops:
  0.6 14.9 %copy-start.3 = (s32[1,416]{1,0:T(1,128)S(1)}, s32[1,416]{1,0:T(1,128)}, u32[]{:S(2)}) copy-start(s32[1,416]{1,0:T(1,128)} %array_ref.3) | copy-start | bytes 4996
  1.6 13.9 %collective-permute-start = (bf16[128,1152]{1,0:T(8,128)(2,1)S(1)}, bf16[128,1152]{1,0:T(8,128)(2,1)S(1)}, u32[]{:S(2)}, u32[]{:S(2)}) collective-permute-start(bf16[128,1152]{1,0:T(8,128)(2,1)S(1)} %slice.3.refs_0_), channel_id=1, source_target_pairs={{0,4},{4,8},{8,12},{12,16},{16,20},{20,24},{24,28},{28,0},{1,5},{5... | collective-permute-start | bytes 884744 | tf_op jit(solution)/shard_map/ppermute | solution.py:20
  4.6 13.5 %collective-permute-start.1 = (bf16[416,1152]{1,0:T(8,128)(2,1)}, bf16[416,1152]{1,0:T(8,128)(2,1)S(1)}, u32[]{:S(2)}, u32[]{:S(2)}) collective-permute-start(bf16[416,1152]{1,0:T(8,128)(2,1)} %image_ref.3), channel_id=1, source_target_pairs={{0,3},{1,0},{2,1},{3,2},{4,7},{5,4},{6,5},{7,6},{8,11},{9,8},{10,9... | collective-permute-start | bytes 2875400 | tf_op jit(solution)/shard_map/ppermute | solution.py:20
  5.3 1.2 %copy-start = (bf16[416,1152]{1,0:T(8,128)(2,1)S(1)}, bf16[416,1152]{1,0:T(8,128)(2,1)}, u32[]{:S(2)}) copy-start(bf16[416,1152]{1,0:T(8,128)(2,1)} %array_ref.5) | copy-start | bytes 2875396
  6.5 9.0 %copy-start.1 = (bf16[416,1152]{1,0:T(8,128)(2,1)S(1)}, bf16[416,1152]{1,0:T(8,128)(2,1)}, u32[]{:S(2)}) copy-start(bf16[416,1152]{1,0:T(8,128)(2,1)} %array_ref.5) | copy-start | bytes 2875396
  6.5 9.0 %copy-start.2 = (bf16[416,1152]{1,0:T(8,128)(2,1)S(1)}, bf16[416,1152]{1,0:T(8,128)(2,1)}, u32[]{:S(2)}) copy-start(bf16[416,1152]{1,0:T(8,128)(2,1)} %image_ref.3) | copy-start | bytes 2875396
  6.6 20.8 %collective-permute-start.2 = (bf16[240,1152]{1,0:T(8,128)(2,1)S(1)}, bf16[240,1152]{1,0:T(8,128)(2,1)S(1)}, u32[]{:S(2)}, u32[]{:S(2)}) collective-permute-start(bf16[240,1152]{1,0:T(8,128)(2,1)S(1)} %fetch.4), channel_id=1, source_target_pairs={{0,4},{4,8},{8,12},{12,16},{16,20},{20,24},{24,28},{28,0},{1,5},{5... | collective-permute-start | bytes 1658888 | tf_op jit(solution)/shard_map/ppermute | solution.py:20
  16.6 12.8 %collective-permute-start.3 = (bf16[48,1152]{1,0:T(8,128)(2,1)S(1)}, bf16[48,1152]{1,0:T(8,128)(2,1)S(1)}, u32[]{:S(2)}, u32[]{:S(2)}) collective-permute-start(bf16[48,1152]{1,0:T(8,128)(2,1)S(1)} %fetch.5), channel_id=1, source_target_pairs={{0,4},{4,8},{8,12},{12,16},{16,20},{20,24},{24,28},{28,0},{1,5},{5... | collective-permute-start | bytes 331784 | tf_op jit(solution)/shard_map/ppermute | solution.py:20
  27.4 8.3 %collective-permute-start.4 = (bf16[128,1152]{1,0:T(8,128)(2,1)S(1)}, bf16[128,1152]{1,0:T(8,128)(2,1)S(1)}, u32[]{:S(2)}, u32[]{:S(2)}) collective-permute-start(bf16[128,1152]{1,0:T(8,128)(2,1)S(1)} %pass_on.6.refs_2_), channel_id=1, source_target_pairs={{0,28},{4,0},{8,4},{12,8},{16,12},{20,16},{24,20},{28,24},{1,29},{... | collective-permute-start | bytes 884744 | tf_op jit(solution)/shard_map/ppermute | solution.py:20
  32.0 13.3 %collective-permute-start.5 = (bf16[416,1152]{1,0:T(8,128)(2,1)S(1)}, bf16[416,1152]{1,0:T(8,128)(2,1)S(1)}, u32[]{:S(2)}, u32[]{:S(2)}) collective-permute-start(bf16[416,1152]{1,0:T(8,128)(2,1)S(1)} %fusion.4.refs_1_), channel_id=1, source_target_pairs={{0,1},{1,2},{2,3},{3,0},{4,5},{5,6},{6,7},{7,4},{8,9},{9,10},{10,1... | collective-permute-start | bytes 2875400 | tf_op jit(solution)/shard_map/ppermute | solution.py:20
  32.1 14.9 %collective-permute-start.7 = (bf16[240,1152]{1,0:T(8,128)(2,1)S(1)}, bf16[240,1152]{1,0:T(8,128)(2,1)S(1)}, u32[]{:S(2)}, u32[]{:S(2)}) collective-permute-start(bf16[240,1152]{1,0:T(8,128)(2,1)S(1)} %pass_on.8.refs_1_), channel_id=1, source_target_pairs={{0,28},{4,0},{8,4},{12,8},{16,12},{20,16},{24,20},{28,24},{1,29},{... | collective-permute-start | bytes 1658888 | tf_op jit(solution)/shard_map/ppermute | solution.py:20
  33.6 15.8 %collective-permute-start.6 = (bf16[48,1152]{1,0:T(8,128)(2,1)S(1)}, bf16[48,1152]{1,0:T(8,128)(2,1)S(1)}, u32[]{:S(2)}, u32[]{:S(2)}) collective-permute-start(bf16[48,1152]{1,0:T(8,128)(2,1)S(1)} %pass_on.9), channel_id=1, source_target_pairs={{0,28},{4,0},{8,4},{12,8},{16,12},{20,16},{24,20},{28,24},{1,29},{... | collective-permute-start | bytes 331784 | tf_op jit(solution)/shard_map/ppermute | solution.py:20

commit v19 on v18

--- a/solution.py
+++ b/solution.py
@@ -8,7 +8,7 @@
 from jax.sharding import PartitionSpec as P
 
 MIB = 2**20
-ENDS = (8, 23)
+ENDS = (6, 12, 23)
 SMEM = pl.BlockSpec(memory_space=pltpu.SMEM)
 VMEM = pl.BlockSpec(memory_space=pltpu.VMEM)
 HBM = pl.BlockSpec(memory_space=pltpu.HBM)
@@ -64,6 +64,7 @@
         out_specs=ANY,
         input_output_aliases={0: 0},
         compiler_params=pltpu.CompilerParams(vmem_limit_bytes=MIB),
+        cost_estimate=pl.CostEstimate(flops=0, bytes_accessed=0, transcendentals=0),
         name="pass_on",
     )(array, *after)
 
@@ -151,21 +152,23 @@
     scale = factor[0]
     bias = shift[0]
     cuts = row_cuts(text.shape[0])
+    around = shifted(text[slice(*cuts[1])], "blk", -1)
     first = text[: cuts[0][1]]
     part = [shifted(first, "blk", 1)]
     image_next = shifted(image, "grp", -1)
-    part.append(shifted(fetch(text, *cuts[1], [first]), "blk", 1))
-
-    target = fetch(target, 0, 1, [part[0]])
+    part.append(shifted(fetch(text, *cuts[2], [first]), "blk", 1))
+
+    target = fetch(target, 0, 1, [around, part[0]])
+    around = shifted(around, "blk", 2)
     own = jax.nn.sigmoid(dot_nt(image, text) * scale + bias)
     column = lax.broadcasted_iota(jnp.int32, own.shape, 1)
     own = (own - (column == target[0][:, None]).astype(jnp.float32)).astype(jnp.bfloat16)
-    part.append(shifted(fetch(text, *cuts[2], [own]), "blk", 1))
     image_grad = dot_nn(own, text)
     text_grad = dot_tn(own, image)
 
     image_next = pass_on(image_next, [image_grad, text_grad])
-    part0, own0, next0, sent0 = chunk(factor, shift, image, image_next, part[:1], [])
+    part.append(shifted(fetch(text, *cuts[3], [image_next]), "blk", 1))
+    part0, own0, next0, sent0 = chunk(factor, shift, image, image_next, [part[0], around], [])
     next_own = jax.nn.sigmoid(dot_nt(image_next, text) * scale + bias).astype(jnp.bfloat16)
     text_grad = scale * (text_grad + dot_tn(next_own, image_next))
     image_sent = dot_nn(next_own, text) + dot_tn(next0, part0)
@@ -185,8 +188,8 @@
     own1 = pass_on(own1, [mark])
     image_grad = scale * (image_grad + dot_tn(own1, part1))
     image_grad, mark = add_rows(image_grad, image_back, 0, None, [], mark=True)
-    result = add_rows(text_grad, back1, cuts[1][0], result, [mark])
-    result = add_rows(text_grad, back2, cuts[2][0], result, [])
+    result = add_rows(text_grad, back1, cuts[2][0], result, [mark])
+    result = add_rows(text_grad, back2, text.shape[0] - lasts, result, [])
     return image_grad, result
 
 

time: 50.3 us -> 56.9 us (1.13)
  starting transfers between devices: 10.2 us -> 24 us
  waiting for transfers between devices: 21.9 us -> 14.8 us
    ppermute x8 -> x10, starting transfers between devices: 10.2 us -> 24 us  [shifted(): lax.ppermute(shard, axis, [(i, (i + by) % devices) for i in range(devices)])]
    ppermute x8 -> x10, waiting for transfers between devices: 21.9 us -> 14.8 us  [shifted(): lax.ppermute(shard, axis, [(i, (i + by) % devices) for i in range(devices)])]
  transfers between devices with their start and end apart: 8 -> 10, of which waited for: 5 -> 6; matrix products, arithmetic and copies ran while one was open for 14% -> 12% of each run, Pallas kernels for 12% -> 10%
where the time goes in v19:
time: 56.9 us; the launch traced here: 56.7 us
  starting transfers between devices  24 us (42%)
  waiting for transfers between devices  14.8 us (26%)
  matrix products  6.7 us (12%)
  Pallas kernels  6.57 us (12%)
  local copies, waits for them, and re-layouts  2.29 us (4%)
  between operations  2.29 us (4%)
    ppermute x10, starting transfers between devices, shifted(): lax.ppermute(shard, axis, [(i, (i + by) % devices) for i in range(devices)])  24 us
    ppermute x10, waiting for transfers between devices, shifted(): lax.ppermute(shard, axis, [(i, (i + by) % devices) for i in range(devices)])  14.8 us
    dot_general x6, matrix products, dot_tn(): lax.dot_general(a, b, (((0,), (0,)), ((), ())), preferred_element_type=jn...  3.55 us
    pallas_call x4, Pallas kernels, add_rows(): pl.pallas_call(kernel, out_shape=(out, jax.ShapeDtypeStruct((8, 128), jnp...  3.31 us
    pallas_call x2, Pallas kernels, chunk(): pl.pallas_call(functools.partial(chunk_kernel, len(pieces), lasts), out_s...  2.88 us
    dot_general x2, matrix products, dot_nt(): lax.dot_general(a, b, (((1,), (1,)), ((), ())), preferred_element_type=jn...  1.72 us
    dot_general x2, matrix products, dot_nn(): return jnp.dot(a, b, preferred_element_type=jnp.float32)  1.43 us
    unnamed x8, local copies, waits for them, and re-layouts  1.2 us
  transfers between devices with their start and end apart: 10, of which 6 were waited for; matrix products, arithmetic and copies ran while one was open for 12% of the time, Pallas kernels for 10%

profile of v19, /device:TPU:0, one launch (start us, length us, event | category | flops | bytes accessed | tf_op | source)
XLA Modules:
  0.0 56.7 jit_solution(13128373793974861449)
XLA Ops:
  0.6 1.1 %fusion.16 = (bf16[96,1152]{1,0:T(8,128)(2,1)S(1)}, bf16[96,1152]{1,0:T(8,128)(2,1)S(1)}) fusion(bf16[416,1152]{1,0:T(8,128)(2,1)} %array_ref.5), kind=kLoop, calls=%fused_computation.24 | loop fusion | bytes 884736 | tf_op jit(solution)/shard_map/slice | solution.py:156
  1.7 6.0 %collective-permute-start = (bf16[96,1152]{1,0:T(8,128)(2,1)S(1)}, bf16[96,1152]{1,0:T(8,128)(2,1)S(1)}, u32[]{:S(2)}, u32[]{:S(2)}) collective-permute-start(bf16[96,1152]{1,0:T(8,128)(2,1)S(1)} %get-tuple-element.29), channel_id=1, source_target_pairs={{0,28},{4,0},{8,4},{12,8},{16,12},{20,16},{24,20},{28,24},{1,29},{... | collective-permute-start | bytes 663560 | tf_op jit(solution)/shard_map/ppermute | solution.py:20
  7.8 0.7 %collective-permute-start.2 = (bf16[416,1152]{1,0:T(8,128)(2,1)}, bf16[416,1152]{1,0:T(8,128)(2,1)S(1)}, u32[]{:S(2)}, u32[]{:S(2)}) collective-permute-start(bf16[416,1152]{1,0:T(8,128)(2,1)} %image_ref.3), channel_id=1, source_target_pairs={{0,3},{1,0},{2,1},{3,2},{4,7},{5,4},{6,5},{7,6},{8,11},{9,8},{10,9... | collective-permute-start | bytes 2875400 | tf_op jit(solution)/shard_map/ppermute | solution.py:20
  8.4 1.2 %copy-done = bf16[416,1152]{1,0:T(8,128)(2,1)S(1)} copy-done((bf16[416,1152]{1,0:T(8,128)(2,1)S(1)}, bf16[416,1152]{1,0:T(8,128)(2,1)}, u32[]{:S(2)}) %copy-start) | copy-done | bytes 958488
  9.6 0.2 fetch.4
  11.3 1.1 %collective-permute-done.refs_0_ = bf16[96,1152]{1,0:T(8,128)(2,1)S(1)} collective-permute-done((bf16[96,1152]{1,0:T(8,128)(2,1)S(1)}, bf16[96,1152]{1,0:T(8,128)(2,1)S(1)}, u32[]{:S(2)}, u32[]{:S(2)}) %collective-permute-start) | collective-permute-done | bytes 221216 | tf_op jit(solution)/shard_map/ppermute | solution.py:20
  12.4 13.0 %collective-permute-start.3 = (bf16[96,1152]{1,0:T(8,128)(2,1)S(1)}, bf16[96,1152]{1,0:T(8,128)(2,1)S(1)}, u32[]{:S(2)}, u32[]{:S(2)}) collective-permute-start(bf16[96,1152]{1,0:T(8,128)(2,1)S(1)} %collective-permute-done.refs_0_), channel_id=1, source_target_pairs={{0,8},{4,12},{8,16},{12,20},{16,24},{20,28},{24,0},{28,4},{1,9},{5... | collective-permute-start | bytes 663560 | tf_op jit(solution)/shard_map/ppermute | solution.py:20
  25.4 0.9 %subtract_convert_fusion = bf16[416,416]{1,0:T(8,128)(2,1)S(1)} fusion(s32[416]{0:T(512)S(1)} %bitcast.30, f32[]{:T(128)} %bitcast.28, bf16[416,1152]{1,0:T(8,128)(2,1)S(1)} %copy-done.2, bf16[416,1152]{1,0:T(8,128)(2,1)S(1)} %copy-done.1, f32[]{:T(128)} %bitcast.24), kind=kOutput, calls=%fused_computation.22 | convolution fusion | flops 400278528 | bytes 2264712 | tf_op jit(solution)/shard_map/dot_general | solution.py:24
  26.3 0.8 %fusion.18.refs_2_ = f32[416,1152]{1,0:T(8,128)S(1)} fusion(bf16[416,416]{1,0:T(8,128)(2,1)S(1)} %subtract_convert_fusion, bf16[416,1152]{1,0:T(8,128)(2,1)S(1)} %copy-done.2), kind=kOutput, calls=%fused_computation.26 | convolution fusion | flops 398721024 | bytes 3221504 | tf_op jit(solution)/shard_map/dot_general | solution.py:28
  27.1 0.7 %fusion.17.refs_1_ = f32[416,1152]{1,0:T(8,128)S(1)} fusion(bf16[416,416]{1,0:T(8,128)(2,1)S(1)} %subtract_convert_fusion, bf16[416,1152]{1,0:T(8,128)(2,1)S(1)} %copy-done.1), kind=kOutput, calls=%fused_computation.25 | convolution fusion | flops 398721024 | bytes 3221504 | tf_op jit(solution)/shard_map/dot_general | solution.py:32
  27.8 0.2 fetch.5
  28.1 0.8 %fusion.15 = bf16[416,416]{1,0:T(8,128)(2,1)S(1)} fusion(bf16[416,1152]{1,0:T(8,128)(2,1)S(1)} %pass_on.5.next_ref.refs_0_, bf16[416,1152]{1,0:T(8,128)(2,1)S(1)} %copy-done.1, f32[]{:T(128)} %bitcast.29, f32[]{:T(128)} %bitcast.27), kind=kOutput, calls=%fused_computation.21 | convolution fusion | flops 399759360 | bytes 2263048 | tf_op jit(solution)/shard_map/dot_general | solution.py:24
  28.9 0.7 %fusion.19 = f32[416,1152]{1,0:T(8,128)S(1)} fusion(bf16[416,416]{1,0:T(8,128)(2,1)S(1)} %fusion.15, bf16[416,1152]{1,0:T(8,128)(2,1)S(1)} %copy-done.1), kind=kOutput, calls=%fused_computation.27 | convolution fusion | flops 398721024 | bytes 3221504 | tf_op jit(solution)/shard_map/dot_general | solution.py:32
  29.6 2.3 %collective-permute-done.3.refs_1_ = bf16[96,1152]{1,0:T(8,128)(2,1)S(1)} collective-permute-done((bf16[96,1152]{1,0:T(8,128)(2,1)S(1)}, bf16[96,1152]{1,0:T(8,128)(2,1)S(1)}, u32[]{:S(2)}, u32[]{:S(2)}) %collective-permute-start.3) | collective-permute-done | bytes 221216 | tf_op jit(solution)/shard_map/ppermute | solution.py:20
  32.0 1.4 %chunk.2 = (bf16[192,1152]{1,0:T(8,128)(2,1)S(1)}, bf16[192,416]{1,0:T(8,128)(2,1)S(1)}, bf16[192,416]{1,0:T(8,128)(2,1)S(1)}, bf16[192,1152]{1,0:T(8,128)(2,1)S(1)}) custom-call(f32[1]{0:T(128)} %copy.21.scale_ref, f32[1]{0:T(128)} %copy.22.bias_ref, bf16[416,1152]{1,0:T(8,128)(2,1)S(1)} %copy-done.2, bf16[416,1152]{1,0:T(8,128)(2,1)S(1)} %pass_on.5.next_ref.refs_0_, ...), custom_call_target="tpu_custom_call" | custom-call | flops 736100352 | bytes 3244032 | tf_op jit(solution)/shard_map/chunk/pallas_call | solution.py:100
  33.4 0.5 convolution_add_fusion.1.refs_2_
  33.9 2.4 %collective-permute-start.6 = (bf16[192,1152]{1,0:T(8,128)(2,1)S(1)}, bf16[192,1152]{1,0:T(8,128)(2,1)S(1)}, u32[]{:S(2)}, u32[]{:S(2)}) collective-permute-start(bf16[192,1152]{1,0:T(8,128)(2,1)S(1)} %pass_on.6.refs_2_), channel_id=1, source_target_pairs={{0,28},{4,0},{8,4},{12,8},{16,12},{20,16},{24,20},{28,24},{1,29},{... | collective-permute-start | bytes 1327112 | tf_op jit(solution)/shard_map/ppermute | solution.py:20
  36.3 1.5 %chunk.3 = (bf16[224,1152]{1,0:T(8,128)(2,1)S(1)}, bf16[224,416]{1,0:T(8,128)(2,1)S(1)}, bf16[224,416]{1,0:T(8,128)(2,1)S(1)}, bf16[176,1152]{1,0:T(8,128)(2,1)S(1)}, bf16[48,1152]{1,0:T(8,128)(2,1)S(1)}) custom-call(f32[1]{0:T(128)} %copy.21.scale_ref, f32[1]{0:T(128)} %copy.22.bias_ref, bf16[416,1152]{1,0:T(8,128)(2,1)S(1)} %copy-done.2, ...), custom_call_target="tpu_custom_call" | custom-call | flops 858783744 | bytes 3465216 | tf_op jit(solution)/shard_map/chunk/pallas_call | solution.py:100
  37.8 0.5 fusion.4.refs_1_
  38.4 0.8 %fusion.total_ref = f32[416,1152]{1,0:T(8,128)S(1)} fusion(f32[416,1152]{1,0:T(8,128)S(1)} %fusion.18.refs_2_, bf16[416,416]{1,0:T(8,128)(2,1)S(1)} %fusion.15, bf16[416,1152]{1,0:T(8,128)(2,1)S(1)} %pass_on.5.next_ref.refs_0_, f32[]{:T(128)} %bitcast.23), kind=kOutput, calls=%fused_computation.1 | convolution fusion | flops 399679488 | bytes 5138436 | tf_op jit(solution)/shard_map/dot_general | solution.py:28
  39.2 0.9 %collective-permute-start.9 = (bf16[176,1152]{1,0:T(8,128)(2,1)S(1)}, bf16[176,1152]{1,0:T(8,128)(2,1)S(1)}, u32[]{:S(2)}, u32[]{:S(2)}) collective-permute-start(bf16[176,1152]{1,0:T(8,128)(2,1)S(1)} %pass_on.8.refs_1_), channel_id=1, source_target_pairs={{0,28},{4,0},{8,4},{12,8},{16,12},{20,16},{24,20},{28,24},{1,29},{... | collective-permute-start | bytes 1216520 | tf_op jit(solution)/shard_map/ppermute | solution.py:20
  40.1 0.9 %collective-permute-start.8 = (bf16[48,1152]{1,0:T(8,128)(2,1)S(1)}, bf16[48,1152]{1,0:T(8,128)(2,1)S(1)}, u32[]{:S(2)}, u32[]{:S(2)}) collective-permute-start(bf16[48,1152]{1,0:T(8,128)(2,1)S(1)} %pass_on.9), channel_id=1, source_target_pairs={{0,28},{4,0},{8,4},{12,8},{16,12},{20,16},{24,20},{28,24},{1,29},{... | collective-permute-start | bytes 331784 | tf_op jit(solution)/shard_map/ppermute | solution.py:20
  40.9 5.8 %collective-permute-done.6.back_ref = bf16[192,1152]{1,0:T(8,128)(2,1)S(1)} collective-permute-done((bf16[192,1152]{1,0:T(8,128)(2,1)S(1)}, bf16[192,1152]{1,0:T(8,128)(2,1)S(1)}, u32[]{:S(2)}, u32[]{:S(2)}) %collective-permute-start.6) | collective-permute-done | bytes 442400 | tf_op jit(solution)/shard_map/ppermute | solution.py:20
  46.8 0.8 %add_rows.4 = (bf16[416,1152]{1,0:T(8,128)(2,1)}, f32[8,128]{1,0:T(8,128)S(1)}) custom-call(f32[416,1152]{1,0:T(8,128)S(1)} %fusion.total_ref, bf16[192,1152]{1,0:T(8,128)(2,1)S(1)} %collective-permute-done.6.back_ref), custom_call_target="tpu_custom_call" | custom-call | tf_op jit(solution)/shard_map/add_rows/pallas_call | solution.py:139
  47.6 0.5 fusion.20
  48.1 0.5 fusion.2.total_ref
  48.6 3.0 %collective-permute-done.7.back_ref = bf16[416,1152]{1,0:T(8,128)(2,1)S(1)} collective-permute-done((bf16[416,1152]{1,0:T(8,128)(2,1)S(1)}, bf16[416,1152]{1,0:T(8,128)(2,1)S(1)}, u32[]{:S(2)}, u32[]{:S(2)}) %collective-permute-start.7) | collective-permute-done | bytes 958496 | tf_op jit(solution)/shard_map/ppermute | solution.py:20
  51.7 1.0 %add_rows.5 = (bf16[416,1152]{1,0:T(8,128)(2,1)}, f32[8,128]{1,0:T(8,128)S(1)}) custom-call(f32[416,1152]{1,0:T(8,128)S(1)} %fusion.2.total_ref, bf16[416,1152]{1,0:T(8,128)(2,1)S(1)} %collective-permute-done.7.back_ref), custom_call_target="tpu_custom_call" | custom-call | tf_op jit(solution)/shard_map/add_rows/pallas_call | solution.py:139
  52.7 2.2 %collective-permute-done.9.back_ref = bf16[176,1152]{1,0:T(8,128)(2,1)S(1)} collective-permute-done((bf16[176,1152]{1,0:T(8,128)(2,1)S(1)}, bf16[176,1152]{1,0:T(8,128)(2,1)S(1)}, u32[]{:S(2)}, u32[]{:S(2)}) %collective-permute-start.9) | collective-permute-done | bytes 405536 | tf_op jit(solution)/shard_map/ppermute | solution.py:20
  54.9 0.8 %add_rows.6.refs_0_ = bf16[416,1152]{1,0:T(8,128)(2,1)} custom-call(f32[416,1152]{1,0:T(8,128)S(1)} %fusion.total_ref, bf16[176,1152]{1,0:T(8,128)(2,1)S(1)} %collective-permute-done.9.back_ref, bf16[416,1152]{1,0:T(8,128)(2,1)} %get-tuple-element.26.refs_0_, f32[8,128]{1,0:T(8,128)S(1)} %get-tuple-element.27.refs_1_), custom_call_target="tpu_custom_call", output_to_operand_aliasing={{}: (2, {})} | custom-call | tf_op jit(solution)/shard_map/add_rows/pallas_call | solution.py:139
  55.7 0.4 collective-permute-done.8.back_ref
  56.0 0.7 %add_rows.7 = bf16[416,1152]{1,0:T(8,128)(2,1)} custom-call(f32[416,1152]{1,0:T(8,128)S(1)} %fusion.total_ref, bf16[48,1152]{1,0:T(8,128)(2,1)S(1)} %collective-permute-done.8.back_ref, bf16[416,1152]{1,0:T(8,128)(2,1)} %add_rows.6.refs_0_), custom_call_target="tpu_custom_call", output_to_operand_aliasing={{}: (2, {})} | custom-call | tf_op jit(solution)/shard_map/add_rows/pallas_call | solution.py:139
  (21 shorter events, 0.2 us)
Async XLA Ops:
  0.6 24.8 %copy-start.3 = (s32[1,416]{1,0:T(1,128)S(1)}, s32[1,416]{1,0:T(1,128)}, u32[]{:S(2)}) copy-start(s32[1,416]{1,0:T(1,128)} %array_ref.3) | copy-start | bytes 4996
  1.7 10.7 %collective-permute-start = (bf16[96,1152]{1,0:T(8,128)(2,1)S(1)}, bf16[96,1152]{1,0:T(8,128)(2,1)S(1)}, u32[]{:S(2)}, u32[]{:S(2)}) collective-permute-start(bf16[96,1152]{1,0:T(8,128)(2,1)S(1)} %get-tuple-element.29), channel_id=1, source_target_pairs={{0,28},{4,0},{8,4},{12,8},{16,12},{20,16},{24,20},{28,24},{1,29},{... | collective-permute-start | bytes 663560 | tf_op jit(solution)/shard_map/ppermute | solution.py:20
  7.8 17.6 %collective-permute-start.1 = (bf16[96,1152]{1,0:T(8,128)(2,1)S(1)}, bf16[96,1152]{1,0:T(8,128)(2,1)S(1)}, u32[]{:S(2)}, u32[]{:S(2)}) collective-permute-start(bf16[96,1152]{1,0:T(8,128)(2,1)S(1)} %get-tuple-element.28.refs_0_), channel_id=1, source_target_pairs={{0,4},{4,8},{8,12},{12,16},{16,20},{20,24},{24,28},{28,0},{1,5},{5... | collective-permute-start | bytes 663560 | tf_op jit(solution)/shard_map/ppermute | solution.py:20
  7.8 20.1 %collective-permute-start.2 = (bf16[416,1152]{1,0:T(8,128)(2,1)}, bf16[416,1152]{1,0:T(8,128)(2,1)S(1)}, u32[]{:S(2)}, u32[]{:S(2)}) collective-permute-start(bf16[416,1152]{1,0:T(8,128)(2,1)} %image_ref.3), channel_id=1, source_target_pairs={{0,3},{1,0},{2,1},{3,2},{4,7},{5,4},{6,5},{7,6},{8,11},{9,8},{10,9... | collective-permute-start | bytes 2875400 | tf_op jit(solution)/shard_map/ppermute | solution.py:20
  8.4 1.2 %copy-start = (bf16[416,1152]{1,0:T(8,128)(2,1)S(1)}, bf16[416,1152]{1,0:T(8,128)(2,1)}, u32[]{:S(2)}) copy-start(bf16[416,1152]{1,0:T(8,128)(2,1)} %array_ref.5) | copy-start | bytes 2875396
  9.6 15.8 %copy-start.1 = (bf16[416,1152]{1,0:T(8,128)(2,1)S(1)}, bf16[416,1152]{1,0:T(8,128)(2,1)}, u32[]{:S(2)}) copy-start(bf16[416,1152]{1,0:T(8,128)(2,1)} %array_ref.5) | copy-start | bytes 2875396
  9.6 15.8 %copy-start.2 = (bf16[416,1152]{1,0:T(8,128)(2,1)S(1)}, bf16[416,1152]{1,0:T(8,128)(2,1)}, u32[]{:S(2)}) copy-start(bf16[416,1152]{1,0:T(8,128)(2,1)} %image_ref.3) | copy-start | bytes 2875396
  9.8 24.0 %collective-permute-start.4 = (bf16[176,1152]{1,0:T(8,128)(2,1)S(1)}, bf16[176,1152]{1,0:T(8,128)(2,1)S(1)}, u32[]{:S(2)}, u32[]{:S(2)}) collective-permute-start(bf16[176,1152]{1,0:T(8,128)(2,1)S(1)} %fetch.4), channel_id=1, source_target_pairs={{0,4},{4,8},{8,12},{12,16},{16,20},{20,24},{24,28},{28,0},{1,5},{5... | collective-permute-start | bytes 1216520 | tf_op jit(solution)/shard_map/ppermute | solution.py:20
  12.4 19.5 %collective-permute-start.3 = (bf16[96,1152]{1,0:T(8,128)(2,1)S(1)}, bf16[96,1152]{1,0:T(8,128)(2,1)S(1)}, u32[]{:S(2)}, u32[]{:S(2)}) collective-permute-start(bf16[96,1152]{1,0:T(8,128)(2,1)S(1)} %collective-permute-done.refs_0_), channel_id=1, source_target_pairs={{0,8},{4,12},{8,16},{12,20},{16,24},{20,28},{24,0},{28,4},{1,9},{5... | collective-permute-start | bytes 663560 | tf_op jit(solution)/shard_map/ppermute | solution.py:20
  28.0 8.3 %collective-permute-start.5 = (bf16[48,1152]{1,0:T(8,128)(2,1)S(1)}, bf16[48,1152]{1,0:T(8,128)(2,1)S(1)}, u32[]{:S(2)}, u32[]{:S(2)}) collective-permute-start(bf16[48,1152]{1,0:T(8,128)(2,1)S(1)} %fetch.5), channel_id=1, source_target_pairs={{0,4},{4,8},{8,12},{12,16},{16,20},{20,24},{24,28},{28,0},{1,5},{5... | collective-permute-start | bytes 331784 | tf_op jit(solution)/shard_map/ppermute | solution.py:20
  33.9 12.9 %collective-permute-start.6 = (bf16[192,1152]{1,0:T(8,128)(2,1)S(1)}, bf16[192,1152]{1,0:T(8,128)(2,1)S(1)}, u32[]{:S(2)}, u32[]{:S(2)}) collective-permute-start(bf16[192,1152]{1,0:T(8,128)(2,1)S(1)} %pass_on.6.refs_2_), channel_id=1, source_target_pairs={{0,28},{4,0},{8,4},{12,8},{16,12},{20,16},{24,20},{28,24},{1,29},{... | collective-permute-start | bytes 1327112 | tf_op jit(solution)/shard_map/ppermute | solution.py:20
  38.4 13.3 %collective-permute-start.7 = (bf16[416,1152]{1,0:T(8,128)(2,1)S(1)}, bf16[416,1152]{1,0:T(8,128)(2,1)S(1)}, u32[]{:S(2)}, u32[]{:S(2)}) collective-permute-start(bf16[416,1152]{1,0:T(8,128)(2,1)S(1)} %fusion.4.refs_1_), channel_id=1, source_target_pairs={{0,1},{1,2},{2,3},{3,0},{4,5},{5,6},{6,7},{7,4},{8,9},{9,10},{10,1... | collective-permute-start | bytes 2875400 | tf_op jit(solution)/shard_map/ppermute | solution.py:20
  39.2 15.6 %collective-permute-start.9 = (bf16[176,1152]{1,0:T(8,128)(2,1)S(1)}, bf16[176,1152]{1,0:T(8,128)(2,1)S(1)}, u32[]{:S(2)}, u32[]{:S(2)}) collective-permute-start(bf16[176,1152]{1,0:T(8,128)(2,1)S(1)} %pass_on.8.refs_1_), channel_id=1, source_target_pairs={{0,28},{4,0},{8,4},{12,8},{16,12},{20,16},{24,20},{28,24},{1,29},{... | collective-permute-start | bytes 1216520 | tf_op jit(solution)/shard_map/ppermute | solution.py:20
  40.1 15.9 %collective-permute-start.8 = (bf16[48,1152]{1,0:T(8,128)(2,1)S(1)}, bf16[48,1152]{1,0:T(8,128)(2,1)S(1)}, u32[]{:S(2)}, u32[]{:S(2)}) collective-permute-start(bf16[48,1152]{1,0:T(8,128)(2,1)S(1)} %pass_on.9), channel_id=1, source_target_pairs={{0,28},{4,0},{8,4},{12,8},{16,12},{20,16},{24,20},{28,24},{1,29},{... | collective-permute-start | bytes 331784 | tf_op jit(solution)/shard_map/ppermute | solution.py:20

commit v20 on v15

--- a/solution.py
+++ b/solution.py
@@ -8,7 +8,7 @@
 from jax.sharding import PartitionSpec as P
 
 MIB = 2**20
-ENDS = (8, 22)
+ENDS = (6, 17, 20)
 SMEM = pl.BlockSpec(memory_space=pltpu.SMEM)
 VMEM = pl.BlockSpec(memory_space=pltpu.VMEM)
 HBM = pl.BlockSpec(memory_space=pltpu.HBM)
@@ -56,7 +56,7 @@
     )(array, *after)
 
 
-def pass_on(array, after):
+def pass_on(array, after, flops=0):
     return pl.pallas_call(
         lambda *refs: None,
         out_shape=jax.ShapeDtypeStruct(array.shape, array.dtype),
@@ -64,18 +64,29 @@
         out_specs=ANY,
         input_output_aliases={0: 0},
         compiler_params=pltpu.CompilerParams(vmem_limit_bytes=MIB),
+        cost_estimate=pl.CostEstimate(flops=flops, bytes_accessed=0, transcendentals=0),
         name="pass_on",
     )(array, *after)
 
 
-def chunk_kernel(count, scale_ref, bias_ref, image_ref, next_ref, *refs):
+def chunk_kernel(count, choice, scale_ref, bias_ref, odd_ref, image_ref, next_ref, *refs):
     sent_ref, joined_ref, own_ref, other_ref = refs[-4:]
     scale, bias = scale_ref[0], bias_ref[0]
     start = 0
-    for piece_ref in refs[:count]:
+    for piece_ref in refs[: count - 2 * choice]:
         rows = piece_ref.shape[0]
         joined_ref[start : start + rows, :] = piece_ref[...]
         start += rows
+    if choice:
+
+        @pl.when(odd_ref[0] != 0)
+        def _():
+            joined_ref[start:, :] = refs[count - 2][...]
+
+        @pl.when(odd_ref[0] == 0)
+        def _():
+            joined_ref[start:, :] = refs[count - 1][...]
+
     part = joined_ref[...]
     image = image_ref[...]
     own = jax.nn.sigmoid(dot_nt(part, image) * scale + bias).astype(jnp.bfloat16)
@@ -88,14 +99,15 @@
     sent_ref[...] = (scale * total).astype(jnp.bfloat16)
 
 
-def chunk(factor, shift, image, image_next, pieces, after):
+def chunk(factor, shift, odd, image, image_next, pieces, after, choice=False):
     rows, (columns, width) = sum(piece.shape[0] for piece in pieces), image.shape
+    rows -= pieces[-1].shape[0] * choice
     text = jax.ShapeDtypeStruct((rows, width), jnp.bfloat16)
     tile = jax.ShapeDtypeStruct((rows, columns), jnp.bfloat16)
     return pl.pallas_call(
-        functools.partial(chunk_kernel, len(pieces)),
+        functools.partial(chunk_kernel, len(pieces), choice),
         out_shape=(text, text, tile, tile),
-        in_specs=[SMEM] * 2 + [VMEM] * (2 + len(pieces)) + [ANY] * len(after),
+        in_specs=[SMEM] * 3 + [VMEM] * (2 + len(pieces)) + [ANY] * len(after),
         out_specs=(VMEM,) * 4,
         compiler_params=pltpu.CompilerParams(vmem_limit_bytes=16 * MIB),
         cost_estimate=pl.CostEstimate(
@@ -104,7 +116,7 @@
             transcendentals=2 * rows * columns,
         ),
         name="chunk",
-    )(factor, shift, image, image_next, *pieces, *after)
+    )(factor, shift, odd, image, image_next, *pieces, *after)
 
 
 def add_rows(total, back, lo, result, after, mark=False):
@@ -143,38 +155,53 @@
     )(total, back, *kept, *after)
 
 
+def exchanged(shard, axis):
+    devices = lax.axis_size(axis)
+    if devices % 2:
+        return shifted(shard, axis, 1)
+    return lax.ppermute(shard, axis, [(i, i ^ 1) for i in range(devices)])
+
+
 def body(image, text, target, factor, shift):
     scale = factor[0]
     bias = shift[0]
     cuts = row_cuts(text.shape[0])
-    first = text[: cuts[0][1]]
+    odd = ((lax.axis_index("blk") % 2) | (lax.axis_size("blk") % 2)).astype(jnp.int32).reshape(1)
+    around = exchanged(text[slice(*cuts[3])], "blk")
+    first = text[slice(*cuts[0])]
     part = [shifted(first, "blk", 1)]
     image_next = shifted(image, "grp", -1)
     part.append(shifted(fetch(text, *cuts[1], [first]), "blk", 1))
 
-    target = fetch(target, 0, 1, [part[0]])
     own = jax.nn.sigmoid(dot_nt(image, text) * scale + bias)
     column = lax.broadcasted_iota(jnp.int32, own.shape, 1)
     own = (own - (column == target[0][:, None]).astype(jnp.float32)).astype(jnp.bfloat16)
-    part.append(shifted(fetch(text, *cuts[2], [own]), "blk", 1))
     image_grad = dot_nn(own, text)
     text_grad = dot_tn(own, image)
 
-    image_next = pass_on(image_next, [image_grad, text_grad])
-    sent0, part0, own0, next0 = chunk(factor, shift, image, image_next, part[:1], [])
+    part[0] = pass_on(part[0], [image_grad], 10**10)
+    image_next = pass_on(image_next, [part[0], text_grad])
+    part.append(shifted(fetch(text, *cuts[2], [image_next]), "blk", 1))
     next_own = jax.nn.sigmoid(dot_nt(image_next, text) * scale + bias).astype(jnp.bfloat16)
     text_grad = scale * (text_grad + dot_tn(next_own, image_next))
-    image_sent = dot_nn(next_own, text) + dot_tn(next0, part0)
+    image_sent = dot_nn(next_own, text)
+
+    around = pass_on(around, [image_sent])
+    two_on = shifted(around, "blk", 2)
+    part[0] = pass_on(part[0], [around])
+    sent0, part0, own0, next0 = chunk(factor, shift, odd, image, image_next, part[:1], [])
+    image_sent = image_sent + dot_tn(next0, part0)
     image_grad = image_grad + dot_tn(own0, part0)
 
-    sent0 = pass_on(sent0, [part[1], image_sent])
+    sent0 = pass_on(sent0, [part[1]])
     back0 = shifted(sent0, "blk", -1)
 
-    sent1, part1, own1, next1 = chunk(factor, shift, image, image_next, part[1:], [sent0])
+    sent1, part1, own1, next1 = chunk(
+        factor, shift, odd, image, image_next, [*part[1:], around, two_on], [sent0], choice=True
+    )
     image_sent = (scale * (image_sent + dot_tn(next1, part1))).astype(jnp.bfloat16)
     image_back = shifted(image_sent, "grp", 1)
-    sent1 = pass_on(sent1, [image_sent])
-    back1 = shifted(sent1, "blk", -1)
+    back1 = shifted(pass_on(sent1, [image_sent]), "blk", -1)
     result, mark = add_rows(text_grad, back0, 0, None, [], mark=True)
     own1 = pass_on(own1, [mark])
     image_grad = scale * (image_grad + dot_tn(own1, part1))

time: 53.5 us -> 60.5 us (1.13); the launches traced: 52.5 us -> 60.1 us
  waiting for transfers between devices: 27.4 us -> 21 us
  starting transfers between devices: 7.5 us -> 13.8 us
  local copies, waits for them, and re-layouts: 2.2 us -> 6.55 us
  Pallas kernels: 6.35 us -> 8.1 us
  matrix products: 6.94 us -> 8.6 us
    ppermute x7 -> x8, waiting for transfers between devices: 27.4 us -> 20.7 us  [shifted(): lax.ppermute(shard, axis, [(i, (i + by) % devices) for i in range(devices)])]
    unnamed x8 -> x22, local copies, waits for them, and re-layouts: 1.2 us -> 5.46 us
    ppermute x7 -> x8, starting transfers between devices: 7.5 us -> 10.8 us  [shifted(): lax.ppermute(shard, axis, [(i, (i + by) % devices) for i in range(devices)])]
    ppermute x0 -> x1, starting transfers between devices: none -> 3 us  [exchanged(): return lax.ppermute(shard, axis, [(i, i ^ 1) for i in range(devices)])]
    dot_general x2, matrix products: 1.72 us -> 3.28 us  [dot_nt(): lax.dot_general(a, b, (((1,), (1,)), ((), ())), preferred_element_type=jn...]
    pallas_call x2, Pallas kernels: 3.09 us -> 4.32 us  [chunk(): pl.pallas_call(functools.partial(chunk_kernel, len(pieces), choice), out_...]
  transfers between devices with their start and end apart: 7 -> 9, of which waited for: 6 -> 6; matrix products, arithmetic and copies ran while one was open for 13% -> 14% of each run, Pallas kernels for 10% -> 12%
where the time goes in v20:
time: 60.5 us; the launch traced here: 60.1 us
  waiting for transfers between devices  21 us (35%)
  starting transfers between devices  13.8 us (23%)
  matrix products  8.6 us (14%)
  Pallas kernels  8.1 us (13%)
  local copies, waits for them, and re-layouts  6.55 us (11%)
  between operations  2.17 us (4%)
    ppermute x8, waiting for transfers between devices, shifted(): lax.ppermute(shard, axis, [(i, (i + by) % devices) for i in range(devices)])  20.7 us
    ppermute x8, starting transfers between devices, shifted(): lax.ppermute(shard, axis, [(i, (i + by) % devices) for i in range(devices)])  10.8 us
    unnamed x22, local copies, waits for them, and re-layouts  5.46 us
    pallas_call x2, Pallas kernels, chunk(): pl.pallas_call(functools.partial(chunk_kernel, len(pieces), choice), out_...  4.32 us
    dot_general x6, matrix products, dot_tn(): lax.dot_general(a, b, (((0,), (0,)), ((), ())), preferred_element_type=jn...  3.92 us
    dot_general x2, matrix products, dot_nt(): lax.dot_general(a, b, (((1,), (1,)), ((), ())), preferred_element_type=jn...  3.28 us
    ppermute x1, starting transfers between devices, exchanged(): return lax.ppermute(shard, axis, [(i, i ^ 1) for i in range(devices)])  3 us
    pallas_call x3, Pallas kernels, add_rows(): pl.pallas_call(kernel, out_shape=(out, jax.ShapeDtypeStruct((8, 128), jnp...  2.7 us
  transfers between devices with their start and end apart: 9, of which 6 were waited for; matrix products, arithmetic and copies ran while one was open for 14% of the time, Pallas kernels for 12%

profile of v20, /device:TPU:0, one launch (start us, length us, event | category | flops | bytes accessed | tf_op | source)
XLA Modules:
  0.0 60.1 jit_solution(12907393506344587770)
XLA Ops:
  0.6 1.1 %fusion.19 = (bf16[96,1152]{1,0:T(8,128)(2,1)S(1)}, bf16[96,1152]{1,0:T(8,128)(2,1)S(1)}) fusion(bf16[416,1152]{1,0:T(8,128)(2,1)} %array_ref.3), kind=kLoop, calls=%fused_computation.25 | loop fusion | bytes 884736 | tf_op jit(solution)/shard_map/slice | solution.py:170
  1.7 3.0 %collective-permute-start.2 = (bf16[96,1152]{1,0:T(8,128)(2,1)S(1)}, bf16[96,1152]{1,0:T(8,128)(2,1)S(1)}, u32[]{:S(2)}, u32[]{:S(2)}) collective-permute-start(bf16[96,1152]{1,0:T(8,128)(2,1)S(1)} %get-tuple-element.26), channel_id=1, source_target_pairs={{0,4},{4,0},{8,12},{12,8},{16,20},{20,16},{24,28},{28,24},{1,5},{5... | collective-permute-start | bytes 663560 | tf_op jit(solution)/shard_map/ppermute | solution.py:162
  4.8 1.2 %copy-done = bf16[416,1152]{1,0:T(8,128)(2,1)S(1)} copy-done((bf16[416,1152]{1,0:T(8,128)(2,1)S(1)}, bf16[416,1152]{1,0:T(8,128)(2,1)}, u32[]{:S(2)}) %copy-start) | copy-done | bytes 958488
  6.0 1.0 %fetch.2 = bf16[176,1152]{1,0:T(8,128)(2,1)} custom-call(bf16[416,1152]{1,0:T(8,128)(2,1)S(1)} %copy-done, bf16[96,1152]{1,0:T(8,128)(2,1)S(1)} %get-tuple-element.27.refs_0_), custom_call_target="tpu_custom_call" | custom-call | tf_op jit(solution)/shard_map/fetch/pallas_call | solution.py:48
  7.0 3.0 %collective-permute-start.3 = (bf16[176,1152]{1,0:T(8,128)(2,1)}, bf16[176,1152]{1,0:T(8,128)(2,1)}, u32[]{:S(2)}, u32[]{:S(2)}) collective-permute-start(bf16[176,1152]{1,0:T(8,128)(2,1)} %fetch.2), channel_id=1, source_target_pairs={{0,4},{4,8},{8,12},{12,16},{16,20},{20,24},{24,28},{28,0},{1,5},{5... | collective-permute-start | bytes 1216520 | tf_op jit(solution)/shard_map/ppermute | solution.py:20
  11.4 2.4 %fusion.18 = bf16[416,416]{1,0:T(8,128)(2,1)S(1)} fusion(bf16[416,1152]{1,0:T(8,128)(2,1)} %image_ref.3, bf16[416,1152]{1,0:T(8,128)(2,1)} %array_ref.3, s32[416]{0:T(512)S(1)} %bitcast.31, f32[]{:T(128)} %bitcast.29, f32[]{:T(128)} %bitcast.25), kind=kOutput, calls=%fused_computation.23 | convolution fusion | flops 400278528 | bytes 2264712 | tf_op jit(solution)/shard_map/dot_general | solution.py:24
  13.9 0.7 %fusion.21.refs_2_ = f32[416,1152]{1,0:T(8,128)S(1)} fusion(bf16[416,416]{1,0:T(8,128)(2,1)S(1)} %fusion.18, bf16[416,1152]{1,0:T(8,128)(2,1)S(1)} %copy-done.6), kind=kOutput, calls=%fused_computation.27 | convolution fusion | flops 398721024 | bytes 3221504 | tf_op jit(solution)/shard_map/dot_general | solution.py:28
  14.6 0.4 copy-done.1
  15.1 0.7 %fusion.20.refs_1_ = f32[416,1152]{1,0:T(8,128)S(1)} fusion(bf16[416,416]{1,0:T(8,128)(2,1)S(1)} %fusion.18, bf16[416,1152]{1,0:T(8,128)(2,1)S(1)} %copy-done.1), kind=kOutput, calls=%fused_computation.26 | convolution fusion | flops 398721024 | bytes 3221504 | tf_op jit(solution)/shard_map/dot_general | solution.py:32
  15.9 1.2 %copy-done.4 = f32[416,1152]{1,0:T(8,128)} copy-done((f32[416,1152]{1,0:T(8,128)}, f32[416,1152]{1,0:T(8,128)S(1)}, u32[]{:S(2)}) %copy-start.4) | copy-done | bytes 1916952
  17.0 4.7 %collective-permute-done.refs_0_ = bf16[416,1152]{1,0:T(8,128)(2,1)S(1)} collective-permute-done((bf16[416,1152]{1,0:T(8,128)(2,1)}, bf16[416,1152]{1,0:T(8,128)(2,1)S(1)}, u32[]{:S(2)}, u32[]{:S(2)}) %collective-permute-start) | collective-permute-done | bytes 958496 | tf_op jit(solution)/shard_map/ppermute | solution.py:20
  21.8 0.8 %fusion.17 = bf16[416,416]{1,0:T(8,128)(2,1)S(1)} fusion(bf16[416,1152]{1,0:T(8,128)(2,1)S(1)} %pass_on.8.next_ref.refs_0_, bf16[416,1152]{1,0:T(8,128)(2,1)S(1)} %copy-done.1, f32[]{:T(128)} %bitcast.30, f32[]{:T(128)} %bitcast.28), kind=kOutput, calls=%fused_computation.22 | convolution fusion | flops 399759360 | bytes 2263048 | tf_op jit(solution)/shard_map/dot_general | solution.py:24
  22.6 0.7 %fusion.22.refs_1_ = f32[416,1152]{1,0:T(8,128)S(1)} fusion(bf16[416,416]{1,0:T(8,128)(2,1)S(1)} %fusion.17, bf16[416,1152]{1,0:T(8,128)(2,1)S(1)} %copy-done.1), kind=kOutput, calls=%fused_computation.28 | convolution fusion | flops 398721024 | bytes 3221504 | tf_op jit(solution)/shard_map/dot_general | solution.py:32
  23.6 1.8 %collective-permute-start.5 = (bf16[96,1152]{1,0:T(8,128)(2,1)S(1)}, bf16[96,1152]{1,0:T(8,128)(2,1)}, u32[]{:S(2)}, u32[]{:S(2)}) collective-permute-start(bf16[96,1152]{1,0:T(8,128)(2,1)S(1)} %pass_on.9.refs_1_.refs_2_), channel_id=1, source_target_pairs={{0,8},{4,12},{8,16},{12,20},{16,24},{20,28},{24,0},{28,4},{1,9},{5... | collective-permute-start | bytes 663560 | tf_op jit(solution)/shard_map/ppermute | solution.py:20
  25.7 1.2 %copy-done.7 = bf16[416,1152]{1,0:T(8,128)(2,1)S(1)} copy-done((bf16[416,1152]{1,0:T(8,128)(2,1)S(1)}, bf16[416,1152]{1,0:T(8,128)(2,1)}, u32[]{:S(2)}) %copy-start.7) | copy-done | bytes 958488
  26.9 1.2 %chunk.2 = (bf16[96,1152]{1,0:T(8,128)(2,1)S(1)}, bf16[96,1152]{1,0:T(8,128)(2,1)S(1)}, bf16[96,416]{1,0:T(8,128)(2,1)S(1)}, bf16[96,416]{1,0:T(8,128)(2,1)S(1)}) custom-call(f32[1]{0:T(128)} %copy.23.scale_ref, f32[1]{0:T(128)} %copy.24.bias_ref, s32[1]{0:T(128)} %bitcast.3.odd_ref, bf16[416,1152]{1,0:T(8,128)(2,1)S(1)} %copy-done.7, ...), custom_call_target="tpu_custom_call" | custom-call | flops 368050176 | bytes 2580480 | tf_op jit(solution)/shard_map/chunk/pallas_call | solution.py:107
  28.1 4.7 %collective-permute-start.6 = (bf16[96,1152]{1,0:T(8,128)(2,1)S(1)}, bf16[96,1152]{1,0:T(8,128)(2,1)S(1)}, u32[]{:S(2)}, u32[]{:S(2)}) collective-permute-start(bf16[96,1152]{1,0:T(8,128)(2,1)S(1)} %pass_on.11.refs_4_), channel_id=1, source_target_pairs={{0,28},{4,0},{8,4},{12,8},{16,12},{20,16},{24,20},{28,24},{1,29},{... | collective-permute-start | bytes 663560 | tf_op jit(solution)/shard_map/ppermute | solution.py:20
  32.8 2.2 %collective-permute-done.4.refs_1_ = bf16[48,1152]{1,0:T(8,128)(2,1)S(1)} collective-permute-done((bf16[48,1152]{1,0:T(8,128)(2,1)S(1)}, bf16[48,1152]{1,0:T(8,128)(2,1)S(1)}, u32[]{:S(2)}, u32[]{:S(2)}) %collective-permute-start.4) | collective-permute-done | bytes 110624 | tf_op jit(solution)/shard_map/ppermute | solution.py:20
  35.0 3.2 %chunk.3 = (bf16[320,1152]{1,0:T(8,128)(2,1)S(1)}, bf16[320,1152]{1,0:T(8,128)(2,1)S(1)}, bf16[320,416]{1,0:T(8,128)(2,1)S(1)}, bf16[320,416]{1,0:T(8,128)(2,1)S(1)}) custom-call(f32[1]{0:T(128)} %copy.23.scale_ref, f32[1]{0:T(128)} %copy.24.bias_ref, s32[1]{0:T(128)} %bitcast.3.odd_ref, bf16[416,1152]{1,0:T(8,128)(2,1)S(1)} %copy-done.7, ...), custom_call_target="tpu_custom_call" | custom-call | flops 1226833920 | bytes 4128768 | tf_op jit(solution)/shard_map/chunk/pallas_call | solution.py:107
  38.1 0.7 %fusion.24 = f32[416,1152]{1,0:T(8,128)S(1)} fusion(bf16[320,416]{1,0:T(8,128)(2,1)S(1)} %get-tuple-element.21, bf16[320,1152]{1,0:T(8,128)(2,1)S(1)} %get-tuple-element.19), kind=kOutput, calls=%fused_computation.30 | convolution fusion | flops 306708480 | bytes 2920448 | tf_op jit(solution)/shard_map/dot_general | solution.py:28
  38.9 0.5 fusion.5.refs_1_
  39.4 0.9 %collective-permute-start.7 = (bf16[416,1152]{1,0:T(8,128)(2,1)S(1)}, bf16[416,1152]{1,0:T(8,128)(2,1)S(1)}, u32[]{:S(2)}, u32[]{:S(2)}) collective-permute-start(bf16[416,1152]{1,0:T(8,128)(2,1)S(1)} %fusion.5.refs_1_), channel_id=1, source_target_pairs={{0,1},{1,2},{2,3},{3,0},{4,5},{5,6},{6,7},{7,4},{8,9},{9,10},{10,1... | collective-permute-start | bytes 2875400 | tf_op jit(solution)/shard_map/ppermute | solution.py:20
  40.3 0.6 %copy-done.3 = f32[416,1152]{1,0:T(8,128)S(1)} copy-done((f32[416,1152]{1,0:T(8,128)S(1)}, f32[416,1152]{1,0:T(8,128)}, u32[]{:S(2)}) %copy-start.3) | copy-done | bytes 1916952
  40.9 0.7 %fusion.total_ref = f32[416,1152]{1,0:T(8,128)S(1)} fusion(f32[416,1152]{1,0:T(8,128)S(1)} %copy-done.3, bf16[416,416]{1,0:T(8,128)(2,1)S(1)} %copy-done.9, bf16[416,1152]{1,0:T(8,128)(2,1)S(1)} %pass_on.8.next_ref.refs_0_, f32[]{:T(128)} %bitcast.24), kind=kOutput, calls=%fused_computation.1 | convolution fusion | flops 399679488 | bytes 5138436 | tf_op jit(solution)/shard_map/dot_general | solution.py:28
  41.7 0.7 %add_rows.3 = (bf16[416,1152]{1,0:T(8,128)(2,1)}, f32[8,128]{1,0:T(8,128)S(1)}) custom-call(f32[416,1152]{1,0:T(8,128)S(1)} %fusion.total_ref, bf16[96,1152]{1,0:T(8,128)(2,1)S(1)} %collective-permute-done.6.back_ref), custom_call_target="tpu_custom_call" | custom-call | tf_op jit(solution)/shard_map/add_rows/pallas_call | solution.py:146
  42.5 0.7 %fusion.23 = f32[416,1152]{1,0:T(8,128)S(1)} fusion(bf16[320,416]{1,0:T(8,128)(2,1)S(1)} %pass_on.12, bf16[320,1152]{1,0:T(8,128)(2,1)S(1)} %get-tuple-element.19), kind=kOutput, calls=%fused_computation.29 | convolution fusion | flops 306708480 | bytes 2920448 | tf_op jit(solution)/shard_map/dot_general | solution.py:28
  43.2 0.8 %copy-done.5 = f32[416,1152]{1,0:T(8,128)S(1)} copy-done((f32[416,1152]{1,0:T(8,128)S(1)}, f32[416,1152]{1,0:T(8,128)}, u32[]{:S(2)}) %copy-start.5) | copy-done | bytes 1916952
  44.0 0.5 fusion.4.total_ref
  44.5 8.3 %collective-permute-done.7.back_ref = bf16[416,1152]{1,0:T(8,128)(2,1)S(1)} collective-permute-done((bf16[416,1152]{1,0:T(8,128)(2,1)S(1)}, bf16[416,1152]{1,0:T(8,128)(2,1)S(1)}, u32[]{:S(2)}, u32[]{:S(2)}) %collective-permute-start.7) | collective-permute-done | bytes 958496 | tf_op jit(solution)/shard_map/ppermute | solution.py:20
  52.8 1.0 %add_rows.4 = (bf16[416,1152]{1,0:T(8,128)(2,1)}, f32[8,128]{1,0:T(8,128)S(1)}) custom-call(f32[416,1152]{1,0:T(8,128)S(1)} %fusion.4.total_ref, bf16[416,1152]{1,0:T(8,128)(2,1)S(1)} %collective-permute-done.7.back_ref), custom_call_target="tpu_custom_call" | custom-call | tf_op jit(solution)/shard_map/add_rows/pallas_call | solution.py:146
  53.8 5.4 %collective-permute-done.8.back_ref = bf16[320,1152]{1,0:T(8,128)(2,1)S(1)} collective-permute-done((bf16[320,1152]{1,0:T(8,128)(2,1)S(1)}, bf16[320,1152]{1,0:T(8,128)(2,1)S(1)}, u32[]{:S(2)}, u32[]{:S(2)}) %collective-permute-start.8) | collective-permute-done | bytes 737312 | tf_op jit(solution)/shard_map/ppermute | solution.py:20
  59.2 0.9 %add_rows.5 = bf16[416,1152]{1,0:T(8,128)(2,1)} custom-call(f32[416,1152]{1,0:T(8,128)S(1)} %fusion.total_ref, bf16[320,1152]{1,0:T(8,128)(2,1)S(1)} %collective-permute-done.8.back_ref, bf16[416,1152]{1,0:T(8,128)(2,1)} %get-tuple-element.24.refs_0_, f32[8,128]{1,0:T(8,128)S(1)} %get-tuple-element.25.refs_1_), custom_call_target="tpu_custom_call", output_to_operand_aliasing={{}: (2, {})} | custom-call | tf_op jit(solution)/shard_map/add_rows/pallas_call | solution.py:146
  (33 shorter events, 0.9 us)
Async XLA Ops:
  0.6 10.8 %copy-start.10 = (s32[1,416]{1,0:T(1,128)S(1)}, s32[1,416]{1,0:T(1,128)}, u32[]{:S(2)}) copy-start(s32[1,416]{1,0:T(1,128)} %param.7) | copy-start | bytes 4996
  1.7 21.9 %collective-permute-start.2 = (bf16[96,1152]{1,0:T(8,128)(2,1)S(1)}, bf16[96,1152]{1,0:T(8,128)(2,1)S(1)}, u32[]{:S(2)}, u32[]{:S(2)}) collective-permute-start(bf16[96,1152]{1,0:T(8,128)(2,1)S(1)} %get-tuple-element.26), channel_id=1, source_target_pairs={{0,4},{4,0},{8,12},{12,8},{16,20},{20,16},{24,28},{28,24},{1,5},{5... | collective-permute-start | bytes 663560 | tf_op jit(solution)/shard_map/ppermute | solution.py:162
  4.7 11.1 %collective-permute-start.1 = (bf16[96,1152]{1,0:T(8,128)(2,1)S(1)}, bf16[96,1152]{1,0:T(8,128)(2,1)S(1)}, u32[]{:S(2)}, u32[]{:S(2)}) collective-permute-start(bf16[96,1152]{1,0:T(8,128)(2,1)S(1)} %get-tuple-element.27.refs_0_), channel_id=1, source_target_pairs={{0,4},{4,8},{8,12},{12,16},{16,20},{20,24},{24,28},{28,0},{1,5},{5... | collective-permute-start | bytes 663560 | tf_op jit(solution)/shard_map/ppermute | solution.py:20
  4.8 1.2 %copy-start = (bf16[416,1152]{1,0:T(8,128)(2,1)S(1)}, bf16[416,1152]{1,0:T(8,128)(2,1)}, u32[]{:S(2)}) copy-start(bf16[416,1152]{1,0:T(8,128)(2,1)} %array_ref.3) | copy-start | bytes 2875396
  7.0 21.1 %collective-permute-start.3 = (bf16[176,1152]{1,0:T(8,128)(2,1)}, bf16[176,1152]{1,0:T(8,128)(2,1)}, u32[]{:S(2)}, u32[]{:S(2)}) collective-permute-start(bf16[176,1152]{1,0:T(8,128)(2,1)} %fetch.2), channel_id=1, source_target_pairs={{0,4},{4,8},{8,12},{12,16},{16,20},{20,24},{24,28},{28,0},{1,5},{5... | collective-permute-start | bytes 1216520 | tf_op jit(solution)/shard_map/ppermute | solution.py:20
  10.0 11.8 %collective-permute-start = (bf16[416,1152]{1,0:T(8,128)(2,1)}, bf16[416,1152]{1,0:T(8,128)(2,1)S(1)}, u32[]{:S(2)}, u32[]{:S(2)}) collective-permute-start(bf16[416,1152]{1,0:T(8,128)(2,1)} %image_ref.3), channel_id=1, source_target_pairs={{0,3},{1,0},{2,1},{3,2},{4,7},{5,4},{6,5},{7,6},{8,11},{9,8},{10,9... | collective-permute-start | bytes 2875400 | tf_op jit(solution)/shard_map/ppermute | solution.py:20
  11.4 2.5 %copy-start.6 = (bf16[416,1152]{1,0:T(8,128)(2,1)S(1)}, bf16[416,1152]{1,0:T(8,128)(2,1)}, u32[]{:S(2)}) copy-start(bf16[416,1152]{1,0:T(8,128)(2,1)} %image_ref.3) | copy-start | bytes 2875396
  13.9 1.2 %copy-start.1 = (bf16[416,1152]{1,0:T(8,128)(2,1)S(1)}, bf16[416,1152]{1,0:T(8,128)(2,1)}, u32[]{:S(2)}) copy-start(bf16[416,1152]{1,0:T(8,128)(2,1)} %array_ref.3) | copy-start | bytes 2875396
  15.1 6.7 %copy-start.2 = (f32[416,1152]{1,0:T(8,128)}, f32[416,1152]{1,0:T(8,128)S(1)}, u32[]{:S(2)}) copy-start(f32[416,1152]{1,0:T(8,128)S(1)} %fusion.21.refs_2_) | copy-start | bytes 5750788
  15.8 1.3 %copy-start.4 = (f32[416,1152]{1,0:T(8,128)}, f32[416,1152]{1,0:T(8,128)S(1)}, u32[]{:S(2)}) copy-start(f32[416,1152]{1,0:T(8,128)S(1)} %fusion.20.refs_1_) | copy-start | bytes 5750788
  22.6 1.0 %copy-start.8 = (bf16[416,416]{1,0:T(8,128)(2,1)}, bf16[416,416]{1,0:T(8,128)(2,1)S(1)}, u32[]{:S(2)}) copy-start(bf16[416,416]{1,0:T(8,128)(2,1)S(1)} %fusion.17) | copy-start | bytes 1038340
  23.6 11.4 %collective-permute-start.5 = (bf16[96,1152]{1,0:T(8,128)(2,1)S(1)}, bf16[96,1152]{1,0:T(8,128)(2,1)}, u32[]{:S(2)}, u32[]{:S(2)}) collective-permute-start(bf16[96,1152]{1,0:T(8,128)(2,1)S(1)} %pass_on.9.refs_1_.refs_2_), channel_id=1, source_target_pairs={{0,8},{4,12},{8,16},{12,20},{16,24},{20,28},{24,0},{28,4},{1,9},{5... | collective-permute-start | bytes 663560 | tf_op jit(solution)/shard_map/ppermute | solution.py:20
  25.5 9.4 %collective-permute-start.4 = (bf16[48,1152]{1,0:T(8,128)(2,1)S(1)}, bf16[48,1152]{1,0:T(8,128)(2,1)S(1)}, u32[]{:S(2)}, u32[]{:S(2)}) collective-permute-start(bf16[48,1152]{1,0:T(8,128)(2,1)S(1)} %fetch.3), channel_id=1, source_target_pairs={{0,4},{4,8},{8,12},{12,16},{16,20},{20,24},{24,28},{28,0},{1,5},{5... | collective-permute-start | bytes 331784 | tf_op jit(solution)/shard_map/ppermute | solution.py:20
  25.7 1.2 %copy-start.7 = (bf16[416,1152]{1,0:T(8,128)(2,1)S(1)}, bf16[416,1152]{1,0:T(8,128)(2,1)}, u32[]{:S(2)}) copy-start(bf16[416,1152]{1,0:T(8,128)(2,1)} %image_ref.3) | copy-start | bytes 2875396
  28.1 13.6 %collective-permute-start.6 = (bf16[96,1152]{1,0:T(8,128)(2,1)S(1)}, bf16[96,1152]{1,0:T(8,128)(2,1)S(1)}, u32[]{:S(2)}, u32[]{:S(2)}) collective-permute-start(bf16[96,1152]{1,0:T(8,128)(2,1)S(1)} %pass_on.11.refs_4_), channel_id=1, source_target_pairs={{0,28},{4,0},{8,4},{12,8},{16,12},{20,16},{24,20},{28,24},{1,29},{... | collective-permute-start | bytes 663560 | tf_op jit(solution)/shard_map/ppermute | solution.py:20
  39.4 1.5 %copy-start.3 = (f32[416,1152]{1,0:T(8,128)S(1)}, f32[416,1152]{1,0:T(8,128)}, u32[]{:S(2)}) copy-start(f32[416,1152]{1,0:T(8,128)} %copy-done.2) | copy-start | bytes 5750788
  39.4 1.6 %copy-start.9 = (bf16[416,416]{1,0:T(8,128)(2,1)S(1)}, bf16[416,416]{1,0:T(8,128)(2,1)}, u32[]{:S(2)}) copy-start(bf16[416,416]{1,0:T(8,128)(2,1)} %copy-done.8) | copy-start | bytes 1038340
  39.4 13.4 %collective-permute-start.7 = (bf16[416,1152]{1,0:T(8,128)(2,1)S(1)}, bf16[416,1152]{1,0:T(8,128)(2,1)S(1)}, u32[]{:S(2)}, u32[]{:S(2)}) collective-permute-start(bf16[416,1152]{1,0:T(8,128)(2,1)S(1)} %fusion.5.refs_1_), channel_id=1, source_target_pairs={{0,1},{1,2},{2,3},{3,0},{4,5},{5,6},{6,7},{7,4},{8,9},{9,10},{10,1... | collective-permute-start | bytes 2875400 | tf_op jit(solution)/shard_map/ppermute | solution.py:20
  40.3 18.9 %collective-permute-start.8 = (bf16[320,1152]{1,0:T(8,128)(2,1)S(1)}, bf16[320,1152]{1,0:T(8,128)(2,1)S(1)}, u32[]{:S(2)}, u32[]{:S(2)}) collective-permute-start(bf16[320,1152]{1,0:T(8,128)(2,1)S(1)} %pass_on.13), channel_id=1, source_target_pairs={{0,28},{4,0},{8,4},{12,8},{16,12},{20,16},{24,20},{28,24},{1,29},{... | collective-permute-start | bytes 2211848 | tf_op jit(solution)/shard_map/ppermute | solution.py:20
  42.4 1.5 %copy-start.5 = (f32[416,1152]{1,0:T(8,128)S(1)}, f32[416,1152]{1,0:T(8,128)}, u32[]{:S(2)}) copy-start(f32[416,1152]{1,0:T(8,128)} %copy-done.4) | copy-start | bytes 5750788

commit v21 on v20

--- a/solution.py
+++ b/solution.py
@@ -8,6 +8,7 @@
 from jax.sharding import PartitionSpec as P
 
 MIB = 2**20
+WAIT = 10**10
 ENDS = (6, 17, 20)
 SMEM = pl.BlockSpec(memory_space=pltpu.SMEM)
 VMEM = pl.BlockSpec(memory_space=pltpu.VMEM)
@@ -179,25 +180,25 @@
     image_grad = dot_nn(own, text)
     text_grad = dot_tn(own, image)
 
-    part[0] = pass_on(part[0], [image_grad], 10**10)
+    part[0] = pass_on(part[0], [image_grad], WAIT)
     image_next = pass_on(image_next, [part[0], text_grad])
-    part.append(shifted(fetch(text, *cuts[2], [image_next]), "blk", 1))
+    last = fetch(text, *cuts[2], [image_next])
+    part.append(shifted(last, "blk", 1))
     next_own = jax.nn.sigmoid(dot_nt(image_next, text) * scale + bias).astype(jnp.bfloat16)
     text_grad = scale * (text_grad + dot_tn(next_own, image_next))
     image_sent = dot_nn(next_own, text)
 
-    around = pass_on(around, [image_sent])
+    around = pass_on(around, [image_sent, last])
     two_on = shifted(around, "blk", 2)
-    part[0] = pass_on(part[0], [around])
-    sent0, part0, own0, next0 = chunk(factor, shift, odd, image, image_next, part[:1], [])
+    sent0, part0, own0, next0 = chunk(factor, shift, odd, image, image_next, part[:2], [around])
+    back0 = shifted(sent0, "blk", -1)
     image_sent = image_sent + dot_tn(next0, part0)
     image_grad = image_grad + dot_tn(own0, part0)
 
-    sent0 = pass_on(sent0, [part[1]])
-    back0 = shifted(sent0, "blk", -1)
-
+    part[2] = pass_on(part[2], [sent0], WAIT)
+    two_on = pass_on(two_on, [part[2]])
     sent1, part1, own1, next1 = chunk(
-        factor, shift, odd, image, image_next, [*part[1:], around, two_on], [sent0], choice=True
+        factor, shift, odd, image, image_next, [part[2], around, two_on], [sent0], choice=True
     )
     image_sent = (scale * (image_sent + dot_tn(next1, part1))).astype(jnp.bfloat16)
     image_back = shifted(image_sent, "grp", 1)
@@ -206,7 +207,7 @@
     own1 = pass_on(own1, [mark])
     image_grad = scale * (image_grad + dot_tn(own1, part1))
     image_grad, mark = add_rows(image_grad, image_back, 0, None, [], mark=True)
-    result = add_rows(text_grad, back1, cuts[1][0], result, [mark])
+    result = add_rows(text_grad, back1, cuts[2][0], result, [mark])
     return image_grad, result
 
 

time: 60.5 us -> 57.4 us (0.949)
  waiting for transfers between devices: 21 us -> 11.5 us
  matrix products: 8.6 us -> 12.4 us
  starting transfers between devices: 13.8 us -> 15.6 us
  Pallas kernels: 8.1 us -> 9.3 us
    ppermute x8, waiting for transfers between devices: 20.7 us -> 11.5 us  [shifted(): lax.ppermute(shard, axis, [(i, (i + by) % devices) for i in range(devices)])]
    ppermute x8, starting transfers between devices: 10.8 us -> 12.7 us  [shifted(): lax.ppermute(shard, axis, [(i, (i + by) % devices) for i in range(devices)])]
    dot_general x2, matrix products: 1.4 us -> 2.71 us  [dot_nn(): return jnp.dot(a, b, preferred_element_type=jnp.float32)]
    dot_general x6, matrix products: 3.92 us -> 5.23 us  [dot_tn(): lax.dot_general(a, b, (((0,), (0,)), ((), ())), preferred_element_type=jn...]
    unnamed x22 -> x14, local copies, waits for them, and re-layouts: 5.46 us -> 4.19 us
    pallas_call x2, Pallas kernels: 4.32 us -> 5.51 us  [chunk(): pl.pallas_call(functools.partial(chunk_kernel, len(pieces), choice), out_...]
    dot_general x2, matrix products: 3.28 us -> 4.47 us  [dot_nt(): lax.dot_general(a, b, (((1,), (1,)), ((), ())), preferred_element_type=jn...]
    slice x1, local copies, waits for them, and re-layouts: 1.08 us -> 1.77 us  [body(): around = exchanged(text[slice(*cuts[3])], 'blk')]
  transfers between devices with their start and end apart: 9 -> 9, of which waited for: 6 -> 5; matrix products, arithmetic and copies ran while one was open for 14% -> 22% of each run, Pallas kernels for 12% -> 15%
where the time goes in v21:
time: 57.4 us; the launch traced here: 56.9 us
  starting transfers between devices  15.6 us (27%)
  matrix products  12.4 us (22%)
  waiting for transfers between devices  11.5 us (20%)
  Pallas kernels  9.3 us (16%)
  local copies, waits for them, and re-layouts  5.96 us (10%)
  between operations  2.12 us (4%)
    ppermute x8, starting transfers between devices, shifted(): lax.ppermute(shard, axis, [(i, (i + by) % devices) for i in range(devices)])  12.7 us
    ppermute x8, waiting for transfers between devices, shifted(): lax.ppermute(shard, axis, [(i, (i + by) % devices) for i in range(devices)])  11.5 us
    pallas_call x2, Pallas kernels, chunk(): pl.pallas_call(functools.partial(chunk_kernel, len(pieces), choice), out_...  5.51 us
    dot_general x6, matrix products, dot_tn(): lax.dot_general(a, b, (((0,), (0,)), ((), ())), preferred_element_type=jn...  5.23 us
    dot_general x2, matrix products, dot_nt(): lax.dot_general(a, b, (((1,), (1,)), ((), ())), preferred_element_type=jn...  4.47 us
    unnamed x14, local copies, waits for them, and re-layouts  4.19 us
    ppermute x1, starting transfers between devices, exchanged(): return lax.ppermute(shard, axis, [(i, i ^ 1) for i in range(devices)])  2.94 us
    dot_general x2, matrix products, dot_nn(): return jnp.dot(a, b, preferred_element_type=jnp.float32)  2.71 us
  transfers between devices with their start and end apart: 9, of which 5 were waited for; matrix products, arithmetic and copies ran while one was open for 22% of the time, Pallas kernels for 15%

profile of v21, /device:TPU:0, one launch (start us, length us, event | category | flops | bytes accessed | tf_op | source)
XLA Modules:
  0.0 56.9 jit_solution(17193045690138737568)
XLA Ops:
  0.6 1.8 %fusion.19 = (bf16[96,1152]{1,0:T(8,128)(2,1)}, bf16[96,1152]{1,0:T(8,128)(2,1)S(1)}) fusion(bf16[416,1152]{1,0:T(8,128)(2,1)} %array_ref.3), kind=kLoop, calls=%fused_computation.25 | loop fusion | bytes 884736 | tf_op jit(solution)/shard_map/slice | solution.py:171
  2.4 2.9 %collective-permute-start.3 = (bf16[96,1152]{1,0:T(8,128)(2,1)}, bf16[96,1152]{1,0:T(8,128)(2,1)S(1)}, u32[]{:S(2)}, u32[]{:S(2)}) collective-permute-start(bf16[96,1152]{1,0:T(8,128)(2,1)} %get-tuple-element.26), channel_id=1, source_target_pairs={{0,4},{4,0},{8,12},{12,8},{16,20},{20,16},{24,28},{28,24},{1,5},{5... | collective-permute-start | bytes 663560 | tf_op jit(solution)/shard_map/ppermute | solution.py:163
  5.4 1.2 %copy-done = bf16[416,1152]{1,0:T(8,128)(2,1)S(1)} copy-done((bf16[416,1152]{1,0:T(8,128)(2,1)S(1)}, bf16[416,1152]{1,0:T(8,128)(2,1)}, u32[]{:S(2)}) %copy-start) | copy-done | bytes 958488
  6.6 1.0 %fetch.2 = bf16[176,1152]{1,0:T(8,128)(2,1)} custom-call(bf16[416,1152]{1,0:T(8,128)(2,1)S(1)} %copy-done, bf16[96,1152]{1,0:T(8,128)(2,1)S(1)} %get-tuple-element.27.refs_0_), custom_call_target="tpu_custom_call" | custom-call | tf_op jit(solution)/shard_map/fetch/pallas_call | solution.py:49
  7.5 3.1 %collective-permute-start.2 = (bf16[176,1152]{1,0:T(8,128)(2,1)}, bf16[176,1152]{1,0:T(8,128)(2,1)}, u32[]{:S(2)}, u32[]{:S(2)}) collective-permute-start(bf16[176,1152]{1,0:T(8,128)(2,1)} %fetch.2), channel_id=1, source_target_pairs={{0,4},{4,8},{8,12},{12,16},{16,20},{20,24},{24,28},{28,0},{1,5},{5... | collective-permute-start | bytes 1216520 | tf_op jit(solution)/shard_map/ppermute | solution.py:21
  12.0 2.4 %fusion.18 = bf16[416,416]{1,0:T(8,128)(2,1)S(1)} fusion(bf16[416,1152]{1,0:T(8,128)(2,1)} %image_ref.3, bf16[416,1152]{1,0:T(8,128)(2,1)} %array_ref.3, s32[416]{0:T(512)S(1)} %bitcast.31, f32[]{:T(128)} %bitcast.29, f32[]{:T(128)} %bitcast.25), kind=kOutput, calls=%fused_computation.23 | convolution fusion | flops 400278528 | bytes 2264712 | tf_op jit(solution)/shard_map/dot_general | solution.py:25
  14.5 0.7 %fusion.21.refs_2_ = f32[416,1152]{1,0:T(8,128)S(1)} fusion(bf16[416,416]{1,0:T(8,128)(2,1)S(1)} %fusion.18, bf16[416,1152]{1,0:T(8,128)(2,1)S(1)} %copy-done.4), kind=kOutput, calls=%fused_computation.27 | convolution fusion | flops 398721024 | bytes 3221504 | tf_op jit(solution)/shard_map/dot_general | solution.py:29
  15.3 0.4 copy-done.1
  15.7 2.0 %fusion.20.refs_1_ = f32[416,1152]{1,0:T(8,128)} fusion(bf16[416,416]{1,0:T(8,128)(2,1)S(1)} %fusion.18, bf16[416,1152]{1,0:T(8,128)(2,1)S(1)} %copy-done.1), kind=kOutput, calls=%fused_computation.26 | convolution fusion | flops 398721024 | bytes 3221504 | tf_op jit(solution)/shard_map/dot_general | solution.py:33
  17.7 1.5 %copy-done.2 = f32[416,1152]{1,0:T(8,128)S(1)} copy-done((f32[416,1152]{1,0:T(8,128)S(1)}, f32[416,1152]{1,0:T(8,128)}, u32[]{:S(2)}) %copy-start.2) | copy-done | bytes 1916952
  19.2 3.2 %collective-permute-done.refs_0_ = bf16[416,1152]{1,0:T(8,128)(2,1)} collective-permute-done((bf16[416,1152]{1,0:T(8,128)(2,1)}, bf16[416,1152]{1,0:T(8,128)(2,1)}, u32[]{:S(2)}, u32[]{:S(2)}) %collective-permute-start) | collective-permute-done | bytes 958496 | tf_op jit(solution)/shard_map/ppermute | solution.py:21
  22.5 0.6 %collective-permute-start.4 = (bf16[48,1152]{1,0:T(8,128)(2,1)S(1)}, bf16[48,1152]{1,0:T(8,128)(2,1)S(1)}, u32[]{:S(2)}, u32[]{:S(2)}) collective-permute-start(bf16[48,1152]{1,0:T(8,128)(2,1)S(1)} %fetch.3.refs_2_), channel_id=1, source_target_pairs={{0,4},{4,8},{8,12},{12,16},{16,20},{20,24},{24,28},{28,0},{1,5},{5... | collective-permute-start | bytes 331784 | tf_op jit(solution)/shard_map/ppermute | solution.py:21
  23.1 2.0 %fusion.17 = bf16[416,416]{1,0:T(8,128)(2,1)S(1)} fusion(bf16[416,1152]{1,0:T(8,128)(2,1)} %pass_on.8.refs_0_.next_ref, bf16[416,1152]{1,0:T(8,128)(2,1)S(1)} %copy-done.1, f32[]{:T(128)} %bitcast.30, f32[]{:T(128)} %bitcast.28), kind=kOutput, calls=%fused_computation.22 | convolution fusion | flops 399759360 | bytes 2263048 | tf_op jit(solution)/shard_map/dot_general | solution.py:25
  25.1 0.7 %fusion.22.refs_1_ = f32[416,1152]{1,0:T(8,128)S(1)} fusion(bf16[416,416]{1,0:T(8,128)(2,1)S(1)} %fusion.17, bf16[416,1152]{1,0:T(8,128)(2,1)S(1)} %copy-done.1), kind=kOutput, calls=%fused_computation.28 | convolution fusion | flops 398721024 | bytes 3221504 | tf_op jit(solution)/shard_map/dot_general | solution.py:33
  25.9 1.6 %collective-permute-start.5 = (bf16[96,1152]{1,0:T(8,128)(2,1)S(1)}, bf16[96,1152]{1,0:T(8,128)(2,1)S(1)}, u32[]{:S(2)}, u32[]{:S(2)}) collective-permute-start(bf16[96,1152]{1,0:T(8,128)(2,1)S(1)} %pass_on.9.refs_2_.refs_1_), channel_id=1, source_target_pairs={{0,8},{4,12},{8,16},{12,20},{16,24},{20,28},{24,0},{28,4},{1,9},{5... | collective-permute-start | bytes 663560 | tf_op jit(solution)/shard_map/ppermute | solution.py:21
  27.5 3.1 %chunk.2 = (bf16[272,1152]{1,0:T(8,128)(2,1)S(1)}, bf16[272,1152]{1,0:T(8,128)(2,1)S(1)}, bf16[272,416]{1,0:T(8,128)(2,1)S(1)}, bf16[272,416]{1,0:T(8,128)(2,1)S(1)}) custom-call(f32[1]{0:T(128)} %copy.23.scale_ref, f32[1]{0:T(128)} %copy.24.bias_ref, s32[1]{0:T(128)} %bitcast.3.odd_ref, bf16[416,1152]{1,0:T(8,128)(2,1)S(1)} %copy-done.5, ...), custom_call_target="tpu_custom_call" | custom-call | flops 1042808832 | bytes 3796992 | tf_op jit(solution)/shard_map/chunk/pallas_call | solution.py:108
  30.6 4.2 %collective-permute-start.6 = (bf16[272,1152]{1,0:T(8,128)(2,1)S(1)}, bf16[272,1152]{1,0:T(8,128)(2,1)S(1)}, u32[]{:S(2)}, u32[]{:S(2)}) collective-permute-start(bf16[272,1152]{1,0:T(8,128)(2,1)S(1)} %get-tuple-element.16.refs_1_.refs_3_), channel_id=1, source_target_pairs={{0,28},{4,0},{8,4},{12,8},{16,12},{20,16},{24,20},{28,24},{1,29},{... | collective-permute-start | bytes 1880072 | tf_op jit(solution)/shard_map/ppermute | solution.py:21
  34.9 0.5 collective-permute-done.5.refs_0_
  35.4 2.4 %chunk.3 = (bf16[144,1152]{1,0:T(8,128)(2,1)S(1)}, bf16[144,1152]{1,0:T(8,128)(2,1)S(1)}, bf16[144,416]{1,0:T(8,128)(2,1)S(1)}, bf16[144,416]{1,0:T(8,128)(2,1)S(1)}) custom-call(f32[1]{0:T(128)} %copy.23.scale_ref, f32[1]{0:T(128)} %copy.24.bias_ref, s32[1]{0:T(128)} %bitcast.3.odd_ref, bf16[416,1152]{1,0:T(8,128)(2,1)S(1)} %copy-done.5, ...), custom_call_target="tpu_custom_call" | custom-call | flops 552075264 | bytes 2912256 | tf_op jit(solution)/shard_map/chunk/pallas_call | solution.py:108
  37.8 0.5 fusion.24
  38.3 0.8 %fusion.5.refs_1_ = bf16[416,1152]{1,0:T(8,128)(2,1)S(1)} fusion(f32[416,1152]{1,0:T(8,128)S(1)} %fusion.24, f32[416,1152]{1,0:T(8,128)S(1)} %fusion.22.refs_1_, bf16[272,416]{1,0:T(8,128)(2,1)S(1)} %get-tuple-element.20, bf16[272,1152]{1,0:T(8,128)(2,1)S(1)} %get-tuple-element.15, f32[]{:T(128)} %bitcast.26), kind=kOutput, calls=%fused_computation.8 | convolution fusion | flops 262619136 | bytes 5645316 | tf_op jit(solution)/shard_map/dot_general | solution.py:29
  39.1 0.6 %collective-permute-start.7 = (bf16[416,1152]{1,0:T(8,128)(2,1)S(1)}, bf16[416,1152]{1,0:T(8,128)(2,1)S(1)}, u32[]{:S(2)}, u32[]{:S(2)}) collective-permute-start(bf16[416,1152]{1,0:T(8,128)(2,1)S(1)} %fusion.5.refs_1_), channel_id=1, source_target_pairs={{0,1},{1,2},{2,3},{3,0},{4,5},{5,6},{6,7},{7,4},{8,9},{9,10},{10,1... | collective-permute-start | bytes 2875400 | tf_op jit(solution)/shard_map/ppermute | solution.py:21
  39.7 2.0 %fusion.total_ref = f32[416,1152]{1,0:T(8,128)S(1)} fusion(f32[416,1152]{1,0:T(8,128)S(1)} %fusion.21.refs_2_, bf16[416,416]{1,0:T(8,128)(2,1)S(1)} %fusion.17, bf16[416,1152]{1,0:T(8,128)(2,1)} %pass_on.8.refs_0_.next_ref, f32[]{:T(128)} %bitcast.24), kind=kOutput, calls=%fused_computation.2 | convolution fusion | flops 399679488 | bytes 5138436 | tf_op jit(solution)/shard_map/dot_general | solution.py:29
  41.7 2.4 %collective-permute-start.8 = (bf16[144,1152]{1,0:T(8,128)(2,1)S(1)}, bf16[144,1152]{1,0:T(8,128)(2,1)S(1)}, u32[]{:S(2)}, u32[]{:S(2)}) collective-permute-start(bf16[144,1152]{1,0:T(8,128)(2,1)S(1)} %pass_on.13), channel_id=1, source_target_pairs={{0,28},{4,0},{8,4},{12,8},{16,12},{20,16},{24,20},{28,24},{1,29},{... | collective-permute-start | bytes 995336 | tf_op jit(solution)/shard_map/ppermute | solution.py:21
  44.1 4.9 %collective-permute-done.6.back_ref = bf16[272,1152]{1,0:T(8,128)(2,1)S(1)} collective-permute-done((bf16[272,1152]{1,0:T(8,128)(2,1)S(1)}, bf16[272,1152]{1,0:T(8,128)(2,1)S(1)}, u32[]{:S(2)}, u32[]{:S(2)}) %collective-permute-start.6) | collective-permute-done | bytes 626720 | tf_op jit(solution)/shard_map/ppermute | solution.py:21
  49.0 0.9 %add_rows.3 = (bf16[416,1152]{1,0:T(8,128)(2,1)}, f32[8,128]{1,0:T(8,128)S(1)}) custom-call(f32[416,1152]{1,0:T(8,128)S(1)} %fusion.total_ref, bf16[272,1152]{1,0:T(8,128)(2,1)S(1)} %collective-permute-done.6.back_ref), custom_call_target="tpu_custom_call" | custom-call | tf_op jit(solution)/shard_map/add_rows/pallas_call | solution.py:147
  49.9 0.5 fusion.23
  50.4 1.0 %copy-done.3 = f32[416,1152]{1,0:T(8,128)S(1)} copy-done((f32[416,1152]{1,0:T(8,128)S(1)}, f32[416,1152]{1,0:T(8,128)}, u32[]{:S(2)}) %copy-start.3) | copy-done | bytes 1916952
  51.5 0.7 %fusion.2.total_ref = f32[416,1152]{1,0:T(8,128)S(1)} fusion(f32[416,1152]{1,0:T(8,128)S(1)} %fusion.23, f32[416,1152]{1,0:T(8,128)S(1)} %copy-done.3, bf16[272,416]{1,0:T(8,128)(2,1)S(1)} %get-tuple-element.14, bf16[272,1152]{1,0:T(8,128)(2,1)S(1)} %get-tuple-element.15, f32[]{:T(128)} %bitcast.27), kind=kOutput, calls=%fused_computation.5 | convolution fusion | flops 262139904 | bytes 6603780 | tf_op jit(solution)/shard_map/dot_general | solution.py:29
  52.4 1.0 %add_rows.4 = (bf16[416,1152]{1,0:T(8,128)(2,1)}, f32[8,128]{1,0:T(8,128)S(1)}) custom-call(f32[416,1152]{1,0:T(8,128)S(1)} %fusion.2.total_ref, bf16[416,1152]{1,0:T(8,128)(2,1)S(1)} %collective-permute-done.7.back_ref), custom_call_target="tpu_custom_call" | custom-call | tf_op jit(solution)/shard_map/add_rows/pallas_call | solution.py:147
  53.5 2.7 %collective-permute-done.8.back_ref = bf16[144,1152]{1,0:T(8,128)(2,1)S(1)} collective-permute-done((bf16[144,1152]{1,0:T(8,128)(2,1)S(1)}, bf16[144,1152]{1,0:T(8,128)(2,1)S(1)}, u32[]{:S(2)}, u32[]{:S(2)}) %collective-permute-start.8) | collective-permute-done | bytes 331808 | tf_op jit(solution)/shard_map/ppermute | solution.py:21
  56.1 0.8 %add_rows.5 = bf16[416,1152]{1,0:T(8,128)(2,1)} custom-call(f32[416,1152]{1,0:T(8,128)S(1)} %fusion.total_ref, bf16[144,1152]{1,0:T(8,128)(2,1)S(1)} %collective-permute-done.8.back_ref, bf16[416,1152]{1,0:T(8,128)(2,1)} %get-tuple-element.24.refs_0_, f32[8,128]{1,0:T(8,128)S(1)} %get-tuple-element.25.refs_1_), custom_call_target="tpu_custom_call", output_to_operand_aliasing={{}: (2, {})} | custom-call | tf_op jit(solution)/shard_map/add_rows/pallas_call | solution.py:147
  (25 shorter events, 0.5 us)
Async XLA Ops:
  0.6 11.4 %copy-start.6 = (s32[1,416]{1,0:T(1,128)S(1)}, s32[1,416]{1,0:T(1,128)}, u32[]{:S(2)}) copy-start(s32[1,416]{1,0:T(1,128)} %param.7) | copy-start | bytes 4996
  2.4 23.5 %collective-permute-start.3 = (bf16[96,1152]{1,0:T(8,128)(2,1)}, bf16[96,1152]{1,0:T(8,128)(2,1)S(1)}, u32[]{:S(2)}, u32[]{:S(2)}) collective-permute-start(bf16[96,1152]{1,0:T(8,128)(2,1)} %get-tuple-element.26), channel_id=1, source_target_pairs={{0,4},{4,0},{8,12},{12,8},{16,20},{20,16},{24,28},{28,24},{1,5},{5... | collective-permute-start | bytes 663560 | tf_op jit(solution)/shard_map/ppermute | solution.py:163
  5.3 12.3 %collective-permute-start.1 = (bf16[96,1152]{1,0:T(8,128)(2,1)S(1)}, bf16[96,1152]{1,0:T(8,128)(2,1)S(1)}, u32[]{:S(2)}, u32[]{:S(2)}) collective-permute-start(bf16[96,1152]{1,0:T(8,128)(2,1)S(1)} %get-tuple-element.27.refs_0_), channel_id=1, source_target_pairs={{0,4},{4,8},{8,12},{12,16},{16,20},{20,24},{24,28},{28,0},{1,5},{5... | collective-permute-start | bytes 663560 | tf_op jit(solution)/shard_map/ppermute | solution.py:21
  5.4 1.2 %copy-start = (bf16[416,1152]{1,0:T(8,128)(2,1)S(1)}, bf16[416,1152]{1,0:T(8,128)(2,1)}, u32[]{:S(2)}) copy-start(bf16[416,1152]{1,0:T(8,128)(2,1)} %array_ref.3) | copy-start | bytes 2875396
  7.5 20.0 %collective-permute-start.2 = (bf16[176,1152]{1,0:T(8,128)(2,1)}, bf16[176,1152]{1,0:T(8,128)(2,1)}, u32[]{:S(2)}, u32[]{:S(2)}) collective-permute-start(bf16[176,1152]{1,0:T(8,128)(2,1)} %fetch.2), channel_id=1, source_target_pairs={{0,4},{4,8},{8,12},{12,16},{16,20},{20,24},{24,28},{28,0},{1,5},{5... | collective-permute-start | bytes 1216520 | tf_op jit(solution)/shard_map/ppermute | solution.py:21
  10.6 11.8 %collective-permute-start = (bf16[416,1152]{1,0:T(8,128)(2,1)}, bf16[416,1152]{1,0:T(8,128)(2,1)}, u32[]{:S(2)}, u32[]{:S(2)}) collective-permute-start(bf16[416,1152]{1,0:T(8,128)(2,1)} %image_ref.3), channel_id=1, source_target_pairs={{0,3},{1,0},{2,1},{3,2},{4,7},{5,4},{6,5},{7,6},{8,11},{9,8},{10,9... | collective-permute-start | bytes 2875400 | tf_op jit(solution)/shard_map/ppermute | solution.py:21
  12.0 2.5 %copy-start.4 = (bf16[416,1152]{1,0:T(8,128)(2,1)S(1)}, bf16[416,1152]{1,0:T(8,128)(2,1)}, u32[]{:S(2)}) copy-start(bf16[416,1152]{1,0:T(8,128)(2,1)} %image_ref.3) | copy-start | bytes 2875396
  14.5 1.2 %copy-start.1 = (bf16[416,1152]{1,0:T(8,128)(2,1)S(1)}, bf16[416,1152]{1,0:T(8,128)(2,1)}, u32[]{:S(2)}) copy-start(bf16[416,1152]{1,0:T(8,128)(2,1)} %array_ref.3) | copy-start | bytes 2875396
  17.7 1.5 %copy-start.2 = (f32[416,1152]{1,0:T(8,128)S(1)}, f32[416,1152]{1,0:T(8,128)}, u32[]{:S(2)}) copy-start(f32[416,1152]{1,0:T(8,128)} %fusion.20.refs_1_) | copy-start | bytes 5750788
  22.5 12.3 %collective-permute-start.4 = (bf16[48,1152]{1,0:T(8,128)(2,1)S(1)}, bf16[48,1152]{1,0:T(8,128)(2,1)S(1)}, u32[]{:S(2)}, u32[]{:S(2)}) collective-permute-start(bf16[48,1152]{1,0:T(8,128)(2,1)S(1)} %fetch.3.refs_2_), channel_id=1, source_target_pairs={{0,4},{4,8},{8,12},{12,16},{16,20},{20,24},{24,28},{28,0},{1,5},{5... | collective-permute-start | bytes 331784 | tf_op jit(solution)/shard_map/ppermute | solution.py:21
  25.9 1.7 %copy-start.5 = (bf16[416,1152]{1,0:T(8,128)(2,1)S(1)}, bf16[416,1152]{1,0:T(8,128)(2,1)}, u32[]{:S(2)}) copy-start(bf16[416,1152]{1,0:T(8,128)(2,1)} %image_ref.3) | copy-start | bytes 2875396
  25.9 9.5 %collective-permute-start.5 = (bf16[96,1152]{1,0:T(8,128)(2,1)S(1)}, bf16[96,1152]{1,0:T(8,128)(2,1)S(1)}, u32[]{:S(2)}, u32[]{:S(2)}) collective-permute-start(bf16[96,1152]{1,0:T(8,128)(2,1)S(1)} %pass_on.9.refs_2_.refs_1_), channel_id=1, source_target_pairs={{0,8},{4,12},{8,16},{12,20},{16,24},{20,28},{24,0},{28,4},{1,9},{5... | collective-permute-start | bytes 663560 | tf_op jit(solution)/shard_map/ppermute | solution.py:21
  30.6 18.4 %collective-permute-start.6 = (bf16[272,1152]{1,0:T(8,128)(2,1)S(1)}, bf16[272,1152]{1,0:T(8,128)(2,1)S(1)}, u32[]{:S(2)}, u32[]{:S(2)}) collective-permute-start(bf16[272,1152]{1,0:T(8,128)(2,1)S(1)} %get-tuple-element.16.refs_1_.refs_3_), channel_id=1, source_target_pairs={{0,28},{4,0},{8,4},{12,8},{16,12},{20,16},{24,20},{28,24},{1,29},{... | collective-permute-start | bytes 1880072 | tf_op jit(solution)/shard_map/ppermute | solution.py:21
  39.1 13.3 %collective-permute-start.7 = (bf16[416,1152]{1,0:T(8,128)(2,1)S(1)}, bf16[416,1152]{1,0:T(8,128)(2,1)S(1)}, u32[]{:S(2)}, u32[]{:S(2)}) collective-permute-start(bf16[416,1152]{1,0:T(8,128)(2,1)S(1)} %fusion.5.refs_1_), channel_id=1, source_target_pairs={{0,1},{1,2},{2,3},{3,0},{4,5},{5,6},{6,7},{7,4},{8,9},{9,10},{10,1... | collective-permute-start | bytes 2875400 | tf_op jit(solution)/shard_map/ppermute | solution.py:21
  41.7 14.5 %collective-permute-start.8 = (bf16[144,1152]{1,0:T(8,128)(2,1)S(1)}, bf16[144,1152]{1,0:T(8,128)(2,1)S(1)}, u32[]{:S(2)}, u32[]{:S(2)}) collective-permute-start(bf16[144,1152]{1,0:T(8,128)(2,1)S(1)} %pass_on.13), channel_id=1, source_target_pairs={{0,28},{4,0},{8,4},{12,8},{16,12},{20,16},{24,20},{28,24},{1,29},{... | collective-permute-start | bytes 995336 | tf_op jit(solution)/shard_map/ppermute | solution.py:21
  49.9 1.5 %copy-start.3 = (f32[416,1152]{1,0:T(8,128)S(1)}, f32[416,1152]{1,0:T(8,128)}, u32[]{:S(2)}) copy-start(f32[416,1152]{1,0:T(8,128)} %fusion.20.refs_1_) | copy-start | bytes 5750788

commit v22 on v18

--- a/solution.py
+++ b/solution.py
@@ -38,7 +38,7 @@
     return list(zip(cuts[:-1], cuts[1:]))
 
 
-def fetch(array, lo, hi, after):
+def fetch(array, lo, hi, after, limit=2 * MIB):
     def kernel(array_ref, *refs):
         out_ref, sem = refs[-2:]
         copy = pltpu.make_async_copy(array_ref.at[pl.ds(lo, hi - lo), :], out_ref, sem)
@@ -51,7 +51,7 @@
         in_specs=[ANY] * (1 + len(after)),
         out_specs=VMEM,
         scratch_shapes=[pltpu.SemaphoreType.DMA],
-        compiler_params=pltpu.CompilerParams(vmem_limit_bytes=2 * MIB),
+        compiler_params=pltpu.CompilerParams(vmem_limit_bytes=limit),
         name="fetch",
     )(array, *after)
 
@@ -151,7 +151,7 @@
     scale = factor[0]
     bias = shift[0]
     cuts = row_cuts(text.shape[0])
-    first = text[: cuts[0][1]]
+    first = fetch(text, *cuts[0], [], 53 * MIB + MIB // 4)
     part = [shifted(first, "blk", 1)]
     image_next = shifted(image, "grp", -1)
     part.append(shifted(fetch(text, *cuts[1], [first]), "blk", 1))

time: 50.3 us -> 50.4 us (level)
  Pallas kernels: 6.65 us -> 7.71 us
  local copies, waits for them, and re-layouts: 2.2 us -> 1.21 us
    pallas_call x3 -> x4, Pallas kernels: 0.25 us -> 1.3 us  [fetch(): pl.pallas_call(kernel, out_shape=jax.ShapeDtypeStruct((hi - lo, array.sha...]
    slice x1 -> x0, local copies, waits for them, and re-layouts: 0.99 us -> none  [body(): first = text[:cuts[0][1]]]
where the time goes in v22:
time: 50.4 us; the launch traced here: 50.2 us
  waiting for transfers between devices  21.9 us (43%)
  starting transfers between devices  10.2 us (20%)
  Pallas kernels  7.71 us (15%)
  matrix products  6.96 us (14%)
  between operations  2.15 us (4%)
  local copies, waits for them, and re-layouts  1.21 us (2%)
    ppermute x8, waiting for transfers between devices, shifted(): lax.ppermute(shard, axis, [(i, (i + by) % devices) for i in range(devices)])  21.9 us
    ppermute x8, starting transfers between devices, shifted(): lax.ppermute(shard, axis, [(i, (i + by) % devices) for i in range(devices)])  10.2 us
    dot_general x6, matrix products, dot_tn(): lax.dot_general(a, b, (((0,), (0,)), ((), ())), preferred_element_type=jn...  3.83 us
    pallas_call x4, Pallas kernels, add_rows(): pl.pallas_call(kernel, out_shape=(out, jax.ShapeDtypeStruct((8, 128), jnp...  3.32 us
    pallas_call x2, Pallas kernels, chunk(): pl.pallas_call(functools.partial(chunk_kernel, len(pieces), lasts), out_s...  3.08 us
    dot_general x2, matrix products, dot_nt(): lax.dot_general(a, b, (((1,), (1,)), ((), ())), preferred_element_type=jn...  1.72 us
    dot_general x2, matrix products, dot_nn(): return jnp.dot(a, b, preferred_element_type=jnp.float32)  1.4 us
    pallas_call x4, Pallas kernels, fetch(): pl.pallas_call(kernel, out_shape=jax.ShapeDtypeStruct((hi - lo, array.sha...  1.3 us
  transfers between devices with their start and end apart: 8, of which 5 were waited for; matrix products, arithmetic and copies ran while one was open for 14% of the time, Pallas kernels for 12%

profile of v22, /device:TPU:0, one launch (start us, length us, event | category | flops | bytes accessed | tf_op | source)
XLA Modules:
  0.0 50.2 jit_solution(16999635673197767441)
XLA Ops:
  0.7 1.1 %fetch.4.refs_0_ = bf16[128,1152]{1,0:T(8,128)(2,1)S(1)} custom-call(bf16[416,1152]{1,0:T(8,128)(2,1)} %array_ref.7), custom_call_target="tpu_custom_call" | custom-call | tf_op jit(solution)/shard_map/fetch/pallas_call | solution.py:48
  1.7 3.0 %collective-permute-start = (bf16[128,1152]{1,0:T(8,128)(2,1)S(1)}, bf16[128,1152]{1,0:T(8,128)(2,1)S(1)}, u32[]{:S(2)}, u32[]{:S(2)}) collective-permute-start(bf16[128,1152]{1,0:T(8,128)(2,1)S(1)} %fetch.4.refs_0_), channel_id=1, source_target_pairs={{0,4},{4,8},{8,12},{12,16},{16,20},{20,24},{24,28},{28,0},{1,5},{5... | collective-permute-start | bytes 884744 | tf_op jit(solution)/shard_map/ppermute | solution.py:20
  4.7 0.7 %collective-permute-start.1 = (bf16[416,1152]{1,0:T(8,128)(2,1)}, bf16[416,1152]{1,0:T(8,128)(2,1)S(1)}, u32[]{:S(2)}, u32[]{:S(2)}) collective-permute-start(bf16[416,1152]{1,0:T(8,128)(2,1)} %image_ref.3), channel_id=1, source_target_pairs={{0,3},{1,0},{2,1},{3,2},{4,7},{5,4},{6,5},{7,6},{8,11},{9,8},{10,9... | collective-permute-start | bytes 2875400 | tf_op jit(solution)/shard_map/ppermute | solution.py:20
  5.4 1.2 %copy-done = bf16[416,1152]{1,0:T(8,128)(2,1)S(1)} copy-done((bf16[416,1152]{1,0:T(8,128)(2,1)S(1)}, bf16[416,1152]{1,0:T(8,128)(2,1)}, u32[]{:S(2)}) %copy-start) | copy-done | bytes 958488
  6.6 0.1 fetch.6
  6.7 1.6 %collective-permute-start.2 = (bf16[240,1152]{1,0:T(8,128)(2,1)S(1)}, bf16[240,1152]{1,0:T(8,128)(2,1)S(1)}, u32[]{:S(2)}, u32[]{:S(2)}) collective-permute-start(bf16[240,1152]{1,0:T(8,128)(2,1)S(1)} %fetch.6), channel_id=1, source_target_pairs={{0,4},{4,8},{8,12},{12,16},{16,20},{20,24},{24,28},{28,0},{1,5},{5... | collective-permute-start | bytes 1658888 | tf_op jit(solution)/shard_map/ppermute | solution.py:20
  9.6 6.0 %collective-permute-done.refs_0_ = bf16[128,1152]{1,0:T(8,128)(2,1)S(1)} collective-permute-done((bf16[128,1152]{1,0:T(8,128)(2,1)S(1)}, bf16[128,1152]{1,0:T(8,128)(2,1)S(1)}, u32[]{:S(2)}, u32[]{:S(2)}) %collective-permute-start) | collective-permute-done | bytes 294944 | tf_op jit(solution)/shard_map/ppermute | solution.py:20
  15.6 0.9 %subtract_convert_fusion.refs_0_ = bf16[416,416]{1,0:T(8,128)(2,1)S(1)} fusion(s32[416]{0:T(512)S(1)} %bitcast.30, f32[]{:T(128)} %bitcast.28, bf16[416,1152]{1,0:T(8,128)(2,1)S(1)} %copy-done.2, bf16[416,1152]{1,0:T(8,128)(2,1)S(1)} %copy-done.1, f32[]{:T(128)} %bitcast.24), kind=kOutput, calls=%fused_computation.22 | convolution fusion | flops 400278528 | bytes 2264712 | tf_op jit(solution)/shard_map/dot_general | solution.py:24
  16.5 0.2 fetch.7
  16.7 0.1 collective-permute-start.3
  16.7 0.7 %fusion.17.refs_2_ = f32[416,1152]{1,0:T(8,128)S(1)} fusion(bf16[416,416]{1,0:T(8,128)(2,1)S(1)} %subtract_convert_fusion.refs_0_, bf16[416,1152]{1,0:T(8,128)(2,1)S(1)} %copy-done.2), kind=kOutput, calls=%fused_computation.25 | convolution fusion | flops 398721024 | bytes 3221504 | tf_op jit(solution)/shard_map/dot_general | solution.py:28
  17.5 0.7 %fusion.16.refs_1_ = f32[416,1152]{1,0:T(8,128)S(1)} fusion(bf16[416,416]{1,0:T(8,128)(2,1)S(1)} %subtract_convert_fusion.refs_0_, bf16[416,1152]{1,0:T(8,128)(2,1)S(1)} %copy-done.1), kind=kOutput, calls=%fused_computation.24 | convolution fusion | flops 398721024 | bytes 3221504 | tf_op jit(solution)/shard_map/dot_general | solution.py:32
  18.2 0.8 %fusion.15 = bf16[416,416]{1,0:T(8,128)(2,1)S(1)} fusion(bf16[416,1152]{1,0:T(8,128)(2,1)S(1)} %pass_on.5.next_ref, bf16[416,1152]{1,0:T(8,128)(2,1)S(1)} %copy-done.1, f32[]{:T(128)} %bitcast.29, f32[]{:T(128)} %bitcast.27), kind=kOutput, calls=%fused_computation.21 | convolution fusion | flops 399759360 | bytes 2263048 | tf_op jit(solution)/shard_map/dot_general | solution.py:24
  19.1 1.2 %chunk.2 = (bf16[128,1152]{1,0:T(8,128)(2,1)S(1)}, bf16[128,416]{1,0:T(8,128)(2,1)S(1)}, bf16[128,416]{1,0:T(8,128)(2,1)S(1)}, bf16[128,1152]{1,0:T(8,128)(2,1)S(1)}) custom-call(f32[1]{0:T(128)} %copy.21.scale_ref, f32[1]{0:T(128)} %copy.22.bias_ref, bf16[416,1152]{1,0:T(8,128)(2,1)S(1)} %copy-done.2, bf16[416,1152]{1,0:T(8,128)(2,1)S(1)} %pass_on.5.next_ref, ...), custom_call_target="tpu_custom_call" | custom-call | flops 490733568 | bytes 2801664 | tf_op jit(solution)/shard_map/chunk/pallas_call | solution.py:99
  20.3 0.7 %fusion.18 = f32[416,1152]{1,0:T(8,128)S(1)} fusion(bf16[416,416]{1,0:T(8,128)(2,1)S(1)} %fusion.15, bf16[416,1152]{1,0:T(8,128)(2,1)S(1)} %copy-done.1), kind=kOutput, calls=%fused_computation.26 | convolution fusion | flops 398721024 | bytes 3221504 | tf_op jit(solution)/shard_map/dot_general | solution.py:32
  21.0 0.4 convolution_add_fusion.1.refs_2_
  21.4 6.0 %collective-permute-done.2.refs_1_.refs_0_ = bf16[240,1152]{1,0:T(8,128)(2,1)S(1)} collective-permute-done((bf16[240,1152]{1,0:T(8,128)(2,1)S(1)}, bf16[240,1152]{1,0:T(8,128)(2,1)S(1)}, u32[]{:S(2)}, u32[]{:S(2)}) %collective-permute-start.2) | collective-permute-done | bytes 552992 | tf_op jit(solution)/shard_map/ppermute | solution.py:20
  27.4 2.1 %collective-permute-start.4 = (bf16[128,1152]{1,0:T(8,128)(2,1)S(1)}, bf16[128,1152]{1,0:T(8,128)(2,1)S(1)}, u32[]{:S(2)}, u32[]{:S(2)}) collective-permute-start(bf16[128,1152]{1,0:T(8,128)(2,1)S(1)} %pass_on.6.refs_2_), channel_id=1, source_target_pairs={{0,28},{4,0},{8,4},{12,8},{16,12},{20,16},{24,20},{28,24},{1,29},{... | collective-permute-start | bytes 884744 | tf_op jit(solution)/shard_map/ppermute | solution.py:20
  29.5 1.9 %chunk.3 = (bf16[288,1152]{1,0:T(8,128)(2,1)S(1)}, bf16[288,416]{1,0:T(8,128)(2,1)S(1)}, bf16[288,416]{1,0:T(8,128)(2,1)S(1)}, bf16[240,1152]{1,0:T(8,128)(2,1)S(1)}, bf16[48,1152]{1,0:T(8,128)(2,1)S(1)}) custom-call(f32[1]{0:T(128)} %copy.21.scale_ref, f32[1]{0:T(128)} %copy.22.bias_ref, bf16[416,1152]{1,0:T(8,128)(2,1)S(1)} %copy-done.2, ...), custom_call_target="tpu_custom_call" | custom-call | flops 1104150528 | bytes 3907584 | tf_op jit(solution)/shard_map/chunk/pallas_call | solution.py:99
  31.4 0.7 %fusion.4.refs_1_ = bf16[416,1152]{1,0:T(8,128)(2,1)S(1)} fusion(f32[416,1152]{1,0:T(8,128)S(1)} %convolution_add_fusion.1.refs_2_, bf16[288,416]{1,0:T(8,128)(2,1)S(1)} %get-tuple-element.22, bf16[288,1152]{1,0:T(8,128)(2,1)S(1)} %get-tuple-element.21, f32[]{:T(128)} %bitcast.25), kind=kOutput, calls=%fused_computation.8 | convolution fusion | flops 277475328 | bytes 3778564 | tf_op jit(solution)/shard_map/dot_general | solution.py:28
  32.2 1.5 %collective-permute-start.7 = (bf16[240,1152]{1,0:T(8,128)(2,1)S(1)}, bf16[240,1152]{1,0:T(8,128)(2,1)S(1)}, u32[]{:S(2)}, u32[]{:S(2)}) collective-permute-start(bf16[240,1152]{1,0:T(8,128)(2,1)S(1)} %pass_on.8.refs_1_), channel_id=1, source_target_pairs={{0,28},{4,0},{8,4},{12,8},{16,12},{20,16},{24,20},{28,24},{1,29},{... | collective-permute-start | bytes 1658888 | tf_op jit(solution)/shard_map/ppermute | solution.py:20
  33.7 1.3 %collective-permute-start.6 = (bf16[48,1152]{1,0:T(8,128)(2,1)S(1)}, bf16[48,1152]{1,0:T(8,128)(2,1)S(1)}, u32[]{:S(2)}, u32[]{:S(2)}) collective-permute-start(bf16[48,1152]{1,0:T(8,128)(2,1)S(1)} %pass_on.9), channel_id=1, source_target_pairs={{0,28},{4,0},{8,4},{12,8},{16,12},{20,16},{24,20},{28,24},{1,29},{... | collective-permute-start | bytes 331784 | tf_op jit(solution)/shard_map/ppermute | solution.py:20
  35.0 0.7 %fusion.total_ref = f32[416,1152]{1,0:T(8,128)S(1)} fusion(f32[416,1152]{1,0:T(8,128)S(1)} %fusion.17.refs_2_, bf16[416,416]{1,0:T(8,128)(2,1)S(1)} %fusion.15, bf16[416,1152]{1,0:T(8,128)(2,1)S(1)} %pass_on.5.next_ref, f32[]{:T(128)} %bitcast.23), kind=kOutput, calls=%fused_computation.1 | convolution fusion | flops 399679488 | bytes 5138436 | tf_op jit(solution)/shard_map/dot_general | solution.py:28
  35.8 0.8 %add_rows.4 = (bf16[416,1152]{1,0:T(8,128)(2,1)}, f32[8,128]{1,0:T(8,128)S(1)}) custom-call(f32[416,1152]{1,0:T(8,128)S(1)} %fusion.total_ref, bf16[128,1152]{1,0:T(8,128)(2,1)S(1)} %collective-permute-done.4.back_ref), custom_call_target="tpu_custom_call" | custom-call | tf_op jit(solution)/shard_map/add_rows/pallas_call | solution.py:138
  36.5 0.7 %fusion.19 = f32[416,1152]{1,0:T(8,128)S(1)} fusion(bf16[288,416]{1,0:T(8,128)(2,1)S(1)} %pass_on.7, bf16[288,1152]{1,0:T(8,128)(2,1)S(1)} %get-tuple-element.21), kind=kOutput, calls=%fused_computation.27 | convolution fusion | flops 276037632 | bytes 2820096 | tf_op jit(solution)/shard_map/dot_general | solution.py:28
  37.3 0.4 fusion.2.total_ref
  37.7 7.7 %collective-permute-done.5.back_ref = bf16[416,1152]{1,0:T(8,128)(2,1)S(1)} collective-permute-done((bf16[416,1152]{1,0:T(8,128)(2,1)S(1)}, bf16[416,1152]{1,0:T(8,128)(2,1)S(1)}, u32[]{:S(2)}, u32[]{:S(2)}) %collective-permute-start.5) | collective-permute-done | bytes 958496 | tf_op jit(solution)/shard_map/ppermute | solution.py:20
  45.4 1.0 %add_rows.5 = (bf16[416,1152]{1,0:T(8,128)(2,1)}, f32[8,128]{1,0:T(8,128)S(1)}) custom-call(f32[416,1152]{1,0:T(8,128)S(1)} %fusion.2.total_ref, bf16[416,1152]{1,0:T(8,128)(2,1)S(1)} %collective-permute-done.5.back_ref), custom_call_target="tpu_custom_call" | custom-call | tf_op jit(solution)/shard_map/add_rows/pallas_call | solution.py:138
  46.5 0.7 %collective-permute-done.7.back_ref = bf16[240,1152]{1,0:T(8,128)(2,1)S(1)} collective-permute-done((bf16[240,1152]{1,0:T(8,128)(2,1)S(1)}, bf16[240,1152]{1,0:T(8,128)(2,1)S(1)}, u32[]{:S(2)}, u32[]{:S(2)}) %collective-permute-start.7) | collective-permute-done | bytes 552992 | tf_op jit(solution)/shard_map/ppermute | solution.py:20
  47.1 0.9 %add_rows.6.refs_0_ = bf16[416,1152]{1,0:T(8,128)(2,1)} custom-call(f32[416,1152]{1,0:T(8,128)S(1)} %fusion.total_ref, bf16[240,1152]{1,0:T(8,128)(2,1)S(1)} %collective-permute-done.7.back_ref, bf16[416,1152]{1,0:T(8,128)(2,1)} %get-tuple-element.26.refs_0_, f32[8,128]{1,0:T(8,128)S(1)} %get-tuple-element.27.refs_1_), custom_call_target="tpu_custom_call", output_to_operand_aliasing={{}: (2, {})} | custom-call | tf_op jit(solution)/shard_map/add_rows/pallas_call | solution.py:138
  48.0 1.5 %collective-permute-done.6.back_ref = bf16[48,1152]{1,0:T(8,128)(2,1)S(1)} collective-permute-done((bf16[48,1152]{1,0:T(8,128)(2,1)S(1)}, bf16[48,1152]{1,0:T(8,128)(2,1)S(1)}, u32[]{:S(2)}, u32[]{:S(2)}) %collective-permute-start.6) | collective-permute-done | bytes 110624 | tf_op jit(solution)/shard_map/ppermute | solution.py:20
  49.5 0.7 %add_rows.7 = bf16[416,1152]{1,0:T(8,128)(2,1)} custom-call(f32[416,1152]{1,0:T(8,128)S(1)} %fusion.total_ref, bf16[48,1152]{1,0:T(8,128)(2,1)S(1)} %collective-permute-done.6.back_ref, bf16[416,1152]{1,0:T(8,128)(2,1)} %add_rows.6.refs_0_), custom_call_target="tpu_custom_call", output_to_operand_aliasing={{}: (2, {})} | custom-call | tf_op jit(solution)/shard_map/add_rows/pallas_call | solution.py:138
  (17 shorter events, 0.1 us)
Async XLA Ops:
  0.6 15.0 %copy-start.1 = (bf16[416,1152]{1,0:T(8,128)(2,1)S(1)}, bf16[416,1152]{1,0:T(8,128)(2,1)}, u32[]{:S(2)}) copy-start(bf16[416,1152]{1,0:T(8,128)(2,1)} %array_ref.7) | copy-start | bytes 2875396
  0.6 14.9 %copy-start.3 = (s32[1,416]{1,0:T(1,128)S(1)}, s32[1,416]{1,0:T(1,128)}, u32[]{:S(2)}) copy-start(s32[1,416]{1,0:T(1,128)} %array_ref.5) | copy-start | bytes 4996
  1.7 13.9 %collective-permute-start = (bf16[128,1152]{1,0:T(8,128)(2,1)S(1)}, bf16[128,1152]{1,0:T(8,128)(2,1)S(1)}, u32[]{:S(2)}, u32[]{:S(2)}) collective-permute-start(bf16[128,1152]{1,0:T(8,128)(2,1)S(1)} %fetch.4.refs_0_), channel_id=1, source_target_pairs={{0,4},{4,8},{8,12},{12,16},{16,20},{20,24},{24,28},{28,0},{1,5},{5... | collective-permute-start | bytes 884744 | tf_op jit(solution)/shard_map/ppermute | solution.py:20
  4.7 13.5 %collective-permute-start.1 = (bf16[416,1152]{1,0:T(8,128)(2,1)}, bf16[416,1152]{1,0:T(8,128)(2,1)S(1)}, u32[]{:S(2)}, u32[]{:S(2)}) collective-permute-start(bf16[416,1152]{1,0:T(8,128)(2,1)} %image_ref.3), channel_id=1, source_target_pairs={{0,3},{1,0},{2,1},{3,2},{4,7},{5,4},{6,5},{7,6},{8,11},{9,8},{10,9... | collective-permute-start | bytes 2875400 | tf_op jit(solution)/shard_map/ppermute | solution.py:20
  5.4 1.2 %copy-start = (bf16[416,1152]{1,0:T(8,128)(2,1)S(1)}, bf16[416,1152]{1,0:T(8,128)(2,1)}, u32[]{:S(2)}) copy-start(bf16[416,1152]{1,0:T(8,128)(2,1)} %array_ref.7) | copy-start | bytes 2875396
  6.6 9.0 %copy-start.2 = (bf16[416,1152]{1,0:T(8,128)(2,1)S(1)}, bf16[416,1152]{1,0:T(8,128)(2,1)}, u32[]{:S(2)}) copy-start(bf16[416,1152]{1,0:T(8,128)(2,1)} %image_ref.3) | copy-start | bytes 2875396
  6.7 20.8 %collective-permute-start.2 = (bf16[240,1152]{1,0:T(8,128)(2,1)S(1)}, bf16[240,1152]{1,0:T(8,128)(2,1)S(1)}, u32[]{:S(2)}, u32[]{:S(2)}) collective-permute-start(bf16[240,1152]{1,0:T(8,128)(2,1)S(1)} %fetch.6), channel_id=1, source_target_pairs={{0,4},{4,8},{8,12},{12,16},{16,20},{20,24},{24,28},{28,0},{1,5},{5... | collective-permute-start | bytes 1658888 | tf_op jit(solution)/shard_map/ppermute | solution.py:20
  16.7 12.8 %collective-permute-start.3 = (bf16[48,1152]{1,0:T(8,128)(2,1)S(1)}, bf16[48,1152]{1,0:T(8,128)(2,1)S(1)}, u32[]{:S(2)}, u32[]{:S(2)}) collective-permute-start(bf16[48,1152]{1,0:T(8,128)(2,1)S(1)} %fetch.7), channel_id=1, source_target_pairs={{0,4},{4,8},{8,12},{12,16},{16,20},{20,24},{24,28},{28,0},{1,5},{5... | collective-permute-start | bytes 331784 | tf_op jit(solution)/shard_map/ppermute | solution.py:20
  27.4 8.3 %collective-permute-start.4 = (bf16[128,1152]{1,0:T(8,128)(2,1)S(1)}, bf16[128,1152]{1,0:T(8,128)(2,1)S(1)}, u32[]{:S(2)}, u32[]{:S(2)}) collective-permute-start(bf16[128,1152]{1,0:T(8,128)(2,1)S(1)} %pass_on.6.refs_2_), channel_id=1, source_target_pairs={{0,28},{4,0},{8,4},{12,8},{16,12},{20,16},{24,20},{28,24},{1,29},{... | collective-permute-start | bytes 884744 | tf_op jit(solution)/shard_map/ppermute | solution.py:20
  32.1 13.3 %collective-permute-start.5 = (bf16[416,1152]{1,0:T(8,128)(2,1)S(1)}, bf16[416,1152]{1,0:T(8,128)(2,1)S(1)}, u32[]{:S(2)}, u32[]{:S(2)}) collective-permute-start(bf16[416,1152]{1,0:T(8,128)(2,1)S(1)} %fusion.4.refs_1_), channel_id=1, source_target_pairs={{0,1},{1,2},{2,3},{3,0},{4,5},{5,6},{6,7},{7,4},{8,9},{9,10},{10,1... | collective-permute-start | bytes 2875400 | tf_op jit(solution)/shard_map/ppermute | solution.py:20
  32.2 14.9 %collective-permute-start.7 = (bf16[240,1152]{1,0:T(8,128)(2,1)S(1)}, bf16[240,1152]{1,0:T(8,128)(2,1)S(1)}, u32[]{:S(2)}, u32[]{:S(2)}) collective-permute-start(bf16[240,1152]{1,0:T(8,128)(2,1)S(1)} %pass_on.8.refs_1_), channel_id=1, source_target_pairs={{0,28},{4,0},{8,4},{12,8},{16,12},{20,16},{24,20},{28,24},{1,29},{... | collective-permute-start | bytes 1658888 | tf_op jit(solution)/shard_map/ppermute | solution.py:20
  33.7 15.8 %collective-permute-start.6 = (bf16[48,1152]{1,0:T(8,128)(2,1)S(1)}, bf16[48,1152]{1,0:T(8,128)(2,1)S(1)}, u32[]{:S(2)}, u32[]{:S(2)}) collective-permute-start(bf16[48,1152]{1,0:T(8,128)(2,1)S(1)} %pass_on.9), channel_id=1, source_target_pairs={{0,28},{4,0},{8,4},{12,8},{16,12},{20,16},{24,20},{28,24},{1,29},{... | collective-permute-start | bytes 331784 | tf_op jit(solution)/shard_map/ppermute | solution.py:20

commit v23 on v18

--- a/solution.py
+++ b/solution.py
@@ -171,11 +171,10 @@
     image_sent = dot_nn(next_own, text) + dot_tn(next0, part0)
     image_grad = image_grad + dot_tn(own0, part0)
 
-    sent0 = pass_on(sent0, [part[1], image_sent])
     back0 = shifted(sent0, "blk", -1)
 
     lasts = part[2].shape[0]
-    part1, own1, next1, sent1, sent2 = chunk(factor, shift, image, image_next, part[1:], [sent0], lasts)
+    part1, own1, next1, sent1, sent2 = chunk(factor, shift, image, image_next, part[1:], [sent0, image_sent], lasts)
     image_sent = (scale * (image_sent + dot_tn(next1, part1))).astype(jnp.bfloat16)
     image_back = shifted(image_sent, "grp", 1)
     sent1 = pass_on(sent1, [image_sent])

time: 50.3 us -> 55.5 us (1.10)
  starting transfers between devices: 10.2 us -> 15.8 us
    ppermute x8, starting transfers between devices: 10.2 us -> 15.8 us  [shifted(): lax.ppermute(shard, axis, [(i, (i + by) % devices) for i in range(devices)])]
  transfers between devices with their start and end apart: 8 -> 8, of which waited for: 5 -> 5; matrix products, arithmetic and copies ran while one was open for 14% -> 13% of each run, Pallas kernels for 12% -> 11%
where the time goes in v23:
time: 55.5 us; the launch traced here: 55.2 us
  waiting for transfers between devices  21.5 us (39%)
  starting transfers between devices  15.8 us (28%)
  matrix products  6.93 us (12%)
  Pallas kernels  6.63 us (12%)
  local copies, waits for them, and re-layouts  2.2 us (4%)
  between operations  2.14 us (4%)
    ppermute x8, waiting for transfers between devices, shifted(): lax.ppermute(shard, axis, [(i, (i + by) % devices) for i in range(devices)])  21.5 us
    ppermute x8, starting transfers between devices, shifted(): lax.ppermute(shard, axis, [(i, (i + by) % devices) for i in range(devices)])  15.8 us
    dot_general x6, matrix products, dot_tn(): lax.dot_general(a, b, (((0,), (0,)), ((), ())), preferred_element_type=jn...  3.81 us
    pallas_call x4, Pallas kernels, add_rows(): pl.pallas_call(kernel, out_shape=(out, jax.ShapeDtypeStruct((8, 128), jnp...  3.3 us
    pallas_call x2, Pallas kernels, chunk(): pl.pallas_call(functools.partial(chunk_kernel, len(pieces), lasts), out_s...  3.08 us
    dot_general x2, matrix products, dot_nt(): lax.dot_general(a, b, (((1,), (1,)), ((), ())), preferred_element_type=jn...  1.72 us
    dot_general x2, matrix products, dot_nn(): return jnp.dot(a, b, preferred_element_type=jnp.float32)  1.4 us
    unnamed x8, local copies, waits for them, and re-layouts  1.2 us
  transfers between devices with their start and end apart: 8, of which 5 were waited for; matrix products, arithmetic and copies ran while one was open for 13% of the time, Pallas kernels for 11%

profile of v23, /device:TPU:0, one launch (start us, length us, event | category | flops | bytes accessed | tf_op | source)
XLA Modules:
  0.0 55.2 jit_solution(13303468157951688460)
XLA Ops:
  0.6 1.0 %slice.3.refs_0_ = bf16[128,1152]{1,0:T(8,128)(2,1)S(1)} slice(bf16[416,1152]{1,0:T(8,128)(2,1)} %array_ref.5), slice={[0:128], [0:1152]} | slice | bytes 589824 | tf_op jit(solution)/shard_map/slice | solution.py:154
  1.6 3.0 %collective-permute-start = (bf16[128,1152]{1,0:T(8,128)(2,1)S(1)}, bf16[128,1152]{1,0:T(8,128)(2,1)S(1)}, u32[]{:S(2)}, u32[]{:S(2)}) collective-permute-start(bf16[128,1152]{1,0:T(8,128)(2,1)S(1)} %slice.3.refs_0_), channel_id=1, source_target_pairs={{0,4},{4,8},{8,12},{12,16},{16,20},{20,24},{24,28},{28,0},{1,5},{5... | collective-permute-start | bytes 884744 | tf_op jit(solution)/shard_map/ppermute | solution.py:20
  4.6 0.7 %collective-permute-start.1 = (bf16[416,1152]{1,0:T(8,128)(2,1)}, bf16[416,1152]{1,0:T(8,128)(2,1)S(1)}, u32[]{:S(2)}, u32[]{:S(2)}) collective-permute-start(bf16[416,1152]{1,0:T(8,128)(2,1)} %image_ref.3), channel_id=1, source_target_pairs={{0,3},{1,0},{2,1},{3,2},{4,7},{5,4},{6,5},{7,6},{8,11},{9,8},{10,9... | collective-permute-start | bytes 2875400 | tf_op jit(solution)/shard_map/ppermute | solution.py:20
  5.3 1.2 %copy-done = bf16[416,1152]{1,0:T(8,128)(2,1)S(1)} copy-done((bf16[416,1152]{1,0:T(8,128)(2,1)S(1)}, bf16[416,1152]{1,0:T(8,128)(2,1)}, u32[]{:S(2)}) %copy-start) | copy-done | bytes 958488
  6.5 0.1 fetch.4
  6.6 1.6 %collective-permute-start.2 = (bf16[240,1152]{1,0:T(8,128)(2,1)S(1)}, bf16[240,1152]{1,0:T(8,128)(2,1)S(1)}, u32[]{:S(2)}, u32[]{:S(2)}) collective-permute-start(bf16[240,1152]{1,0:T(8,128)(2,1)S(1)} %fetch.4), channel_id=1, source_target_pairs={{0,4},{4,8},{8,12},{12,16},{16,20},{20,24},{24,28},{28,0},{1,5},{5... | collective-permute-start | bytes 1658888 | tf_op jit(solution)/shard_map/ppermute | solution.py:20
  9.5 6.0 %collective-permute-done.refs_0_ = bf16[128,1152]{1,0:T(8,128)(2,1)S(1)} collective-permute-done((bf16[128,1152]{1,0:T(8,128)(2,1)S(1)}, bf16[128,1152]{1,0:T(8,128)(2,1)S(1)}, u32[]{:S(2)}, u32[]{:S(2)}) %collective-permute-start) | collective-permute-done | bytes 294944 | tf_op jit(solution)/shard_map/ppermute | solution.py:20
  15.5 0.9 %subtract_convert_fusion.refs_0_ = bf16[416,416]{1,0:T(8,128)(2,1)S(1)} fusion(s32[416]{0:T(512)S(1)} %bitcast.30, f32[]{:T(128)} %bitcast.28, bf16[416,1152]{1,0:T(8,128)(2,1)S(1)} %copy-done.2, bf16[416,1152]{1,0:T(8,128)(2,1)S(1)} %copy-done.1, f32[]{:T(128)} %bitcast.24), kind=kOutput, calls=%fused_computation.22 | convolution fusion | flops 400278528 | bytes 2264712 | tf_op jit(solution)/shard_map/dot_general | solution.py:24
  16.4 0.2 fetch.5
  16.6 0.1 collective-permute-start.3
  16.7 0.7 %fusion.16.refs_1_ = f32[416,1152]{1,0:T(8,128)S(1)} fusion(bf16[416,416]{1,0:T(8,128)(2,1)S(1)} %subtract_convert_fusion.refs_0_, bf16[416,1152]{1,0:T(8,128)(2,1)S(1)} %copy-done.1), kind=kOutput, calls=%fused_computation.24 | convolution fusion | flops 398721024 | bytes 3221504 | tf_op jit(solution)/shard_map/dot_general | solution.py:32
  17.4 0.7 %fusion.17.refs_2_ = f32[416,1152]{1,0:T(8,128)S(1)} fusion(bf16[416,416]{1,0:T(8,128)(2,1)S(1)} %subtract_convert_fusion.refs_0_, bf16[416,1152]{1,0:T(8,128)(2,1)S(1)} %copy-done.2), kind=kOutput, calls=%fused_computation.25 | convolution fusion | flops 398721024 | bytes 3221504 | tf_op jit(solution)/shard_map/dot_general | solution.py:28
  18.1 1.2 %chunk.2 = (bf16[128,1152]{1,0:T(8,128)(2,1)S(1)}, bf16[128,416]{1,0:T(8,128)(2,1)S(1)}, bf16[128,416]{1,0:T(8,128)(2,1)S(1)}, bf16[128,1152]{1,0:T(8,128)(2,1)S(1)}) custom-call(f32[1]{0:T(128)} %copy.19.scale_ref, f32[1]{0:T(128)} %copy.20.bias_ref, bf16[416,1152]{1,0:T(8,128)(2,1)S(1)} %copy-done.2, bf16[416,1152]{1,0:T(8,128)(2,1)S(1)} %pass_on.4.next_ref, ...), custom_call_target="tpu_custom_call" | custom-call | flops 490733568 | bytes 2801664 | tf_op jit(solution)/shard_map/chunk/pallas_call | solution.py:99
  19.3 4.8 %collective-permute-start.4 = (bf16[128,1152]{1,0:T(8,128)(2,1)S(1)}, bf16[128,1152]{1,0:T(8,128)(2,1)S(1)}, u32[]{:S(2)}, u32[]{:S(2)}) collective-permute-start(bf16[128,1152]{1,0:T(8,128)(2,1)S(1)} %get-tuple-element.17.refs_2_), channel_id=1, source_target_pairs={{0,28},{4,0},{8,4},{12,8},{16,12},{20,16},{24,20},{28,24},{1,29},{... | collective-permute-start | bytes 884744 | tf_op jit(solution)/shard_map/ppermute | solution.py:20
  24.1 0.8 %fusion.15 = bf16[416,416]{1,0:T(8,128)(2,1)S(1)} fusion(bf16[416,1152]{1,0:T(8,128)(2,1)S(1)} %pass_on.4.next_ref, bf16[416,1152]{1,0:T(8,128)(2,1)S(1)} %copy-done.1, f32[]{:T(128)} %bitcast.29, f32[]{:T(128)} %bitcast.27), kind=kOutput, calls=%fused_computation.21 | convolution fusion | flops 399759360 | bytes 2263048 | tf_op jit(solution)/shard_map/dot_general | solution.py:24
  24.9 0.7 %fusion.18 = f32[416,1152]{1,0:T(8,128)S(1)} fusion(bf16[416,416]{1,0:T(8,128)(2,1)S(1)} %fusion.15, bf16[416,1152]{1,0:T(8,128)(2,1)S(1)} %copy-done.1), kind=kOutput, calls=%fused_computation.26 | convolution fusion | flops 398721024 | bytes 3221504 | tf_op jit(solution)/shard_map/dot_general | solution.py:32
  25.7 0.4 convolution_add_fusion.1.refs_3_
  26.1 5.3 %collective-permute-done.3.refs_1_ = bf16[48,1152]{1,0:T(8,128)(2,1)S(1)} collective-permute-done((bf16[48,1152]{1,0:T(8,128)(2,1)S(1)}, bf16[48,1152]{1,0:T(8,128)(2,1)S(1)}, u32[]{:S(2)}, u32[]{:S(2)}) %collective-permute-start.3) | collective-permute-done | bytes 110624 | tf_op jit(solution)/shard_map/ppermute | solution.py:20
  31.4 1.9 %chunk.3 = (bf16[288,1152]{1,0:T(8,128)(2,1)S(1)}, bf16[288,416]{1,0:T(8,128)(2,1)S(1)}, bf16[288,416]{1,0:T(8,128)(2,1)S(1)}, bf16[240,1152]{1,0:T(8,128)(2,1)S(1)}, bf16[48,1152]{1,0:T(8,128)(2,1)S(1)}) custom-call(f32[1]{0:T(128)} %copy.19.scale_ref, f32[1]{0:T(128)} %copy.20.bias_ref, bf16[416,1152]{1,0:T(8,128)(2,1)S(1)} %copy-done.2, ...), custom_call_target="tpu_custom_call" | custom-call | flops 1104150528 | bytes 3907584 | tf_op jit(solution)/shard_map/chunk/pallas_call | solution.py:99
  33.3 0.7 %fusion.4.refs_1_ = bf16[416,1152]{1,0:T(8,128)(2,1)S(1)} fusion(f32[416,1152]{1,0:T(8,128)S(1)} %convolution_add_fusion.1.refs_3_, bf16[288,416]{1,0:T(8,128)(2,1)S(1)} %get-tuple-element.22, bf16[288,1152]{1,0:T(8,128)(2,1)S(1)} %get-tuple-element.21, f32[]{:T(128)} %bitcast.25), kind=kOutput, calls=%fused_computation.8 | convolution fusion | flops 277475328 | bytes 3778564 | tf_op jit(solution)/shard_map/dot_general | solution.py:28
  34.1 5.6 %collective-permute-start.7 = (bf16[240,1152]{1,0:T(8,128)(2,1)S(1)}, bf16[240,1152]{1,0:T(8,128)(2,1)S(1)}, u32[]{:S(2)}, u32[]{:S(2)}) collective-permute-start(bf16[240,1152]{1,0:T(8,128)(2,1)S(1)} %pass_on.6.refs_1_), channel_id=1, source_target_pairs={{0,28},{4,0},{8,4},{12,8},{16,12},{20,16},{24,20},{28,24},{1,29},{... | collective-permute-start | bytes 1658888 | tf_op jit(solution)/shard_map/ppermute | solution.py:20
  39.7 0.1 collective-permute-start.6
  39.8 0.7 %fusion.total_ref = f32[416,1152]{1,0:T(8,128)S(1)} fusion(f32[416,1152]{1,0:T(8,128)S(1)} %fusion.17.refs_2_, bf16[416,416]{1,0:T(8,128)(2,1)S(1)} %fusion.15, bf16[416,1152]{1,0:T(8,128)(2,1)S(1)} %pass_on.4.next_ref, f32[]{:T(128)} %bitcast.23), kind=kOutput, calls=%fused_computation.1 | convolution fusion | flops 399679488 | bytes 5138436 | tf_op jit(solution)/shard_map/dot_general | solution.py:28
  40.5 0.8 %add_rows.4 = (bf16[416,1152]{1,0:T(8,128)(2,1)}, f32[8,128]{1,0:T(8,128)S(1)}) custom-call(f32[416,1152]{1,0:T(8,128)S(1)} %fusion.total_ref, bf16[128,1152]{1,0:T(8,128)(2,1)S(1)} %collective-permute-done.4.back_ref), custom_call_target="tpu_custom_call" | custom-call | tf_op jit(solution)/shard_map/add_rows/pallas_call | solution.py:138
  41.3 0.7 %fusion.19 = f32[416,1152]{1,0:T(8,128)S(1)} fusion(bf16[288,416]{1,0:T(8,128)(2,1)S(1)} %pass_on.5, bf16[288,1152]{1,0:T(8,128)(2,1)S(1)} %get-tuple-element.21), kind=kOutput, calls=%fused_computation.27 | convolution fusion | flops 276037632 | bytes 2820096 | tf_op jit(solution)/shard_map/dot_general | solution.py:28
  42.0 0.4 fusion.2.total_ref
  42.5 4.9 %collective-permute-done.5.back_ref = bf16[416,1152]{1,0:T(8,128)(2,1)S(1)} collective-permute-done((bf16[416,1152]{1,0:T(8,128)(2,1)S(1)}, bf16[416,1152]{1,0:T(8,128)(2,1)S(1)}, u32[]{:S(2)}, u32[]{:S(2)}) %collective-permute-start.5) | collective-permute-done | bytes 958496 | tf_op jit(solution)/shard_map/ppermute | solution.py:20
  47.4 1.0 %add_rows.5 = (bf16[416,1152]{1,0:T(8,128)(2,1)}, f32[8,128]{1,0:T(8,128)S(1)}) custom-call(f32[416,1152]{1,0:T(8,128)S(1)} %fusion.2.total_ref, bf16[416,1152]{1,0:T(8,128)(2,1)S(1)} %collective-permute-done.5.back_ref), custom_call_target="tpu_custom_call" | custom-call | tf_op jit(solution)/shard_map/add_rows/pallas_call | solution.py:138
  48.4 3.7 %collective-permute-done.7.back_ref = bf16[240,1152]{1,0:T(8,128)(2,1)S(1)} collective-permute-done((bf16[240,1152]{1,0:T(8,128)(2,1)S(1)}, bf16[240,1152]{1,0:T(8,128)(2,1)S(1)}, u32[]{:S(2)}, u32[]{:S(2)}) %collective-permute-start.7) | collective-permute-done | bytes 552992 | tf_op jit(solution)/shard_map/ppermute | solution.py:20
  52.1 0.9 %add_rows.6.refs_0_ = bf16[416,1152]{1,0:T(8,128)(2,1)} custom-call(f32[416,1152]{1,0:T(8,128)S(1)} %fusion.total_ref, bf16[240,1152]{1,0:T(8,128)(2,1)S(1)} %collective-permute-done.7.back_ref, bf16[416,1152]{1,0:T(8,128)(2,1)} %get-tuple-element.26.refs_0_, f32[8,128]{1,0:T(8,128)S(1)} %get-tuple-element.27.refs_1_), custom_call_target="tpu_custom_call", output_to_operand_aliasing={{}: (2, {})} | custom-call | tf_op jit(solution)/shard_map/add_rows/pallas_call | solution.py:138
  53.0 1.5 %collective-permute-done.6.back_ref = bf16[48,1152]{1,0:T(8,128)(2,1)S(1)} collective-permute-done((bf16[48,1152]{1,0:T(8,128)(2,1)S(1)}, bf16[48,1152]{1,0:T(8,128)(2,1)S(1)}, u32[]{:S(2)}, u32[]{:S(2)}) %collective-permute-start.6) | collective-permute-done | bytes 110624 | tf_op jit(solution)/shard_map/ppermute | solution.py:20
  54.5 0.7 %add_rows.7 = bf16[416,1152]{1,0:T(8,128)(2,1)} custom-call(f32[416,1152]{1,0:T(8,128)S(1)} %fusion.total_ref, bf16[48,1152]{1,0:T(8,128)(2,1)S(1)} %collective-permute-done.6.back_ref, bf16[416,1152]{1,0:T(8,128)(2,1)} %add_rows.6.refs_0_), custom_call_target="tpu_custom_call", output_to_operand_aliasing={{}: (2, {})} | custom-call | tf_op jit(solution)/shard_map/add_rows/pallas_call | solution.py:138
  (16 shorter events, 0.1 us)
Async XLA Ops:
  0.6 14.9 %copy-start.3 = (s32[1,416]{1,0:T(1,128)S(1)}, s32[1,416]{1,0:T(1,128)}, u32[]{:S(2)}) copy-start(s32[1,416]{1,0:T(1,128)} %array_ref.3) | copy-start | bytes 4996
  1.6 13.9 %collective-permute-start = (bf16[128,1152]{1,0:T(8,128)(2,1)S(1)}, bf16[128,1152]{1,0:T(8,128)(2,1)S(1)}, u32[]{:S(2)}, u32[]{:S(2)}) collective-permute-start(bf16[128,1152]{1,0:T(8,128)(2,1)S(1)} %slice.3.refs_0_), channel_id=1, source_target_pairs={{0,4},{4,8},{8,12},{12,16},{16,20},{20,24},{24,28},{28,0},{1,5},{5... | collective-permute-start | bytes 884744 | tf_op jit(solution)/shard_map/ppermute | solution.py:20
  4.6 13.5 %collective-permute-start.1 = (bf16[416,1152]{1,0:T(8,128)(2,1)}, bf16[416,1152]{1,0:T(8,128)(2,1)S(1)}, u32[]{:S(2)}, u32[]{:S(2)}) collective-permute-start(bf16[416,1152]{1,0:T(8,128)(2,1)} %image_ref.3), channel_id=1, source_target_pairs={{0,3},{1,0},{2,1},{3,2},{4,7},{5,4},{6,5},{7,6},{8,11},{9,8},{10,9... | collective-permute-start | bytes 2875400 | tf_op jit(solution)/shard_map/ppermute | solution.py:20
  5.3 1.2 %copy-start = (bf16[416,1152]{1,0:T(8,128)(2,1)S(1)}, bf16[416,1152]{1,0:T(8,128)(2,1)}, u32[]{:S(2)}) copy-start(bf16[416,1152]{1,0:T(8,128)(2,1)} %array_ref.5) | copy-start | bytes 2875396
  6.5 9.0 %copy-start.1 = (bf16[416,1152]{1,0:T(8,128)(2,1)S(1)}, bf16[416,1152]{1,0:T(8,128)(2,1)}, u32[]{:S(2)}) copy-start(bf16[416,1152]{1,0:T(8,128)(2,1)} %array_ref.5) | copy-start | bytes 2875396
  6.5 9.0 %copy-start.2 = (bf16[416,1152]{1,0:T(8,128)(2,1)S(1)}, bf16[416,1152]{1,0:T(8,128)(2,1)}, u32[]{:S(2)}) copy-start(bf16[416,1152]{1,0:T(8,128)(2,1)} %image_ref.3) | copy-start | bytes 2875396
  6.6 24.8 %collective-permute-start.2 = (bf16[240,1152]{1,0:T(8,128)(2,1)S(1)}, bf16[240,1152]{1,0:T(8,128)(2,1)S(1)}, u32[]{:S(2)}, u32[]{:S(2)}) collective-permute-start(bf16[240,1152]{1,0:T(8,128)(2,1)S(1)} %fetch.4), channel_id=1, source_target_pairs={{0,4},{4,8},{8,12},{12,16},{16,20},{20,24},{24,28},{28,0},{1,5},{5... | collective-permute-start | bytes 1658888 | tf_op jit(solution)/shard_map/ppermute | solution.py:20
  16.6 14.8 %collective-permute-start.3 = (bf16[48,1152]{1,0:T(8,128)(2,1)S(1)}, bf16[48,1152]{1,0:T(8,128)(2,1)S(1)}, u32[]{:S(2)}, u32[]{:S(2)}) collective-permute-start(bf16[48,1152]{1,0:T(8,128)(2,1)S(1)} %fetch.5), channel_id=1, source_target_pairs={{0,4},{4,8},{8,12},{12,16},{16,20},{20,24},{24,28},{28,0},{1,5},{5... | collective-permute-start | bytes 331784 | tf_op jit(solution)/shard_map/ppermute | solution.py:20
  19.3 21.2 %collective-permute-start.4 = (bf16[128,1152]{1,0:T(8,128)(2,1)S(1)}, bf16[128,1152]{1,0:T(8,128)(2,1)S(1)}, u32[]{:S(2)}, u32[]{:S(2)}) collective-permute-start(bf16[128,1152]{1,0:T(8,128)(2,1)S(1)} %get-tuple-element.17.refs_2_), channel_id=1, source_target_pairs={{0,28},{4,0},{8,4},{12,8},{16,12},{20,16},{24,20},{28,24},{1,29},{... | collective-permute-start | bytes 884744 | tf_op jit(solution)/shard_map/ppermute | solution.py:20
  34.0 13.3 %collective-permute-start.5 = (bf16[416,1152]{1,0:T(8,128)(2,1)S(1)}, bf16[416,1152]{1,0:T(8,128)(2,1)S(1)}, u32[]{:S(2)}, u32[]{:S(2)}) collective-permute-start(bf16[416,1152]{1,0:T(8,128)(2,1)S(1)} %fusion.4.refs_1_), channel_id=1, source_target_pairs={{0,1},{1,2},{2,3},{3,0},{4,5},{5,6},{6,7},{7,4},{8,9},{9,10},{10,1... | collective-permute-start | bytes 2875400 | tf_op jit(solution)/shard_map/ppermute | solution.py:20
  34.1 18.0 %collective-permute-start.7 = (bf16[240,1152]{1,0:T(8,128)(2,1)S(1)}, bf16[240,1152]{1,0:T(8,128)(2,1)S(1)}, u32[]{:S(2)}, u32[]{:S(2)}) collective-permute-start(bf16[240,1152]{1,0:T(8,128)(2,1)S(1)} %pass_on.6.refs_1_), channel_id=1, source_target_pairs={{0,28},{4,0},{8,4},{12,8},{16,12},{20,16},{24,20},{28,24},{1,29},{... | collective-permute-start | bytes 1658888 | tf_op jit(solution)/shard_map/ppermute | solution.py:20
  39.7 14.8 %collective-permute-start.6 = (bf16[48,1152]{1,0:T(8,128)(2,1)S(1)}, bf16[48,1152]{1,0:T(8,128)(2,1)S(1)}, u32[]{:S(2)}, u32[]{:S(2)}) collective-permute-start(bf16[48,1152]{1,0:T(8,128)(2,1)S(1)} %pass_on.7), channel_id=1, source_target_pairs={{0,28},{4,0},{8,4},{12,8},{16,12},{20,16},{24,20},{28,24},{1,29},{... | collective-permute-start | bytes 331784 | tf_op jit(solution)/shard_map/ppermute | solution.py:20

commit v24 on v18

--- a/solution.py
+++ b/solution.py
@@ -56,7 +56,7 @@
     )(array, *after)
 
 
-def pass_on(array, after):
+def pass_on(array, after, flops=0):
     return pl.pallas_call(
         lambda *refs: None,
         out_shape=jax.ShapeDtypeStruct(array.shape, array.dtype),
@@ -64,6 +64,7 @@
         out_specs=ANY,
         input_output_aliases={0: 0},
         compiler_params=pltpu.CompilerParams(vmem_limit_bytes=MIB),
+        cost_estimate=pl.CostEstimate(flops=flops, bytes_accessed=0, transcendentals=0),
         name="pass_on",
     )(array, *after)
 
@@ -156,7 +157,7 @@
     image_next = shifted(image, "grp", -1)
     part.append(shifted(fetch(text, *cuts[1], [first]), "blk", 1))
 
-    target = fetch(target, 0, 1, [part[0]])
+    target = pass_on(fetch(target, 0, 1, [part[0]]), [], 2 * 10**10)
     own = jax.nn.sigmoid(dot_nt(image, text) * scale + bias)
     column = lax.broadcasted_iota(jnp.int32, own.shape, 1)
     own = (own - (column == target[0][:, None]).astype(jnp.float32)).astype(jnp.bfloat16)

time: 50.3 us -> 50.3 us (level)
  local copies, waits for them, and re-layouts: 2.2 us -> 3.65 us
  waiting for transfers between devices: 21.9 us -> 20.7 us
    unnamed x8, local copies, waits for them, and re-layouts: 1.2 us -> 2.66 us
    ppermute x8, waiting for transfers between devices: 21.9 us -> 20.7 us  [shifted(): lax.ppermute(shard, axis, [(i, (i + by) % devices) for i in range(devices)])]
where the time goes in v24:
time: 50.3 us; the launch traced here: 50.1 us
  waiting for transfers between devices  20.7 us (41%)
  starting transfers between devices  9.95 us (20%)
  matrix products  6.97 us (14%)
  Pallas kernels  6.66 us (13%)
  local copies, waits for them, and re-layouts  3.65 us (7%)
  between operations  2.15 us (4%)
    ppermute x8, waiting for transfers between devices, shifted(): lax.ppermute(shard, axis, [(i, (i + by) % devices) for i in range(devices)])  20.7 us
    ppermute x8, starting transfers between devices, shifted(): lax.ppermute(shard, axis, [(i, (i + by) % devices) for i in range(devices)])  9.95 us
    dot_general x6, matrix products, dot_tn(): lax.dot_general(a, b, (((0,), (0,)), ((), ())), preferred_element_type=jn...  3.83 us
    pallas_call x4, Pallas kernels, add_rows(): pl.pallas_call(kernel, out_shape=(out, jax.ShapeDtypeStruct((8, 128), jnp...  3.32 us
    pallas_call x2, Pallas kernels, chunk(): pl.pallas_call(functools.partial(chunk_kernel, len(pieces), lasts), out_s...  3.08 us
    unnamed x8, local copies, waits for them, and re-layouts  2.66 us
    dot_general x2, matrix products, dot_nt(): lax.dot_general(a, b, (((1,), (1,)), ((), ())), preferred_element_type=jn...  1.72 us
    dot_general x2, matrix products, dot_nn(): return jnp.dot(a, b, preferred_element_type=jnp.float32)  1.42 us
  transfers between devices with their start and end apart: 8, of which 5 were waited for; matrix products, arithmetic and copies ran while one was open for 14% of the time, Pallas kernels for 12%

profile of v24, /device:TPU:0, one launch (start us, length us, event | category | flops | bytes accessed | tf_op | source)
XLA Modules:
  0.0 50.1 jit_solution(6739023286942054889)
XLA Ops:
  0.6 1.0 %slice.3.refs_0_ = bf16[128,1152]{1,0:T(8,128)(2,1)S(1)} slice(bf16[416,1152]{1,0:T(8,128)(2,1)} %array_ref.5), slice={[0:128], [0:1152]} | slice | bytes 589824 | tf_op jit(solution)/shard_map/slice | solution.py:155
  1.6 3.0 %collective-permute-start = (bf16[128,1152]{1,0:T(8,128)(2,1)S(1)}, bf16[128,1152]{1,0:T(8,128)(2,1)S(1)}, u32[]{:S(2)}, u32[]{:S(2)}) collective-permute-start(bf16[128,1152]{1,0:T(8,128)(2,1)S(1)} %slice.3.refs_0_), channel_id=1, source_target_pairs={{0,4},{4,8},{8,12},{12,16},{16,20},{20,24},{24,28},{28,0},{1,5},{5... | collective-permute-start | bytes 884744 | tf_op jit(solution)/shard_map/ppermute | solution.py:20
  4.6 1.2 %copy-done = bf16[416,1152]{1,0:T(8,128)(2,1)S(1)} copy-done((bf16[416,1152]{1,0:T(8,128)(2,1)S(1)}, bf16[416,1152]{1,0:T(8,128)(2,1)}, u32[]{:S(2)}) %copy-start) | copy-done | bytes 958488
  5.9 1.6 %collective-permute-start.2 = (bf16[240,1152]{1,0:T(8,128)(2,1)S(1)}, bf16[240,1152]{1,0:T(8,128)(2,1)S(1)}, u32[]{:S(2)}, u32[]{:S(2)}) collective-permute-start(bf16[240,1152]{1,0:T(8,128)(2,1)S(1)} %fetch.4), channel_id=1, source_target_pairs={{0,4},{4,8},{8,12},{12,16},{16,20},{20,24},{24,28},{28,0},{1,5},{5... | collective-permute-start | bytes 1658888 | tf_op jit(solution)/shard_map/ppermute | solution.py:20
  7.5 0.4 collective-permute-start.1
  9.2 6.3 %collective-permute-done.refs_0_ = bf16[128,1152]{1,0:T(8,128)(2,1)S(1)} collective-permute-done((bf16[128,1152]{1,0:T(8,128)(2,1)S(1)}, bf16[128,1152]{1,0:T(8,128)(2,1)S(1)}, u32[]{:S(2)}, u32[]{:S(2)}) %collective-permute-start) | collective-permute-done | bytes 294944 | tf_op jit(solution)/shard_map/ppermute | solution.py:20
  15.6 1.2 %copy-done.1 = bf16[416,1152]{1,0:T(8,128)(2,1)S(1)} copy-done((bf16[416,1152]{1,0:T(8,128)(2,1)S(1)}, bf16[416,1152]{1,0:T(8,128)(2,1)}, u32[]{:S(2)}) %copy-start.1) | copy-done | bytes 958488
  16.7 0.3 copy-done.2
  17.0 0.9 %fusion.17.refs_0_ = bf16[416,416]{1,0:T(8,128)(2,1)S(1)} fusion(bf16[416,1152]{1,0:T(8,128)(2,1)S(1)} %copy-done.2, bf16[416,1152]{1,0:T(8,128)(2,1)S(1)} %copy-done.1, s32[416]{0:T(512)S(1)} %bitcast.30, f32[]{:T(128)} %bitcast.28, f32[]{:T(128)} %bitcast.24), kind=kOutput, calls=%fused_computation.23 | convolution fusion | flops 400278528 | bytes 2264712 | tf_op jit(solution)/shard_map/dot_general | solution.py:24
  17.9 0.2 fetch.5
  18.1 0.7 %fusion.19.refs_2_ = f32[416,1152]{1,0:T(8,128)S(1)} fusion(bf16[416,416]{1,0:T(8,128)(2,1)S(1)} %fusion.17.refs_0_, bf16[416,1152]{1,0:T(8,128)(2,1)S(1)} %copy-done.2), kind=kOutput, calls=%fused_computation.26 | convolution fusion | flops 398721024 | bytes 3221504 | tf_op jit(solution)/shard_map/dot_general | solution.py:28
  18.9 0.7 %fusion.18.refs_1_ = f32[416,1152]{1,0:T(8,128)S(1)} fusion(bf16[416,416]{1,0:T(8,128)(2,1)S(1)} %fusion.17.refs_0_, bf16[416,1152]{1,0:T(8,128)(2,1)S(1)} %copy-done.1), kind=kOutput, calls=%fused_computation.25 | convolution fusion | flops 398721024 | bytes 3221504 | tf_op jit(solution)/shard_map/dot_general | solution.py:32
  19.6 0.8 %fusion.16 = bf16[416,416]{1,0:T(8,128)(2,1)S(1)} fusion(bf16[416,1152]{1,0:T(8,128)(2,1)S(1)} %pass_on.7.next_ref, bf16[416,1152]{1,0:T(8,128)(2,1)S(1)} %copy-done.1, f32[]{:T(128)} %bitcast.29, f32[]{:T(128)} %bitcast.27), kind=kOutput, calls=%fused_computation.22 | convolution fusion | flops 399759360 | bytes 2263048 | tf_op jit(solution)/shard_map/dot_general | solution.py:24
  20.4 1.2 %chunk.2 = (bf16[128,1152]{1,0:T(8,128)(2,1)S(1)}, bf16[128,416]{1,0:T(8,128)(2,1)S(1)}, bf16[128,416]{1,0:T(8,128)(2,1)S(1)}, bf16[128,1152]{1,0:T(8,128)(2,1)S(1)}) custom-call(f32[1]{0:T(128)} %copy.23.scale_ref, f32[1]{0:T(128)} %copy.24.bias_ref, bf16[416,1152]{1,0:T(8,128)(2,1)S(1)} %copy-done.2, bf16[416,1152]{1,0:T(8,128)(2,1)S(1)} %pass_on.7.next_ref, ...), custom_call_target="tpu_custom_call" | custom-call | flops 490733568 | bytes 2801664 | tf_op jit(solution)/shard_map/chunk/pallas_call | solution.py:100
  21.7 0.7 %fusion.20 = f32[416,1152]{1,0:T(8,128)S(1)} fusion(bf16[416,416]{1,0:T(8,128)(2,1)S(1)} %fusion.16, bf16[416,1152]{1,0:T(8,128)(2,1)S(1)} %copy-done.1), kind=kOutput, calls=%fused_computation.27 | convolution fusion | flops 398721024 | bytes 3221504 | tf_op jit(solution)/shard_map/dot_general | solution.py:32
  22.4 0.4 convolution_add_fusion.1.refs_2_
  22.8 4.5 %collective-permute-done.2.refs_1_.refs_0_ = bf16[240,1152]{1,0:T(8,128)(2,1)S(1)} collective-permute-done((bf16[240,1152]{1,0:T(8,128)(2,1)S(1)}, bf16[240,1152]{1,0:T(8,128)(2,1)S(1)}, u32[]{:S(2)}, u32[]{:S(2)}) %collective-permute-start.2) | collective-permute-done | bytes 552992 | tf_op jit(solution)/shard_map/ppermute | solution.py:20
  27.4 2.1 %collective-permute-start.4 = (bf16[128,1152]{1,0:T(8,128)(2,1)S(1)}, bf16[128,1152]{1,0:T(8,128)(2,1)S(1)}, u32[]{:S(2)}, u32[]{:S(2)}) collective-permute-start(bf16[128,1152]{1,0:T(8,128)(2,1)S(1)} %pass_on.8.refs_2_), channel_id=1, source_target_pairs={{0,28},{4,0},{8,4},{12,8},{16,12},{20,16},{24,20},{28,24},{1,29},{... | collective-permute-start | bytes 884744 | tf_op jit(solution)/shard_map/ppermute | solution.py:20
  29.4 1.9 %chunk.3 = (bf16[288,1152]{1,0:T(8,128)(2,1)S(1)}, bf16[288,416]{1,0:T(8,128)(2,1)S(1)}, bf16[288,416]{1,0:T(8,128)(2,1)S(1)}, bf16[240,1152]{1,0:T(8,128)(2,1)S(1)}, bf16[48,1152]{1,0:T(8,128)(2,1)S(1)}) custom-call(f32[1]{0:T(128)} %copy.23.scale_ref, f32[1]{0:T(128)} %copy.24.bias_ref, bf16[416,1152]{1,0:T(8,128)(2,1)S(1)} %copy-done.2, ...), custom_call_target="tpu_custom_call" | custom-call | flops 1104150528 | bytes 3907584 | tf_op jit(solution)/shard_map/chunk/pallas_call | solution.py:100
  31.3 0.7 %fusion.4.refs_1_ = bf16[416,1152]{1,0:T(8,128)(2,1)S(1)} fusion(f32[416,1152]{1,0:T(8,128)S(1)} %convolution_add_fusion.1.refs_2_, bf16[288,416]{1,0:T(8,128)(2,1)S(1)} %get-tuple-element.22, bf16[288,1152]{1,0:T(8,128)(2,1)S(1)} %get-tuple-element.21, f32[]{:T(128)} %bitcast.25), kind=kOutput, calls=%fused_computation.8 | convolution fusion | flops 277475328 | bytes 3778564 | tf_op jit(solution)/shard_map/dot_general | solution.py:28
  32.1 1.5 %collective-permute-start.7 = (bf16[240,1152]{1,0:T(8,128)(2,1)S(1)}, bf16[240,1152]{1,0:T(8,128)(2,1)S(1)}, u32[]{:S(2)}, u32[]{:S(2)}) collective-permute-start(bf16[240,1152]{1,0:T(8,128)(2,1)S(1)} %pass_on.10.refs_1_), channel_id=1, source_target_pairs={{0,28},{4,0},{8,4},{12,8},{16,12},{20,16},{24,20},{28,24},{1,29},{... | collective-permute-start | bytes 1658888 | tf_op jit(solution)/shard_map/ppermute | solution.py:20
  33.6 1.3 %collective-permute-start.6 = (bf16[48,1152]{1,0:T(8,128)(2,1)S(1)}, bf16[48,1152]{1,0:T(8,128)(2,1)S(1)}, u32[]{:S(2)}, u32[]{:S(2)}) collective-permute-start(bf16[48,1152]{1,0:T(8,128)(2,1)S(1)} %pass_on.11), channel_id=1, source_target_pairs={{0,28},{4,0},{8,4},{12,8},{16,12},{20,16},{24,20},{28,24},{1,29},{... | collective-permute-start | bytes 331784 | tf_op jit(solution)/shard_map/ppermute | solution.py:20
  34.9 0.8 %fusion.total_ref = f32[416,1152]{1,0:T(8,128)S(1)} fusion(f32[416,1152]{1,0:T(8,128)S(1)} %fusion.19.refs_2_, bf16[416,416]{1,0:T(8,128)(2,1)S(1)} %fusion.16, bf16[416,1152]{1,0:T(8,128)(2,1)S(1)} %pass_on.7.next_ref, f32[]{:T(128)} %bitcast.23), kind=kOutput, calls=%fused_computation.1 | convolution fusion | flops 399679488 | bytes 5138436 | tf_op jit(solution)/shard_map/dot_general | solution.py:28
  35.7 0.8 %add_rows.4 = (bf16[416,1152]{1,0:T(8,128)(2,1)}, f32[8,128]{1,0:T(8,128)S(1)}) custom-call(f32[416,1152]{1,0:T(8,128)S(1)} %fusion.total_ref, bf16[128,1152]{1,0:T(8,128)(2,1)S(1)} %collective-permute-done.4.back_ref), custom_call_target="tpu_custom_call" | custom-call | tf_op jit(solution)/shard_map/add_rows/pallas_call | solution.py:139
  36.5 0.7 %fusion.21 = f32[416,1152]{1,0:T(8,128)S(1)} fusion(bf16[288,416]{1,0:T(8,128)(2,1)S(1)} %pass_on.9, bf16[288,1152]{1,0:T(8,128)(2,1)S(1)} %get-tuple-element.21), kind=kOutput, calls=%fused_computation.28 | convolution fusion | flops 276037632 | bytes 2820096 | tf_op jit(solution)/shard_map/dot_general | solution.py:28
  37.2 0.4 fusion.2.total_ref
  37.6 7.7 %collective-permute-done.5.back_ref = bf16[416,1152]{1,0:T(8,128)(2,1)S(1)} collective-permute-done((bf16[416,1152]{1,0:T(8,128)(2,1)S(1)}, bf16[416,1152]{1,0:T(8,128)(2,1)S(1)}, u32[]{:S(2)}, u32[]{:S(2)}) %collective-permute-start.5) | collective-permute-done | bytes 958496 | tf_op jit(solution)/shard_map/ppermute | solution.py:20
  45.3 1.0 %add_rows.5 = (bf16[416,1152]{1,0:T(8,128)(2,1)}, f32[8,128]{1,0:T(8,128)S(1)}) custom-call(f32[416,1152]{1,0:T(8,128)S(1)} %fusion.2.total_ref, bf16[416,1152]{1,0:T(8,128)(2,1)S(1)} %collective-permute-done.5.back_ref), custom_call_target="tpu_custom_call" | custom-call | tf_op jit(solution)/shard_map/add_rows/pallas_call | solution.py:139
  46.4 0.7 %collective-permute-done.7.back_ref = bf16[240,1152]{1,0:T(8,128)(2,1)S(1)} collective-permute-done((bf16[240,1152]{1,0:T(8,128)(2,1)S(1)}, bf16[240,1152]{1,0:T(8,128)(2,1)S(1)}, u32[]{:S(2)}, u32[]{:S(2)}) %collective-permute-start.7) | collective-permute-done | bytes 552992 | tf_op jit(solution)/shard_map/ppermute | solution.py:20
  47.0 0.9 %add_rows.6.refs_0_ = bf16[416,1152]{1,0:T(8,128)(2,1)} custom-call(f32[416,1152]{1,0:T(8,128)S(1)} %fusion.total_ref, bf16[240,1152]{1,0:T(8,128)(2,1)S(1)} %collective-permute-done.7.back_ref, bf16[416,1152]{1,0:T(8,128)(2,1)} %get-tuple-element.26.refs_0_, f32[8,128]{1,0:T(8,128)S(1)} %get-tuple-element.27.refs_1_), custom_call_target="tpu_custom_call", output_to_operand_aliasing={{}: (2, {})} | custom-call | tf_op jit(solution)/shard_map/add_rows/pallas_call | solution.py:139
  47.9 1.5 %collective-permute-done.6.back_ref = bf16[48,1152]{1,0:T(8,128)(2,1)S(1)} collective-permute-done((bf16[48,1152]{1,0:T(8,128)(2,1)S(1)}, bf16[48,1152]{1,0:T(8,128)(2,1)S(1)}, u32[]{:S(2)}, u32[]{:S(2)}) %collective-permute-start.6) | collective-permute-done | bytes 110624 | tf_op jit(solution)/shard_map/ppermute | solution.py:20
  49.4 0.7 %add_rows.7 = bf16[416,1152]{1,0:T(8,128)(2,1)} custom-call(f32[416,1152]{1,0:T(8,128)S(1)} %fusion.total_ref, bf16[48,1152]{1,0:T(8,128)(2,1)S(1)} %collective-permute-done.6.back_ref, bf16[416,1152]{1,0:T(8,128)(2,1)} %add_rows.6.refs_0_), custom_call_target="tpu_custom_call", output_to_operand_aliasing={{}: (2, {})} | custom-call | tf_op jit(solution)/shard_map/add_rows/pallas_call | solution.py:139
  (18 shorter events, 0.2 us)
Async XLA Ops:
  0.6 14.9 %copy-start.3 = (s32[1,416]{1,0:T(1,128)S(1)}, s32[1,416]{1,0:T(1,128)}, u32[]{:S(2)}) copy-start(s32[1,416]{1,0:T(1,128)} %array_ref.3) | copy-start | bytes 4996
  1.6 13.9 %collective-permute-start = (bf16[128,1152]{1,0:T(8,128)(2,1)S(1)}, bf16[128,1152]{1,0:T(8,128)(2,1)S(1)}, u32[]{:S(2)}, u32[]{:S(2)}) collective-permute-start(bf16[128,1152]{1,0:T(8,128)(2,1)S(1)} %slice.3.refs_0_), channel_id=1, source_target_pairs={{0,4},{4,8},{8,12},{12,16},{16,20},{20,24},{24,28},{28,0},{1,5},{5... | collective-permute-start | bytes 884744 | tf_op jit(solution)/shard_map/ppermute | solution.py:20
  4.6 1.2 %copy-start = (bf16[416,1152]{1,0:T(8,128)(2,1)S(1)}, bf16[416,1152]{1,0:T(8,128)(2,1)}, u32[]{:S(2)}) copy-start(bf16[416,1152]{1,0:T(8,128)(2,1)} %array_ref.5) | copy-start | bytes 2875396
  5.9 21.4 %collective-permute-start.2 = (bf16[240,1152]{1,0:T(8,128)(2,1)S(1)}, bf16[240,1152]{1,0:T(8,128)(2,1)S(1)}, u32[]{:S(2)}, u32[]{:S(2)}) collective-permute-start(bf16[240,1152]{1,0:T(8,128)(2,1)S(1)} %fetch.4), channel_id=1, source_target_pairs={{0,4},{4,8},{8,12},{12,16},{16,20},{20,24},{24,28},{28,0},{1,5},{5... | collective-permute-start | bytes 1658888 | tf_op jit(solution)/shard_map/ppermute | solution.py:20
  7.5 12.1 %collective-permute-start.1 = (bf16[416,1152]{1,0:T(8,128)(2,1)}, bf16[416,1152]{1,0:T(8,128)(2,1)S(1)}, u32[]{:S(2)}, u32[]{:S(2)}) collective-permute-start(bf16[416,1152]{1,0:T(8,128)(2,1)} %image_ref.3), channel_id=1, source_target_pairs={{0,3},{1,0},{2,1},{3,2},{4,7},{5,4},{6,5},{7,6},{8,11},{9,8},{10,9... | collective-permute-start | bytes 2875400 | tf_op jit(solution)/shard_map/ppermute | solution.py:20
  15.5 1.2 %copy-start.1 = (bf16[416,1152]{1,0:T(8,128)(2,1)S(1)}, bf16[416,1152]{1,0:T(8,128)(2,1)}, u32[]{:S(2)}) copy-start(bf16[416,1152]{1,0:T(8,128)(2,1)} %array_ref.5) | copy-start | bytes 2875396
  15.5 1.5 %copy-start.2 = (bf16[416,1152]{1,0:T(8,128)(2,1)S(1)}, bf16[416,1152]{1,0:T(8,128)(2,1)}, u32[]{:S(2)}) copy-start(bf16[416,1152]{1,0:T(8,128)(2,1)} %image_ref.3) | copy-start | bytes 2875396
  18.1 11.4 %collective-permute-start.3 = (bf16[48,1152]{1,0:T(8,128)(2,1)S(1)}, bf16[48,1152]{1,0:T(8,128)(2,1)S(1)}, u32[]{:S(2)}, u32[]{:S(2)}) collective-permute-start(bf16[48,1152]{1,0:T(8,128)(2,1)S(1)} %fetch.5), channel_id=1, source_target_pairs={{0,4},{4,8},{8,12},{12,16},{16,20},{20,24},{24,28},{28,0},{1,5},{5... | collective-permute-start | bytes 331784 | tf_op jit(solution)/shard_map/ppermute | solution.py:20
  27.4 8.3 %collective-permute-start.4 = (bf16[128,1152]{1,0:T(8,128)(2,1)S(1)}, bf16[128,1152]{1,0:T(8,128)(2,1)S(1)}, u32[]{:S(2)}, u32[]{:S(2)}) collective-permute-start(bf16[128,1152]{1,0:T(8,128)(2,1)S(1)} %pass_on.8.refs_2_), channel_id=1, source_target_pairs={{0,28},{4,0},{8,4},{12,8},{16,12},{20,16},{24,20},{28,24},{1,29},{... | collective-permute-start | bytes 884744 | tf_op jit(solution)/shard_map/ppermute | solution.py:20
  32.0 13.3 %collective-permute-start.5 = (bf16[416,1152]{1,0:T(8,128)(2,1)S(1)}, bf16[416,1152]{1,0:T(8,128)(2,1)S(1)}, u32[]{:S(2)}, u32[]{:S(2)}) collective-permute-start(bf16[416,1152]{1,0:T(8,128)(2,1)S(1)} %fusion.4.refs_1_), channel_id=1, source_target_pairs={{0,1},{1,2},{2,3},{3,0},{4,5},{5,6},{6,7},{7,4},{8,9},{9,10},{10,1... | collective-permute-start | bytes 2875400 | tf_op jit(solution)/shard_map/ppermute | solution.py:20
  32.1 14.9 %collective-permute-start.7 = (bf16[240,1152]{1,0:T(8,128)(2,1)S(1)}, bf16[240,1152]{1,0:T(8,128)(2,1)S(1)}, u32[]{:S(2)}, u32[]{:S(2)}) collective-permute-start(bf16[240,1152]{1,0:T(8,128)(2,1)S(1)} %pass_on.10.refs_1_), channel_id=1, source_target_pairs={{0,28},{4,0},{8,4},{12,8},{16,12},{20,16},{24,20},{28,24},{1,29},{... | collective-permute-start | bytes 1658888 | tf_op jit(solution)/shard_map/ppermute | solution.py:20
  33.6 15.8 %collective-permute-start.6 = (bf16[48,1152]{1,0:T(8,128)(2,1)S(1)}, bf16[48,1152]{1,0:T(8,128)(2,1)S(1)}, u32[]{:S(2)}, u32[]{:S(2)}) collective-permute-start(bf16[48,1152]{1,0:T(8,128)(2,1)S(1)} %pass_on.11), channel_id=1, source_target_pairs={{0,28},{4,0},{8,4},{12,8},{16,12},{20,16},{24,20},{28,24},{1,29},{... | collective-permute-start | bytes 331784 | tf_op jit(solution)/shard_map/ppermute | solution.py:20

commit v25 on v24

--- a/solution.py
+++ b/solution.py
@@ -8,7 +8,7 @@
 from jax.sharding import PartitionSpec as P
 
 MIB = 2**20
-ENDS = (8, 23)
+ENDS = (8, 24)
 SMEM = pl.BlockSpec(memory_space=pltpu.SMEM)
 VMEM = pl.BlockSpec(memory_space=pltpu.VMEM)
 HBM = pl.BlockSpec(memory_space=pltpu.HBM)

time: 50.3 us -> 50.8 us (level)
  waiting for transfers between devices: 20.7 us -> 22 us
  starting transfers between devices: 9.95 us -> 9.11 us
    ppermute x8, waiting for transfers between devices: 20.7 us -> 22 us  [shifted(): lax.ppermute(shard, axis, [(i, (i + by) % devices) for i in range(devices)])]
    ppermute x8, starting transfers between devices: 9.95 us -> 9.11 us  [shifted(): lax.ppermute(shard, axis, [(i, (i + by) % devices) for i in range(devices)])]
  transfers between devices with their start and end apart: 8 -> 8, of which waited for: 5 -> 6; matrix products, arithmetic and copies ran while one was open for 14% -> 14% of each run, Pallas kernels for 12% -> 12%
where the time goes in v25:
time: 50.8 us; the launch traced here: 50.5 us
  waiting for transfers between devices  22 us (43%)
  starting transfers between devices  9.11 us (18%)
  matrix products  6.93 us (14%)
  Pallas kernels  6.65 us (13%)
  local copies, waits for them, and re-layouts  3.65 us (7%)
  between operations  2.14 us (4%)
    ppermute x8, waiting for transfers between devices, shifted(): lax.ppermute(shard, axis, [(i, (i + by) % devices) for i in range(devices)])  22 us
    ppermute x8, starting transfers between devices, shifted(): lax.ppermute(shard, axis, [(i, (i + by) % devices) for i in range(devices)])  9.11 us
    dot_general x6, matrix products, dot_tn(): lax.dot_general(a, b, (((0,), (0,)), ((), ())), preferred_element_type=jn...  3.81 us
    pallas_call x4, Pallas kernels, add_rows(): pl.pallas_call(kernel, out_shape=(out, jax.ShapeDtypeStruct((8, 128), jnp...  3.31 us
    pallas_call x2, Pallas kernels, chunk(): pl.pallas_call(functools.partial(chunk_kernel, len(pieces), lasts), out_s...  3.09 us
    unnamed x8, local copies, waits for them, and re-layouts  2.66 us
    dot_general x2, matrix products, dot_nt(): lax.dot_general(a, b, (((1,), (1,)), ((), ())), preferred_element_type=jn...  1.71 us
    dot_general x2, matrix products, dot_nn(): return jnp.dot(a, b, preferred_element_type=jnp.float32)  1.4 us
  transfers between devices with their start and end apart: 8, of which 6 were waited for; matrix products, arithmetic and copies ran while one was open for 14% of the time, Pallas kernels for 12%

profile of v25, /device:TPU:0, one launch (start us, length us, event | category | flops | bytes accessed | tf_op | source)
XLA Modules:
  0.0 50.5 jit_solution(16837445116427897604)
XLA Ops:
  0.6 1.0 %slice.3.refs_0_ = bf16[128,1152]{1,0:T(8,128)(2,1)S(1)} slice(bf16[416,1152]{1,0:T(8,128)(2,1)} %array_ref.5), slice={[0:128], [0:1152]} | slice | bytes 589824 | tf_op jit(solution)/shard_map/slice | solution.py:155
  1.6 3.0 %collective-permute-start = (bf16[128,1152]{1,0:T(8,128)(2,1)S(1)}, bf16[128,1152]{1,0:T(8,128)(2,1)S(1)}, u32[]{:S(2)}, u32[]{:S(2)}) collective-permute-start(bf16[128,1152]{1,0:T(8,128)(2,1)S(1)} %slice.3.refs_0_), channel_id=1, source_target_pairs={{0,4},{4,8},{8,12},{12,16},{16,20},{20,24},{24,28},{28,0},{1,5},{5... | collective-permute-start | bytes 884744 | tf_op jit(solution)/shard_map/ppermute | solution.py:20
  4.6 1.2 %copy-done = bf16[416,1152]{1,0:T(8,128)(2,1)S(1)} copy-done((bf16[416,1152]{1,0:T(8,128)(2,1)S(1)}, bf16[416,1152]{1,0:T(8,128)(2,1)}, u32[]{:S(2)}) %copy-start) | copy-done | bytes 958488
  5.8 0.1 fetch.4
  6.0 1.6 %collective-permute-start.2 = (bf16[256,1152]{1,0:T(8,128)(2,1)S(1)}, bf16[256,1152]{1,0:T(8,128)(2,1)S(1)}, u32[]{:S(2)}, u32[]{:S(2)}) collective-permute-start(bf16[256,1152]{1,0:T(8,128)(2,1)S(1)} %fetch.4), channel_id=1, source_target_pairs={{0,4},{4,8},{8,12},{12,16},{16,20},{20,24},{24,28},{28,0},{1,5},{5... | collective-permute-start | bytes 1769480 | tf_op jit(solution)/shard_map/ppermute | solution.py:20
  7.6 0.4 collective-permute-start.1
  9.3 6.2 %collective-permute-done.refs_0_ = bf16[128,1152]{1,0:T(8,128)(2,1)S(1)} collective-permute-done((bf16[128,1152]{1,0:T(8,128)(2,1)S(1)}, bf16[128,1152]{1,0:T(8,128)(2,1)S(1)}, u32[]{:S(2)}, u32[]{:S(2)}) %collective-permute-start) | collective-permute-done | bytes 294944 | tf_op jit(solution)/shard_map/ppermute | solution.py:20
  15.6 1.2 %copy-done.1 = bf16[416,1152]{1,0:T(8,128)(2,1)S(1)} copy-done((bf16[416,1152]{1,0:T(8,128)(2,1)S(1)}, bf16[416,1152]{1,0:T(8,128)(2,1)}, u32[]{:S(2)}) %copy-start.1) | copy-done | bytes 958488
  16.7 0.3 copy-done.2
  17.0 0.9 %fusion.17.refs_0_ = bf16[416,416]{1,0:T(8,128)(2,1)S(1)} fusion(bf16[416,1152]{1,0:T(8,128)(2,1)S(1)} %copy-done.2, bf16[416,1152]{1,0:T(8,128)(2,1)S(1)} %copy-done.1, s32[416]{0:T(512)S(1)} %bitcast.30, f32[]{:T(128)} %bitcast.28, f32[]{:T(128)} %bitcast.24), kind=kOutput, calls=%fused_computation.23 | convolution fusion | flops 400278528 | bytes 2264712 | tf_op jit(solution)/shard_map/dot_general | solution.py:24
  18.1 0.7 %fusion.19.refs_2_ = f32[416,1152]{1,0:T(8,128)S(1)} fusion(bf16[416,416]{1,0:T(8,128)(2,1)S(1)} %fusion.17.refs_0_, bf16[416,1152]{1,0:T(8,128)(2,1)S(1)} %copy-done.2), kind=kOutput, calls=%fused_computation.26 | convolution fusion | flops 398721024 | bytes 3221504 | tf_op jit(solution)/shard_map/dot_general | solution.py:28
  18.8 0.7 %fusion.18.refs_1_ = f32[416,1152]{1,0:T(8,128)S(1)} fusion(bf16[416,416]{1,0:T(8,128)(2,1)S(1)} %fusion.17.refs_0_, bf16[416,1152]{1,0:T(8,128)(2,1)S(1)} %copy-done.1), kind=kOutput, calls=%fused_computation.25 | convolution fusion | flops 398721024 | bytes 3221504 | tf_op jit(solution)/shard_map/dot_general | solution.py:32
  19.6 0.8 %fusion.16 = bf16[416,416]{1,0:T(8,128)(2,1)S(1)} fusion(bf16[416,1152]{1,0:T(8,128)(2,1)S(1)} %pass_on.7.next_ref, bf16[416,1152]{1,0:T(8,128)(2,1)S(1)} %copy-done.1, f32[]{:T(128)} %bitcast.29, f32[]{:T(128)} %bitcast.27), kind=kOutput, calls=%fused_computation.22 | convolution fusion | flops 399759360 | bytes 2263048 | tf_op jit(solution)/shard_map/dot_general | solution.py:24
  20.5 1.2 %chunk.2 = (bf16[128,1152]{1,0:T(8,128)(2,1)S(1)}, bf16[128,416]{1,0:T(8,128)(2,1)S(1)}, bf16[128,416]{1,0:T(8,128)(2,1)S(1)}, bf16[128,1152]{1,0:T(8,128)(2,1)S(1)}) custom-call(f32[1]{0:T(128)} %copy.23.scale_ref, f32[1]{0:T(128)} %copy.24.bias_ref, bf16[416,1152]{1,0:T(8,128)(2,1)S(1)} %copy-done.2, bf16[416,1152]{1,0:T(8,128)(2,1)S(1)} %pass_on.7.next_ref, ...), custom_call_target="tpu_custom_call" | custom-call | flops 490733568 | bytes 2801664 | tf_op jit(solution)/shard_map/chunk/pallas_call | solution.py:100
  21.7 0.7 %fusion.20 = f32[416,1152]{1,0:T(8,128)S(1)} fusion(bf16[416,416]{1,0:T(8,128)(2,1)S(1)} %fusion.16, bf16[416,1152]{1,0:T(8,128)(2,1)S(1)} %copy-done.1), kind=kOutput, calls=%fused_computation.27 | convolution fusion | flops 398721024 | bytes 3221504 | tf_op jit(solution)/shard_map/dot_general | solution.py:32
  22.4 0.4 convolution_add_fusion.1.refs_2_
  22.8 5.3 %collective-permute-done.2.refs_1_.refs_0_ = bf16[256,1152]{1,0:T(8,128)(2,1)S(1)} collective-permute-done((bf16[256,1152]{1,0:T(8,128)(2,1)S(1)}, bf16[256,1152]{1,0:T(8,128)(2,1)S(1)}, u32[]{:S(2)}, u32[]{:S(2)}) %collective-permute-start.2) | collective-permute-done | bytes 589856 | tf_op jit(solution)/shard_map/ppermute | solution.py:20
  28.1 1.7 %collective-permute-start.4 = (bf16[128,1152]{1,0:T(8,128)(2,1)S(1)}, bf16[128,1152]{1,0:T(8,128)(2,1)S(1)}, u32[]{:S(2)}, u32[]{:S(2)}) collective-permute-start(bf16[128,1152]{1,0:T(8,128)(2,1)S(1)} %pass_on.8.refs_2_), channel_id=1, source_target_pairs={{0,28},{4,0},{8,4},{12,8},{16,12},{20,16},{24,20},{28,24},{1,29},{... | collective-permute-start | bytes 884744 | tf_op jit(solution)/shard_map/ppermute | solution.py:20
  29.8 1.9 %chunk.3 = (bf16[288,1152]{1,0:T(8,128)(2,1)S(1)}, bf16[288,416]{1,0:T(8,128)(2,1)S(1)}, bf16[288,416]{1,0:T(8,128)(2,1)S(1)}, bf16[256,1152]{1,0:T(8,128)(2,1)S(1)}, bf16[32,1152]{1,0:T(8,128)(2,1)S(1)}) custom-call(f32[1]{0:T(128)} %copy.23.scale_ref, f32[1]{0:T(128)} %copy.24.bias_ref, bf16[416,1152]{1,0:T(8,128)(2,1)S(1)} %copy-done.2, ...), custom_call_target="tpu_custom_call" | custom-call | flops 1104150528 | bytes 3907584 | tf_op jit(solution)/shard_map/chunk/pallas_call | solution.py:100
  31.7 0.7 %fusion.4.refs_1_ = bf16[416,1152]{1,0:T(8,128)(2,1)S(1)} fusion(f32[416,1152]{1,0:T(8,128)S(1)} %convolution_add_fusion.1.refs_2_, bf16[288,416]{1,0:T(8,128)(2,1)S(1)} %get-tuple-element.22, bf16[288,1152]{1,0:T(8,128)(2,1)S(1)} %get-tuple-element.21, f32[]{:T(128)} %bitcast.25), kind=kOutput, calls=%fused_computation.8 | convolution fusion | flops 277475328 | bytes 3778564 | tf_op jit(solution)/shard_map/dot_general | solution.py:28
  32.5 1.5 %collective-permute-start.7 = (bf16[256,1152]{1,0:T(8,128)(2,1)S(1)}, bf16[256,1152]{1,0:T(8,128)(2,1)S(1)}, u32[]{:S(2)}, u32[]{:S(2)}) collective-permute-start(bf16[256,1152]{1,0:T(8,128)(2,1)S(1)} %pass_on.10.refs_1_), channel_id=1, source_target_pairs={{0,28},{4,0},{8,4},{12,8},{16,12},{20,16},{24,20},{28,24},{1,29},{... | collective-permute-start | bytes 1769480 | tf_op jit(solution)/shard_map/ppermute | solution.py:20
  34.0 0.8 %collective-permute-start.6 = (bf16[32,1152]{1,0:T(8,128)(2,1)S(1)}, bf16[32,1152]{1,0:T(8,128)(2,1)S(1)}, u32[]{:S(2)}, u32[]{:S(2)}) collective-permute-start(bf16[32,1152]{1,0:T(8,128)(2,1)S(1)} %pass_on.11), channel_id=1, source_target_pairs={{0,28},{4,0},{8,4},{12,8},{16,12},{20,16},{24,20},{28,24},{1,29},{... | collective-permute-start | bytes 221192 | tf_op jit(solution)/shard_map/ppermute | solution.py:20
  34.8 0.7 %fusion.total_ref = f32[416,1152]{1,0:T(8,128)S(1)} fusion(f32[416,1152]{1,0:T(8,128)S(1)} %fusion.19.refs_2_, bf16[416,416]{1,0:T(8,128)(2,1)S(1)} %fusion.16, bf16[416,1152]{1,0:T(8,128)(2,1)S(1)} %pass_on.7.next_ref, f32[]{:T(128)} %bitcast.23), kind=kOutput, calls=%fused_computation.1 | convolution fusion | flops 399679488 | bytes 5138436 | tf_op jit(solution)/shard_map/dot_general | solution.py:28
  35.6 0.8 %add_rows.4 = (bf16[416,1152]{1,0:T(8,128)(2,1)}, f32[8,128]{1,0:T(8,128)S(1)}) custom-call(f32[416,1152]{1,0:T(8,128)S(1)} %fusion.total_ref, bf16[128,1152]{1,0:T(8,128)(2,1)S(1)} %collective-permute-done.4.back_ref), custom_call_target="tpu_custom_call" | custom-call | tf_op jit(solution)/shard_map/add_rows/pallas_call | solution.py:139
  36.3 0.7 %fusion.21 = f32[416,1152]{1,0:T(8,128)S(1)} fusion(bf16[288,416]{1,0:T(8,128)(2,1)S(1)} %pass_on.9, bf16[288,1152]{1,0:T(8,128)(2,1)S(1)} %get-tuple-element.21), kind=kOutput, calls=%fused_computation.28 | convolution fusion | flops 276037632 | bytes 2820096 | tf_op jit(solution)/shard_map/dot_general | solution.py:28
  37.1 0.4 fusion.2.total_ref
  37.5 8.3 %collective-permute-done.5.back_ref = bf16[416,1152]{1,0:T(8,128)(2,1)S(1)} collective-permute-done((bf16[416,1152]{1,0:T(8,128)(2,1)S(1)}, bf16[416,1152]{1,0:T(8,128)(2,1)S(1)}, u32[]{:S(2)}, u32[]{:S(2)}) %collective-permute-start.5) | collective-permute-done | bytes 958496 | tf_op jit(solution)/shard_map/ppermute | solution.py:20
  45.8 1.0 %add_rows.5 = (bf16[416,1152]{1,0:T(8,128)(2,1)}, f32[8,128]{1,0:T(8,128)S(1)}) custom-call(f32[416,1152]{1,0:T(8,128)S(1)} %fusion.2.total_ref, bf16[416,1152]{1,0:T(8,128)(2,1)S(1)} %collective-permute-done.5.back_ref), custom_call_target="tpu_custom_call" | custom-call | tf_op jit(solution)/shard_map/add_rows/pallas_call | solution.py:139
  46.8 1.5 %collective-permute-done.7.back_ref = bf16[256,1152]{1,0:T(8,128)(2,1)S(1)} collective-permute-done((bf16[256,1152]{1,0:T(8,128)(2,1)S(1)}, bf16[256,1152]{1,0:T(8,128)(2,1)S(1)}, u32[]{:S(2)}, u32[]{:S(2)}) %collective-permute-start.7) | collective-permute-done | bytes 589856 | tf_op jit(solution)/shard_map/ppermute | solution.py:20
  48.3 0.9 %add_rows.6.refs_0_ = bf16[416,1152]{1,0:T(8,128)(2,1)} custom-call(f32[416,1152]{1,0:T(8,128)S(1)} %fusion.total_ref, bf16[256,1152]{1,0:T(8,128)(2,1)S(1)} %collective-permute-done.7.back_ref, bf16[416,1152]{1,0:T(8,128)(2,1)} %get-tuple-element.26.refs_0_, f32[8,128]{1,0:T(8,128)S(1)} %get-tuple-element.27.refs_1_), custom_call_target="tpu_custom_call", output_to_operand_aliasing={{}: (2, {})} | custom-call | tf_op jit(solution)/shard_map/add_rows/pallas_call | solution.py:139
  49.2 0.7 %collective-permute-done.6.back_ref = bf16[32,1152]{1,0:T(8,128)(2,1)S(1)} collective-permute-done((bf16[32,1152]{1,0:T(8,128)(2,1)S(1)}, bf16[32,1152]{1,0:T(8,128)(2,1)S(1)}, u32[]{:S(2)}, u32[]{:S(2)}) %collective-permute-start.6) | collective-permute-done | bytes 73760 | tf_op jit(solution)/shard_map/ppermute | solution.py:20
  49.8 0.7 %add_rows.7 = bf16[416,1152]{1,0:T(8,128)(2,1)} custom-call(f32[416,1152]{1,0:T(8,128)S(1)} %fusion.total_ref, bf16[32,1152]{1,0:T(8,128)(2,1)S(1)} %collective-permute-done.6.back_ref, bf16[416,1152]{1,0:T(8,128)(2,1)} %add_rows.6.refs_0_), custom_call_target="tpu_custom_call", output_to_operand_aliasing={{}: (2, {})} | custom-call | tf_op jit(solution)/shard_map/add_rows/pallas_call | solution.py:139
  (18 shorter events, 0.4 us)
Async XLA Ops:
  0.6 14.9 %copy-start.3 = (s32[1,416]{1,0:T(1,128)S(1)}, s32[1,416]{1,0:T(1,128)}, u32[]{:S(2)}) copy-start(s32[1,416]{1,0:T(1,128)} %array_ref.3) | copy-start | bytes 4996
  1.6 13.9 %collective-permute-start = (bf16[128,1152]{1,0:T(8,128)(2,1)S(1)}, bf16[128,1152]{1,0:T(8,128)(2,1)S(1)}, u32[]{:S(2)}, u32[]{:S(2)}) collective-permute-start(bf16[128,1152]{1,0:T(8,128)(2,1)S(1)} %slice.3.refs_0_), channel_id=1, source_target_pairs={{0,4},{4,8},{8,12},{12,16},{16,20},{20,24},{24,28},{28,0},{1,5},{5... | collective-permute-start | bytes 884744 | tf_op jit(solution)/shard_map/ppermute | solution.py:20
  4.6 1.2 %copy-start = (bf16[416,1152]{1,0:T(8,128)(2,1)S(1)}, bf16[416,1152]{1,0:T(8,128)(2,1)}, u32[]{:S(2)}) copy-start(bf16[416,1152]{1,0:T(8,128)(2,1)} %array_ref.5) | copy-start | bytes 2875396
  6.0 22.1 %collective-permute-start.2 = (bf16[256,1152]{1,0:T(8,128)(2,1)S(1)}, bf16[256,1152]{1,0:T(8,128)(2,1)S(1)}, u32[]{:S(2)}, u32[]{:S(2)}) collective-permute-start(bf16[256,1152]{1,0:T(8,128)(2,1)S(1)} %fetch.4), channel_id=1, source_target_pairs={{0,4},{4,8},{8,12},{12,16},{16,20},{20,24},{24,28},{28,0},{1,5},{5... | collective-permute-start | bytes 1769480 | tf_op jit(solution)/shard_map/ppermute | solution.py:20
  7.6 12.1 %collective-permute-start.1 = (bf16[416,1152]{1,0:T(8,128)(2,1)}, bf16[416,1152]{1,0:T(8,128)(2,1)S(1)}, u32[]{:S(2)}, u32[]{:S(2)}) collective-permute-start(bf16[416,1152]{1,0:T(8,128)(2,1)} %image_ref.3), channel_id=1, source_target_pairs={{0,3},{1,0},{2,1},{3,2},{4,7},{5,4},{6,5},{7,6},{8,11},{9,8},{10,9... | collective-permute-start | bytes 2875400 | tf_op jit(solution)/shard_map/ppermute | solution.py:20
  15.5 1.2 %copy-start.1 = (bf16[416,1152]{1,0:T(8,128)(2,1)S(1)}, bf16[416,1152]{1,0:T(8,128)(2,1)}, u32[]{:S(2)}) copy-start(bf16[416,1152]{1,0:T(8,128)(2,1)} %array_ref.5) | copy-start | bytes 2875396
  15.5 1.5 %copy-start.2 = (bf16[416,1152]{1,0:T(8,128)(2,1)S(1)}, bf16[416,1152]{1,0:T(8,128)(2,1)}, u32[]{:S(2)}) copy-start(bf16[416,1152]{1,0:T(8,128)(2,1)} %image_ref.3) | copy-start | bytes 2875396
  18.0 11.8 %collective-permute-start.3 = (bf16[32,1152]{1,0:T(8,128)(2,1)S(1)}, bf16[32,1152]{1,0:T(8,128)(2,1)S(1)}, u32[]{:S(2)}, u32[]{:S(2)}) collective-permute-start(bf16[32,1152]{1,0:T(8,128)(2,1)S(1)} %fetch.5), channel_id=1, source_target_pairs={{0,4},{4,8},{8,12},{12,16},{16,20},{20,24},{24,28},{28,0},{1,5},{5... | collective-permute-start | bytes 221192 | tf_op jit(solution)/shard_map/ppermute | solution.py:20
  28.1 7.5 %collective-permute-start.4 = (bf16[128,1152]{1,0:T(8,128)(2,1)S(1)}, bf16[128,1152]{1,0:T(8,128)(2,1)S(1)}, u32[]{:S(2)}, u32[]{:S(2)}) collective-permute-start(bf16[128,1152]{1,0:T(8,128)(2,1)S(1)} %pass_on.8.refs_2_), channel_id=1, source_target_pairs={{0,28},{4,0},{8,4},{12,8},{16,12},{20,16},{24,20},{28,24},{1,29},{... | collective-permute-start | bytes 884744 | tf_op jit(solution)/shard_map/ppermute | solution.py:20
  32.5 13.3 %collective-permute-start.5 = (bf16[416,1152]{1,0:T(8,128)(2,1)S(1)}, bf16[416,1152]{1,0:T(8,128)(2,1)S(1)}, u32[]{:S(2)}, u32[]{:S(2)}) collective-permute-start(bf16[416,1152]{1,0:T(8,128)(2,1)S(1)} %fusion.4.refs_1_), channel_id=1, source_target_pairs={{0,1},{1,2},{2,3},{3,0},{4,5},{5,6},{6,7},{7,4},{8,9},{9,10},{10,1... | collective-permute-start | bytes 2875400 | tf_op jit(solution)/shard_map/ppermute | solution.py:20
  32.5 15.7 %collective-permute-start.7 = (bf16[256,1152]{1,0:T(8,128)(2,1)S(1)}, bf16[256,1152]{1,0:T(8,128)(2,1)S(1)}, u32[]{:S(2)}, u32[]{:S(2)}) collective-permute-start(bf16[256,1152]{1,0:T(8,128)(2,1)S(1)} %pass_on.10.refs_1_), channel_id=1, source_target_pairs={{0,28},{4,0},{8,4},{12,8},{16,12},{20,16},{24,20},{28,24},{1,29},{... | collective-permute-start | bytes 1769480 | tf_op jit(solution)/shard_map/ppermute | solution.py:20
  34.0 15.8 %collective-permute-start.6 = (bf16[32,1152]{1,0:T(8,128)(2,1)S(1)}, bf16[32,1152]{1,0:T(8,128)(2,1)S(1)}, u32[]{:S(2)}, u32[]{:S(2)}) collective-permute-start(bf16[32,1152]{1,0:T(8,128)(2,1)S(1)} %pass_on.11), channel_id=1, source_target_pairs={{0,28},{4,0},{8,4},{12,8},{16,12},{20,16},{24,20},{28,24},{1,29},{... | collective-permute-start | bytes 221192 | tf_op jit(solution)/shard_map/ppermute | solution.py:20

commit v26 on v24

--- a/solution.py
+++ b/solution.py
@@ -177,11 +177,11 @@
 
     lasts = part[2].shape[0]
     part1, own1, next1, sent1, sent2 = chunk(factor, shift, image, image_next, part[1:], [sent0], lasts)
+    back1 = shifted(sent1, "blk", -1)
+    next1 = pass_on(next1, [sent1], 2 * 10**10)
     image_sent = (scale * (image_sent + dot_tn(next1, part1))).astype(jnp.bfloat16)
     image_back = shifted(image_sent, "grp", 1)
-    sent1 = pass_on(sent1, [image_sent])
-    back1 = shifted(sent1, "blk", -1)
-    back2 = shifted(pass_on(sent2, [sent1]), "blk", -1)
+    back2 = shifted(pass_on(sent2, [image_sent]), "blk", -1)
     result, mark = add_rows(text_grad, back0, 0, None, [], mark=True)
     own1 = pass_on(own1, [mark])
     image_grad = scale * (image_grad + dot_tn(own1, part1))

time: 50.3 us -> 50.3 us (level)
  transfers between devices with their start and end apart: 8 -> 8, of which waited for: 5 -> 6; matrix products, arithmetic and copies ran while one was open for 14% -> 14% of each run, Pallas kernels for 12% -> 12%
where the time goes in v26:
time: 50.3 us; the launch traced here: 50.1 us
  waiting for transfers between devices  20.7 us (41%)
  starting transfers between devices  10 us (20%)
  matrix products  6.93 us (14%)
  Pallas kernels  6.65 us (13%)
  local copies, waits for them, and re-layouts  3.65 us (7%)
  between operations  2.14 us (4%)
    ppermute x8, waiting for transfers between devices, shifted(): lax.ppermute(shard, axis, [(i, (i + by) % devices) for i in range(devices)])  20.7 us
    ppermute x8, starting transfers between devices, shifted(): lax.ppermute(shard, axis, [(i, (i + by) % devices) for i in range(devices)])  10 us
    dot_general x6, matrix products, dot_tn(): lax.dot_general(a, b, (((0,), (0,)), ((), ())), preferred_element_type=jn...  3.81 us
    pallas_call x4, Pallas kernels, add_rows(): pl.pallas_call(kernel, out_shape=(out, jax.ShapeDtypeStruct((8, 128), jnp...  3.31 us
    pallas_call x2, Pallas kernels, chunk(): pl.pallas_call(functools.partial(chunk_kernel, len(pieces), lasts), out_s...  3.08 us
    unnamed x8, local copies, waits for them, and re-layouts  2.66 us
    dot_general x2, matrix products, dot_nt(): lax.dot_general(a, b, (((1,), (1,)), ((), ())), preferred_element_type=jn...  1.72 us
    dot_general x2, matrix products, dot_nn(): return jnp.dot(a, b, preferred_element_type=jnp.float32)  1.4 us
  transfers between devices with their start and end apart: 8, of which 6 were waited for; matrix products, arithmetic and copies ran while one was open for 14% of the time, Pallas kernels for 12%

profile of v26, /device:TPU:0, one launch (start us, length us, event | category | flops | bytes accessed | tf_op | source)
XLA Modules:
  0.0 50.1 jit_solution(2479341555771205945)
XLA Ops:
  0.6 1.0 %slice.3.refs_0_ = bf16[128,1152]{1,0:T(8,128)(2,1)S(1)} slice(bf16[416,1152]{1,0:T(8,128)(2,1)} %array_ref.5), slice={[0:128], [0:1152]} | slice | bytes 589824 | tf_op jit(solution)/shard_map/slice | solution.py:155
  1.6 3.0 %collective-permute-start = (bf16[128,1152]{1,0:T(8,128)(2,1)S(1)}, bf16[128,1152]{1,0:T(8,128)(2,1)S(1)}, u32[]{:S(2)}, u32[]{:S(2)}) collective-permute-start(bf16[128,1152]{1,0:T(8,128)(2,1)S(1)} %slice.3.refs_0_), channel_id=1, source_target_pairs={{0,4},{4,8},{8,12},{12,16},{16,20},{20,24},{24,28},{28,0},{1,5},{5... | collective-permute-start | bytes 884744 | tf_op jit(solution)/shard_map/ppermute | solution.py:20
  4.6 1.2 %copy-done = bf16[416,1152]{1,0:T(8,128)(2,1)S(1)} copy-done((bf16[416,1152]{1,0:T(8,128)(2,1)S(1)}, bf16[416,1152]{1,0:T(8,128)(2,1)}, u32[]{:S(2)}) %copy-start) | copy-done | bytes 958488
  5.9 1.6 %collective-permute-start.2 = (bf16[240,1152]{1,0:T(8,128)(2,1)S(1)}, bf16[240,1152]{1,0:T(8,128)(2,1)S(1)}, u32[]{:S(2)}, u32[]{:S(2)}) collective-permute-start(bf16[240,1152]{1,0:T(8,128)(2,1)S(1)} %fetch.4), channel_id=1, source_target_pairs={{0,4},{4,8},{8,12},{12,16},{16,20},{20,24},{24,28},{28,0},{1,5},{5... | collective-permute-start | bytes 1658888 | tf_op jit(solution)/shard_map/ppermute | solution.py:20
  7.5 0.4 collective-permute-start.1
  9.2 6.3 %collective-permute-done.refs_0_ = bf16[128,1152]{1,0:T(8,128)(2,1)S(1)} collective-permute-done((bf16[128,1152]{1,0:T(8,128)(2,1)S(1)}, bf16[128,1152]{1,0:T(8,128)(2,1)S(1)}, u32[]{:S(2)}, u32[]{:S(2)}) %collective-permute-start) | collective-permute-done | bytes 294944 | tf_op jit(solution)/shard_map/ppermute | solution.py:20
  15.6 1.2 %copy-done.1 = bf16[416,1152]{1,0:T(8,128)(2,1)S(1)} copy-done((bf16[416,1152]{1,0:T(8,128)(2,1)S(1)}, bf16[416,1152]{1,0:T(8,128)(2,1)}, u32[]{:S(2)}) %copy-start.1) | copy-done | bytes 958488
  16.7 0.3 copy-done.2
  17.0 0.9 %fusion.17.refs_0_ = bf16[416,416]{1,0:T(8,128)(2,1)S(1)} fusion(bf16[416,1152]{1,0:T(8,128)(2,1)S(1)} %copy-done.2, bf16[416,1152]{1,0:T(8,128)(2,1)S(1)} %copy-done.1, s32[416]{0:T(512)S(1)} %bitcast.30, f32[]{:T(128)} %bitcast.28, f32[]{:T(128)} %bitcast.24), kind=kOutput, calls=%fused_computation.23 | convolution fusion | flops 400278528 | bytes 2264712 | tf_op jit(solution)/shard_map/dot_general | solution.py:24
  18.1 0.7 %fusion.19.refs_2_ = f32[416,1152]{1,0:T(8,128)S(1)} fusion(bf16[416,416]{1,0:T(8,128)(2,1)S(1)} %fusion.17.refs_0_, bf16[416,1152]{1,0:T(8,128)(2,1)S(1)} %copy-done.2), kind=kOutput, calls=%fused_computation.26 | convolution fusion | flops 398721024 | bytes 3221504 | tf_op jit(solution)/shard_map/dot_general | solution.py:28
  18.9 0.7 %fusion.18.refs_1_ = f32[416,1152]{1,0:T(8,128)S(1)} fusion(bf16[416,416]{1,0:T(8,128)(2,1)S(1)} %fusion.17.refs_0_, bf16[416,1152]{1,0:T(8,128)(2,1)S(1)} %copy-done.1), kind=kOutput, calls=%fused_computation.25 | convolution fusion | flops 398721024 | bytes 3221504 | tf_op jit(solution)/shard_map/dot_general | solution.py:32
  19.6 0.8 %fusion.16 = bf16[416,416]{1,0:T(8,128)(2,1)S(1)} fusion(bf16[416,1152]{1,0:T(8,128)(2,1)S(1)} %pass_on.7.next_ref, bf16[416,1152]{1,0:T(8,128)(2,1)S(1)} %copy-done.1, f32[]{:T(128)} %bitcast.29, f32[]{:T(128)} %bitcast.27), kind=kOutput, calls=%fused_computation.22 | convolution fusion | flops 399759360 | bytes 2263048 | tf_op jit(solution)/shard_map/dot_general | solution.py:24
  20.4 1.2 %chunk.2 = (bf16[128,1152]{1,0:T(8,128)(2,1)S(1)}, bf16[128,416]{1,0:T(8,128)(2,1)S(1)}, bf16[128,416]{1,0:T(8,128)(2,1)S(1)}, bf16[128,1152]{1,0:T(8,128)(2,1)S(1)}) custom-call(f32[1]{0:T(128)} %copy.23.scale_ref, f32[1]{0:T(128)} %copy.24.bias_ref, bf16[416,1152]{1,0:T(8,128)(2,1)S(1)} %copy-done.2, bf16[416,1152]{1,0:T(8,128)(2,1)S(1)} %pass_on.7.next_ref, ...), custom_call_target="tpu_custom_call" | custom-call | flops 490733568 | bytes 2801664 | tf_op jit(solution)/shard_map/chunk/pallas_call | solution.py:100
  21.7 0.7 %fusion.20 = f32[416,1152]{1,0:T(8,128)S(1)} fusion(bf16[416,416]{1,0:T(8,128)(2,1)S(1)} %fusion.16, bf16[416,1152]{1,0:T(8,128)(2,1)S(1)} %copy-done.1), kind=kOutput, calls=%fused_computation.27 | convolution fusion | flops 398721024 | bytes 3221504 | tf_op jit(solution)/shard_map/dot_general | solution.py:32
  22.4 0.4 convolution_add_fusion.1.refs_2_
  22.8 4.5 %collective-permute-done.2.refs_1_.refs_0_ = bf16[240,1152]{1,0:T(8,128)(2,1)S(1)} collective-permute-done((bf16[240,1152]{1,0:T(8,128)(2,1)S(1)}, bf16[240,1152]{1,0:T(8,128)(2,1)S(1)}, u32[]{:S(2)}, u32[]{:S(2)}) %collective-permute-start.2) | collective-permute-done | bytes 552992 | tf_op jit(solution)/shard_map/ppermute | solution.py:20
  27.4 2.1 %collective-permute-start.4 = (bf16[128,1152]{1,0:T(8,128)(2,1)S(1)}, bf16[128,1152]{1,0:T(8,128)(2,1)S(1)}, u32[]{:S(2)}, u32[]{:S(2)}) collective-permute-start(bf16[128,1152]{1,0:T(8,128)(2,1)S(1)} %pass_on.8.refs_2_), channel_id=1, source_target_pairs={{0,28},{4,0},{8,4},{12,8},{16,12},{20,16},{24,20},{28,24},{1,29},{... | collective-permute-start | bytes 884744 | tf_op jit(solution)/shard_map/ppermute | solution.py:20
  29.4 1.9 %chunk.3 = (bf16[288,1152]{1,0:T(8,128)(2,1)S(1)}, bf16[288,416]{1,0:T(8,128)(2,1)S(1)}, bf16[288,416]{1,0:T(8,128)(2,1)S(1)}, bf16[240,1152]{1,0:T(8,128)(2,1)S(1)}, bf16[48,1152]{1,0:T(8,128)(2,1)S(1)}) custom-call(f32[1]{0:T(128)} %copy.23.scale_ref, f32[1]{0:T(128)} %copy.24.bias_ref, bf16[416,1152]{1,0:T(8,128)(2,1)S(1)} %copy-done.2, ...), custom_call_target="tpu_custom_call" | custom-call | flops 1104150528 | bytes 3907584 | tf_op jit(solution)/shard_map/chunk/pallas_call | solution.py:100
  31.3 1.5 %collective-permute-start.7 = (bf16[240,1152]{1,0:T(8,128)(2,1)S(1)}, bf16[240,1152]{1,0:T(8,128)(2,1)S(1)}, u32[]{:S(2)}, u32[]{:S(2)}) collective-permute-start(bf16[240,1152]{1,0:T(8,128)(2,1)S(1)} %get-tuple-element.23.refs_1_), channel_id=1, source_target_pairs={{0,28},{4,0},{8,4},{12,8},{16,12},{20,16},{24,20},{28,24},{1,29},{... | collective-permute-start | bytes 1658888 | tf_op jit(solution)/shard_map/ppermute | solution.py:20
  32.8 0.7 %fusion.4.refs_1_ = bf16[416,1152]{1,0:T(8,128)(2,1)S(1)} fusion(f32[416,1152]{1,0:T(8,128)S(1)} %convolution_add_fusion.1.refs_2_, bf16[288,416]{1,0:T(8,128)(2,1)S(1)} %pass_on.10, bf16[288,1152]{1,0:T(8,128)(2,1)S(1)} %get-tuple-element.21, f32[]{:T(128)} %bitcast.25), kind=kOutput, calls=%fused_computation.8 | convolution fusion | flops 277475328 | bytes 3778564 | tf_op jit(solution)/shard_map/dot_general | solution.py:28
  33.6 1.4 %collective-permute-start.6 = (bf16[48,1152]{1,0:T(8,128)(2,1)S(1)}, bf16[48,1152]{1,0:T(8,128)(2,1)S(1)}, u32[]{:S(2)}, u32[]{:S(2)}) collective-permute-start(bf16[48,1152]{1,0:T(8,128)(2,1)S(1)} %pass_on.11), channel_id=1, source_target_pairs={{0,28},{4,0},{8,4},{12,8},{16,12},{20,16},{24,20},{28,24},{1,29},{... | collective-permute-start | bytes 331784 | tf_op jit(solution)/shard_map/ppermute | solution.py:20
  34.9 0.7 %fusion.total_ref = f32[416,1152]{1,0:T(8,128)S(1)} fusion(f32[416,1152]{1,0:T(8,128)S(1)} %fusion.19.refs_2_, bf16[416,416]{1,0:T(8,128)(2,1)S(1)} %fusion.16, bf16[416,1152]{1,0:T(8,128)(2,1)S(1)} %pass_on.7.next_ref, f32[]{:T(128)} %bitcast.23), kind=kOutput, calls=%fused_computation.1 | convolution fusion | flops 399679488 | bytes 5138436 | tf_op jit(solution)/shard_map/dot_general | solution.py:28
  35.7 1.6 %collective-permute-done.4.back_ref = bf16[128,1152]{1,0:T(8,128)(2,1)S(1)} collective-permute-done((bf16[128,1152]{1,0:T(8,128)(2,1)S(1)}, bf16[128,1152]{1,0:T(8,128)(2,1)S(1)}, u32[]{:S(2)}, u32[]{:S(2)}) %collective-permute-start.4) | collective-permute-done | bytes 294944 | tf_op jit(solution)/shard_map/ppermute | solution.py:20
  37.3 0.8 %add_rows.4 = (bf16[416,1152]{1,0:T(8,128)(2,1)}, f32[8,128]{1,0:T(8,128)S(1)}) custom-call(f32[416,1152]{1,0:T(8,128)S(1)} %fusion.total_ref, bf16[128,1152]{1,0:T(8,128)(2,1)S(1)} %collective-permute-done.4.back_ref), custom_call_target="tpu_custom_call" | custom-call | tf_op jit(solution)/shard_map/add_rows/pallas_call | solution.py:139
  38.1 0.7 %fusion.21 = f32[416,1152]{1,0:T(8,128)S(1)} fusion(bf16[288,416]{1,0:T(8,128)(2,1)S(1)} %pass_on.9, bf16[288,1152]{1,0:T(8,128)(2,1)S(1)} %get-tuple-element.21), kind=kOutput, calls=%fused_computation.28 | convolution fusion | flops 276037632 | bytes 2820096 | tf_op jit(solution)/shard_map/dot_general | solution.py:28
  38.8 0.4 fusion.2.total_ref
  39.2 7.6 %collective-permute-done.5.back_ref = bf16[416,1152]{1,0:T(8,128)(2,1)S(1)} collective-permute-done((bf16[416,1152]{1,0:T(8,128)(2,1)S(1)}, bf16[416,1152]{1,0:T(8,128)(2,1)S(1)}, u32[]{:S(2)}, u32[]{:S(2)}) %collective-permute-start.5) | collective-permute-done | bytes 958496 | tf_op jit(solution)/shard_map/ppermute | solution.py:20
  46.8 1.0 %add_rows.5 = (bf16[416,1152]{1,0:T(8,128)(2,1)}, f32[8,128]{1,0:T(8,128)S(1)}) custom-call(f32[416,1152]{1,0:T(8,128)S(1)} %fusion.2.total_ref, bf16[416,1152]{1,0:T(8,128)(2,1)S(1)} %collective-permute-done.5.back_ref), custom_call_target="tpu_custom_call" | custom-call | tf_op jit(solution)/shard_map/add_rows/pallas_call | solution.py:139
  47.8 0.4 collective-permute-done.7.back_ref
  48.2 0.9 %add_rows.6.refs_0_ = bf16[416,1152]{1,0:T(8,128)(2,1)} custom-call(f32[416,1152]{1,0:T(8,128)S(1)} %fusion.total_ref, bf16[240,1152]{1,0:T(8,128)(2,1)S(1)} %collective-permute-done.7.back_ref, bf16[416,1152]{1,0:T(8,128)(2,1)} %get-tuple-element.26.refs_0_, f32[8,128]{1,0:T(8,128)S(1)} %get-tuple-element.27.refs_1_), custom_call_target="tpu_custom_call", output_to_operand_aliasing={{}: (2, {})} | custom-call | tf_op jit(solution)/shard_map/add_rows/pallas_call | solution.py:139
  49.1 0.3 collective-permute-done.6.back_ref
  49.4 0.7 %add_rows.7 = bf16[416,1152]{1,0:T(8,128)(2,1)} custom-call(f32[416,1152]{1,0:T(8,128)S(1)} %fusion.total_ref, bf16[48,1152]{1,0:T(8,128)(2,1)S(1)} %collective-permute-done.6.back_ref, bf16[416,1152]{1,0:T(8,128)(2,1)} %add_rows.6.refs_0_), custom_call_target="tpu_custom_call", output_to_operand_aliasing={{}: (2, {})} | custom-call | tf_op jit(solution)/shard_map/add_rows/pallas_call | solution.py:139
  (18 shorter events, 0.4 us)
Async XLA Ops:
  0.6 14.9 %copy-start.3 = (s32[1,416]{1,0:T(1,128)S(1)}, s32[1,416]{1,0:T(1,128)}, u32[]{:S(2)}) copy-start(s32[1,416]{1,0:T(1,128)} %array_ref.3) | copy-start | bytes 4996
  1.6 13.9 %collective-permute-start = (bf16[128,1152]{1,0:T(8,128)(2,1)S(1)}, bf16[128,1152]{1,0:T(8,128)(2,1)S(1)}, u32[]{:S(2)}, u32[]{:S(2)}) collective-permute-start(bf16[128,1152]{1,0:T(8,128)(2,1)S(1)} %slice.3.refs_0_), channel_id=1, source_target_pairs={{0,4},{4,8},{8,12},{12,16},{16,20},{20,24},{24,28},{28,0},{1,5},{5... | collective-permute-start | bytes 884744 | tf_op jit(solution)/shard_map/ppermute | solution.py:20
  4.6 1.2 %copy-start = (bf16[416,1152]{1,0:T(8,128)(2,1)S(1)}, bf16[416,1152]{1,0:T(8,128)(2,1)}, u32[]{:S(2)}) copy-start(bf16[416,1152]{1,0:T(8,128)(2,1)} %array_ref.5) | copy-start | bytes 2875396
  5.9 21.4 %collective-permute-start.2 = (bf16[240,1152]{1,0:T(8,128)(2,1)S(1)}, bf16[240,1152]{1,0:T(8,128)(2,1)S(1)}, u32[]{:S(2)}, u32[]{:S(2)}) collective-permute-start(bf16[240,1152]{1,0:T(8,128)(2,1)S(1)} %fetch.4), channel_id=1, source_target_pairs={{0,4},{4,8},{8,12},{12,16},{16,20},{20,24},{24,28},{28,0},{1,5},{5... | collective-permute-start | bytes 1658888 | tf_op jit(solution)/shard_map/ppermute | solution.py:20
  7.5 12.1 %collective-permute-start.1 = (bf16[416,1152]{1,0:T(8,128)(2,1)}, bf16[416,1152]{1,0:T(8,128)(2,1)S(1)}, u32[]{:S(2)}, u32[]{:S(2)}) collective-permute-start(bf16[416,1152]{1,0:T(8,128)(2,1)} %image_ref.3), channel_id=1, source_target_pairs={{0,3},{1,0},{2,1},{3,2},{4,7},{5,4},{6,5},{7,6},{8,11},{9,8},{10,9... | collective-permute-start | bytes 2875400 | tf_op jit(solution)/shard_map/ppermute | solution.py:20
  15.5 1.2 %copy-start.1 = (bf16[416,1152]{1,0:T(8,128)(2,1)S(1)}, bf16[416,1152]{1,0:T(8,128)(2,1)}, u32[]{:S(2)}) copy-start(bf16[416,1152]{1,0:T(8,128)(2,1)} %array_ref.5) | copy-start | bytes 2875396
  15.5 1.5 %copy-start.2 = (bf16[416,1152]{1,0:T(8,128)(2,1)S(1)}, bf16[416,1152]{1,0:T(8,128)(2,1)}, u32[]{:S(2)}) copy-start(bf16[416,1152]{1,0:T(8,128)(2,1)} %image_ref.3) | copy-start | bytes 2875396
  18.1 11.4 %collective-permute-start.3 = (bf16[48,1152]{1,0:T(8,128)(2,1)S(1)}, bf16[48,1152]{1,0:T(8,128)(2,1)S(1)}, u32[]{:S(2)}, u32[]{:S(2)}) collective-permute-start(bf16[48,1152]{1,0:T(8,128)(2,1)S(1)} %fetch.5), channel_id=1, source_target_pairs={{0,4},{4,8},{8,12},{12,16},{16,20},{20,24},{24,28},{28,0},{1,5},{5... | collective-permute-start | bytes 331784 | tf_op jit(solution)/shard_map/ppermute | solution.py:20
  27.4 9.9 %collective-permute-start.4 = (bf16[128,1152]{1,0:T(8,128)(2,1)S(1)}, bf16[128,1152]{1,0:T(8,128)(2,1)S(1)}, u32[]{:S(2)}, u32[]{:S(2)}) collective-permute-start(bf16[128,1152]{1,0:T(8,128)(2,1)S(1)} %pass_on.8.refs_2_), channel_id=1, source_target_pairs={{0,28},{4,0},{8,4},{12,8},{16,12},{20,16},{24,20},{28,24},{1,29},{... | collective-permute-start | bytes 884744 | tf_op jit(solution)/shard_map/ppermute | solution.py:20
  31.3 17.0 %collective-permute-start.7 = (bf16[240,1152]{1,0:T(8,128)(2,1)S(1)}, bf16[240,1152]{1,0:T(8,128)(2,1)S(1)}, u32[]{:S(2)}, u32[]{:S(2)}) collective-permute-start(bf16[240,1152]{1,0:T(8,128)(2,1)S(1)} %get-tuple-element.23.refs_1_), channel_id=1, source_target_pairs={{0,28},{4,0},{8,4},{12,8},{16,12},{20,16},{24,20},{28,24},{1,29},{... | collective-permute-start | bytes 1658888 | tf_op jit(solution)/shard_map/ppermute | solution.py:20
  33.5 13.3 %collective-permute-start.5 = (bf16[416,1152]{1,0:T(8,128)(2,1)S(1)}, bf16[416,1152]{1,0:T(8,128)(2,1)S(1)}, u32[]{:S(2)}, u32[]{:S(2)}) collective-permute-start(bf16[416,1152]{1,0:T(8,128)(2,1)S(1)} %fusion.4.refs_1_), channel_id=1, source_target_pairs={{0,1},{1,2},{2,3},{3,0},{4,5},{5,6},{6,7},{7,4},{8,9},{9,10},{10,1... | collective-permute-start | bytes 2875400 | tf_op jit(solution)/shard_map/ppermute | solution.py:20
  33.6 15.9 %collective-permute-start.6 = (bf16[48,1152]{1,0:T(8,128)(2,1)S(1)}, bf16[48,1152]{1,0:T(8,128)(2,1)S(1)}, u32[]{:S(2)}, u32[]{:S(2)}) collective-permute-start(bf16[48,1152]{1,0:T(8,128)(2,1)S(1)} %pass_on.11), channel_id=1, source_target_pairs={{0,28},{4,0},{8,4},{12,8},{16,12},{20,16},{24,20},{28,24},{1,29},{... | collective-permute-start | bytes 331784 | tf_op jit(solution)/shard_map/ppermute | solution.py:20

commit v27 on v26

--- a/solution.py
+++ b/solution.py
@@ -8,7 +8,7 @@
 from jax.sharding import PartitionSpec as P
 
 MIB = 2**20
-ENDS = (8, 23)
+ENDS = (6, 23)
 SMEM = pl.BlockSpec(memory_space=pltpu.SMEM)
 VMEM = pl.BlockSpec(memory_space=pltpu.VMEM)
 HBM = pl.BlockSpec(memory_space=pltpu.HBM)

time: 50.3 us -> 50.3 us (level)
  no operation moved by 1% of the time
where the time goes in v27:
time: 50.3 us; the launch traced here: 50.1 us
  waiting for transfers between devices  20.4 us (41%)
  starting transfers between devices  10 us (20%)
  matrix products  6.98 us (14%)
  Pallas kernels  6.89 us (14%)
  local copies, waits for them, and re-layouts  3.62 us (7%)
  between operations  2.14 us (4%)
    ppermute x8, waiting for transfers between devices, shifted(): lax.ppermute(shard, axis, [(i, (i + by) % devices) for i in range(devices)])  20.4 us
    ppermute x8, starting transfers between devices, shifted(): lax.ppermute(shard, axis, [(i, (i + by) % devices) for i in range(devices)])  10 us
    dot_general x6, matrix products, dot_tn(): lax.dot_general(a, b, (((0,), (0,)), ((), ())), preferred_element_type=jn...  3.84 us
    pallas_call x4, Pallas kernels, add_rows(): pl.pallas_call(kernel, out_shape=(out, jax.ShapeDtypeStruct((8, 128), jnp...  3.32 us
    pallas_call x2, Pallas kernels, chunk(): pl.pallas_call(functools.partial(chunk_kernel, len(pieces), lasts), out_s...  3.23 us
    unnamed x8, local copies, waits for them, and re-layouts  2.66 us
    dot_general x2, matrix products, dot_nt(): lax.dot_general(a, b, (((1,), (1,)), ((), ())), preferred_element_type=jn...  1.72 us
    dot_general x2, matrix products, dot_nn(): return jnp.dot(a, b, preferred_element_type=jnp.float32)  1.42 us
  transfers between devices with their start and end apart: 8, of which 6 were waited for; matrix products, arithmetic and copies ran while one was open for 14% of the time, Pallas kernels for 12%

profile of v27, /device:TPU:0, one launch (start us, length us, event | category | flops | bytes accessed | tf_op | source)
XLA Modules:
  0.0 50.1 jit_solution(16629396579075638339)
XLA Ops:
  0.6 1.0 %slice.3.refs_0_ = bf16[96,1152]{1,0:T(8,128)(2,1)S(1)} slice(bf16[416,1152]{1,0:T(8,128)(2,1)} %array_ref.5), slice={[0:96], [0:1152]} | slice | bytes 442368 | tf_op jit(solution)/shard_map/slice | solution.py:155
  1.6 3.0 %collective-permute-start = (bf16[96,1152]{1,0:T(8,128)(2,1)S(1)}, bf16[96,1152]{1,0:T(8,128)(2,1)S(1)}, u32[]{:S(2)}, u32[]{:S(2)}) collective-permute-start(bf16[96,1152]{1,0:T(8,128)(2,1)S(1)} %slice.3.refs_0_), channel_id=1, source_target_pairs={{0,4},{4,8},{8,12},{12,16},{16,20},{20,24},{24,28},{28,0},{1,5},{5... | collective-permute-start | bytes 663560 | tf_op jit(solution)/shard_map/ppermute | solution.py:20
  4.6 1.2 %copy-done = bf16[416,1152]{1,0:T(8,128)(2,1)S(1)} copy-done((bf16[416,1152]{1,0:T(8,128)(2,1)S(1)}, bf16[416,1152]{1,0:T(8,128)(2,1)}, u32[]{:S(2)}) %copy-start) | copy-done | bytes 958488
  6.0 1.6 %collective-permute-start.2 = (bf16[272,1152]{1,0:T(8,128)(2,1)S(1)}, bf16[272,1152]{1,0:T(8,128)(2,1)S(1)}, u32[]{:S(2)}, u32[]{:S(2)}) collective-permute-start(bf16[272,1152]{1,0:T(8,128)(2,1)S(1)} %fetch.4), channel_id=1, source_target_pairs={{0,4},{4,8},{8,12},{12,16},{16,20},{20,24},{24,28},{28,0},{1,5},{5... | collective-permute-start | bytes 1880072 | tf_op jit(solution)/shard_map/ppermute | solution.py:20
  7.6 0.4 collective-permute-start.1
  9.3 4.6 %collective-permute-done.refs_0_ = bf16[96,1152]{1,0:T(8,128)(2,1)S(1)} collective-permute-done((bf16[96,1152]{1,0:T(8,128)(2,1)S(1)}, bf16[96,1152]{1,0:T(8,128)(2,1)S(1)}, u32[]{:S(2)}, u32[]{:S(2)}) %collective-permute-start) | collective-permute-done | bytes 221216 | tf_op jit(solution)/shard_map/ppermute | solution.py:20
  13.9 1.2 %copy-done.1 = bf16[416,1152]{1,0:T(8,128)(2,1)S(1)} copy-done((bf16[416,1152]{1,0:T(8,128)(2,1)S(1)}, bf16[416,1152]{1,0:T(8,128)(2,1)}, u32[]{:S(2)}) %copy-start.1) | copy-done | bytes 958488
  15.1 0.3 copy-done.2
  15.4 0.9 %fusion.17.refs_0_ = bf16[416,416]{1,0:T(8,128)(2,1)S(1)} fusion(bf16[416,1152]{1,0:T(8,128)(2,1)S(1)} %copy-done.2, bf16[416,1152]{1,0:T(8,128)(2,1)S(1)} %copy-done.1, s32[416]{0:T(512)S(1)} %bitcast.30, f32[]{:T(128)} %bitcast.28, f32[]{:T(128)} %bitcast.24), kind=kOutput, calls=%fused_computation.23 | convolution fusion | flops 400278528 | bytes 2264712 | tf_op jit(solution)/shard_map/dot_general | solution.py:24
  16.5 0.7 %fusion.19.refs_2_ = f32[416,1152]{1,0:T(8,128)S(1)} fusion(bf16[416,416]{1,0:T(8,128)(2,1)S(1)} %fusion.17.refs_0_, bf16[416,1152]{1,0:T(8,128)(2,1)S(1)} %copy-done.2), kind=kOutput, calls=%fused_computation.26 | convolution fusion | flops 398721024 | bytes 3221504 | tf_op jit(solution)/shard_map/dot_general | solution.py:28
  17.3 0.7 %fusion.18.refs_1_ = f32[416,1152]{1,0:T(8,128)S(1)} fusion(bf16[416,416]{1,0:T(8,128)(2,1)S(1)} %fusion.17.refs_0_, bf16[416,1152]{1,0:T(8,128)(2,1)S(1)} %copy-done.1), kind=kOutput, calls=%fused_computation.25 | convolution fusion | flops 398721024 | bytes 3221504 | tf_op jit(solution)/shard_map/dot_general | solution.py:32
  18.0 1.7 %collective-permute-done.1.refs_0_ = bf16[416,1152]{1,0:T(8,128)(2,1)S(1)} collective-permute-done((bf16[416,1152]{1,0:T(8,128)(2,1)}, bf16[416,1152]{1,0:T(8,128)(2,1)S(1)}, u32[]{:S(2)}, u32[]{:S(2)}) %collective-permute-start.1) | collective-permute-done | bytes 958496 | tf_op jit(solution)/shard_map/ppermute | solution.py:20
  19.6 0.8 %fusion.16 = bf16[416,416]{1,0:T(8,128)(2,1)S(1)} fusion(bf16[416,1152]{1,0:T(8,128)(2,1)S(1)} %pass_on.7.next_ref, bf16[416,1152]{1,0:T(8,128)(2,1)S(1)} %copy-done.1, f32[]{:T(128)} %bitcast.29, f32[]{:T(128)} %bitcast.27), kind=kOutput, calls=%fused_computation.22 | convolution fusion | flops 399759360 | bytes 2263048 | tf_op jit(solution)/shard_map/dot_general | solution.py:24
  20.5 1.2 %chunk.2 = (bf16[96,1152]{1,0:T(8,128)(2,1)S(1)}, bf16[96,416]{1,0:T(8,128)(2,1)S(1)}, bf16[96,416]{1,0:T(8,128)(2,1)S(1)}, bf16[96,1152]{1,0:T(8,128)(2,1)S(1)}) custom-call(f32[1]{0:T(128)} %copy.23.scale_ref, f32[1]{0:T(128)} %copy.24.bias_ref, bf16[416,1152]{1,0:T(8,128)(2,1)S(1)} %copy-done.2, bf16[416,1152]{1,0:T(8,128)(2,1)S(1)} %pass_on.7.next_ref, ...), custom_call_target="tpu_custom_call" | custom-call | flops 368050176 | bytes 2580480 | tf_op jit(solution)/shard_map/chunk/pallas_call | solution.py:100
  21.7 0.7 %fusion.20 = f32[416,1152]{1,0:T(8,128)S(1)} fusion(bf16[416,416]{1,0:T(8,128)(2,1)S(1)} %fusion.16, bf16[416,1152]{1,0:T(8,128)(2,1)S(1)} %copy-done.1), kind=kOutput, calls=%fused_computation.27 | convolution fusion | flops 398721024 | bytes 3221504 | tf_op jit(solution)/shard_map/dot_general | solution.py:32
  22.4 0.4 convolution_add_fusion.1.refs_2_
  22.8 4.5 %collective-permute-done.2.refs_1_.refs_0_ = bf16[272,1152]{1,0:T(8,128)(2,1)S(1)} collective-permute-done((bf16[272,1152]{1,0:T(8,128)(2,1)S(1)}, bf16[272,1152]{1,0:T(8,128)(2,1)S(1)}, u32[]{:S(2)}, u32[]{:S(2)}) %collective-permute-start.2) | collective-permute-done | bytes 626720 | tf_op jit(solution)/shard_map/ppermute | solution.py:20
  27.3 2.1 %collective-permute-start.4 = (bf16[96,1152]{1,0:T(8,128)(2,1)S(1)}, bf16[96,1152]{1,0:T(8,128)(2,1)S(1)}, u32[]{:S(2)}, u32[]{:S(2)}) collective-permute-start(bf16[96,1152]{1,0:T(8,128)(2,1)S(1)} %pass_on.8.refs_2_), channel_id=1, source_target_pairs={{0,28},{4,0},{8,4},{12,8},{16,12},{20,16},{24,20},{28,24},{1,29},{... | collective-permute-start | bytes 663560 | tf_op jit(solution)/shard_map/ppermute | solution.py:20
  29.4 2.0 %chunk.3 = (bf16[320,1152]{1,0:T(8,128)(2,1)S(1)}, bf16[320,416]{1,0:T(8,128)(2,1)S(1)}, bf16[320,416]{1,0:T(8,128)(2,1)S(1)}, bf16[272,1152]{1,0:T(8,128)(2,1)S(1)}, bf16[48,1152]{1,0:T(8,128)(2,1)S(1)}) custom-call(f32[1]{0:T(128)} %copy.23.scale_ref, f32[1]{0:T(128)} %copy.24.bias_ref, bf16[416,1152]{1,0:T(8,128)(2,1)S(1)} %copy-done.2, ...), custom_call_target="tpu_custom_call" | custom-call | flops 1226833920 | bytes 4128768 | tf_op jit(solution)/shard_map/chunk/pallas_call | solution.py:100
  31.4 1.5 %collective-permute-start.7 = (bf16[272,1152]{1,0:T(8,128)(2,1)S(1)}, bf16[272,1152]{1,0:T(8,128)(2,1)S(1)}, u32[]{:S(2)}, u32[]{:S(2)}) collective-permute-start(bf16[272,1152]{1,0:T(8,128)(2,1)S(1)} %get-tuple-element.23.refs_1_), channel_id=1, source_target_pairs={{0,28},{4,0},{8,4},{12,8},{16,12},{20,16},{24,20},{28,24},{1,29},{... | collective-permute-start | bytes 1880072 | tf_op jit(solution)/shard_map/ppermute | solution.py:20
  32.9 0.7 %fusion.4.refs_1_ = bf16[416,1152]{1,0:T(8,128)(2,1)S(1)} fusion(f32[416,1152]{1,0:T(8,128)S(1)} %convolution_add_fusion.1.refs_2_, bf16[320,416]{1,0:T(8,128)(2,1)S(1)} %pass_on.10, bf16[320,1152]{1,0:T(8,128)(2,1)S(1)} %get-tuple-element.21, f32[]{:T(128)} %bitcast.25), kind=kOutput, calls=%fused_computation.8 | convolution fusion | flops 308146176 | bytes 3878916 | tf_op jit(solution)/shard_map/dot_general | solution.py:28
  33.7 1.4 %collective-permute-start.6 = (bf16[48,1152]{1,0:T(8,128)(2,1)S(1)}, bf16[48,1152]{1,0:T(8,128)(2,1)S(1)}, u32[]{:S(2)}, u32[]{:S(2)}) collective-permute-start(bf16[48,1152]{1,0:T(8,128)(2,1)S(1)} %pass_on.11), channel_id=1, source_target_pairs={{0,28},{4,0},{8,4},{12,8},{16,12},{20,16},{24,20},{28,24},{1,29},{... | collective-permute-start | bytes 331784 | tf_op jit(solution)/shard_map/ppermute | solution.py:20
  35.1 0.8 %fusion.total_ref = f32[416,1152]{1,0:T(8,128)S(1)} fusion(f32[416,1152]{1,0:T(8,128)S(1)} %fusion.19.refs_2_, bf16[416,416]{1,0:T(8,128)(2,1)S(1)} %fusion.16, bf16[416,1152]{1,0:T(8,128)(2,1)S(1)} %pass_on.7.next_ref, f32[]{:T(128)} %bitcast.23), kind=kOutput, calls=%fused_computation.1 | convolution fusion | flops 399679488 | bytes 5138436 | tf_op jit(solution)/shard_map/dot_general | solution.py:28
  35.9 0.7 %add_rows.4 = (bf16[416,1152]{1,0:T(8,128)(2,1)}, f32[8,128]{1,0:T(8,128)S(1)}) custom-call(f32[416,1152]{1,0:T(8,128)S(1)} %fusion.total_ref, bf16[96,1152]{1,0:T(8,128)(2,1)S(1)} %collective-permute-done.4.back_ref), custom_call_target="tpu_custom_call" | custom-call | tf_op jit(solution)/shard_map/add_rows/pallas_call | solution.py:139
  36.6 0.7 %fusion.21 = f32[416,1152]{1,0:T(8,128)S(1)} fusion(bf16[320,416]{1,0:T(8,128)(2,1)S(1)} %pass_on.9, bf16[320,1152]{1,0:T(8,128)(2,1)S(1)} %get-tuple-element.21), kind=kOutput, calls=%fused_computation.28 | convolution fusion | flops 306708480 | bytes 2920448 | tf_op jit(solution)/shard_map/dot_general | solution.py:28
  37.4 0.4 fusion.2.total_ref
  37.8 9.2 %collective-permute-done.5.back_ref = bf16[416,1152]{1,0:T(8,128)(2,1)S(1)} collective-permute-done((bf16[416,1152]{1,0:T(8,128)(2,1)S(1)}, bf16[416,1152]{1,0:T(8,128)(2,1)S(1)}, u32[]{:S(2)}, u32[]{:S(2)}) %collective-permute-start.5) | collective-permute-done | bytes 958496 | tf_op jit(solution)/shard_map/ppermute | solution.py:20
  47.0 1.0 %add_rows.5 = (bf16[416,1152]{1,0:T(8,128)(2,1)}, f32[8,128]{1,0:T(8,128)S(1)}) custom-call(f32[416,1152]{1,0:T(8,128)S(1)} %fusion.2.total_ref, bf16[416,1152]{1,0:T(8,128)(2,1)S(1)} %collective-permute-done.5.back_ref), custom_call_target="tpu_custom_call" | custom-call | tf_op jit(solution)/shard_map/add_rows/pallas_call | solution.py:139
  48.0 0.2 collective-permute-done.7.back_ref
  48.2 0.9 %add_rows.6.refs_0_ = bf16[416,1152]{1,0:T(8,128)(2,1)} custom-call(f32[416,1152]{1,0:T(8,128)S(1)} %fusion.total_ref, bf16[272,1152]{1,0:T(8,128)(2,1)S(1)} %collective-permute-done.7.back_ref, bf16[416,1152]{1,0:T(8,128)(2,1)} %get-tuple-element.26.refs_0_, f32[8,128]{1,0:T(8,128)S(1)} %get-tuple-element.27.refs_1_), custom_call_target="tpu_custom_call", output_to_operand_aliasing={{}: (2, {})} | custom-call | tf_op jit(solution)/shard_map/add_rows/pallas_call | solution.py:139
  49.1 0.3 collective-permute-done.6.back_ref
  49.4 0.7 %add_rows.7 = bf16[416,1152]{1,0:T(8,128)(2,1)} custom-call(f32[416,1152]{1,0:T(8,128)S(1)} %fusion.total_ref, bf16[48,1152]{1,0:T(8,128)(2,1)S(1)} %collective-permute-done.6.back_ref, bf16[416,1152]{1,0:T(8,128)(2,1)} %add_rows.6.refs_0_), custom_call_target="tpu_custom_call", output_to_operand_aliasing={{}: (2, {})} | custom-call | tf_op jit(solution)/shard_map/add_rows/pallas_call | solution.py:139
  (18 shorter events, 0.5 us)
Async XLA Ops:
  0.6 13.3 %copy-start.3 = (s32[1,416]{1,0:T(1,128)S(1)}, s32[1,416]{1,0:T(1,128)}, u32[]{:S(2)}) copy-start(s32[1,416]{1,0:T(1,128)} %array_ref.3) | copy-start | bytes 4996
  1.6 12.3 %collective-permute-start = (bf16[96,1152]{1,0:T(8,128)(2,1)S(1)}, bf16[96,1152]{1,0:T(8,128)(2,1)S(1)}, u32[]{:S(2)}, u32[]{:S(2)}) collective-permute-start(bf16[96,1152]{1,0:T(8,128)(2,1)S(1)} %slice.3.refs_0_), channel_id=1, source_target_pairs={{0,4},{4,8},{8,12},{12,16},{16,20},{20,24},{24,28},{28,0},{1,5},{5... | collective-permute-start | bytes 663560 | tf_op jit(solution)/shard_map/ppermute | solution.py:20
  4.6 1.2 %copy-start = (bf16[416,1152]{1,0:T(8,128)(2,1)S(1)}, bf16[416,1152]{1,0:T(8,128)(2,1)}, u32[]{:S(2)}) copy-start(bf16[416,1152]{1,0:T(8,128)(2,1)} %array_ref.5) | copy-start | bytes 2875396
  6.0 21.3 %collective-permute-start.2 = (bf16[272,1152]{1,0:T(8,128)(2,1)S(1)}, bf16[272,1152]{1,0:T(8,128)(2,1)S(1)}, u32[]{:S(2)}, u32[]{:S(2)}) collective-permute-start(bf16[272,1152]{1,0:T(8,128)(2,1)S(1)} %fetch.4), channel_id=1, source_target_pairs={{0,4},{4,8},{8,12},{12,16},{16,20},{20,24},{24,28},{28,0},{1,5},{5... | collective-permute-start | bytes 1880072 | tf_op jit(solution)/shard_map/ppermute | solution.py:20
  7.6 12.1 %collective-permute-start.1 = (bf16[416,1152]{1,0:T(8,128)(2,1)}, bf16[416,1152]{1,0:T(8,128)(2,1)S(1)}, u32[]{:S(2)}, u32[]{:S(2)}) collective-permute-start(bf16[416,1152]{1,0:T(8,128)(2,1)} %image_ref.3), channel_id=1, source_target_pairs={{0,3},{1,0},{2,1},{3,2},{4,7},{5,4},{6,5},{7,6},{8,11},{9,8},{10,9... | collective-permute-start | bytes 2875400 | tf_op jit(solution)/shard_map/ppermute | solution.py:20
  13.9 1.2 %copy-start.1 = (bf16[416,1152]{1,0:T(8,128)(2,1)S(1)}, bf16[416,1152]{1,0:T(8,128)(2,1)}, u32[]{:S(2)}) copy-start(bf16[416,1152]{1,0:T(8,128)(2,1)} %array_ref.5) | copy-start | bytes 2875396
  13.9 1.5 %copy-start.2 = (bf16[416,1152]{1,0:T(8,128)(2,1)S(1)}, bf16[416,1152]{1,0:T(8,128)(2,1)}, u32[]{:S(2)}) copy-start(bf16[416,1152]{1,0:T(8,128)(2,1)} %image_ref.3) | copy-start | bytes 2875396
  16.5 12.9 %collective-permute-start.3 = (bf16[48,1152]{1,0:T(8,128)(2,1)S(1)}, bf16[48,1152]{1,0:T(8,128)(2,1)S(1)}, u32[]{:S(2)}, u32[]{:S(2)}) collective-permute-start(bf16[48,1152]{1,0:T(8,128)(2,1)S(1)} %fetch.5), channel_id=1, source_target_pairs={{0,4},{4,8},{8,12},{12,16},{16,20},{20,24},{24,28},{28,0},{1,5},{5... | collective-permute-start | bytes 331784 | tf_op jit(solution)/shard_map/ppermute | solution.py:20
  27.3 8.6 %collective-permute-start.4 = (bf16[96,1152]{1,0:T(8,128)(2,1)S(1)}, bf16[96,1152]{1,0:T(8,128)(2,1)S(1)}, u32[]{:S(2)}, u32[]{:S(2)}) collective-permute-start(bf16[96,1152]{1,0:T(8,128)(2,1)S(1)} %pass_on.8.refs_2_), channel_id=1, source_target_pairs={{0,28},{4,0},{8,4},{12,8},{16,12},{20,16},{24,20},{28,24},{1,29},{... | collective-permute-start | bytes 663560 | tf_op jit(solution)/shard_map/ppermute | solution.py:20
  31.4 16.8 %collective-permute-start.7 = (bf16[272,1152]{1,0:T(8,128)(2,1)S(1)}, bf16[272,1152]{1,0:T(8,128)(2,1)S(1)}, u32[]{:S(2)}, u32[]{:S(2)}) collective-permute-start(bf16[272,1152]{1,0:T(8,128)(2,1)S(1)} %get-tuple-element.23.refs_1_), channel_id=1, source_target_pairs={{0,28},{4,0},{8,4},{12,8},{16,12},{20,16},{24,20},{28,24},{1,29},{... | collective-permute-start | bytes 1880072 | tf_op jit(solution)/shard_map/ppermute | solution.py:20
  33.7 13.3 %collective-permute-start.5 = (bf16[416,1152]{1,0:T(8,128)(2,1)S(1)}, bf16[416,1152]{1,0:T(8,128)(2,1)S(1)}, u32[]{:S(2)}, u32[]{:S(2)}) collective-permute-start(bf16[416,1152]{1,0:T(8,128)(2,1)S(1)} %fusion.4.refs_1_), channel_id=1, source_target_pairs={{0,1},{1,2},{2,3},{3,0},{4,5},{5,6},{6,7},{7,4},{8,9},{9,10},{10,1... | collective-permute-start | bytes 2875400 | tf_op jit(solution)/shard_map/ppermute | solution.py:20
  33.7 15.7 %collective-permute-start.6 = (bf16[48,1152]{1,0:T(8,128)(2,1)S(1)}, bf16[48,1152]{1,0:T(8,128)(2,1)S(1)}, u32[]{:S(2)}, u32[]{:S(2)}) collective-permute-start(bf16[48,1152]{1,0:T(8,128)(2,1)S(1)} %pass_on.11), channel_id=1, source_target_pairs={{0,28},{4,0},{8,4},{12,8},{16,12},{20,16},{24,20},{28,24},{1,29},{... | collective-permute-start | bytes 331784 | tf_op jit(solution)/shard_map/ppermute | solution.py:20

commit v28 on v27

--- a/solution.py
+++ b/solution.py
@@ -8,7 +8,7 @@
 from jax.sharding import PartitionSpec as P
 
 MIB = 2**20
-ENDS = (6, 23)
+ENDS = (10, 23)
 SMEM = pl.BlockSpec(memory_space=pltpu.SMEM)
 VMEM = pl.BlockSpec(memory_space=pltpu.VMEM)
 HBM = pl.BlockSpec(memory_space=pltpu.HBM)

time: 50.3 us -> 50.4 us (level)
  waiting for transfers between devices: 20.4 us -> 21 us
    ppermute x8, waiting for transfers between devices: 20.4 us -> 21 us  [shifted(): lax.ppermute(shard, axis, [(i, (i + by) % devices) for i in range(devices)])]
  transfers between devices with their start and end apart: 8 -> 8, of which waited for: 6 -> 6; matrix products, arithmetic and copies ran while one was open for 14% -> 13% of each run, Pallas kernels for 12% -> 12%
where the time goes in v28:
time: 50.4 us; the launch traced here: 50.1 us
  waiting for transfers between devices  21 us (42%)
  starting transfers between devices  10 us (20%)
  Pallas kernels  6.73 us (13%)
  matrix products  6.62 us (13%)
  local copies, waits for them, and re-layouts  3.68 us (7%)
  between operations  2.14 us (4%)
    ppermute x8, waiting for transfers between devices, shifted(): lax.ppermute(shard, axis, [(i, (i + by) % devices) for i in range(devices)])  21 us
    ppermute x8, starting transfers between devices, shifted(): lax.ppermute(shard, axis, [(i, (i + by) % devices) for i in range(devices)])  10 us
    dot_general x6, matrix products, dot_tn(): lax.dot_general(a, b, (((0,), (0,)), ((), ())), preferred_element_type=jn...  3.49 us
    pallas_call x4, Pallas kernels, add_rows(): pl.pallas_call(kernel, out_shape=(out, jax.ShapeDtypeStruct((8, 128), jnp...  3.34 us
    pallas_call x2, Pallas kernels, chunk(): pl.pallas_call(functools.partial(chunk_kernel, len(pieces), lasts), out_s...  2.91 us
    unnamed x8, local copies, waits for them, and re-layouts  2.66 us
    dot_general x2, matrix products, dot_nt(): lax.dot_general(a, b, (((1,), (1,)), ((), ())), preferred_element_type=jn...  1.72 us
    dot_general x2, matrix products, dot_nn(): return jnp.dot(a, b, preferred_element_type=jnp.float32)  1.42 us
  transfers between devices with their start and end apart: 8, of which 6 were waited for; matrix products, arithmetic and copies ran while one was open for 13% of the time, Pallas kernels for 12%

profile of v28, /device:TPU:0, one launch (start us, length us, event | category | flops | bytes accessed | tf_op | source)
XLA Modules:
  0.0 50.1 jit_solution(7719391412367112728)
XLA Ops:
  0.6 1.0 %slice.3.refs_0_ = bf16[160,1152]{1,0:T(8,128)(2,1)S(1)} slice(bf16[416,1152]{1,0:T(8,128)(2,1)} %array_ref.5), slice={[0:160], [0:1152]} | slice | bytes 737280 | tf_op jit(solution)/shard_map/slice | solution.py:155
  1.7 3.0 %collective-permute-start = (bf16[160,1152]{1,0:T(8,128)(2,1)S(1)}, bf16[160,1152]{1,0:T(8,128)(2,1)S(1)}, u32[]{:S(2)}, u32[]{:S(2)}) collective-permute-start(bf16[160,1152]{1,0:T(8,128)(2,1)S(1)} %slice.3.refs_0_), channel_id=1, source_target_pairs={{0,4},{4,8},{8,12},{12,16},{16,20},{20,24},{24,28},{28,0},{1,5},{5... | collective-permute-start | bytes 1105928 | tf_op jit(solution)/shard_map/ppermute | solution.py:20
  4.7 1.2 %copy-done = bf16[416,1152]{1,0:T(8,128)(2,1)S(1)} copy-done((bf16[416,1152]{1,0:T(8,128)(2,1)S(1)}, bf16[416,1152]{1,0:T(8,128)(2,1)}, u32[]{:S(2)}) %copy-start) | copy-done | bytes 958488
  5.8 0.3 fetch.4
  6.2 1.6 %collective-permute-start.2 = (bf16[208,1152]{1,0:T(8,128)(2,1)S(1)}, bf16[208,1152]{1,0:T(8,128)(2,1)S(1)}, u32[]{:S(2)}, u32[]{:S(2)}) collective-permute-start(bf16[208,1152]{1,0:T(8,128)(2,1)S(1)} %fetch.4), channel_id=1, source_target_pairs={{0,4},{4,8},{8,12},{12,16},{16,20},{20,24},{24,28},{28,0},{1,5},{5... | collective-permute-start | bytes 1437704 | tf_op jit(solution)/shard_map/ppermute | solution.py:20
  7.8 0.4 collective-permute-start.1
  9.5 7.7 %collective-permute-done.refs_0_ = bf16[160,1152]{1,0:T(8,128)(2,1)S(1)} collective-permute-done((bf16[160,1152]{1,0:T(8,128)(2,1)S(1)}, bf16[160,1152]{1,0:T(8,128)(2,1)S(1)}, u32[]{:S(2)}, u32[]{:S(2)}) %collective-permute-start) | collective-permute-done | bytes 368672 | tf_op jit(solution)/shard_map/ppermute | solution.py:20
  17.2 1.2 %copy-done.1 = bf16[416,1152]{1,0:T(8,128)(2,1)S(1)} copy-done((bf16[416,1152]{1,0:T(8,128)(2,1)S(1)}, bf16[416,1152]{1,0:T(8,128)(2,1)}, u32[]{:S(2)}) %copy-start.1) | copy-done | bytes 958488
  18.6 0.9 %fusion.17.refs_0_ = bf16[416,416]{1,0:T(8,128)(2,1)S(1)} fusion(bf16[416,1152]{1,0:T(8,128)(2,1)S(1)} %copy-done.2, bf16[416,1152]{1,0:T(8,128)(2,1)S(1)} %copy-done.1, s32[416]{0:T(512)S(1)} %bitcast.30, f32[]{:T(128)} %bitcast.28, f32[]{:T(128)} %bitcast.24), kind=kOutput, calls=%fused_computation.23 | convolution fusion | flops 400278528 | bytes 2264712 | tf_op jit(solution)/shard_map/dot_general | solution.py:24
  19.7 0.7 %fusion.19.refs_2_ = f32[416,1152]{1,0:T(8,128)S(1)} fusion(bf16[416,416]{1,0:T(8,128)(2,1)S(1)} %fusion.17.refs_0_, bf16[416,1152]{1,0:T(8,128)(2,1)S(1)} %copy-done.2), kind=kOutput, calls=%fused_computation.26 | convolution fusion | flops 398721024 | bytes 3221504 | tf_op jit(solution)/shard_map/dot_general | solution.py:28
  20.5 0.7 %fusion.18.refs_1_ = f32[416,1152]{1,0:T(8,128)S(1)} fusion(bf16[416,416]{1,0:T(8,128)(2,1)S(1)} %fusion.17.refs_0_, bf16[416,1152]{1,0:T(8,128)(2,1)S(1)} %copy-done.1), kind=kOutput, calls=%fused_computation.25 | convolution fusion | flops 398721024 | bytes 3221504 | tf_op jit(solution)/shard_map/dot_general | solution.py:32
  21.2 0.8 %fusion.16 = bf16[416,416]{1,0:T(8,128)(2,1)S(1)} fusion(bf16[416,1152]{1,0:T(8,128)(2,1)S(1)} %pass_on.7.next_ref, bf16[416,1152]{1,0:T(8,128)(2,1)S(1)} %copy-done.1, f32[]{:T(128)} %bitcast.29, f32[]{:T(128)} %bitcast.27), kind=kOutput, calls=%fused_computation.22 | convolution fusion | flops 399759360 | bytes 2263048 | tf_op jit(solution)/shard_map/dot_general | solution.py:24
  22.1 0.7 %fusion.20 = f32[416,1152]{1,0:T(8,128)S(1)} fusion(bf16[416,416]{1,0:T(8,128)(2,1)S(1)} %fusion.16, bf16[416,1152]{1,0:T(8,128)(2,1)S(1)} %copy-done.1), kind=kOutput, calls=%fused_computation.27 | convolution fusion | flops 398721024 | bytes 3221504 | tf_op jit(solution)/shard_map/dot_general | solution.py:32
  22.8 1.3 %chunk.2 = (bf16[160,1152]{1,0:T(8,128)(2,1)S(1)}, bf16[160,416]{1,0:T(8,128)(2,1)S(1)}, bf16[160,416]{1,0:T(8,128)(2,1)S(1)}, bf16[160,1152]{1,0:T(8,128)(2,1)S(1)}) custom-call(f32[1]{0:T(128)} %copy.23.scale_ref, f32[1]{0:T(128)} %copy.24.bias_ref, bf16[416,1152]{1,0:T(8,128)(2,1)S(1)} %copy-done.2, bf16[416,1152]{1,0:T(8,128)(2,1)S(1)} %pass_on.7.next_ref, ...), custom_call_target="tpu_custom_call" | custom-call | flops 613416960 | bytes 3022848 | tf_op jit(solution)/shard_map/chunk/pallas_call | solution.py:100
  24.1 0.5 convolution_add_fusion.1.refs_2_
  24.6 2.8 %collective-permute-done.2.refs_1_.refs_0_ = bf16[208,1152]{1,0:T(8,128)(2,1)S(1)} collective-permute-done((bf16[208,1152]{1,0:T(8,128)(2,1)S(1)}, bf16[208,1152]{1,0:T(8,128)(2,1)S(1)}, u32[]{:S(2)}, u32[]{:S(2)}) %collective-permute-start.2) | collective-permute-done | bytes 479264 | tf_op jit(solution)/shard_map/ppermute | solution.py:20
  27.4 2.1 %collective-permute-start.4 = (bf16[160,1152]{1,0:T(8,128)(2,1)S(1)}, bf16[160,1152]{1,0:T(8,128)(2,1)S(1)}, u32[]{:S(2)}, u32[]{:S(2)}) collective-permute-start(bf16[160,1152]{1,0:T(8,128)(2,1)S(1)} %pass_on.8.refs_2_), channel_id=1, source_target_pairs={{0,28},{4,0},{8,4},{12,8},{16,12},{20,16},{24,20},{28,24},{1,29},{... | collective-permute-start | bytes 1105928 | tf_op jit(solution)/shard_map/ppermute | solution.py:20
  29.4 1.6 %chunk.3 = (bf16[256,1152]{1,0:T(8,128)(2,1)S(1)}, bf16[256,416]{1,0:T(8,128)(2,1)S(1)}, bf16[256,416]{1,0:T(8,128)(2,1)S(1)}, bf16[208,1152]{1,0:T(8,128)(2,1)S(1)}, bf16[48,1152]{1,0:T(8,128)(2,1)S(1)}) custom-call(f32[1]{0:T(128)} %copy.23.scale_ref, f32[1]{0:T(128)} %copy.24.bias_ref, bf16[416,1152]{1,0:T(8,128)(2,1)S(1)} %copy-done.2, ...), custom_call_target="tpu_custom_call" | custom-call | flops 981467136 | bytes 3686400 | tf_op jit(solution)/shard_map/chunk/pallas_call | solution.py:100
  31.1 1.5 %collective-permute-start.7 = (bf16[208,1152]{1,0:T(8,128)(2,1)S(1)}, bf16[208,1152]{1,0:T(8,128)(2,1)S(1)}, u32[]{:S(2)}, u32[]{:S(2)}) collective-permute-start(bf16[208,1152]{1,0:T(8,128)(2,1)S(1)} %get-tuple-element.23.refs_1_), channel_id=1, source_target_pairs={{0,28},{4,0},{8,4},{12,8},{16,12},{20,16},{24,20},{28,24},{1,29},{... | collective-permute-start | bytes 1437704 | tf_op jit(solution)/shard_map/ppermute | solution.py:20
  32.6 0.5 fusion.4.refs_1_
  33.2 1.4 %collective-permute-start.6 = (bf16[48,1152]{1,0:T(8,128)(2,1)S(1)}, bf16[48,1152]{1,0:T(8,128)(2,1)S(1)}, u32[]{:S(2)}, u32[]{:S(2)}) collective-permute-start(bf16[48,1152]{1,0:T(8,128)(2,1)S(1)} %pass_on.11), channel_id=1, source_target_pairs={{0,28},{4,0},{8,4},{12,8},{16,12},{20,16},{24,20},{28,24},{1,29},{... | collective-permute-start | bytes 331784 | tf_op jit(solution)/shard_map/ppermute | solution.py:20
  34.5 0.8 %fusion.total_ref = f32[416,1152]{1,0:T(8,128)S(1)} fusion(f32[416,1152]{1,0:T(8,128)S(1)} %fusion.19.refs_2_, bf16[416,416]{1,0:T(8,128)(2,1)S(1)} %fusion.16, bf16[416,1152]{1,0:T(8,128)(2,1)S(1)} %pass_on.7.next_ref, f32[]{:T(128)} %bitcast.23), kind=kOutput, calls=%fused_computation.1 | convolution fusion | flops 399679488 | bytes 5138436 | tf_op jit(solution)/shard_map/dot_general | solution.py:28
  35.3 3.6 %collective-permute-done.4.back_ref = bf16[160,1152]{1,0:T(8,128)(2,1)S(1)} collective-permute-done((bf16[160,1152]{1,0:T(8,128)(2,1)S(1)}, bf16[160,1152]{1,0:T(8,128)(2,1)S(1)}, u32[]{:S(2)}, u32[]{:S(2)}) %collective-permute-start.4) | collective-permute-done | bytes 368672 | tf_op jit(solution)/shard_map/ppermute | solution.py:20
  38.9 0.8 %add_rows.4 = (bf16[416,1152]{1,0:T(8,128)(2,1)}, f32[8,128]{1,0:T(8,128)S(1)}) custom-call(f32[416,1152]{1,0:T(8,128)S(1)} %fusion.total_ref, bf16[160,1152]{1,0:T(8,128)(2,1)S(1)} %collective-permute-done.4.back_ref), custom_call_target="tpu_custom_call" | custom-call | tf_op jit(solution)/shard_map/add_rows/pallas_call | solution.py:139
  39.7 0.5 fusion.21
  40.2 0.5 fusion.2.total_ref
  40.7 5.7 %collective-permute-done.5.back_ref = bf16[416,1152]{1,0:T(8,128)(2,1)S(1)} collective-permute-done((bf16[416,1152]{1,0:T(8,128)(2,1)S(1)}, bf16[416,1152]{1,0:T(8,128)(2,1)S(1)}, u32[]{:S(2)}, u32[]{:S(2)}) %collective-permute-start.5) | collective-permute-done | bytes 958496 | tf_op jit(solution)/shard_map/ppermute | solution.py:20
  46.4 1.0 %add_rows.5 = (bf16[416,1152]{1,0:T(8,128)(2,1)}, f32[8,128]{1,0:T(8,128)S(1)}) custom-call(f32[416,1152]{1,0:T(8,128)S(1)} %fusion.2.total_ref, bf16[416,1152]{1,0:T(8,128)(2,1)S(1)} %collective-permute-done.5.back_ref), custom_call_target="tpu_custom_call" | custom-call | tf_op jit(solution)/shard_map/add_rows/pallas_call | solution.py:139
  47.4 0.9 %collective-permute-done.7.back_ref = bf16[208,1152]{1,0:T(8,128)(2,1)S(1)} collective-permute-done((bf16[208,1152]{1,0:T(8,128)(2,1)S(1)}, bf16[208,1152]{1,0:T(8,128)(2,1)S(1)}, u32[]{:S(2)}, u32[]{:S(2)}) %collective-permute-start.7) | collective-permute-done | bytes 479264 | tf_op jit(solution)/shard_map/ppermute | solution.py:20
  48.3 0.8 %add_rows.6.refs_0_ = bf16[416,1152]{1,0:T(8,128)(2,1)} custom-call(f32[416,1152]{1,0:T(8,128)S(1)} %fusion.total_ref, bf16[208,1152]{1,0:T(8,128)(2,1)S(1)} %collective-permute-done.7.back_ref, bf16[416,1152]{1,0:T(8,128)(2,1)} %get-tuple-element.26.refs_0_, f32[8,128]{1,0:T(8,128)S(1)} %get-tuple-element.27.refs_1_), custom_call_target="tpu_custom_call", output_to_operand_aliasing={{}: (2, {})} | custom-call | tf_op jit(solution)/shard_map/add_rows/pallas_call | solution.py:139
  49.1 0.3 collective-permute-done.6.back_ref
  49.5 0.7 %add_rows.7 = bf16[416,1152]{1,0:T(8,128)(2,1)} custom-call(f32[416,1152]{1,0:T(8,128)S(1)} %fusion.total_ref, bf16[48,1152]{1,0:T(8,128)(2,1)S(1)} %collective-permute-done.6.back_ref, bf16[416,1152]{1,0:T(8,128)(2,1)} %add_rows.6.refs_0_), custom_call_target="tpu_custom_call", output_to_operand_aliasing={{}: (2, {})} | custom-call | tf_op jit(solution)/shard_map/add_rows/pallas_call | solution.py:139
  (18 shorter events, 0.6 us)
Async XLA Ops:
  0.6 16.5 %copy-start.3 = (s32[1,416]{1,0:T(1,128)S(1)}, s32[1,416]{1,0:T(1,128)}, u32[]{:S(2)}) copy-start(s32[1,416]{1,0:T(1,128)} %array_ref.3) | copy-start | bytes 4996
  1.7 15.4 %collective-permute-start = (bf16[160,1152]{1,0:T(8,128)(2,1)S(1)}, bf16[160,1152]{1,0:T(8,128)(2,1)S(1)}, u32[]{:S(2)}, u32[]{:S(2)}) collective-permute-start(bf16[160,1152]{1,0:T(8,128)(2,1)S(1)} %slice.3.refs_0_), channel_id=1, source_target_pairs={{0,4},{4,8},{8,12},{12,16},{16,20},{20,24},{24,28},{28,0},{1,5},{5... | collective-permute-start | bytes 1105928 | tf_op jit(solution)/shard_map/ppermute | solution.py:20
  4.7 1.2 %copy-start = (bf16[416,1152]{1,0:T(8,128)(2,1)S(1)}, bf16[416,1152]{1,0:T(8,128)(2,1)}, u32[]{:S(2)}) copy-start(bf16[416,1152]{1,0:T(8,128)(2,1)} %array_ref.5) | copy-start | bytes 2875396
  6.2 21.2 %collective-permute-start.2 = (bf16[208,1152]{1,0:T(8,128)(2,1)S(1)}, bf16[208,1152]{1,0:T(8,128)(2,1)S(1)}, u32[]{:S(2)}, u32[]{:S(2)}) collective-permute-start(bf16[208,1152]{1,0:T(8,128)(2,1)S(1)} %fetch.4), channel_id=1, source_target_pairs={{0,4},{4,8},{8,12},{12,16},{16,20},{20,24},{24,28},{28,0},{1,5},{5... | collective-permute-start | bytes 1437704 | tf_op jit(solution)/shard_map/ppermute | solution.py:20
  7.8 13.4 %collective-permute-start.1 = (bf16[416,1152]{1,0:T(8,128)(2,1)}, bf16[416,1152]{1,0:T(8,128)(2,1)S(1)}, u32[]{:S(2)}, u32[]{:S(2)}) collective-permute-start(bf16[416,1152]{1,0:T(8,128)(2,1)} %image_ref.3), channel_id=1, source_target_pairs={{0,3},{1,0},{2,1},{3,2},{4,7},{5,4},{6,5},{7,6},{8,11},{9,8},{10,9... | collective-permute-start | bytes 2875400 | tf_op jit(solution)/shard_map/ppermute | solution.py:20
  17.1 1.2 %copy-start.1 = (bf16[416,1152]{1,0:T(8,128)(2,1)S(1)}, bf16[416,1152]{1,0:T(8,128)(2,1)}, u32[]{:S(2)}) copy-start(bf16[416,1152]{1,0:T(8,128)(2,1)} %array_ref.5) | copy-start | bytes 2875396
  17.1 1.5 %copy-start.2 = (bf16[416,1152]{1,0:T(8,128)(2,1)S(1)}, bf16[416,1152]{1,0:T(8,128)(2,1)}, u32[]{:S(2)}) copy-start(bf16[416,1152]{1,0:T(8,128)(2,1)} %image_ref.3) | copy-start | bytes 2875396
  19.7 9.8 %collective-permute-start.3 = (bf16[48,1152]{1,0:T(8,128)(2,1)S(1)}, bf16[48,1152]{1,0:T(8,128)(2,1)S(1)}, u32[]{:S(2)}, u32[]{:S(2)}) collective-permute-start(bf16[48,1152]{1,0:T(8,128)(2,1)S(1)} %fetch.5), channel_id=1, source_target_pairs={{0,4},{4,8},{8,12},{12,16},{16,20},{20,24},{24,28},{28,0},{1,5},{5... | collective-permute-start | bytes 331784 | tf_op jit(solution)/shard_map/ppermute | solution.py:20
  27.4 11.5 %collective-permute-start.4 = (bf16[160,1152]{1,0:T(8,128)(2,1)S(1)}, bf16[160,1152]{1,0:T(8,128)(2,1)S(1)}, u32[]{:S(2)}, u32[]{:S(2)}) collective-permute-start(bf16[160,1152]{1,0:T(8,128)(2,1)S(1)} %pass_on.8.refs_2_), channel_id=1, source_target_pairs={{0,28},{4,0},{8,4},{12,8},{16,12},{20,16},{24,20},{28,24},{1,29},{... | collective-permute-start | bytes 1105928 | tf_op jit(solution)/shard_map/ppermute | solution.py:20
  31.1 17.2 %collective-permute-start.7 = (bf16[208,1152]{1,0:T(8,128)(2,1)S(1)}, bf16[208,1152]{1,0:T(8,128)(2,1)S(1)}, u32[]{:S(2)}, u32[]{:S(2)}) collective-permute-start(bf16[208,1152]{1,0:T(8,128)(2,1)S(1)} %get-tuple-element.23.refs_1_), channel_id=1, source_target_pairs={{0,28},{4,0},{8,4},{12,8},{16,12},{20,16},{24,20},{28,24},{1,29},{... | collective-permute-start | bytes 1437704 | tf_op jit(solution)/shard_map/ppermute | solution.py:20
  33.1 13.3 %collective-permute-start.5 = (bf16[416,1152]{1,0:T(8,128)(2,1)S(1)}, bf16[416,1152]{1,0:T(8,128)(2,1)S(1)}, u32[]{:S(2)}, u32[]{:S(2)}) collective-permute-start(bf16[416,1152]{1,0:T(8,128)(2,1)S(1)} %fusion.4.refs_1_), channel_id=1, source_target_pairs={{0,1},{1,2},{2,3},{3,0},{4,5},{5,6},{6,7},{7,4},{8,9},{9,10},{10,1... | collective-permute-start | bytes 2875400 | tf_op jit(solution)/shard_map/ppermute | solution.py:20
  33.2 16.3 %collective-permute-start.6 = (bf16[48,1152]{1,0:T(8,128)(2,1)S(1)}, bf16[48,1152]{1,0:T(8,128)(2,1)S(1)}, u32[]{:S(2)}, u32[]{:S(2)}) collective-permute-start(bf16[48,1152]{1,0:T(8,128)(2,1)S(1)} %pass_on.11), channel_id=1, source_target_pairs={{0,28},{4,0},{8,4},{12,8},{16,12},{20,16},{24,20},{28,24},{1,29},{... | collective-permute-start | bytes 331784 | tf_op jit(solution)/shard_map/ppermute | solution.py:20

commit v29 on v26

--- a/solution.py
+++ b/solution.py
@@ -157,7 +157,7 @@
     image_next = shifted(image, "grp", -1)
     part.append(shifted(fetch(text, *cuts[1], [first]), "blk", 1))
 
-    target = pass_on(fetch(target, 0, 1, [part[0]]), [], 2 * 10**10)
+    target = fetch(target, 0, 1, [part[0]])
     own = jax.nn.sigmoid(dot_nt(image, text) * scale + bias)
     column = lax.broadcasted_iota(jnp.int32, own.shape, 1)
     own = (own - (column == target[0][:, None]).astype(jnp.float32)).astype(jnp.bfloat16)

time: 50.3 us -> 50.3 us (level)
  local copies, waits for them, and re-layouts: 3.65 us -> 2.2 us
  waiting for transfers between devices: 20.7 us -> 21.9 us
    unnamed x8, local copies, waits for them, and re-layouts: 2.66 us -> 1.2 us
    ppermute x8, waiting for transfers between devices: 20.7 us -> 21.9 us  [shifted(): lax.ppermute(shard, axis, [(i, (i + by) % devices) for i in range(devices)])]
where the time goes in v29:
time: 50.3 us; the launch traced here: 50.1 us
  waiting for transfers between devices  21.9 us (44%)
  starting transfers between devices  10.3 us (20%)
  matrix products  6.93 us (14%)
  Pallas kernels  6.65 us (13%)
  local copies, waits for them, and re-layouts  2.2 us (4%)
  between operations  2.14 us (4%)
    ppermute x8, waiting for transfers between devices, shifted(): lax.ppermute(shard, axis, [(i, (i + by) % devices) for i in range(devices)])  21.9 us
    ppermute x8, starting transfers between devices, shifted(): lax.ppermute(shard, axis, [(i, (i + by) % devices) for i in range(devices)])  10.3 us
    dot_general x6, matrix products, dot_tn(): lax.dot_general(a, b, (((0,), (0,)), ((), ())), preferred_element_type=jn...  3.81 us
    pallas_call x4, Pallas kernels, add_rows(): pl.pallas_call(kernel, out_shape=(out, jax.ShapeDtypeStruct((8, 128), jnp...  3.31 us
    pallas_call x2, Pallas kernels, chunk(): pl.pallas_call(functools.partial(chunk_kernel, len(pieces), lasts), out_s...  3.08 us
    dot_general x2, matrix products, dot_nt(): lax.dot_general(a, b, (((1,), (1,)), ((), ())), preferred_element_type=jn...  1.72 us
    dot_general x2, matrix products, dot_nn(): return jnp.dot(a, b, preferred_element_type=jnp.float32)  1.4 us
    unnamed x8, local copies, waits for them, and re-layouts  1.2 us
  transfers between devices with their start and end apart: 8, of which 6 were waited for; matrix products, arithmetic and copies ran while one was open for 14% of the time, Pallas kernels for 12%

profile of v29, /device:TPU:0, one launch (start us, length us, event | category | flops | bytes accessed | tf_op | source)
XLA Modules:
  0.0 50.1 jit_solution(9191732524960997268)
XLA Ops:
  0.6 1.0 %slice.3.refs_0_ = bf16[128,1152]{1,0:T(8,128)(2,1)S(1)} slice(bf16[416,1152]{1,0:T(8,128)(2,1)} %array_ref.5), slice={[0:128], [0:1152]} | slice | bytes 589824 | tf_op jit(solution)/shard_map/slice | solution.py:155
  1.6 3.0 %collective-permute-start = (bf16[128,1152]{1,0:T(8,128)(2,1)S(1)}, bf16[128,1152]{1,0:T(8,128)(2,1)S(1)}, u32[]{:S(2)}, u32[]{:S(2)}) collective-permute-start(bf16[128,1152]{1,0:T(8,128)(2,1)S(1)} %slice.3.refs_0_), channel_id=1, source_target_pairs={{0,4},{4,8},{8,12},{12,16},{16,20},{20,24},{24,28},{28,0},{1,5},{5... | collective-permute-start | bytes 884744 | tf_op jit(solution)/shard_map/ppermute | solution.py:20
  4.6 0.7 %collective-permute-start.1 = (bf16[416,1152]{1,0:T(8,128)(2,1)}, bf16[416,1152]{1,0:T(8,128)(2,1)S(1)}, u32[]{:S(2)}, u32[]{:S(2)}) collective-permute-start(bf16[416,1152]{1,0:T(8,128)(2,1)} %image_ref.3), channel_id=1, source_target_pairs={{0,3},{1,0},{2,1},{3,2},{4,7},{5,4},{6,5},{7,6},{8,11},{9,8},{10,9... | collective-permute-start | bytes 2875400 | tf_op jit(solution)/shard_map/ppermute | solution.py:20
  5.3 1.2 %copy-done = bf16[416,1152]{1,0:T(8,128)(2,1)S(1)} copy-done((bf16[416,1152]{1,0:T(8,128)(2,1)S(1)}, bf16[416,1152]{1,0:T(8,128)(2,1)}, u32[]{:S(2)}) %copy-start) | copy-done | bytes 958488
  6.5 0.1 fetch.4
  6.6 1.6 %collective-permute-start.2 = (bf16[240,1152]{1,0:T(8,128)(2,1)S(1)}, bf16[240,1152]{1,0:T(8,128)(2,1)S(1)}, u32[]{:S(2)}, u32[]{:S(2)}) collective-permute-start(bf16[240,1152]{1,0:T(8,128)(2,1)S(1)} %fetch.4), channel_id=1, source_target_pairs={{0,4},{4,8},{8,12},{12,16},{16,20},{20,24},{24,28},{28,0},{1,5},{5... | collective-permute-start | bytes 1658888 | tf_op jit(solution)/shard_map/ppermute | solution.py:20
  9.5 6.0 %collective-permute-done.refs_0_ = bf16[128,1152]{1,0:T(8,128)(2,1)S(1)} collective-permute-done((bf16[128,1152]{1,0:T(8,128)(2,1)S(1)}, bf16[128,1152]{1,0:T(8,128)(2,1)S(1)}, u32[]{:S(2)}, u32[]{:S(2)}) %collective-permute-start) | collective-permute-done | bytes 294944 | tf_op jit(solution)/shard_map/ppermute | solution.py:20
  15.5 0.9 %subtract_convert_fusion.refs_0_ = bf16[416,416]{1,0:T(8,128)(2,1)S(1)} fusion(s32[416]{0:T(512)S(1)} %bitcast.30, f32[]{:T(128)} %bitcast.28, bf16[416,1152]{1,0:T(8,128)(2,1)S(1)} %copy-done.2, bf16[416,1152]{1,0:T(8,128)(2,1)S(1)} %copy-done.1, f32[]{:T(128)} %bitcast.24), kind=kOutput, calls=%fused_computation.22 | convolution fusion | flops 400278528 | bytes 2264712 | tf_op jit(solution)/shard_map/dot_general | solution.py:24
  16.4 0.2 fetch.5
  16.7 0.7 %fusion.17.refs_2_ = f32[416,1152]{1,0:T(8,128)S(1)} fusion(bf16[416,416]{1,0:T(8,128)(2,1)S(1)} %subtract_convert_fusion.refs_0_, bf16[416,1152]{1,0:T(8,128)(2,1)S(1)} %copy-done.2), kind=kOutput, calls=%fused_computation.25 | convolution fusion | flops 398721024 | bytes 3221504 | tf_op jit(solution)/shard_map/dot_general | solution.py:28
  17.4 0.7 %fusion.16.refs_1_ = f32[416,1152]{1,0:T(8,128)S(1)} fusion(bf16[416,416]{1,0:T(8,128)(2,1)S(1)} %subtract_convert_fusion.refs_0_, bf16[416,1152]{1,0:T(8,128)(2,1)S(1)} %copy-done.1), kind=kOutput, calls=%fused_computation.24 | convolution fusion | flops 398721024 | bytes 3221504 | tf_op jit(solution)/shard_map/dot_general | solution.py:32
  18.1 0.8 %fusion.15 = bf16[416,416]{1,0:T(8,128)(2,1)S(1)} fusion(bf16[416,1152]{1,0:T(8,128)(2,1)S(1)} %pass_on.5.next_ref, bf16[416,1152]{1,0:T(8,128)(2,1)S(1)} %copy-done.1, f32[]{:T(128)} %bitcast.29, f32[]{:T(128)} %bitcast.27), kind=kOutput, calls=%fused_computation.21 | convolution fusion | flops 399759360 | bytes 2263048 | tf_op jit(solution)/shard_map/dot_general | solution.py:24
  19.0 1.2 %chunk.2 = (bf16[128,1152]{1,0:T(8,128)(2,1)S(1)}, bf16[128,416]{1,0:T(8,128)(2,1)S(1)}, bf16[128,416]{1,0:T(8,128)(2,1)S(1)}, bf16[128,1152]{1,0:T(8,128)(2,1)S(1)}) custom-call(f32[1]{0:T(128)} %copy.21.scale_ref, f32[1]{0:T(128)} %copy.22.bias_ref, bf16[416,1152]{1,0:T(8,128)(2,1)S(1)} %copy-done.2, bf16[416,1152]{1,0:T(8,128)(2,1)S(1)} %pass_on.5.next_ref, ...), custom_call_target="tpu_custom_call" | custom-call | flops 490733568 | bytes 2801664 | tf_op jit(solution)/shard_map/chunk/pallas_call | solution.py:100
  20.2 0.7 %fusion.18 = f32[416,1152]{1,0:T(8,128)S(1)} fusion(bf16[416,416]{1,0:T(8,128)(2,1)S(1)} %fusion.15, bf16[416,1152]{1,0:T(8,128)(2,1)S(1)} %copy-done.1), kind=kOutput, calls=%fused_computation.26 | convolution fusion | flops 398721024 | bytes 3221504 | tf_op jit(solution)/shard_map/dot_general | solution.py:32
  20.9 0.4 convolution_add_fusion.1.refs_2_
  21.4 6.0 %collective-permute-done.2.refs_1_.refs_0_ = bf16[240,1152]{1,0:T(8,128)(2,1)S(1)} collective-permute-done((bf16[240,1152]{1,0:T(8,128)(2,1)S(1)}, bf16[240,1152]{1,0:T(8,128)(2,1)S(1)}, u32[]{:S(2)}, u32[]{:S(2)}) %collective-permute-start.2) | collective-permute-done | bytes 552992 | tf_op jit(solution)/shard_map/ppermute | solution.py:20
  27.4 2.1 %collective-permute-start.4 = (bf16[128,1152]{1,0:T(8,128)(2,1)S(1)}, bf16[128,1152]{1,0:T(8,128)(2,1)S(1)}, u32[]{:S(2)}, u32[]{:S(2)}) collective-permute-start(bf16[128,1152]{1,0:T(8,128)(2,1)S(1)} %pass_on.6.refs_2_), channel_id=1, source_target_pairs={{0,28},{4,0},{8,4},{12,8},{16,12},{20,16},{24,20},{28,24},{1,29},{... | collective-permute-start | bytes 884744 | tf_op jit(solution)/shard_map/ppermute | solution.py:20
  29.4 1.9 %chunk.3 = (bf16[288,1152]{1,0:T(8,128)(2,1)S(1)}, bf16[288,416]{1,0:T(8,128)(2,1)S(1)}, bf16[288,416]{1,0:T(8,128)(2,1)S(1)}, bf16[240,1152]{1,0:T(8,128)(2,1)S(1)}, bf16[48,1152]{1,0:T(8,128)(2,1)S(1)}) custom-call(f32[1]{0:T(128)} %copy.21.scale_ref, f32[1]{0:T(128)} %copy.22.bias_ref, bf16[416,1152]{1,0:T(8,128)(2,1)S(1)} %copy-done.2, ...), custom_call_target="tpu_custom_call" | custom-call | flops 1104150528 | bytes 3907584 | tf_op jit(solution)/shard_map/chunk/pallas_call | solution.py:100
  31.3 1.5 %collective-permute-start.7 = (bf16[240,1152]{1,0:T(8,128)(2,1)S(1)}, bf16[240,1152]{1,0:T(8,128)(2,1)S(1)}, u32[]{:S(2)}, u32[]{:S(2)}) collective-permute-start(bf16[240,1152]{1,0:T(8,128)(2,1)S(1)} %get-tuple-element.23.refs_1_), channel_id=1, source_target_pairs={{0,28},{4,0},{8,4},{12,8},{16,12},{20,16},{24,20},{28,24},{1,29},{... | collective-permute-start | bytes 1658888 | tf_op jit(solution)/shard_map/ppermute | solution.py:20
  32.8 0.7 %fusion.4.refs_1_ = bf16[416,1152]{1,0:T(8,128)(2,1)S(1)} fusion(f32[416,1152]{1,0:T(8,128)S(1)} %convolution_add_fusion.1.refs_2_, bf16[288,416]{1,0:T(8,128)(2,1)S(1)} %pass_on.8, bf16[288,1152]{1,0:T(8,128)(2,1)S(1)} %get-tuple-element.21, f32[]{:T(128)} %bitcast.25), kind=kOutput, calls=%fused_computation.8 | convolution fusion | flops 277475328 | bytes 3778564 | tf_op jit(solution)/shard_map/dot_general | solution.py:28
  33.6 1.4 %collective-permute-start.6 = (bf16[48,1152]{1,0:T(8,128)(2,1)S(1)}, bf16[48,1152]{1,0:T(8,128)(2,1)S(1)}, u32[]{:S(2)}, u32[]{:S(2)}) collective-permute-start(bf16[48,1152]{1,0:T(8,128)(2,1)S(1)} %pass_on.9), channel_id=1, source_target_pairs={{0,28},{4,0},{8,4},{12,8},{16,12},{20,16},{24,20},{28,24},{1,29},{... | collective-permute-start | bytes 331784 | tf_op jit(solution)/shard_map/ppermute | solution.py:20
  34.9 0.7 %fusion.total_ref = f32[416,1152]{1,0:T(8,128)S(1)} fusion(f32[416,1152]{1,0:T(8,128)S(1)} %fusion.17.refs_2_, bf16[416,416]{1,0:T(8,128)(2,1)S(1)} %fusion.15, bf16[416,1152]{1,0:T(8,128)(2,1)S(1)} %pass_on.5.next_ref, f32[]{:T(128)} %bitcast.23), kind=kOutput, calls=%fused_computation.1 | convolution fusion | flops 399679488 | bytes 5138436 | tf_op jit(solution)/shard_map/dot_general | solution.py:28
  35.7 1.6 %collective-permute-done.4.back_ref = bf16[128,1152]{1,0:T(8,128)(2,1)S(1)} collective-permute-done((bf16[128,1152]{1,0:T(8,128)(2,1)S(1)}, bf16[128,1152]{1,0:T(8,128)(2,1)S(1)}, u32[]{:S(2)}, u32[]{:S(2)}) %collective-permute-start.4) | collective-permute-done | bytes 294944 | tf_op jit(solution)/shard_map/ppermute | solution.py:20
  37.3 0.8 %add_rows.4 = (bf16[416,1152]{1,0:T(8,128)(2,1)}, f32[8,128]{1,0:T(8,128)S(1)}) custom-call(f32[416,1152]{1,0:T(8,128)S(1)} %fusion.total_ref, bf16[128,1152]{1,0:T(8,128)(2,1)S(1)} %collective-permute-done.4.back_ref), custom_call_target="tpu_custom_call" | custom-call | tf_op jit(solution)/shard_map/add_rows/pallas_call | solution.py:139
  38.1 0.7 %fusion.19 = f32[416,1152]{1,0:T(8,128)S(1)} fusion(bf16[288,416]{1,0:T(8,128)(2,1)S(1)} %pass_on.7, bf16[288,1152]{1,0:T(8,128)(2,1)S(1)} %get-tuple-element.21), kind=kOutput, calls=%fused_computation.27 | convolution fusion | flops 276037632 | bytes 2820096 | tf_op jit(solution)/shard_map/dot_general | solution.py:28
  38.8 0.4 fusion.2.total_ref
  39.2 7.6 %collective-permute-done.5.back_ref = bf16[416,1152]{1,0:T(8,128)(2,1)S(1)} collective-permute-done((bf16[416,1152]{1,0:T(8,128)(2,1)S(1)}, bf16[416,1152]{1,0:T(8,128)(2,1)S(1)}, u32[]{:S(2)}, u32[]{:S(2)}) %collective-permute-start.5) | collective-permute-done | bytes 958496 | tf_op jit(solution)/shard_map/ppermute | solution.py:20
  46.8 1.0 %add_rows.5 = (bf16[416,1152]{1,0:T(8,128)(2,1)}, f32[8,128]{1,0:T(8,128)S(1)}) custom-call(f32[416,1152]{1,0:T(8,128)S(1)} %fusion.2.total_ref, bf16[416,1152]{1,0:T(8,128)(2,1)S(1)} %collective-permute-done.5.back_ref), custom_call_target="tpu_custom_call" | custom-call | tf_op jit(solution)/shard_map/add_rows/pallas_call | solution.py:139
  47.8 0.4 collective-permute-done.7.back_ref
  48.2 0.9 %add_rows.6.refs_0_ = bf16[416,1152]{1,0:T(8,128)(2,1)} custom-call(f32[416,1152]{1,0:T(8,128)S(1)} %fusion.total_ref, bf16[240,1152]{1,0:T(8,128)(2,1)S(1)} %collective-permute-done.7.back_ref, bf16[416,1152]{1,0:T(8,128)(2,1)} %get-tuple-element.26.refs_0_, f32[8,128]{1,0:T(8,128)S(1)} %get-tuple-element.27.refs_1_), custom_call_target="tpu_custom_call", output_to_operand_aliasing={{}: (2, {})} | custom-call | tf_op jit(solution)/shard_map/add_rows/pallas_call | solution.py:139
  49.1 0.3 collective-permute-done.6.back_ref
  49.4 0.7 %add_rows.7 = bf16[416,1152]{1,0:T(8,128)(2,1)} custom-call(f32[416,1152]{1,0:T(8,128)S(1)} %fusion.total_ref, bf16[48,1152]{1,0:T(8,128)(2,1)S(1)} %collective-permute-done.6.back_ref, bf16[416,1152]{1,0:T(8,128)(2,1)} %add_rows.6.refs_0_), custom_call_target="tpu_custom_call", output_to_operand_aliasing={{}: (2, {})} | custom-call | tf_op jit(solution)/shard_map/add_rows/pallas_call | solution.py:139
  (17 shorter events, 0.2 us)
Async XLA Ops:
  0.6 14.9 %copy-start.3 = (s32[1,416]{1,0:T(1,128)S(1)}, s32[1,416]{1,0:T(1,128)}, u32[]{:S(2)}) copy-start(s32[1,416]{1,0:T(1,128)} %array_ref.3) | copy-start | bytes 4996
  1.6 13.9 %collective-permute-start = (bf16[128,1152]{1,0:T(8,128)(2,1)S(1)}, bf16[128,1152]{1,0:T(8,128)(2,1)S(1)}, u32[]{:S(2)}, u32[]{:S(2)}) collective-permute-start(bf16[128,1152]{1,0:T(8,128)(2,1)S(1)} %slice.3.refs_0_), channel_id=1, source_target_pairs={{0,4},{4,8},{8,12},{12,16},{16,20},{20,24},{24,28},{28,0},{1,5},{5... | collective-permute-start | bytes 884744 | tf_op jit(solution)/shard_map/ppermute | solution.py:20
  4.6 13.5 %collective-permute-start.1 = (bf16[416,1152]{1,0:T(8,128)(2,1)}, bf16[416,1152]{1,0:T(8,128)(2,1)S(1)}, u32[]{:S(2)}, u32[]{:S(2)}) collective-permute-start(bf16[416,1152]{1,0:T(8,128)(2,1)} %image_ref.3), channel_id=1, source_target_pairs={{0,3},{1,0},{2,1},{3,2},{4,7},{5,4},{6,5},{7,6},{8,11},{9,8},{10,9... | collective-permute-start | bytes 2875400 | tf_op jit(solution)/shard_map/ppermute | solution.py:20
  5.3 1.2 %copy-start = (bf16[416,1152]{1,0:T(8,128)(2,1)S(1)}, bf16[416,1152]{1,0:T(8,128)(2,1)}, u32[]{:S(2)}) copy-start(bf16[416,1152]{1,0:T(8,128)(2,1)} %array_ref.5) | copy-start | bytes 2875396
  6.5 9.0 %copy-start.1 = (bf16[416,1152]{1,0:T(8,128)(2,1)S(1)}, bf16[416,1152]{1,0:T(8,128)(2,1)}, u32[]{:S(2)}) copy-start(bf16[416,1152]{1,0:T(8,128)(2,1)} %array_ref.5) | copy-start | bytes 2875396
  6.5 9.0 %copy-start.2 = (bf16[416,1152]{1,0:T(8,128)(2,1)S(1)}, bf16[416,1152]{1,0:T(8,128)(2,1)}, u32[]{:S(2)}) copy-start(bf16[416,1152]{1,0:T(8,128)(2,1)} %image_ref.3) | copy-start | bytes 2875396
  6.6 20.8 %collective-permute-start.2 = (bf16[240,1152]{1,0:T(8,128)(2,1)S(1)}, bf16[240,1152]{1,0:T(8,128)(2,1)S(1)}, u32[]{:S(2)}, u32[]{:S(2)}) collective-permute-start(bf16[240,1152]{1,0:T(8,128)(2,1)S(1)} %fetch.4), channel_id=1, source_target_pairs={{0,4},{4,8},{8,12},{12,16},{16,20},{20,24},{24,28},{28,0},{1,5},{5... | collective-permute-start | bytes 1658888 | tf_op jit(solution)/shard_map/ppermute | solution.py:20
  16.6 12.8 %collective-permute-start.3 = (bf16[48,1152]{1,0:T(8,128)(2,1)S(1)}, bf16[48,1152]{1,0:T(8,128)(2,1)S(1)}, u32[]{:S(2)}, u32[]{:S(2)}) collective-permute-start(bf16[48,1152]{1,0:T(8,128)(2,1)S(1)} %fetch.5), channel_id=1, source_target_pairs={{0,4},{4,8},{8,12},{12,16},{16,20},{20,24},{24,28},{28,0},{1,5},{5... | collective-permute-start | bytes 331784 | tf_op jit(solution)/shard_map/ppermute | solution.py:20
  27.4 9.9 %collective-permute-start.4 = (bf16[128,1152]{1,0:T(8,128)(2,1)S(1)}, bf16[128,1152]{1,0:T(8,128)(2,1)S(1)}, u32[]{:S(2)}, u32[]{:S(2)}) collective-permute-start(bf16[128,1152]{1,0:T(8,128)(2,1)S(1)} %pass_on.6.refs_2_), channel_id=1, source_target_pairs={{0,28},{4,0},{8,4},{12,8},{16,12},{20,16},{24,20},{28,24},{1,29},{... | collective-permute-start | bytes 884744 | tf_op jit(solution)/shard_map/ppermute | solution.py:20
  31.3 17.0 %collective-permute-start.7 = (bf16[240,1152]{1,0:T(8,128)(2,1)S(1)}, bf16[240,1152]{1,0:T(8,128)(2,1)S(1)}, u32[]{:S(2)}, u32[]{:S(2)}) collective-permute-start(bf16[240,1152]{1,0:T(8,128)(2,1)S(1)} %get-tuple-element.23.refs_1_), channel_id=1, source_target_pairs={{0,28},{4,0},{8,4},{12,8},{16,12},{20,16},{24,20},{28,24},{1,29},{... | collective-permute-start | bytes 1658888 | tf_op jit(solution)/shard_map/ppermute | solution.py:20
  33.5 13.3 %collective-permute-start.5 = (bf16[416,1152]{1,0:T(8,128)(2,1)S(1)}, bf16[416,1152]{1,0:T(8,128)(2,1)S(1)}, u32[]{:S(2)}, u32[]{:S(2)}) collective-permute-start(bf16[416,1152]{1,0:T(8,128)(2,1)S(1)} %fusion.4.refs_1_), channel_id=1, source_target_pairs={{0,1},{1,2},{2,3},{3,0},{4,5},{5,6},{6,7},{7,4},{8,9},{9,10},{10,1... | collective-permute-start | bytes 2875400 | tf_op jit(solution)/shard_map/ppermute | solution.py:20
  33.6 15.9 %collective-permute-start.6 = (bf16[48,1152]{1,0:T(8,128)(2,1)S(1)}, bf16[48,1152]{1,0:T(8,128)(2,1)S(1)}, u32[]{:S(2)}, u32[]{:S(2)}) collective-permute-start(bf16[48,1152]{1,0:T(8,128)(2,1)S(1)} %pass_on.9), channel_id=1, source_target_pairs={{0,28},{4,0},{8,4},{12,8},{16,12},{20,16},{24,20},{28,24},{1,29},{... | collective-permute-start | bytes 331784 | tf_op jit(solution)/shard_map/ppermute | solution.py:20

commit v30 on v26

--- a/solution.py
+++ b/solution.py
@@ -175,7 +175,7 @@
     sent0 = pass_on(sent0, [part[1], image_sent])
     back0 = shifted(sent0, "blk", -1)
 
-    lasts = part[2].shape[0]
+    lasts = part[2].shape[0] + 32
     part1, own1, next1, sent1, sent2 = chunk(factor, shift, image, image_next, part[1:], [sent0], lasts)
     back1 = shifted(sent1, "blk", -1)
     next1 = pass_on(next1, [sent1], 2 * 10**10)
@@ -187,7 +187,7 @@
     image_grad = scale * (image_grad + dot_tn(own1, part1))
     image_grad, mark = add_rows(image_grad, image_back, 0, None, [], mark=True)
     result = add_rows(text_grad, back1, cuts[1][0], result, [mark])
-    result = add_rows(text_grad, back2, cuts[2][0], result, [])
+    result = add_rows(text_grad, back2, text.shape[0] - lasts, result, [])
     return image_grad, result
 
 

time: 50.3 us -> 50.4 us (level)
  transfers between devices with their start and end apart: 8 -> 8, of which waited for: 6 -> 5; matrix products, arithmetic and copies ran while one was open for 14% -> 14% of each run, Pallas kernels for 12% -> 12%
where the time goes in v30:
time: 50.4 us; the launch traced here: 50.2 us
  waiting for transfers between devices  20.7 us (41%)
  starting transfers between devices  10 us (20%)
  matrix products  6.93 us (14%)
  Pallas kernels  6.67 us (13%)
  local copies, waits for them, and re-layouts  3.65 us (7%)
  between operations  2.15 us (4%)
    ppermute x8, waiting for transfers between devices, shifted(): lax.ppermute(shard, axis, [(i, (i + by) % devices) for i in range(devices)])  20.7 us
    ppermute x8, starting transfers between devices, shifted(): lax.ppermute(shard, axis, [(i, (i + by) % devices) for i in range(devices)])  10 us
    dot_general x6, matrix products, dot_tn(): lax.dot_general(a, b, (((0,), (0,)), ((), ())), preferred_element_type=jn...  3.81 us
    pallas_call x4, Pallas kernels, add_rows(): pl.pallas_call(kernel, out_shape=(out, jax.ShapeDtypeStruct((8, 128), jnp...  3.33 us
    pallas_call x2, Pallas kernels, chunk(): pl.pallas_call(functools.partial(chunk_kernel, len(pieces), lasts), out_s...  3.08 us
    unnamed x8, local copies, waits for them, and re-layouts  2.66 us
    dot_general x2, matrix products, dot_nt(): lax.dot_general(a, b, (((1,), (1,)), ((), ())), preferred_element_type=jn...  1.72 us
    dot_general x2, matrix products, dot_nn(): return jnp.dot(a, b, preferred_element_type=jnp.float32)  1.4 us
  transfers between devices with their start and end apart: 8, of which 5 were waited for; matrix products, arithmetic and copies ran while one was open for 14% of the time, Pallas kernels for 12%

profile of v30, /device:TPU:0, one launch (start us, length us, event | category | flops | bytes accessed | tf_op | source)
XLA Modules:
  0.0 50.2 jit_solution(8182858587836771776)
XLA Ops:
  0.6 1.0 %slice.3.refs_0_ = bf16[128,1152]{1,0:T(8,128)(2,1)S(1)} slice(bf16[416,1152]{1,0:T(8,128)(2,1)} %array_ref.5), slice={[0:128], [0:1152]} | slice | bytes 589824 | tf_op jit(solution)/shard_map/slice | solution.py:155
  1.6 3.0 %collective-permute-start = (bf16[128,1152]{1,0:T(8,128)(2,1)S(1)}, bf16[128,1152]{1,0:T(8,128)(2,1)S(1)}, u32[]{:S(2)}, u32[]{:S(2)}) collective-permute-start(bf16[128,1152]{1,0:T(8,128)(2,1)S(1)} %slice.3.refs_0_), channel_id=1, source_target_pairs={{0,4},{4,8},{8,12},{12,16},{16,20},{20,24},{24,28},{28,0},{1,5},{5... | collective-permute-start | bytes 884744 | tf_op jit(solution)/shard_map/ppermute | solution.py:20
  4.6 1.2 %copy-done = bf16[416,1152]{1,0:T(8,128)(2,1)S(1)} copy-done((bf16[416,1152]{1,0:T(8,128)(2,1)S(1)}, bf16[416,1152]{1,0:T(8,128)(2,1)}, u32[]{:S(2)}) %copy-start) | copy-done | bytes 958488
  5.9 1.6 %collective-permute-start.2 = (bf16[240,1152]{1,0:T(8,128)(2,1)S(1)}, bf16[240,1152]{1,0:T(8,128)(2,1)S(1)}, u32[]{:S(2)}, u32[]{:S(2)}) collective-permute-start(bf16[240,1152]{1,0:T(8,128)(2,1)S(1)} %fetch.4), channel_id=1, source_target_pairs={{0,4},{4,8},{8,12},{12,16},{16,20},{20,24},{24,28},{28,0},{1,5},{5... | collective-permute-start | bytes 1658888 | tf_op jit(solution)/shard_map/ppermute | solution.py:20
  7.5 0.4 collective-permute-start.1
  9.2 6.3 %collective-permute-done.refs_0_ = bf16[128,1152]{1,0:T(8,128)(2,1)S(1)} collective-permute-done((bf16[128,1152]{1,0:T(8,128)(2,1)S(1)}, bf16[128,1152]{1,0:T(8,128)(2,1)S(1)}, u32[]{:S(2)}, u32[]{:S(2)}) %collective-permute-start) | collective-permute-done | bytes 294944 | tf_op jit(solution)/shard_map/ppermute | solution.py:20
  15.6 1.2 %copy-done.1 = bf16[416,1152]{1,0:T(8,128)(2,1)S(1)} copy-done((bf16[416,1152]{1,0:T(8,128)(2,1)S(1)}, bf16[416,1152]{1,0:T(8,128)(2,1)}, u32[]{:S(2)}) %copy-start.1) | copy-done | bytes 958488
  16.7 0.3 copy-done.2
  17.0 0.9 %fusion.17.refs_0_ = bf16[416,416]{1,0:T(8,128)(2,1)S(1)} fusion(bf16[416,1152]{1,0:T(8,128)(2,1)S(1)} %copy-done.2, bf16[416,1152]{1,0:T(8,128)(2,1)S(1)} %copy-done.1, s32[416]{0:T(512)S(1)} %bitcast.30, f32[]{:T(128)} %bitcast.28, f32[]{:T(128)} %bitcast.24), kind=kOutput, calls=%fused_computation.23 | convolution fusion | flops 400278528 | bytes 2264712 | tf_op jit(solution)/shard_map/dot_general | solution.py:24
  17.9 0.2 fetch.5
  18.1 0.7 %fusion.19.refs_2_ = f32[416,1152]{1,0:T(8,128)S(1)} fusion(bf16[416,416]{1,0:T(8,128)(2,1)S(1)} %fusion.17.refs_0_, bf16[416,1152]{1,0:T(8,128)(2,1)S(1)} %copy-done.2), kind=kOutput, calls=%fused_computation.26 | convolution fusion | flops 398721024 | bytes 3221504 | tf_op jit(solution)/shard_map/dot_general | solution.py:28
  18.9 0.7 %fusion.18.refs_1_ = f32[416,1152]{1,0:T(8,128)S(1)} fusion(bf16[416,416]{1,0:T(8,128)(2,1)S(1)} %fusion.17.refs_0_, bf16[416,1152]{1,0:T(8,128)(2,1)S(1)} %copy-done.1), kind=kOutput, calls=%fused_computation.25 | convolution fusion | flops 398721024 | bytes 3221504 | tf_op jit(solution)/shard_map/dot_general | solution.py:32
  19.6 0.8 %fusion.16 = bf16[416,416]{1,0:T(8,128)(2,1)S(1)} fusion(bf16[416,1152]{1,0:T(8,128)(2,1)S(1)} %pass_on.7.next_ref, bf16[416,1152]{1,0:T(8,128)(2,1)S(1)} %copy-done.1, f32[]{:T(128)} %bitcast.29, f32[]{:T(128)} %bitcast.27), kind=kOutput, calls=%fused_computation.22 | convolution fusion | flops 399759360 | bytes 2263048 | tf_op jit(solution)/shard_map/dot_general | solution.py:24
  20.4 1.2 %chunk.2 = (bf16[128,1152]{1,0:T(8,128)(2,1)S(1)}, bf16[128,416]{1,0:T(8,128)(2,1)S(1)}, bf16[128,416]{1,0:T(8,128)(2,1)S(1)}, bf16[128,1152]{1,0:T(8,128)(2,1)S(1)}) custom-call(f32[1]{0:T(128)} %copy.23.scale_ref, f32[1]{0:T(128)} %copy.24.bias_ref, bf16[416,1152]{1,0:T(8,128)(2,1)S(1)} %copy-done.2, bf16[416,1152]{1,0:T(8,128)(2,1)S(1)} %pass_on.7.next_ref, ...), custom_call_target="tpu_custom_call" | custom-call | flops 490733568 | bytes 2801664 | tf_op jit(solution)/shard_map/chunk/pallas_call | solution.py:100
  21.7 0.7 %fusion.20 = f32[416,1152]{1,0:T(8,128)S(1)} fusion(bf16[416,416]{1,0:T(8,128)(2,1)S(1)} %fusion.16, bf16[416,1152]{1,0:T(8,128)(2,1)S(1)} %copy-done.1), kind=kOutput, calls=%fused_computation.27 | convolution fusion | flops 398721024 | bytes 3221504 | tf_op jit(solution)/shard_map/dot_general | solution.py:32
  22.4 0.4 convolution_add_fusion.1.refs_2_
  22.8 4.5 %collective-permute-done.2.refs_1_.refs_0_ = bf16[240,1152]{1,0:T(8,128)(2,1)S(1)} collective-permute-done((bf16[240,1152]{1,0:T(8,128)(2,1)S(1)}, bf16[240,1152]{1,0:T(8,128)(2,1)S(1)}, u32[]{:S(2)}, u32[]{:S(2)}) %collective-permute-start.2) | collective-permute-done | bytes 552992 | tf_op jit(solution)/shard_map/ppermute | solution.py:20
  27.4 2.1 %collective-permute-start.4 = (bf16[128,1152]{1,0:T(8,128)(2,1)S(1)}, bf16[128,1152]{1,0:T(8,128)(2,1)S(1)}, u32[]{:S(2)}, u32[]{:S(2)}) collective-permute-start(bf16[128,1152]{1,0:T(8,128)(2,1)S(1)} %pass_on.8.refs_2_), channel_id=1, source_target_pairs={{0,28},{4,0},{8,4},{12,8},{16,12},{20,16},{24,20},{28,24},{1,29},{... | collective-permute-start | bytes 884744 | tf_op jit(solution)/shard_map/ppermute | solution.py:20
  29.4 1.9 %chunk.3 = (bf16[288,1152]{1,0:T(8,128)(2,1)S(1)}, bf16[288,416]{1,0:T(8,128)(2,1)S(1)}, bf16[288,416]{1,0:T(8,128)(2,1)S(1)}, bf16[208,1152]{1,0:T(8,128)(2,1)S(1)}, bf16[80,1152]{1,0:T(8,128)(2,1)S(1)}) custom-call(f32[1]{0:T(128)} %copy.23.scale_ref, f32[1]{0:T(128)} %copy.24.bias_ref, bf16[416,1152]{1,0:T(8,128)(2,1)S(1)} %copy-done.2, ...), custom_call_target="tpu_custom_call" | custom-call | flops 1104150528 | bytes 3907584 | tf_op jit(solution)/shard_map/chunk/pallas_call | solution.py:100
  31.3 1.5 %collective-permute-start.7 = (bf16[208,1152]{1,0:T(8,128)(2,1)S(1)}, bf16[208,1152]{1,0:T(8,128)(2,1)S(1)}, u32[]{:S(2)}, u32[]{:S(2)}) collective-permute-start(bf16[208,1152]{1,0:T(8,128)(2,1)S(1)} %get-tuple-element.23.refs_1_), channel_id=1, source_target_pairs={{0,28},{4,0},{8,4},{12,8},{16,12},{20,16},{24,20},{28,24},{1,29},{... | collective-permute-start | bytes 1437704 | tf_op jit(solution)/shard_map/ppermute | solution.py:20
  32.8 0.7 %fusion.4.refs_1_ = bf16[416,1152]{1,0:T(8,128)(2,1)S(1)} fusion(f32[416,1152]{1,0:T(8,128)S(1)} %convolution_add_fusion.1.refs_2_, bf16[288,416]{1,0:T(8,128)(2,1)S(1)} %pass_on.10, bf16[288,1152]{1,0:T(8,128)(2,1)S(1)} %get-tuple-element.21, f32[]{:T(128)} %bitcast.25), kind=kOutput, calls=%fused_computation.8 | convolution fusion | flops 277475328 | bytes 3778564 | tf_op jit(solution)/shard_map/dot_general | solution.py:28
  33.6 1.4 %collective-permute-start.6 = (bf16[80,1152]{1,0:T(8,128)(2,1)S(1)}, bf16[80,1152]{1,0:T(8,128)(2,1)S(1)}, u32[]{:S(2)}, u32[]{:S(2)}) collective-permute-start(bf16[80,1152]{1,0:T(8,128)(2,1)S(1)} %pass_on.11), channel_id=1, source_target_pairs={{0,28},{4,0},{8,4},{12,8},{16,12},{20,16},{24,20},{28,24},{1,29},{... | collective-permute-start | bytes 552968 | tf_op jit(solution)/shard_map/ppermute | solution.py:20
  34.9 0.7 %fusion.total_ref = f32[416,1152]{1,0:T(8,128)S(1)} fusion(f32[416,1152]{1,0:T(8,128)S(1)} %fusion.19.refs_2_, bf16[416,416]{1,0:T(8,128)(2,1)S(1)} %fusion.16, bf16[416,1152]{1,0:T(8,128)(2,1)S(1)} %pass_on.7.next_ref, f32[]{:T(128)} %bitcast.23), kind=kOutput, calls=%fused_computation.1 | convolution fusion | flops 399679488 | bytes 5138436 | tf_op jit(solution)/shard_map/dot_general | solution.py:28
  35.7 1.6 %collective-permute-done.4.back_ref = bf16[128,1152]{1,0:T(8,128)(2,1)S(1)} collective-permute-done((bf16[128,1152]{1,0:T(8,128)(2,1)S(1)}, bf16[128,1152]{1,0:T(8,128)(2,1)S(1)}, u32[]{:S(2)}, u32[]{:S(2)}) %collective-permute-start.4) | collective-permute-done | bytes 294944 | tf_op jit(solution)/shard_map/ppermute | solution.py:20
  37.3 0.8 %add_rows.4 = (bf16[416,1152]{1,0:T(8,128)(2,1)}, f32[8,128]{1,0:T(8,128)S(1)}) custom-call(f32[416,1152]{1,0:T(8,128)S(1)} %fusion.total_ref, bf16[128,1152]{1,0:T(8,128)(2,1)S(1)} %collective-permute-done.4.back_ref), custom_call_target="tpu_custom_call" | custom-call | tf_op jit(solution)/shard_map/add_rows/pallas_call | solution.py:139
  38.1 0.7 %fusion.21 = f32[416,1152]{1,0:T(8,128)S(1)} fusion(bf16[288,416]{1,0:T(8,128)(2,1)S(1)} %pass_on.9, bf16[288,1152]{1,0:T(8,128)(2,1)S(1)} %get-tuple-element.21), kind=kOutput, calls=%fused_computation.28 | convolution fusion | flops 276037632 | bytes 2820096 | tf_op jit(solution)/shard_map/dot_general | solution.py:28
  38.8 0.4 fusion.2.total_ref
  39.2 7.6 %collective-permute-done.5.back_ref = bf16[416,1152]{1,0:T(8,128)(2,1)S(1)} collective-permute-done((bf16[416,1152]{1,0:T(8,128)(2,1)S(1)}, bf16[416,1152]{1,0:T(8,128)(2,1)S(1)}, u32[]{:S(2)}, u32[]{:S(2)}) %collective-permute-start.5) | collective-permute-done | bytes 958496 | tf_op jit(solution)/shard_map/ppermute | solution.py:20
  46.8 1.0 %add_rows.5 = (bf16[416,1152]{1,0:T(8,128)(2,1)}, f32[8,128]{1,0:T(8,128)S(1)}) custom-call(f32[416,1152]{1,0:T(8,128)S(1)} %fusion.2.total_ref, bf16[416,1152]{1,0:T(8,128)(2,1)S(1)} %collective-permute-done.5.back_ref), custom_call_target="tpu_custom_call" | custom-call | tf_op jit(solution)/shard_map/add_rows/pallas_call | solution.py:139
  47.8 0.8 %add_rows.6.refs_0_ = bf16[416,1152]{1,0:T(8,128)(2,1)} custom-call(f32[416,1152]{1,0:T(8,128)S(1)} %fusion.total_ref, bf16[208,1152]{1,0:T(8,128)(2,1)S(1)} %collective-permute-done.7.back_ref, bf16[416,1152]{1,0:T(8,128)(2,1)} %get-tuple-element.26.refs_0_, f32[8,128]{1,0:T(8,128)S(1)} %get-tuple-element.27.refs_1_), custom_call_target="tpu_custom_call", output_to_operand_aliasing={{}: (2, {})} | custom-call | tf_op jit(solution)/shard_map/add_rows/pallas_call | solution.py:139
  48.7 0.7 %collective-permute-done.6.back_ref = bf16[80,1152]{1,0:T(8,128)(2,1)S(1)} collective-permute-done((bf16[80,1152]{1,0:T(8,128)(2,1)S(1)}, bf16[80,1152]{1,0:T(8,128)(2,1)S(1)}, u32[]{:S(2)}, u32[]{:S(2)}) %collective-permute-start.6) | collective-permute-done | bytes 184352 | tf_op jit(solution)/shard_map/ppermute | solution.py:20
  49.4 0.7 %add_rows.7 = bf16[416,1152]{1,0:T(8,128)(2,1)} custom-call(f32[416,1152]{1,0:T(8,128)S(1)} %fusion.total_ref, bf16[80,1152]{1,0:T(8,128)(2,1)S(1)} %collective-permute-done.6.back_ref, bf16[416,1152]{1,0:T(8,128)(2,1)} %add_rows.6.refs_0_), custom_call_target="tpu_custom_call", output_to_operand_aliasing={{}: (2, {})} | custom-call | tf_op jit(solution)/shard_map/add_rows/pallas_call | solution.py:139
  (18 shorter events, 0.2 us)
Async XLA Ops:
  0.6 14.9 %copy-start.3 = (s32[1,416]{1,0:T(1,128)S(1)}, s32[1,416]{1,0:T(1,128)}, u32[]{:S(2)}) copy-start(s32[1,416]{1,0:T(1,128)} %array_ref.3) | copy-start | bytes 4996
  1.6 13.9 %collective-permute-start = (bf16[128,1152]{1,0:T(8,128)(2,1)S(1)}, bf16[128,1152]{1,0:T(8,128)(2,1)S(1)}, u32[]{:S(2)}, u32[]{:S(2)}) collective-permute-start(bf16[128,1152]{1,0:T(8,128)(2,1)S(1)} %slice.3.refs_0_), channel_id=1, source_target_pairs={{0,4},{4,8},{8,12},{12,16},{16,20},{20,24},{24,28},{28,0},{1,5},{5... | collective-permute-start | bytes 884744 | tf_op jit(solution)/shard_map/ppermute | solution.py:20
  4.6 1.2 %copy-start = (bf16[416,1152]{1,0:T(8,128)(2,1)S(1)}, bf16[416,1152]{1,0:T(8,128)(2,1)}, u32[]{:S(2)}) copy-start(bf16[416,1152]{1,0:T(8,128)(2,1)} %array_ref.5) | copy-start | bytes 2875396
  5.9 21.4 %collective-permute-start.2 = (bf16[240,1152]{1,0:T(8,128)(2,1)S(1)}, bf16[240,1152]{1,0:T(8,128)(2,1)S(1)}, u32[]{:S(2)}, u32[]{:S(2)}) collective-permute-start(bf16[240,1152]{1,0:T(8,128)(2,1)S(1)} %fetch.4), channel_id=1, source_target_pairs={{0,4},{4,8},{8,12},{12,16},{16,20},{20,24},{24,28},{28,0},{1,5},{5... | collective-permute-start | bytes 1658888 | tf_op jit(solution)/shard_map/ppermute | solution.py:20
  7.5 12.1 %collective-permute-start.1 = (bf16[416,1152]{1,0:T(8,128)(2,1)}, bf16[416,1152]{1,0:T(8,128)(2,1)S(1)}, u32[]{:S(2)}, u32[]{:S(2)}) collective-permute-start(bf16[416,1152]{1,0:T(8,128)(2,1)} %image_ref.3), channel_id=1, source_target_pairs={{0,3},{1,0},{2,1},{3,2},{4,7},{5,4},{6,5},{7,6},{8,11},{9,8},{10,9... | collective-permute-start | bytes 2875400 | tf_op jit(solution)/shard_map/ppermute | solution.py:20
  15.5 1.2 %copy-start.1 = (bf16[416,1152]{1,0:T(8,128)(2,1)S(1)}, bf16[416,1152]{1,0:T(8,128)(2,1)}, u32[]{:S(2)}) copy-start(bf16[416,1152]{1,0:T(8,128)(2,1)} %array_ref.5) | copy-start | bytes 2875396
  15.5 1.5 %copy-start.2 = (bf16[416,1152]{1,0:T(8,128)(2,1)S(1)}, bf16[416,1152]{1,0:T(8,128)(2,1)}, u32[]{:S(2)}) copy-start(bf16[416,1152]{1,0:T(8,128)(2,1)} %image_ref.3) | copy-start | bytes 2875396
  18.1 11.4 %collective-permute-start.3 = (bf16[48,1152]{1,0:T(8,128)(2,1)S(1)}, bf16[48,1152]{1,0:T(8,128)(2,1)S(1)}, u32[]{:S(2)}, u32[]{:S(2)}) collective-permute-start(bf16[48,1152]{1,0:T(8,128)(2,1)S(1)} %fetch.5), channel_id=1, source_target_pairs={{0,4},{4,8},{8,12},{12,16},{16,20},{20,24},{24,28},{28,0},{1,5},{5... | collective-permute-start | bytes 331784 | tf_op jit(solution)/shard_map/ppermute | solution.py:20
  27.4 9.9 %collective-permute-start.4 = (bf16[128,1152]{1,0:T(8,128)(2,1)S(1)}, bf16[128,1152]{1,0:T(8,128)(2,1)S(1)}, u32[]{:S(2)}, u32[]{:S(2)}) collective-permute-start(bf16[128,1152]{1,0:T(8,128)(2,1)S(1)} %pass_on.8.refs_2_), channel_id=1, source_target_pairs={{0,28},{4,0},{8,4},{12,8},{16,12},{20,16},{24,20},{28,24},{1,29},{... | collective-permute-start | bytes 884744 | tf_op jit(solution)/shard_map/ppermute | solution.py:20
  31.3 16.5 %collective-permute-start.7 = (bf16[208,1152]{1,0:T(8,128)(2,1)S(1)}, bf16[208,1152]{1,0:T(8,128)(2,1)S(1)}, u32[]{:S(2)}, u32[]{:S(2)}) collective-permute-start(bf16[208,1152]{1,0:T(8,128)(2,1)S(1)} %get-tuple-element.23.refs_1_), channel_id=1, source_target_pairs={{0,28},{4,0},{8,4},{12,8},{16,12},{20,16},{24,20},{28,24},{1,29},{... | collective-permute-start | bytes 1437704 | tf_op jit(solution)/shard_map/ppermute | solution.py:20
  33.5 13.3 %collective-permute-start.5 = (bf16[416,1152]{1,0:T(8,128)(2,1)S(1)}, bf16[416,1152]{1,0:T(8,128)(2,1)S(1)}, u32[]{:S(2)}, u32[]{:S(2)}) collective-permute-start(bf16[416,1152]{1,0:T(8,128)(2,1)S(1)} %fusion.4.refs_1_), channel_id=1, source_target_pairs={{0,1},{1,2},{2,3},{3,0},{4,5},{5,6},{6,7},{7,4},{8,9},{9,10},{10,1... | collective-permute-start | bytes 2875400 | tf_op jit(solution)/shard_map/ppermute | solution.py:20
  33.6 15.9 %collective-permute-start.6 = (bf16[80,1152]{1,0:T(8,128)(2,1)S(1)}, bf16[80,1152]{1,0:T(8,128)(2,1)S(1)}, u32[]{:S(2)}, u32[]{:S(2)}) collective-permute-start(bf16[80,1152]{1,0:T(8,128)(2,1)S(1)} %pass_on.11), channel_id=1, source_target_pairs={{0,28},{4,0},{8,4},{12,8},{16,12},{20,16},{24,20},{28,24},{1,29},{... | collective-permute-start | bytes 552968 | tf_op jit(solution)/shard_map/ppermute | solution.py:20

commit v31 on v30

--- a/solution.py
+++ b/solution.py
@@ -157,7 +157,7 @@
     image_next = shifted(image, "grp", -1)
     part.append(shifted(fetch(text, *cuts[1], [first]), "blk", 1))
 
-    target = pass_on(fetch(target, 0, 1, [part[0]]), [], 2 * 10**10)
+    target = fetch(target, 0, 1, [part[0]])
     own = jax.nn.sigmoid(dot_nt(image, text) * scale + bias)
     column = lax.broadcasted_iota(jnp.int32, own.shape, 1)
     own = (own - (column == target[0][:, None]).astype(jnp.float32)).astype(jnp.bfloat16)

time: 50.4 us -> 50.3 us (level)
  local copies, waits for them, and re-layouts: 3.65 us -> 2.2 us
  waiting for transfers between devices: 20.7 us -> 21.9 us
    unnamed x8, local copies, waits for them, and re-layouts: 2.66 us -> 1.2 us
    ppermute x8, waiting for transfers between devices: 20.7 us -> 21.9 us  [shifted(): lax.ppermute(shard, axis, [(i, (i + by) % devices) for i in range(devices)])]
where the time goes in v31:
time: 50.3 us; the launch traced here: 50.2 us
  waiting for transfers between devices  21.9 us (44%)
  starting transfers between devices  10.3 us (20%)
  matrix products  6.93 us (14%)
  Pallas kernels  6.67 us (13%)
  local copies, waits for them, and re-layouts  2.2 us (4%)
  between operations  2.14 us (4%)
    ppermute x8, waiting for transfers between devices, shifted(): lax.ppermute(shard, axis, [(i, (i + by) % devices) for i in range(devices)])  21.9 us
    ppermute x8, starting transfers between devices, shifted(): lax.ppermute(shard, axis, [(i, (i + by) % devices) for i in range(devices)])  10.3 us
    dot_general x6, matrix products, dot_tn(): lax.dot_general(a, b, (((0,), (0,)), ((), ())), preferred_element_type=jn...  3.81 us
    pallas_call x4, Pallas kernels, add_rows(): pl.pallas_call(kernel, out_shape=(out, jax.ShapeDtypeStruct((8, 128), jnp...  3.33 us
    pallas_call x2, Pallas kernels, chunk(): pl.pallas_call(functools.partial(chunk_kernel, len(pieces), lasts), out_s...  3.08 us
    dot_general x2, matrix products, dot_nt(): lax.dot_general(a, b, (((1,), (1,)), ((), ())), preferred_element_type=jn...  1.72 us
    dot_general x2, matrix products, dot_nn(): return jnp.dot(a, b, preferred_element_type=jnp.float32)  1.4 us
    unnamed x8, local copies, waits for them, and re-layouts  1.2 us
  transfers between devices with their start and end apart: 8, of which 5 were waited for; matrix products, arithmetic and copies ran while one was open for 14% of the time, Pallas kernels for 12%

profile of v31, /device:TPU:0, one launch (start us, length us, event | category | flops | bytes accessed | tf_op | source)
XLA Modules:
  0.0 50.2 jit_solution(16669449397896318604)
XLA Ops:
  0.6 1.0 %slice.3.refs_0_ = bf16[128,1152]{1,0:T(8,128)(2,1)S(1)} slice(bf16[416,1152]{1,0:T(8,128)(2,1)} %array_ref.5), slice={[0:128], [0:1152]} | slice | bytes 589824 | tf_op jit(solution)/shard_map/slice | solution.py:155
  1.6 3.0 %collective-permute-start = (bf16[128,1152]{1,0:T(8,128)(2,1)S(1)}, bf16[128,1152]{1,0:T(8,128)(2,1)S(1)}, u32[]{:S(2)}, u32[]{:S(2)}) collective-permute-start(bf16[128,1152]{1,0:T(8,128)(2,1)S(1)} %slice.3.refs_0_), channel_id=1, source_target_pairs={{0,4},{4,8},{8,12},{12,16},{16,20},{20,24},{24,28},{28,0},{1,5},{5... | collective-permute-start | bytes 884744 | tf_op jit(solution)/shard_map/ppermute | solution.py:20
  4.6 0.7 %collective-permute-start.1 = (bf16[416,1152]{1,0:T(8,128)(2,1)}, bf16[416,1152]{1,0:T(8,128)(2,1)S(1)}, u32[]{:S(2)}, u32[]{:S(2)}) collective-permute-start(bf16[416,1152]{1,0:T(8,128)(2,1)} %image_ref.3), channel_id=1, source_target_pairs={{0,3},{1,0},{2,1},{3,2},{4,7},{5,4},{6,5},{7,6},{8,11},{9,8},{10,9... | collective-permute-start | bytes 2875400 | tf_op jit(solution)/shard_map/ppermute | solution.py:20
  5.3 1.2 %copy-done = bf16[416,1152]{1,0:T(8,128)(2,1)S(1)} copy-done((bf16[416,1152]{1,0:T(8,128)(2,1)S(1)}, bf16[416,1152]{1,0:T(8,128)(2,1)}, u32[]{:S(2)}) %copy-start) | copy-done | bytes 958488
  6.5 0.1 fetch.4
  6.6 1.6 %collective-permute-start.2 = (bf16[240,1152]{1,0:T(8,128)(2,1)S(1)}, bf16[240,1152]{1,0:T(8,128)(2,1)S(1)}, u32[]{:S(2)}, u32[]{:S(2)}) collective-permute-start(bf16[240,1152]{1,0:T(8,128)(2,1)S(1)} %fetch.4), channel_id=1, source_target_pairs={{0,4},{4,8},{8,12},{12,16},{16,20},{20,24},{24,28},{28,0},{1,5},{5... | collective-permute-start | bytes 1658888 | tf_op jit(solution)/shard_map/ppermute | solution.py:20
  9.5 6.0 %collective-permute-done.refs_0_ = bf16[128,1152]{1,0:T(8,128)(2,1)S(1)} collective-permute-done((bf16[128,1152]{1,0:T(8,128)(2,1)S(1)}, bf16[128,1152]{1,0:T(8,128)(2,1)S(1)}, u32[]{:S(2)}, u32[]{:S(2)}) %collective-permute-start) | collective-permute-done | bytes 294944 | tf_op jit(solution)/shard_map/ppermute | solution.py:20
  15.5 0.9 %subtract_convert_fusion.refs_0_ = bf16[416,416]{1,0:T(8,128)(2,1)S(1)} fusion(s32[416]{0:T(512)S(1)} %bitcast.30, f32[]{:T(128)} %bitcast.28, bf16[416,1152]{1,0:T(8,128)(2,1)S(1)} %copy-done.2, bf16[416,1152]{1,0:T(8,128)(2,1)S(1)} %copy-done.1, f32[]{:T(128)} %bitcast.24), kind=kOutput, calls=%fused_computation.22 | convolution fusion | flops 400278528 | bytes 2264712 | tf_op jit(solution)/shard_map/dot_general | solution.py:24
  16.4 0.2 fetch.5
  16.6 0.1 collective-permute-start.3
  16.7 0.7 %fusion.17.refs_2_ = f32[416,1152]{1,0:T(8,128)S(1)} fusion(bf16[416,416]{1,0:T(8,128)(2,1)S(1)} %subtract_convert_fusion.refs_0_, bf16[416,1152]{1,0:T(8,128)(2,1)S(1)} %copy-done.2), kind=kOutput, calls=%fused_computation.25 | convolution fusion | flops 398721024 | bytes 3221504 | tf_op jit(solution)/shard_map/dot_general | solution.py:28
  17.4 0.7 %fusion.16.refs_1_ = f32[416,1152]{1,0:T(8,128)S(1)} fusion(bf16[416,416]{1,0:T(8,128)(2,1)S(1)} %subtract_convert_fusion.refs_0_, bf16[416,1152]{1,0:T(8,128)(2,1)S(1)} %copy-done.1), kind=kOutput, calls=%fused_computation.24 | convolution fusion | flops 398721024 | bytes 3221504 | tf_op jit(solution)/shard_map/dot_general | solution.py:32
  18.1 0.8 %fusion.15 = bf16[416,416]{1,0:T(8,128)(2,1)S(1)} fusion(bf16[416,1152]{1,0:T(8,128)(2,1)S(1)} %pass_on.5.next_ref, bf16[416,1152]{1,0:T(8,128)(2,1)S(1)} %copy-done.1, f32[]{:T(128)} %bitcast.29, f32[]{:T(128)} %bitcast.27), kind=kOutput, calls=%fused_computation.21 | convolution fusion | flops 399759360 | bytes 2263048 | tf_op jit(solution)/shard_map/dot_general | solution.py:24
  19.0 1.2 %chunk.2 = (bf16[128,1152]{1,0:T(8,128)(2,1)S(1)}, bf16[128,416]{1,0:T(8,128)(2,1)S(1)}, bf16[128,416]{1,0:T(8,128)(2,1)S(1)}, bf16[128,1152]{1,0:T(8,128)(2,1)S(1)}) custom-call(f32[1]{0:T(128)} %copy.21.scale_ref, f32[1]{0:T(128)} %copy.22.bias_ref, bf16[416,1152]{1,0:T(8,128)(2,1)S(1)} %copy-done.2, bf16[416,1152]{1,0:T(8,128)(2,1)S(1)} %pass_on.5.next_ref, ...), custom_call_target="tpu_custom_call" | custom-call | flops 490733568 | bytes 2801664 | tf_op jit(solution)/shard_map/chunk/pallas_call | solution.py:100
  20.2 0.7 %fusion.18 = f32[416,1152]{1,0:T(8,128)S(1)} fusion(bf16[416,416]{1,0:T(8,128)(2,1)S(1)} %fusion.15, bf16[416,1152]{1,0:T(8,128)(2,1)S(1)} %copy-done.1), kind=kOutput, calls=%fused_computation.26 | convolution fusion | flops 398721024 | bytes 3221504 | tf_op jit(solution)/shard_map/dot_general | solution.py:32
  20.9 0.4 convolution_add_fusion.1.refs_2_
  21.4 6.0 %collective-permute-done.2.refs_1_.refs_0_ = bf16[240,1152]{1,0:T(8,128)(2,1)S(1)} collective-permute-done((bf16[240,1152]{1,0:T(8,128)(2,1)S(1)}, bf16[240,1152]{1,0:T(8,128)(2,1)S(1)}, u32[]{:S(2)}, u32[]{:S(2)}) %collective-permute-start.2) | collective-permute-done | bytes 552992 | tf_op jit(solution)/shard_map/ppermute | solution.py:20
  27.4 2.1 %collective-permute-start.4 = (bf16[128,1152]{1,0:T(8,128)(2,1)S(1)}, bf16[128,1152]{1,0:T(8,128)(2,1)S(1)}, u32[]{:S(2)}, u32[]{:S(2)}) collective-permute-start(bf16[128,1152]{1,0:T(8,128)(2,1)S(1)} %pass_on.6.refs_2_), channel_id=1, source_target_pairs={{0,28},{4,0},{8,4},{12,8},{16,12},{20,16},{24,20},{28,24},{1,29},{... | collective-permute-start | bytes 884744 | tf_op jit(solution)/shard_map/ppermute | solution.py:20
  29.4 1.9 %chunk.3 = (bf16[288,1152]{1,0:T(8,128)(2,1)S(1)}, bf16[288,416]{1,0:T(8,128)(2,1)S(1)}, bf16[288,416]{1,0:T(8,128)(2,1)S(1)}, bf16[208,1152]{1,0:T(8,128)(2,1)S(1)}, bf16[80,1152]{1,0:T(8,128)(2,1)S(1)}) custom-call(f32[1]{0:T(128)} %copy.21.scale_ref, f32[1]{0:T(128)} %copy.22.bias_ref, bf16[416,1152]{1,0:T(8,128)(2,1)S(1)} %copy-done.2, ...), custom_call_target="tpu_custom_call" | custom-call | flops 1104150528 | bytes 3907584 | tf_op jit(solution)/shard_map/chunk/pallas_call | solution.py:100
  31.3 1.5 %collective-permute-start.7 = (bf16[208,1152]{1,0:T(8,128)(2,1)S(1)}, bf16[208,1152]{1,0:T(8,128)(2,1)S(1)}, u32[]{:S(2)}, u32[]{:S(2)}) collective-permute-start(bf16[208,1152]{1,0:T(8,128)(2,1)S(1)} %get-tuple-element.23.refs_1_), channel_id=1, source_target_pairs={{0,28},{4,0},{8,4},{12,8},{16,12},{20,16},{24,20},{28,24},{1,29},{... | collective-permute-start | bytes 1437704 | tf_op jit(solution)/shard_map/ppermute | solution.py:20
  32.8 0.7 %fusion.4.refs_1_ = bf16[416,1152]{1,0:T(8,128)(2,1)S(1)} fusion(f32[416,1152]{1,0:T(8,128)S(1)} %convolution_add_fusion.1.refs_2_, bf16[288,416]{1,0:T(8,128)(2,1)S(1)} %pass_on.8, bf16[288,1152]{1,0:T(8,128)(2,1)S(1)} %get-tuple-element.21, f32[]{:T(128)} %bitcast.25), kind=kOutput, calls=%fused_computation.8 | convolution fusion | flops 277475328 | bytes 3778564 | tf_op jit(solution)/shard_map/dot_general | solution.py:28
  33.6 1.4 %collective-permute-start.6 = (bf16[80,1152]{1,0:T(8,128)(2,1)S(1)}, bf16[80,1152]{1,0:T(8,128)(2,1)S(1)}, u32[]{:S(2)}, u32[]{:S(2)}) collective-permute-start(bf16[80,1152]{1,0:T(8,128)(2,1)S(1)} %pass_on.9), channel_id=1, source_target_pairs={{0,28},{4,0},{8,4},{12,8},{16,12},{20,16},{24,20},{28,24},{1,29},{... | collective-permute-start | bytes 552968 | tf_op jit(solution)/shard_map/ppermute | solution.py:20
  34.9 0.7 %fusion.total_ref = f32[416,1152]{1,0:T(8,128)S(1)} fusion(f32[416,1152]{1,0:T(8,128)S(1)} %fusion.17.refs_2_, bf16[416,416]{1,0:T(8,128)(2,1)S(1)} %fusion.15, bf16[416,1152]{1,0:T(8,128)(2,1)S(1)} %pass_on.5.next_ref, f32[]{:T(128)} %bitcast.23), kind=kOutput, calls=%fused_computation.1 | convolution fusion | flops 399679488 | bytes 5138436 | tf_op jit(solution)/shard_map/dot_general | solution.py:28
  35.7 1.6 %collective-permute-done.4.back_ref = bf16[128,1152]{1,0:T(8,128)(2,1)S(1)} collective-permute-done((bf16[128,1152]{1,0:T(8,128)(2,1)S(1)}, bf16[128,1152]{1,0:T(8,128)(2,1)S(1)}, u32[]{:S(2)}, u32[]{:S(2)}) %collective-permute-start.4) | collective-permute-done | bytes 294944 | tf_op jit(solution)/shard_map/ppermute | solution.py:20
  37.3 0.8 %add_rows.4 = (bf16[416,1152]{1,0:T(8,128)(2,1)}, f32[8,128]{1,0:T(8,128)S(1)}) custom-call(f32[416,1152]{1,0:T(8,128)S(1)} %fusion.total_ref, bf16[128,1152]{1,0:T(8,128)(2,1)S(1)} %collective-permute-done.4.back_ref), custom_call_target="tpu_custom_call" | custom-call | tf_op jit(solution)/shard_map/add_rows/pallas_call | solution.py:139
  38.1 0.7 %fusion.19 = f32[416,1152]{1,0:T(8,128)S(1)} fusion(bf16[288,416]{1,0:T(8,128)(2,1)S(1)} %pass_on.7, bf16[288,1152]{1,0:T(8,128)(2,1)S(1)} %get-tuple-element.21), kind=kOutput, calls=%fused_computation.27 | convolution fusion | flops 276037632 | bytes 2820096 | tf_op jit(solution)/shard_map/dot_general | solution.py:28
  38.8 0.4 fusion.2.total_ref
  39.2 7.6 %collective-permute-done.5.back_ref = bf16[416,1152]{1,0:T(8,128)(2,1)S(1)} collective-permute-done((bf16[416,1152]{1,0:T(8,128)(2,1)S(1)}, bf16[416,1152]{1,0:T(8,128)(2,1)S(1)}, u32[]{:S(2)}, u32[]{:S(2)}) %collective-permute-start.5) | collective-permute-done | bytes 958496 | tf_op jit(solution)/shard_map/ppermute | solution.py:20
  46.8 1.0 %add_rows.5 = (bf16[416,1152]{1,0:T(8,128)(2,1)}, f32[8,128]{1,0:T(8,128)S(1)}) custom-call(f32[416,1152]{1,0:T(8,128)S(1)} %fusion.2.total_ref, bf16[416,1152]{1,0:T(8,128)(2,1)S(1)} %collective-permute-done.5.back_ref), custom_call_target="tpu_custom_call" | custom-call | tf_op jit(solution)/shard_map/add_rows/pallas_call | solution.py:139
  47.8 0.8 %add_rows.6.refs_0_ = bf16[416,1152]{1,0:T(8,128)(2,1)} custom-call(f32[416,1152]{1,0:T(8,128)S(1)} %fusion.total_ref, bf16[208,1152]{1,0:T(8,128)(2,1)S(1)} %collective-permute-done.7.back_ref, bf16[416,1152]{1,0:T(8,128)(2,1)} %get-tuple-element.26.refs_0_, f32[8,128]{1,0:T(8,128)S(1)} %get-tuple-element.27.refs_1_), custom_call_target="tpu_custom_call", output_to_operand_aliasing={{}: (2, {})} | custom-call | tf_op jit(solution)/shard_map/add_rows/pallas_call | solution.py:139
  48.7 0.7 %collective-permute-done.6.back_ref = bf16[80,1152]{1,0:T(8,128)(2,1)S(1)} collective-permute-done((bf16[80,1152]{1,0:T(8,128)(2,1)S(1)}, bf16[80,1152]{1,0:T(8,128)(2,1)S(1)}, u32[]{:S(2)}, u32[]{:S(2)}) %collective-permute-start.6) | collective-permute-done | bytes 184352 | tf_op jit(solution)/shard_map/ppermute | solution.py:20
  49.4 0.7 %add_rows.7 = bf16[416,1152]{1,0:T(8,128)(2,1)} custom-call(f32[416,1152]{1,0:T(8,128)S(1)} %fusion.total_ref, bf16[80,1152]{1,0:T(8,128)(2,1)S(1)} %collective-permute-done.6.back_ref, bf16[416,1152]{1,0:T(8,128)(2,1)} %add_rows.6.refs_0_), custom_call_target="tpu_custom_call", output_to_operand_aliasing={{}: (2, {})} | custom-call | tf_op jit(solution)/shard_map/add_rows/pallas_call | solution.py:139
  (17 shorter events, 0.1 us)
Async XLA Ops:
  0.6 14.9 %copy-start.3 = (s32[1,416]{1,0:T(1,128)S(1)}, s32[1,416]{1,0:T(1,128)}, u32[]{:S(2)}) copy-start(s32[1,416]{1,0:T(1,128)} %array_ref.3) | copy-start | bytes 4996
  1.6 13.9 %collective-permute-start = (bf16[128,1152]{1,0:T(8,128)(2,1)S(1)}, bf16[128,1152]{1,0:T(8,128)(2,1)S(1)}, u32[]{:S(2)}, u32[]{:S(2)}) collective-permute-start(bf16[128,1152]{1,0:T(8,128)(2,1)S(1)} %slice.3.refs_0_), channel_id=1, source_target_pairs={{0,4},{4,8},{8,12},{12,16},{16,20},{20,24},{24,28},{28,0},{1,5},{5... | collective-permute-start | bytes 884744 | tf_op jit(solution)/shard_map/ppermute | solution.py:20
  4.6 13.5 %collective-permute-start.1 = (bf16[416,1152]{1,0:T(8,128)(2,1)}, bf16[416,1152]{1,0:T(8,128)(2,1)S(1)}, u32[]{:S(2)}, u32[]{:S(2)}) collective-permute-start(bf16[416,1152]{1,0:T(8,128)(2,1)} %image_ref.3), channel_id=1, source_target_pairs={{0,3},{1,0},{2,1},{3,2},{4,7},{5,4},{6,5},{7,6},{8,11},{9,8},{10,9... | collective-permute-start | bytes 2875400 | tf_op jit(solution)/shard_map/ppermute | solution.py:20
  5.3 1.2 %copy-start = (bf16[416,1152]{1,0:T(8,128)(2,1)S(1)}, bf16[416,1152]{1,0:T(8,128)(2,1)}, u32[]{:S(2)}) copy-start(bf16[416,1152]{1,0:T(8,128)(2,1)} %array_ref.5) | copy-start | bytes 2875396
  6.5 9.0 %copy-start.1 = (bf16[416,1152]{1,0:T(8,128)(2,1)S(1)}, bf16[416,1152]{1,0:T(8,128)(2,1)}, u32[]{:S(2)}) copy-start(bf16[416,1152]{1,0:T(8,128)(2,1)} %array_ref.5) | copy-start | bytes 2875396
  6.5 9.0 %copy-start.2 = (bf16[416,1152]{1,0:T(8,128)(2,1)S(1)}, bf16[416,1152]{1,0:T(8,128)(2,1)}, u32[]{:S(2)}) copy-start(bf16[416,1152]{1,0:T(8,128)(2,1)} %image_ref.3) | copy-start | bytes 2875396
  6.6 20.8 %collective-permute-start.2 = (bf16[240,1152]{1,0:T(8,128)(2,1)S(1)}, bf16[240,1152]{1,0:T(8,128)(2,1)S(1)}, u32[]{:S(2)}, u32[]{:S(2)}) collective-permute-start(bf16[240,1152]{1,0:T(8,128)(2,1)S(1)} %fetch.4), channel_id=1, source_target_pairs={{0,4},{4,8},{8,12},{12,16},{16,20},{20,24},{24,28},{28,0},{1,5},{5... | collective-permute-start | bytes 1658888 | tf_op jit(solution)/shard_map/ppermute | solution.py:20
  16.6 12.8 %collective-permute-start.3 = (bf16[48,1152]{1,0:T(8,128)(2,1)S(1)}, bf16[48,1152]{1,0:T(8,128)(2,1)S(1)}, u32[]{:S(2)}, u32[]{:S(2)}) collective-permute-start(bf16[48,1152]{1,0:T(8,128)(2,1)S(1)} %fetch.5), channel_id=1, source_target_pairs={{0,4},{4,8},{8,12},{12,16},{16,20},{20,24},{24,28},{28,0},{1,5},{5... | collective-permute-start | bytes 331784 | tf_op jit(solution)/shard_map/ppermute | solution.py:20
  27.4 9.9 %collective-permute-start.4 = (bf16[128,1152]{1,0:T(8,128)(2,1)S(1)}, bf16[128,1152]{1,0:T(8,128)(2,1)S(1)}, u32[]{:S(2)}, u32[]{:S(2)}) collective-permute-start(bf16[128,1152]{1,0:T(8,128)(2,1)S(1)} %pass_on.6.refs_2_), channel_id=1, source_target_pairs={{0,28},{4,0},{8,4},{12,8},{16,12},{20,16},{24,20},{28,24},{1,29},{... | collective-permute-start | bytes 884744 | tf_op jit(solution)/shard_map/ppermute | solution.py:20
  31.3 16.5 %collective-permute-start.7 = (bf16[208,1152]{1,0:T(8,128)(2,1)S(1)}, bf16[208,1152]{1,0:T(8,128)(2,1)S(1)}, u32[]{:S(2)}, u32[]{:S(2)}) collective-permute-start(bf16[208,1152]{1,0:T(8,128)(2,1)S(1)} %get-tuple-element.23.refs_1_), channel_id=1, source_target_pairs={{0,28},{4,0},{8,4},{12,8},{16,12},{20,16},{24,20},{28,24},{1,29},{... | collective-permute-start | bytes 1437704 | tf_op jit(solution)/shard_map/ppermute | solution.py:20
  33.5 13.3 %collective-permute-start.5 = (bf16[416,1152]{1,0:T(8,128)(2,1)S(1)}, bf16[416,1152]{1,0:T(8,128)(2,1)S(1)}, u32[]{:S(2)}, u32[]{:S(2)}) collective-permute-start(bf16[416,1152]{1,0:T(8,128)(2,1)S(1)} %fusion.4.refs_1_), channel_id=1, source_target_pairs={{0,1},{1,2},{2,3},{3,0},{4,5},{5,6},{6,7},{7,4},{8,9},{9,10},{10,1... | collective-permute-start | bytes 2875400 | tf_op jit(solution)/shard_map/ppermute | solution.py:20
  33.6 15.9 %collective-permute-start.6 = (bf16[80,1152]{1,0:T(8,128)(2,1)S(1)}, bf16[80,1152]{1,0:T(8,128)(2,1)S(1)}, u32[]{:S(2)}, u32[]{:S(2)}) collective-permute-start(bf16[80,1152]{1,0:T(8,128)(2,1)S(1)} %pass_on.9), channel_id=1, source_target_pairs={{0,28},{4,0},{8,4},{12,8},{16,12},{20,16},{24,20},{28,24},{1,29},{... | collective-permute-start | bytes 552968 | tf_op jit(solution)/shard_map/ppermute | solution.py:20

commit v32 on v30

--- a/solution.py
+++ b/solution.py
@@ -175,7 +175,7 @@
     sent0 = pass_on(sent0, [part[1], image_sent])
     back0 = shifted(sent0, "blk", -1)
 
-    lasts = part[2].shape[0] + 32
+    lasts = part[2].shape[0] + 64
     part1, own1, next1, sent1, sent2 = chunk(factor, shift, image, image_next, part[1:], [sent0], lasts)
     back1 = shifted(sent1, "blk", -1)
     next1 = pass_on(next1, [sent1], 2 * 10**10)

time: 50.4 us -> 50.4 us (level)
  no operation moved by 1% of the time
where the time goes in v32:
time: 50.4 us; the launch traced here: 50.2 us
  waiting for transfers between devices  20.7 us (41%)
  starting transfers between devices  10 us (20%)
  matrix products  6.97 us (14%)
  Pallas kernels  6.66 us (13%)
  local copies, waits for them, and re-layouts  3.65 us (7%)
  between operations  2.15 us (4%)
    ppermute x8, waiting for transfers between devices, shifted(): lax.ppermute(shard, axis, [(i, (i + by) % devices) for i in range(devices)])  20.7 us
    ppermute x8, starting transfers between devices, shifted(): lax.ppermute(shard, axis, [(i, (i + by) % devices) for i in range(devices)])  10 us
    dot_general x6, matrix products, dot_tn(): lax.dot_general(a, b, (((0,), (0,)), ((), ())), preferred_element_type=jn...  3.83 us
    pallas_call x4, Pallas kernels, add_rows(): pl.pallas_call(kernel, out_shape=(out, jax.ShapeDtypeStruct((8, 128), jnp...  3.32 us
    pallas_call x2, Pallas kernels, chunk(): pl.pallas_call(functools.partial(chunk_kernel, len(pieces), lasts), out_s...  3.08 us
    unnamed x8, local copies, waits for them, and re-layouts  2.66 us
    dot_general x2, matrix products, dot_nt(): lax.dot_general(a, b, (((1,), (1,)), ((), ())), preferred_element_type=jn...  1.72 us
    dot_general x2, matrix products, dot_nn(): return jnp.dot(a, b, preferred_element_type=jnp.float32)  1.42 us
  transfers between devices with their start and end apart: 8, of which 5 were waited for; matrix products, arithmetic and copies ran while one was open for 14% of the time, Pallas kernels for 12%

profile of v32, /device:TPU:0, one launch (start us, length us, event | category | flops | bytes accessed | tf_op | source)
XLA Modules:
  0.0 50.2 jit_solution(6734112887493745281)
XLA Ops:
  0.6 1.0 %slice.3.refs_0_ = bf16[128,1152]{1,0:T(8,128)(2,1)S(1)} slice(bf16[416,1152]{1,0:T(8,128)(2,1)} %array_ref.5), slice={[0:128], [0:1152]} | slice | bytes 589824 | tf_op jit(solution)/shard_map/slice | solution.py:155
  1.6 3.0 %collective-permute-start = (bf16[128,1152]{1,0:T(8,128)(2,1)S(1)}, bf16[128,1152]{1,0:T(8,128)(2,1)S(1)}, u32[]{:S(2)}, u32[]{:S(2)}) collective-permute-start(bf16[128,1152]{1,0:T(8,128)(2,1)S(1)} %slice.3.refs_0_), channel_id=1, source_target_pairs={{0,4},{4,8},{8,12},{12,16},{16,20},{20,24},{24,28},{28,0},{1,5},{5... | collective-permute-start | bytes 884744 | tf_op jit(solution)/shard_map/ppermute | solution.py:20
  4.6 1.2 %copy-done = bf16[416,1152]{1,0:T(8,128)(2,1)S(1)} copy-done((bf16[416,1152]{1,0:T(8,128)(2,1)S(1)}, bf16[416,1152]{1,0:T(8,128)(2,1)}, u32[]{:S(2)}) %copy-start) | copy-done | bytes 958488
  5.9 1.6 %collective-permute-start.2 = (bf16[240,1152]{1,0:T(8,128)(2,1)S(1)}, bf16[240,1152]{1,0:T(8,128)(2,1)S(1)}, u32[]{:S(2)}, u32[]{:S(2)}) collective-permute-start(bf16[240,1152]{1,0:T(8,128)(2,1)S(1)} %fetch.4), channel_id=1, source_target_pairs={{0,4},{4,8},{8,12},{12,16},{16,20},{20,24},{24,28},{28,0},{1,5},{5... | collective-permute-start | bytes 1658888 | tf_op jit(solution)/shard_map/ppermute | solution.py:20
  7.5 0.4 collective-permute-start.1
  9.2 6.3 %collective-permute-done.refs_0_ = bf16[128,1152]{1,0:T(8,128)(2,1)S(1)} collective-permute-done((bf16[128,1152]{1,0:T(8,128)(2,1)S(1)}, bf16[128,1152]{1,0:T(8,128)(2,1)S(1)}, u32[]{:S(2)}, u32[]{:S(2)}) %collective-permute-start) | collective-permute-done | bytes 294944 | tf_op jit(solution)/shard_map/ppermute | solution.py:20
  15.6 1.2 %copy-done.1 = bf16[416,1152]{1,0:T(8,128)(2,1)S(1)} copy-done((bf16[416,1152]{1,0:T(8,128)(2,1)S(1)}, bf16[416,1152]{1,0:T(8,128)(2,1)}, u32[]{:S(2)}) %copy-start.1) | copy-done | bytes 958488
  16.7 0.3 copy-done.2
  17.0 0.9 %fusion.17.refs_0_ = bf16[416,416]{1,0:T(8,128)(2,1)S(1)} fusion(bf16[416,1152]{1,0:T(8,128)(2,1)S(1)} %copy-done.2, bf16[416,1152]{1,0:T(8,128)(2,1)S(1)} %copy-done.1, s32[416]{0:T(512)S(1)} %bitcast.30, f32[]{:T(128)} %bitcast.28, f32[]{:T(128)} %bitcast.24), kind=kOutput, calls=%fused_computation.23 | convolution fusion | flops 400278528 | bytes 2264712 | tf_op jit(solution)/shard_map/dot_general | solution.py:24
  17.9 0.2 fetch.5
  18.1 0.7 %fusion.19.refs_2_ = f32[416,1152]{1,0:T(8,128)S(1)} fusion(bf16[416,416]{1,0:T(8,128)(2,1)S(1)} %fusion.17.refs_0_, bf16[416,1152]{1,0:T(8,128)(2,1)S(1)} %copy-done.2), kind=kOutput, calls=%fused_computation.26 | convolution fusion | flops 398721024 | bytes 3221504 | tf_op jit(solution)/shard_map/dot_general | solution.py:28
  18.9 0.7 %fusion.18.refs_1_ = f32[416,1152]{1,0:T(8,128)S(1)} fusion(bf16[416,416]{1,0:T(8,128)(2,1)S(1)} %fusion.17.refs_0_, bf16[416,1152]{1,0:T(8,128)(2,1)S(1)} %copy-done.1), kind=kOutput, calls=%fused_computation.25 | convolution fusion | flops 398721024 | bytes 3221504 | tf_op jit(solution)/shard_map/dot_general | solution.py:32
  19.6 0.8 %fusion.16 = bf16[416,416]{1,0:T(8,128)(2,1)S(1)} fusion(bf16[416,1152]{1,0:T(8,128)(2,1)S(1)} %pass_on.7.next_ref, bf16[416,1152]{1,0:T(8,128)(2,1)S(1)} %copy-done.1, f32[]{:T(128)} %bitcast.29, f32[]{:T(128)} %bitcast.27), kind=kOutput, calls=%fused_computation.22 | convolution fusion | flops 399759360 | bytes 2263048 | tf_op jit(solution)/shard_map/dot_general | solution.py:24
  20.4 1.2 %chunk.2 = (bf16[128,1152]{1,0:T(8,128)(2,1)S(1)}, bf16[128,416]{1,0:T(8,128)(2,1)S(1)}, bf16[128,416]{1,0:T(8,128)(2,1)S(1)}, bf16[128,1152]{1,0:T(8,128)(2,1)S(1)}) custom-call(f32[1]{0:T(128)} %copy.23.scale_ref, f32[1]{0:T(128)} %copy.24.bias_ref, bf16[416,1152]{1,0:T(8,128)(2,1)S(1)} %copy-done.2, bf16[416,1152]{1,0:T(8,128)(2,1)S(1)} %pass_on.7.next_ref, ...), custom_call_target="tpu_custom_call" | custom-call | flops 490733568 | bytes 2801664 | tf_op jit(solution)/shard_map/chunk/pallas_call | solution.py:100
  21.7 0.7 %fusion.20 = f32[416,1152]{1,0:T(8,128)S(1)} fusion(bf16[416,416]{1,0:T(8,128)(2,1)S(1)} %fusion.16, bf16[416,1152]{1,0:T(8,128)(2,1)S(1)} %copy-done.1), kind=kOutput, calls=%fused_computation.27 | convolution fusion | flops 398721024 | bytes 3221504 | tf_op jit(solution)/shard_map/dot_general | solution.py:32
  22.4 0.4 convolution_add_fusion.1.refs_2_
  22.8 4.5 %collective-permute-done.2.refs_1_.refs_0_ = bf16[240,1152]{1,0:T(8,128)(2,1)S(1)} collective-permute-done((bf16[240,1152]{1,0:T(8,128)(2,1)S(1)}, bf16[240,1152]{1,0:T(8,128)(2,1)S(1)}, u32[]{:S(2)}, u32[]{:S(2)}) %collective-permute-start.2) | collective-permute-done | bytes 552992 | tf_op jit(solution)/shard_map/ppermute | solution.py:20
  27.4 2.1 %collective-permute-start.4 = (bf16[128,1152]{1,0:T(8,128)(2,1)S(1)}, bf16[128,1152]{1,0:T(8,128)(2,1)S(1)}, u32[]{:S(2)}, u32[]{:S(2)}) collective-permute-start(bf16[128,1152]{1,0:T(8,128)(2,1)S(1)} %pass_on.8.refs_2_), channel_id=1, source_target_pairs={{0,28},{4,0},{8,4},{12,8},{16,12},{20,16},{24,20},{28,24},{1,29},{... | collective-permute-start | bytes 884744 | tf_op jit(solution)/shard_map/ppermute | solution.py:20
  29.4 1.9 %chunk.3 = (bf16[288,1152]{1,0:T(8,128)(2,1)S(1)}, bf16[288,416]{1,0:T(8,128)(2,1)S(1)}, bf16[288,416]{1,0:T(8,128)(2,1)S(1)}, bf16[176,1152]{1,0:T(8,128)(2,1)S(1)}, bf16[112,1152]{1,0:T(8,128)(2,1)S(1)}) custom-call(f32[1]{0:T(128)} %copy.23.scale_ref, f32[1]{0:T(128)} %copy.24.bias_ref, bf16[416,1152]{1,0:T(8,128)(2,1)S(1)} %copy-done.2, ...), custom_call_target="tpu_custom_call" | custom-call | flops 1104150528 | bytes 3907584 | tf_op jit(solution)/shard_map/chunk/pallas_call | solution.py:100
  31.3 1.5 %collective-permute-start.7 = (bf16[176,1152]{1,0:T(8,128)(2,1)S(1)}, bf16[176,1152]{1,0:T(8,128)(2,1)S(1)}, u32[]{:S(2)}, u32[]{:S(2)}) collective-permute-start(bf16[176,1152]{1,0:T(8,128)(2,1)S(1)} %get-tuple-element.23.refs_1_), channel_id=1, source_target_pairs={{0,28},{4,0},{8,4},{12,8},{16,12},{20,16},{24,20},{28,24},{1,29},{... | collective-permute-start | bytes 1216520 | tf_op jit(solution)/shard_map/ppermute | solution.py:20
  32.8 0.7 %fusion.4.refs_1_ = bf16[416,1152]{1,0:T(8,128)(2,1)S(1)} fusion(f32[416,1152]{1,0:T(8,128)S(1)} %convolution_add_fusion.1.refs_2_, bf16[288,416]{1,0:T(8,128)(2,1)S(1)} %pass_on.10, bf16[288,1152]{1,0:T(8,128)(2,1)S(1)} %get-tuple-element.21, f32[]{:T(128)} %bitcast.25), kind=kOutput, calls=%fused_computation.8 | convolution fusion | flops 277475328 | bytes 3778564 | tf_op jit(solution)/shard_map/dot_general | solution.py:28
  33.6 1.4 %collective-permute-start.6 = (bf16[112,1152]{1,0:T(8,128)(2,1)S(1)}, bf16[112,1152]{1,0:T(8,128)(2,1)S(1)}, u32[]{:S(2)}, u32[]{:S(2)}) collective-permute-start(bf16[112,1152]{1,0:T(8,128)(2,1)S(1)} %pass_on.11), channel_id=1, source_target_pairs={{0,28},{4,0},{8,4},{12,8},{16,12},{20,16},{24,20},{28,24},{1,29},{... | collective-permute-start | bytes 774152 | tf_op jit(solution)/shard_map/ppermute | solution.py:20
  34.9 0.8 %fusion.total_ref = f32[416,1152]{1,0:T(8,128)S(1)} fusion(f32[416,1152]{1,0:T(8,128)S(1)} %fusion.19.refs_2_, bf16[416,416]{1,0:T(8,128)(2,1)S(1)} %fusion.16, bf16[416,1152]{1,0:T(8,128)(2,1)S(1)} %pass_on.7.next_ref, f32[]{:T(128)} %bitcast.23), kind=kOutput, calls=%fused_computation.1 | convolution fusion | flops 399679488 | bytes 5138436 | tf_op jit(solution)/shard_map/dot_general | solution.py:28
  35.7 1.6 %collective-permute-done.4.back_ref = bf16[128,1152]{1,0:T(8,128)(2,1)S(1)} collective-permute-done((bf16[128,1152]{1,0:T(8,128)(2,1)S(1)}, bf16[128,1152]{1,0:T(8,128)(2,1)S(1)}, u32[]{:S(2)}, u32[]{:S(2)}) %collective-permute-start.4) | collective-permute-done | bytes 294944 | tf_op jit(solution)/shard_map/ppermute | solution.py:20
  37.3 0.8 %add_rows.4 = (bf16[416,1152]{1,0:T(8,128)(2,1)}, f32[8,128]{1,0:T(8,128)S(1)}) custom-call(f32[416,1152]{1,0:T(8,128)S(1)} %fusion.total_ref, bf16[128,1152]{1,0:T(8,128)(2,1)S(1)} %collective-permute-done.4.back_ref), custom_call_target="tpu_custom_call" | custom-call | tf_op jit(solution)/shard_map/add_rows/pallas_call | solution.py:139
  38.1 0.7 %fusion.21 = f32[416,1152]{1,0:T(8,128)S(1)} fusion(bf16[288,416]{1,0:T(8,128)(2,1)S(1)} %pass_on.9, bf16[288,1152]{1,0:T(8,128)(2,1)S(1)} %get-tuple-element.21), kind=kOutput, calls=%fused_computation.28 | convolution fusion | flops 276037632 | bytes 2820096 | tf_op jit(solution)/shard_map/dot_general | solution.py:28
  38.8 0.4 fusion.2.total_ref
  39.2 7.6 %collective-permute-done.5.back_ref = bf16[416,1152]{1,0:T(8,128)(2,1)S(1)} collective-permute-done((bf16[416,1152]{1,0:T(8,128)(2,1)S(1)}, bf16[416,1152]{1,0:T(8,128)(2,1)S(1)}, u32[]{:S(2)}, u32[]{:S(2)}) %collective-permute-start.5) | collective-permute-done | bytes 958496 | tf_op jit(solution)/shard_map/ppermute | solution.py:20
  46.8 1.0 %add_rows.5 = (bf16[416,1152]{1,0:T(8,128)(2,1)}, f32[8,128]{1,0:T(8,128)S(1)}) custom-call(f32[416,1152]{1,0:T(8,128)S(1)} %fusion.2.total_ref, bf16[416,1152]{1,0:T(8,128)(2,1)S(1)} %collective-permute-done.5.back_ref), custom_call_target="tpu_custom_call" | custom-call | tf_op jit(solution)/shard_map/add_rows/pallas_call | solution.py:139
  47.8 0.8 %add_rows.6.refs_0_ = bf16[416,1152]{1,0:T(8,128)(2,1)} custom-call(f32[416,1152]{1,0:T(8,128)S(1)} %fusion.total_ref, bf16[176,1152]{1,0:T(8,128)(2,1)S(1)} %collective-permute-done.7.back_ref, bf16[416,1152]{1,0:T(8,128)(2,1)} %get-tuple-element.26.refs_0_, f32[8,128]{1,0:T(8,128)S(1)} %get-tuple-element.27.refs_1_), custom_call_target="tpu_custom_call", output_to_operand_aliasing={{}: (2, {})} | custom-call | tf_op jit(solution)/shard_map/add_rows/pallas_call | solution.py:139
  48.7 0.8 %collective-permute-done.6.back_ref = bf16[112,1152]{1,0:T(8,128)(2,1)S(1)} collective-permute-done((bf16[112,1152]{1,0:T(8,128)(2,1)S(1)}, bf16[112,1152]{1,0:T(8,128)(2,1)S(1)}, u32[]{:S(2)}, u32[]{:S(2)}) %collective-permute-start.6) | collective-permute-done | bytes 258080 | tf_op jit(solution)/shard_map/ppermute | solution.py:20
  49.4 0.7 %add_rows.7 = bf16[416,1152]{1,0:T(8,128)(2,1)} custom-call(f32[416,1152]{1,0:T(8,128)S(1)} %fusion.total_ref, bf16[112,1152]{1,0:T(8,128)(2,1)S(1)} %collective-permute-done.6.back_ref, bf16[416,1152]{1,0:T(8,128)(2,1)} %add_rows.6.refs_0_), custom_call_target="tpu_custom_call", output_to_operand_aliasing={{}: (2, {})} | custom-call | tf_op jit(solution)/shard_map/add_rows/pallas_call | solution.py:139
  (18 shorter events, 0.2 us)
Async XLA Ops:
  0.6 14.9 %copy-start.3 = (s32[1,416]{1,0:T(1,128)S(1)}, s32[1,416]{1,0:T(1,128)}, u32[]{:S(2)}) copy-start(s32[1,416]{1,0:T(1,128)} %array_ref.3) | copy-start | bytes 4996
  1.6 13.9 %collective-permute-start = (bf16[128,1152]{1,0:T(8,128)(2,1)S(1)}, bf16[128,1152]{1,0:T(8,128)(2,1)S(1)}, u32[]{:S(2)}, u32[]{:S(2)}) collective-permute-start(bf16[128,1152]{1,0:T(8,128)(2,1)S(1)} %slice.3.refs_0_), channel_id=1, source_target_pairs={{0,4},{4,8},{8,12},{12,16},{16,20},{20,24},{24,28},{28,0},{1,5},{5... | collective-permute-start | bytes 884744 | tf_op jit(solution)/shard_map/ppermute | solution.py:20
  4.6 1.2 %copy-start = (bf16[416,1152]{1,0:T(8,128)(2,1)S(1)}, bf16[416,1152]{1,0:T(8,128)(2,1)}, u32[]{:S(2)}) copy-start(bf16[416,1152]{1,0:T(8,128)(2,1)} %array_ref.5) | copy-start | bytes 2875396
  5.9 21.4 %collective-permute-start.2 = (bf16[240,1152]{1,0:T(8,128)(2,1)S(1)}, bf16[240,1152]{1,0:T(8,128)(2,1)S(1)}, u32[]{:S(2)}, u32[]{:S(2)}) collective-permute-start(bf16[240,1152]{1,0:T(8,128)(2,1)S(1)} %fetch.4), channel_id=1, source_target_pairs={{0,4},{4,8},{8,12},{12,16},{16,20},{20,24},{24,28},{28,0},{1,5},{5... | collective-permute-start | bytes 1658888 | tf_op jit(solution)/shard_map/ppermute | solution.py:20
  7.5 12.1 %collective-permute-start.1 = (bf16[416,1152]{1,0:T(8,128)(2,1)}, bf16[416,1152]{1,0:T(8,128)(2,1)S(1)}, u32[]{:S(2)}, u32[]{:S(2)}) collective-permute-start(bf16[416,1152]{1,0:T(8,128)(2,1)} %image_ref.3), channel_id=1, source_target_pairs={{0,3},{1,0},{2,1},{3,2},{4,7},{5,4},{6,5},{7,6},{8,11},{9,8},{10,9... | collective-permute-start | bytes 2875400 | tf_op jit(solution)/shard_map/ppermute | solution.py:20
  15.5 1.2 %copy-start.1 = (bf16[416,1152]{1,0:T(8,128)(2,1)S(1)}, bf16[416,1152]{1,0:T(8,128)(2,1)}, u32[]{:S(2)}) copy-start(bf16[416,1152]{1,0:T(8,128)(2,1)} %array_ref.5) | copy-start | bytes 2875396
  15.5 1.5 %copy-start.2 = (bf16[416,1152]{1,0:T(8,128)(2,1)S(1)}, bf16[416,1152]{1,0:T(8,128)(2,1)}, u32[]{:S(2)}) copy-start(bf16[416,1152]{1,0:T(8,128)(2,1)} %image_ref.3) | copy-start | bytes 2875396
  18.1 11.4 %collective-permute-start.3 = (bf16[48,1152]{1,0:T(8,128)(2,1)S(1)}, bf16[48,1152]{1,0:T(8,128)(2,1)S(1)}, u32[]{:S(2)}, u32[]{:S(2)}) collective-permute-start(bf16[48,1152]{1,0:T(8,128)(2,1)S(1)} %fetch.5), channel_id=1, source_target_pairs={{0,4},{4,8},{8,12},{12,16},{16,20},{20,24},{24,28},{28,0},{1,5},{5... | collective-permute-start | bytes 331784 | tf_op jit(solution)/shard_map/ppermute | solution.py:20
  27.4 9.9 %collective-permute-start.4 = (bf16[128,1152]{1,0:T(8,128)(2,1)S(1)}, bf16[128,1152]{1,0:T(8,128)(2,1)S(1)}, u32[]{:S(2)}, u32[]{:S(2)}) collective-permute-start(bf16[128,1152]{1,0:T(8,128)(2,1)S(1)} %pass_on.8.refs_2_), channel_id=1, source_target_pairs={{0,28},{4,0},{8,4},{12,8},{16,12},{20,16},{24,20},{28,24},{1,29},{... | collective-permute-start | bytes 884744 | tf_op jit(solution)/shard_map/ppermute | solution.py:20
  31.3 16.5 %collective-permute-start.7 = (bf16[176,1152]{1,0:T(8,128)(2,1)S(1)}, bf16[176,1152]{1,0:T(8,128)(2,1)S(1)}, u32[]{:S(2)}, u32[]{:S(2)}) collective-permute-start(bf16[176,1152]{1,0:T(8,128)(2,1)S(1)} %get-tuple-element.23.refs_1_), channel_id=1, source_target_pairs={{0,28},{4,0},{8,4},{12,8},{16,12},{20,16},{24,20},{28,24},{1,29},{... | collective-permute-start | bytes 1216520 | tf_op jit(solution)/shard_map/ppermute | solution.py:20
  33.5 13.3 %collective-permute-start.5 = (bf16[416,1152]{1,0:T(8,128)(2,1)S(1)}, bf16[416,1152]{1,0:T(8,128)(2,1)S(1)}, u32[]{:S(2)}, u32[]{:S(2)}) collective-permute-start(bf16[416,1152]{1,0:T(8,128)(2,1)S(1)} %fusion.4.refs_1_), channel_id=1, source_target_pairs={{0,1},{1,2},{2,3},{3,0},{4,5},{5,6},{6,7},{7,4},{8,9},{9,10},{10,1... | collective-permute-start | bytes 2875400 | tf_op jit(solution)/shard_map/ppermute | solution.py:20
  33.6 15.9 %collective-permute-start.6 = (bf16[112,1152]{1,0:T(8,128)(2,1)S(1)}, bf16[112,1152]{1,0:T(8,128)(2,1)S(1)}, u32[]{:S(2)}, u32[]{:S(2)}) collective-permute-start(bf16[112,1152]{1,0:T(8,128)(2,1)S(1)} %pass_on.11), channel_id=1, source_target_pairs={{0,28},{4,0},{8,4},{12,8},{16,12},{20,16},{24,20},{28,24},{1,29},{... | collective-permute-start | bytes 774152 | tf_op jit(solution)/shard_map/ppermute | solution.py:20
